TPU v7x, 32 devices: a whole 2x2x4 slice. The times are simulated.
32 devices in a mesh: groups: 2 (over y), dp: 4 (over z), owner: 4 (over x, core).
Axes of the slice: x: 2, y: 2, z: 4, core: 2. Of those that a mesh axis runs over, the one named last changes fastest.
Arguments:
- activations: bfloat16 [4096, 4096], P(('groups', 'dp'), 'owner'), parts along dimension 0, may hold values from -64 to 64
- gradients: bfloat16 [4096, 14336], P(('groups', 'dp'), 'owner'), parts along dimension 0, may hold values from -64 to 64
- basis_act: bfloat16 [32, 128, 128], P('owner', 'dp'), may hold values from -0.5 to 0.5
- basis_grad: bfloat16 [112, 128, 128], P('owner', 'dp'), may hold values from -0.5 to 0.5
Outputs:
- act_covariance: float32 [64, 128, 128], P(('groups', 'owner'), 'dp'), parts along dimension 0
- grad_covariance: float32 [224, 128, 128], P(('groups', 'owner'), 'dp'), parts along dimension 0
- act_eigen: float32 [8192], P(('groups', 'owner')), parts along dimension 0
- grad_eigen: float32 [28672], P(('groups', 'owner')), parts along dimension 0
- token_scores: float32 [4096], P(('groups', 'dp')), parts along dimension 0
There are 2 independent parts, one for each index of `groups`. A program takes and returns all parts, laid end to end along the dimension named above; an argument that names none is the same for every part. Nothing has to cross between parts.
All inputs are finite; a program needn't handle non-finite values.
Results may differ from a plain program's by a relative error of at most 0.0003.
Values may be sent and summed in bfloat16 or wider, within the bound.
No kernel may reach another device: no remote copies, remote signals or barrier semaphores. Data moves between devices by JAX's collectives and lax.ppermute only.
A program may use at most 64 MiB of HBM per device.

v0:
```python
import jax
import jax.numpy as jnp
from jax import lax
from jax.sharding import PartitionSpec as P

D = 4096
FF = 14336


highest = lax.Precision.HIGHEST
damp_root = 0.31622776601683794


def partial_eigen(covariance, full_basis, own_basis):
    rotated = jnp.einsum(
        "nrk,nkj->nrj", covariance, full_basis.astype(jnp.float32), precision=highest
    )
    return jnp.sum(rotated * own_basis.astype(jnp.float32), axis=1).reshape(-1)


def local(activations, gradients, basis_act, basis_grad):
    rows_local = activations.shape[0]
    block_width = basis_act.shape[2]
    scale_rows = 1.0 / (rows_local * lax.axis_size("dp"))
    act_blocks = activations.reshape(rows_local, -1, block_width)
    grad_blocks = gradients.reshape(rows_local, -1, block_width)
    part_act = (
        jnp.einsum("tni,tnj->nij", act_blocks, act_blocks, preferred_element_type=jnp.float32)
        * scale_rows
    )
    part_grad = (
        jnp.einsum("tni,tnj->nij", grad_blocks, grad_blocks, preferred_element_type=jnp.float32)
        * scale_rows
    )
    full_act, full_grad = (
        lax.all_gather(basis_act, "dp", axis=1, tiled=True),
        lax.all_gather(basis_grad, "dp", axis=1, tiled=True),
    )
    proj_act = jnp.einsum("tni,nij->tnj", act_blocks, full_act, preferred_element_type=jnp.float32)
    proj_grad = jnp.einsum(
        "tni,nij->tnj", grad_blocks, full_grad, preferred_element_type=jnp.float32
    )
    power_act = proj_act * proj_act
    power_grad = proj_grad * proj_grad
    act_covariance, grad_covariance = (
        lax.psum_scatter(part_act, "dp", scatter_dimension=1, tiled=True),
        lax.psum_scatter(part_grad, "dp", scatter_dimension=1, tiled=True),
    )
    act_eigen, grad_eigen = lax.psum(
        (
            partial_eigen(act_covariance, full_act, basis_act),
            partial_eigen(grad_covariance, full_grad, basis_grad),
        ),
        "dp",
    )
    act_total, grad_total = lax.psum((jnp.sum(act_eigen), jnp.sum(grad_eigen)), "owner")
    damp_act = damp_root * (act_total * (1.0 / D))
    damp_grad = damp_root * (grad_total * (1.0 / FF))
    act_part = jnp.sum(power_act.reshape(rows_local, -1) / (act_eigen[None, :] + damp_act), axis=1)
    grad_part = jnp.sum(
        power_grad.reshape(rows_local, -1) / (grad_eigen[None, :] + damp_grad), axis=1
    )
    act_weight, grad_weight = lax.psum((act_part, grad_part), "owner")
    token_scores = act_weight * grad_weight * (1.0 / (D * FF))
    return (act_covariance, grad_covariance, act_eigen, grad_eigen, token_scores)


def solution(mesh):
    return jax.shard_map(
        local,
        mesh=mesh,
        in_specs=(
            P(("groups", "dp"), "owner"),
            P(("groups", "dp"), "owner"),
            P("owner", "dp", None),
            P("owner", "dp", None),
        ),
        out_specs=(
            P(("groups", "owner"), "dp", None),
            P(("groups", "owner"), "dp", None),
            P(("groups", "owner")),
            P(("groups", "owner")),
            P(("groups", "dp")),
        ),
        check_vma=False,
    )
```

profile of v0, /device:TPU:0, one launch (start us, length us, event | category | flops | bytes accessed | tf_op | source)
XLA Modules:
  0.0 134.1 jit_solution(4447936046702680951)
XLA Ops:
  7.2 0.0 copy-start
  7.2 0.0 reduce-scatter.3.cloned.1.call-start
  7.2 1.2 copy-done
  8.4 1.4 %convolution_multiply_fusion.1 = f32[8,128,128]{2,1,0:T(8,128)} fusion(bf16[512,1024]{1,0:T(8,128)(2,1)S(1)} %copy-done), kind=kOutput, calls=%fused_computation.5 | convolution fusion | flops 134348800 | bytes 1572864 | tf_op jit(solution)/shard_map/tni,tnj->nij/dot_general | solution.py:28
  9.8 0.0 reduce-scatter.3.cloned.1.call-update
  9.8 0.0 reduce-scatter.5.cloned.1.call-start
  9.8 5.9 %copy.17 = bf16[512,3584]{0,1:T(8,128)(2,1)} copy(bf16[512,3584]{1,0:T(8,128)(2,1)} %param.5) | data formatting | bytes 7340032 | tf_op args[1]
  15.8 0.0 copy-start.2
  15.8 0.0 copy-start.1
  15.8 5.6 %convolution_multiply_fusion = f32[28,128,128]{2,1,0:T(8,128)} fusion(bf16[512,28,128]{0,2,1:T(8,128)(2,1)} %bitcast.28), kind=kOutput, calls=%fused_computation.4 | convolution fusion | flops 470220800 | bytes 5505024 | tf_op jit(solution)/shard_map/tni,tnj->nij/dot_general | solution.py:32
  21.3 0.0 reduce-scatter.5.cloned.1.call-update
  21.4 0.0 copy-done.2
  21.4 17.4 %all_gather.6 = bf16[8,128,128]{2,1,0:T(8,128)(2,1)S(1)} all-gather(bf16[8,32,128]{2,1,0:T(8,128)(2,1)S(1)} %copy-done.2), channel_id=1, replica_groups=mesh['groups'=2,'dp'=4,'owner'=4] {'dp'}, dimensions={1}, use_global_device_ids=true | all-gather | bytes 327680 | tf_op jit(solution)/shard_map/all_gather | solution.py:36
  38.8 0.0 copy-done.1
  38.8 30.7 %all_gather.7 = bf16[28,128,128]{2,1,0:T(8,128)(2,1)S(1)} all-gather(bf16[28,32,128]{2,1,0:T(8,128)(2,1)S(1)} %copy-done.1), channel_id=1, replica_groups=mesh['groups'=2,'dp'=4,'owner'=4] {'dp'}, dimensions={1}, use_global_device_ids=true | all-gather | bytes 1146880 | tf_op jit(solution)/shard_map/all_gather | solution.py:37
  69.5 0.0 reduce-scatter.3.cloned.1.call-done
  69.5 1.2 fusion.3
  70.7 16.1 %reduce-scatter.5.cloned.1.call-done = f32[28,32,128]{2,1,0:T(8,128)} async-done(((f32[28,128,128]{2,1,0:T(8,128)}), f32[28,32,128]{2,1,0:T(8,128)}) %reduce-scatter.5.cloned.1.call-update) | async-done | bytes 458768 | tf_op jit(solution)/shard_map/reduce_scatter | solution.py:47
  86.8 1.9 %fusion.2 = f32[28,128]{1,0:T(8,128)S(1)} fusion(f32[28,32,128]{2,1,0:T(8,128)} %reduce-scatter.5.cloned.1.call-done, bf16[28,128,128]{2,1,0:T(8,128)(2,1)S(1)} %all_gather.7, bf16[28,32,128]{2,1,0:T(8,128)(2,1)S(1)} %copy-done.1), kind=kOutput, calls=%fused_computation.7 | convolution fusion | flops 176501248 | bytes 1619968 | tf_op jit(solution)/shard_map/nrk,nkj->nrj/dot_general | solution.py:15
  88.7 18.8 %all-reduce.2 = (f32[1024]{0:T(1024)S(1)}, f32[3584]{0:T(1024)S(1)}) all-reduce(f32[1024]{0:T(1024)S(1)} %bitcast.31, f32[3584]{0:T(1024)S(1)} %bitcast.30), channel_id=1, replica_groups=mesh['groups'=2,'dp'=4,'owner'=4] {'dp'}, use_global_device_ids=true, to_apply=%region_3.0 | all-reduce | flops 4608 | bytes 36864 | tf_op jit(solution)/shard_map/psum | solution.py:49
  107.4 0.0 copy-start.3
  107.4 0.0 copy-start.4
  107.4 0.6 reduce_sum.56
  108.0 0.6 reduce_sum.58
  108.6 6.3 %all-reduce.1 = (f32[]{:T(128)}, f32[]{:T(128)}) all-reduce(f32[]{:T(128)} %reduce_sum.56, f32[]{:T(128)} %reduce_sum.58), channel_id=1, replica_groups=mesh['groups'=2,'dp'=4,'owner'=4] {'owner'}, use_global_device_ids=true, to_apply=%region_7.0 | all-reduce | flops 2 | bytes 16 | tf_op jit(solution)/shard_map/psum | solution.py:56
  115.5 3.4 %fusion = f32[512]{0:T(512)S(1)} fusion(bf16[28,128,128]{2,1,0:T(8,128)(2,1)S(1)} %all_gather.7, bf16[512,28,128]{0,2,1:T(8,128)(2,1)} %bitcast.29, f32[28,128]{1,0:T(8,128)S(1)} %add_bitcast_fusion), kind=kOutput, calls=%fused_computation.1 | convolution fusion | flops 475266560 | bytes 4603904 | tf_op jit(solution)/shard_map/tni,nij->tnj/dot_general | solution.py:40
  118.9 0.0 copy-done.3
  119.5 0.0 copy-done.4
  119.5 0.5 fusion.1
  120.1 6.6 %all-reduce = (f32[512]{0:T(512)S(1)}, f32[512]{0:T(512)S(1)}) all-reduce(f32[512]{0:T(512)S(1)} %fusion.1, f32[512]{0:T(512)S(1)} %fusion), channel_id=1, replica_groups=mesh['groups'=2,'dp'=4,'owner'=4] {'owner'}, use_global_device_ids=true, to_apply=%region_9.0 | all-reduce | flops 1024 | bytes 8192 | tf_op jit(solution)/shard_map/psum | solution.py:63
  126.7 0.6 multiply_multiply_fusion
  (2 shorter events, 0.0 us)
Async XLA Ops:
  7.2 1.2 copy-start
  7.2 62.3 %reduce-scatter.3.cloned.1.call-start = ((), (), s32[]{:S(2)}) async-start(), calls=%async_computation.2 | async-start | bytes 655360 | tf_op jit(solution)/shard_map/reduce_scatter | solution.py:46
  9.8 77.0 %reduce-scatter.5.cloned.1.call-start = ((), (), s32[]{:S(2)}) async-start(), calls=%async_computation.3 | async-start | bytes 2293760 | tf_op jit(solution)/shard_map/reduce_scatter | solution.py:47
  15.8 5.6 %copy-start.2 = (bf16[8,32,128]{2,1,0:T(8,128)(2,1)S(1)}, bf16[8,32,128]{2,1,0:T(8,128)(2,1)}, u32[]{:S(2)}) copy-start(bf16[8,32,128]{2,1,0:T(8,128)(2,1)} %param.6) | copy-start | bytes 196612
  15.8 23.0 %copy-start.1 = (bf16[28,32,128]{2,1,0:T(8,128)(2,1)S(1)}, bf16[28,32,128]{2,1,0:T(8,128)(2,1)}, u32[]{:S(2)}) copy-start(bf16[28,32,128]{2,1,0:T(8,128)(2,1)} %param.7) | copy-start | bytes 688132
  107.4 11.4 %copy-start.3 = (f32[3584]{0:T(1024)}, f32[3584]{0:T(1024)S(1)}, u32[]{:S(2)}) copy-start(f32[3584]{0:T(1024)S(1)} %get-tuple-element.10) | copy-start | bytes 43012
  107.4 12.1 %copy-start.4 = (f32[1024]{0:T(1024)}, f32[1024]{0:T(1024)S(1)}, u32[]{:S(2)}) copy-start(f32[1024]{0:T(1024)S(1)} %get-tuple-element.9) | copy-start | bytes 12292
Sparse Core Ops, SparseCore 0:
  10.9 25.1 reduce-scatter.2
  38.9 47.8 reduce-scatter.4
where the time goes:
time: 135 us; the launch traced here: 134 us
  blocking collectives  79.8 us (59%)
  waiting for transfers between devices  16.1 us (12%)
  between operations  15.3 us (11%)
  matrix products  13.9 us (10%)
  local copies, waits for them, and re-layouts  7.12 us (5%)
  other arithmetic  1.8 us (1%)
    all_gather x1, blocking collectives, local(): lax.all_gather(basis_grad, 'dp', axis=1, tiled=True)  30.7 us
    psum x1, blocking collectives, local(): lax.psum((partial_eigen(act_covariance, full_act, basis_act), partial_eig...  18.8 us
    all_gather x1, blocking collectives, local(): lax.all_gather(basis_act, 'dp', axis=1, tiled=True)  17.4 us
    reduce_scatter x1, waiting for transfers between devices, local(): lax.psum_scatter(part_grad, 'dp', scatter_dimension=1, tiled=True)  16.1 us
    unnamed x11, local copies, waits for them, and re-layouts  7.12 us
    psum x1, blocking collectives, local(): act_weight, grad_weight = lax.psum((act_part, grad_part), 'owner')  6.63 us
    psum x1, blocking collectives, local(): lax.psum((jnp.sum(act_eigen), jnp.sum(grad_eigen)), 'owner')  6.27 us
    dot_general x1, matrix products, local(): jnp.einsum('tni,tnj->nij', grad_blocks, grad_blocks, preferred_element_ty...  5.56 us
  transfers between devices with their start and end apart: 2, of which 1 were waited for; matrix products, arithmetic and copies ran while one was open for 9% of the time, Pallas kernels for 0%

commit v1 on v0

v1 whole, which is shorter than its diff:
```python
import functools

import jax
import jax.numpy as jnp
from jax import lax
from jax.experimental import pallas as pl
from jax.experimental.pallas import tpu as pltpu
from jax.sharding import PartitionSpec as P

D = 4096
FF = 14336
BLK = 128
STEPS = 4
VMEM_LIMIT = 48 * 1024 * 1024

damp_root = 0.31622776601683794
contract_rows = (((0,), (0,)), ((), ()))
contract_lanes = (((1,), (1,)), ((), ()))


def params():
    return pltpu.CompilerParams(vmem_limit_bytes=VMEM_LIMIT)


def gram_kernel(pieces, scale, me_ref, act_ref, grad_ref, *refs):
    out_refs, whole = refs[:pieces], refs[pieces]
    rows = BLK // pieces
    me = me_ref[0]
    act_here = act_ref.shape[1] // BLK
    grad_here = grad_ref.shape[1] // BLK
    for block in range(act_here + grad_here):
        if block < act_here:
            values = act_ref[:, block * BLK : (block + 1) * BLK]
        else:
            at = block - act_here
            values = grad_ref[:, at * BLK : (at + 1) * BLK]
        gram = lax.dot_general(
            values, values, contract_rows, preferred_element_type=jnp.float32
        )
        whole[block] = gram * scale
        for shift in range(pieces):
            first = pl.multiple_of(lax.rem(me + shift, pieces) * rows, rows)
            out_refs[shift][0, block] = whole[block, pl.ds(first, rows), :]


def partial_gram(me, activations, gradients, pieces, scale):
    tokens, act_width = activations.shape
    grad_width = gradients.shape[1]
    act_step, grad_step = act_width // STEPS, grad_width // STEPS
    blocks = (act_step + grad_step) // BLK
    rows = BLK // pieces
    return pl.pallas_call(
        functools.partial(gram_kernel, pieces, scale),
        grid_spec=pltpu.PrefetchScalarGridSpec(
            num_scalar_prefetch=1,
            grid=(STEPS,),
            in_specs=[
                pl.BlockSpec((tokens, act_step), lambda i, me: (0, i)),
                pl.BlockSpec((tokens, grad_step), lambda i, me: (0, i)),
            ],
            out_specs=[
                pl.BlockSpec((1, blocks, rows, BLK), lambda i, me: (i, 0, 0, 0))
            ]
            * pieces,
            scratch_shapes=[pltpu.VMEM((blocks, BLK, BLK), jnp.float32)],
        ),
        out_shape=[jax.ShapeDtypeStruct((STEPS, blocks, rows, BLK), jnp.float32)] * pieces,
        compiler_params=params(),
        name="partial_gram",
    )(me, activations, gradients)


def sum_kernel(*refs):
    parts, (act_ref, grad_ref) = refs[:-2], refs[-2:]
    act_here = act_ref.shape[0]
    total = parts[0][0]
    for part in parts[1:]:
        total = total + part[0]
    act_ref[...] = total[:act_here]
    grad_ref[...] = total[act_here:]


def sum_pieces(parts, act_blocks, grad_blocks):
    _, blocks, rows, _ = parts[0].shape
    return pl.pallas_call(
        sum_kernel,
        grid=(STEPS,),
        in_specs=[pl.BlockSpec((1, blocks, rows, BLK), lambda i: (i, 0, 0, 0))] * len(parts),
        out_specs=[
            pl.BlockSpec((act_blocks // STEPS, rows, BLK), lambda i: (i, 0, 0)),
            pl.BlockSpec((grad_blocks // STEPS, rows, BLK), lambda i: (i, 0, 0)),
        ],
        out_shape=[
            jax.ShapeDtypeStruct((act_blocks, rows, BLK), jnp.float32),
            jax.ShapeDtypeStruct((grad_blocks, rows, BLK), jnp.float32),
        ],
        compiler_params=params(),
        name="sum_pieces",
    )(*parts)


def project(me, values, shard_refs, block, basis):
    pieces = len(shard_refs)
    rows = BLK // pieces
    for shift in range(pieces):
        first = pl.multiple_of(lax.rem(me - shift + pieces, pieces) * rows, rows)
        basis[pl.ds(first, rows), :] = shard_refs[shift][block]
    return lax.dot_general(
        values, basis[...], (((1,), (0,)), ((), ())), preferred_element_type=jnp.float32
    )


def eigen_kernel(pieces, scale, me_ref, act_ref, grad_ref, *refs):
    act_shards, grad_shards = refs[:pieces], refs[pieces : 2 * pieces]
    eigen_ref, basis = refs[2 * pieces :]
    me = me_ref[0]
    act_here = act_ref.shape[1] // BLK
    grad_here = grad_ref.shape[1] // BLK
    for block in range(act_here + grad_here):
        if block < act_here:
            source, shards, at = act_ref, act_shards, block
        else:
            source, shards, at = grad_ref, grad_shards, block - act_here
        values = source[:, at * BLK : (at + 1) * BLK]
        projected = project(me, values, shards, at, basis.at[block])
        eigen_ref[0, block : block + 1, :] = (
            jnp.sum(projected * projected, axis=0, keepdims=True) * scale
        )


def shard_specs(shards, step_blocks):
    rows = shards[0].shape[1]
    return [pl.BlockSpec((step_blocks, rows, BLK), lambda i, me: (i, 0, 0))] * len(shards)


def partial_eigen(me, activations, gradients, act_shards, grad_shards, scale):
    tokens, act_width = activations.shape
    grad_width = gradients.shape[1]
    act_step, grad_step = act_width // STEPS, grad_width // STEPS
    blocks = (act_step + grad_step) // BLK
    pieces = len(act_shards)
    return pl.pallas_call(
        functools.partial(eigen_kernel, pieces, scale),
        grid_spec=pltpu.PrefetchScalarGridSpec(
            num_scalar_prefetch=1,
            grid=(STEPS,),
            in_specs=[
                pl.BlockSpec((tokens, act_step), lambda i, me: (0, i)),
                pl.BlockSpec((tokens, grad_step), lambda i, me: (0, i)),
                *shard_specs(act_shards, act_step // BLK),
                *shard_specs(grad_shards, grad_step // BLK),
            ],
            out_specs=pl.BlockSpec((1, blocks, BLK), lambda i, me: (i, 0, 0)),
            scratch_shapes=[pltpu.VMEM((blocks, BLK, BLK), jnp.bfloat16)],
        ),
        out_shape=jax.ShapeDtypeStruct((STEPS, blocks, BLK), jnp.float32),
        compiler_params=params(),
        name="partial_eigen",
    )(me, activations, gradients, *act_shards, *grad_shards)


def weight_kernel(pieces, me_ref, act_ref, grad_ref, eigen_ref, damp_ref, *refs):
    act_shards, grad_shards = refs[:pieces], refs[pieces : 2 * pieces]
    weight_ref, basis, act_sum, grad_sum = refs[2 * pieces :]
    me = me_ref[0]
    step = pl.program_id(0)
    act_here = act_ref.shape[1] // BLK
    grad_here = grad_ref.shape[1] // BLK

    @pl.when(step == 0)
    def _():
        act_sum[...] = jnp.zeros_like(act_sum)
        grad_sum[...] = jnp.zeros_like(grad_sum)

    for block in range(act_here + grad_here):
        if block < act_here:
            source, shards, at, total, damp = act_ref, act_shards, block, act_sum, damp_ref[0]
        else:
            source, shards, at = grad_ref, grad_shards, block - act_here
            total, damp = grad_sum, damp_ref[1]
        values = source[:, at * BLK : (at + 1) * BLK]
        projected = project(me, values, shards, at, basis.at[block])
        inverse = 1.0 / (eigen_ref[0, block : block + 1, :] + damp)
        total[...] += projected * projected * inverse

    @pl.when(step == STEPS - 1)
    def _():
        ones = jnp.ones((8, BLK), jnp.float32)
        for index, total in enumerate((act_sum, grad_sum)):
            sums = lax.dot_general(
                ones,
                total[...],
                contract_lanes,
                precision=lax.Precision.HIGHEST,
                preferred_element_type=jnp.float32,
            )
            weight_ref[index : index + 1, :] = sums[0:1]


def partial_weights(me, activations, gradients, eigen, damp, act_shards, grad_shards):
    tokens, act_width = activations.shape
    grad_width = gradients.shape[1]
    act_step, grad_step = act_width // STEPS, grad_width // STEPS
    blocks = (act_step + grad_step) // BLK
    pieces = len(act_shards)
    return pl.pallas_call(
        functools.partial(weight_kernel, pieces),
        grid_spec=pltpu.PrefetchScalarGridSpec(
            num_scalar_prefetch=1,
            grid=(STEPS,),
            in_specs=[
                pl.BlockSpec((tokens, act_step), lambda i, me: (0, i)),
                pl.BlockSpec((tokens, grad_step), lambda i, me: (0, i)),
                pl.BlockSpec((1, blocks, BLK), lambda i, me: (i, 0, 0)),
                pl.BlockSpec(memory_space=pltpu.SMEM),
                *shard_specs(act_shards, act_step // BLK),
                *shard_specs(grad_shards, grad_step // BLK),
            ],
            out_specs=pl.BlockSpec((2, tokens), lambda i, me: (0, 0)),
            scratch_shapes=[
                pltpu.VMEM((blocks, BLK, BLK), jnp.bfloat16),
                pltpu.VMEM((tokens, BLK), jnp.float32),
                pltpu.VMEM((tokens, BLK), jnp.float32),
            ],
        ),
        out_shape=jax.ShapeDtypeStruct((2, tokens), jnp.float32),
        compiler_params=params(),
        name="partial_weights",
    )(me, activations, gradients, eigen, damp, *act_shards, *grad_shards)


def rotate(value, axis, shift):
    count = lax.axis_size(axis)
    return lax.ppermute(value, axis, [(i, (i + shift) % count) for i in range(count)])


def sum_over(value, axis, direct):
    if not direct:
        return lax.psum(value, axis)
    total = value
    for shift in range(1, lax.axis_size(axis)):
        total = total + rotate(value, axis, shift)
    return total


def local(activations, gradients, basis_act, basis_grad):
    tokens = activations.shape[0]
    act_blocks, grad_blocks = basis_act.shape[0], basis_grad.shape[0]
    act_per_step = act_blocks // STEPS
    dp = lax.axis_size("dp")
    scale = 1.0 / (tokens * dp)
    direct = BLK // dp >= 32
    pieces = dp if direct else 1
    me = jnp.full((1,), lax.axis_index("dp") if direct else 0, jnp.int32)

    if direct:
        act_shards = [basis_act] + [rotate(basis_act, "dp", s) for s in range(1, dp)]
        grad_shards = [basis_grad] + [rotate(basis_grad, "dp", s) for s in range(1, dp)]
    else:
        act_shards = [lax.all_gather(basis_act, "dp", axis=1, tiled=True)]
        grad_shards = [lax.all_gather(basis_grad, "dp", axis=1, tiled=True)]

    grams = partial_gram(me, activations, gradients, pieces, scale)
    if direct:
        parts = [grams[0]] + [rotate(grams[s], "dp", s) for s in range(1, dp)]
    else:
        parts = [lax.psum_scatter(grams[0], "dp", scatter_dimension=2, tiled=True)]
    act_covariance, grad_covariance = sum_pieces(parts, act_blocks, grad_blocks)

    eigen = partial_eigen(me, activations, gradients, act_shards, grad_shards, scale)
    eigen = sum_over(eigen, "dp", direct)
    act_eigen, grad_eigen = eigen[:, :act_per_step], eigen[:, act_per_step:]
    sums = jnp.stack([jnp.sum(act_eigen), jnp.sum(grad_eigen)])
    sums = sum_over(sums, "owner", direct)
    damp = sums * jnp.array([damp_root / D, damp_root / FF], jnp.float32)
    weights = partial_weights(
        me, activations, gradients, eigen, damp, act_shards, grad_shards
    )
    weights = sum_over(weights, "owner", direct)
    token_scores = weights[0] * weights[1] * (1.0 / (D * FF))
    return (
        act_covariance,
        grad_covariance,
        act_eigen.reshape(-1),
        grad_eigen.reshape(-1),
        token_scores,
    )


def solution(mesh):
    return jax.shard_map(
        local,
        mesh=mesh,
        in_specs=(
            P(("groups", "dp"), "owner"),
            P(("groups", "dp"), "owner"),
            P("owner", "dp", None),
            P("owner", "dp", None),
        ),
        out_specs=(
            P(("groups", "owner"), "dp", None),
            P(("groups", "owner"), "dp", None),
            P(("groups", "owner")),
            P(("groups", "owner")),
            P(("groups", "dp")),
        ),
        check_vma=False,
    )
```

time: 135 us -> 102 us (0.76)
  the two profiles are of different devices: /device:TPU:0 before, /device:TPU:14 now
where the time goes in v1:
time: 102 us; the launch traced here: 101 us
  waiting for transfers between devices  57.7 us (57%)
  starting transfers between devices  19.4 us (19%)
  Pallas kernels  12.5 us (12%)
  local copies, waits for them, and re-layouts  5.65 us (6%)
  other arithmetic  5.13 us (5%)
    ppermute x18, waiting for transfers between devices, rotate(): lax.ppermute(value, axis, [(i, (i + shift) % count) for i in range(count)])  57.7 us
    ppermute x18, starting transfers between devices, rotate(): lax.ppermute(value, axis, [(i, (i + shift) % count) for i in range(count)])  19.4 us
    pallas_call x1, Pallas kernels, partial_gram(): pl.pallas_call(functools.partial(gram_kernel, pieces, scale), grid_spec=p...  5.14 us
    unnamed x12, local copies, waits for them, and re-layouts  5.05 us
    pallas_call x1, Pallas kernels, partial_weights(): pl.pallas_call(functools.partial(weight_kernel, pieces), grid_spec=pltpu....  3.46 us
    pallas_call x1, Pallas kernels, partial_eigen(): pl.pallas_call(functools.partial(eigen_kernel, pieces, scale), grid_spec=...  2.49 us
  transfers between devices with their start and end apart: 18, of which 12 were waited for; matrix products, arithmetic and copies ran while one was open for 6% of the time, Pallas kernels for 9%

profile of v1, /device:TPU:14, one launch (start us, length us, event | category | flops | bytes accessed | tf_op | source)
XLA Modules:
  0.0 101.1 jit_solution(7523718296276198549)
XLA Ops:
  0.6 1.6 %collective-permute-start.6 = (bf16[28,32,128]{2,1,0:T(8,128)(2,1)}, bf16[28,32,128]{2,1,0:T(8,128)(2,1)S(1)}, u32[]{:S(2)}, u32[]{:S(2)}) collective-permute-start(bf16[28,32,128]{2,1,0:T(8,128)(2,1)} %refs_4_.3), channel_id=1, source_target_pairs={{0,4},{4,8},{8,12},{12,0},{1,5},{5,9},{9,13},{13,1},{2,6},{6,10},{... | collective-permute-start | bytes 688136 | tf_op jit(solution)/shard_map/ppermute | solution.py:234
  2.3 1.2 %collective-permute-start.7 = (bf16[28,32,128]{2,1,0:T(8,128)(2,1)}, bf16[28,32,128]{2,1,0:T(8,128)(2,1)S(1)}, u32[]{:S(2)}, u32[]{:S(2)}) collective-permute-start(bf16[28,32,128]{2,1,0:T(8,128)(2,1)} %refs_4_.3), channel_id=1, source_target_pairs={{0,8},{4,12},{8,0},{12,4},{1,9},{5,13},{9,1},{13,5},{2,10},{6,14},... | collective-permute-start | bytes 688136 | tf_op jit(solution)/shard_map/ppermute | solution.py:234
  3.5 1.8 %collective-permute-start.8 = (bf16[28,32,128]{2,1,0:T(8,128)(2,1)}, bf16[28,32,128]{2,1,0:T(8,128)(2,1)S(1)}, u32[]{:S(2)}, u32[]{:S(2)}) collective-permute-start(bf16[28,32,128]{2,1,0:T(8,128)(2,1)} %refs_4_.3), channel_id=1, source_target_pairs={{0,12},{4,0},{8,4},{12,8},{1,13},{5,1},{9,5},{13,9},{2,14},{6,2},{... | collective-permute-start | bytes 688136 | tf_op jit(solution)/shard_map/ppermute | solution.py:234
  5.3 0.2 collective-permute-start.3
  5.5 3.5 %collective-permute-start.4 = (bf16[8,32,128]{2,1,0:T(8,128)(2,1)}, bf16[8,32,128]{2,1,0:T(8,128)(2,1)S(1)}, u32[]{:S(2)}, u32[]{:S(2)}) collective-permute-start(bf16[8,32,128]{2,1,0:T(8,128)(2,1)} %refs_0_.3), channel_id=1, source_target_pairs={{0,8},{4,12},{8,0},{12,4},{1,9},{5,13},{9,1},{13,5},{2,10},{6,14},... | collective-permute-start | bytes 196616 | tf_op jit(solution)/shard_map/ppermute | solution.py:234
  9.0 18.1 %collective-permute-done.3.refs_1_ = bf16[8,32,128]{2,1,0:T(8,128)(2,1)S(1)} collective-permute-done((bf16[8,32,128]{2,1,0:T(8,128)(2,1)}, bf16[8,32,128]{2,1,0:T(8,128)(2,1)S(1)}, u32[]{:S(2)}, u32[]{:S(2)}) %collective-permute-start.3) | collective-permute-done | bytes 65568 | tf_op jit(solution)/shard_map/ppermute | solution.py:234
  27.1 0.0 collective-permute-start.5
  27.1 0.7 collective-permute-done.4.refs_2_
  27.8 4.1 %collective-permute-done.5.refs_3_ = bf16[8,32,128]{2,1,0:T(8,128)(2,1)S(1)} collective-permute-done((bf16[8,32,128]{2,1,0:T(8,128)(2,1)}, bf16[8,32,128]{2,1,0:T(8,128)(2,1)S(1)}, u32[]{:S(2)}, u32[]{:S(2)}) %collective-permute-start.5) | collective-permute-done | bytes 65568 | tf_op jit(solution)/shard_map/ppermute | solution.py:234
  31.9 0.0 collective-permute-done.6.refs_5_
  31.9 0.0 collective-permute-done.7.refs_6_
  31.9 0.0 collective-permute-done.8.refs_7_
  31.9 0.0 copy-start
  32.0 2.0 %copy-done = bf16[512,3584]{1,0:T(8,128)(2,1)S(1)} copy-done((bf16[512,3584]{1,0:T(8,128)(2,1)S(1)}, bf16[512,3584]{1,0:T(8,128)(2,1)}, u32[]{:S(2)}) %copy-start) | copy-done | bytes 3670040
  34.0 0.0 copy-start.2
  34.0 1.2 %copy-done.2 = bf16[512,1024]{1,0:T(8,128)(2,1)S(1)} copy-done((bf16[512,1024]{1,0:T(8,128)(2,1)S(1)}, bf16[512,1024]{1,0:T(8,128)(2,1)}, u32[]{:S(2)}) %copy-start.2) | copy-done | bytes 1048600
  35.2 0.0 copy-start.3
  35.2 0.9 copy-done.3
  36.1 0.0 copy-start.4
  36.2 0.8 copy-done.4
  37.0 2.5 %partial_eigen.1 = f32[4,9,128]{2,1,0:T(8,128)S(1)} custom-call(s32[1]{0:T(128)} %bitcast.me_ref, bf16[512,1024]{1,0:T(8,128)(2,1)S(1)} %copy-done.2, bf16[512,3584]{1,0:T(8,128)(2,1)S(1)} %copy-done, bf16[8,32,128]{2,1,0:T(8,128)(2,1)S(1)} %copy-done.4, bf16[8,32,128]{2,1,0:T(8,128)(2,1)S(1)} %collective-permute-done.3.refs_1_, ...), custom_call_target="tpu_custom_call" | custom-call | tf_op jit(solution)/shard_map/partial_eigen/pallas_call | solution.py:142
  39.5 0.0 copy-start.5
  39.5 0.0 copy-start.1
  39.5 0.1 collective-permute-start.11
  39.6 3.5 %collective-permute-start.10 = (f32[4,9,128]{2,1,0:T(8,128)S(1)}, f32[4,9,128]{2,1,0:T(8,128)S(1)}, u32[]{:S(2)}, u32[]{:S(2)}) collective-permute-start(f32[4,9,128]{2,1,0:T(8,128)S(1)} %partial_eigen.1), channel_id=1, source_target_pairs={{0,8},{4,12},{8,0},{12,4},{1,9},{5,13},{9,1},{13,5},{2,10},{6,14},... | collective-permute-start | bytes 55304 | tf_op jit(solution)/shard_map/ppermute | solution.py:234
  43.1 0.7 collective-permute-start.9
  43.7 5.1 %partial_gram.1 = (f32[4,9,32,128]{3,2,1,0:T(8,128)S(1)}, f32[4,9,32,128]{3,2,1,0:T(8,128)}, f32[4,9,32,128]{3,2,1,0:T(8,128)}, f32[4,9,32,128]{3,2,1,0:T(8,128)}) custom-call(s32[1]{0:T(128)} %bitcast.me_ref, bf16[512,1024]{1,0:T(8,128)(2,1)S(1)} %copy-done.2, bf16[512,3584]{1,0:T(8,128)(2,1)} %grad_ref.5), custom_call_target="tpu_custom_call" | custom-call | tf_op jit(solution)/shard_map/partial_gram/pallas_call | solution.py:52
  48.9 0.0 collective-permute-start
  48.9 3.7 %collective-permute-start.1 = (f32[4,9,32,128]{3,2,1,0:T(8,128)}, f32[4,9,32,128]{3,2,1,0:T(8,128)S(1)}, u32[]{:S(2)}, u32[]{:S(2)}) collective-permute-start(f32[4,9,32,128]{3,2,1,0:T(8,128)} %get-tuple-element.13), channel_id=1, source_target_pairs={{0,8},{4,12},{8,0},{12,4},{1,9},{5,13},{9,1},{13,5},{2,10},{6,14},... | collective-permute-start | bytes 1769480 | tf_op jit(solution)/shard_map/ppermute | solution.py:234
  52.6 0.0 collective-permute-done.11
  52.6 0.1 collective-permute-start.2
  52.7 0.0 collective-permute-done.10
  52.7 0.0 collective-permute-done.9
  52.7 1.2 %slice_reduce_fusion.1 = (f32[]{:T(128)}, f32[4,2,128]{2,1,0:T(2,128)}) fusion(f32[4,9,128]{2,1,0:T(8,128)S(1)} %add_add_fusion.eigen_ref), kind=kLoop, calls=%fused_computation.7 | loop fusion | flops 1023 | bytes 8196 | tf_op jit(solution)/shard_map/reduce_sum | solution.py:273
  53.9 0.6 slice_reduce_fusion
  54.5 1.4 %pad_maximum_fusion = f32[2]{0:T(128)S(1)} fusion(f32[1]{0:T(128)} %bitcast.3, f32[1]{0:T(128)} %bitcast.2), kind=kLoop, calls=%fused_computation.4 | loop fusion | flops 2 | bytes 16 | tf_op jit(solution)/shard_map/stack | solution.py:273
  55.9 0.0 collective-permute-start.14
  55.9 0.6 collective-permute-start.13
  56.5 0.7 collective-permute-done.14
  57.2 0.9 collective-permute-start.12
  58.0 1.4 %collective-permute-done.13 = f32[2]{0:T(128)S(1)} collective-permute-done((f32[2]{0:T(128)S(1)}, f32[2]{0:T(128)S(1)}, u32[]{:S(2)}, u32[]{:S(2)}) %collective-permute-start.13) | collective-permute-done | bytes 40 | tf_op jit(solution)/shard_map/ppermute | solution.py:234
  59.5 0.9 collective-permute-done.12
  60.4 0.0 copy-done.5
  60.4 1.4 %add_multiply_fusion.damp_ref = f32[2]{0:T(128)S(1)} fusion(f32[2]{0:T(128)S(1)} %copy-done.5, f32[2]{0:T(128)S(1)} %collective-permute-done.14, f32[2]{0:T(128)S(1)} %collective-permute-done.13, f32[2]{0:T(128)S(1)} %collective-permute-done.12, f32[1]{0:T(128)} %bitcast.3, f32[1]{0:T(128)} %bitcast.2), kind=kLoop, calls=%fused_computation.5 | loop fusion | flops 10 | bytes 48 | tf_op jit(solution)/shard_map/mul | solution.py:275
  61.7 0.0 copy-done.1
  61.7 3.5 %partial_weights.1 = f32[2,512]{1,0:T(2,128)S(1)} custom-call(s32[1]{0:T(128)} %bitcast.me_ref, bf16[512,1024]{1,0:T(8,128)(2,1)S(1)} %copy-done.2, bf16[512,3584]{1,0:T(8,128)(2,1)S(1)} %copy-done.1, f32[4,9,128]{2,1,0:T(8,128)S(1)} %add_add_fusion.eigen_ref, f32[2]{0:T(128)S(1)} %add_multiply_fusion.damp_ref, bf16[8,32,128]{2,1,0:T(8,128)(2,1)S(1)} %copy-done.4, ...), custom_call_target="tpu_custom_call" | custom-call | tf_op jit(solution)/shard_map/partial_weights/pallas_call | solution.py:206
  65.2 0.0 collective-permute-start.17
  65.2 0.6 collective-permute-start.16
  65.8 0.7 collective-permute-done.17
  66.5 0.9 collective-permute-start.15
  67.5 0.6 reshape.20
  68.1 0.8 collective-permute-done.16
  68.9 1.0 collective-permute-done.15
  69.8 0.6 fusion
  70.4 17.8 %collective-permute-done.refs_1_ = f32[4,9,32,128]{3,2,1,0:T(8,128)S(1)} collective-permute-done((f32[4,9,32,128]{3,2,1,0:T(8,128)}, f32[4,9,32,128]{3,2,1,0:T(8,128)S(1)}, u32[]{:S(2)}, u32[]{:S(2)}) %collective-permute-start) | collective-permute-done | bytes 589856 | tf_op jit(solution)/shard_map/ppermute | solution.py:234
  88.2 8.3 %collective-permute-done.1.refs_2_ = f32[4,9,32,128]{3,2,1,0:T(8,128)S(1)} collective-permute-done((f32[4,9,32,128]{3,2,1,0:T(8,128)}, f32[4,9,32,128]{3,2,1,0:T(8,128)S(1)}, u32[]{:S(2)}, u32[]{:S(2)}) %collective-permute-start.1) | collective-permute-done | bytes 589856 | tf_op jit(solution)/shard_map/ppermute | solution.py:234
  96.5 3.2 %collective-permute-done.2.refs_3_ = f32[4,9,32,128]{3,2,1,0:T(8,128)S(1)} collective-permute-done((f32[4,9,32,128]{3,2,1,0:T(8,128)}, f32[4,9,32,128]{3,2,1,0:T(8,128)S(1)}, u32[]{:S(2)}, u32[]{:S(2)}) %collective-permute-start.2) | collective-permute-done | bytes 589856 | tf_op jit(solution)/shard_map/ppermute | solution.py:234
  99.7 1.4 %sum_pieces.1 = (f32[8,32,128]{2,1,0:T(8,128)}, f32[28,32,128]{2,1,0:T(8,128)}) custom-call(f32[4,9,32,128]{3,2,1,0:T(8,128)S(1)} %get-tuple-element.11.refs_0_, f32[4,9,32,128]{3,2,1,0:T(8,128)S(1)} %collective-permute-done.refs_1_, f32[4,9,32,128]{3,2,1,0:T(8,128)S(1)} %collective-permute-done.1.refs_2_, f32[4,9,32,128]{3,2,1,0:T(8,128)S(1)} %collective-permute-done.2.refs_3_), custom_call_target="tpu_custom_call" | custom-call | tf_op jit(solution)/shard_map/sum_pieces/pallas_call | solution.py:85
  (2 shorter events, 0.0 us)
Async XLA Ops:
  0.6 31.3 %collective-permute-start.6 = (bf16[28,32,128]{2,1,0:T(8,128)(2,1)}, bf16[28,32,128]{2,1,0:T(8,128)(2,1)S(1)}, u32[]{:S(2)}, u32[]{:S(2)}) collective-permute-start(bf16[28,32,128]{2,1,0:T(8,128)(2,1)} %refs_4_.3), channel_id=1, source_target_pairs={{0,4},{4,8},{8,12},{12,0},{1,5},{5,9},{9,13},{13,1},{2,6},{6,10},{... | collective-permute-start | bytes 688136 | tf_op jit(solution)/shard_map/ppermute | solution.py:234
  2.3 29.7 %collective-permute-start.7 = (bf16[28,32,128]{2,1,0:T(8,128)(2,1)}, bf16[28,32,128]{2,1,0:T(8,128)(2,1)S(1)}, u32[]{:S(2)}, u32[]{:S(2)}) collective-permute-start(bf16[28,32,128]{2,1,0:T(8,128)(2,1)} %refs_4_.3), channel_id=1, source_target_pairs={{0,8},{4,12},{8,0},{12,4},{1,9},{5,13},{9,1},{13,5},{2,10},{6,14},... | collective-permute-start | bytes 688136 | tf_op jit(solution)/shard_map/ppermute | solution.py:234
  3.5 28.4 %collective-permute-start.8 = (bf16[28,32,128]{2,1,0:T(8,128)(2,1)}, bf16[28,32,128]{2,1,0:T(8,128)(2,1)S(1)}, u32[]{:S(2)}, u32[]{:S(2)}) collective-permute-start(bf16[28,32,128]{2,1,0:T(8,128)(2,1)} %refs_4_.3), channel_id=1, source_target_pairs={{0,12},{4,0},{8,4},{12,8},{1,13},{5,1},{9,5},{13,9},{2,14},{6,2},{... | collective-permute-start | bytes 688136 | tf_op jit(solution)/shard_map/ppermute | solution.py:234
  5.3 21.8 %collective-permute-start.3 = (bf16[8,32,128]{2,1,0:T(8,128)(2,1)}, bf16[8,32,128]{2,1,0:T(8,128)(2,1)S(1)}, u32[]{:S(2)}, u32[]{:S(2)}) collective-permute-start(bf16[8,32,128]{2,1,0:T(8,128)(2,1)} %refs_0_.3), channel_id=1, source_target_pairs={{0,4},{4,8},{8,12},{12,0},{1,5},{5,9},{9,13},{13,1},{2,6},{6,10},{... | collective-permute-start | bytes 196616 | tf_op jit(solution)/shard_map/ppermute | solution.py:234
  5.5 22.3 %collective-permute-start.4 = (bf16[8,32,128]{2,1,0:T(8,128)(2,1)}, bf16[8,32,128]{2,1,0:T(8,128)(2,1)S(1)}, u32[]{:S(2)}, u32[]{:S(2)}) collective-permute-start(bf16[8,32,128]{2,1,0:T(8,128)(2,1)} %refs_0_.3), channel_id=1, source_target_pairs={{0,8},{4,12},{8,0},{12,4},{1,9},{5,13},{9,1},{13,5},{2,10},{6,14},... | collective-permute-start | bytes 196616 | tf_op jit(solution)/shard_map/ppermute | solution.py:234
  27.1 4.8 %collective-permute-start.5 = (bf16[8,32,128]{2,1,0:T(8,128)(2,1)}, bf16[8,32,128]{2,1,0:T(8,128)(2,1)S(1)}, u32[]{:S(2)}, u32[]{:S(2)}) collective-permute-start(bf16[8,32,128]{2,1,0:T(8,128)(2,1)} %refs_0_.3), channel_id=1, source_target_pairs={{0,12},{4,0},{8,4},{12,8},{1,13},{5,1},{9,5},{13,9},{2,14},{6,2},{... | collective-permute-start | bytes 196616 | tf_op jit(solution)/shard_map/ppermute | solution.py:234
  31.9 2.0 %copy-start = (bf16[512,3584]{1,0:T(8,128)(2,1)S(1)}, bf16[512,3584]{1,0:T(8,128)(2,1)}, u32[]{:S(2)}) copy-start(bf16[512,3584]{1,0:T(8,128)(2,1)} %grad_ref.5) | copy-start | bytes 11010052
  34.0 1.2 %copy-start.2 = (bf16[512,1024]{1,0:T(8,128)(2,1)S(1)}, bf16[512,1024]{1,0:T(8,128)(2,1)}, u32[]{:S(2)}) copy-start(bf16[512,1024]{1,0:T(8,128)(2,1)} %act_ref.5) | copy-start | bytes 3145732
  35.2 0.9 copy-start.3
  36.1 0.8 copy-start.4
  39.5 20.9 %copy-start.5 = (f32[2]{0:T(128)S(1)}, f32[2]{0:T(128)}, u32[]{:S(2)}) copy-start(f32[2]{0:T(128)} %constant.11.clone) | copy-start | bytes 28
  39.5 22.2 %copy-start.1 = (bf16[512,3584]{1,0:T(8,128)(2,1)S(1)}, bf16[512,3584]{1,0:T(8,128)(2,1)}, u32[]{:S(2)}) copy-start(bf16[512,3584]{1,0:T(8,128)(2,1)} %grad_ref.5) | copy-start | bytes 11010052
  39.5 13.1 %collective-permute-start.11 = (f32[4,9,128]{2,1,0:T(8,128)S(1)}, f32[4,9,128]{2,1,0:T(8,128)S(1)}, u32[]{:S(2)}, u32[]{:S(2)}) collective-permute-start(f32[4,9,128]{2,1,0:T(8,128)S(1)} %partial_eigen.1), channel_id=1, source_target_pairs={{0,12},{4,0},{8,4},{12,8},{1,13},{5,1},{9,5},{13,9},{2,14},{6,2},{... | collective-permute-start | bytes 55304 | tf_op jit(solution)/shard_map/ppermute | solution.py:234
  39.6 13.1 %collective-permute-start.10 = (f32[4,9,128]{2,1,0:T(8,128)S(1)}, f32[4,9,128]{2,1,0:T(8,128)S(1)}, u32[]{:S(2)}, u32[]{:S(2)}) collective-permute-start(f32[4,9,128]{2,1,0:T(8,128)S(1)} %partial_eigen.1), channel_id=1, source_target_pairs={{0,8},{4,12},{8,0},{12,4},{1,9},{5,13},{9,1},{13,5},{2,10},{6,14},... | collective-permute-start | bytes 55304 | tf_op jit(solution)/shard_map/ppermute | solution.py:234
  43.1 9.6 %collective-permute-start.9 = (f32[4,9,128]{2,1,0:T(8,128)S(1)}, f32[4,9,128]{2,1,0:T(8,128)S(1)}, u32[]{:S(2)}, u32[]{:S(2)}) collective-permute-start(f32[4,9,128]{2,1,0:T(8,128)S(1)} %partial_eigen.1), channel_id=1, source_target_pairs={{0,4},{4,8},{8,12},{12,0},{1,5},{5,9},{9,13},{13,1},{2,6},{6,10},{... | collective-permute-start | bytes 55304 | tf_op jit(solution)/shard_map/ppermute | solution.py:234
  48.9 39.4 %collective-permute-start = (f32[4,9,32,128]{3,2,1,0:T(8,128)}, f32[4,9,32,128]{3,2,1,0:T(8,128)S(1)}, u32[]{:S(2)}, u32[]{:S(2)}) collective-permute-start(f32[4,9,32,128]{3,2,1,0:T(8,128)} %get-tuple-element.12), channel_id=1, source_target_pairs={{0,4},{4,8},{8,12},{12,0},{1,5},{5,9},{9,13},{13,1},{2,6},{6,10},{... | collective-permute-start | bytes 1769480 | tf_op jit(solution)/shard_map/ppermute | solution.py:234
  48.9 47.7 %collective-permute-start.1 = (f32[4,9,32,128]{3,2,1,0:T(8,128)}, f32[4,9,32,128]{3,2,1,0:T(8,128)S(1)}, u32[]{:S(2)}, u32[]{:S(2)}) collective-permute-start(f32[4,9,32,128]{3,2,1,0:T(8,128)} %get-tuple-element.13), channel_id=1, source_target_pairs={{0,8},{4,12},{8,0},{12,4},{1,9},{5,13},{9,1},{13,5},{2,10},{6,14},... | collective-permute-start | bytes 1769480 | tf_op jit(solution)/shard_map/ppermute | solution.py:234
  52.6 47.1 %collective-permute-start.2 = (f32[4,9,32,128]{3,2,1,0:T(8,128)}, f32[4,9,32,128]{3,2,1,0:T(8,128)S(1)}, u32[]{:S(2)}, u32[]{:S(2)}) collective-permute-start(f32[4,9,32,128]{3,2,1,0:T(8,128)} %get-tuple-element.14), channel_id=1, source_target_pairs={{0,12},{4,0},{8,4},{12,8},{1,13},{5,1},{9,5},{13,9},{2,14},{6,2},{... | collective-permute-start | bytes 1769480 | tf_op jit(solution)/shard_map/ppermute | solution.py:234
  55.9 1.3 %collective-permute-start.14 = (f32[2]{0:T(128)S(1)}, f32[2]{0:T(128)S(1)}, u32[]{:S(2)}, u32[]{:S(2)}) collective-permute-start(f32[2]{0:T(128)S(1)} %pad_maximum_fusion), channel_id=1, source_target_pairs={{0,3},{1,0},{2,1},{3,2},{4,7},{5,4},{6,5},{7,6},{8,11},{9,8},{10,9... | collective-permute-start | bytes 32 | tf_op jit(solution)/shard_map/ppermute | solution.py:234
  55.9 3.6 %collective-permute-start.13 = (f32[2]{0:T(128)S(1)}, f32[2]{0:T(128)S(1)}, u32[]{:S(2)}, u32[]{:S(2)}) collective-permute-start(f32[2]{0:T(128)S(1)} %pad_maximum_fusion), channel_id=1, source_target_pairs={{0,2},{1,3},{2,0},{3,1},{4,6},{5,7},{6,4},{7,5},{8,10},{9,11},{10,... | collective-permute-start | bytes 32 | tf_op jit(solution)/shard_map/ppermute | solution.py:234
  57.2 3.2 %collective-permute-start.12 = (f32[2]{0:T(128)S(1)}, f32[2]{0:T(128)S(1)}, u32[]{:S(2)}, u32[]{:S(2)}) collective-permute-start(f32[2]{0:T(128)S(1)} %pad_maximum_fusion), channel_id=1, source_target_pairs={{0,1},{1,2},{2,3},{3,0},{4,5},{5,6},{6,7},{7,4},{8,9},{9,10},{10,1... | collective-permute-start | bytes 32 | tf_op jit(solution)/shard_map/ppermute | solution.py:234
  65.2 1.3 %collective-permute-start.17 = (f32[2,512]{1,0:T(2,128)S(1)}, f32[2,512]{1,0:T(2,128)S(1)}, u32[]{:S(2)}, u32[]{:S(2)}) collective-permute-start(f32[2,512]{1,0:T(2,128)S(1)} %partial_weights.1), channel_id=1, source_target_pairs={{0,3},{1,0},{2,1},{3,2},{4,7},{5,4},{6,5},{7,6},{8,11},{9,8},{10,9... | collective-permute-start | bytes 12296 | tf_op jit(solution)/shard_map/ppermute | solution.py:234
  65.2 3.7 %collective-permute-start.16 = (f32[2,512]{1,0:T(2,128)S(1)}, f32[2,512]{1,0:T(2,128)S(1)}, u32[]{:S(2)}, u32[]{:S(2)}) collective-permute-start(f32[2,512]{1,0:T(2,128)S(1)} %partial_weights.1), channel_id=1, source_target_pairs={{0,2},{1,3},{2,0},{3,1},{4,6},{5,7},{6,4},{7,5},{8,10},{9,11},{10,... | collective-permute-start | bytes 12296 | tf_op jit(solution)/shard_map/ppermute | solution.py:234
  66.5 3.3 %collective-permute-start.15 = (f32[2,512]{1,0:T(2,128)S(1)}, f32[2,512]{1,0:T(2,128)S(1)}, u32[]{:S(2)}, u32[]{:S(2)}) collective-permute-start(f32[2,512]{1,0:T(2,128)S(1)} %partial_weights.1), channel_id=1, source_target_pairs={{0,1},{1,2},{2,3},{3,0},{4,5},{5,6},{6,7},{7,4},{8,9},{9,10},{10,1... | collective-permute-start | bytes 12296 | tf_op jit(solution)/shard_map/ppermute | solution.py:234

commit v2 on v0

v2 whole, which is shorter than its diff:
```python
import functools

import jax
import jax.numpy as jnp
from jax import lax
from jax.experimental import pallas as pl
from jax.experimental.pallas import tpu as pltpu
from jax.sharding import PartitionSpec as P

D = 4096
FF = 14336
BLK = 128
GROUP = 4
VMEM_LIMIT = 40 * 1024 * 1024
CODE_TOP = 2.0**7.875
SMALLEST = 1e-36

damp_root = 0.31622776601683794
contract_rows = (((0,), (0,)), ((), ()))
contract_inner = (((1,), (0,)), ((), ()))
contract_lanes = (((1,), (1,)), ((), ()))


def call(kernel, out_shape, name, flops, bytes_accessed, in_specs, scratch_shapes=()):
    return pl.pallas_call(
        kernel,
        out_shape=out_shape,
        in_specs=in_specs,
        out_specs=jax.tree.map(lambda _: pl.BlockSpec(memory_space=pltpu.VMEM), out_shape),
        scratch_shapes=scratch_shapes,
        compiler_params=pltpu.CompilerParams(vmem_limit_bytes=VMEM_LIMIT),
        cost_estimate=pl.CostEstimate(
            flops=flops, bytes_accessed=bytes_accessed, transcendentals=0
        ),
        name=name,
    )


def vmem(count):
    return [pl.BlockSpec(memory_space=pltpu.VMEM)] * count


def smem(count):
    return [pl.BlockSpec(memory_space=pltpu.SMEM)] * count


def f32(*shape):
    return jax.ShapeDtypeStruct(shape, jnp.float32)


def bf16(*shape):
    return jax.ShapeDtypeStruct(shape, jnp.bfloat16)


def over_blocks(act_ref, grad_ref, visit):
    first = 0
    for ref in (act_ref, grad_ref):
        blocks = ref.shape[1] // BLK

        @pl.loop(0, blocks // GROUP)
        def _(step, ref=ref, first=first):
            for offset in range(GROUP):
                block = step * GROUP + offset
                columns = pl.ds(pl.multiple_of(block * BLK, BLK), BLK)
                visit(ref, columns, first + block)

        first += blocks


def encode(values):
    power = values * values
    power = power * power
    power = power * power
    power = power * power
    return jnp.where(values < 0.0, -power, power).astype(jnp.bfloat16)


def decode(coded):
    coded = coded.astype(jnp.float32)
    root = jnp.abs(coded)
    for _ in range(4):
        root = lax.rsqrt(root)
    return jnp.where(coded > 0.0, root, jnp.where(coded < 0.0, -root, 0.0))


def gram_kernel(pieces, scale, me_ref, act_ref, grad_ref, own_ref, *refs):
    sent_refs, top_ref, whole = refs[: pieces - 1], refs[pieces - 1], refs[pieces]
    rows = BLK // pieces
    me = me_ref[0]

    def visit(ref, columns, block):
        values = ref[:, columns]
        gram = scale * lax.dot_general(
            values, values, contract_rows, preferred_element_type=jnp.float32
        )
        if pieces == 1:
            own_ref[block] = gram
            return
        slot = lax.rem(block, GROUP)
        whole[slot] = gram
        top = jnp.maximum(jnp.max(jnp.abs(gram), axis=0, keepdims=True), SMALLEST)
        top_ref[pl.ds(block, 1), :] = top * (1.0 / CODE_TOP)
        gain = CODE_TOP / top
        own_ref[block] = whole[slot, pl.ds(pl.multiple_of(me * rows, rows), rows), :]
        for shift in range(1, pieces):
            first = pl.multiple_of(lax.rem(me + shift, pieces) * rows, rows)
            sent_refs[shift - 1][block] = encode(whole[slot, pl.ds(first, rows), :] * gain)

    over_blocks(act_ref, grad_ref, visit)


def sum_kernel(blocks, me_ref, sums_ref, own_ref, *refs):
    sent_refs, (act_ref, grad_ref) = refs[:-2], refs[-2:]
    pieces = len(sent_refs) + 1
    me = me_ref[0]
    act_blocks = act_ref.shape[0]

    def total(block):
        value = own_ref[block]
        for shift in range(1, pieces):
            sender = lax.rem(me - shift + pieces, pieces)
            top = sums_ref[sender, pl.ds(blocks + block, 1), :]
            value = value + decode(sent_refs[shift - 1][block]) * top
        return value

    @pl.loop(0, act_blocks)
    def _(block):
        act_ref[block] = total(block)

    @pl.loop(0, blocks - act_blocks)
    def _(block):
        grad_ref[block] = total(act_blocks + block)


def eigen_kernel(pieces, scale, me_ref, side_ref, act_ref, grad_ref, top_ref, *refs):
    *shard_refs, basis_ref, sums_ref = refs
    act_blocks = act_ref.shape[1] // BLK
    blocks = act_blocks + grad_ref.shape[1] // BLK
    rows = BLK // pieces
    me, side = me_ref[0], side_ref[0]
    act_basis_ref, grad_basis_ref = shard_refs[:2]
    own = pl.ds(pl.multiple_of(me * rows, rows), rows)
    basis_ref[:act_blocks, own, :] = act_basis_ref[...]
    basis_ref[act_blocks:, own, :] = grad_basis_ref[...]
    received = shard_refs[2:]
    if received:
        halves = 2 if len(received) > pieces - 1 else 1
        act_half, grad_half = act_blocks // halves, (blocks - act_blocks) // halves
        for index, ref in enumerate(received):
            shift, other = index % (pieces - 1) + 1, index // (pieces - 1)
            half = (side + other) % halves if halves > 1 else 0
            place = pl.ds(pl.multiple_of(lax.rem(me - shift + pieces, pieces) * rows, rows), rows)
            basis_ref[pl.ds(half * act_half, act_half), place, :] = ref[:act_half]
            basis_ref[pl.ds(act_blocks + half * grad_half, grad_half), place, :] = ref[act_half:]

    def visit(ref, columns, block):
        projected = lax.dot_general(
            ref[:, columns], basis_ref[block], contract_inner, preferred_element_type=jnp.float32
        )
        sums_ref[pl.ds(block, 1), :] = scale * jnp.sum(
            projected * projected, axis=0, keepdims=True
        )

    over_blocks(act_ref, grad_ref, visit)
    sums_ref[blocks:, :] = top_ref[...]


def combine_kernel(sums_ref, act_eigen_ref, grad_eigen_ref, total_ref):
    act_blocks, grad_blocks = act_eigen_ref.shape[0], grad_eigen_ref.shape[0]
    blocks = act_blocks + grad_blocks
    eigen = jnp.sum(sums_ref[:, :blocks, :], axis=0)
    act_eigen_ref[...] = eigen[:act_blocks]
    grad_eigen_ref[...] = eigen[act_blocks:]
    total_ref[0:1, :] = jnp.sum(eigen[:act_blocks], axis=0, keepdims=True)
    total_ref[1:2, :] = jnp.sum(eigen[act_blocks:], axis=0, keepdims=True)


def weight_kernel(
    act_ref, grad_ref, basis_ref, act_eigen_ref, grad_eigen_ref, total_ref, weight_ref,
    inverse, act_sum, grad_sum,
):
    act_blocks = act_ref.shape[1] // BLK
    totals = jnp.sum(total_ref[...], axis=0)
    totals = jnp.sum(totals, axis=1, keepdims=True)
    inverse[:act_blocks] = 1.0 / (act_eigen_ref[...] + totals[0:1] * (damp_root / D))
    inverse[act_blocks:] = 1.0 / (grad_eigen_ref[...] + totals[1:2] * (damp_root / FF))
    act_sum[...] = jnp.zeros_like(act_sum)
    grad_sum[...] = jnp.zeros_like(grad_sum)

    def visit(ref, columns, block):
        total = act_sum if ref is act_ref else grad_sum
        projected = lax.dot_general(
            ref[:, columns], basis_ref[block], contract_inner, preferred_element_type=jnp.float32
        )
        total[...] += projected * projected * inverse[pl.ds(block, 1), :]

    over_blocks(act_ref, grad_ref, visit)
    ones = jnp.ones((8, BLK), jnp.float32)
    for index, total in enumerate((act_sum, grad_sum)):
        sums = lax.dot_general(
            ones,
            total[...],
            contract_lanes,
            precision=lax.Precision.HIGHEST,
            preferred_element_type=jnp.float32,
        )
        weight_ref[index : index + 1, :] = sums[0:1]


def score_kernel(weight_ref, score_ref):
    weights = jnp.sum(weight_ref[...], axis=0)
    score_ref[...] = weights[0:1] * weights[1:2] * (1.0 / (D * FF))


def half_kernel(side_ref, act_ref, grad_ref, half_ref):
    side = side_ref[0]
    act_half, grad_half = act_ref.shape[0] // 2, grad_ref.shape[0] // 2
    half_ref[:act_half] = act_ref[pl.ds(side * act_half, act_half)]
    half_ref[act_half:] = grad_ref[pl.ds(side * grad_half, grad_half)]


def rotate(value, axis, shift):
    count = lax.axis_size(axis)
    return lax.ppermute(value, axis, [(i, (i + shift) % count) for i in range(count)])


def gather_or_sum(value, axis, direct):
    if direct:
        return lax.all_gather(value, axis)
    return lax.psum(value, axis)[None]


def local(activations, gradients, basis_act, basis_grad):
    tokens = activations.shape[0]
    act_blocks, grad_blocks = basis_act.shape[0], basis_grad.shape[0]
    blocks = act_blocks + grad_blocks
    dp, groups = lax.axis_size("dp"), lax.axis_size("groups")
    scale = 1.0 / (tokens * dp)
    direct = dp > 1 and BLK // dp >= 32
    pieces = dp if direct else 1
    rows = BLK // pieces
    me = jnp.full((1,), lax.axis_index("dp") if direct else 0, jnp.int32)
    side = jnp.full((1,), lax.axis_index("groups"), jnp.int32)
    macs = tokens * blocks * BLK * BLK
    input_bytes = 2 * tokens * blocks * BLK

    if direct and groups == 2:
        half = call(
            half_kernel, bf16(blocks // 2, rows, BLK), "basis_half", 0, blocks * rows * BLK,
            smem(1) + vmem(2),
        )(side, basis_act, basis_grad)
        own_half = [rotate(half, "dp", shift) for shift in range(1, pieces)]
        other_half = [rotate(part, "groups", 1) for part in own_half]
        shards = [basis_act, basis_grad, *own_half, *other_half]
        first_received = own_half
    elif direct:
        both = jnp.concatenate([basis_act, basis_grad])
        received = [rotate(both, "dp", shift) for shift in range(1, pieces)]
        shards = [basis_act, basis_grad, *received]
        first_received = received
    else:
        shards = [
            lax.all_gather(basis_act, "dp", axis=1, tiled=True),
            lax.all_gather(basis_grad, "dp", axis=1, tiled=True),
        ]

    own, *sent, top = call(
        functools.partial(gram_kernel, pieces, scale),
        [
            f32(blocks, rows, BLK),
            *[bf16(blocks, rows, BLK)] * (pieces - 1),
            f32(blocks, BLK),
        ],
        "partial_gram", 4 * macs, input_bytes,
        smem(1) + vmem(2),
        [pltpu.VMEM((GROUP, BLK, BLK), jnp.float32)],
    )(me, activations, gradients)
    if direct:
        *sent, _ = lax.optimization_barrier((*sent, first_received))
        received = [rotate(part, "dp", shift + 1) for shift, part in enumerate(sent)]
    else:
        own = lax.psum_scatter(own, "dp", scatter_dimension=1, tiled=True)
        received = []

    basis, sums = call(
        functools.partial(eigen_kernel, pieces, scale),
        [bf16(blocks, BLK, BLK), f32(2 * blocks, BLK)],
        "partial_eigen", 2 * macs, input_bytes,
        smem(2) + vmem(3 + len(shards)),
    )(me, side, activations, gradients, top, *shards)
    sums = gather_or_sum(sums, "dp", direct)
    act_eigen, grad_eigen, totals = call(
        combine_kernel,
        [f32(act_blocks, BLK), f32(grad_blocks, BLK), f32(2, BLK)],
        "combine_eigen", 0, 4 * sums.size, vmem(1),
    )(sums)
    totals = gather_or_sum(totals, "owner", direct)
    weights = call(
        weight_kernel, f32(2, tokens), "partial_weights", 2 * macs, input_bytes, vmem(6),
        [
            pltpu.VMEM((blocks, BLK), jnp.float32),
            pltpu.VMEM((tokens, BLK), jnp.float32),
            pltpu.VMEM((tokens, BLK), jnp.float32),
        ],
    )(activations, gradients, basis, act_eigen, grad_eigen, totals)
    weights = gather_or_sum(weights, "owner", direct)
    token_scores = call(
        score_kernel, f32(1, tokens), "token_scores", 0, 4 * weights.size, vmem(1)
    )(weights)
    act_covariance, grad_covariance = call(
        functools.partial(sum_kernel, blocks),
        [f32(act_blocks, *own.shape[1:]), f32(grad_blocks, *own.shape[1:])],
        "sum_covariance", 0, 4 * own.size * pieces, smem(1) + vmem(2 + len(received)),
    )(me, sums, own, *received)
    return (
        act_covariance,
        grad_covariance,
        act_eigen.reshape(-1),
        grad_eigen.reshape(-1),
        token_scores.reshape(-1),
    )


def solution(mesh):
    return jax.shard_map(
        local,
        mesh=mesh,
        in_specs=(
            P(("groups", "dp"), "owner"),
            P(("groups", "dp"), "owner"),
            P("owner", "dp", None),
            P("owner", "dp", None),
        ),
        out_specs=(
            P(("groups", "owner"), "dp", None),
            P(("groups", "owner"), "dp", None),
            P(("groups", "owner")),
            P(("groups", "owner")),
            P(("groups", "dp")),
        ),
        check_vma=False,
    )
```

time: 135 us -> 83.2 us (0.62)
  blocking collectives: 79.8 us -> 37.3 us
  starting transfers between devices: 0.08 us -> 14.9 us
  between operations: 15.3 us -> 0.71 us
  matrix products: 13.9 us -> 0 us
  Pallas kernels: 0 us -> 13.5 us
  waiting for transfers between devices: 16.1 us -> 9.96 us
  other arithmetic: 1.8 us -> 0 us
    psum x3 -> x0, blocking collectives: 31.7 us -> none  [the longest x1 18.8 us: local(): lax.psum((partial_eigen(act_covariance, full_act, basis_act), partial_eig...]
    reduce_scatter x2 -> x0, waiting for transfers between devices: 16.1 us -> none  [the longest x1 16.1 us: local(): lax.psum_scatter(part_grad, 'dp', scatter_dimension=1, tiled=True)]
    ppermute x0 -> x9, starting transfers between devices: none -> 14.9 us  [rotate(): lax.ppermute(value, axis, [(i, (i + shift) % count) for i in range(count)])]
    dot_general x6 -> x0, matrix products: 13.9 us -> none  [the longest x1 5.56 us: local(): jnp.einsum('tni,tnj->nij', grad_blocks, grad_blocks, preferred_element_ty...]
    pallas_call x0 -> x7, Pallas kernels: none -> 13.5 us  [the longest x1 3.51 us: local(): call(functools.partial(gram_kernel, pieces, scale), [f32(blocks, rows, BL...]
    all_gather x2 -> x3, blocking collectives: 48.1 us -> 37.3 us  [gather_or_sum(): return lax.all_gather(value, axis)]
    ppermute x0 -> x9, waiting for transfers between devices: none -> 9.96 us  [rotate(): lax.ppermute(value, axis, [(i, (i + shift) % count) for i in range(count)])]
    unnamed x11 -> x20, local copies, waits for them, and re-layouts: 7.12 us -> 6.46 us
  transfers between devices with their start and end apart: 2 -> 9, of which waited for: 1 -> 2; matrix products, arithmetic and copies ran while one was open for 9% -> 0% of each run, Pallas kernels for 0% -> 13%
where the time goes in v2:
time: 83.2 us; the launch traced here: 82.8 us
  blocking collectives  37.3 us (45%)
  starting transfers between devices  14.9 us (18%)
  Pallas kernels  13.5 us (16%)
  waiting for transfers between devices  9.96 us (12%)
  local copies, waits for them, and re-layouts  6.46 us (8%)
    all_gather x3, blocking collectives, gather_or_sum(): return lax.all_gather(value, axis)  37.3 us
    ppermute x9, starting transfers between devices, rotate(): lax.ppermute(value, axis, [(i, (i + shift) % count) for i in range(count)])  14.9 us
    ppermute x9, waiting for transfers between devices, rotate(): lax.ppermute(value, axis, [(i, (i + shift) % count) for i in range(count)])  9.96 us
    unnamed x20, local copies, waits for them, and re-layouts  6.46 us
    pallas_call x1, Pallas kernels, local(): call(functools.partial(gram_kernel, pieces, scale), [f32(blocks, rows, BL...  3.51 us
    pallas_call x1, Pallas kernels, local(): call(weight_kernel, f32(2, tokens), 'partial_weights', 2 * macs, input_by...  3.25 us
    pallas_call x1, Pallas kernels, local(): call(functools.partial(eigen_kernel, pieces, scale), [bf16(blocks, BLK, B...  2.79 us
    pallas_call x1, Pallas kernels, local(): call(functools.partial(sum_kernel, blocks), [f32(act_blocks, *own.shape[1...  2.72 us
  transfers between devices with their start and end apart: 9, of which 2 were waited for; matrix products, arithmetic and copies ran while one was open for 0% of the time, Pallas kernels for 13%

profile of v2, /device:TPU:0, one launch (start us, length us, event | category | flops | bytes accessed | tf_op | source)
XLA Modules:
  0.0 82.8 jit_solution(141747900063243838)
XLA Ops:
  0.6 0.0 copy-start.4
  0.6 0.9 %copy-done.4 = bf16[28,32,128]{2,1,0:T(8,128)(2,1)S(1)} copy-done((bf16[28,32,128]{2,1,0:T(8,128)(2,1)S(1)}, bf16[28,32,128]{2,1,0:T(8,128)(2,1)}, u32[]{:S(2)}) %copy-start.4) | copy-done | bytes 229400
  1.6 0.0 copy-start.6
  1.6 0.8 %copy-done.6 = bf16[8,32,128]{2,1,0:T(8,128)(2,1)S(1)} copy-done((bf16[8,32,128]{2,1,0:T(8,128)(2,1)S(1)}, bf16[8,32,128]{2,1,0:T(8,128)(2,1)}, u32[]{:S(2)}) %copy-start.6) | copy-done | bytes 65560
  2.4 0.0 copy-start.5
  2.4 0.0 copy-start.7
  2.4 5.1 %collective-permute-start.2 = (bf16[18,32,128]{2,1,0:T(8,128)(2,1)S(1)}, bf16[18,32,128]{2,1,0:T(8,128)(2,1)S(1)}, u32[]{:S(2)}, u32[]{:S(2)}) collective-permute-start(bf16[18,32,128]{2,1,0:T(8,128)(2,1)S(1)} %basis_half.1), channel_id=1, source_target_pairs={{0,12},{4,0},{8,4},{12,8},{1,13},{5,1},{9,5},{13,9},{2,14},{6,2},{... | collective-permute-start | bytes 442376 | tf_op jit(solution)/shard_map/ppermute | solution.py:224
  7.5 0.0 collective-permute-start.1
  7.5 1.0 %collective-permute-start = (bf16[18,32,128]{2,1,0:T(8,128)(2,1)S(1)}, bf16[18,32,128]{2,1,0:T(8,128)(2,1)S(1)}, u32[]{:S(2)}, u32[]{:S(2)}) collective-permute-start(bf16[18,32,128]{2,1,0:T(8,128)(2,1)S(1)} %basis_half.1), channel_id=1, source_target_pairs={{0,4},{4,8},{8,12},{12,0},{1,5},{5,9},{9,13},{13,1},{2,6},{6,10},{... | collective-permute-start | bytes 442376 | tf_op jit(solution)/shard_map/ppermute | solution.py:224
  8.6 3.3 %collective-permute-done.2.refs_4_ = bf16[18,32,128]{2,1,0:T(8,128)(2,1)S(1)} collective-permute-done((bf16[18,32,128]{2,1,0:T(8,128)(2,1)S(1)}, bf16[18,32,128]{2,1,0:T(8,128)(2,1)S(1)}, u32[]{:S(2)}, u32[]{:S(2)}) %collective-permute-start.2) | collective-permute-done | bytes 147488 | tf_op jit(solution)/shard_map/ppermute | solution.py:224
  11.8 1.5 %collective-permute-start.5 = (bf16[18,32,128]{2,1,0:T(8,128)(2,1)S(1)}, bf16[18,32,128]{2,1,0:T(8,128)(2,1)S(1)}, u32[]{:S(2)}, u32[]{:S(2)}) collective-permute-start(bf16[18,32,128]{2,1,0:T(8,128)(2,1)S(1)} %collective-permute-done.2.refs_4_), channel_id=1, source_target_pairs={{0,16},{16,0},{1,17},{17,1},{2,18},{18,2},{3,19},{19,3},{4,20},{20... | collective-permute-start | bytes 442376 | tf_op jit(solution)/shard_map/ppermute | solution.py:224
  13.4 6.7 %collective-permute-done.1.refs_3_ = bf16[18,32,128]{2,1,0:T(8,128)(2,1)S(1)} collective-permute-done((bf16[18,32,128]{2,1,0:T(8,128)(2,1)S(1)}, bf16[18,32,128]{2,1,0:T(8,128)(2,1)S(1)}, u32[]{:S(2)}, u32[]{:S(2)}) %collective-permute-start.1) | collective-permute-done | bytes 147488 | tf_op jit(solution)/shard_map/ppermute | solution.py:224
  20.0 1.5 %collective-permute-start.4 = (bf16[18,32,128]{2,1,0:T(8,128)(2,1)S(1)}, bf16[18,32,128]{2,1,0:T(8,128)(2,1)S(1)}, u32[]{:S(2)}, u32[]{:S(2)}) collective-permute-start(bf16[18,32,128]{2,1,0:T(8,128)(2,1)S(1)} %collective-permute-done.1.refs_3_), channel_id=1, source_target_pairs={{0,16},{16,0},{1,17},{17,1},{2,18},{18,2},{3,19},{19,3},{4,20},{20... | collective-permute-start | bytes 442376 | tf_op jit(solution)/shard_map/ppermute | solution.py:224
  21.5 0.0 collective-permute-done.refs_2_
  21.5 0.5 collective-permute-start.3
  22.0 0.0 copy-start
  22.0 2.0 %copy-done = bf16[512,3584]{1,0:T(8,128)(2,1)S(1)} copy-done((bf16[512,3584]{1,0:T(8,128)(2,1)S(1)}, bf16[512,3584]{1,0:T(8,128)(2,1)}, u32[]{:S(2)}) %copy-start) | copy-done | bytes 3670040
  24.1 0.0 copy-start.2
  24.1 1.2 %copy-done.2 = bf16[512,1024]{1,0:T(8,128)(2,1)S(1)} copy-done((bf16[512,1024]{1,0:T(8,128)(2,1)S(1)}, bf16[512,1024]{1,0:T(8,128)(2,1)}, u32[]{:S(2)}) %copy-start.2) | copy-done | bytes 1048600
  25.3 3.5 %partial_gram.1 = (f32[36,32,128]{2,1,0:T(8,128)S(1)}, bf16[36,32,128]{2,1,0:T(8,128)(2,1)S(1)}, bf16[36,32,128]{2,1,0:T(8,128)(2,1)S(1)}, bf16[36,32,128]{2,1,0:T(8,128)(2,1)S(1)}, f32[36,128]{1,0:T(8,128)S(1)}) custom-call(s32[1]{0:T(128)} %bitcast.me_ref, bf16[512,1024]{1,0:T(8,128)(2,1)S(1)} %copy-done.2, bf16[512,3584]{1,0:T(8,128)(2,1)S(1)} %copy-done), custom_call_target="tpu_custom_call" | custom-call | flops 1207959552 | bytes 4718592 | tf_op jit(solution)/shard_map/partial_gram/pallas_call | solution.py:267
  28.8 0.0 copy-start.1
  28.8 0.0 copy-start.3
  28.9 0.4 collective-permute-start.6
  29.3 2.0 %collective-permute-start.7 = (bf16[36,32,128]{2,1,0:T(8,128)(2,1)S(1)}, bf16[36,32,128]{2,1,0:T(8,128)(2,1)S(1)}, u32[]{:S(2)}, u32[]{:S(2)}) collective-permute-start(bf16[36,32,128]{2,1,0:T(8,128)(2,1)S(1)} %get-tuple-element.27), channel_id=1, source_target_pairs={{0,8},{4,12},{8,0},{12,4},{1,9},{5,13},{9,1},{13,5},{2,10},{6,14},... | collective-permute-start | bytes 884744 | tf_op jit(solution)/shard_map/ppermute | solution.py:224
  31.3 0.0 collective-permute-done.5.refs_7_
  31.3 2.8 %collective-permute-start.8 = (bf16[36,32,128]{2,1,0:T(8,128)(2,1)S(1)}, bf16[36,32,128]{2,1,0:T(8,128)(2,1)S(1)}, u32[]{:S(2)}, u32[]{:S(2)}) collective-permute-start(bf16[36,32,128]{2,1,0:T(8,128)(2,1)S(1)} %get-tuple-element.28), channel_id=1, source_target_pairs={{0,12},{4,0},{8,4},{12,8},{1,13},{5,1},{9,5},{13,9},{2,14},{6,2},{... | collective-permute-start | bytes 884744 | tf_op jit(solution)/shard_map/ppermute | solution.py:224
  34.1 0.0 collective-permute-done.4.refs_6_
  34.1 0.0 collective-permute-done.3.refs_5_
  34.1 0.0 copy-done.5
  34.1 0.0 copy-done.7
  34.1 2.8 %partial_eigen.1 = (bf16[36,128,128]{2,1,0:T(8,128)(2,1)S(1)}, f32[72,128]{1,0:T(8,128)S(1)}) custom-call(s32[1]{0:T(128)} %bitcast.me_ref, s32[1]{0:T(128)} %bitcast.1.side_ref, bf16[512,1024]{1,0:T(8,128)(2,1)S(1)} %copy-done.2, bf16[512,3584]{1,0:T(8,128)(2,1)S(1)} %copy-done, f32[36,128]{1,0:T(8,128)S(1)} %get-tuple-element.20.top_ref, ...), custom_call_target="tpu_custom_call" | custom-call | flops 603979776 | bytes 4718592 | tf_op jit(solution)/shard_map/partial_eigen/pallas_call | solution.py:285
  36.9 27.0 %all-gather = f32[288,128]{1,0:T(8,128)S(1)} all-gather(f32[72,128]{1,0:T(8,128)S(1)} %get-tuple-element.21), channel_id=2, replica_groups=mesh['groups'=2,'dp'=4,'owner'=4] {'dp'}, dimensions={0}, use_global_device_ids=true | all-gather | bytes 184320 | tf_op jit(solution)/shard_map/all_gather | solution.py:229
  64.0 0.6 combine_eigen.1
  64.6 5.1 %all-gather.3.total_ref = f32[4,2,128]{2,1,0:T(2,128)S(1)} all-gather(f32[1,2,128]{2,1,0:T(2,128)S(1)} %bitcast.13), channel_id=3, replica_groups=mesh['groups'=2,'dp'=4,'owner'=4] {'owner'}, dimensions={0}, use_global_device_ids=true | all-gather | bytes 5120 | tf_op jit(solution)/shard_map/all_gather | solution.py:229
  69.7 0.0 copy-done.1
  69.7 0.0 copy-done.3
  69.7 0.0 copy-start.8
  69.7 0.7 copy-done.8
  70.4 0.0 copy-start.9
  70.4 0.7 copy-done.9
  71.1 3.2 %partial_weights.1 = f32[2,512]{1,0:T(2,128)S(1)} custom-call(bf16[512,1024]{1,0:T(8,128)(2,1)S(1)} %copy-done.3, bf16[512,3584]{1,0:T(8,128)(2,1)S(1)} %copy-done.1, bf16[36,128,128]{2,1,0:T(8,128)(2,1)S(1)} %get-tuple-element.33.basis_ref, f32[8,128]{1,0:T(8,128)S(1)} %copy-done.9, f32[28,128]{1,0:T(8,128)S(1)} %copy-done.8, ...), custom_call_target="tpu_custom_call" | custom-call | flops 603979776 | bytes 4718592 | tf_op jit(solution)/shard_map/partial_weights/pallas_call | solution.py:298
  74.3 5.2 %all-gather.4.weight_ref = f32[4,2,512]{2,1,0:T(2,128)S(1)} all-gather(f32[1,2,512]{2,1,0:T(2,128)S(1)} %bitcast.11), channel_id=4, replica_groups=mesh['groups'=2,'dp'=4,'owner'=4] {'owner'}, dimensions={0}, use_global_device_ids=true | all-gather | bytes 20480 | tf_op jit(solution)/shard_map/all_gather | solution.py:229
  79.5 0.6 token_scores.1
  80.1 0.0 collective-permute-done.6.refs_0_
  80.1 0.0 collective-permute-done.7.refs_1_
  80.1 0.0 collective-permute-done.8.refs_2_
  80.1 2.7 %sum_covariance.1 = (f32[8,32,128]{2,1,0:T(8,128)}, f32[28,32,128]{2,1,0:T(8,128)}) custom-call(s32[1]{0:T(128)} %bitcast.me_ref, f32[4,72,128]{2,1,0:T(8,128)S(1)} %bitcast.9, f32[36,32,128]{2,1,0:T(8,128)S(1)} %get-tuple-element.22.own_ref, bf16[36,32,128]{2,1,0:T(8,128)(2,1)S(1)} %collective-permute-done.6.refs_0_, ...), custom_call_target="tpu_custom_call" | custom-call | bytes 2359296 | tf_op jit(solution)/shard_map/sum_covariance/pallas_call | solution.py:310
  (1 shorter events, 0.0 us)
Async XLA Ops:
  0.6 0.9 %copy-start.4 = (bf16[28,32,128]{2,1,0:T(8,128)(2,1)S(1)}, bf16[28,32,128]{2,1,0:T(8,128)(2,1)}, u32[]{:S(2)}) copy-start(bf16[28,32,128]{2,1,0:T(8,128)(2,1)} %refs_1_.1) | copy-start | bytes 688132
  1.6 0.8 %copy-start.6 = (bf16[8,32,128]{2,1,0:T(8,128)(2,1)S(1)}, bf16[8,32,128]{2,1,0:T(8,128)(2,1)}, u32[]{:S(2)}) copy-start(bf16[8,32,128]{2,1,0:T(8,128)(2,1)} %refs_0_.1) | copy-start | bytes 196612
  2.4 31.7 %copy-start.5 = (bf16[28,32,128]{2,1,0:T(8,128)(2,1)S(1)}, bf16[28,32,128]{2,1,0:T(8,128)(2,1)}, u32[]{:S(2)}) copy-start(bf16[28,32,128]{2,1,0:T(8,128)(2,1)} %refs_1_.1) | copy-start | bytes 688132
  2.4 31.7 %copy-start.7 = (bf16[8,32,128]{2,1,0:T(8,128)(2,1)S(1)}, bf16[8,32,128]{2,1,0:T(8,128)(2,1)}, u32[]{:S(2)}) copy-start(bf16[8,32,128]{2,1,0:T(8,128)(2,1)} %refs_0_.1) | copy-start | bytes 196612
  2.4 9.4 %collective-permute-start.2 = (bf16[18,32,128]{2,1,0:T(8,128)(2,1)S(1)}, bf16[18,32,128]{2,1,0:T(8,128)(2,1)S(1)}, u32[]{:S(2)}, u32[]{:S(2)}) collective-permute-start(bf16[18,32,128]{2,1,0:T(8,128)(2,1)S(1)} %basis_half.1), channel_id=1, source_target_pairs={{0,12},{4,0},{8,4},{12,8},{1,13},{5,1},{9,5},{13,9},{2,14},{6,2},{... | collective-permute-start | bytes 442376 | tf_op jit(solution)/shard_map/ppermute | solution.py:224
  7.5 12.5 %collective-permute-start.1 = (bf16[18,32,128]{2,1,0:T(8,128)(2,1)S(1)}, bf16[18,32,128]{2,1,0:T(8,128)(2,1)S(1)}, u32[]{:S(2)}, u32[]{:S(2)}) collective-permute-start(bf16[18,32,128]{2,1,0:T(8,128)(2,1)S(1)} %basis_half.1), channel_id=1, source_target_pairs={{0,8},{4,12},{8,0},{12,4},{1,9},{5,13},{9,1},{13,5},{2,10},{6,14},... | collective-permute-start | bytes 442376 | tf_op jit(solution)/shard_map/ppermute | solution.py:224
  7.5 14.0 %collective-permute-start = (bf16[18,32,128]{2,1,0:T(8,128)(2,1)S(1)}, bf16[18,32,128]{2,1,0:T(8,128)(2,1)S(1)}, u32[]{:S(2)}, u32[]{:S(2)}) collective-permute-start(bf16[18,32,128]{2,1,0:T(8,128)(2,1)S(1)} %basis_half.1), channel_id=1, source_target_pairs={{0,4},{4,8},{8,12},{12,0},{1,5},{5,9},{9,13},{13,1},{2,6},{6,10},{... | collective-permute-start | bytes 442376 | tf_op jit(solution)/shard_map/ppermute | solution.py:224
  11.8 19.4 %collective-permute-start.5 = (bf16[18,32,128]{2,1,0:T(8,128)(2,1)S(1)}, bf16[18,32,128]{2,1,0:T(8,128)(2,1)S(1)}, u32[]{:S(2)}, u32[]{:S(2)}) collective-permute-start(bf16[18,32,128]{2,1,0:T(8,128)(2,1)S(1)} %collective-permute-done.2.refs_4_), channel_id=1, source_target_pairs={{0,16},{16,0},{1,17},{17,1},{2,18},{18,2},{3,19},{19,3},{4,20},{20... | collective-permute-start | bytes 442376 | tf_op jit(solution)/shard_map/ppermute | solution.py:224
  20.0 14.1 %collective-permute-start.4 = (bf16[18,32,128]{2,1,0:T(8,128)(2,1)S(1)}, bf16[18,32,128]{2,1,0:T(8,128)(2,1)S(1)}, u32[]{:S(2)}, u32[]{:S(2)}) collective-permute-start(bf16[18,32,128]{2,1,0:T(8,128)(2,1)S(1)} %collective-permute-done.1.refs_3_), channel_id=1, source_target_pairs={{0,16},{16,0},{1,17},{17,1},{2,18},{18,2},{3,19},{19,3},{4,20},{20... | collective-permute-start | bytes 442376 | tf_op jit(solution)/shard_map/ppermute | solution.py:224
  21.5 12.6 %collective-permute-start.3 = (bf16[18,32,128]{2,1,0:T(8,128)(2,1)S(1)}, bf16[18,32,128]{2,1,0:T(8,128)(2,1)S(1)}, u32[]{:S(2)}, u32[]{:S(2)}) collective-permute-start(bf16[18,32,128]{2,1,0:T(8,128)(2,1)S(1)} %collective-permute-done.refs_2_), channel_id=1, source_target_pairs={{0,16},{16,0},{1,17},{17,1},{2,18},{18,2},{3,19},{19,3},{4,20},{20... | collective-permute-start | bytes 442376 | tf_op jit(solution)/shard_map/ppermute | solution.py:224
  22.0 2.0 %copy-start = (bf16[512,3584]{1,0:T(8,128)(2,1)S(1)}, bf16[512,3584]{1,0:T(8,128)(2,1)}, u32[]{:S(2)}) copy-start(bf16[512,3584]{1,0:T(8,128)(2,1)} %grad_ref.7) | copy-start | bytes 11010052
  24.1 1.2 %copy-start.2 = (bf16[512,1024]{1,0:T(8,128)(2,1)S(1)}, bf16[512,1024]{1,0:T(8,128)(2,1)}, u32[]{:S(2)}) copy-start(bf16[512,1024]{1,0:T(8,128)(2,1)} %act_ref.7) | copy-start | bytes 3145732
  28.8 40.8 %copy-start.1 = (bf16[512,3584]{1,0:T(8,128)(2,1)S(1)}, bf16[512,3584]{1,0:T(8,128)(2,1)}, u32[]{:S(2)}) copy-start(bf16[512,3584]{1,0:T(8,128)(2,1)} %grad_ref.7) | copy-start | bytes 11010052
  28.8 40.8 %copy-start.3 = (bf16[512,1024]{1,0:T(8,128)(2,1)S(1)}, bf16[512,1024]{1,0:T(8,128)(2,1)}, u32[]{:S(2)}) copy-start(bf16[512,1024]{1,0:T(8,128)(2,1)} %act_ref.7) | copy-start | bytes 3145732
  28.9 51.3 %collective-permute-start.6 = (bf16[36,32,128]{2,1,0:T(8,128)(2,1)S(1)}, bf16[36,32,128]{2,1,0:T(8,128)(2,1)S(1)}, u32[]{:S(2)}, u32[]{:S(2)}) collective-permute-start(bf16[36,32,128]{2,1,0:T(8,128)(2,1)S(1)} %get-tuple-element.26), channel_id=1, source_target_pairs={{0,4},{4,8},{8,12},{12,0},{1,5},{5,9},{9,13},{13,1},{2,6},{6,10},{... | collective-permute-start | bytes 884744 | tf_op jit(solution)/shard_map/ppermute | solution.py:224
  29.3 50.8 %collective-permute-start.7 = (bf16[36,32,128]{2,1,0:T(8,128)(2,1)S(1)}, bf16[36,32,128]{2,1,0:T(8,128)(2,1)S(1)}, u32[]{:S(2)}, u32[]{:S(2)}) collective-permute-start(bf16[36,32,128]{2,1,0:T(8,128)(2,1)S(1)} %get-tuple-element.27), channel_id=1, source_target_pairs={{0,8},{4,12},{8,0},{12,4},{1,9},{5,13},{9,1},{13,5},{2,10},{6,14},... | collective-permute-start | bytes 884744 | tf_op jit(solution)/shard_map/ppermute | solution.py:224
  31.3 48.8 %collective-permute-start.8 = (bf16[36,32,128]{2,1,0:T(8,128)(2,1)S(1)}, bf16[36,32,128]{2,1,0:T(8,128)(2,1)S(1)}, u32[]{:S(2)}, u32[]{:S(2)}) collective-permute-start(bf16[36,32,128]{2,1,0:T(8,128)(2,1)S(1)} %get-tuple-element.28), channel_id=1, source_target_pairs={{0,12},{4,0},{8,4},{12,8},{1,13},{5,1},{9,5},{13,9},{2,14},{6,2},{... | collective-permute-start | bytes 884744 | tf_op jit(solution)/shard_map/ppermute | solution.py:224
  69.7 0.7 copy-start.8
  70.4 0.7 copy-start.9

commit v3 on v0

v3 whole, which is shorter than its diff:
```python
import functools

import jax
import jax.numpy as jnp
from jax import lax
from jax.experimental import pallas as pl
from jax.experimental.pallas import tpu as pltpu
from jax.sharding import PartitionSpec as P

D = 4096
FF = 14336
BLK = 128
PAIR = 2 * BLK
GROUP = 4
VMEM_LIMIT = 40 * 1024 * 1024
CODE_TOP = 2.0**7.875
SMALLEST = 1e-36

damp_root = 0.31622776601683794
contract_rows = (((0,), (0,)), ((), ()))
contract_inner = (((1,), (0,)), ((), ()))
contract_lanes = (((1,), (1,)), ((), ()))

IN_VMEM = pl.BlockSpec(memory_space=pltpu.VMEM)
IN_SMEM = pl.BlockSpec(memory_space=pltpu.SMEM)
IN_HBM = pl.BlockSpec(memory_space=pltpu.HBM)


def call(
    kernel, out_shape, name, flops, bytes_accessed, in_specs, scratch_shapes=(), limit=VMEM_LIMIT
):
    return pl.pallas_call(
        kernel,
        out_shape=out_shape,
        in_specs=in_specs,
        out_specs=jax.tree.map(lambda _: IN_VMEM, out_shape),
        scratch_shapes=scratch_shapes,
        compiler_params=pltpu.CompilerParams(vmem_limit_bytes=limit),
        cost_estimate=pl.CostEstimate(
            flops=flops, bytes_accessed=bytes_accessed, transcendentals=0
        ),
        name=name,
    )


def f32(*shape):
    return jax.ShapeDtypeStruct(shape, jnp.float32)


def bf16(*shape):
    return jax.ShapeDtypeStruct(shape, jnp.bfloat16)


def encode(values):
    power = values * values
    power = power * power
    power = power * power
    power = power * power
    return jnp.where(values < 0.0, -power, power).astype(jnp.bfloat16)


def decode(coded):
    coded = coded.astype(jnp.float32)
    root = jnp.abs(coded)
    for _ in range(4):
        root = lax.rsqrt(root)
    return jnp.where(coded > 0.0, root, jnp.where(coded < 0.0, -root, 0.0))


def half_kernel(side_ref, act_ref, grad_ref, half_ref, sems):
    side = side_ref[0]
    act_half, grad_half = act_ref.shape[0] // 2, grad_ref.shape[0] // 2
    copies = [
        pltpu.make_async_copy(
            act_ref.at[pl.ds(side * act_half, act_half)],
            half_ref.at[pl.ds(0, act_half)],
            sems.at[0],
        ),
        pltpu.make_async_copy(
            grad_ref.at[pl.ds(side * grad_half, grad_half)],
            half_ref.at[pl.ds(act_half, grad_half)],
            sems.at[1],
        ),
    ]
    for copy in copies:
        copy.start()
    for copy in copies:
        copy.wait()


def gram_kernel(pieces, scale, me_ref, act_ref, grad_ref, own_ref, *refs):
    sent_refs, (whole, tops) = refs[:-2], refs[-2:]
    rows = BLK // pieces
    me = me_ref[0]
    first = 0
    tops[...] = jnp.zeros_like(tops)
    for ref in (act_ref, grad_ref):

        @pl.loop(0, ref.shape[1] // BLK // GROUP)
        def _(step, ref=ref, first=first):
            for offset in range(GROUP):
                block = first + step * GROUP + offset
                at = pl.multiple_of((step * GROUP + offset) * BLK, BLK)
                values = ref[:, pl.ds(at, BLK)]
                gram = scale * lax.dot_general(
                    values, values, contract_rows, preferred_element_type=jnp.float32
                )
                if pieces == 1:
                    own_ref[block] = gram
                    continue
                whole[offset] = gram
                top = jnp.maximum(jnp.max(jnp.abs(gram), axis=0, keepdims=True), SMALLEST)
                top = (top * (1.0 + 2.0**-8)).astype(jnp.bfloat16).astype(jnp.float32)
                tops[pl.ds(block, 1), :] = top
                gain = CODE_TOP / top
                own_ref[block] = whole[offset, pl.ds(pl.multiple_of(me * rows, rows), rows), :]
                for shift in range(1, pieces):
                    row = pl.multiple_of(lax.rem(me + shift, pieces) * rows, rows)
                    place = pl.multiple_of(block * rows, rows)
                    sent_refs[shift - 1][pl.ds(place, rows), :] = encode(
                        whole[offset, pl.ds(row, rows), :] * gain
                    )

        first += ref.shape[1] // BLK
    for sent_ref in sent_refs:
        sent_ref[first * rows :, :] = tops[...].astype(jnp.bfloat16)


def add_kernel(own_ref, sent_ref, *refs):
    out_refs, tops = refs[:-1], refs[-1]
    blocks, rows, _ = own_ref.shape
    tops[...] = sent_ref[blocks * rows :, :].astype(jnp.float32) * (1.0 / CODE_TOP)
    first = 0
    for out_ref in out_refs:

        @pl.loop(0, out_ref.shape[0] // GROUP)
        def _(step, out_ref=out_ref, first=first):
            for offset in range(GROUP):
                at = step * GROUP + offset
                block = first + at
                place = pl.multiple_of(block * rows, rows)
                values = decode(sent_ref[pl.ds(place, rows), :])
                out_ref[at] = own_ref[block] + values * tops[pl.ds(block, 1), :]

        first += out_ref.shape[0]


def pairs_of(part, side, halves, act_ref, grad_ref):
    half = lax.rem(side + part, halves)
    for ref in (act_ref, grad_ref):
        count = ref.shape[1] // PAIR // halves
        for pair in range(count):
            yield ref, pl.multiple_of((half * count + pair) * PAIR, PAIR)


def eigen_kernel(
    part, halves, pieces, scale, me_ref, side_ref, act_ref, grad_ref, act_own, grad_own, *refs
):
    *received, basis_ref, sums_ref = refs
    me, side = me_ref[0], side_ref[0]
    rows = BLK // pieces
    done = 0
    if part:
        *received, done_ref = received
        done = done_ref.shape[0]
        sums_ref[:done] = done_ref[...]
    half = lax.rem(side + part, halves)
    act_half, grad_half = act_own.shape[0] // halves, grad_own.shape[0] // halves
    basis_ref[...] = jnp.zeros_like(basis_ref)

    def put(shard_of, piece):
        for block in range(act_half + grad_half):
            corner = block % 2
            row = pl.multiple_of(corner * BLK + piece * rows, rows)
            columns = slice(corner * BLK, (corner + 1) * BLK)
            basis_ref[block // 2, pl.ds(row, rows), columns] = shard_of(block)

    def own_shard(block):
        if block < act_half:
            return act_own[half * act_half + block]
        return grad_own[half * grad_half + block - act_half]

    put(own_shard, me)
    for index, ref in enumerate(received):
        put(lambda block, ref=ref: ref[block], lax.rem(me - index - 1 + pieces, pieces))

    for pair, (ref, column) in enumerate(pairs_of(part, side, halves, act_ref, grad_ref)):
        projected = lax.dot_general(
            ref[:, pl.ds(column, PAIR)],
            basis_ref[pair],
            contract_inner,
            preferred_element_type=jnp.float32,
        )
        sums = scale * jnp.sum(projected * projected, axis=0, keepdims=True)
        row = done + 2 * pair
        sums_ref[row : row + 1, :] = sums[:, :BLK]
        sums_ref[row + 1 : row + 2, :] = sums[:, BLK:]


def combine_kernel(halves, side_ref, sums_ref, act_eigen_ref, grad_eigen_ref, eigen_ref, total_ref):
    side = side_ref[0]
    act_half, grad_half = act_eigen_ref.shape[0] // halves, grad_eigen_ref.shape[0] // halves
    eigen = jnp.sum(sums_ref[...], axis=0)
    eigen_ref[...] = eigen
    act_total = jnp.zeros((1, BLK), jnp.float32)
    grad_total = jnp.zeros((1, BLK), jnp.float32)
    for part in range(halves):
        half = lax.rem(side + part, halves)
        first = part * (act_half + grad_half)
        act = eigen[first : first + act_half]
        grad = eigen[first + act_half : first + act_half + grad_half]
        act_total += jnp.sum(act, axis=0, keepdims=True)
        grad_total += jnp.sum(grad, axis=0, keepdims=True)
        act_eigen_ref[pl.ds(half * act_half, act_half), :] = act
        grad_eigen_ref[pl.ds(half * grad_half, grad_half), :] = grad
    for copy in range(total_ref.shape[0]):
        total_ref[copy, 0:1, :] = act_total
        total_ref[copy, 1:2, :] = grad_total


def weight_kernel(halves, side_ref, act_ref, grad_ref, eigen_ref, total_ref, *refs):
    *basis_refs, weight_ref, inverse, act_sum, grad_sum = refs
    side = side_ref[0]
    totals = jnp.sum(total_ref[...], axis=0)
    totals = jnp.sum(totals, axis=1, keepdims=True)
    act_half = act_ref.shape[1] // BLK // halves
    grad_half = grad_ref.shape[1] // BLK // halves
    for part in range(halves):
        first = part * (act_half + grad_half)
        act = slice(first, first + act_half)
        grad = slice(first + act_half, first + act_half + grad_half)
        inverse[act] = 1.0 / (eigen_ref[act] + totals[0:1] * (damp_root / D))
        inverse[grad] = 1.0 / (eigen_ref[grad] + totals[1:2] * (damp_root / FF))
    act_sum[...] = jnp.zeros_like(act_sum)
    grad_sum[...] = jnp.zeros_like(grad_sum)
    for part in range(halves):
        first = part * (act_half + grad_half)
        for pair, (ref, column) in enumerate(pairs_of(part, side, halves, act_ref, grad_ref)):
            total = act_sum if ref is act_ref else grad_sum
            projected = lax.dot_general(
                ref[:, pl.ds(column, PAIR)],
                basis_refs[part][pair],
                contract_inner,
                preferred_element_type=jnp.float32,
            )
            row = first + 2 * pair
            left, right = projected[:, :BLK], projected[:, BLK:]
            total[...] += (
                left * left * inverse[row : row + 1, :]
                + right * right * inverse[row + 1 : row + 2, :]
            )
    ones = jnp.ones((8, BLK), jnp.float32)
    for index, total in enumerate((act_sum, grad_sum)):
        sums = lax.dot_general(
            ones,
            total[...],
            contract_lanes,
            precision=lax.Precision.HIGHEST,
            preferred_element_type=jnp.float32,
        )
        weight_ref[index : index + 1, :] = sums[0:1]


def score_kernel(weight_ref, score_ref):
    weights = jnp.sum(weight_ref[...], axis=0)
    score_ref[...] = weights[0:1] * weights[1:2] * (1.0 / (D * FF))


def rotate(value, axis, shift):
    count = lax.axis_size(axis)
    return lax.ppermute(value, axis, [(i, (i + shift) % count) for i in range(count)])


def gather_or_sum(value, axis, direct):
    if direct:
        return lax.all_gather(value, axis)
    return lax.psum(value, axis)[None]


def after(values, done):
    return list(lax.optimization_barrier((tuple(values), done))[0])


def local(activations, gradients, basis_act, basis_grad):
    tokens = activations.shape[0]
    act_blocks, grad_blocks = basis_act.shape[0], basis_grad.shape[0]
    blocks = act_blocks + grad_blocks
    dp, owners = lax.axis_size("dp"), lax.axis_size("owner")
    scale = 1.0 / (tokens * dp)
    direct = dp > 1 and BLK // dp >= 32
    pieces = dp if direct else 1
    halves = 2 if direct and lax.axis_size("groups") == 2 else 1
    rows = BLK // pieces
    me = jnp.full((1,), lax.axis_index("dp") if direct else 0, jnp.int32)
    side = jnp.full((1,), lax.axis_index("groups"), jnp.int32)
    macs = tokens * blocks * BLK * BLK
    input_bytes = 2 * tokens * blocks * BLK
    shifts = range(1, pieces)

    if halves == 2:
        shard = call(
            half_kernel, bf16(blocks // 2, rows, BLK), "basis_half", 0, blocks * rows * BLK,
            [IN_SMEM, IN_HBM, IN_HBM], [pltpu.SemaphoreType.DMA((2,))], 62 * 1024 * 1024,
        )(side, basis_act, basis_grad)
    elif direct:
        shard = jnp.concatenate([basis_act, basis_grad])
    if direct:
        ways = sorted(shifts, key=lambda shift: -min(shift, pieces - shift))
        received = {shift: rotate(shard, "dp", shift) for shift in ways}
        received = [received[shift] for shift in shifts]
    else:
        basis_act = lax.all_gather(basis_act, "dp", axis=1, tiled=True)
        basis_grad = lax.all_gather(basis_grad, "dp", axis=1, tiled=True)
        received = []

    message = blocks * rows + 16 * pl.cdiv(blocks, 16)
    own, *sent = call(
        functools.partial(gram_kernel, pieces, scale),
        [f32(blocks, rows, BLK), *[bf16(message, BLK)] * (pieces - 1)],
        "partial_gram", 4 * macs, input_bytes,
        [IN_SMEM, IN_VMEM, IN_VMEM],
        [
            pltpu.VMEM((GROUP, BLK, BLK), jnp.float32),
            pltpu.VMEM((16 * pl.cdiv(blocks, 16), BLK), jnp.float32),
        ],
    )(me, activations, gradients)
    arrived = []
    if direct:
        arrived.append(rotate(sent[0], "dp", 1))
    else:
        own = lax.psum_scatter(own, "dp", scatter_dimension=1, tiled=True)

    parts = [received]
    if halves == 2:
        parts.append([rotate(after([part], own)[0], "groups", 1) for part in received])
    bases, sums = [], []
    for part, shards in enumerate(parts):
        basis, *sums = call(
            functools.partial(eigen_kernel, part, halves, pieces, scale),
            [bf16(blocks // halves // 2, PAIR, PAIR), f32(blocks // halves * (part + 1), BLK)],
            "partial_eigen", 2 * macs // halves, input_bytes // halves,
            [IN_SMEM, IN_SMEM] + [IN_VMEM] * (4 + len(shards) + len(sums)),
        )(me, side, activations, gradients, basis_act, basis_grad, *shards, *sums)
        bases.append(basis)
    sums = after(sums, arrived)
    sums = gather_or_sum(sums[0], "dp", direct)
    if direct:
        sent[1:] = after(sent[1:], sums)
        for shift in shifts[1:]:
            arrived.append(rotate(sent[shift - 1], "dp", shift))

    copies = owners if direct else 1
    act_eigen, grad_eigen, eigen, totals = call(
        functools.partial(combine_kernel, halves),
        [
            f32(act_blocks, BLK),
            f32(grad_blocks, BLK),
            f32(blocks, BLK),
            f32(copies, 2, BLK),
        ],
        "combine_eigen", 0, 4 * sums.size, [IN_SMEM, IN_VMEM],
    )(side, sums)
    if direct:
        totals = lax.all_to_all(totals, "owner", 0, 0, tiled=True)
    else:
        totals = lax.psum(totals, "owner")
    weights = call(
        functools.partial(weight_kernel, halves),
        f32(2, tokens), "partial_weights", 2 * macs, input_bytes,
        [IN_SMEM] + [IN_VMEM] * (4 + halves),
        [
            pltpu.VMEM((blocks, BLK), jnp.float32),
            pltpu.VMEM((tokens, BLK), jnp.float32),
            pltpu.VMEM((tokens, BLK), jnp.float32),
        ],
    )(side, activations, gradients, eigen, totals, *bases)
    weights = gather_or_sum(weights, "owner", direct)
    token_scores = call(
        score_kernel, f32(1, tokens), "token_scores", 0, 4 * weights.size, [IN_VMEM]
    )(weights)

    covariance = own
    for index, chunk in enumerate(arrived):
        last = index == len(arrived) - 1
        shape = own.shape[1:]
        covariance = call(
            add_kernel,
            [f32(act_blocks, *shape), f32(grad_blocks, *shape)] if last else [f32(*own.shape)],
            "add_chunk", 0, 10 * own.size, [IN_VMEM, IN_VMEM],
            [pltpu.VMEM((message - blocks * rows, BLK), jnp.float32)],
        )(covariance, chunk)
        covariance = covariance if last else covariance[0]
    if not arrived:
        covariance = covariance[:act_blocks], covariance[act_blocks:]
    return (
        *covariance,
        act_eigen.reshape(-1),
        grad_eigen.reshape(-1),
        token_scores.reshape(-1),
    )


def solution(mesh):
    return jax.shard_map(
        local,
        mesh=mesh,
        in_specs=(
            P(("groups", "dp"), "owner"),
            P(("groups", "dp"), "owner"),
            P("owner", "dp", None),
            P("owner", "dp", None),
        ),
        out_specs=(
            P(("groups", "owner"), "dp", None),
            P(("groups", "owner"), "dp", None),
            P(("groups", "owner")),
            P(("groups", "owner")),
            P(("groups", "dp")),
        ),
        check_vma=False,
    )
```

time: 135 us -> 76 us (0.56)
  blocking collectives: 79.8 us -> 18.8 us
  starting transfers between devices: 0.08 us -> 17.3 us
  Pallas kernels: 0 us -> 15.3 us
  between operations: 15.3 us -> 0.73 us
  matrix products: 13.9 us -> 0 us
  local copies, waits for them, and re-layouts: 7.12 us -> 9.29 us
  waiting for transfers between devices: 16.1 us -> 14.1 us
  other arithmetic: 1.8 us -> 0 us
    psum x3 -> x0, blocking collectives: 31.7 us -> none  [the longest x1 18.8 us: local(): lax.psum((partial_eigen(act_covariance, full_act, basis_act), partial_eig...]
    all_gather x2, blocking collectives: 48.1 us -> 18.8 us  [gather_or_sum(): return lax.all_gather(value, axis)]
    reduce_scatter x2 -> x0, waiting for transfers between devices: 16.1 us -> none  [the longest x1 16.1 us: local(): lax.psum_scatter(part_grad, 'dp', scatter_dimension=1, tiled=True)]
    pallas_call x0 -> x10, Pallas kernels: none -> 15.3 us  [the longest x1 4.44 us: local(): call(functools.partial(gram_kernel, pieces, scale), [f32(blocks, rows, BL...]
    ppermute x0 -> x9, starting transfers between devices: none -> 14 us  [rotate(): lax.ppermute(value, axis, [(i, (i + shift) % count) for i in range(count)])]
    dot_general x6 -> x0, matrix products: 13.9 us -> none  [the longest x1 5.56 us: local(): jnp.einsum('tni,tnj->nij', grad_blocks, grad_blocks, preferred_element_ty...]
    ppermute x0 -> x9, waiting for transfers between devices: none -> 11.9 us  [rotate(): lax.ppermute(value, axis, [(i, (i + shift) % count) for i in range(count)])]
    all_to_all x0 -> x1, starting transfers between devices: none -> 3.25 us  [local(): totals = lax.all_to_all(totals, 'owner', 0, 0, tiled=True)]
  transfers between devices with their start and end apart: 2 -> 10, of which waited for: 1 -> 5; matrix products, arithmetic and copies ran while one was open for 9% -> 0% of each run, Pallas kernels for 0% -> 15%
where the time goes in v3:
time: 76 us; the launch traced here: 75.5 us
  blocking collectives  18.8 us (25%)
  starting transfers between devices  17.3 us (23%)
  Pallas kernels  15.3 us (20%)
  waiting for transfers between devices  14.1 us (19%)
  local copies, waits for them, and re-layouts  9.29 us (12%)
    all_gather x2, blocking collectives, gather_or_sum(): return lax.all_gather(value, axis)  18.8 us
    ppermute x9, starting transfers between devices, rotate(): lax.ppermute(value, axis, [(i, (i + shift) % count) for i in range(count)])  14 us
    ppermute x9, waiting for transfers between devices, rotate(): lax.ppermute(value, axis, [(i, (i + shift) % count) for i in range(count)])  11.9 us
    unnamed x20, local copies, waits for them, and re-layouts  9.29 us
    pallas_call x1, Pallas kernels, local(): call(functools.partial(gram_kernel, pieces, scale), [f32(blocks, rows, BL...  4.44 us
    pallas_call x3, Pallas kernels, local(): call(add_kernel, [f32(act_blocks, *shape), f32(grad_blocks, *shape)] if l...  4.4 us
    all_to_all x1, starting transfers between devices, local(): totals = lax.all_to_all(totals, 'owner', 0, 0, tiled=True)  3.25 us
    all_to_all x1, waiting for transfers between devices, local(): totals = lax.all_to_all(totals, 'owner', 0, 0, tiled=True)  2.21 us
  transfers between devices with their start and end apart: 10, of which 5 were waited for; matrix products, arithmetic and copies ran while one was open for 0% of the time, Pallas kernels for 15%

profile of v3, /device:TPU:0, one launch (start us, length us, event | category | flops | bytes accessed | tf_op | source)
XLA Modules:
  0.0 75.5 jit_solution(6310216457964196968)
XLA Ops:
  0.6 1.6 %basis_half.1 = bf16[18,32,128]{2,1,0:T(8,128)(2,1)} custom-call(s32[1]{0:T(128)} %bitcast.1.side_ref, bf16[8,32,128]{2,1,0:T(8,128)(2,1)} %act_own.3, bf16[28,32,128]{2,1,0:T(8,128)(2,1)} %grad_own.3), custom_call_target="tpu_custom_call" | custom-call | bytes 147456 | tf_op jit(solution)/shard_map/basis_half/pallas_call | solution.py:301
  2.2 5.1 %collective-permute-start.5 = (bf16[18,32,128]{2,1,0:T(8,128)(2,1)}, bf16[18,32,128]{2,1,0:T(8,128)(2,1)S(1)}, u32[]{:S(2)}, u32[]{:S(2)}) collective-permute-start(bf16[18,32,128]{2,1,0:T(8,128)(2,1)} %basis_half.1), channel_id=1, source_target_pairs={{0,12},{4,0},{8,4},{12,8},{1,13},{5,1},{9,5},{13,9},{2,14},{6,2},{... | collective-permute-start | bytes 442376 | tf_op jit(solution)/shard_map/ppermute | solution.py:271
  7.3 0.0 collective-permute-start.3
  7.3 1.0 %collective-permute-start.1 = (bf16[18,32,128]{2,1,0:T(8,128)(2,1)}, bf16[18,32,128]{2,1,0:T(8,128)(2,1)S(1)}, u32[]{:S(2)}, u32[]{:S(2)}) collective-permute-start(bf16[18,32,128]{2,1,0:T(8,128)(2,1)} %basis_half.1), channel_id=1, source_target_pairs={{0,4},{4,8},{8,12},{12,0},{1,5},{5,9},{9,13},{13,1},{2,6},{6,10},{... | collective-permute-start | bytes 442376 | tf_op jit(solution)/shard_map/ppermute | solution.py:271
  8.4 0.0 copy-start
  8.4 2.0 %copy-done = bf16[512,3584]{1,0:T(8,128)(2,1)S(1)} copy-done((bf16[512,3584]{1,0:T(8,128)(2,1)S(1)}, bf16[512,3584]{1,0:T(8,128)(2,1)}, u32[]{:S(2)}) %copy-start) | copy-done | bytes 3670040
  10.4 0.0 copy-start.2
  10.4 1.2 %copy-done.2 = bf16[512,1024]{1,0:T(8,128)(2,1)S(1)} copy-done((bf16[512,1024]{1,0:T(8,128)(2,1)S(1)}, bf16[512,1024]{1,0:T(8,128)(2,1)}, u32[]{:S(2)}) %copy-start.2) | copy-done | bytes 1048600
  11.6 0.0 copy-start.4
  11.6 0.0 copy-start.7
  11.6 4.4 %partial_gram.1 = (f32[36,32,128]{2,1,0:T(8,128)S(1)}, bf16[1200,128]{1,0:T(8,128)(2,1)S(1)}, bf16[1200,128]{1,0:T(8,128)(2,1)}, bf16[1200,128]{1,0:T(8,128)(2,1)}) custom-call(s32[1]{0:T(128)} %bitcast.me_ref, bf16[512,1024]{1,0:T(8,128)(2,1)S(1)} %copy-done.2, bf16[512,3584]{1,0:T(8,128)(2,1)S(1)} %copy-done), custom_call_target="tpu_custom_call" | custom-call | flops 1207959552 | bytes 4718592 | tf_op jit(solution)/shard_map/partial_gram/pallas_call | solution.py:317
  16.1 2.5 %collective-permute-start = (bf16[1200,128]{1,0:T(8,128)(2,1)S(1)}, bf16[1200,128]{1,0:T(8,128)(2,1)S(1)}, u32[]{:S(2)}, u32[]{:S(2)}) collective-permute-start(bf16[1200,128]{1,0:T(8,128)(2,1)S(1)} %get-tuple-element.26), channel_id=1, source_target_pairs={{0,4},{4,8},{8,12},{12,0},{1,5},{5,9},{9,13},{13,1},{2,6},{6,10},{... | collective-permute-start | bytes 921608 | tf_op jit(solution)/shard_map/ppermute | solution.py:271
  18.5 0.0 collective-permute-done.5.refs_2_
  18.5 8.1 %collective-permute-done.3.refs_1_ = bf16[18,32,128]{2,1,0:T(8,128)(2,1)S(1)} collective-permute-done((bf16[18,32,128]{2,1,0:T(8,128)(2,1)}, bf16[18,32,128]{2,1,0:T(8,128)(2,1)S(1)}, u32[]{:S(2)}, u32[]{:S(2)}) %collective-permute-start.3) | collective-permute-done | bytes 147488 | tf_op jit(solution)/shard_map/ppermute | solution.py:271
  26.6 0.0 collective-permute-done.1.refs_0_
  26.6 1.5 %collective-permute-start.2 = (bf16[18,32,128]{2,1,0:T(8,128)(2,1)S(1)}, bf16[18,32,128]{2,1,0:T(8,128)(2,1)S(1)}, u32[]{:S(2)}, u32[]{:S(2)}) collective-permute-start(bf16[18,32,128]{2,1,0:T(8,128)(2,1)S(1)} %collective-permute-done.1.refs_0_), channel_id=1, source_target_pairs={{0,16},{16,0},{1,17},{17,1},{2,18},{18,2},{3,19},{19,3},{4,20},{20... | collective-permute-start | bytes 442376 | tf_op jit(solution)/shard_map/ppermute | solution.py:271
  28.1 0.5 collective-permute-start.4
  28.6 1.5 %collective-permute-start.6 = (bf16[18,32,128]{2,1,0:T(8,128)(2,1)S(1)}, bf16[18,32,128]{2,1,0:T(8,128)(2,1)S(1)}, u32[]{:S(2)}, u32[]{:S(2)}) collective-permute-start(bf16[18,32,128]{2,1,0:T(8,128)(2,1)S(1)} %collective-permute-done.5.refs_2_), channel_id=1, source_target_pairs={{0,16},{16,0},{1,17},{17,1},{2,18},{18,2},{3,19},{19,3},{4,20},{20... | collective-permute-start | bytes 442376 | tf_op jit(solution)/shard_map/ppermute | solution.py:271
  30.2 0.0 copy-done.4
  30.2 0.0 copy-done.7
  30.2 0.9 %partial_eigen.2 = (bf16[9,256,256]{2,1,0:T(8,128)(2,1)S(1)}, f32[18,128]{1,0:T(8,128)S(1)}) custom-call(s32[1]{0:T(128)} %bitcast.me_ref, s32[1]{0:T(128)} %bitcast.1.side_ref, bf16[512,1024]{1,0:T(8,128)(2,1)S(1)} %copy-done.2, bf16[512,3584]{1,0:T(8,128)(2,1)S(1)} %copy-done, bf16[8,32,128]{2,1,0:T(8,128)(2,1)S(1)} %copy-done.7, ...), custom_call_target="tpu_custom_call" | custom-call | flops 301989888 | bytes 2359296 | tf_op jit(solution)/shard_map/partial_eigen/pallas_call | solution.py:338
  31.1 0.7 collective-permute-done.2.refs_0_
  31.8 1.6 %collective-permute-done.4.refs_1_ = bf16[18,32,128]{2,1,0:T(8,128)(2,1)S(1)} collective-permute-done((bf16[18,32,128]{2,1,0:T(8,128)(2,1)S(1)}, bf16[18,32,128]{2,1,0:T(8,128)(2,1)S(1)}, u32[]{:S(2)}, u32[]{:S(2)}) %collective-permute-start.4) | collective-permute-done | bytes 147488 | tf_op jit(solution)/shard_map/ppermute | solution.py:271
  33.3 1.6 %collective-permute-done.6.refs_2_ = bf16[18,32,128]{2,1,0:T(8,128)(2,1)S(1)} collective-permute-done((bf16[18,32,128]{2,1,0:T(8,128)(2,1)S(1)}, bf16[18,32,128]{2,1,0:T(8,128)(2,1)S(1)}, u32[]{:S(2)}, u32[]{:S(2)}) %collective-permute-start.6) | collective-permute-done | bytes 147488 | tf_op jit(solution)/shard_map/ppermute | solution.py:271
  34.9 0.9 %partial_eigen.3 = (bf16[9,256,256]{2,1,0:T(8,128)(2,1)S(1)}, f32[36,128]{1,0:T(8,128)S(1)}) custom-call(s32[1]{0:T(128)} %bitcast.me_ref, s32[1]{0:T(128)} %bitcast.1.side_ref, bf16[512,1024]{1,0:T(8,128)(2,1)S(1)} %copy-done.2, bf16[512,3584]{1,0:T(8,128)(2,1)S(1)} %copy-done, bf16[8,32,128]{2,1,0:T(8,128)(2,1)S(1)} %copy-done.7, ...), custom_call_target="tpu_custom_call" | custom-call | flops 301989888 | bytes 2359296 | tf_op jit(solution)/shard_map/partial_eigen/pallas_call | solution.py:338
  35.8 0.0 copy-start.5
  35.9 1.0 %copy-done.5 = bf16[9,256,256]{2,1,0:T(8,128)(2,1)} copy-done((bf16[9,256,256]{2,1,0:T(8,128)(2,1)}, bf16[9,256,256]{2,1,0:T(8,128)(2,1)S(1)}, u32[]{:S(2)}) %copy-start.5) | copy-done | bytes 1179672
  36.9 0.0 copy-start.3
  36.9 0.0 collective-permute-done.sent_ref
  36.9 0.0 copy-start.8
  36.9 0.7 copy-done.8
  37.6 13.6 %all-gather.2.sums_ref = f32[4,36,128]{2,1,0:T(8,128)S(1)} all-gather(f32[1,36,128]{2,1,0:T(8,128)S(1)} %bitcast.7), channel_id=2, replica_groups=mesh['groups'=2,'dp'=4,'owner'=4] {'dp'}, dimensions={0}, use_global_device_ids=true | all-gather | bytes 92160 | tf_op jit(solution)/shard_map/all_gather | solution.py:276
  51.2 0.5 collective-permute-start.7
  51.7 1.4 %collective-permute-start.8 = (bf16[1200,128]{1,0:T(8,128)(2,1)}, bf16[1200,128]{1,0:T(8,128)(2,1)}, u32[]{:S(2)}, u32[]{:S(2)}) collective-permute-start(bf16[1200,128]{1,0:T(8,128)(2,1)} %get-tuple-element.36), channel_id=1, source_target_pairs={{0,12},{4,0},{8,4},{12,8},{1,13},{5,1},{9,5},{13,9},{2,14},{6,2},{... | collective-permute-start | bytes 921608 | tf_op jit(solution)/shard_map/ppermute | solution.py:271
  53.1 0.6 combine_eigen.1
  53.7 3.2 %all-to-all-start = ((f32[4,2,128]{2,1,0:T(2,128)}), f32[4,2,128]{2,1,0:T(2,128)S(1)}, u32[]{:S(2)}, u32[]{:S(2)}) async-start(f32[4,2,128]{2,1,0:T(2,128)} %get-tuple-element.42), calls=%async_computation | async-start | bytes 8192 | tf_op jit(solution)/shard_map/all_to_all | solution.py:364
  57.0 0.0 copy-start.9
  57.0 1.0 %copy-done.9 = bf16[1200,128]{1,0:T(8,128)(2,1)S(1)} copy-done((bf16[1200,128]{1,0:T(8,128)(2,1)S(1)}, bf16[1200,128]{1,0:T(8,128)(2,1)}, u32[]{:S(2)}) %copy-start.9) | copy-done | bytes 307224
  57.9 0.6 add_chunk.3.own_ref
  58.5 2.2 %all-to-all-done.total_ref = f32[4,2,128]{2,1,0:T(2,128)S(1)} async-done(((f32[4,2,128]{2,1,0:T(2,128)}), f32[4,2,128]{2,1,0:T(2,128)S(1)}, u32[]{:S(2)}, u32[]{:S(2)}) %all-to-all-start) | async-done | bytes 4128 | tf_op jit(solution)/shard_map/all_to_all | solution.py:364
  60.7 0.0 copy-done.3
  60.7 0.0 copy-start.1
  60.7 2.0 %copy-done.1 = bf16[512,3584]{1,0:T(8,128)(2,1)S(1)} copy-done((bf16[512,3584]{1,0:T(8,128)(2,1)S(1)}, bf16[512,3584]{1,0:T(8,128)(2,1)}, u32[]{:S(2)}) %copy-start.1) | copy-done | bytes 3670040
  62.8 0.0 copy-start.6
  62.8 1.3 %copy-done.6 = bf16[9,256,256]{2,1,0:T(8,128)(2,1)S(1)} copy-done((bf16[9,256,256]{2,1,0:T(8,128)(2,1)S(1)}, bf16[9,256,256]{2,1,0:T(8,128)(2,1)}, u32[]{:S(2)}) %copy-start.6) | copy-done | bytes 1179672
  64.0 1.8 %partial_weights.1 = f32[2,512]{1,0:T(2,128)S(1)} custom-call(s32[1]{0:T(128)} %bitcast.1.side_ref, bf16[512,1024]{1,0:T(8,128)(2,1)S(1)} %copy-done.3, bf16[512,3584]{1,0:T(8,128)(2,1)S(1)} %copy-done.1, f32[36,128]{1,0:T(8,128)S(1)} %get-tuple-element.41.eigen_ref, f32[4,2,128]{2,1,0:T(2,128)S(1)} %all-to-all-done.total_ref, ...), custom_call_target="tpu_custom_call" | custom-call | flops 603979776 | bytes 4718592 | tf_op jit(solution)/shard_map/partial_weights/pallas_call | solution.py:367
  65.9 5.2 %all-gather.3.weight_ref = f32[4,2,512]{2,1,0:T(2,128)S(1)} all-gather(f32[1,2,512]{2,1,0:T(2,128)S(1)} %bitcast.8), channel_id=3, replica_groups=mesh['groups'=2,'dp'=4,'owner'=4] {'owner'}, dimensions={0}, use_global_device_ids=true | all-gather | bytes 20480 | tf_op jit(solution)/shard_map/all_gather | solution.py:276
  71.1 0.6 token_scores.1
  71.7 0.0 collective-permute-done.7.sent_ref
  71.7 1.5 %add_chunk.4.own_ref = f32[36,32,128]{2,1,0:T(8,128)S(1)} custom-call(f32[36,32,128]{2,1,0:T(8,128)S(1)} %add_chunk.3.own_ref, bf16[1200,128]{1,0:T(8,128)(2,1)} %collective-permute-done.7.sent_ref), custom_call_target="tpu_custom_call" | custom-call | bytes 1474560 | tf_op jit(solution)/shard_map/add_chunk/pallas_call | solution.py:386
  73.2 0.0 collective-permute-done.8.sent_ref
  73.2 2.3 %add_chunk.5 = (f32[8,32,128]{2,1,0:T(8,128)}, f32[28,32,128]{2,1,0:T(8,128)}) custom-call(f32[36,32,128]{2,1,0:T(8,128)S(1)} %add_chunk.4.own_ref, bf16[1200,128]{1,0:T(8,128)(2,1)} %collective-permute-done.8.sent_ref), custom_call_target="tpu_custom_call" | custom-call | bytes 1474560 | tf_op jit(solution)/shard_map/add_chunk/pallas_call | solution.py:386
Async XLA Ops:
  2.2 16.3 %collective-permute-start.5 = (bf16[18,32,128]{2,1,0:T(8,128)(2,1)}, bf16[18,32,128]{2,1,0:T(8,128)(2,1)S(1)}, u32[]{:S(2)}, u32[]{:S(2)}) collective-permute-start(bf16[18,32,128]{2,1,0:T(8,128)(2,1)} %basis_half.1), channel_id=1, source_target_pairs={{0,12},{4,0},{8,4},{12,8},{1,13},{5,1},{9,5},{13,9},{2,14},{6,2},{... | collective-permute-start | bytes 442376 | tf_op jit(solution)/shard_map/ppermute | solution.py:271
  7.3 19.3 %collective-permute-start.3 = (bf16[18,32,128]{2,1,0:T(8,128)(2,1)}, bf16[18,32,128]{2,1,0:T(8,128)(2,1)S(1)}, u32[]{:S(2)}, u32[]{:S(2)}) collective-permute-start(bf16[18,32,128]{2,1,0:T(8,128)(2,1)} %basis_half.1), channel_id=1, source_target_pairs={{0,8},{4,12},{8,0},{12,4},{1,9},{5,13},{9,1},{13,5},{2,10},{6,14},... | collective-permute-start | bytes 442376 | tf_op jit(solution)/shard_map/ppermute | solution.py:271
  7.3 19.3 %collective-permute-start.1 = (bf16[18,32,128]{2,1,0:T(8,128)(2,1)}, bf16[18,32,128]{2,1,0:T(8,128)(2,1)S(1)}, u32[]{:S(2)}, u32[]{:S(2)}) collective-permute-start(bf16[18,32,128]{2,1,0:T(8,128)(2,1)} %basis_half.1), channel_id=1, source_target_pairs={{0,4},{4,8},{8,12},{12,0},{1,5},{5,9},{9,13},{13,1},{2,6},{6,10},{... | collective-permute-start | bytes 442376 | tf_op jit(solution)/shard_map/ppermute | solution.py:271
  8.4 2.0 %copy-start = (bf16[512,3584]{1,0:T(8,128)(2,1)S(1)}, bf16[512,3584]{1,0:T(8,128)(2,1)}, u32[]{:S(2)}) copy-start(bf16[512,3584]{1,0:T(8,128)(2,1)} %grad_ref.9) | copy-start | bytes 11010052
  10.4 1.2 %copy-start.2 = (bf16[512,1024]{1,0:T(8,128)(2,1)S(1)}, bf16[512,1024]{1,0:T(8,128)(2,1)}, u32[]{:S(2)}) copy-start(bf16[512,1024]{1,0:T(8,128)(2,1)} %act_ref.9) | copy-start | bytes 3145732
  11.6 18.5 %copy-start.4 = (bf16[28,32,128]{2,1,0:T(8,128)(2,1)S(1)}, bf16[28,32,128]{2,1,0:T(8,128)(2,1)}, u32[]{:S(2)}) copy-start(bf16[28,32,128]{2,1,0:T(8,128)(2,1)} %grad_own.3) | copy-start | bytes 688132
  11.6 18.5 %copy-start.7 = (bf16[8,32,128]{2,1,0:T(8,128)(2,1)S(1)}, bf16[8,32,128]{2,1,0:T(8,128)(2,1)}, u32[]{:S(2)}) copy-start(bf16[8,32,128]{2,1,0:T(8,128)(2,1)} %act_own.3) | copy-start | bytes 196612
  16.1 20.8 %collective-permute-start = (bf16[1200,128]{1,0:T(8,128)(2,1)S(1)}, bf16[1200,128]{1,0:T(8,128)(2,1)S(1)}, u32[]{:S(2)}, u32[]{:S(2)}) collective-permute-start(bf16[1200,128]{1,0:T(8,128)(2,1)S(1)} %get-tuple-element.26), channel_id=1, source_target_pairs={{0,4},{4,8},{8,12},{12,0},{1,5},{5,9},{9,13},{13,1},{2,6},{6,10},{... | collective-permute-start | bytes 921608 | tf_op jit(solution)/shard_map/ppermute | solution.py:271
  26.6 5.1 %collective-permute-start.2 = (bf16[18,32,128]{2,1,0:T(8,128)(2,1)S(1)}, bf16[18,32,128]{2,1,0:T(8,128)(2,1)S(1)}, u32[]{:S(2)}, u32[]{:S(2)}) collective-permute-start(bf16[18,32,128]{2,1,0:T(8,128)(2,1)S(1)} %collective-permute-done.1.refs_0_), channel_id=1, source_target_pairs={{0,16},{16,0},{1,17},{17,1},{2,18},{18,2},{3,19},{19,3},{4,20},{20... | collective-permute-start | bytes 442376 | tf_op jit(solution)/shard_map/ppermute | solution.py:271
  28.1 5.2 %collective-permute-start.4 = (bf16[18,32,128]{2,1,0:T(8,128)(2,1)S(1)}, bf16[18,32,128]{2,1,0:T(8,128)(2,1)S(1)}, u32[]{:S(2)}, u32[]{:S(2)}) collective-permute-start(bf16[18,32,128]{2,1,0:T(8,128)(2,1)S(1)} %collective-permute-done.3.refs_1_), channel_id=1, source_target_pairs={{0,16},{16,0},{1,17},{17,1},{2,18},{18,2},{3,19},{19,3},{4,20},{20... | collective-permute-start | bytes 442376 | tf_op jit(solution)/shard_map/ppermute | solution.py:271
  28.6 6.3 %collective-permute-start.6 = (bf16[18,32,128]{2,1,0:T(8,128)(2,1)S(1)}, bf16[18,32,128]{2,1,0:T(8,128)(2,1)S(1)}, u32[]{:S(2)}, u32[]{:S(2)}) collective-permute-start(bf16[18,32,128]{2,1,0:T(8,128)(2,1)S(1)} %collective-permute-done.5.refs_2_), channel_id=1, source_target_pairs={{0,16},{16,0},{1,17},{17,1},{2,18},{18,2},{3,19},{19,3},{4,20},{20... | collective-permute-start | bytes 442376 | tf_op jit(solution)/shard_map/ppermute | solution.py:271
  35.8 1.0 %copy-start.5 = (bf16[9,256,256]{2,1,0:T(8,128)(2,1)}, bf16[9,256,256]{2,1,0:T(8,128)(2,1)S(1)}, u32[]{:S(2)}) copy-start(bf16[9,256,256]{2,1,0:T(8,128)(2,1)S(1)} %get-tuple-element.44.refs_1_) | copy-start | bytes 3538948
  36.9 23.8 %copy-start.3 = (bf16[512,1024]{1,0:T(8,128)(2,1)S(1)}, bf16[512,1024]{1,0:T(8,128)(2,1)}, u32[]{:S(2)}) copy-start(bf16[512,1024]{1,0:T(8,128)(2,1)} %act_ref.9) | copy-start | bytes 3145732
  36.9 0.7 copy-start.8
  51.2 20.5 %collective-permute-start.7 = (bf16[1200,128]{1,0:T(8,128)(2,1)}, bf16[1200,128]{1,0:T(8,128)(2,1)}, u32[]{:S(2)}, u32[]{:S(2)}) collective-permute-start(bf16[1200,128]{1,0:T(8,128)(2,1)} %get-tuple-element.35), channel_id=1, source_target_pairs={{0,8},{4,12},{8,0},{12,4},{1,9},{5,13},{9,1},{13,5},{2,10},{6,14},... | collective-permute-start | bytes 921608 | tf_op jit(solution)/shard_map/ppermute | solution.py:271
  51.7 21.5 %collective-permute-start.8 = (bf16[1200,128]{1,0:T(8,128)(2,1)}, bf16[1200,128]{1,0:T(8,128)(2,1)}, u32[]{:S(2)}, u32[]{:S(2)}) collective-permute-start(bf16[1200,128]{1,0:T(8,128)(2,1)} %get-tuple-element.36), channel_id=1, source_target_pairs={{0,12},{4,0},{8,4},{12,8},{1,13},{5,1},{9,5},{13,9},{2,14},{6,2},{... | collective-permute-start | bytes 921608 | tf_op jit(solution)/shard_map/ppermute | solution.py:271
  53.7 7.0 %all-to-all-start = ((f32[4,2,128]{2,1,0:T(2,128)}), f32[4,2,128]{2,1,0:T(2,128)S(1)}, u32[]{:S(2)}, u32[]{:S(2)}) async-start(f32[4,2,128]{2,1,0:T(2,128)} %get-tuple-element.42), calls=%async_computation | async-start | bytes 8192 | tf_op jit(solution)/shard_map/all_to_all | solution.py:364
  57.0 1.0 %copy-start.9 = (bf16[1200,128]{1,0:T(8,128)(2,1)S(1)}, bf16[1200,128]{1,0:T(8,128)(2,1)}, u32[]{:S(2)}) copy-start(bf16[1200,128]{1,0:T(8,128)(2,1)} %copy-done.8) | copy-start | bytes 921604
  60.7 2.0 %copy-start.1 = (bf16[512,3584]{1,0:T(8,128)(2,1)S(1)}, bf16[512,3584]{1,0:T(8,128)(2,1)}, u32[]{:S(2)}) copy-start(bf16[512,3584]{1,0:T(8,128)(2,1)} %grad_ref.9) | copy-start | bytes 11010052
  62.8 1.3 %copy-start.6 = (bf16[9,256,256]{2,1,0:T(8,128)(2,1)S(1)}, bf16[9,256,256]{2,1,0:T(8,128)(2,1)}, u32[]{:S(2)}) copy-start(bf16[9,256,256]{2,1,0:T(8,128)(2,1)} %copy-done.5) | copy-start | bytes 3538948

commit v4 on v3

v4 whole, which is shorter than its diff:
```python
import functools

import jax
import jax.numpy as jnp
from jax import lax
from jax.experimental import pallas as pl
from jax.experimental.pallas import tpu as pltpu
from jax.sharding import PartitionSpec as P

D = 4096
FF = 14336
BLK = 128
PAIR = 2 * BLK
GROUP = 4
TILE = 64
VMEM_LIMIT = 24 * 1024 * 1024
CODE_TOP = 2.0**7.875
SMALLEST = 1e-36

damp_root = 0.31622776601683794
contract_rows = (((0,), (0,)), ((), ()))
contract_inner = (((1,), (0,)), ((), ()))
contract_lanes = (((1,), (1,)), ((), ()))

IN_VMEM = pl.BlockSpec(memory_space=pltpu.VMEM)
IN_SMEM = pl.BlockSpec(memory_space=pltpu.SMEM)
IN_HBM = pl.BlockSpec(memory_space=pltpu.HBM)


def call(
    kernel, out_shape, name, flops, bytes_accessed, in_specs, scratch_shapes=(),
    out_spec=IN_VMEM, limit=VMEM_LIMIT,
):
    return pl.pallas_call(
        kernel,
        out_shape=out_shape,
        in_specs=in_specs,
        out_specs=jax.tree.map(lambda _: out_spec, out_shape),
        scratch_shapes=scratch_shapes,
        compiler_params=pltpu.CompilerParams(vmem_limit_bytes=limit),
        cost_estimate=pl.CostEstimate(
            flops=flops, bytes_accessed=bytes_accessed, transcendentals=0
        ),
        name=name,
    )


def f32(*shape):
    return jax.ShapeDtypeStruct(shape, jnp.float32)


def bf16(*shape):
    return jax.ShapeDtypeStruct(shape, jnp.bfloat16)


def encode(values):
    power = values * values
    power = power * power
    power = power * power
    power = power * power
    return jnp.where(values < 0.0, -power, power).astype(jnp.bfloat16)


def decode(coded):
    coded = coded.astype(jnp.float32)
    root = jnp.abs(coded)
    for _ in range(4):
        root = lax.rsqrt(root)
    return jnp.where(coded > 0.0, root, jnp.where(coded < 0.0, -root, 0.0))


def half_kernel(side_ref, act_ref, grad_ref, half_ref, sems):
    side = side_ref[0]
    act_half, grad_half = act_ref.shape[0] // 2, grad_ref.shape[0] // 2
    copies = [
        pltpu.make_async_copy(
            act_ref.at[pl.ds(side * act_half, act_half)],
            half_ref.at[pl.ds(0, act_half)],
            sems.at[0],
        ),
        pltpu.make_async_copy(
            grad_ref.at[pl.ds(side * grad_half, grad_half)],
            half_ref.at[pl.ds(act_half, grad_half)],
            sems.at[1],
        ),
    ]
    for copy in copies:
        copy.start()
    for copy in copies:
        copy.wait()


def gram_kernel(pieces, scale, me_ref, act_ref, grad_ref, own_ref, *refs):
    sent_refs, (whole, tops) = refs[:-2], refs[-2:]
    rows = BLK // pieces
    me = me_ref[0]
    first = 0
    tops[...] = jnp.zeros_like(tops)
    for ref in (act_ref, grad_ref):

        @pl.loop(0, ref.shape[1] // BLK // GROUP)
        def _(step, ref=ref, first=first):
            for offset in range(GROUP):
                block = first + step * GROUP + offset
                at = pl.multiple_of((step * GROUP + offset) * BLK, BLK)
                values = ref[:, pl.ds(at, BLK)]
                gram = scale * lax.dot_general(
                    values, values, contract_rows, preferred_element_type=jnp.float32
                )
                if pieces == 1:
                    own_ref[block] = gram
                    continue
                whole[offset] = gram
                top = jnp.maximum(jnp.max(jnp.abs(gram), axis=0, keepdims=True), SMALLEST)
                top = (top * (1.0 + 2.0**-8)).astype(jnp.bfloat16).astype(jnp.float32)
                tops[pl.ds(block, 1), :] = top
                gain = CODE_TOP / top
                own_ref[block] = whole[offset, pl.ds(pl.multiple_of(me * rows, rows), rows), :]
                for shift in range(1, pieces):
                    row = pl.multiple_of((me ^ shift) * rows, rows)
                    place = pl.multiple_of(block * rows, rows)
                    sent_refs[shift - 1][pl.ds(place, rows), :] = encode(
                        whole[offset, pl.ds(row, rows), :] * gain
                    )

        first += ref.shape[1] // BLK
    for sent_ref in sent_refs:
        sent_ref[first * rows :, :] = tops[...].astype(jnp.bfloat16)


def add_group(own_ref, sent_ref, tops, first):
    rows = own_ref.shape[1]
    for block in [first + offset for offset in range(GROUP)]:
        values = decode(sent_ref[pl.ds(pl.multiple_of(block * rows, rows), rows), :])
        yield block, own_ref[block] + values * tops[pl.ds(block, 1), :]


def add_kernel(own_ref, sent_ref, sum_ref, tops):
    blocks, rows, _ = own_ref.shape
    tops[...] = sent_ref[blocks * rows :, :].astype(jnp.float32) * (1.0 / CODE_TOP)

    @pl.loop(0, blocks // GROUP)
    def _(step):
        for block, total in add_group(own_ref, sent_ref, tops, step * GROUP):
            sum_ref[block] = total


def last_add_kernel(own_ref, sent_ref, act_ref, grad_ref, tops, sums, sems):
    blocks, rows, _ = own_ref.shape
    tops[...] = sent_ref[blocks * rows :, :].astype(jnp.float32) * (1.0 / CODE_TOP)
    act_steps, grad_steps = act_ref.shape[0] // GROUP, grad_ref.shape[0] // GROUP

    def write(ref, step, first):
        return pltpu.make_async_copy(
            sums.at[pl.ds((first + step) * GROUP, GROUP)],
            ref.at[pl.ds(step * GROUP, GROUP)],
            sems.at[first + step],
        )

    for ref, first, steps in ((act_ref, 0, act_steps), (grad_ref, act_steps, grad_steps)):

        @pl.loop(0, steps)
        def _(step, ref=ref, first=first):
            for block, total in add_group(own_ref, sent_ref, tops, (first + step) * GROUP):
                sums[block] = total
            write(ref, step, first).start()

    for ref, first, steps in ((act_ref, 0, act_steps), (grad_ref, act_steps, grad_steps)):

        @pl.loop(0, steps)
        def _(step, ref=ref, first=first):
            write(ref, step, first).wait()


def pairs_of(part, side, halves, act_ref, grad_ref):
    half = lax.rem(side + part, halves)
    for ref in (act_ref, grad_ref):
        count = ref.shape[1] // PAIR // halves
        for pair in range(count):
            yield ref, pl.multiple_of((half * count + pair) * PAIR, PAIR)


def eigen_kernel(
    part, halves, pieces, scale, me_ref, side_ref, act_ref, grad_ref, act_own, grad_own, *refs
):
    *received, power_ref, sums_ref, basis_ref = refs
    me, side = me_ref[0], side_ref[0]
    rows = BLK // pieces
    done = 0
    if part:
        *received, done_ref = received
        done = done_ref.shape[0]
        sums_ref[:done] = done_ref[...]
    half = lax.rem(side + part, halves)
    act_half, grad_half = act_own.shape[0] // halves, grad_own.shape[0] // halves
    basis_ref[...] = jnp.zeros_like(basis_ref)

    def put(shard_of, piece):
        for block in range(act_half + grad_half):
            corner = block % 2
            row = pl.multiple_of(corner * BLK + piece * rows, rows)
            columns = slice(corner * BLK, (corner + 1) * BLK)
            basis_ref[block // 2, pl.ds(row, rows), columns] = shard_of(block)

    def own_shard(block):
        if block < act_half:
            return act_own[half * act_half + block]
        return grad_own[half * grad_half + block - act_half]

    put(own_shard, me)
    for index, ref in enumerate(received):
        put(lambda block, ref=ref: ref[block], me ^ (index + 1))

    for pair, (ref, column) in enumerate(pairs_of(part, side, halves, act_ref, grad_ref)):
        projected = lax.dot_general(
            ref[:, pl.ds(column, PAIR)],
            basis_ref[pair],
            contract_inner,
            preferred_element_type=jnp.float32,
        )
        power = projected * projected
        power_ref[pair] = power
        sums = scale * jnp.sum(power, axis=0, keepdims=True)
        row = done + 2 * pair
        sums_ref[row : row + 1, :] = sums[:, :BLK]
        sums_ref[row + 1 : row + 2, :] = sums[:, BLK:]


def combine_kernel(halves, side_ref, *refs):
    *sums_refs, act_eigen_ref, grad_eigen_ref, eigen_ref, total_ref = refs
    side = side_ref[0]
    act_half, grad_half = act_eigen_ref.shape[0] // halves, grad_eigen_ref.shape[0] // halves
    eigen = sums_refs[0][...]
    for sums_ref in sums_refs[1:]:
        eigen = eigen + sums_ref[...]
    eigen_ref[...] = eigen
    act_total = jnp.zeros((1, BLK), jnp.float32)
    grad_total = jnp.zeros((1, BLK), jnp.float32)
    for part in range(halves):
        half = lax.rem(side + part, halves)
        first = part * (act_half + grad_half)
        act = eigen[first : first + act_half]
        grad = eigen[first + act_half : first + act_half + grad_half]
        act_total += jnp.sum(act, axis=0, keepdims=True)
        grad_total += jnp.sum(grad, axis=0, keepdims=True)
        act_eigen_ref[pl.ds(half * act_half, act_half), :] = act
        grad_eigen_ref[pl.ds(half * grad_half, grad_half), :] = grad
    total_ref[0:1, :] = act_total
    total_ref[1:2, :] = grad_total


def weight_kernel(halves, act_half, eigen_ref, *refs):
    *refs, weight_ref, inverse, act_sum, grad_sum = refs
    power_refs, total_refs = refs[:halves], refs[halves:]
    totals = total_refs[0][...]
    for total_ref in total_refs[1:]:
        totals = totals + total_ref[...]
    totals = jnp.sum(totals, axis=1, keepdims=True)
    blocks_half = eigen_ref.shape[0] // halves
    for part in range(halves):
        first = part * blocks_half
        act = slice(first, first + act_half)
        grad = slice(first + act_half, first + blocks_half)
        inverse[act] = 1.0 / (eigen_ref[act] + totals[0:1] * (damp_root / D))
        inverse[grad] = 1.0 / (eigen_ref[grad] + totals[1:2] * (damp_root / FF))
    tokens = act_sum.shape[0]

    @pl.loop(0, tokens // TILE)
    def _(tile):
        here = pl.ds(pl.multiple_of(tile * TILE, TILE), TILE)
        sums = [jnp.zeros((TILE, BLK), jnp.float32), jnp.zeros((TILE, BLK), jnp.float32)]
        for part, power_ref in enumerate(power_refs):
            for pair in range(power_ref.shape[0]):
                which = 0 if 2 * pair < act_half else 1
                for side in range(2):
                    row = part * blocks_half + 2 * pair + side
                    power = power_ref[pair, here, side * BLK : (side + 1) * BLK]
                    sums[which] += power * inverse[row : row + 1, :]
        act_sum[here, :], grad_sum[here, :] = sums

    ones = jnp.ones((8, BLK), jnp.float32)
    for index, total in enumerate((act_sum, grad_sum)):
        sums = lax.dot_general(
            ones,
            total[...],
            contract_lanes,
            precision=lax.Precision.HIGHEST,
            preferred_element_type=jnp.float32,
        )
        weight_ref[index : index + 1, :] = sums[0:1]


def score_kernel(*refs):
    *weight_refs, score_ref = refs
    weights = weight_refs[0][...]
    for weight_ref in weight_refs[1:]:
        weights = weights + weight_ref[...]
    score_ref[...] = weights[0:1] * weights[1:2] * (1.0 / (D * FF))


def swap(value, axis, mask):
    count = lax.axis_size(axis)
    return lax.ppermute(value, axis, [(i, i ^ mask) for i in range(count)])


def share(value, axis, direct):
    if not direct:
        return [lax.psum(value, axis)]
    return [value] + [swap(value, axis, mask) for mask in range(1, lax.axis_size(axis))]


def after(values, done):
    return list(lax.optimization_barrier((tuple(values), done))[0])


def local(activations, gradients, basis_act, basis_grad):
    tokens = activations.shape[0]
    act_blocks, grad_blocks = basis_act.shape[0], basis_grad.shape[0]
    blocks = act_blocks + grad_blocks
    dp, owners = lax.axis_size("dp"), lax.axis_size("owner")
    scale = 1.0 / (tokens * dp)
    direct = dp in (2, 4) and owners in (1, 2, 4)
    pieces = dp if direct else 1
    halves = 2 if direct and lax.axis_size("groups") == 2 else 1
    rows = BLK // pieces
    me = jnp.full((1,), lax.axis_index("dp") if direct else 0, jnp.int32)
    side = jnp.full((1,), lax.axis_index("groups"), jnp.int32)
    macs = tokens * blocks * BLK * BLK
    input_bytes = 2 * tokens * blocks * BLK
    masks = range(1, pieces)

    if halves == 2:
        shard = call(
            half_kernel, bf16(blocks // 2, rows, BLK), "basis_half", 0, blocks * rows * BLK,
            [IN_SMEM, IN_HBM, IN_HBM], [pltpu.SemaphoreType.DMA((2,))],
            limit=62 * 1024 * 1024,
        )(side, basis_act, basis_grad)
    elif direct:
        shard = jnp.concatenate([basis_act, basis_grad])
    if direct:
        received = [swap(shard, "dp", mask) for mask in masks]
    else:
        basis_act = lax.all_gather(basis_act, "dp", axis=1, tiled=True)
        basis_grad = lax.all_gather(basis_grad, "dp", axis=1, tiled=True)
        received = []

    scale_rows = 16 * pl.cdiv(blocks, 16)
    message = blocks * rows + scale_rows
    own, *sent = call(
        functools.partial(gram_kernel, pieces, scale),
        [f32(blocks, rows, BLK), *[bf16(message, BLK)] * (pieces - 1)],
        "partial_gram", 4 * macs, input_bytes,
        [IN_SMEM, IN_VMEM, IN_VMEM],
        [pltpu.VMEM((GROUP, BLK, BLK), jnp.float32), pltpu.VMEM((scale_rows, BLK), jnp.float32)],
    )(me, activations, gradients)
    late = 2 if pieces > 2 else None
    arrived = [swap(sent[mask - 1], "dp", mask) for mask in masks if mask != late]
    if not direct:
        own = lax.psum_scatter(own, "dp", scatter_dimension=1, tiled=True)

    parts = [received]
    if halves == 2:
        parts.append([swap(after([part], own)[0], "groups", 1) for part in received])
    powers, sums = [], []
    for part, shards in enumerate(parts):
        power, *sums = call(
            functools.partial(eigen_kernel, part, halves, pieces, scale),
            [f32(blocks // halves // 2, tokens, PAIR), f32(blocks // halves * (part + 1), BLK)],
            "partial_eigen", 2 * macs // halves, input_bytes // halves,
            [IN_SMEM, IN_SMEM] + [IN_VMEM] * (4 + len(shards) + len(sums)),
            [pltpu.VMEM((blocks // halves // 2, PAIR, PAIR), jnp.bfloat16)],
        )(me, side, activations, gradients, basis_act, basis_grad, *shards, *sums)
        powers.append(power)
    sums = share(after(sums, arrived)[0], "dp", direct)
    if late:
        arrived.append(swap(after([sent[late - 1]], sums)[0], "dp", late))
    act_eigen, grad_eigen, eigen, totals = call(
        functools.partial(combine_kernel, halves),
        [f32(act_blocks, BLK), f32(grad_blocks, BLK), f32(blocks, BLK), f32(2, BLK)],
        "combine_eigen", 0, 4 * blocks * BLK * pieces, [IN_SMEM] + [IN_VMEM] * len(sums),
    )(side, *sums)
    totals = share(totals, "owner", direct)
    weights = call(
        functools.partial(weight_kernel, halves, act_blocks // halves),
        f32(2, tokens), "partial_weights", 0, 4 * tokens * blocks * BLK,
        [IN_VMEM] * (1 + halves + len(totals)),
        [
            pltpu.VMEM((blocks, BLK), jnp.float32),
            pltpu.VMEM((tokens, BLK), jnp.float32),
            pltpu.VMEM((tokens, BLK), jnp.float32),
        ],
    )(eigen, *powers, *totals)
    weights = share(weights, "owner", direct)
    token_scores = call(
        score_kernel, f32(1, tokens), "token_scores", 0, 8 * tokens * len(weights),
        [IN_VMEM] * len(weights),
    )(*weights)

    for chunk in arrived[:-1]:
        own = call(
            add_kernel, f32(*own.shape), "add_chunk", 0, 10 * own.size, [IN_VMEM, IN_VMEM],
            [pltpu.VMEM((scale_rows, BLK), jnp.float32)],
        )(own, chunk)
    if arrived:
        covariance = call(
            last_add_kernel, [f32(act_blocks, rows, BLK), f32(grad_blocks, rows, BLK)],
            "add_last_chunk", 0, 10 * own.size, [IN_VMEM, IN_VMEM],
            [
                pltpu.VMEM((scale_rows, BLK), jnp.float32),
                pltpu.VMEM(own.shape, jnp.float32),
                pltpu.SemaphoreType.DMA((blocks // GROUP,)),
            ],
            out_spec=pl.BlockSpec(memory_space=pl.ANY),
        )(own, arrived[-1])
    else:
        covariance = own[:act_blocks], own[act_blocks:]
    return (
        *covariance,
        act_eigen.reshape(-1),
        grad_eigen.reshape(-1),
        token_scores.reshape(-1),
    )


def solution(mesh):
    return jax.shard_map(
        local,
        mesh=mesh,
        in_specs=(
            P(("groups", "dp"), "owner"),
            P(("groups", "dp"), "owner"),
            P("owner", "dp", None),
            P("owner", "dp", None),
        ),
        out_specs=(
            P(("groups", "owner"), "dp", None),
            P(("groups", "owner"), "dp", None),
            P(("groups", "owner")),
            P(("groups", "owner")),
            P(("groups", "dp")),
        ),
        check_vma=False,
    )
```

time: 76 us -> 56.3 us (0.74)
  blocking collectives: 18.8 us -> 0 us
  starting transfers between devices: 17.3 us -> 23.8 us
  local copies, waits for them, and re-layouts: 9.29 us -> 3.27 us
  Pallas kernels: 15.3 us -> 12.2 us
  waiting for transfers between devices: 14.1 us -> 16.2 us
    all_gather x2 -> x0, blocking collectives: 18.8 us -> none  [gather_or_sum(): return lax.all_gather(value, axis)]
    ppermute x9 -> x18, starting transfers between devices: 14 us -> 23.8 us  [swap(): return lax.ppermute(value, axis, [(i, i ^ mask) for i in range(count)])]
    unnamed x20 -> x8, local copies, waits for them, and re-layouts: 9.29 us -> 3.27 us
    ppermute x9 -> x18, waiting for transfers between devices: 11.9 us -> 16.2 us  [swap(): return lax.ppermute(value, axis, [(i, i ^ mask) for i in range(count)])]
    all_to_all x1 -> x0, starting transfers between devices: 3.25 us -> none  [local(): totals = lax.all_to_all(totals, 'owner', 0, 0, tiled=True)]
    pallas_call x7, Pallas kernels: 8.65 us -> 6.36 us  [the longest x2 1.94 us: local(): call(functools.partial(eigen_kernel, part, halves, pieces, scale), [f32(b...]
    all_to_all x1 -> x0, waiting for transfers between devices: 2.21 us -> none  [local(): totals = lax.all_to_all(totals, 'owner', 0, 0, tiled=True)]
    pallas_call x1, Pallas kernels: 4.44 us -> 3.57 us  [local(): call(functools.partial(gram_kernel, pieces, scale), [f32(blocks, rows, BL...]
  transfers between devices with their start and end apart: 10 -> 18, of which waited for: 5 -> 11; matrix products, arithmetic and copies ran while one was open for 0% -> 0% of each run, Pallas kernels for 15% -> 17%
where the time goes in v4:
time: 56.3 us; the launch traced here: 56.1 us
  starting transfers between devices  23.8 us (42%)
  waiting for transfers between devices  16.2 us (29%)
  Pallas kernels  12.2 us (22%)
  local copies, waits for them, and re-layouts  3.27 us (6%)
  between operations  0.73 us (1%)
    ppermute x18, starting transfers between devices, swap(): return lax.ppermute(value, axis, [(i, i ^ mask) for i in range(count)])  23.8 us
    ppermute x18, waiting for transfers between devices, swap(): return lax.ppermute(value, axis, [(i, i ^ mask) for i in range(count)])  16.2 us
    pallas_call x1, Pallas kernels, local(): call(functools.partial(gram_kernel, pieces, scale), [f32(blocks, rows, BL...  3.57 us
    unnamed x8, local copies, waits for them, and re-layouts  3.27 us
    pallas_call x2, Pallas kernels, local(): call(functools.partial(eigen_kernel, part, halves, pieces, scale), [f32(b...  1.94 us
    pallas_call x1, Pallas kernels, local(): call(half_kernel, bf16(blocks // 2, rows, BLK), 'basis_half', 0, blocks *...  1.64 us
    pallas_call x1, Pallas kernels, local(): call(functools.partial(weight_kernel, halves, act_blocks // halves), f32(...  1.47 us
    pallas_call x1, Pallas kernels, local(): call(last_add_kernel, [f32(act_blocks, rows, BLK), f32(grad_blocks, rows,...  1.24 us
  transfers between devices with their start and end apart: 18, of which 11 were waited for; matrix products, arithmetic and copies ran while one was open for 0% of the time, Pallas kernels for 17%

profile of v4, /device:TPU:0, one launch (start us, length us, event | category | flops | bytes accessed | tf_op | source)
XLA Modules:
  0.0 56.1 jit_solution(18258027075445626716)
XLA Ops:
  0.6 0.0 copy-start.2
  0.6 0.0 copy-start.3
  0.7 1.6 %basis_half.1 = bf16[18,32,128]{2,1,0:T(8,128)(2,1)} custom-call(s32[1]{0:T(128)} %bitcast.1.side_ref, bf16[8,32,128]{2,1,0:T(8,128)(2,1)} %act_own.3, bf16[28,32,128]{2,1,0:T(8,128)(2,1)} %grad_own.3), custom_call_target="tpu_custom_call" | custom-call | bytes 147456 | tf_op jit(solution)/shard_map/basis_half/pallas_call | solution.py:333
  2.3 5.1 %collective-permute-start.6 = (bf16[18,32,128]{2,1,0:T(8,128)(2,1)}, bf16[18,32,128]{2,1,0:T(8,128)(2,1)S(1)}, u32[]{:S(2)}, u32[]{:S(2)}) collective-permute-start(bf16[18,32,128]{2,1,0:T(8,128)(2,1)} %basis_half.1), channel_id=1, source_target_pairs={{0,12},{4,8},{8,4},{12,0},{1,13},{5,9},{9,5},{13,1},{2,14},{6,10},... | collective-permute-start | bytes 442376 | tf_op jit(solution)/shard_map/ppermute | solution.py:303
  7.4 0.0 collective-permute-start.4
  7.4 0.6 %collective-permute-start.2 = (bf16[18,32,128]{2,1,0:T(8,128)(2,1)}, bf16[18,32,128]{2,1,0:T(8,128)(2,1)S(1)}, u32[]{:S(2)}, u32[]{:S(2)}) collective-permute-start(bf16[18,32,128]{2,1,0:T(8,128)(2,1)} %basis_half.1), channel_id=1, source_target_pairs={{0,4},{4,0},{8,12},{12,8},{1,5},{5,1},{9,13},{13,9},{2,6},{6,2},{1... | collective-permute-start | bytes 442376 | tf_op jit(solution)/shard_map/ppermute | solution.py:303
  8.1 0.0 copy-start
  8.1 2.0 %copy-done = bf16[512,3584]{1,0:T(8,128)(2,1)S(1)} copy-done((bf16[512,3584]{1,0:T(8,128)(2,1)S(1)}, bf16[512,3584]{1,0:T(8,128)(2,1)}, u32[]{:S(2)}) %copy-start) | copy-done | bytes 3670040
  10.1 0.0 copy-start.1
  10.1 1.2 %copy-done.1 = bf16[512,1024]{1,0:T(8,128)(2,1)S(1)} copy-done((bf16[512,1024]{1,0:T(8,128)(2,1)S(1)}, bf16[512,1024]{1,0:T(8,128)(2,1)}, u32[]{:S(2)}) %copy-start.1) | copy-done | bytes 1048600
  11.3 3.6 %partial_gram.1 = (f32[36,32,128]{2,1,0:T(8,128)S(1)}, bf16[1200,128]{1,0:T(8,128)(2,1)S(1)}, bf16[1200,128]{1,0:T(8,128)(2,1)S(1)}, bf16[1200,128]{1,0:T(8,128)(2,1)S(1)}) custom-call(s32[1]{0:T(128)} %bitcast.me_ref, bf16[512,1024]{1,0:T(8,128)(2,1)S(1)} %copy-done.1, bf16[512,3584]{1,0:T(8,128)(2,1)S(1)} %copy-done), custom_call_target="tpu_custom_call" | custom-call | flops 1207959552 | bytes 4718592 | tf_op jit(solution)/shard_map/partial_gram/pallas_call | solution.py:349
  14.9 1.5 %collective-permute-start = (bf16[1200,128]{1,0:T(8,128)(2,1)S(1)}, bf16[1200,128]{1,0:T(8,128)(2,1)S(1)}, u32[]{:S(2)}, u32[]{:S(2)}) collective-permute-start(bf16[1200,128]{1,0:T(8,128)(2,1)S(1)} %get-tuple-element.25), channel_id=1, source_target_pairs={{0,4},{4,0},{8,12},{12,8},{1,5},{5,1},{9,13},{13,9},{2,6},{6,2},{1... | collective-permute-start | bytes 921608 | tf_op jit(solution)/shard_map/ppermute | solution.py:303
  16.4 2.4 %collective-permute-start.1 = (bf16[1200,128]{1,0:T(8,128)(2,1)S(1)}, bf16[1200,128]{1,0:T(8,128)(2,1)S(1)}, u32[]{:S(2)}, u32[]{:S(2)}) collective-permute-start(bf16[1200,128]{1,0:T(8,128)(2,1)S(1)} %get-tuple-element.26), channel_id=1, source_target_pairs={{0,12},{4,8},{8,4},{12,0},{1,13},{5,9},{9,5},{13,1},{2,14},{6,10},... | collective-permute-start | bytes 921608 | tf_op jit(solution)/shard_map/ppermute | solution.py:303
  18.8 0.0 collective-permute-done.6.refs_2_
  18.8 2.3 %collective-permute-done.4.refs_1_ = bf16[18,32,128]{2,1,0:T(8,128)(2,1)S(1)} collective-permute-done((bf16[18,32,128]{2,1,0:T(8,128)(2,1)}, bf16[18,32,128]{2,1,0:T(8,128)(2,1)S(1)}, u32[]{:S(2)}, u32[]{:S(2)}) %collective-permute-start.4) | collective-permute-done | bytes 147488 | tf_op jit(solution)/shard_map/ppermute | solution.py:303
  21.1 0.0 collective-permute-done.2.refs_0_
  21.1 1.5 %collective-permute-start.3 = (bf16[18,32,128]{2,1,0:T(8,128)(2,1)S(1)}, bf16[18,32,128]{2,1,0:T(8,128)(2,1)S(1)}, u32[]{:S(2)}, u32[]{:S(2)}) collective-permute-start(bf16[18,32,128]{2,1,0:T(8,128)(2,1)S(1)} %collective-permute-done.2.refs_0_), channel_id=1, source_target_pairs={{0,16},{16,0},{1,17},{17,1},{2,18},{18,2},{3,19},{19,3},{4,20},{20... | collective-permute-start | bytes 442376 | tf_op jit(solution)/shard_map/ppermute | solution.py:303
  22.6 0.5 collective-permute-start.5
  23.1 1.5 %collective-permute-start.7 = (bf16[18,32,128]{2,1,0:T(8,128)(2,1)S(1)}, bf16[18,32,128]{2,1,0:T(8,128)(2,1)S(1)}, u32[]{:S(2)}, u32[]{:S(2)}) collective-permute-start(bf16[18,32,128]{2,1,0:T(8,128)(2,1)S(1)} %collective-permute-done.6.refs_2_), channel_id=1, source_target_pairs={{0,16},{16,0},{1,17},{17,1},{2,18},{18,2},{3,19},{19,3},{4,20},{20... | collective-permute-start | bytes 442376 | tf_op jit(solution)/shard_map/ppermute | solution.py:303
  24.7 0.0 copy-done.2
  24.7 0.0 copy-done.3
  24.7 1.0 %partial_eigen.2 = (f32[9,512,256]{2,1,0:T(8,128)S(1)}, f32[18,128]{1,0:T(8,128)S(1)}) custom-call(s32[1]{0:T(128)} %bitcast.me_ref, s32[1]{0:T(128)} %bitcast.1.side_ref, bf16[512,1024]{1,0:T(8,128)(2,1)S(1)} %copy-done.1, bf16[512,3584]{1,0:T(8,128)(2,1)S(1)} %copy-done, bf16[8,32,128]{2,1,0:T(8,128)(2,1)S(1)} %copy-done.3, ...), custom_call_target="tpu_custom_call" | custom-call | flops 301989888 | bytes 2359296 | tf_op jit(solution)/shard_map/partial_eigen/pallas_call | solution.py:366
  25.7 2.3 %collective-permute-done.3.refs_0_ = bf16[18,32,128]{2,1,0:T(8,128)(2,1)S(1)} collective-permute-done((bf16[18,32,128]{2,1,0:T(8,128)(2,1)S(1)}, bf16[18,32,128]{2,1,0:T(8,128)(2,1)S(1)}, u32[]{:S(2)}, u32[]{:S(2)}) %collective-permute-start.3) | collective-permute-done | bytes 147488 | tf_op jit(solution)/shard_map/ppermute | solution.py:303
  27.9 1.9 %collective-permute-done.5.refs_1_ = bf16[18,32,128]{2,1,0:T(8,128)(2,1)S(1)} collective-permute-done((bf16[18,32,128]{2,1,0:T(8,128)(2,1)S(1)}, bf16[18,32,128]{2,1,0:T(8,128)(2,1)S(1)}, u32[]{:S(2)}, u32[]{:S(2)}) %collective-permute-start.5) | collective-permute-done | bytes 147488 | tf_op jit(solution)/shard_map/ppermute | solution.py:303
  29.8 1.6 %collective-permute-done.7.refs_2_ = bf16[18,32,128]{2,1,0:T(8,128)(2,1)S(1)} collective-permute-done((bf16[18,32,128]{2,1,0:T(8,128)(2,1)S(1)}, bf16[18,32,128]{2,1,0:T(8,128)(2,1)S(1)}, u32[]{:S(2)}, u32[]{:S(2)}) %collective-permute-start.7) | collective-permute-done | bytes 147488 | tf_op jit(solution)/shard_map/ppermute | solution.py:303
  31.4 1.0 %partial_eigen.3 = (f32[9,512,256]{2,1,0:T(8,128)S(1)}, f32[36,128]{1,0:T(8,128)S(1)}) custom-call(s32[1]{0:T(128)} %bitcast.me_ref, s32[1]{0:T(128)} %bitcast.1.side_ref, bf16[512,1024]{1,0:T(8,128)(2,1)S(1)} %copy-done.1, bf16[512,3584]{1,0:T(8,128)(2,1)S(1)} %copy-done, bf16[8,32,128]{2,1,0:T(8,128)(2,1)S(1)} %copy-done.3, ...), custom_call_target="tpu_custom_call" | custom-call | flops 301989888 | bytes 2359296 | tf_op jit(solution)/shard_map/partial_eigen/pallas_call | solution.py:366
  32.4 0.4 collective-permute-done.sent_ref
  32.7 0.0 collective-permute-done.1.sent_ref
  32.7 2.9 %collective-permute-start.10 = (f32[36,128]{1,0:T(8,128)S(1)}, f32[36,128]{1,0:T(8,128)S(1)}, u32[]{:S(2)}, u32[]{:S(2)}) collective-permute-start(f32[36,128]{1,0:T(8,128)S(1)} %get-tuple-element.33.refs_0_), channel_id=1, source_target_pairs={{0,12},{4,8},{8,4},{12,0},{1,13},{5,9},{9,5},{13,1},{2,14},{6,10},... | collective-permute-start | bytes 55304 | tf_op jit(solution)/shard_map/ppermute | solution.py:303
  35.6 0.0 collective-permute-start.9
  35.6 1.5 %collective-permute-start.8 = (f32[36,128]{1,0:T(8,128)S(1)}, f32[36,128]{1,0:T(8,128)S(1)}, u32[]{:S(2)}, u32[]{:S(2)}) collective-permute-start(f32[36,128]{1,0:T(8,128)S(1)} %get-tuple-element.33.refs_0_), channel_id=1, source_target_pairs={{0,4},{4,0},{8,12},{12,8},{1,5},{5,1},{9,13},{13,9},{2,6},{6,2},{1... | collective-permute-start | bytes 55304 | tf_op jit(solution)/shard_map/ppermute | solution.py:303
  37.1 1.2 %collective-permute-done.10.refs_3_ = f32[36,128]{1,0:T(8,128)S(1)} collective-permute-done((f32[36,128]{1,0:T(8,128)S(1)}, f32[36,128]{1,0:T(8,128)S(1)}, u32[]{:S(2)}, u32[]{:S(2)}) %collective-permute-start.10) | collective-permute-done | bytes 18464 | tf_op jit(solution)/shard_map/ppermute | solution.py:303
  38.3 2.0 %collective-permute-done.9.refs_2_ = f32[36,128]{1,0:T(8,128)S(1)} collective-permute-done((f32[36,128]{1,0:T(8,128)S(1)}, f32[36,128]{1,0:T(8,128)S(1)}, u32[]{:S(2)}, u32[]{:S(2)}) %collective-permute-start.9) | collective-permute-done | bytes 18464 | tf_op jit(solution)/shard_map/ppermute | solution.py:303
  40.3 0.0 collective-permute-done.8.refs_1_
  40.3 2.2 %collective-permute-start.11 = (bf16[1200,128]{1,0:T(8,128)(2,1)S(1)}, bf16[1200,128]{1,0:T(8,128)(2,1)S(1)}, u32[]{:S(2)}, u32[]{:S(2)}) collective-permute-start(bf16[1200,128]{1,0:T(8,128)(2,1)S(1)} %get-tuple-element.34), channel_id=1, source_target_pairs={{0,8},{4,12},{8,0},{12,4},{1,9},{5,13},{9,1},{13,5},{2,10},{6,14},... | collective-permute-start | bytes 921608 | tf_op jit(solution)/shard_map/ppermute | solution.py:303
  42.6 0.6 %combine_eigen.1 = (f32[8,128]{1,0:T(8,128)}, f32[28,128]{1,0:T(8,128)}, f32[36,128]{1,0:T(8,128)S(1)}, f32[2,128]{1,0:T(2,128)S(1)}) custom-call(s32[1]{0:T(128)} %bitcast.1.side_ref, f32[36,128]{1,0:T(8,128)S(1)} %get-tuple-element.33.refs_0_, f32[36,128]{1,0:T(8,128)S(1)} %collective-permute-done.8.refs_1_, f32[36,128]{1,0:T(8,128)S(1)} %collective-permute-done.9.refs_2_, ...), custom_call_target="tpu_custom_call" | custom-call | bytes 73728 | tf_op jit(solution)/shard_map/combine_eigen/pallas_call | solution.py:377
  43.2 0.0 collective-permute-start.14
  43.2 1.5 %collective-permute-start.13 = (f32[2,128]{1,0:T(2,128)S(1)}, f32[2,128]{1,0:T(2,128)S(1)}, u32[]{:S(2)}, u32[]{:S(2)}) collective-permute-start(f32[2,128]{1,0:T(2,128)S(1)} %get-tuple-element.42.refs_2_), channel_id=1, source_target_pairs={{0,2},{1,3},{2,0},{3,1},{4,6},{5,7},{6,4},{7,5},{8,10},{9,11},{10,... | collective-permute-start | bytes 3080 | tf_op jit(solution)/shard_map/ppermute | solution.py:303
  44.7 0.3 collective-permute-start.12
  45.1 1.1 %collective-permute-done.14.refs_5_ = f32[2,128]{1,0:T(2,128)S(1)} collective-permute-done((f32[2,128]{1,0:T(2,128)S(1)}, f32[2,128]{1,0:T(2,128)S(1)}, u32[]{:S(2)}, u32[]{:S(2)}) %collective-permute-start.14) | collective-permute-done | bytes 1056 | tf_op jit(solution)/shard_map/ppermute | solution.py:303
  46.2 0.6 %collective-permute-done.13.refs_4_ = f32[2,128]{1,0:T(2,128)S(1)} collective-permute-done((f32[2,128]{1,0:T(2,128)S(1)}, f32[2,128]{1,0:T(2,128)S(1)}, u32[]{:S(2)}, u32[]{:S(2)}) %collective-permute-start.13) | collective-permute-done | bytes 1056 | tf_op jit(solution)/shard_map/ppermute | solution.py:303
  46.8 0.0 collective-permute-done.12.refs_3_
  46.8 1.5 %partial_weights.1.refs_0_ = f32[2,512]{1,0:T(2,128)S(1)} custom-call(f32[36,128]{1,0:T(8,128)S(1)} %get-tuple-element.39.eigen_ref, f32[9,512,256]{2,1,0:T(8,128)S(1)} %get-tuple-element.40.refs_0_, f32[9,512,256]{2,1,0:T(8,128)S(1)} %get-tuple-element.41.refs_1_, f32[2,128]{1,0:T(2,128)S(1)} %get-tuple-element.42.refs_2_, ...), custom_call_target="tpu_custom_call" | custom-call | bytes 9437184 | tf_op jit(solution)/shard_map/partial_weights/pallas_call | solution.py:383
  48.3 0.6 %collective-permute-start.17 = (f32[2,512]{1,0:T(2,128)S(1)}, f32[2,512]{1,0:T(2,128)S(1)}, u32[]{:S(2)}, u32[]{:S(2)}) collective-permute-start(f32[2,512]{1,0:T(2,128)S(1)} %partial_weights.1.refs_0_), channel_id=1, source_target_pairs={{0,3},{1,2},{2,1},{3,0},{4,7},{5,6},{6,5},{7,4},{8,11},{9,10},{10,... | collective-permute-start | bytes 12296 | tf_op jit(solution)/shard_map/ppermute | solution.py:303
  48.9 1.5 %collective-permute-start.16 = (f32[2,512]{1,0:T(2,128)S(1)}, f32[2,512]{1,0:T(2,128)S(1)}, u32[]{:S(2)}, u32[]{:S(2)}) collective-permute-start(f32[2,512]{1,0:T(2,128)S(1)} %partial_weights.1.refs_0_), channel_id=1, source_target_pairs={{0,2},{1,3},{2,0},{3,1},{4,6},{5,7},{6,4},{7,5},{8,10},{9,11},{10,... | collective-permute-start | bytes 12296 | tf_op jit(solution)/shard_map/ppermute | solution.py:303
  50.4 0.0 collective-permute-start.15
  50.4 0.6 %add_chunk.2.own_ref = f32[36,32,128]{2,1,0:T(8,128)S(1)} custom-call(f32[36,32,128]{2,1,0:T(8,128)S(1)} %get-tuple-element.24.own_ref, bf16[1200,128]{1,0:T(8,128)(2,1)S(1)} %collective-permute-done.sent_ref), custom_call_target="tpu_custom_call" | custom-call | bytes 1474560 | tf_op jit(solution)/shard_map/add_chunk/pallas_call | solution.py:400
  50.9 0.6 %add_chunk.3.own_ref = f32[36,32,128]{2,1,0:T(8,128)S(1)} custom-call(f32[36,32,128]{2,1,0:T(8,128)S(1)} %add_chunk.2.own_ref, bf16[1200,128]{1,0:T(8,128)(2,1)S(1)} %collective-permute-done.1.sent_ref), custom_call_target="tpu_custom_call" | custom-call | bytes 1474560 | tf_op jit(solution)/shard_map/add_chunk/pallas_call | solution.py:400
  51.5 0.0 collective-permute-done.17.refs_3_
  51.5 1.0 %collective-permute-done.16.refs_2_ = f32[2,512]{1,0:T(2,128)S(1)} collective-permute-done((f32[2,512]{1,0:T(2,128)S(1)}, f32[2,512]{1,0:T(2,128)S(1)}, u32[]{:S(2)}, u32[]{:S(2)}) %collective-permute-start.16) | collective-permute-done | bytes 4128 | tf_op jit(solution)/shard_map/ppermute | solution.py:303
  52.5 0.0 collective-permute-done.15.refs_1_
  52.5 0.6 %token_scores.1 = f32[1,512]{1,0:T(1,128)} custom-call(f32[2,512]{1,0:T(2,128)S(1)} %partial_weights.1.refs_0_, f32[2,512]{1,0:T(2,128)S(1)} %collective-permute-done.15.refs_1_, f32[2,512]{1,0:T(2,128)S(1)} %collective-permute-done.16.refs_2_, f32[2,512]{1,0:T(2,128)S(1)} %collective-permute-done.17.refs_3_), custom_call_target="tpu_custom_call" | custom-call | bytes 16384 | tf_op jit(solution)/shard_map/token_scores/pallas_call | solution.py:394
  53.1 1.8 %collective-permute-done.11.sent_ref = bf16[1200,128]{1,0:T(8,128)(2,1)S(1)} collective-permute-done((bf16[1200,128]{1,0:T(8,128)(2,1)S(1)}, bf16[1200,128]{1,0:T(8,128)(2,1)S(1)}, u32[]{:S(2)}, u32[]{:S(2)}) %collective-permute-start.11) | collective-permute-done | bytes 307232 | tf_op jit(solution)/shard_map/ppermute | solution.py:303
  54.9 1.2 %add_last_chunk.1 = (f32[8,32,128]{2,1,0:T(8,128)}, f32[28,32,128]{2,1,0:T(8,128)}) custom-call(f32[36,32,128]{2,1,0:T(8,128)S(1)} %add_chunk.3.own_ref, bf16[1200,128]{1,0:T(8,128)(2,1)S(1)} %collective-permute-done.11.sent_ref), custom_call_target="tpu_custom_call" | custom-call | bytes 1474560 | tf_op jit(solution)/shard_map/add_last_chunk/pallas_call | solution.py:405
Async XLA Ops:
  0.6 24.0 %copy-start.2 = (bf16[28,32,128]{2,1,0:T(8,128)(2,1)S(1)}, bf16[28,32,128]{2,1,0:T(8,128)(2,1)}, u32[]{:S(2)}) copy-start(bf16[28,32,128]{2,1,0:T(8,128)(2,1)} %grad_own.3) | copy-start | bytes 688132
  0.6 24.0 %copy-start.3 = (bf16[8,32,128]{2,1,0:T(8,128)(2,1)S(1)}, bf16[8,32,128]{2,1,0:T(8,128)(2,1)}, u32[]{:S(2)}) copy-start(bf16[8,32,128]{2,1,0:T(8,128)(2,1)} %act_own.3) | copy-start | bytes 196612
  2.3 16.5 %collective-permute-start.6 = (bf16[18,32,128]{2,1,0:T(8,128)(2,1)}, bf16[18,32,128]{2,1,0:T(8,128)(2,1)S(1)}, u32[]{:S(2)}, u32[]{:S(2)}) collective-permute-start(bf16[18,32,128]{2,1,0:T(8,128)(2,1)} %basis_half.1), channel_id=1, source_target_pairs={{0,12},{4,8},{8,4},{12,0},{1,13},{5,9},{9,5},{13,1},{2,14},{6,10},... | collective-permute-start | bytes 442376 | tf_op jit(solution)/shard_map/ppermute | solution.py:303
  7.4 13.7 %collective-permute-start.4 = (bf16[18,32,128]{2,1,0:T(8,128)(2,1)}, bf16[18,32,128]{2,1,0:T(8,128)(2,1)S(1)}, u32[]{:S(2)}, u32[]{:S(2)}) collective-permute-start(bf16[18,32,128]{2,1,0:T(8,128)(2,1)} %basis_half.1), channel_id=1, source_target_pairs={{0,8},{4,12},{8,0},{12,4},{1,9},{5,13},{9,1},{13,5},{2,10},{6,14},... | collective-permute-start | bytes 442376 | tf_op jit(solution)/shard_map/ppermute | solution.py:303
  7.4 13.7 %collective-permute-start.2 = (bf16[18,32,128]{2,1,0:T(8,128)(2,1)}, bf16[18,32,128]{2,1,0:T(8,128)(2,1)S(1)}, u32[]{:S(2)}, u32[]{:S(2)}) collective-permute-start(bf16[18,32,128]{2,1,0:T(8,128)(2,1)} %basis_half.1), channel_id=1, source_target_pairs={{0,4},{4,0},{8,12},{12,8},{1,5},{5,1},{9,13},{13,9},{2,6},{6,2},{1... | collective-permute-start | bytes 442376 | tf_op jit(solution)/shard_map/ppermute | solution.py:303
  8.1 2.0 %copy-start = (bf16[512,3584]{1,0:T(8,128)(2,1)S(1)}, bf16[512,3584]{1,0:T(8,128)(2,1)}, u32[]{:S(2)}) copy-start(bf16[512,3584]{1,0:T(8,128)(2,1)} %grad_ref.7) | copy-start | bytes 11010052
  10.1 1.2 %copy-start.1 = (bf16[512,1024]{1,0:T(8,128)(2,1)S(1)}, bf16[512,1024]{1,0:T(8,128)(2,1)}, u32[]{:S(2)}) copy-start(bf16[512,1024]{1,0:T(8,128)(2,1)} %act_ref.7) | copy-start | bytes 3145732
  14.9 17.8 %collective-permute-start = (bf16[1200,128]{1,0:T(8,128)(2,1)S(1)}, bf16[1200,128]{1,0:T(8,128)(2,1)S(1)}, u32[]{:S(2)}, u32[]{:S(2)}) collective-permute-start(bf16[1200,128]{1,0:T(8,128)(2,1)S(1)} %get-tuple-element.25), channel_id=1, source_target_pairs={{0,4},{4,0},{8,12},{12,8},{1,5},{5,1},{9,13},{13,9},{2,6},{6,2},{1... | collective-permute-start | bytes 921608 | tf_op jit(solution)/shard_map/ppermute | solution.py:303
  16.4 16.4 %collective-permute-start.1 = (bf16[1200,128]{1,0:T(8,128)(2,1)S(1)}, bf16[1200,128]{1,0:T(8,128)(2,1)S(1)}, u32[]{:S(2)}, u32[]{:S(2)}) collective-permute-start(bf16[1200,128]{1,0:T(8,128)(2,1)S(1)} %get-tuple-element.26), channel_id=1, source_target_pairs={{0,12},{4,8},{8,4},{12,0},{1,13},{5,9},{9,5},{13,1},{2,14},{6,10},... | collective-permute-start | bytes 921608 | tf_op jit(solution)/shard_map/ppermute | solution.py:303
  21.1 6.8 %collective-permute-start.3 = (bf16[18,32,128]{2,1,0:T(8,128)(2,1)S(1)}, bf16[18,32,128]{2,1,0:T(8,128)(2,1)S(1)}, u32[]{:S(2)}, u32[]{:S(2)}) collective-permute-start(bf16[18,32,128]{2,1,0:T(8,128)(2,1)S(1)} %collective-permute-done.2.refs_0_), channel_id=1, source_target_pairs={{0,16},{16,0},{1,17},{17,1},{2,18},{18,2},{3,19},{19,3},{4,20},{20... | collective-permute-start | bytes 442376 | tf_op jit(solution)/shard_map/ppermute | solution.py:303
  22.6 7.2 %collective-permute-start.5 = (bf16[18,32,128]{2,1,0:T(8,128)(2,1)S(1)}, bf16[18,32,128]{2,1,0:T(8,128)(2,1)S(1)}, u32[]{:S(2)}, u32[]{:S(2)}) collective-permute-start(bf16[18,32,128]{2,1,0:T(8,128)(2,1)S(1)} %collective-permute-done.4.refs_1_), channel_id=1, source_target_pairs={{0,16},{16,0},{1,17},{17,1},{2,18},{18,2},{3,19},{19,3},{4,20},{20... | collective-permute-start | bytes 442376 | tf_op jit(solution)/shard_map/ppermute | solution.py:303
  23.1 8.2 %collective-permute-start.7 = (bf16[18,32,128]{2,1,0:T(8,128)(2,1)S(1)}, bf16[18,32,128]{2,1,0:T(8,128)(2,1)S(1)}, u32[]{:S(2)}, u32[]{:S(2)}) collective-permute-start(bf16[18,32,128]{2,1,0:T(8,128)(2,1)S(1)} %collective-permute-done.6.refs_2_), channel_id=1, source_target_pairs={{0,16},{16,0},{1,17},{17,1},{2,18},{18,2},{3,19},{19,3},{4,20},{20... | collective-permute-start | bytes 442376 | tf_op jit(solution)/shard_map/ppermute | solution.py:303
  32.7 5.6 %collective-permute-start.10 = (f32[36,128]{1,0:T(8,128)S(1)}, f32[36,128]{1,0:T(8,128)S(1)}, u32[]{:S(2)}, u32[]{:S(2)}) collective-permute-start(f32[36,128]{1,0:T(8,128)S(1)} %get-tuple-element.33.refs_0_), channel_id=1, source_target_pairs={{0,12},{4,8},{8,4},{12,0},{1,13},{5,9},{9,5},{13,1},{2,14},{6,10},... | collective-permute-start | bytes 55304 | tf_op jit(solution)/shard_map/ppermute | solution.py:303
  35.6 4.7 %collective-permute-start.9 = (f32[36,128]{1,0:T(8,128)S(1)}, f32[36,128]{1,0:T(8,128)S(1)}, u32[]{:S(2)}, u32[]{:S(2)}) collective-permute-start(f32[36,128]{1,0:T(8,128)S(1)} %get-tuple-element.33.refs_0_), channel_id=1, source_target_pairs={{0,8},{4,12},{8,0},{12,4},{1,9},{5,13},{9,1},{13,5},{2,10},{6,14},... | collective-permute-start | bytes 55304 | tf_op jit(solution)/shard_map/ppermute | solution.py:303
  35.6 4.7 %collective-permute-start.8 = (f32[36,128]{1,0:T(8,128)S(1)}, f32[36,128]{1,0:T(8,128)S(1)}, u32[]{:S(2)}, u32[]{:S(2)}) collective-permute-start(f32[36,128]{1,0:T(8,128)S(1)} %get-tuple-element.33.refs_0_), channel_id=1, source_target_pairs={{0,4},{4,0},{8,12},{12,8},{1,5},{5,1},{9,13},{13,9},{2,6},{6,2},{1... | collective-permute-start | bytes 55304 | tf_op jit(solution)/shard_map/ppermute | solution.py:303
  40.3 14.6 %collective-permute-start.11 = (bf16[1200,128]{1,0:T(8,128)(2,1)S(1)}, bf16[1200,128]{1,0:T(8,128)(2,1)S(1)}, u32[]{:S(2)}, u32[]{:S(2)}) collective-permute-start(bf16[1200,128]{1,0:T(8,128)(2,1)S(1)} %get-tuple-element.34), channel_id=1, source_target_pairs={{0,8},{4,12},{8,0},{12,4},{1,9},{5,13},{9,1},{13,5},{2,10},{6,14},... | collective-permute-start | bytes 921608 | tf_op jit(solution)/shard_map/ppermute | solution.py:303
  43.2 3.0 %collective-permute-start.14 = (f32[2,128]{1,0:T(2,128)S(1)}, f32[2,128]{1,0:T(2,128)S(1)}, u32[]{:S(2)}, u32[]{:S(2)}) collective-permute-start(f32[2,128]{1,0:T(2,128)S(1)} %get-tuple-element.42.refs_2_), channel_id=1, source_target_pairs={{0,3},{1,2},{2,1},{3,0},{4,7},{5,6},{6,5},{7,4},{8,11},{9,10},{10,... | collective-permute-start | bytes 3080 | tf_op jit(solution)/shard_map/ppermute | solution.py:303
  43.2 3.6 %collective-permute-start.13 = (f32[2,128]{1,0:T(2,128)S(1)}, f32[2,128]{1,0:T(2,128)S(1)}, u32[]{:S(2)}, u32[]{:S(2)}) collective-permute-start(f32[2,128]{1,0:T(2,128)S(1)} %get-tuple-element.42.refs_2_), channel_id=1, source_target_pairs={{0,2},{1,3},{2,0},{3,1},{4,6},{5,7},{6,4},{7,5},{8,10},{9,11},{10,... | collective-permute-start | bytes 3080 | tf_op jit(solution)/shard_map/ppermute | solution.py:303
  44.7 2.1 %collective-permute-start.12 = (f32[2,128]{1,0:T(2,128)S(1)}, f32[2,128]{1,0:T(2,128)S(1)}, u32[]{:S(2)}, u32[]{:S(2)}) collective-permute-start(f32[2,128]{1,0:T(2,128)S(1)} %get-tuple-element.42.refs_2_), channel_id=1, source_target_pairs={{0,1},{1,0},{2,3},{3,2},{4,5},{5,4},{6,7},{7,6},{8,9},{9,8},{10,11... | collective-permute-start | bytes 3080 | tf_op jit(solution)/shard_map/ppermute | solution.py:303
  48.3 3.2 %collective-permute-start.17 = (f32[2,512]{1,0:T(2,128)S(1)}, f32[2,512]{1,0:T(2,128)S(1)}, u32[]{:S(2)}, u32[]{:S(2)}) collective-permute-start(f32[2,512]{1,0:T(2,128)S(1)} %partial_weights.1.refs_0_), channel_id=1, source_target_pairs={{0,3},{1,2},{2,1},{3,0},{4,7},{5,6},{6,5},{7,4},{8,11},{9,10},{10,... | collective-permute-start | bytes 12296 | tf_op jit(solution)/shard_map/ppermute | solution.py:303
  48.9 3.6 %collective-permute-start.16 = (f32[2,512]{1,0:T(2,128)S(1)}, f32[2,512]{1,0:T(2,128)S(1)}, u32[]{:S(2)}, u32[]{:S(2)}) collective-permute-start(f32[2,512]{1,0:T(2,128)S(1)} %partial_weights.1.refs_0_), channel_id=1, source_target_pairs={{0,2},{1,3},{2,0},{3,1},{4,6},{5,7},{6,4},{7,5},{8,10},{9,11},{10,... | collective-permute-start | bytes 12296 | tf_op jit(solution)/shard_map/ppermute | solution.py:303
  50.4 2.1 %collective-permute-start.15 = (f32[2,512]{1,0:T(2,128)S(1)}, f32[2,512]{1,0:T(2,128)S(1)}, u32[]{:S(2)}, u32[]{:S(2)}) collective-permute-start(f32[2,512]{1,0:T(2,128)S(1)} %partial_weights.1.refs_0_), channel_id=1, source_target_pairs={{0,1},{1,0},{2,3},{3,2},{4,5},{5,4},{6,7},{7,6},{8,9},{9,8},{10,11... | collective-permute-start | bytes 12296 | tf_op jit(solution)/shard_map/ppermute | solution.py:303

commit v5 on v4

--- a/solution.py
+++ b/solution.py
@@ -27,9 +27,13 @@
 IN_HBM = pl.BlockSpec(memory_space=pltpu.HBM)
 
 
+def scale_rows(first, end):
+    return 16 * pl.cdiv(end - first, 16)
+
+
 def call(
     kernel, out_shape, name, flops, bytes_accessed, in_specs, scratch_shapes=(),
-    out_spec=IN_VMEM, limit=VMEM_LIMIT,
+    out_spec=IN_VMEM,
 ):
     return pl.pallas_call(
         kernel,
@@ -37,12 +41,16 @@
         in_specs=in_specs,
         out_specs=jax.tree.map(lambda _: out_spec, out_shape),
         scratch_shapes=scratch_shapes,
-        compiler_params=pltpu.CompilerParams(vmem_limit_bytes=limit),
+        compiler_params=pltpu.CompilerParams(vmem_limit_bytes=VMEM_LIMIT),
         cost_estimate=pl.CostEstimate(
             flops=flops, bytes_accessed=bytes_accessed, transcendentals=0
         ),
         name=name,
     )
+
+
+def in_hbm(value):
+    return pltpu.with_memory_space_constraint(value, pltpu.HBM)
 
 
 def f32(*shape):
@@ -90,86 +98,95 @@
         copy.wait()
 
 
-def gram_kernel(pieces, scale, me_ref, act_ref, grad_ref, own_ref, *refs):
-    sent_refs, (whole, tops) = refs[:-2], refs[-2:]
+def gram_kernel(pieces, messages, scale, me_ref, act_hbm, grad_hbm, act_ref, grad_ref, own_ref, *refs):
+    sent_refs, (whole, tops, sems) = refs[:-3], refs[-3:]
     rows = BLK // pieces
     me = me_ref[0]
-    first = 0
+    steps = []
+    for source, target in ((act_hbm, act_ref), (grad_hbm, grad_ref)):
+        for first in range(0, source.shape[1], GROUP * BLK):
+            columns = slice(first, first + GROUP * BLK)
+            copy = pltpu.make_async_copy(
+                source.at[:, columns], target.at[:, columns], sems.at[len(steps)]
+            )
+            copy.start()
+            steps.append((target, columns, copy))
     tops[...] = jnp.zeros_like(tops)
-    for ref in (act_ref, grad_ref):
-
-        @pl.loop(0, ref.shape[1] // BLK // GROUP)
-        def _(step, ref=ref, first=first):
-            for offset in range(GROUP):
-                block = first + step * GROUP + offset
-                at = pl.multiple_of((step * GROUP + offset) * BLK, BLK)
-                values = ref[:, pl.ds(at, BLK)]
-                gram = scale * lax.dot_general(
-                    values, values, contract_rows, preferred_element_type=jnp.float32
-                )
-                if pieces == 1:
-                    own_ref[block] = gram
-                    continue
-                whole[offset] = gram
-                top = jnp.maximum(jnp.max(jnp.abs(gram), axis=0, keepdims=True), SMALLEST)
-                top = (top * (1.0 + 2.0**-8)).astype(jnp.bfloat16).astype(jnp.float32)
-                tops[pl.ds(block, 1), :] = top
-                gain = CODE_TOP / top
-                own_ref[block] = whole[offset, pl.ds(pl.multiple_of(me * rows, rows), rows), :]
-                for shift in range(1, pieces):
-                    row = pl.multiple_of((me ^ shift) * rows, rows)
-                    place = pl.multiple_of(block * rows, rows)
-                    sent_refs[shift - 1][pl.ds(place, rows), :] = encode(
-                        whole[offset, pl.ds(row, rows), :] * gain
-                    )
-
-        first += ref.shape[1] // BLK
-    for sent_ref in sent_refs:
-        sent_ref[first * rows :, :] = tops[...].astype(jnp.bfloat16)
-
-
-def add_group(own_ref, sent_ref, tops, first):
-    rows = own_ref.shape[1]
-    for block in [first + offset for offset in range(GROUP)]:
-        values = decode(sent_ref[pl.ds(pl.multiple_of(block * rows, rows), rows), :])
-        yield block, own_ref[block] + values * tops[pl.ds(block, 1), :]
-
-
-def add_kernel(own_ref, sent_ref, sum_ref, tops):
+    for step, (ref, columns, copy) in enumerate(steps):
+        copy.wait()
+        for offset in range(GROUP):
+            block = step * GROUP + offset
+            at = columns.start + offset * BLK
+            values = ref[:, at : at + BLK]
+            gram = scale * lax.dot_general(
+                values, values, contract_rows, preferred_element_type=jnp.float32
+            )
+            if pieces == 1:
+                own_ref[block] = gram
+                continue
+            whole[offset] = gram
+            top = jnp.maximum(jnp.max(jnp.abs(gram), axis=0, keepdims=True), SMALLEST)
+            top = (top * (1.0 + 2.0**-8)).astype(jnp.bfloat16).astype(jnp.float32)
+            tops[block : block + 1, :] = top
+            gain = CODE_TOP / top
+            own_ref[block] = whole[offset, pl.ds(pl.multiple_of(me * rows, rows), rows), :]
+            for sent_ref, (mask, first, end) in zip(sent_refs, messages):
+                if first <= block < end:
+                    row = pl.multiple_of((me ^ mask) * rows, rows)
+                    place = slice((block - first) * rows, (block - first + 1) * rows)
+                    sent_ref[place, :] = encode(whole[offset, pl.ds(row, rows), :] * gain)
+    for sent_ref, (_, first, end) in zip(sent_refs, messages):
+        sent_ref[(end - first) * rows :, :] = tops[
+            first : first + scale_rows(first, end), :
+        ].astype(jnp.bfloat16)
+
+
+def add_group(messages, rows, own_ref, sent_refs, tops_refs, step):
+    for block in range(step * GROUP, (step + 1) * GROUP):
+        total = own_ref[block]
+        for (_, first, end), sent_ref, tops in zip(messages, sent_refs, tops_refs):
+            if first <= block < end:
+                at = block - first
+                values = decode(sent_ref[at * rows : (at + 1) * rows, :])
+                total = total + values * tops[at : at + 1, :]
+        yield block, total
+
+
+def load_tops(messages, rows, sent_refs, tops_refs):
+    for (_, first, end), sent_ref, tops in zip(messages, sent_refs, tops_refs):
+        tops[...] = sent_ref[(end - first) * rows :, :].astype(jnp.float32) * (1.0 / CODE_TOP)
+
+
+def add_kernel(messages, own_ref, *refs):
+    sent_refs, sum_ref, tops_refs = refs[: len(messages)], refs[len(messages)], refs[len(messages) + 1 :]
     blocks, rows, _ = own_ref.shape
-    tops[...] = sent_ref[blocks * rows :, :].astype(jnp.float32) * (1.0 / CODE_TOP)
-
-    @pl.loop(0, blocks // GROUP)
-    def _(step):
-        for block, total in add_group(own_ref, sent_ref, tops, step * GROUP):
+    load_tops(messages, rows, sent_refs, tops_refs)
+    for step in range(blocks // GROUP):
+        for block, total in add_group(messages, rows, own_ref, sent_refs, tops_refs, step):
             sum_ref[block] = total
 
 
-def last_add_kernel(own_ref, sent_ref, act_ref, grad_ref, tops, sums, sems):
+def last_add_kernel(messages, own_ref, *refs):
+    sent_refs, refs = refs[: len(messages)], refs[len(messages) :]
+    act_ref, grad_ref, *tops_refs, sums, sems = refs
     blocks, rows, _ = own_ref.shape
-    tops[...] = sent_ref[blocks * rows :, :].astype(jnp.float32) * (1.0 / CODE_TOP)
-    act_steps, grad_steps = act_ref.shape[0] // GROUP, grad_ref.shape[0] // GROUP
-
-    def write(ref, step, first):
-        return pltpu.make_async_copy(
-            sums.at[pl.ds((first + step) * GROUP, GROUP)],
-            ref.at[pl.ds(step * GROUP, GROUP)],
-            sems.at[first + step],
+    load_tops(messages, rows, sent_refs, tops_refs)
+    copies = []
+    for step in range(blocks // GROUP):
+        for block, total in add_group(messages, rows, own_ref, sent_refs, tops_refs, step):
+            sums[block] = total
+        first = step * GROUP
+        ref, at = act_ref, first
+        if first >= act_ref.shape[0]:
+            ref, at = grad_ref, first - act_ref.shape[0]
+        copies.append(
+            pltpu.make_async_copy(
+                sums.at[pl.ds(first, GROUP)], ref.at[pl.ds(at, GROUP)], sems.at[step]
+            )
         )
-
-    for ref, first, steps in ((act_ref, 0, act_steps), (grad_ref, act_steps, grad_steps)):
-
-        @pl.loop(0, steps)
-        def _(step, ref=ref, first=first):
-            for block, total in add_group(own_ref, sent_ref, tops, (first + step) * GROUP):
-                sums[block] = total
-            write(ref, step, first).start()
-
-    for ref, first, steps in ((act_ref, 0, act_steps), (grad_ref, act_steps, grad_steps)):
-
-        @pl.loop(0, steps)
-        def _(step, ref=ref, first=first):
-            write(ref, step, first).wait()
+        copies[-1].start()
+    for copy in copies:
+        copy.wait()
 
 
 def pairs_of(part, side, halves, act_ref, grad_ref):
@@ -333,8 +350,7 @@
         shard = call(
             half_kernel, bf16(blocks // 2, rows, BLK), "basis_half", 0, blocks * rows * BLK,
             [IN_SMEM, IN_HBM, IN_HBM], [pltpu.SemaphoreType.DMA((2,))],
-            limit=62 * 1024 * 1024,
-        )(side, basis_act, basis_grad)
+        )(side, in_hbm(basis_act), in_hbm(basis_grad))
     elif direct:
         shard = jnp.concatenate([basis_act, basis_grad])
     if direct:
@@ -344,23 +360,50 @@
         basis_grad = lax.all_gather(basis_grad, "dp", axis=1, tiled=True)
         received = []
 
-    scale_rows = 16 * pl.cdiv(blocks, 16)
-    message = blocks * rows + scale_rows
-    own, *sent = call(
-        functools.partial(gram_kernel, pieces, scale),
-        [f32(blocks, rows, BLK), *[bf16(message, BLK)] * (pieces - 1)],
+    early, beside, late = [], [], []
+    if pieces == 4:
+        early = [(1, 0, blocks)]
+        beside = [(3, 0, blocks)]
+        late = [(2, 0, blocks)]
+    elif pieces == 2:
+        late = [(1, 0, blocks)]
+    messages = early + beside + late
+    act_here, grad_here, own, *sent = call(
+        functools.partial(gram_kernel, pieces, messages, scale),
+        [
+            bf16(*activations.shape),
+            bf16(*gradients.shape),
+            f32(blocks, rows, BLK),
+            *[bf16((end - first) * rows + scale_rows(first, end), BLK) for _, first, end in messages],
+        ],
         "partial_gram", 4 * macs, input_bytes,
-        [IN_SMEM, IN_VMEM, IN_VMEM],
-        [pltpu.VMEM((GROUP, BLK, BLK), jnp.float32), pltpu.VMEM((scale_rows, BLK), jnp.float32)],
-    )(me, activations, gradients)
-    late = 2 if pieces > 2 else None
-    arrived = [swap(sent[mask - 1], "dp", mask) for mask in masks if mask != late]
+        [IN_SMEM, IN_HBM, IN_HBM],
+        [
+            pltpu.VMEM((GROUP, BLK, BLK), jnp.float32),
+            pltpu.VMEM((scale_rows(0, blocks), BLK), jnp.float32),
+            pltpu.SemaphoreType.DMA((blocks // GROUP,)),
+        ],
+    )(me, in_hbm(activations), in_hbm(gradients))
+    sent = dict(zip(messages, sent))
     if not direct:
         own = lax.psum_scatter(own, "dp", scatter_dimension=1, tiled=True)
 
+    def send(messages, done=None):
+        chunks = [sent[message] for message in messages]
+        if done is not None:
+            chunks = after(chunks, done)
+        return [swap(chunk, "dp", message[0]) for chunk, message in zip(chunks, messages)]
+
+    early_chunks, beside_chunks = send(early), send(beside)
+
     parts = [received]
     if halves == 2:
-        parts.append([swap(after([part], own)[0], "groups", 1) for part in received])
+        swapped, last = {}, ()
+        for mask in sorted(masks, key=lambda mask: (mask != 1, -mask)):
+            last = swap(after([received[mask - 1]], last)[0], "groups", 1)
+            swapped[mask] = last
+            last = (last, own)
+        parts.append([swapped[mask] for mask in masks])
     powers, sums = [], []
     for part, shards in enumerate(parts):
         power, *sums = call(
@@ -369,16 +412,16 @@
             "partial_eigen", 2 * macs // halves, input_bytes // halves,
             [IN_SMEM, IN_SMEM] + [IN_VMEM] * (4 + len(shards) + len(sums)),
             [pltpu.VMEM((blocks // halves // 2, PAIR, PAIR), jnp.bfloat16)],
-        )(me, side, activations, gradients, basis_act, basis_grad, *shards, *sums)
+        )(me, side, act_here, grad_here, basis_act, basis_grad, *shards, *sums)
         powers.append(power)
-    sums = share(after(sums, arrived)[0], "dp", direct)
-    if late:
-        arrived.append(swap(after([sent[late - 1]], sums)[0], "dp", late))
+    sums = share(after(sums, early_chunks)[0], "dp", direct)
+    sums = after(sums, beside_chunks)
     act_eigen, grad_eigen, eigen, totals = call(
         functools.partial(combine_kernel, halves),
         [f32(act_blocks, BLK), f32(grad_blocks, BLK), f32(blocks, BLK), f32(2, BLK)],
         "combine_eigen", 0, 4 * blocks * BLK * pieces, [IN_SMEM] + [IN_VMEM] * len(sums),
     )(side, *sums)
+    late_chunks = send(late, totals)
     totals = share(totals, "owner", direct)
     weights = call(
         functools.partial(weight_kernel, halves, act_blocks // halves),
@@ -396,22 +439,27 @@
         [IN_VMEM] * len(weights),
     )(*weights)
 
-    for chunk in arrived[:-1]:
+    def tops_of(messages):
+        return [pltpu.VMEM((scale_rows(first, end), BLK), jnp.float32) for _, first, end in messages]
+
+    if early:
         own = call(
-            add_kernel, f32(*own.shape), "add_chunk", 0, 10 * own.size, [IN_VMEM, IN_VMEM],
-            [pltpu.VMEM((scale_rows, BLK), jnp.float32)],
-        )(own, chunk)
-    if arrived:
+            functools.partial(add_kernel, early + beside), f32(*own.shape),
+            "add_chunks", 0, 12 * own.size, [IN_VMEM] * (1 + len(early + beside)),
+            tops_of(early + beside),
+        )(own, *early_chunks, *beside_chunks)
+    if late:
         covariance = call(
-            last_add_kernel, [f32(act_blocks, rows, BLK), f32(grad_blocks, rows, BLK)],
-            "add_last_chunk", 0, 10 * own.size, [IN_VMEM, IN_VMEM],
+            functools.partial(last_add_kernel, late),
+            [f32(act_blocks, rows, BLK), f32(grad_blocks, rows, BLK)],
+            "add_last_chunk", 0, 10 * own.size, [IN_VMEM] * (1 + len(late)),
             [
-                pltpu.VMEM((scale_rows, BLK), jnp.float32),
+                *tops_of(late),
                 pltpu.VMEM(own.shape, jnp.float32),
                 pltpu.SemaphoreType.DMA((blocks // GROUP,)),
             ],
             out_spec=pl.BlockSpec(memory_space=pl.ANY),
-        )(own, arrived[-1])
+        )(own, *late_chunks)
     else:
         covariance = own[:act_blocks], own[act_blocks:]
     return (

time: 56.3 us -> 53.3 us (0.947)
  local copies, waits for them, and re-layouts: 3.27 us -> 0.01 us
    unnamed x8 -> x4, local copies, waits for them, and re-layouts: 3.27 us -> 0.01 us
    pallas_call x1, Pallas kernels: 1.64 us -> 0.98 us  [local(): call(half_kernel, bf16(blocks // 2, rows, BLK), 'basis_half', 0, blocks *...]
    pallas_call x4 -> x3, Pallas kernels: 5.93 us -> 6.37 us  [the longest x1 4.7 us: local(): call(functools.partial(gram_kernel, pieces, messages, scale), [bf16(*acti...]
  transfers between devices with their start and end apart: 18 -> 18, of which waited for: 11 -> 9; matrix products, arithmetic and copies ran while one was open for 0% -> 0% of each run, Pallas kernels for 17% -> 18%
where the time goes in v5:
time: 53.3 us; the launch traced here: 53.2 us
  starting transfers between devices  23.8 us (45%)
  waiting for transfers between devices  16.6 us (31%)
  Pallas kernels  12 us (23%)
  between operations  0.73 us (1%)
    ppermute x18, starting transfers between devices, swap(): return lax.ppermute(value, axis, [(i, i ^ mask) for i in range(count)])  23.8 us
    ppermute x18, waiting for transfers between devices, swap(): return lax.ppermute(value, axis, [(i, i ^ mask) for i in range(count)])  16.6 us
    pallas_call x1, Pallas kernels, local(): call(functools.partial(gram_kernel, pieces, messages, scale), [bf16(*acti...  4.7 us
    pallas_call x2, Pallas kernels, local(): call(functools.partial(eigen_kernel, part, halves, pieces, scale), [f32(b...  1.95 us
    pallas_call x1, Pallas kernels, local(): call(functools.partial(weight_kernel, halves, act_blocks // halves), f32(...  1.48 us
  transfers between devices with their start and end apart: 18, of which 9 were waited for; matrix products, arithmetic and copies ran while one was open for 0% of the time, Pallas kernels for 18%

profile of v5, /device:TPU:0, one launch (start us, length us, event | category | flops | bytes accessed | tf_op | source)
XLA Modules:
  0.0 53.2 jit_solution(9928151830324861019)
XLA Ops:
  0.6 0.0 copy-start
  0.6 0.0 copy-start.1
  0.7 1.0 %basis_half.1 = bf16[18,32,128]{2,1,0:T(8,128)(2,1)S(1)} custom-call(s32[1]{0:T(128)} %bitcast.1.side_ref, bf16[8,32,128]{2,1,0:T(8,128)(2,1)} %act_own.3, bf16[28,32,128]{2,1,0:T(8,128)(2,1)} %grad_own.3), custom_call_target="tpu_custom_call" | custom-call | bytes 147456 | tf_op jit(solution)/shard_map/basis_half/pallas_call | solution.py:350
  1.6 3.1 %collective-permute-start.2 = (bf16[18,32,128]{2,1,0:T(8,128)(2,1)S(1)}, bf16[18,32,128]{2,1,0:T(8,128)(2,1)S(1)}, u32[]{:S(2)}, u32[]{:S(2)}) collective-permute-start(bf16[18,32,128]{2,1,0:T(8,128)(2,1)S(1)} %basis_half.1), channel_id=1, source_target_pairs={{0,4},{4,0},{8,12},{12,8},{1,5},{5,1},{9,13},{13,9},{2,6},{6,2},{1... | collective-permute-start | bytes 442376 | tf_op jit(solution)/shard_map/ppermute | solution.py:320
  4.7 2.5 %collective-permute-start.5 = (bf16[18,32,128]{2,1,0:T(8,128)(2,1)S(1)}, bf16[18,32,128]{2,1,0:T(8,128)(2,1)S(1)}, u32[]{:S(2)}, u32[]{:S(2)}) collective-permute-start(bf16[18,32,128]{2,1,0:T(8,128)(2,1)S(1)} %basis_half.1), channel_id=1, source_target_pairs={{0,12},{4,8},{8,4},{12,0},{1,13},{5,9},{9,5},{13,1},{2,14},{6,10},... | collective-permute-start | bytes 442376 | tf_op jit(solution)/shard_map/ppermute | solution.py:320
  7.2 1.6 %collective-permute-done.2.refs_0_ = bf16[18,32,128]{2,1,0:T(8,128)(2,1)S(1)} collective-permute-done((bf16[18,32,128]{2,1,0:T(8,128)(2,1)S(1)}, bf16[18,32,128]{2,1,0:T(8,128)(2,1)S(1)}, u32[]{:S(2)}, u32[]{:S(2)}) %collective-permute-start.2) | collective-permute-done | bytes 147488 | tf_op jit(solution)/shard_map/ppermute | solution.py:320
  8.8 1.5 %collective-permute-start.3 = (bf16[18,32,128]{2,1,0:T(8,128)(2,1)S(1)}, bf16[18,32,128]{2,1,0:T(8,128)(2,1)S(1)}, u32[]{:S(2)}, u32[]{:S(2)}) collective-permute-start(bf16[18,32,128]{2,1,0:T(8,128)(2,1)S(1)} %collective-permute-done.2.refs_0_), channel_id=1, source_target_pairs={{0,16},{16,0},{1,17},{17,1},{2,18},{18,2},{3,19},{19,3},{4,20},{20... | collective-permute-start | bytes 442376 | tf_op jit(solution)/shard_map/ppermute | solution.py:320
  10.3 3.7 %collective-permute-start.4 = (bf16[18,32,128]{2,1,0:T(8,128)(2,1)S(1)}, bf16[18,32,128]{2,1,0:T(8,128)(2,1)S(1)}, u32[]{:S(2)}, u32[]{:S(2)}) collective-permute-start(bf16[18,32,128]{2,1,0:T(8,128)(2,1)S(1)} %basis_half.1), channel_id=1, source_target_pairs={{0,8},{4,12},{8,0},{12,4},{1,9},{5,13},{9,1},{13,5},{2,10},{6,14},... | collective-permute-start | bytes 442376 | tf_op jit(solution)/shard_map/ppermute | solution.py:320
  14.0 4.7 %partial_gram.1 = (bf16[512,1024]{1,0:T(8,128)(2,1)S(1)}, bf16[512,3584]{1,0:T(8,128)(2,1)S(1)}, f32[36,32,128]{2,1,0:T(8,128)S(1)}, bf16[1200,128]{1,0:T(8,128)...) custom-call(s32[1]{0:T(128)} %bitcast.me_ref, bf16[512,1024]{1,0:T(8,128)(2,1)} %act_hbm.1, ...), custom_call_target="tpu_custom_call" | custom-call | flops 1207959552 | bytes 4718592 | tf_op jit(solution)/shard_map/partial_gram/pallas_call | solution.py:371
  18.7 0.0 collective-permute-done.5.refs_2_
  18.7 0.0 collective-permute-done.3.refs_0_
  18.7 0.6 %collective-permute-start.6 = (bf16[18,32,128]{2,1,0:T(8,128)(2,1)S(1)}, bf16[18,32,128]{2,1,0:T(8,128)(2,1)S(1)}, u32[]{:S(2)}, u32[]{:S(2)}) collective-permute-start(bf16[18,32,128]{2,1,0:T(8,128)(2,1)S(1)} %collective-permute-done.5.refs_2_), channel_id=1, source_target_pairs={{0,16},{16,0},{1,17},{17,1},{2,18},{18,2},{3,19},{19,3},{4,20},{20... | collective-permute-start | bytes 442376 | tf_op jit(solution)/shard_map/ppermute | solution.py:320
  19.3 3.6 %collective-permute-start = (bf16[1200,128]{1,0:T(8,128)(2,1)S(1)}, bf16[1200,128]{1,0:T(8,128)(2,1)S(1)}, u32[]{:S(2)}, u32[]{:S(2)}) collective-permute-start(bf16[1200,128]{1,0:T(8,128)(2,1)S(1)} %get-tuple-element.30), channel_id=1, source_target_pairs={{0,4},{4,0},{8,12},{12,8},{1,5},{5,1},{9,13},{13,9},{2,6},{6,2},{1... | collective-permute-start | bytes 921608 | tf_op jit(solution)/shard_map/ppermute | solution.py:320
  22.9 0.5 collective-permute-start.1
  23.4 0.0 collective-permute-done.4.refs_1_
  23.4 1.5 %collective-permute-done.6.refs_2_ = bf16[18,32,128]{2,1,0:T(8,128)(2,1)S(1)} collective-permute-done((bf16[18,32,128]{2,1,0:T(8,128)(2,1)S(1)}, bf16[18,32,128]{2,1,0:T(8,128)(2,1)S(1)}, u32[]{:S(2)}, u32[]{:S(2)}) %collective-permute-start.6) | collective-permute-done | bytes 147488 | tf_op jit(solution)/shard_map/ppermute | solution.py:320
  24.9 0.0 collective-permute-start.7
  24.9 0.0 copy-done
  24.9 0.0 copy-done.1
  24.9 1.0 %partial_eigen.2 = (f32[9,512,256]{2,1,0:T(8,128)S(1)}, f32[18,128]{1,0:T(8,128)S(1)}) custom-call(s32[1]{0:T(128)} %bitcast.me_ref, s32[1]{0:T(128)} %bitcast.1.side_ref, bf16[512,1024]{1,0:T(8,128)(2,1)S(1)} %get-tuple-element.33.act_ref, bf16[512,3584]{1,0:T(8,128)(2,1)S(1)} %get-tuple-element.34.grad_ref, bf16[8,32,128]{2,1,0:T(8,128)(2,1)S(1)} %copy-done.1, ...), custom_call_target="tpu_custom_call" | custom-call | flops 301989888 | bytes 2359296 | tf_op jit(solution)/shard_map/partial_eigen/pallas_call | solution.py:409
  25.9 4.1 %collective-permute-done.7.refs_1_ = bf16[18,32,128]{2,1,0:T(8,128)(2,1)S(1)} collective-permute-done((bf16[18,32,128]{2,1,0:T(8,128)(2,1)S(1)}, bf16[18,32,128]{2,1,0:T(8,128)(2,1)S(1)}, u32[]{:S(2)}, u32[]{:S(2)}) %collective-permute-start.7) | collective-permute-done | bytes 147488 | tf_op jit(solution)/shard_map/ppermute | solution.py:320
  30.0 1.0 %partial_eigen.3 = (f32[9,512,256]{2,1,0:T(8,128)S(1)}, f32[36,128]{1,0:T(8,128)S(1)}) custom-call(s32[1]{0:T(128)} %bitcast.me_ref, s32[1]{0:T(128)} %bitcast.1.side_ref, bf16[512,1024]{1,0:T(8,128)(2,1)S(1)} %get-tuple-element.33.act_ref, bf16[512,3584]{1,0:T(8,128)(2,1)S(1)} %get-tuple-element.34.grad_ref, bf16[8,32,128]{2,1,0:T(8,128)(2,1)S(1)} %copy-done.1, ...), custom_call_target="tpu_custom_call" | custom-call | flops 301989888 | bytes 2359296 | tf_op jit(solution)/shard_map/partial_eigen/pallas_call | solution.py:409
  31.0 0.0 collective-permute-done.refs_0_
  31.0 3.3 %collective-permute-start.10 = (f32[36,128]{1,0:T(8,128)S(1)}, f32[36,128]{1,0:T(8,128)S(1)}, u32[]{:S(2)}, u32[]{:S(2)}) collective-permute-start(f32[36,128]{1,0:T(8,128)S(1)} %get-tuple-element.40.refs_0_), channel_id=1, source_target_pairs={{0,12},{4,8},{8,4},{12,0},{1,13},{5,9},{9,5},{13,1},{2,14},{6,10},... | collective-permute-start | bytes 55304 | tf_op jit(solution)/shard_map/ppermute | solution.py:320
  34.3 0.8 %collective-permute-start.9 = (f32[36,128]{1,0:T(8,128)S(1)}, f32[36,128]{1,0:T(8,128)S(1)}, u32[]{:S(2)}, u32[]{:S(2)}) collective-permute-start(f32[36,128]{1,0:T(8,128)S(1)} %get-tuple-element.40.refs_0_), channel_id=1, source_target_pairs={{0,8},{4,12},{8,0},{12,4},{1,9},{5,13},{9,1},{13,5},{2,10},{6,14},... | collective-permute-start | bytes 55304 | tf_op jit(solution)/shard_map/ppermute | solution.py:320
  35.1 0.4 collective-permute-start.8
  35.5 0.0 collective-permute-done.1.refs_1_
  35.5 1.2 %collective-permute-done.10.refs_3_ = f32[36,128]{1,0:T(8,128)S(1)} collective-permute-done((f32[36,128]{1,0:T(8,128)S(1)}, f32[36,128]{1,0:T(8,128)S(1)}, u32[]{:S(2)}, u32[]{:S(2)}) %collective-permute-start.10) | collective-permute-done | bytes 18464 | tf_op jit(solution)/shard_map/ppermute | solution.py:320
  36.7 4.9 %collective-permute-done.9.refs_2_ = f32[36,128]{1,0:T(8,128)S(1)} collective-permute-done((f32[36,128]{1,0:T(8,128)S(1)}, f32[36,128]{1,0:T(8,128)S(1)}, u32[]{:S(2)}, u32[]{:S(2)}) %collective-permute-start.9) | collective-permute-done | bytes 18464 | tf_op jit(solution)/shard_map/ppermute | solution.py:320
  41.6 0.0 collective-permute-done.8.refs_1_
  41.6 0.6 %combine_eigen.1 = (f32[8,128]{1,0:T(8,128)}, f32[28,128]{1,0:T(8,128)}, f32[36,128]{1,0:T(8,128)S(1)}, f32[2,128]{1,0:T(2,128)S(1)}) custom-call(s32[1]{0:T(128)} %bitcast.1.side_ref, f32[36,128]{1,0:T(8,128)S(1)} %get-tuple-element.40.refs_0_, f32[36,128]{1,0:T(8,128)S(1)} %collective-permute-done.8.refs_1_, f32[36,128]{1,0:T(8,128)S(1)} %collective-permute-done.9.refs_2_, ...), custom_call_target="tpu_custom_call" | custom-call | bytes 73728 | tf_op jit(solution)/shard_map/combine_eigen/pallas_call | solution.py:419
  42.2 0.0 collective-permute-start.11
  42.2 0.0 collective-permute-start.14
  42.2 1.6 %collective-permute-start.13 = (f32[2,128]{1,0:T(2,128)S(1)}, f32[2,128]{1,0:T(2,128)S(1)}, u32[]{:S(2)}, u32[]{:S(2)}) collective-permute-start(f32[2,128]{1,0:T(2,128)S(1)} %get-tuple-element.44.refs_2_), channel_id=1, source_target_pairs={{0,2},{1,3},{2,0},{3,1},{4,6},{5,7},{6,4},{7,5},{8,10},{9,11},{10,... | collective-permute-start | bytes 3080 | tf_op jit(solution)/shard_map/ppermute | solution.py:320
  43.8 0.3 collective-permute-start.12
  44.1 1.1 %collective-permute-done.14.refs_5_ = f32[2,128]{1,0:T(2,128)S(1)} collective-permute-done((f32[2,128]{1,0:T(2,128)S(1)}, f32[2,128]{1,0:T(2,128)S(1)}, u32[]{:S(2)}, u32[]{:S(2)}) %collective-permute-start.14) | collective-permute-done | bytes 1056 | tf_op jit(solution)/shard_map/ppermute | solution.py:320
  45.2 0.6 %collective-permute-done.13.refs_4_ = f32[2,128]{1,0:T(2,128)S(1)} collective-permute-done((f32[2,128]{1,0:T(2,128)S(1)}, f32[2,128]{1,0:T(2,128)S(1)}, u32[]{:S(2)}, u32[]{:S(2)}) %collective-permute-start.13) | collective-permute-done | bytes 1056 | tf_op jit(solution)/shard_map/ppermute | solution.py:320
  45.9 0.0 collective-permute-done.12.refs_3_
  45.9 1.5 %partial_weights.1.refs_0_ = f32[2,512]{1,0:T(2,128)S(1)} custom-call(f32[36,128]{1,0:T(8,128)S(1)} %get-tuple-element.50.eigen_ref, f32[9,512,256]{2,1,0:T(8,128)S(1)} %get-tuple-element.51.refs_0_, f32[9,512,256]{2,1,0:T(8,128)S(1)} %get-tuple-element.52.refs_1_, f32[2,128]{1,0:T(2,128)S(1)} %get-tuple-element.44.refs_2_, ...), custom_call_target="tpu_custom_call" | custom-call | bytes 9437184 | tf_op jit(solution)/shard_map/partial_weights/pallas_call | solution.py:426
  47.3 0.6 %collective-permute-start.17 = (f32[2,512]{1,0:T(2,128)S(1)}, f32[2,512]{1,0:T(2,128)S(1)}, u32[]{:S(2)}, u32[]{:S(2)}) collective-permute-start(f32[2,512]{1,0:T(2,128)S(1)} %partial_weights.1.refs_0_), channel_id=1, source_target_pairs={{0,3},{1,2},{2,1},{3,0},{4,7},{5,6},{6,5},{7,4},{8,11},{9,10},{10,... | collective-permute-start | bytes 12296 | tf_op jit(solution)/shard_map/ppermute | solution.py:320
  48.0 1.5 %collective-permute-start.16 = (f32[2,512]{1,0:T(2,128)S(1)}, f32[2,512]{1,0:T(2,128)S(1)}, u32[]{:S(2)}, u32[]{:S(2)}) collective-permute-start(f32[2,512]{1,0:T(2,128)S(1)} %partial_weights.1.refs_0_), channel_id=1, source_target_pairs={{0,2},{1,3},{2,0},{3,1},{4,6},{5,7},{6,4},{7,5},{8,10},{9,11},{10,... | collective-permute-start | bytes 12296 | tf_op jit(solution)/shard_map/ppermute | solution.py:320
  49.4 0.0 collective-permute-start.15
  49.4 0.6 %add_chunks.1.own_ref = f32[36,32,128]{2,1,0:T(8,128)S(1)} custom-call(f32[36,32,128]{2,1,0:T(8,128)S(1)} %get-tuple-element.29.own_ref, bf16[1200,128]{1,0:T(8,128)(2,1)S(1)} %collective-permute-done.refs_0_, bf16[1200,128]{1,0:T(8,128)(2,1)S(1)} %collective-permute-done.1.refs_1_), custom_call_target="tpu_custom_call" | custom-call | bytes 1769472 | tf_op jit(solution)/shard_map/add_chunks/pallas_call | solution.py:446
  50.1 0.3 collective-permute-done.17.refs_3_
  50.4 1.2 %collective-permute-done.16.refs_2_ = f32[2,512]{1,0:T(2,128)S(1)} collective-permute-done((f32[2,512]{1,0:T(2,128)S(1)}, f32[2,512]{1,0:T(2,128)S(1)}, u32[]{:S(2)}, u32[]{:S(2)}) %collective-permute-start.16) | collective-permute-done | bytes 4128 | tf_op jit(solution)/shard_map/ppermute | solution.py:320
  51.6 0.0 collective-permute-done.15.refs_1_
  51.6 0.6 %token_scores.1 = f32[1,512]{1,0:T(1,128)} custom-call(f32[2,512]{1,0:T(2,128)S(1)} %partial_weights.1.refs_0_, f32[2,512]{1,0:T(2,128)S(1)} %collective-permute-done.15.refs_1_, f32[2,512]{1,0:T(2,128)S(1)} %collective-permute-done.16.refs_2_, f32[2,512]{1,0:T(2,128)S(1)} %collective-permute-done.17.refs_3_), custom_call_target="tpu_custom_call" | custom-call | bytes 16384 | tf_op jit(solution)/shard_map/token_scores/pallas_call | solution.py:437
  52.2 0.0 collective-permute-done.11.refs_0_
  52.2 1.0 %add_last_chunk.1 = (f32[8,32,128]{2,1,0:T(8,128)}, f32[28,32,128]{2,1,0:T(8,128)}) custom-call(f32[36,32,128]{2,1,0:T(8,128)S(1)} %add_chunks.1.own_ref, bf16[1200,128]{1,0:T(8,128)(2,1)S(1)} %collective-permute-done.11.refs_0_), custom_call_target="tpu_custom_call" | custom-call | bytes 1474560 | tf_op jit(solution)/shard_map/add_last_chunk/pallas_call | solution.py:452
Async XLA Ops:
  0.6 24.3 %copy-start = (bf16[28,32,128]{2,1,0:T(8,128)(2,1)S(1)}, bf16[28,32,128]{2,1,0:T(8,128)(2,1)}, u32[]{:S(2)}) copy-start(bf16[28,32,128]{2,1,0:T(8,128)(2,1)} %grad_own.3) | copy-start | bytes 688132
  0.6 24.3 %copy-start.1 = (bf16[8,32,128]{2,1,0:T(8,128)(2,1)S(1)}, bf16[8,32,128]{2,1,0:T(8,128)(2,1)}, u32[]{:S(2)}) copy-start(bf16[8,32,128]{2,1,0:T(8,128)(2,1)} %act_own.3) | copy-start | bytes 196612
  1.6 7.2 %collective-permute-start.2 = (bf16[18,32,128]{2,1,0:T(8,128)(2,1)S(1)}, bf16[18,32,128]{2,1,0:T(8,128)(2,1)S(1)}, u32[]{:S(2)}, u32[]{:S(2)}) collective-permute-start(bf16[18,32,128]{2,1,0:T(8,128)(2,1)S(1)} %basis_half.1), channel_id=1, source_target_pairs={{0,4},{4,0},{8,12},{12,8},{1,5},{5,1},{9,13},{13,9},{2,6},{6,2},{1... | collective-permute-start | bytes 442376 | tf_op jit(solution)/shard_map/ppermute | solution.py:320
  4.7 14.0 %collective-permute-start.5 = (bf16[18,32,128]{2,1,0:T(8,128)(2,1)S(1)}, bf16[18,32,128]{2,1,0:T(8,128)(2,1)S(1)}, u32[]{:S(2)}, u32[]{:S(2)}) collective-permute-start(bf16[18,32,128]{2,1,0:T(8,128)(2,1)S(1)} %basis_half.1), channel_id=1, source_target_pairs={{0,12},{4,8},{8,4},{12,0},{1,13},{5,9},{9,5},{13,1},{2,14},{6,10},... | collective-permute-start | bytes 442376 | tf_op jit(solution)/shard_map/ppermute | solution.py:320
  8.8 9.9 %collective-permute-start.3 = (bf16[18,32,128]{2,1,0:T(8,128)(2,1)S(1)}, bf16[18,32,128]{2,1,0:T(8,128)(2,1)S(1)}, u32[]{:S(2)}, u32[]{:S(2)}) collective-permute-start(bf16[18,32,128]{2,1,0:T(8,128)(2,1)S(1)} %collective-permute-done.2.refs_0_), channel_id=1, source_target_pairs={{0,16},{16,0},{1,17},{17,1},{2,18},{18,2},{3,19},{19,3},{4,20},{20... | collective-permute-start | bytes 442376 | tf_op jit(solution)/shard_map/ppermute | solution.py:320
  10.3 13.1 %collective-permute-start.4 = (bf16[18,32,128]{2,1,0:T(8,128)(2,1)S(1)}, bf16[18,32,128]{2,1,0:T(8,128)(2,1)S(1)}, u32[]{:S(2)}, u32[]{:S(2)}) collective-permute-start(bf16[18,32,128]{2,1,0:T(8,128)(2,1)S(1)} %basis_half.1), channel_id=1, source_target_pairs={{0,8},{4,12},{8,0},{12,4},{1,9},{5,13},{9,1},{13,5},{2,10},{6,14},... | collective-permute-start | bytes 442376 | tf_op jit(solution)/shard_map/ppermute | solution.py:320
  18.7 6.2 %collective-permute-start.6 = (bf16[18,32,128]{2,1,0:T(8,128)(2,1)S(1)}, bf16[18,32,128]{2,1,0:T(8,128)(2,1)S(1)}, u32[]{:S(2)}, u32[]{:S(2)}) collective-permute-start(bf16[18,32,128]{2,1,0:T(8,128)(2,1)S(1)} %collective-permute-done.5.refs_2_), channel_id=1, source_target_pairs={{0,16},{16,0},{1,17},{17,1},{2,18},{18,2},{3,19},{19,3},{4,20},{20... | collective-permute-start | bytes 442376 | tf_op jit(solution)/shard_map/ppermute | solution.py:320
  19.3 11.7 %collective-permute-start = (bf16[1200,128]{1,0:T(8,128)(2,1)S(1)}, bf16[1200,128]{1,0:T(8,128)(2,1)S(1)}, u32[]{:S(2)}, u32[]{:S(2)}) collective-permute-start(bf16[1200,128]{1,0:T(8,128)(2,1)S(1)} %get-tuple-element.30), channel_id=1, source_target_pairs={{0,4},{4,0},{8,12},{12,8},{1,5},{5,1},{9,13},{13,9},{2,6},{6,2},{1... | collective-permute-start | bytes 921608 | tf_op jit(solution)/shard_map/ppermute | solution.py:320
  22.9 12.6 %collective-permute-start.1 = (bf16[1200,128]{1,0:T(8,128)(2,1)S(1)}, bf16[1200,128]{1,0:T(8,128)(2,1)S(1)}, u32[]{:S(2)}, u32[]{:S(2)}) collective-permute-start(bf16[1200,128]{1,0:T(8,128)(2,1)S(1)} %get-tuple-element.31), channel_id=1, source_target_pairs={{0,12},{4,8},{8,4},{12,0},{1,13},{5,9},{9,5},{13,1},{2,14},{6,10},... | collective-permute-start | bytes 921608 | tf_op jit(solution)/shard_map/ppermute | solution.py:320
  24.9 5.1 %collective-permute-start.7 = (bf16[18,32,128]{2,1,0:T(8,128)(2,1)S(1)}, bf16[18,32,128]{2,1,0:T(8,128)(2,1)S(1)}, u32[]{:S(2)}, u32[]{:S(2)}) collective-permute-start(bf16[18,32,128]{2,1,0:T(8,128)(2,1)S(1)} %collective-permute-done.4.refs_1_), channel_id=1, source_target_pairs={{0,16},{16,0},{1,17},{17,1},{2,18},{18,2},{3,19},{19,3},{4,20},{20... | collective-permute-start | bytes 442376 | tf_op jit(solution)/shard_map/ppermute | solution.py:320
  31.0 5.7 %collective-permute-start.10 = (f32[36,128]{1,0:T(8,128)S(1)}, f32[36,128]{1,0:T(8,128)S(1)}, u32[]{:S(2)}, u32[]{:S(2)}) collective-permute-start(f32[36,128]{1,0:T(8,128)S(1)} %get-tuple-element.40.refs_0_), channel_id=1, source_target_pairs={{0,12},{4,8},{8,4},{12,0},{1,13},{5,9},{9,5},{13,1},{2,14},{6,10},... | collective-permute-start | bytes 55304 | tf_op jit(solution)/shard_map/ppermute | solution.py:320
  34.3 7.3 %collective-permute-start.9 = (f32[36,128]{1,0:T(8,128)S(1)}, f32[36,128]{1,0:T(8,128)S(1)}, u32[]{:S(2)}, u32[]{:S(2)}) collective-permute-start(f32[36,128]{1,0:T(8,128)S(1)} %get-tuple-element.40.refs_0_), channel_id=1, source_target_pairs={{0,8},{4,12},{8,0},{12,4},{1,9},{5,13},{9,1},{13,5},{2,10},{6,14},... | collective-permute-start | bytes 55304 | tf_op jit(solution)/shard_map/ppermute | solution.py:320
  35.1 6.5 %collective-permute-start.8 = (f32[36,128]{1,0:T(8,128)S(1)}, f32[36,128]{1,0:T(8,128)S(1)}, u32[]{:S(2)}, u32[]{:S(2)}) collective-permute-start(f32[36,128]{1,0:T(8,128)S(1)} %get-tuple-element.40.refs_0_), channel_id=1, source_target_pairs={{0,4},{4,0},{8,12},{12,8},{1,5},{5,1},{9,13},{13,9},{2,6},{6,2},{1... | collective-permute-start | bytes 55304 | tf_op jit(solution)/shard_map/ppermute | solution.py:320
  42.2 9.9 %collective-permute-start.11 = (bf16[1200,128]{1,0:T(8,128)(2,1)S(1)}, bf16[1200,128]{1,0:T(8,128)(2,1)S(1)}, u32[]{:S(2)}, u32[]{:S(2)}) collective-permute-start(bf16[1200,128]{1,0:T(8,128)(2,1)S(1)} %get-tuple-element.45), channel_id=1, source_target_pairs={{0,8},{4,12},{8,0},{12,4},{1,9},{5,13},{9,1},{13,5},{2,10},{6,14},... | collective-permute-start | bytes 921608 | tf_op jit(solution)/shard_map/ppermute | solution.py:320
  42.2 3.0 %collective-permute-start.14 = (f32[2,128]{1,0:T(2,128)S(1)}, f32[2,128]{1,0:T(2,128)S(1)}, u32[]{:S(2)}, u32[]{:S(2)}) collective-permute-start(f32[2,128]{1,0:T(2,128)S(1)} %get-tuple-element.44.refs_2_), channel_id=1, source_target_pairs={{0,3},{1,2},{2,1},{3,0},{4,7},{5,6},{6,5},{7,4},{8,11},{9,10},{10,... | collective-permute-start | bytes 3080 | tf_op jit(solution)/shard_map/ppermute | solution.py:320
  42.2 3.6 %collective-permute-start.13 = (f32[2,128]{1,0:T(2,128)S(1)}, f32[2,128]{1,0:T(2,128)S(1)}, u32[]{:S(2)}, u32[]{:S(2)}) collective-permute-start(f32[2,128]{1,0:T(2,128)S(1)} %get-tuple-element.44.refs_2_), channel_id=1, source_target_pairs={{0,2},{1,3},{2,0},{3,1},{4,6},{5,7},{6,4},{7,5},{8,10},{9,11},{10,... | collective-permute-start | bytes 3080 | tf_op jit(solution)/shard_map/ppermute | solution.py:320
  43.8 2.1 %collective-permute-start.12 = (f32[2,128]{1,0:T(2,128)S(1)}, f32[2,128]{1,0:T(2,128)S(1)}, u32[]{:S(2)}, u32[]{:S(2)}) collective-permute-start(f32[2,128]{1,0:T(2,128)S(1)} %get-tuple-element.44.refs_2_), channel_id=1, source_target_pairs={{0,1},{1,0},{2,3},{3,2},{4,5},{5,4},{6,7},{7,6},{8,9},{9,8},{10,11... | collective-permute-start | bytes 3080 | tf_op jit(solution)/shard_map/ppermute | solution.py:320
  47.3 3.1 %collective-permute-start.17 = (f32[2,512]{1,0:T(2,128)S(1)}, f32[2,512]{1,0:T(2,128)S(1)}, u32[]{:S(2)}, u32[]{:S(2)}) collective-permute-start(f32[2,512]{1,0:T(2,128)S(1)} %partial_weights.1.refs_0_), channel_id=1, source_target_pairs={{0,3},{1,2},{2,1},{3,0},{4,7},{5,6},{6,5},{7,4},{8,11},{9,10},{10,... | collective-permute-start | bytes 12296 | tf_op jit(solution)/shard_map/ppermute | solution.py:320
  48.0 3.6 %collective-permute-start.16 = (f32[2,512]{1,0:T(2,128)S(1)}, f32[2,512]{1,0:T(2,128)S(1)}, u32[]{:S(2)}, u32[]{:S(2)}) collective-permute-start(f32[2,512]{1,0:T(2,128)S(1)} %partial_weights.1.refs_0_), channel_id=1, source_target_pairs={{0,2},{1,3},{2,0},{3,1},{4,6},{5,7},{6,4},{7,5},{8,10},{9,11},{10,... | collective-permute-start | bytes 12296 | tf_op jit(solution)/shard_map/ppermute | solution.py:320
  49.4 2.1 %collective-permute-start.15 = (f32[2,512]{1,0:T(2,128)S(1)}, f32[2,512]{1,0:T(2,128)S(1)}, u32[]{:S(2)}, u32[]{:S(2)}) collective-permute-start(f32[2,512]{1,0:T(2,128)S(1)} %partial_weights.1.refs_0_), channel_id=1, source_target_pairs={{0,1},{1,0},{2,3},{3,2},{4,5},{5,4},{6,7},{7,6},{8,9},{9,8},{10,11... | collective-permute-start | bytes 12296 | tf_op jit(solution)/shard_map/ppermute | solution.py:320

commit v6 on v5

--- a/solution.py
+++ b/solution.py
@@ -77,21 +77,24 @@
     return jnp.where(coded > 0.0, root, jnp.where(coded < 0.0, -root, 0.0))
 
 
-def half_kernel(side_ref, act_ref, grad_ref, half_ref, sems):
+def pack_kernel(side_ref, act_ref, grad_ref, *refs):
+    *out_refs, sems = refs
     side = side_ref[0]
-    act_half, grad_half = act_ref.shape[0] // 2, grad_ref.shape[0] // 2
-    copies = [
-        pltpu.make_async_copy(
-            act_ref.at[pl.ds(side * act_half, act_half)],
-            half_ref.at[pl.ds(0, act_half)],
-            sems.at[0],
-        ),
-        pltpu.make_async_copy(
-            grad_ref.at[pl.ds(side * grad_half, grad_half)],
-            half_ref.at[pl.ds(act_half, grad_half)],
-            sems.at[1],
-        ),
-    ]
+    blocks = out_refs[0].shape[0]
+    copies = []
+    for out_ref in reversed(out_refs):
+        halves = blocks // out_ref.shape[0]
+        at = 0
+        for ref in (act_ref, grad_ref):
+            count = ref.shape[0] // halves
+            copies.append(
+                pltpu.make_async_copy(
+                    ref.at[pl.ds(side * count if halves > 1 else 0, count)],
+                    out_ref.at[pl.ds(at, count)],
+                    sems.at[len(copies)],
+                )
+            )
+            at += count
     for copy in copies:
         copy.start()
     for copy in copies:
@@ -197,36 +200,31 @@
             yield ref, pl.multiple_of((half * count + pair) * PAIR, PAIR)
 
 
-def eigen_kernel(
-    part, halves, pieces, scale, me_ref, side_ref, act_ref, grad_ref, act_own, grad_own, *refs
-):
-    *received, power_ref, sums_ref, basis_ref = refs
+def eigen_kernel(part, halves, masks, pieces, scale, me_ref, side_ref, act_ref, grad_ref, *refs):
+    *shard_refs, power_ref, sums_ref, basis_ref = refs
     me, side = me_ref[0], side_ref[0]
     rows = BLK // pieces
     done = 0
     if part:
-        *received, done_ref = received
+        *shard_refs, done_ref = shard_refs
         done = done_ref.shape[0]
         sums_ref[:done] = done_ref[...]
     half = lax.rem(side + part, halves)
-    act_half, grad_half = act_own.shape[0] // halves, grad_own.shape[0] // halves
+    act_half = act_ref.shape[1] // BLK // halves
+    grad_half = grad_ref.shape[1] // BLK // halves
     basis_ref[...] = jnp.zeros_like(basis_ref)
-
-    def put(shard_of, piece):
+    for mask, ref in zip(masks, shard_refs):
+        whole = halves > 1 and ref.shape[0] == halves * (act_half + grad_half)
         for block in range(act_half + grad_half):
+            at = block
+            if whole and block < act_half:
+                at = half * act_half + block
+            elif whole:
+                at = (halves - 1) * act_half + half * grad_half + block
             corner = block % 2
-            row = pl.multiple_of(corner * BLK + piece * rows, rows)
+            row = pl.multiple_of(corner * BLK + (me ^ mask) * rows, rows)
             columns = slice(corner * BLK, (corner + 1) * BLK)
-            basis_ref[block // 2, pl.ds(row, rows), columns] = shard_of(block)
-
-    def own_shard(block):
-        if block < act_half:
-            return act_own[half * act_half + block]
-        return grad_own[half * grad_half + block - act_half]
-
-    put(own_shard, me)
-    for index, ref in enumerate(received):
-        put(lambda block, ref=ref: ref[block], me ^ (index + 1))
+            basis_ref[block // 2, pl.ds(row, rows), columns] = ref[at]
 
     for pair, (ref, column) in enumerate(pairs_of(part, side, halves, act_ref, grad_ref)):
         projected = lax.dot_general(
@@ -338,27 +336,29 @@
     scale = 1.0 / (tokens * dp)
     direct = dp in (2, 4) and owners in (1, 2, 4)
     pieces = dp if direct else 1
-    halves = 2 if direct and lax.axis_size("groups") == 2 else 1
+    halves = 2 if pieces == 4 and lax.axis_size("groups") == 2 else 1
     rows = BLK // pieces
     me = jnp.full((1,), lax.axis_index("dp") if direct else 0, jnp.int32)
     side = jnp.full((1,), lax.axis_index("groups"), jnp.int32)
     macs = tokens * blocks * BLK * BLK
     input_bytes = 2 * tokens * blocks * BLK
-    masks = range(1, pieces)
-
-    if halves == 2:
-        shard = call(
-            half_kernel, bf16(blocks // 2, rows, BLK), "basis_half", 0, blocks * rows * BLK,
-            [IN_SMEM, IN_HBM, IN_HBM], [pltpu.SemaphoreType.DMA((2,))],
+    if direct:
+        shards = call(
+            pack_kernel,
+            [bf16(blocks // part, rows, BLK) for part in range(1, halves + 1)],
+            "pack_basis", 0, 2 * blocks * rows * BLK,
+            [IN_SMEM, IN_HBM, IN_HBM], [pltpu.SemaphoreType.DMA((2 * halves,))],
         )(side, in_hbm(basis_act), in_hbm(basis_grad))
-    elif direct:
-        shard = jnp.concatenate([basis_act, basis_grad])
-    if direct:
-        received = [swap(shard, "dp", mask) for mask in masks]
+        near = [shards[0], swap(shards[0], "dp", 1)]
+        far = {mask: swap(shards[-1], "dp", mask) for mask in range(pieces - 1, 1, -1)}
     else:
-        basis_act = lax.all_gather(basis_act, "dp", axis=1, tiled=True)
-        basis_grad = lax.all_gather(basis_grad, "dp", axis=1, tiled=True)
-        received = []
+        near = [
+            jnp.concatenate(
+                [lax.all_gather(part, "dp", axis=1, tiled=True) for part in (basis_act, basis_grad)]
+            )
+        ]
+        far = {}
+    masks = [*range(len(near)), *far]
 
     early, beside, late = [], [], []
     if pieces == 4:
@@ -396,23 +396,21 @@
 
     early_chunks, beside_chunks = send(early), send(beside)
 
-    parts = [received]
+    parts = [[*near, *far.values()]]
     if halves == 2:
-        swapped, last = {}, ()
-        for mask in sorted(masks, key=lambda mask: (mask != 1, -mask)):
-            last = swap(after([received[mask - 1]], last)[0], "groups", 1)
-            swapped[mask] = last
-            last = (last, own)
-        parts.append([swapped[mask] for mask in masks])
+        swapped = [own]
+        for part in far.values():
+            swapped.append(swap(after([part], swapped[-1])[0], "groups", 1))
+        parts.append([*near, *swapped[1:]])
     powers, sums = [], []
     for part, shards in enumerate(parts):
         power, *sums = call(
-            functools.partial(eigen_kernel, part, halves, pieces, scale),
+            functools.partial(eigen_kernel, part, halves, masks, pieces, scale),
             [f32(blocks // halves // 2, tokens, PAIR), f32(blocks // halves * (part + 1), BLK)],
             "partial_eigen", 2 * macs // halves, input_bytes // halves,
-            [IN_SMEM, IN_SMEM] + [IN_VMEM] * (4 + len(shards) + len(sums)),
+            [IN_SMEM, IN_SMEM] + [IN_VMEM] * (2 + len(shards) + len(sums)),
             [pltpu.VMEM((blocks // halves // 2, PAIR, PAIR), jnp.bfloat16)],
-        )(me, side, act_here, grad_here, basis_act, basis_grad, *shards, *sums)
+        )(me, side, act_here, grad_here, *shards, *sums)
         powers.append(power)
     sums = share(after(sums, early_chunks)[0], "dp", direct)
     sums = after(sums, beside_chunks)

time: 53.3 us -> 53.2 us (level)
  waiting for transfers between devices: 16.6 us -> 14.6 us
  starting transfers between devices: 23.8 us -> 25.7 us
    ppermute x18 -> x17, waiting for transfers between devices: 16.6 us -> 14.6 us  [swap(): return lax.ppermute(value, axis, [(i, i ^ mask) for i in range(count)])]
    ppermute x18 -> x17, starting transfers between devices: 23.8 us -> 25.7 us  [swap(): return lax.ppermute(value, axis, [(i, i ^ mask) for i in range(count)])]
  transfers between devices with their start and end apart: 18 -> 17, of which waited for: 9 -> 10; matrix products, arithmetic and copies ran while one was open for 0% -> 0% of each run, Pallas kernels for 18% -> 18%
where the time goes in v6:
time: 53.2 us; the launch traced here: 53.1 us
  starting transfers between devices  25.7 us (48%)
  waiting for transfers between devices  14.6 us (27%)
  Pallas kernels  12.1 us (23%)
  between operations  0.7 us (1%)
    ppermute x17, starting transfers between devices, swap(): return lax.ppermute(value, axis, [(i, i ^ mask) for i in range(count)])  25.7 us
    ppermute x17, waiting for transfers between devices, swap(): return lax.ppermute(value, axis, [(i, i ^ mask) for i in range(count)])  14.6 us
    pallas_call x1, Pallas kernels, local(): call(functools.partial(gram_kernel, pieces, messages, scale), [bf16(*acti...  4.71 us
    pallas_call x2, Pallas kernels, local(): call(functools.partial(eigen_kernel, part, halves, masks, pieces, scale),...  1.94 us
    pallas_call x1, Pallas kernels, local(): call(functools.partial(weight_kernel, halves, act_blocks // halves), f32(...  1.48 us
    pallas_call x1, Pallas kernels, local(): call(pack_kernel, [bf16(blocks // part, rows, BLK) for part in range(1, h...  1.08 us
  transfers between devices with their start and end apart: 17, of which 10 were waited for; matrix products, arithmetic and copies ran while one was open for 0% of the time, Pallas kernels for 18%

profile of v6, /device:TPU:0, one launch (start us, length us, event | category | flops | bytes accessed | tf_op | source)
XLA Modules:
  0.0 53.1 jit_solution(3006540728706586595)
XLA Ops:
  0.6 1.1 %pack_basis.1 = (bf16[36,32,128]{2,1,0:T(8,128)(2,1)S(1)}, bf16[18,32,128]{2,1,0:T(8,128)(2,1)S(1)}) custom-call(s32[1]{0:T(128)} %bitcast.1.side_ref, bf16[8,32,128]{2,1,0:T(8,128)(2,1)} %act_ref.1, bf16[28,32,128]{2,1,0:T(8,128)(2,1)} %grad_ref.1), custom_call_target="tpu_custom_call" | custom-call | bytes 294912 | tf_op jit(solution)/shard_map/pack_basis/pallas_call | solution.py:346
  1.7 5.1 %collective-permute-start.3 = (bf16[18,32,128]{2,1,0:T(8,128)(2,1)S(1)}, bf16[18,32,128]{2,1,0:T(8,128)(2,1)S(1)}, u32[]{:S(2)}, u32[]{:S(2)}) collective-permute-start(bf16[18,32,128]{2,1,0:T(8,128)(2,1)S(1)} %get-tuple-element.38), channel_id=1, source_target_pairs={{0,12},{4,8},{8,4},{12,0},{1,13},{5,9},{9,5},{13,1},{2,14},{6,10},... | collective-permute-start | bytes 442376 | tf_op jit(solution)/shard_map/ppermute | solution.py:318
  6.8 0.0 collective-permute-start.5
  6.8 0.6 %collective-permute-start.2 = (bf16[36,32,128]{2,1,0:T(8,128)(2,1)S(1)}, bf16[36,32,128]{2,1,0:T(8,128)(2,1)S(1)}, u32[]{:S(2)}, u32[]{:S(2)}) collective-permute-start(bf16[36,32,128]{2,1,0:T(8,128)(2,1)S(1)} %get-tuple-element.37.refs_0_), channel_id=1, source_target_pairs={{0,4},{4,0},{8,12},{12,8},{1,5},{5,1},{9,13},{13,9},{2,6},{6,2},{1... | collective-permute-start | bytes 884744 | tf_op jit(solution)/shard_map/ppermute | solution.py:318
  7.5 4.7 %partial_gram.1 = (bf16[512,1024]{1,0:T(8,128)(2,1)S(1)}, bf16[512,3584]{1,0:T(8,128)(2,1)S(1)}, f32[36,32,128]{2,1,0:T(8,128)S(1)}, bf16[1200,128]{1,0:T(8,128)...) custom-call(s32[1]{0:T(128)} %bitcast.me_ref, bf16[512,1024]{1,0:T(8,128)(2,1)} %act_hbm.1, ...), custom_call_target="tpu_custom_call" | custom-call | flops 1207959552 | bytes 4718592 | tf_op jit(solution)/shard_map/partial_gram/pallas_call | solution.py:371
  12.2 0.0 collective-permute-done.3.refs_2_
  12.2 1.7 %collective-permute-start.4 = (bf16[18,32,128]{2,1,0:T(8,128)(2,1)S(1)}, bf16[18,32,128]{2,1,0:T(8,128)(2,1)S(1)}, u32[]{:S(2)}, u32[]{:S(2)}) collective-permute-start(bf16[18,32,128]{2,1,0:T(8,128)(2,1)S(1)} %collective-permute-done.3.refs_2_), channel_id=1, source_target_pairs={{0,16},{16,0},{1,17},{17,1},{2,18},{18,2},{3,19},{19,3},{4,20},{20... | collective-permute-start | bytes 442376 | tf_op jit(solution)/shard_map/ppermute | solution.py:318
  13.9 5.3 %collective-permute-start = (bf16[1200,128]{1,0:T(8,128)(2,1)S(1)}, bf16[1200,128]{1,0:T(8,128)(2,1)S(1)}, u32[]{:S(2)}, u32[]{:S(2)}) collective-permute-start(bf16[1200,128]{1,0:T(8,128)(2,1)S(1)} %get-tuple-element.32), channel_id=1, source_target_pairs={{0,4},{4,0},{8,12},{12,8},{1,5},{5,1},{9,13},{13,9},{2,6},{6,2},{1... | collective-permute-start | bytes 921608 | tf_op jit(solution)/shard_map/ppermute | solution.py:318
  19.2 2.7 %collective-permute-start.1 = (bf16[1200,128]{1,0:T(8,128)(2,1)S(1)}, bf16[1200,128]{1,0:T(8,128)(2,1)S(1)}, u32[]{:S(2)}, u32[]{:S(2)}) collective-permute-start(bf16[1200,128]{1,0:T(8,128)(2,1)S(1)} %get-tuple-element.33), channel_id=1, source_target_pairs={{0,12},{4,8},{8,4},{12,0},{1,13},{5,9},{9,5},{13,1},{2,14},{6,10},... | collective-permute-start | bytes 921608 | tf_op jit(solution)/shard_map/ppermute | solution.py:318
  21.9 0.0 collective-permute-done.5.refs_3_
  21.9 0.0 collective-permute-done.4.refs_2_
  21.9 0.5 collective-permute-start.6
  22.4 0.0 collective-permute-done.2.refs_1_
  22.4 1.0 %partial_eigen.2 = (f32[9,512,256]{2,1,0:T(8,128)S(1)}, f32[18,128]{1,0:T(8,128)S(1)}) custom-call(s32[1]{0:T(128)} %bitcast.me_ref, s32[1]{0:T(128)} %bitcast.1.side_ref, bf16[512,1024]{1,0:T(8,128)(2,1)S(1)} %get-tuple-element.35.act_ref, bf16[512,3584]{1,0:T(8,128)(2,1)S(1)} %get-tuple-element.36.grad_ref, ...), custom_call_target="tpu_custom_call" | custom-call | flops 301989888 | bytes 2359296 | tf_op jit(solution)/shard_map/partial_eigen/pallas_call | solution.py:407
  23.4 3.7 %collective-permute-done.6.refs_3_ = bf16[18,32,128]{2,1,0:T(8,128)(2,1)S(1)} collective-permute-done((bf16[18,32,128]{2,1,0:T(8,128)(2,1)S(1)}, bf16[18,32,128]{2,1,0:T(8,128)(2,1)S(1)}, u32[]{:S(2)}, u32[]{:S(2)}) %collective-permute-start.6) | collective-permute-done | bytes 147488 | tf_op jit(solution)/shard_map/ppermute | solution.py:318
  27.1 1.0 %partial_eigen.3 = (f32[9,512,256]{2,1,0:T(8,128)S(1)}, f32[36,128]{1,0:T(8,128)S(1)}) custom-call(s32[1]{0:T(128)} %bitcast.me_ref, s32[1]{0:T(128)} %bitcast.1.side_ref, bf16[512,1024]{1,0:T(8,128)(2,1)S(1)} %get-tuple-element.35.act_ref, bf16[512,3584]{1,0:T(8,128)(2,1)S(1)} %get-tuple-element.36.grad_ref, ...), custom_call_target="tpu_custom_call" | custom-call | flops 301989888 | bytes 2359296 | tf_op jit(solution)/shard_map/partial_eigen/pallas_call | solution.py:407
  28.0 2.6 %collective-permute-done.refs_0_ = bf16[1200,128]{1,0:T(8,128)(2,1)S(1)} collective-permute-done((bf16[1200,128]{1,0:T(8,128)(2,1)S(1)}, bf16[1200,128]{1,0:T(8,128)(2,1)S(1)}, u32[]{:S(2)}, u32[]{:S(2)}) %collective-permute-start) | collective-permute-done | bytes 307232 | tf_op jit(solution)/shard_map/ppermute | solution.py:318
  30.6 0.9 %collective-permute-start.9 = (f32[36,128]{1,0:T(8,128)S(1)}, f32[36,128]{1,0:T(8,128)S(1)}, u32[]{:S(2)}, u32[]{:S(2)}) collective-permute-start(f32[36,128]{1,0:T(8,128)S(1)} %get-tuple-element.44.refs_0_), channel_id=1, source_target_pairs={{0,12},{4,8},{8,4},{12,0},{1,13},{5,9},{9,5},{13,1},{2,14},{6,10},... | collective-permute-start | bytes 55304 | tf_op jit(solution)/shard_map/ppermute | solution.py:318
  31.5 0.0 collective-permute-start.8
  31.5 3.5 %collective-permute-start.7 = (f32[36,128]{1,0:T(8,128)S(1)}, f32[36,128]{1,0:T(8,128)S(1)}, u32[]{:S(2)}, u32[]{:S(2)}) collective-permute-start(f32[36,128]{1,0:T(8,128)S(1)} %get-tuple-element.44.refs_0_), channel_id=1, source_target_pairs={{0,4},{4,0},{8,12},{12,8},{1,5},{5,1},{9,13},{13,9},{2,6},{6,2},{1... | collective-permute-start | bytes 55304 | tf_op jit(solution)/shard_map/ppermute | solution.py:318
  35.0 0.0 collective-permute-done.1.refs_1_
  35.0 1.3 %collective-permute-done.9.refs_3_ = f32[36,128]{1,0:T(8,128)S(1)} collective-permute-done((f32[36,128]{1,0:T(8,128)S(1)}, f32[36,128]{1,0:T(8,128)S(1)}, u32[]{:S(2)}, u32[]{:S(2)}) %collective-permute-start.9) | collective-permute-done | bytes 18464 | tf_op jit(solution)/shard_map/ppermute | solution.py:318
  36.4 0.4 collective-permute-done.8.refs_2_
  36.7 0.1 collective-permute-done.7.refs_1_
  36.8 0.6 %combine_eigen.1 = (f32[8,128]{1,0:T(8,128)}, f32[28,128]{1,0:T(8,128)}, f32[36,128]{1,0:T(8,128)S(1)}, f32[2,128]{1,0:T(2,128)S(1)}) custom-call(s32[1]{0:T(128)} %bitcast.1.side_ref, f32[36,128]{1,0:T(8,128)S(1)} %get-tuple-element.44.refs_0_, f32[36,128]{1,0:T(8,128)S(1)} %collective-permute-done.7.refs_1_, f32[36,128]{1,0:T(8,128)S(1)} %collective-permute-done.8.refs_2_, ...), custom_call_target="tpu_custom_call" | custom-call | bytes 73728 | tf_op jit(solution)/shard_map/combine_eigen/pallas_call | solution.py:417
  37.5 1.4 %collective-permute-start.10 = (bf16[1200,128]{1,0:T(8,128)(2,1)S(1)}, bf16[1200,128]{1,0:T(8,128)(2,1)S(1)}, u32[]{:S(2)}, u32[]{:S(2)}) collective-permute-start(bf16[1200,128]{1,0:T(8,128)(2,1)S(1)} %get-tuple-element.49), channel_id=1, source_target_pairs={{0,8},{4,12},{8,0},{12,4},{1,9},{5,13},{9,1},{13,5},{2,10},{6,14},... | collective-permute-start | bytes 921608 | tf_op jit(solution)/shard_map/ppermute | solution.py:318
  38.8 0.0 collective-permute-start.13
  38.8 1.5 %collective-permute-start.12 = (f32[2,128]{1,0:T(2,128)S(1)}, f32[2,128]{1,0:T(2,128)S(1)}, u32[]{:S(2)}, u32[]{:S(2)}) collective-permute-start(f32[2,128]{1,0:T(2,128)S(1)} %get-tuple-element.48.refs_2_), channel_id=1, source_target_pairs={{0,2},{1,3},{2,0},{3,1},{4,6},{5,7},{6,4},{7,5},{8,10},{9,11},{10,... | collective-permute-start | bytes 3080 | tf_op jit(solution)/shard_map/ppermute | solution.py:318
  40.4 0.3 collective-permute-start.11
  40.7 1.1 %collective-permute-done.13.refs_5_ = f32[2,128]{1,0:T(2,128)S(1)} collective-permute-done((f32[2,128]{1,0:T(2,128)S(1)}, f32[2,128]{1,0:T(2,128)S(1)}, u32[]{:S(2)}, u32[]{:S(2)}) %collective-permute-start.13) | collective-permute-done | bytes 1056 | tf_op jit(solution)/shard_map/ppermute | solution.py:318
  41.8 0.6 %collective-permute-done.12.refs_4_ = f32[2,128]{1,0:T(2,128)S(1)} collective-permute-done((f32[2,128]{1,0:T(2,128)S(1)}, f32[2,128]{1,0:T(2,128)S(1)}, u32[]{:S(2)}, u32[]{:S(2)}) %collective-permute-start.12) | collective-permute-done | bytes 1056 | tf_op jit(solution)/shard_map/ppermute | solution.py:318
  42.4 0.0 collective-permute-done.11.refs_3_
  42.4 1.5 %partial_weights.1.refs_0_ = f32[2,512]{1,0:T(2,128)S(1)} custom-call(f32[36,128]{1,0:T(8,128)S(1)} %get-tuple-element.54.eigen_ref, f32[9,512,256]{2,1,0:T(8,128)S(1)} %get-tuple-element.55.refs_0_, f32[9,512,256]{2,1,0:T(8,128)S(1)} %get-tuple-element.56.refs_1_, f32[2,128]{1,0:T(2,128)S(1)} %get-tuple-element.48.refs_2_, ...), custom_call_target="tpu_custom_call" | custom-call | bytes 9437184 | tf_op jit(solution)/shard_map/partial_weights/pallas_call | solution.py:424
  43.9 0.6 %collective-permute-start.16 = (f32[2,512]{1,0:T(2,128)S(1)}, f32[2,512]{1,0:T(2,128)S(1)}, u32[]{:S(2)}, u32[]{:S(2)}) collective-permute-start(f32[2,512]{1,0:T(2,128)S(1)} %partial_weights.1.refs_0_), channel_id=1, source_target_pairs={{0,3},{1,2},{2,1},{3,0},{4,7},{5,6},{6,5},{7,4},{8,11},{9,10},{10,... | collective-permute-start | bytes 12296 | tf_op jit(solution)/shard_map/ppermute | solution.py:318
  44.5 1.5 %collective-permute-start.15 = (f32[2,512]{1,0:T(2,128)S(1)}, f32[2,512]{1,0:T(2,128)S(1)}, u32[]{:S(2)}, u32[]{:S(2)}) collective-permute-start(f32[2,512]{1,0:T(2,128)S(1)} %partial_weights.1.refs_0_), channel_id=1, source_target_pairs={{0,2},{1,3},{2,0},{3,1},{4,6},{5,7},{6,4},{7,5},{8,10},{9,11},{10,... | collective-permute-start | bytes 12296 | tf_op jit(solution)/shard_map/ppermute | solution.py:318
  46.0 0.0 collective-permute-start.14
  46.0 0.6 %add_chunks.1.own_ref = f32[36,32,128]{2,1,0:T(8,128)S(1)} custom-call(f32[36,32,128]{2,1,0:T(8,128)S(1)} %get-tuple-element.31.own_ref, bf16[1200,128]{1,0:T(8,128)(2,1)S(1)} %collective-permute-done.refs_0_, bf16[1200,128]{1,0:T(8,128)(2,1)S(1)} %collective-permute-done.1.refs_1_), custom_call_target="tpu_custom_call" | custom-call | bytes 1769472 | tf_op jit(solution)/shard_map/add_chunks/pallas_call | solution.py:444
  46.7 0.3 collective-permute-done.16.refs_3_
  47.0 1.2 %collective-permute-done.15.refs_2_ = f32[2,512]{1,0:T(2,128)S(1)} collective-permute-done((f32[2,512]{1,0:T(2,128)S(1)}, f32[2,512]{1,0:T(2,128)S(1)}, u32[]{:S(2)}, u32[]{:S(2)}) %collective-permute-start.15) | collective-permute-done | bytes 4128 | tf_op jit(solution)/shard_map/ppermute | solution.py:318
  48.2 0.0 collective-permute-done.14.refs_1_
  48.2 0.6 %token_scores.1 = f32[1,512]{1,0:T(1,128)} custom-call(f32[2,512]{1,0:T(2,128)S(1)} %partial_weights.1.refs_0_, f32[2,512]{1,0:T(2,128)S(1)} %collective-permute-done.14.refs_1_, f32[2,512]{1,0:T(2,128)S(1)} %collective-permute-done.15.refs_2_, f32[2,512]{1,0:T(2,128)S(1)} %collective-permute-done.16.refs_3_), custom_call_target="tpu_custom_call" | custom-call | bytes 16384 | tf_op jit(solution)/shard_map/token_scores/pallas_call | solution.py:435
  48.8 3.3 %collective-permute-done.10.refs_0_ = bf16[1200,128]{1,0:T(8,128)(2,1)S(1)} collective-permute-done((bf16[1200,128]{1,0:T(8,128)(2,1)S(1)}, bf16[1200,128]{1,0:T(8,128)(2,1)S(1)}, u32[]{:S(2)}, u32[]{:S(2)}) %collective-permute-start.10) | collective-permute-done | bytes 307232 | tf_op jit(solution)/shard_map/ppermute | solution.py:318
  52.0 1.0 %add_last_chunk.1 = (f32[8,32,128]{2,1,0:T(8,128)}, f32[28,32,128]{2,1,0:T(8,128)}) custom-call(f32[36,32,128]{2,1,0:T(8,128)S(1)} %add_chunks.1.own_ref, bf16[1200,128]{1,0:T(8,128)(2,1)S(1)} %collective-permute-done.10.refs_0_), custom_call_target="tpu_custom_call" | custom-call | bytes 1474560 | tf_op jit(solution)/shard_map/add_last_chunk/pallas_call | solution.py:450
Async XLA Ops:
  1.7 10.5 %collective-permute-start.3 = (bf16[18,32,128]{2,1,0:T(8,128)(2,1)S(1)}, bf16[18,32,128]{2,1,0:T(8,128)(2,1)S(1)}, u32[]{:S(2)}, u32[]{:S(2)}) collective-permute-start(bf16[18,32,128]{2,1,0:T(8,128)(2,1)S(1)} %get-tuple-element.38), channel_id=1, source_target_pairs={{0,12},{4,8},{8,4},{12,0},{1,13},{5,9},{9,5},{13,1},{2,14},{6,10},... | collective-permute-start | bytes 442376 | tf_op jit(solution)/shard_map/ppermute | solution.py:318
  6.8 15.1 %collective-permute-start.5 = (bf16[18,32,128]{2,1,0:T(8,128)(2,1)S(1)}, bf16[18,32,128]{2,1,0:T(8,128)(2,1)S(1)}, u32[]{:S(2)}, u32[]{:S(2)}) collective-permute-start(bf16[18,32,128]{2,1,0:T(8,128)(2,1)S(1)} %get-tuple-element.38), channel_id=1, source_target_pairs={{0,8},{4,12},{8,0},{12,4},{1,9},{5,13},{9,1},{13,5},{2,10},{6,14},... | collective-permute-start | bytes 442376 | tf_op jit(solution)/shard_map/ppermute | solution.py:318
  6.8 15.6 %collective-permute-start.2 = (bf16[36,32,128]{2,1,0:T(8,128)(2,1)S(1)}, bf16[36,32,128]{2,1,0:T(8,128)(2,1)S(1)}, u32[]{:S(2)}, u32[]{:S(2)}) collective-permute-start(bf16[36,32,128]{2,1,0:T(8,128)(2,1)S(1)} %get-tuple-element.37.refs_0_), channel_id=1, source_target_pairs={{0,4},{4,0},{8,12},{12,8},{1,5},{5,1},{9,13},{13,9},{2,6},{6,2},{1... | collective-permute-start | bytes 884744 | tf_op jit(solution)/shard_map/ppermute | solution.py:318
  12.2 9.7 %collective-permute-start.4 = (bf16[18,32,128]{2,1,0:T(8,128)(2,1)S(1)}, bf16[18,32,128]{2,1,0:T(8,128)(2,1)S(1)}, u32[]{:S(2)}, u32[]{:S(2)}) collective-permute-start(bf16[18,32,128]{2,1,0:T(8,128)(2,1)S(1)} %collective-permute-done.3.refs_2_), channel_id=1, source_target_pairs={{0,16},{16,0},{1,17},{17,1},{2,18},{18,2},{3,19},{19,3},{4,20},{20... | collective-permute-start | bytes 442376 | tf_op jit(solution)/shard_map/ppermute | solution.py:318
  13.9 16.7 %collective-permute-start = (bf16[1200,128]{1,0:T(8,128)(2,1)S(1)}, bf16[1200,128]{1,0:T(8,128)(2,1)S(1)}, u32[]{:S(2)}, u32[]{:S(2)}) collective-permute-start(bf16[1200,128]{1,0:T(8,128)(2,1)S(1)} %get-tuple-element.32), channel_id=1, source_target_pairs={{0,4},{4,0},{8,12},{12,8},{1,5},{5,1},{9,13},{13,9},{2,6},{6,2},{1... | collective-permute-start | bytes 921608 | tf_op jit(solution)/shard_map/ppermute | solution.py:318
  19.2 15.8 %collective-permute-start.1 = (bf16[1200,128]{1,0:T(8,128)(2,1)S(1)}, bf16[1200,128]{1,0:T(8,128)(2,1)S(1)}, u32[]{:S(2)}, u32[]{:S(2)}) collective-permute-start(bf16[1200,128]{1,0:T(8,128)(2,1)S(1)} %get-tuple-element.33), channel_id=1, source_target_pairs={{0,12},{4,8},{8,4},{12,0},{1,13},{5,9},{9,5},{13,1},{2,14},{6,10},... | collective-permute-start | bytes 921608 | tf_op jit(solution)/shard_map/ppermute | solution.py:318
  21.9 5.1 %collective-permute-start.6 = (bf16[18,32,128]{2,1,0:T(8,128)(2,1)S(1)}, bf16[18,32,128]{2,1,0:T(8,128)(2,1)S(1)}, u32[]{:S(2)}, u32[]{:S(2)}) collective-permute-start(bf16[18,32,128]{2,1,0:T(8,128)(2,1)S(1)} %collective-permute-done.5.refs_3_), channel_id=1, source_target_pairs={{0,16},{16,0},{1,17},{17,1},{2,18},{18,2},{3,19},{19,3},{4,20},{20... | collective-permute-start | bytes 442376 | tf_op jit(solution)/shard_map/ppermute | solution.py:318
  30.6 5.7 %collective-permute-start.9 = (f32[36,128]{1,0:T(8,128)S(1)}, f32[36,128]{1,0:T(8,128)S(1)}, u32[]{:S(2)}, u32[]{:S(2)}) collective-permute-start(f32[36,128]{1,0:T(8,128)S(1)} %get-tuple-element.44.refs_0_), channel_id=1, source_target_pairs={{0,12},{4,8},{8,4},{12,0},{1,13},{5,9},{9,5},{13,1},{2,14},{6,10},... | collective-permute-start | bytes 55304 | tf_op jit(solution)/shard_map/ppermute | solution.py:318
  31.5 5.2 %collective-permute-start.8 = (f32[36,128]{1,0:T(8,128)S(1)}, f32[36,128]{1,0:T(8,128)S(1)}, u32[]{:S(2)}, u32[]{:S(2)}) collective-permute-start(f32[36,128]{1,0:T(8,128)S(1)} %get-tuple-element.44.refs_0_), channel_id=1, source_target_pairs={{0,8},{4,12},{8,0},{12,4},{1,9},{5,13},{9,1},{13,5},{2,10},{6,14},... | collective-permute-start | bytes 55304 | tf_op jit(solution)/shard_map/ppermute | solution.py:318
  31.5 5.3 %collective-permute-start.7 = (f32[36,128]{1,0:T(8,128)S(1)}, f32[36,128]{1,0:T(8,128)S(1)}, u32[]{:S(2)}, u32[]{:S(2)}) collective-permute-start(f32[36,128]{1,0:T(8,128)S(1)} %get-tuple-element.44.refs_0_), channel_id=1, source_target_pairs={{0,4},{4,0},{8,12},{12,8},{1,5},{5,1},{9,13},{13,9},{2,6},{6,2},{1... | collective-permute-start | bytes 55304 | tf_op jit(solution)/shard_map/ppermute | solution.py:318
  37.5 14.6 %collective-permute-start.10 = (bf16[1200,128]{1,0:T(8,128)(2,1)S(1)}, bf16[1200,128]{1,0:T(8,128)(2,1)S(1)}, u32[]{:S(2)}, u32[]{:S(2)}) collective-permute-start(bf16[1200,128]{1,0:T(8,128)(2,1)S(1)} %get-tuple-element.49), channel_id=1, source_target_pairs={{0,8},{4,12},{8,0},{12,4},{1,9},{5,13},{9,1},{13,5},{2,10},{6,14},... | collective-permute-start | bytes 921608 | tf_op jit(solution)/shard_map/ppermute | solution.py:318
  38.8 3.0 %collective-permute-start.13 = (f32[2,128]{1,0:T(2,128)S(1)}, f32[2,128]{1,0:T(2,128)S(1)}, u32[]{:S(2)}, u32[]{:S(2)}) collective-permute-start(f32[2,128]{1,0:T(2,128)S(1)} %get-tuple-element.48.refs_2_), channel_id=1, source_target_pairs={{0,3},{1,2},{2,1},{3,0},{4,7},{5,6},{6,5},{7,4},{8,11},{9,10},{10,... | collective-permute-start | bytes 3080 | tf_op jit(solution)/shard_map/ppermute | solution.py:318
  38.8 3.6 %collective-permute-start.12 = (f32[2,128]{1,0:T(2,128)S(1)}, f32[2,128]{1,0:T(2,128)S(1)}, u32[]{:S(2)}, u32[]{:S(2)}) collective-permute-start(f32[2,128]{1,0:T(2,128)S(1)} %get-tuple-element.48.refs_2_), channel_id=1, source_target_pairs={{0,2},{1,3},{2,0},{3,1},{4,6},{5,7},{6,4},{7,5},{8,10},{9,11},{10,... | collective-permute-start | bytes 3080 | tf_op jit(solution)/shard_map/ppermute | solution.py:318
  40.4 2.1 %collective-permute-start.11 = (f32[2,128]{1,0:T(2,128)S(1)}, f32[2,128]{1,0:T(2,128)S(1)}, u32[]{:S(2)}, u32[]{:S(2)}) collective-permute-start(f32[2,128]{1,0:T(2,128)S(1)} %get-tuple-element.48.refs_2_), channel_id=1, source_target_pairs={{0,1},{1,0},{2,3},{3,2},{4,5},{5,4},{6,7},{7,6},{8,9},{9,8},{10,11... | collective-permute-start | bytes 3080 | tf_op jit(solution)/shard_map/ppermute | solution.py:318
  43.9 3.1 %collective-permute-start.16 = (f32[2,512]{1,0:T(2,128)S(1)}, f32[2,512]{1,0:T(2,128)S(1)}, u32[]{:S(2)}, u32[]{:S(2)}) collective-permute-start(f32[2,512]{1,0:T(2,128)S(1)} %partial_weights.1.refs_0_), channel_id=1, source_target_pairs={{0,3},{1,2},{2,1},{3,0},{4,7},{5,6},{6,5},{7,4},{8,11},{9,10},{10,... | collective-permute-start | bytes 12296 | tf_op jit(solution)/shard_map/ppermute | solution.py:318
  44.5 3.6 %collective-permute-start.15 = (f32[2,512]{1,0:T(2,128)S(1)}, f32[2,512]{1,0:T(2,128)S(1)}, u32[]{:S(2)}, u32[]{:S(2)}) collective-permute-start(f32[2,512]{1,0:T(2,128)S(1)} %partial_weights.1.refs_0_), channel_id=1, source_target_pairs={{0,2},{1,3},{2,0},{3,1},{4,6},{5,7},{6,4},{7,5},{8,10},{9,11},{10,... | collective-permute-start | bytes 12296 | tf_op jit(solution)/shard_map/ppermute | solution.py:318
  46.0 2.1 %collective-permute-start.14 = (f32[2,512]{1,0:T(2,128)S(1)}, f32[2,512]{1,0:T(2,128)S(1)}, u32[]{:S(2)}, u32[]{:S(2)}) collective-permute-start(f32[2,512]{1,0:T(2,128)S(1)} %partial_weights.1.refs_0_), channel_id=1, source_target_pairs={{0,1},{1,0},{2,3},{3,2},{4,5},{5,4},{6,7},{7,6},{8,9},{9,8},{10,11... | collective-permute-start | bytes 12296 | tf_op jit(solution)/shard_map/ppermute | solution.py:318

commit v7 on v6

--- a/solution.py
+++ b/solution.py
@@ -67,6 +67,11 @@
     power = power * power
     power = power * power
     return jnp.where(values < 0.0, -power, power).astype(jnp.bfloat16)
+
+
+def top_of(values):
+    top = jnp.maximum(jnp.max(jnp.abs(values), axis=0, keepdims=True), SMALLEST)
+    return (top * (1.0 + 2.0**-8)).astype(jnp.bfloat16).astype(jnp.float32)
 
 
 def decode(coded):
@@ -101,8 +106,9 @@
         copy.wait()
 
 
-def gram_kernel(pieces, messages, scale, me_ref, act_hbm, grad_hbm, act_ref, grad_ref, own_ref, *refs):
-    sent_refs, (whole, tops, sems) = refs[:-3], refs[-3:]
+def gram_kernel(pieces, messages, scale, me_ref, act_hbm, grad_hbm, act_ref, grad_ref, *refs):
+    refs, (whole, tops, sems) = refs[:-3], refs[-3:]
+    plain_refs, sent_refs = refs[: len(refs) - len(messages)], refs[len(refs) - len(messages) :]
     rows = BLK // pieces
     me = me_ref[0]
     steps = []
@@ -125,14 +131,15 @@
                 values, values, contract_rows, preferred_element_type=jnp.float32
             )
             if pieces == 1:
-                own_ref[block] = gram
+                plain_refs[0][block] = gram
                 continue
             whole[offset] = gram
-            top = jnp.maximum(jnp.max(jnp.abs(gram), axis=0, keepdims=True), SMALLEST)
-            top = (top * (1.0 + 2.0**-8)).astype(jnp.bfloat16).astype(jnp.float32)
+            for ref_at, mask in zip(plain_refs, (0, 2)):
+                row = pl.multiple_of((me ^ mask) * rows, rows)
+                ref_at[block] = whole[offset, pl.ds(row, rows), :]
+            top = top_of(gram)
             tops[block : block + 1, :] = top
             gain = CODE_TOP / top
-            own_ref[block] = whole[offset, pl.ds(pl.multiple_of(me * rows, rows), rows), :]
             for sent_ref, (mask, first, end) in zip(sent_refs, messages):
                 if first <= block < end:
                     row = pl.multiple_of((me ^ mask) * rows, rows)
@@ -167,6 +174,21 @@
     for step in range(blocks // GROUP):
         for block, total in add_group(messages, rows, own_ref, sent_refs, tops_refs, step):
             sum_ref[block] = total
+
+
+def relay_kernel(message, far_ref, relayed_ref, sent_ref, relayed_tops, tops):
+    messages = (message,)
+    blocks, rows, _ = far_ref.shape
+    load_tops(messages, rows, (relayed_ref,), (relayed_tops,))
+    tops[...] = jnp.zeros_like(tops)
+    for step in range(blocks // GROUP):
+        for block, total in add_group(
+            messages, rows, far_ref, (relayed_ref,), (relayed_tops,), step
+        ):
+            top = top_of(total)
+            tops[block : block + 1, :] = top
+            sent_ref[block * rows : (block + 1) * rows, :] = encode(total * (CODE_TOP / top))
+    sent_ref[blocks * rows :, :] = tops[...].astype(jnp.bfloat16)
 
 
 def last_add_kernel(messages, own_ref, *refs):
@@ -360,21 +382,17 @@
         far = {}
     masks = [*range(len(near)), *far]
 
-    early, beside, late = [], [], []
-    if pieces == 4:
-        early = [(1, 0, blocks)]
-        beside = [(3, 0, blocks)]
-        late = [(2, 0, blocks)]
-    elif pieces == 2:
-        late = [(1, 0, blocks)]
-    messages = early + beside + late
-    act_here, grad_here, own, *sent = call(
-        functools.partial(gram_kernel, pieces, messages, scale),
+    message = bf16(blocks * rows + scale_rows(0, blocks), BLK)
+    whole_range = (0, blocks)
+    coded = {4: [(3, *whole_range), (1, *whole_range)], 2: [(1, *whole_range)], 1: []}[pieces]
+    plain = 2 if pieces == 4 else 1
+    act_here, grad_here, *grams = call(
+        functools.partial(gram_kernel, pieces, coded, scale),
         [
             bf16(*activations.shape),
             bf16(*gradients.shape),
-            f32(blocks, rows, BLK),
-            *[bf16((end - first) * rows + scale_rows(first, end), BLK) for _, first, end in messages],
+            *[f32(blocks, rows, BLK)] * plain,
+            *[message] * len(coded),
         ],
         "partial_gram", 4 * macs, input_bytes,
         [IN_SMEM, IN_HBM, IN_HBM],
@@ -384,24 +402,18 @@
             pltpu.SemaphoreType.DMA((blocks // GROUP,)),
         ],
     )(me, in_hbm(activations), in_hbm(gradients))
-    sent = dict(zip(messages, sent))
+    own = grams[0]
+    sent = {message[0]: chunk for message, chunk in zip(coded, grams[plain:])}
     if not direct:
         own = lax.psum_scatter(own, "dp", scatter_dimension=1, tiled=True)
-
-    def send(messages, done=None):
-        chunks = [sent[message] for message in messages]
-        if done is not None:
-            chunks = after(chunks, done)
-        return [swap(chunk, "dp", message[0]) for chunk, message in zip(chunks, messages)]
-
-    early_chunks, beside_chunks = send(early), send(beside)
+    if pieces == 4:
+        middle = lax.ppermute(sent[3], "dp", [(1, 2), (2, 1)])
+        relayed = lax.ppermute(sent[3], "dp", [(0, 1), (3, 2)])
 
     parts = [[*near, *far.values()]]
     if halves == 2:
-        swapped = [own]
-        for part in far.values():
-            swapped.append(swap(after([part], swapped[-1])[0], "groups", 1))
-        parts.append([*near, *swapped[1:]])
+        swapped = [swap(after([part], own)[0], "groups", 1) for part in far.values()]
+        parts.append([*near, *swapped])
     powers, sums = [], []
     for part, shards in enumerate(parts):
         power, *sums = call(
@@ -412,14 +424,24 @@
             [pltpu.VMEM((blocks // halves // 2, PAIR, PAIR), jnp.bfloat16)],
         )(me, side, act_here, grad_here, *shards, *sums)
         powers.append(power)
-    sums = share(after(sums, early_chunks)[0], "dp", direct)
-    sums = after(sums, beside_chunks)
+    if pieces == 4:
+        sent[2] = call(
+            functools.partial(relay_kernel, coded[0]), message, "relay_chunk", 0, 12 * own.size,
+            [IN_VMEM, IN_VMEM],
+            [pltpu.VMEM((scale_rows(0, blocks), BLK), jnp.float32)] * 2,
+        )(*after([grams[1], relayed], sums))
+    sums = share(sums[0], "dp", direct)
+    if pieces == 4:
+        sums = after(sums, middle)
     act_eigen, grad_eigen, eigen, totals = call(
         functools.partial(combine_kernel, halves),
         [f32(act_blocks, BLK), f32(grad_blocks, BLK), f32(blocks, BLK), f32(2, BLK)],
         "combine_eigen", 0, 4 * blocks * BLK * pieces, [IN_SMEM] + [IN_VMEM] * len(sums),
     )(side, *sums)
-    late_chunks = send(late, totals)
+    arrived = {}
+    sent.pop(3, None)
+    for mask in sent:
+        arrived[mask] = swap(after([sent[mask]], totals)[0], "dp", mask)
     totals = share(totals, "owner", direct)
     weights = call(
         functools.partial(weight_kernel, halves, act_blocks // halves),
@@ -437,27 +459,25 @@
         [IN_VMEM] * len(weights),
     )(*weights)
 
-    def tops_of(messages):
-        return [pltpu.VMEM((scale_rows(first, end), BLK), jnp.float32) for _, first, end in messages]
-
-    if early:
-        own = call(
-            functools.partial(add_kernel, early + beside), f32(*own.shape),
-            "add_chunks", 0, 12 * own.size, [IN_VMEM] * (1 + len(early + beside)),
-            tops_of(early + beside),
-        )(own, *early_chunks, *beside_chunks)
-    if late:
-        covariance = call(
-            functools.partial(last_add_kernel, late),
+    def add(kernel, chunks, out_shape, scratch_shapes=(), **options):
+        messages = [(None, *whole_range)] * len(chunks)
+        return call(
+            functools.partial(kernel, messages), out_shape, "add_chunks", 0, 12 * own.size,
+            [IN_VMEM] * (1 + len(chunks)),
+            [pltpu.VMEM((scale_rows(*whole_range), BLK), jnp.float32)] * len(chunks)
+            + [*scratch_shapes],
+            **options,
+        )(own, *chunks)
+
+    if pieces == 4:
+        own = add(add_kernel, [middle, arrived.pop(1)], f32(*own.shape))
+    if arrived:
+        covariance = add(
+            last_add_kernel, [*arrived.values()],
             [f32(act_blocks, rows, BLK), f32(grad_blocks, rows, BLK)],
-            "add_last_chunk", 0, 10 * own.size, [IN_VMEM] * (1 + len(late)),
-            [
-                *tops_of(late),
-                pltpu.VMEM(own.shape, jnp.float32),
-                pltpu.SemaphoreType.DMA((blocks // GROUP,)),
-            ],
+            [pltpu.VMEM(own.shape, jnp.float32), pltpu.SemaphoreType.DMA((blocks // GROUP,))],
             out_spec=pl.BlockSpec(memory_space=pl.ANY),
-        )(own, *late_chunks)
+        )
     else:
         covariance = own[:act_blocks], own[act_blocks:]
     return (

time: 53.2 us -> 50.5 us (0.949)
  starting transfers between devices: 25.7 us -> 22.6 us
    ppermute x17 -> x16, starting transfers between devices: 25.7 us -> 18.6 us  [swap(): return lax.ppermute(value, axis, [(i, i ^ mask) for i in range(count)])]
    ppermute x0 -> x2, starting transfers between devices: none -> 4 us  [the longest x1 3.32 us: local(): relayed = lax.ppermute(sent[3], 'dp', [(0, 1), (3, 2)])]
    pallas_call x3 -> x4, Pallas kernels: 6.38 us -> 6.81 us  [the longest x1 4.56 us: local(): call(functools.partial(gram_kernel, pieces, coded, scale), [bf16(*activat...]
    ppermute x17 -> x16, waiting for transfers between devices: 14.6 us -> 14.5 us  [swap(): return lax.ppermute(value, axis, [(i, i ^ mask) for i in range(count)])]
  transfers between devices with their start and end apart: 17 -> 18, of which waited for: 10 -> 7; matrix products, arithmetic and copies ran while one was open for 0% -> 0% of each run, Pallas kernels for 18% -> 19%
where the time goes in v7:
time: 50.5 us; the launch traced here: 50.3 us
  starting transfers between devices  22.6 us (45%)
  waiting for transfers between devices  14.5 us (29%)
  Pallas kernels  12.5 us (25%)
  between operations  0.75 us (1%)
    ppermute x16, starting transfers between devices, swap(): return lax.ppermute(value, axis, [(i, i ^ mask) for i in range(count)])  18.6 us
    ppermute x16, waiting for transfers between devices, swap(): return lax.ppermute(value, axis, [(i, i ^ mask) for i in range(count)])  14.5 us
    pallas_call x1, Pallas kernels, local(): call(functools.partial(gram_kernel, pieces, coded, scale), [bf16(*activat...  4.56 us
    ppermute x1, starting transfers between devices, local(): relayed = lax.ppermute(sent[3], 'dp', [(0, 1), (3, 2)])  3.32 us
    pallas_call x2, Pallas kernels, local(): call(functools.partial(eigen_kernel, part, halves, masks, pieces, scale),...  1.95 us
    pallas_call x2, Pallas kernels, add(): call(functools.partial(kernel, messages), out_shape, 'add_chunks', 0, 12...  1.67 us
    pallas_call x1, Pallas kernels, local(): call(functools.partial(weight_kernel, halves, act_blocks // halves), f32(...  1.48 us
    pallas_call x1, Pallas kernels, local(): call(pack_kernel, [bf16(blocks // part, rows, BLK) for part in range(1, h...  1.08 us
  transfers between devices with their start and end apart: 18, of which 7 were waited for; matrix products, arithmetic and copies ran while one was open for 0% of the time, Pallas kernels for 19%

profile of v7, /device:TPU:0, one launch (start us, length us, event | category | flops | bytes accessed | tf_op | source)
XLA Modules:
  0.0 50.3 jit_solution(10767114773947502888)
XLA Ops:
  0.6 1.1 %pack_basis.1 = (bf16[36,32,128]{2,1,0:T(8,128)(2,1)S(1)}, bf16[18,32,128]{2,1,0:T(8,128)(2,1)S(1)}) custom-call(s32[1]{0:T(128)} %bitcast.1.side_ref, bf16[8,32,128]{2,1,0:T(8,128)(2,1)} %act_ref.1, bf16[28,32,128]{2,1,0:T(8,128)(2,1)} %grad_ref.1), custom_call_target="tpu_custom_call" | custom-call | bytes 294912 | tf_op jit(solution)/shard_map/pack_basis/pallas_call | solution.py:368
  1.7 5.1 %collective-permute-start.2 = (bf16[18,32,128]{2,1,0:T(8,128)(2,1)S(1)}, bf16[18,32,128]{2,1,0:T(8,128)(2,1)S(1)}, u32[]{:S(2)}, u32[]{:S(2)}) collective-permute-start(bf16[18,32,128]{2,1,0:T(8,128)(2,1)S(1)} %get-tuple-element.39), channel_id=1, source_target_pairs={{0,12},{4,8},{8,4},{12,0},{1,13},{5,9},{9,5},{13,1},{2,14},{6,10},... | collective-permute-start | bytes 442376 | tf_op jit(solution)/shard_map/ppermute | solution.py:340
  6.8 0.0 collective-permute-start.4
  6.8 0.6 %collective-permute-start.1 = (bf16[36,32,128]{2,1,0:T(8,128)(2,1)S(1)}, bf16[36,32,128]{2,1,0:T(8,128)(2,1)S(1)}, u32[]{:S(2)}, u32[]{:S(2)}) collective-permute-start(bf16[36,32,128]{2,1,0:T(8,128)(2,1)S(1)} %get-tuple-element.38.refs_0_), channel_id=1, source_target_pairs={{0,4},{4,0},{8,12},{12,8},{1,5},{5,1},{9,13},{13,9},{2,6},{6,2},{1... | collective-permute-start | bytes 884744 | tf_op jit(solution)/shard_map/ppermute | solution.py:340
  7.5 4.6 %partial_gram.1 = (bf16[512,1024]{1,0:T(8,128)(2,1)S(1)}, bf16[512,3584]{1,0:T(8,128)(2,1)S(1)}, f32[36,32,128]{2,1,0:T(8,128)S(1)}, f32[36,32,128]{2,1,0:T(8,12...) custom-call(s32[1]{0:T(128)} %bitcast.me_ref, bf16[512,1024]{1,0:T(8,128)(2,1)} %act_hbm.1, ...), custom_call_target="tpu_custom_call" | custom-call | flops 1207959552 | bytes 4718592 | tf_op jit(solution)/shard_map/partial_gram/pallas_call | solution.py:389
  12.0 3.3 %collective-permute-start.10 = (bf16[1200,128]{1,0:T(8,128)(2,1)S(1)}, bf16[1200,128]{1,0:T(8,128)(2,1)S(1)}, u32[]{:S(2)}, u32[]{:S(2)}) collective-permute-start(bf16[1200,128]{1,0:T(8,128)(2,1)S(1)} %get-tuple-element.34), channel_id=1, source_target_pairs={{0,4},{12,8},{1,5},{13,9},{2,6},{14,10},{3,7},{15,11},{16,20},{28,... | collective-permute-start | bytes 921608 | tf_op jit(solution)/shard_map/ppermute | solution.py:411
  15.4 0.7 %collective-permute-start = (bf16[1200,128]{1,0:T(8,128)(2,1)S(1)}, bf16[1200,128]{1,0:T(8,128)(2,1)S(1)}, u32[]{:S(2)}, u32[]{:S(2)}) collective-permute-start(bf16[1200,128]{1,0:T(8,128)(2,1)S(1)} %get-tuple-element.34), channel_id=1, source_target_pairs={{4,8},{8,4},{5,9},{9,5},{6,10},{10,6},{7,11},{11,7},{20,24},{24,20... | collective-permute-start | bytes 921608 | tf_op jit(solution)/shard_map/ppermute | solution.py:410
  16.1 0.0 collective-permute-done.2.refs_2_
  16.1 1.6 %collective-permute-start.3 = (bf16[18,32,128]{2,1,0:T(8,128)(2,1)S(1)}, bf16[18,32,128]{2,1,0:T(8,128)(2,1)S(1)}, u32[]{:S(2)}, u32[]{:S(2)}) collective-permute-start(bf16[18,32,128]{2,1,0:T(8,128)(2,1)S(1)} %collective-permute-done.2.refs_2_), channel_id=1, source_target_pairs={{0,16},{16,0},{1,17},{17,1},{2,18},{18,2},{3,19},{19,3},{4,20},{20... | collective-permute-start | bytes 442376 | tf_op jit(solution)/shard_map/ppermute | solution.py:340
  17.6 2.7 %collective-permute-done.4.refs_3_ = bf16[18,32,128]{2,1,0:T(8,128)(2,1)S(1)} collective-permute-done((bf16[18,32,128]{2,1,0:T(8,128)(2,1)S(1)}, bf16[18,32,128]{2,1,0:T(8,128)(2,1)S(1)}, u32[]{:S(2)}, u32[]{:S(2)}) %collective-permute-start.4) | collective-permute-done | bytes 147488 | tf_op jit(solution)/shard_map/ppermute | solution.py:340
  20.3 1.5 %collective-permute-start.5 = (bf16[18,32,128]{2,1,0:T(8,128)(2,1)S(1)}, bf16[18,32,128]{2,1,0:T(8,128)(2,1)S(1)}, u32[]{:S(2)}, u32[]{:S(2)}) collective-permute-start(bf16[18,32,128]{2,1,0:T(8,128)(2,1)S(1)} %collective-permute-done.4.refs_3_), channel_id=1, source_target_pairs={{0,16},{16,0},{1,17},{17,1},{2,18},{18,2},{3,19},{19,3},{4,20},{20... | collective-permute-start | bytes 442376 | tf_op jit(solution)/shard_map/ppermute | solution.py:340
  21.8 0.0 collective-permute-done.1.refs_1_
  21.8 1.0 %partial_eigen.2 = (f32[9,512,256]{2,1,0:T(8,128)S(1)}, f32[18,128]{1,0:T(8,128)S(1)}) custom-call(s32[1]{0:T(128)} %bitcast.me_ref, s32[1]{0:T(128)} %bitcast.1.side_ref, bf16[512,1024]{1,0:T(8,128)(2,1)S(1)} %get-tuple-element.36.act_ref, bf16[512,3584]{1,0:T(8,128)(2,1)S(1)} %get-tuple-element.37.grad_ref, ...), custom_call_target="tpu_custom_call" | custom-call | flops 301989888 | bytes 2359296 | tf_op jit(solution)/shard_map/partial_eigen/pallas_call | solution.py:419
  22.8 0.0 collective-permute-done.3.refs_2_
  22.8 2.6 %collective-permute-done.5.refs_3_ = bf16[18,32,128]{2,1,0:T(8,128)(2,1)S(1)} collective-permute-done((bf16[18,32,128]{2,1,0:T(8,128)(2,1)S(1)}, bf16[18,32,128]{2,1,0:T(8,128)(2,1)S(1)}, u32[]{:S(2)}, u32[]{:S(2)}) %collective-permute-start.5) | collective-permute-done | bytes 147488 | tf_op jit(solution)/shard_map/ppermute | solution.py:340
  25.5 1.0 %partial_eigen.3 = (f32[9,512,256]{2,1,0:T(8,128)S(1)}, f32[36,128]{1,0:T(8,128)S(1)}) custom-call(s32[1]{0:T(128)} %bitcast.me_ref, s32[1]{0:T(128)} %bitcast.1.side_ref, bf16[512,1024]{1,0:T(8,128)(2,1)S(1)} %get-tuple-element.36.act_ref, bf16[512,3584]{1,0:T(8,128)(2,1)S(1)} %get-tuple-element.37.grad_ref, ...), custom_call_target="tpu_custom_call" | custom-call | flops 301989888 | bytes 2359296 | tf_op jit(solution)/shard_map/partial_eigen/pallas_call | solution.py:419
  26.5 0.7 %collective-permute-start.6 = (f32[36,128]{1,0:T(8,128)S(1)}, f32[36,128]{1,0:T(8,128)S(1)}, u32[]{:S(2)}, u32[]{:S(2)}) collective-permute-start(f32[36,128]{1,0:T(8,128)S(1)} %get-tuple-element.44.refs_0_), channel_id=1, source_target_pairs={{0,4},{4,0},{8,12},{12,8},{1,5},{5,1},{9,13},{13,9},{2,6},{6,2},{1... | collective-permute-start | bytes 55304 | tf_op jit(solution)/shard_map/ppermute | solution.py:340
  27.2 2.6 %collective-permute-start.7 = (f32[36,128]{1,0:T(8,128)S(1)}, f32[36,128]{1,0:T(8,128)S(1)}, u32[]{:S(2)}, u32[]{:S(2)}) collective-permute-start(f32[36,128]{1,0:T(8,128)S(1)} %get-tuple-element.44.refs_0_), channel_id=1, source_target_pairs={{0,8},{4,12},{8,0},{12,4},{1,9},{5,13},{9,1},{13,5},{2,10},{6,14},... | collective-permute-start | bytes 55304 | tf_op jit(solution)/shard_map/ppermute | solution.py:340
  29.7 1.2 %collective-permute-start.8 = (f32[36,128]{1,0:T(8,128)S(1)}, f32[36,128]{1,0:T(8,128)S(1)}, u32[]{:S(2)}, u32[]{:S(2)}) collective-permute-start(f32[36,128]{1,0:T(8,128)S(1)} %get-tuple-element.44.refs_0_), channel_id=1, source_target_pairs={{0,12},{4,8},{8,4},{12,0},{1,13},{5,9},{9,5},{13,1},{2,14},{6,10},... | collective-permute-start | bytes 55304 | tf_op jit(solution)/shard_map/ppermute | solution.py:340
  30.9 0.0 collective-permute-done.10.relayed_ref
  30.9 0.6 %relay_chunk.1 = bf16[1200,128]{1,0:T(8,128)(2,1)S(1)} custom-call(f32[36,32,128]{2,1,0:T(8,128)S(1)} %get-tuple-element.51.far_ref, bf16[1200,128]{1,0:T(8,128)(2,1)S(1)} %collective-permute-done.10.relayed_ref), custom_call_target="tpu_custom_call" | custom-call | bytes 1769472 | tf_op jit(solution)/shard_map/relay_chunk/pallas_call | solution.py:428
  31.5 0.0 collective-permute-done.refs_0_
  31.5 0.0 collective-permute-done.6.refs_1_
  31.5 0.3 collective-permute-done.7.refs_2_
  31.8 4.0 %collective-permute-done.8.refs_3_ = f32[36,128]{1,0:T(8,128)S(1)} collective-permute-done((f32[36,128]{1,0:T(8,128)S(1)}, f32[36,128]{1,0:T(8,128)S(1)}, u32[]{:S(2)}, u32[]{:S(2)}) %collective-permute-start.8) | collective-permute-done | bytes 18464 | tf_op jit(solution)/shard_map/ppermute | solution.py:340
  35.8 0.6 %combine_eigen.1 = (f32[8,128]{1,0:T(8,128)}, f32[28,128]{1,0:T(8,128)}, f32[36,128]{1,0:T(8,128)S(1)}, f32[2,128]{1,0:T(2,128)S(1)}) custom-call(s32[1]{0:T(128)} %bitcast.1.side_ref, f32[36,128]{1,0:T(8,128)S(1)} %get-tuple-element.44.refs_0_, f32[36,128]{1,0:T(8,128)S(1)} %collective-permute-done.6.refs_1_, f32[36,128]{1,0:T(8,128)S(1)} %collective-permute-done.7.refs_2_, ...), custom_call_target="tpu_custom_call" | custom-call | bytes 73728 | tf_op jit(solution)/shard_map/combine_eigen/pallas_call | solution.py:436
  36.4 0.0 collective-permute-start.9
  36.4 1.5 %collective-permute-start.11 = (bf16[1200,128]{1,0:T(8,128)(2,1)S(1)}, bf16[1200,128]{1,0:T(8,128)(2,1)S(1)}, u32[]{:S(2)}, u32[]{:S(2)}) collective-permute-start(bf16[1200,128]{1,0:T(8,128)(2,1)S(1)} %relay_chunk.1), channel_id=1, source_target_pairs={{0,8},{4,12},{8,0},{12,4},{1,9},{5,13},{9,1},{13,5},{2,10},{6,14},... | collective-permute-start | bytes 921608 | tf_op jit(solution)/shard_map/ppermute | solution.py:340
  37.9 0.0 collective-permute-start.12
  37.9 1.5 %collective-permute-start.13 = (f32[2,128]{1,0:T(2,128)S(1)}, f32[2,128]{1,0:T(2,128)S(1)}, u32[]{:S(2)}, u32[]{:S(2)}) collective-permute-start(f32[2,128]{1,0:T(2,128)S(1)} %get-tuple-element.48.refs_2_), channel_id=1, source_target_pairs={{0,2},{1,3},{2,0},{3,1},{4,6},{5,7},{6,4},{7,5},{8,10},{9,11},{10,... | collective-permute-start | bytes 3080 | tf_op jit(solution)/shard_map/ppermute | solution.py:340
  39.4 0.4 collective-permute-start.14
  39.8 0.0 collective-permute-done.12.refs_3_
  39.8 1.7 %collective-permute-done.13.refs_4_ = f32[2,128]{1,0:T(2,128)S(1)} collective-permute-done((f32[2,128]{1,0:T(2,128)S(1)}, f32[2,128]{1,0:T(2,128)S(1)}, u32[]{:S(2)}, u32[]{:S(2)}) %collective-permute-start.13) | collective-permute-done | bytes 1056 | tf_op jit(solution)/shard_map/ppermute | solution.py:340
  41.5 0.9 %collective-permute-done.14.refs_5_ = f32[2,128]{1,0:T(2,128)S(1)} collective-permute-done((f32[2,128]{1,0:T(2,128)S(1)}, f32[2,128]{1,0:T(2,128)S(1)}, u32[]{:S(2)}, u32[]{:S(2)}) %collective-permute-start.14) | collective-permute-done | bytes 1056 | tf_op jit(solution)/shard_map/ppermute | solution.py:340
  42.4 1.5 %partial_weights.1.refs_0_ = f32[2,512]{1,0:T(2,128)S(1)} custom-call(f32[36,128]{1,0:T(8,128)S(1)} %get-tuple-element.58.eigen_ref, f32[9,512,256]{2,1,0:T(8,128)S(1)} %get-tuple-element.59.refs_0_, f32[9,512,256]{2,1,0:T(8,128)S(1)} %get-tuple-element.60.refs_1_, f32[2,128]{1,0:T(2,128)S(1)} %get-tuple-element.48.refs_2_, ...), custom_call_target="tpu_custom_call" | custom-call | bytes 9437184 | tf_op jit(solution)/shard_map/partial_weights/pallas_call | solution.py:446
  43.9 0.5 %collective-permute-start.15 = (f32[2,512]{1,0:T(2,128)S(1)}, f32[2,512]{1,0:T(2,128)S(1)}, u32[]{:S(2)}, u32[]{:S(2)}) collective-permute-start(f32[2,512]{1,0:T(2,128)S(1)} %partial_weights.1.refs_0_), channel_id=1, source_target_pairs={{0,1},{1,0},{2,3},{3,2},{4,5},{5,4},{6,7},{7,6},{8,9},{9,8},{10,11... | collective-permute-start | bytes 12296 | tf_op jit(solution)/shard_map/ppermute | solution.py:340
  44.4 0.5 %collective-permute-start.16 = (f32[2,512]{1,0:T(2,128)S(1)}, f32[2,512]{1,0:T(2,128)S(1)}, u32[]{:S(2)}, u32[]{:S(2)}) collective-permute-start(f32[2,512]{1,0:T(2,128)S(1)} %partial_weights.1.refs_0_), channel_id=1, source_target_pairs={{0,2},{1,3},{2,0},{3,1},{4,6},{5,7},{6,4},{7,5},{8,10},{9,11},{10,... | collective-permute-start | bytes 12296 | tf_op jit(solution)/shard_map/ppermute | solution.py:340
  45.0 0.9 %collective-permute-start.17 = (f32[2,512]{1,0:T(2,128)S(1)}, f32[2,512]{1,0:T(2,128)S(1)}, u32[]{:S(2)}, u32[]{:S(2)}) collective-permute-start(f32[2,512]{1,0:T(2,128)S(1)} %partial_weights.1.refs_0_), channel_id=1, source_target_pairs={{0,3},{1,2},{2,1},{3,0},{4,7},{5,6},{6,5},{7,4},{8,11},{9,10},{10,... | collective-permute-start | bytes 12296 | tf_op jit(solution)/shard_map/ppermute | solution.py:340
  45.8 0.0 collective-permute-done.15.refs_1_
  45.8 2.2 %collective-permute-done.16.refs_2_ = f32[2,512]{1,0:T(2,128)S(1)} collective-permute-done((f32[2,512]{1,0:T(2,128)S(1)}, f32[2,512]{1,0:T(2,128)S(1)}, u32[]{:S(2)}, u32[]{:S(2)}) %collective-permute-start.16) | collective-permute-done | bytes 4128 | tf_op jit(solution)/shard_map/ppermute | solution.py:340
  48.0 0.0 collective-permute-done.17.refs_3_
  48.0 0.6 %token_scores.1 = f32[1,512]{1,0:T(1,128)} custom-call(f32[2,512]{1,0:T(2,128)S(1)} %partial_weights.1.refs_0_, f32[2,512]{1,0:T(2,128)S(1)} %collective-permute-done.15.refs_1_, f32[2,512]{1,0:T(2,128)S(1)} %collective-permute-done.16.refs_2_, f32[2,512]{1,0:T(2,128)S(1)} %collective-permute-done.17.refs_3_), custom_call_target="tpu_custom_call" | custom-call | bytes 16384 | tf_op jit(solution)/shard_map/token_scores/pallas_call | solution.py:457
  48.6 0.0 collective-permute-done.9.refs_1_
  48.6 0.6 %add_chunks.2.own_ref = f32[36,32,128]{2,1,0:T(8,128)S(1)} custom-call(f32[36,32,128]{2,1,0:T(8,128)S(1)} %get-tuple-element.33.own_ref, bf16[1200,128]{1,0:T(8,128)(2,1)S(1)} %collective-permute-done.refs_0_, bf16[1200,128]{1,0:T(8,128)(2,1)S(1)} %collective-permute-done.9.refs_1_), custom_call_target="tpu_custom_call" | custom-call | bytes 1769472 | tf_op jit(solution)/shard_map/add_chunks/pallas_call | solution.py:464
  49.3 0.0 collective-permute-done.11.refs_0_
  49.3 1.0 %add_chunks.3 = (f32[8,32,128]{2,1,0:T(8,128)}, f32[28,32,128]{2,1,0:T(8,128)}) custom-call(f32[36,32,128]{2,1,0:T(8,128)S(1)} %add_chunks.2.own_ref, bf16[1200,128]{1,0:T(8,128)(2,1)S(1)} %collective-permute-done.11.refs_0_), custom_call_target="tpu_custom_call" | custom-call | bytes 1769472 | tf_op jit(solution)/shard_map/add_chunks/pallas_call | solution.py:464
Async XLA Ops:
  1.7 14.3 %collective-permute-start.2 = (bf16[18,32,128]{2,1,0:T(8,128)(2,1)S(1)}, bf16[18,32,128]{2,1,0:T(8,128)(2,1)S(1)}, u32[]{:S(2)}, u32[]{:S(2)}) collective-permute-start(bf16[18,32,128]{2,1,0:T(8,128)(2,1)S(1)} %get-tuple-element.39), channel_id=1, source_target_pairs={{0,12},{4,8},{8,4},{12,0},{1,13},{5,9},{9,5},{13,1},{2,14},{6,10},... | collective-permute-start | bytes 442376 | tf_op jit(solution)/shard_map/ppermute | solution.py:340
  6.8 13.5 %collective-permute-start.4 = (bf16[18,32,128]{2,1,0:T(8,128)(2,1)S(1)}, bf16[18,32,128]{2,1,0:T(8,128)(2,1)S(1)}, u32[]{:S(2)}, u32[]{:S(2)}) collective-permute-start(bf16[18,32,128]{2,1,0:T(8,128)(2,1)S(1)} %get-tuple-element.39), channel_id=1, source_target_pairs={{0,8},{4,12},{8,0},{12,4},{1,9},{5,13},{9,1},{13,5},{2,10},{6,14},... | collective-permute-start | bytes 442376 | tf_op jit(solution)/shard_map/ppermute | solution.py:340
  6.8 15.0 %collective-permute-start.1 = (bf16[36,32,128]{2,1,0:T(8,128)(2,1)S(1)}, bf16[36,32,128]{2,1,0:T(8,128)(2,1)S(1)}, u32[]{:S(2)}, u32[]{:S(2)}) collective-permute-start(bf16[36,32,128]{2,1,0:T(8,128)(2,1)S(1)} %get-tuple-element.38.refs_0_), channel_id=1, source_target_pairs={{0,4},{4,0},{8,12},{12,8},{1,5},{5,1},{9,13},{13,9},{2,6},{6,2},{1... | collective-permute-start | bytes 884744 | tf_op jit(solution)/shard_map/ppermute | solution.py:340
  12.0 18.9 %collective-permute-start.10 = (bf16[1200,128]{1,0:T(8,128)(2,1)S(1)}, bf16[1200,128]{1,0:T(8,128)(2,1)S(1)}, u32[]{:S(2)}, u32[]{:S(2)}) collective-permute-start(bf16[1200,128]{1,0:T(8,128)(2,1)S(1)} %get-tuple-element.34), channel_id=1, source_target_pairs={{0,4},{12,8},{1,5},{13,9},{2,6},{14,10},{3,7},{15,11},{16,20},{28,... | collective-permute-start | bytes 921608 | tf_op jit(solution)/shard_map/ppermute | solution.py:411
  15.4 16.1 %collective-permute-start = (bf16[1200,128]{1,0:T(8,128)(2,1)S(1)}, bf16[1200,128]{1,0:T(8,128)(2,1)S(1)}, u32[]{:S(2)}, u32[]{:S(2)}) collective-permute-start(bf16[1200,128]{1,0:T(8,128)(2,1)S(1)} %get-tuple-element.34), channel_id=1, source_target_pairs={{4,8},{8,4},{5,9},{9,5},{6,10},{10,6},{7,11},{11,7},{20,24},{24,20... | collective-permute-start | bytes 921608 | tf_op jit(solution)/shard_map/ppermute | solution.py:410
  16.1 6.8 %collective-permute-start.3 = (bf16[18,32,128]{2,1,0:T(8,128)(2,1)S(1)}, bf16[18,32,128]{2,1,0:T(8,128)(2,1)S(1)}, u32[]{:S(2)}, u32[]{:S(2)}) collective-permute-start(bf16[18,32,128]{2,1,0:T(8,128)(2,1)S(1)} %collective-permute-done.2.refs_2_), channel_id=1, source_target_pairs={{0,16},{16,0},{1,17},{17,1},{2,18},{18,2},{3,19},{19,3},{4,20},{20... | collective-permute-start | bytes 442376 | tf_op jit(solution)/shard_map/ppermute | solution.py:340
  20.3 5.1 %collective-permute-start.5 = (bf16[18,32,128]{2,1,0:T(8,128)(2,1)S(1)}, bf16[18,32,128]{2,1,0:T(8,128)(2,1)S(1)}, u32[]{:S(2)}, u32[]{:S(2)}) collective-permute-start(bf16[18,32,128]{2,1,0:T(8,128)(2,1)S(1)} %collective-permute-done.4.refs_3_), channel_id=1, source_target_pairs={{0,16},{16,0},{1,17},{17,1},{2,18},{18,2},{3,19},{19,3},{4,20},{20... | collective-permute-start | bytes 442376 | tf_op jit(solution)/shard_map/ppermute | solution.py:340
  26.5 5.1 %collective-permute-start.6 = (f32[36,128]{1,0:T(8,128)S(1)}, f32[36,128]{1,0:T(8,128)S(1)}, u32[]{:S(2)}, u32[]{:S(2)}) collective-permute-start(f32[36,128]{1,0:T(8,128)S(1)} %get-tuple-element.44.refs_0_), channel_id=1, source_target_pairs={{0,4},{4,0},{8,12},{12,8},{1,5},{5,1},{9,13},{13,9},{2,6},{6,2},{1... | collective-permute-start | bytes 55304 | tf_op jit(solution)/shard_map/ppermute | solution.py:340
  27.2 4.7 %collective-permute-start.7 = (f32[36,128]{1,0:T(8,128)S(1)}, f32[36,128]{1,0:T(8,128)S(1)}, u32[]{:S(2)}, u32[]{:S(2)}) collective-permute-start(f32[36,128]{1,0:T(8,128)S(1)} %get-tuple-element.44.refs_0_), channel_id=1, source_target_pairs={{0,8},{4,12},{8,0},{12,4},{1,9},{5,13},{9,1},{13,5},{2,10},{6,14},... | collective-permute-start | bytes 55304 | tf_op jit(solution)/shard_map/ppermute | solution.py:340
  29.7 6.1 %collective-permute-start.8 = (f32[36,128]{1,0:T(8,128)S(1)}, f32[36,128]{1,0:T(8,128)S(1)}, u32[]{:S(2)}, u32[]{:S(2)}) collective-permute-start(f32[36,128]{1,0:T(8,128)S(1)} %get-tuple-element.44.refs_0_), channel_id=1, source_target_pairs={{0,12},{4,8},{8,4},{12,0},{1,13},{5,9},{9,5},{13,1},{2,14},{6,10},... | collective-permute-start | bytes 55304 | tf_op jit(solution)/shard_map/ppermute | solution.py:340
  36.4 12.2 %collective-permute-start.9 = (bf16[1200,128]{1,0:T(8,128)(2,1)S(1)}, bf16[1200,128]{1,0:T(8,128)(2,1)S(1)}, u32[]{:S(2)}, u32[]{:S(2)}) collective-permute-start(bf16[1200,128]{1,0:T(8,128)(2,1)S(1)} %get-tuple-element.49), channel_id=1, source_target_pairs={{0,4},{4,0},{8,12},{12,8},{1,5},{5,1},{9,13},{13,9},{2,6},{6,2},{1... | collective-permute-start | bytes 921608 | tf_op jit(solution)/shard_map/ppermute | solution.py:340
  36.4 12.8 %collective-permute-start.11 = (bf16[1200,128]{1,0:T(8,128)(2,1)S(1)}, bf16[1200,128]{1,0:T(8,128)(2,1)S(1)}, u32[]{:S(2)}, u32[]{:S(2)}) collective-permute-start(bf16[1200,128]{1,0:T(8,128)(2,1)S(1)} %relay_chunk.1), channel_id=1, source_target_pairs={{0,8},{4,12},{8,0},{12,4},{1,9},{5,13},{9,1},{13,5},{2,10},{6,14},... | collective-permute-start | bytes 921608 | tf_op jit(solution)/shard_map/ppermute | solution.py:340
  37.9 1.9 %collective-permute-start.12 = (f32[2,128]{1,0:T(2,128)S(1)}, f32[2,128]{1,0:T(2,128)S(1)}, u32[]{:S(2)}, u32[]{:S(2)}) collective-permute-start(f32[2,128]{1,0:T(2,128)S(1)} %get-tuple-element.48.refs_2_), channel_id=1, source_target_pairs={{0,1},{1,0},{2,3},{3,2},{4,5},{5,4},{6,7},{7,6},{8,9},{9,8},{10,11... | collective-permute-start | bytes 3080 | tf_op jit(solution)/shard_map/ppermute | solution.py:340
  37.9 3.6 %collective-permute-start.13 = (f32[2,128]{1,0:T(2,128)S(1)}, f32[2,128]{1,0:T(2,128)S(1)}, u32[]{:S(2)}, u32[]{:S(2)}) collective-permute-start(f32[2,128]{1,0:T(2,128)S(1)} %get-tuple-element.48.refs_2_), channel_id=1, source_target_pairs={{0,2},{1,3},{2,0},{3,1},{4,6},{5,7},{6,4},{7,5},{8,10},{9,11},{10,... | collective-permute-start | bytes 3080 | tf_op jit(solution)/shard_map/ppermute | solution.py:340
  39.4 3.0 %collective-permute-start.14 = (f32[2,128]{1,0:T(2,128)S(1)}, f32[2,128]{1,0:T(2,128)S(1)}, u32[]{:S(2)}, u32[]{:S(2)}) collective-permute-start(f32[2,128]{1,0:T(2,128)S(1)} %get-tuple-element.48.refs_2_), channel_id=1, source_target_pairs={{0,3},{1,2},{2,1},{3,0},{4,7},{5,6},{6,5},{7,4},{8,11},{9,10},{10,... | collective-permute-start | bytes 3080 | tf_op jit(solution)/shard_map/ppermute | solution.py:340
  43.9 1.9 %collective-permute-start.15 = (f32[2,512]{1,0:T(2,128)S(1)}, f32[2,512]{1,0:T(2,128)S(1)}, u32[]{:S(2)}, u32[]{:S(2)}) collective-permute-start(f32[2,512]{1,0:T(2,128)S(1)} %partial_weights.1.refs_0_), channel_id=1, source_target_pairs={{0,1},{1,0},{2,3},{3,2},{4,5},{5,4},{6,7},{7,6},{8,9},{9,8},{10,11... | collective-permute-start | bytes 12296 | tf_op jit(solution)/shard_map/ppermute | solution.py:340
  44.4 3.6 %collective-permute-start.16 = (f32[2,512]{1,0:T(2,128)S(1)}, f32[2,512]{1,0:T(2,128)S(1)}, u32[]{:S(2)}, u32[]{:S(2)}) collective-permute-start(f32[2,512]{1,0:T(2,128)S(1)} %partial_weights.1.refs_0_), channel_id=1, source_target_pairs={{0,2},{1,3},{2,0},{3,1},{4,6},{5,7},{6,4},{7,5},{8,10},{9,11},{10,... | collective-permute-start | bytes 12296 | tf_op jit(solution)/shard_map/ppermute | solution.py:340
  45.0 3.1 %collective-permute-start.17 = (f32[2,512]{1,0:T(2,128)S(1)}, f32[2,512]{1,0:T(2,128)S(1)}, u32[]{:S(2)}, u32[]{:S(2)}) collective-permute-start(f32[2,512]{1,0:T(2,128)S(1)} %partial_weights.1.refs_0_), channel_id=1, source_target_pairs={{0,3},{1,2},{2,1},{3,0},{4,7},{5,6},{6,5},{7,4},{8,11},{9,10},{10,... | collective-permute-start | bytes 12296 | tf_op jit(solution)/shard_map/ppermute | solution.py:340

commit v8 on v7

--- a/solution.py
+++ b/solution.py
@@ -33,13 +33,13 @@
 
 def call(
     kernel, out_shape, name, flops, bytes_accessed, in_specs, scratch_shapes=(),
-    out_spec=IN_VMEM,
+    out_spec=None,
 ):
     return pl.pallas_call(
         kernel,
         out_shape=out_shape,
         in_specs=in_specs,
-        out_specs=jax.tree.map(lambda _: out_spec, out_shape),
+        out_specs=out_spec or jax.tree.map(lambda _: IN_VMEM, out_shape),
         scratch_shapes=scratch_shapes,
         compiler_params=pltpu.CompilerParams(vmem_limit_bytes=VMEM_LIMIT),
         cost_estimate=pl.CostEstimate(
@@ -191,9 +191,10 @@
     sent_ref[blocks * rows :, :] = tops[...].astype(jnp.bfloat16)
 
 
-def last_add_kernel(messages, own_ref, *refs):
+def last_add_kernel(messages, owners, own_ref, *refs):
     sent_refs, refs = refs[: len(messages)], refs[len(messages) :]
-    act_ref, grad_ref, *tops_refs, sums, sems = refs
+    weight_refs, refs = refs[:owners], refs[owners:]
+    act_ref, grad_ref, score_ref, *tops_refs, sums, sems = refs
     blocks, rows, _ = own_ref.shape
     load_tops(messages, rows, sent_refs, tops_refs)
     copies = []
@@ -210,6 +211,7 @@
             )
         )
         copies[-1].start()
+    score_kernel(weight_refs, score_ref)
     for copy in copies:
         copy.wait()
 
@@ -327,8 +329,7 @@
         weight_ref[index : index + 1, :] = sums[0:1]
 
 
-def score_kernel(*refs):
-    *weight_refs, score_ref = refs
+def score_kernel(weight_refs, score_ref):
     weights = weight_refs[0][...]
     for weight_ref in weight_refs[1:]:
         weights = weights + weight_ref[...]
@@ -432,7 +433,7 @@
         )(*after([grams[1], relayed], sums))
     sums = share(sums[0], "dp", direct)
     if pieces == 4:
-        sums = after(sums, middle)
+        sums = after(sums, (middle, sent[2]))
     act_eigen, grad_eigen, eigen, totals = call(
         functools.partial(combine_kernel, halves),
         [f32(act_blocks, BLK), f32(grad_blocks, BLK), f32(blocks, BLK), f32(2, BLK)],
@@ -440,9 +441,9 @@
     )(side, *sums)
     arrived = {}
     sent.pop(3, None)
+    totals = share(totals, "owner", direct)
     for mask in sent:
-        arrived[mask] = swap(after([sent[mask]], totals)[0], "dp", mask)
-    totals = share(totals, "owner", direct)
+        arrived[mask] = swap(after([sent[mask]], totals[:2])[0], "dp", mask)
     weights = call(
         functools.partial(weight_kernel, halves, act_blocks // halves),
         f32(2, tokens), "partial_weights", 0, 4 * tokens * blocks * BLK,
@@ -454,32 +455,36 @@
         ],
     )(eigen, *powers, *totals)
     weights = share(weights, "owner", direct)
-    token_scores = call(
-        score_kernel, f32(1, tokens), "token_scores", 0, 8 * tokens * len(weights),
-        [IN_VMEM] * len(weights),
-    )(*weights)
-
-    def add(kernel, chunks, out_shape, scratch_shapes=(), **options):
-        messages = [(None, *whole_range)] * len(chunks)
-        return call(
-            functools.partial(kernel, messages), out_shape, "add_chunks", 0, 12 * own.size,
-            [IN_VMEM] * (1 + len(chunks)),
-            [pltpu.VMEM((scale_rows(*whole_range), BLK), jnp.float32)] * len(chunks)
-            + [*scratch_shapes],
-            **options,
-        )(own, *chunks)
+
+    def tops_of(count):
+        return [pltpu.VMEM((scale_rows(0, blocks), BLK), jnp.float32)] * count
 
     if pieces == 4:
-        own = add(add_kernel, [middle, arrived.pop(1)], f32(*own.shape))
-    if arrived:
-        covariance = add(
-            last_add_kernel, [*arrived.values()],
-            [f32(act_blocks, rows, BLK), f32(grad_blocks, rows, BLK)],
-            [pltpu.VMEM(own.shape, jnp.float32), pltpu.SemaphoreType.DMA((blocks // GROUP,))],
-            out_spec=pl.BlockSpec(memory_space=pl.ANY),
-        )
+        own = call(
+            functools.partial(add_kernel, [(None, 0, blocks)] * 2),
+            f32(*own.shape), "add_chunks", 0, 16 * own.size, [IN_VMEM] * 3, tops_of(2),
+        )(own, middle, arrived.pop(1))
+        weights[1:] = after(weights[1:], own)
+    chunks = list(arrived.values())
+    if chunks:
+        anywhere = pl.BlockSpec(memory_space=pl.ANY)
+        *covariance, token_scores = call(
+            functools.partial(last_add_kernel, [(None, 0, blocks)] * len(chunks), len(weights)),
+            [f32(act_blocks, rows, BLK), f32(grad_blocks, rows, BLK), f32(1, tokens)],
+            "last_sums", 0, 12 * own.size, [IN_VMEM] * (1 + len(chunks) + len(weights)),
+            [
+                *tops_of(len(chunks)),
+                pltpu.VMEM(own.shape, jnp.float32),
+                pltpu.SemaphoreType.DMA((blocks // GROUP,)),
+            ],
+            out_spec=[anywhere, anywhere, IN_VMEM],
+        )(own, *chunks, *weights)
     else:
         covariance = own[:act_blocks], own[act_blocks:]
+        token_scores = call(
+            lambda *refs: score_kernel(refs[:-1], refs[-1]),
+            f32(1, tokens), "token_scores", 0, 8 * tokens, [IN_VMEM] * len(weights),
+        )(*weights)
     return (
         *covariance,
         act_eigen.reshape(-1),

time: 50.5 us -> 55.8 us (1.10)
  waiting for transfers between devices: 14.5 us -> 19.9 us
    ppermute x16, waiting for transfers between devices: 14.5 us -> 19.9 us  [swap(): return lax.ppermute(value, axis, [(i, i ^ mask) for i in range(count)])]
    pallas_call x3 -> x2, Pallas kernels: 2.26 us -> 2.25 us  [the longest x1 1.62 us: local(): call(functools.partial(last_add_kernel, [(None, 0, blocks)] * len(chunks)...]
  transfers between devices with their start and end apart: 18 -> 18, of which waited for: 7 -> 9; matrix products, arithmetic and copies ran while one was open for 0% -> 0% of each run, Pallas kernels for 19% -> 17%
where the time goes in v8:
time: 55.8 us; the launch traced here: 55.6 us
  starting transfers between devices  22.4 us (40%)
  waiting for transfers between devices  19.9 us (36%)
  Pallas kernels  12.5 us (22%)
  between operations  0.76 us (1%)
    ppermute x16, waiting for transfers between devices, swap(): return lax.ppermute(value, axis, [(i, i ^ mask) for i in range(count)])  19.9 us
    ppermute x16, starting transfers between devices, swap(): return lax.ppermute(value, axis, [(i, i ^ mask) for i in range(count)])  18.4 us
    pallas_call x1, Pallas kernels, local(): call(functools.partial(gram_kernel, pieces, coded, scale), [bf16(*activat...  4.56 us
    ppermute x1, starting transfers between devices, local(): relayed = lax.ppermute(sent[3], 'dp', [(0, 1), (3, 2)])  3.32 us
    pallas_call x2, Pallas kernels, local(): call(functools.partial(eigen_kernel, part, halves, masks, pieces, scale),...  1.95 us
    pallas_call x1, Pallas kernels, local(): call(functools.partial(last_add_kernel, [(None, 0, blocks)] * len(chunks)...  1.62 us
    pallas_call x1, Pallas kernels, local(): call(functools.partial(weight_kernel, halves, act_blocks // halves), f32(...  1.48 us
  transfers between devices with their start and end apart: 18, of which 9 were waited for; matrix products, arithmetic and copies ran while one was open for 0% of the time, Pallas kernels for 17%

profile of v8, /device:TPU:0, one launch (start us, length us, event | category | flops | bytes accessed | tf_op | source)
XLA Modules:
  0.0 55.6 jit_solution(16795461820880078709)
XLA Ops:
  0.6 1.1 %pack_basis.1 = (bf16[36,32,128]{2,1,0:T(8,128)(2,1)S(1)}, bf16[18,32,128]{2,1,0:T(8,128)(2,1)S(1)}) custom-call(s32[1]{0:T(128)} %bitcast.1.side_ref, bf16[8,32,128]{2,1,0:T(8,128)(2,1)} %act_ref.1, bf16[28,32,128]{2,1,0:T(8,128)(2,1)} %grad_ref.1), custom_call_target="tpu_custom_call" | custom-call | bytes 294912 | tf_op jit(solution)/shard_map/pack_basis/pallas_call | solution.py:369
  1.7 5.1 %collective-permute-start.2 = (bf16[18,32,128]{2,1,0:T(8,128)(2,1)S(1)}, bf16[18,32,128]{2,1,0:T(8,128)(2,1)S(1)}, u32[]{:S(2)}, u32[]{:S(2)}) collective-permute-start(bf16[18,32,128]{2,1,0:T(8,128)(2,1)S(1)} %get-tuple-element.43), channel_id=1, source_target_pairs={{0,12},{4,8},{8,4},{12,0},{1,13},{5,9},{9,5},{13,1},{2,14},{6,10},... | collective-permute-start | bytes 442376 | tf_op jit(solution)/shard_map/ppermute | solution.py:341
  6.8 0.0 collective-permute-start.4
  6.8 0.6 %collective-permute-start.1 = (bf16[36,32,128]{2,1,0:T(8,128)(2,1)S(1)}, bf16[36,32,128]{2,1,0:T(8,128)(2,1)S(1)}, u32[]{:S(2)}, u32[]{:S(2)}) collective-permute-start(bf16[36,32,128]{2,1,0:T(8,128)(2,1)S(1)} %get-tuple-element.42.refs_0_), channel_id=1, source_target_pairs={{0,4},{4,0},{8,12},{12,8},{1,5},{5,1},{9,13},{13,9},{2,6},{6,2},{1... | collective-permute-start | bytes 884744 | tf_op jit(solution)/shard_map/ppermute | solution.py:341
  7.5 4.6 %partial_gram.1 = (bf16[512,1024]{1,0:T(8,128)(2,1)S(1)}, bf16[512,3584]{1,0:T(8,128)(2,1)S(1)}, f32[36,32,128]{2,1,0:T(8,128)S(1)}, f32[36,32,128]{2,1,0:T(8,12...) custom-call(s32[1]{0:T(128)} %bitcast.me_ref, bf16[512,1024]{1,0:T(8,128)(2,1)} %act_hbm.1, ...), custom_call_target="tpu_custom_call" | custom-call | flops 1207959552 | bytes 4718592 | tf_op jit(solution)/shard_map/partial_gram/pallas_call | solution.py:390
  12.0 3.3 %collective-permute-start.9 = (bf16[1200,128]{1,0:T(8,128)(2,1)S(1)}, bf16[1200,128]{1,0:T(8,128)(2,1)S(1)}, u32[]{:S(2)}, u32[]{:S(2)}) collective-permute-start(bf16[1200,128]{1,0:T(8,128)(2,1)S(1)} %get-tuple-element.38), channel_id=1, source_target_pairs={{0,4},{12,8},{1,5},{13,9},{2,6},{14,10},{3,7},{15,11},{16,20},{28,... | collective-permute-start | bytes 921608 | tf_op jit(solution)/shard_map/ppermute | solution.py:412
  15.4 0.7 %collective-permute-start = (bf16[1200,128]{1,0:T(8,128)(2,1)S(1)}, bf16[1200,128]{1,0:T(8,128)(2,1)S(1)}, u32[]{:S(2)}, u32[]{:S(2)}) collective-permute-start(bf16[1200,128]{1,0:T(8,128)(2,1)S(1)} %get-tuple-element.38), channel_id=1, source_target_pairs={{4,8},{8,4},{5,9},{9,5},{6,10},{10,6},{7,11},{11,7},{20,24},{24,20... | collective-permute-start | bytes 921608 | tf_op jit(solution)/shard_map/ppermute | solution.py:411
  16.1 0.0 collective-permute-done.2.refs_2_
  16.1 1.6 %collective-permute-start.3 = (bf16[18,32,128]{2,1,0:T(8,128)(2,1)S(1)}, bf16[18,32,128]{2,1,0:T(8,128)(2,1)S(1)}, u32[]{:S(2)}, u32[]{:S(2)}) collective-permute-start(bf16[18,32,128]{2,1,0:T(8,128)(2,1)S(1)} %collective-permute-done.2.refs_2_), channel_id=1, source_target_pairs={{0,16},{16,0},{1,17},{17,1},{2,18},{18,2},{3,19},{19,3},{4,20},{20... | collective-permute-start | bytes 442376 | tf_op jit(solution)/shard_map/ppermute | solution.py:341
  17.6 2.7 %collective-permute-done.4.refs_3_ = bf16[18,32,128]{2,1,0:T(8,128)(2,1)S(1)} collective-permute-done((bf16[18,32,128]{2,1,0:T(8,128)(2,1)S(1)}, bf16[18,32,128]{2,1,0:T(8,128)(2,1)S(1)}, u32[]{:S(2)}, u32[]{:S(2)}) %collective-permute-start.4) | collective-permute-done | bytes 147488 | tf_op jit(solution)/shard_map/ppermute | solution.py:341
  20.3 1.5 %collective-permute-start.5 = (bf16[18,32,128]{2,1,0:T(8,128)(2,1)S(1)}, bf16[18,32,128]{2,1,0:T(8,128)(2,1)S(1)}, u32[]{:S(2)}, u32[]{:S(2)}) collective-permute-start(bf16[18,32,128]{2,1,0:T(8,128)(2,1)S(1)} %collective-permute-done.4.refs_3_), channel_id=1, source_target_pairs={{0,16},{16,0},{1,17},{17,1},{2,18},{18,2},{3,19},{19,3},{4,20},{20... | collective-permute-start | bytes 442376 | tf_op jit(solution)/shard_map/ppermute | solution.py:341
  21.8 0.0 collective-permute-done.1.refs_1_
  21.8 1.0 %partial_eigen.2 = (f32[9,512,256]{2,1,0:T(8,128)S(1)}, f32[18,128]{1,0:T(8,128)S(1)}) custom-call(s32[1]{0:T(128)} %bitcast.me_ref, s32[1]{0:T(128)} %bitcast.1.side_ref, bf16[512,1024]{1,0:T(8,128)(2,1)S(1)} %get-tuple-element.40.act_ref, bf16[512,3584]{1,0:T(8,128)(2,1)S(1)} %get-tuple-element.41.grad_ref, ...), custom_call_target="tpu_custom_call" | custom-call | flops 301989888 | bytes 2359296 | tf_op jit(solution)/shard_map/partial_eigen/pallas_call | solution.py:420
  22.8 0.0 collective-permute-done.3.refs_2_
  22.8 2.6 %collective-permute-done.5.refs_3_ = bf16[18,32,128]{2,1,0:T(8,128)(2,1)S(1)} collective-permute-done((bf16[18,32,128]{2,1,0:T(8,128)(2,1)S(1)}, bf16[18,32,128]{2,1,0:T(8,128)(2,1)S(1)}, u32[]{:S(2)}, u32[]{:S(2)}) %collective-permute-start.5) | collective-permute-done | bytes 147488 | tf_op jit(solution)/shard_map/ppermute | solution.py:341
  25.5 1.0 %partial_eigen.3 = (f32[9,512,256]{2,1,0:T(8,128)S(1)}, f32[36,128]{1,0:T(8,128)S(1)}) custom-call(s32[1]{0:T(128)} %bitcast.me_ref, s32[1]{0:T(128)} %bitcast.1.side_ref, bf16[512,1024]{1,0:T(8,128)(2,1)S(1)} %get-tuple-element.40.act_ref, bf16[512,3584]{1,0:T(8,128)(2,1)S(1)} %get-tuple-element.41.grad_ref, ...), custom_call_target="tpu_custom_call" | custom-call | flops 301989888 | bytes 2359296 | tf_op jit(solution)/shard_map/partial_eigen/pallas_call | solution.py:420
  26.5 0.7 %collective-permute-start.6 = (f32[36,128]{1,0:T(8,128)S(1)}, f32[36,128]{1,0:T(8,128)S(1)}, u32[]{:S(2)}, u32[]{:S(2)}) collective-permute-start(f32[36,128]{1,0:T(8,128)S(1)} %get-tuple-element.51.refs_0_), channel_id=1, source_target_pairs={{0,4},{4,0},{8,12},{12,8},{1,5},{5,1},{9,13},{13,9},{2,6},{6,2},{1... | collective-permute-start | bytes 55304 | tf_op jit(solution)/shard_map/ppermute | solution.py:341
  27.2 2.6 %collective-permute-start.7 = (f32[36,128]{1,0:T(8,128)S(1)}, f32[36,128]{1,0:T(8,128)S(1)}, u32[]{:S(2)}, u32[]{:S(2)}) collective-permute-start(f32[36,128]{1,0:T(8,128)S(1)} %get-tuple-element.51.refs_0_), channel_id=1, source_target_pairs={{0,8},{4,12},{8,0},{12,4},{1,9},{5,13},{9,1},{13,5},{2,10},{6,14},... | collective-permute-start | bytes 55304 | tf_op jit(solution)/shard_map/ppermute | solution.py:341
  29.7 1.2 %collective-permute-start.8 = (f32[36,128]{1,0:T(8,128)S(1)}, f32[36,128]{1,0:T(8,128)S(1)}, u32[]{:S(2)}, u32[]{:S(2)}) collective-permute-start(f32[36,128]{1,0:T(8,128)S(1)} %get-tuple-element.51.refs_0_), channel_id=1, source_target_pairs={{0,12},{4,8},{8,4},{12,0},{1,13},{5,9},{9,5},{13,1},{2,14},{6,10},... | collective-permute-start | bytes 55304 | tf_op jit(solution)/shard_map/ppermute | solution.py:341
  30.9 0.0 collective-permute-done.9.relayed_ref
  30.9 0.6 %relay_chunk.1 = bf16[1200,128]{1,0:T(8,128)(2,1)S(1)} custom-call(f32[36,32,128]{2,1,0:T(8,128)S(1)} %get-tuple-element.49.far_ref, bf16[1200,128]{1,0:T(8,128)(2,1)S(1)} %collective-permute-done.9.relayed_ref), custom_call_target="tpu_custom_call" | custom-call | bytes 1769472 | tf_op jit(solution)/shard_map/relay_chunk/pallas_call | solution.py:429
  31.5 0.0 collective-permute-done.refs_0_
  31.5 0.0 collective-permute-done.6.refs_1_
  31.5 0.3 collective-permute-done.7.refs_2_
  31.8 3.5 %collective-permute-done.8.refs_3_ = f32[36,128]{1,0:T(8,128)S(1)} collective-permute-done((f32[36,128]{1,0:T(8,128)S(1)}, f32[36,128]{1,0:T(8,128)S(1)}, u32[]{:S(2)}, u32[]{:S(2)}) %collective-permute-start.8) | collective-permute-done | bytes 18464 | tf_op jit(solution)/shard_map/ppermute | solution.py:341
  35.3 0.6 %combine_eigen.1 = (f32[8,128]{1,0:T(8,128)}, f32[28,128]{1,0:T(8,128)}, f32[36,128]{1,0:T(8,128)S(1)}, f32[2,128]{1,0:T(2,128)S(1)}) custom-call(s32[1]{0:T(128)} %bitcast.1.side_ref, f32[36,128]{1,0:T(8,128)S(1)} %get-tuple-element.51.refs_0_, f32[36,128]{1,0:T(8,128)S(1)} %collective-permute-done.6.refs_1_, f32[36,128]{1,0:T(8,128)S(1)} %collective-permute-done.7.refs_2_, ...), custom_call_target="tpu_custom_call" | custom-call | bytes 73728 | tf_op jit(solution)/shard_map/combine_eigen/pallas_call | solution.py:437
  35.9 0.0 collective-permute-start.10
  35.9 1.1 %collective-permute-done.10.refs_3_ = f32[2,128]{1,0:T(2,128)S(1)} collective-permute-done((f32[2,128]{1,0:T(2,128)S(1)}, f32[2,128]{1,0:T(2,128)S(1)}, u32[]{:S(2)}, u32[]{:S(2)}) %collective-permute-start.10) | collective-permute-done | bytes 1056 | tf_op jit(solution)/shard_map/ppermute | solution.py:341
  37.1 0.0 collective-permute-start.11
  37.1 1.7 %collective-permute-start.12 = (bf16[1200,128]{1,0:T(8,128)(2,1)S(1)}, bf16[1200,128]{1,0:T(8,128)(2,1)S(1)}, u32[]{:S(2)}, u32[]{:S(2)}) collective-permute-start(bf16[1200,128]{1,0:T(8,128)(2,1)S(1)} %relay_chunk.1), channel_id=1, source_target_pairs={{0,8},{4,12},{8,0},{12,4},{1,9},{5,13},{9,1},{13,5},{2,10},{6,14},... | collective-permute-start | bytes 921608 | tf_op jit(solution)/shard_map/ppermute | solution.py:341
  38.8 1.5 %collective-permute-start.13 = (f32[2,128]{1,0:T(2,128)S(1)}, f32[2,128]{1,0:T(2,128)S(1)}, u32[]{:S(2)}, u32[]{:S(2)}) collective-permute-start(f32[2,128]{1,0:T(2,128)S(1)} %get-tuple-element.55.refs_2_), channel_id=1, source_target_pairs={{0,2},{1,3},{2,0},{3,1},{4,6},{5,7},{6,4},{7,5},{8,10},{9,11},{10,... | collective-permute-start | bytes 3080 | tf_op jit(solution)/shard_map/ppermute | solution.py:341
  40.3 0.0 collective-permute-start.14
  40.3 2.1 %collective-permute-done.13.refs_4_ = f32[2,128]{1,0:T(2,128)S(1)} collective-permute-done((f32[2,128]{1,0:T(2,128)S(1)}, f32[2,128]{1,0:T(2,128)S(1)}, u32[]{:S(2)}, u32[]{:S(2)}) %collective-permute-start.13) | collective-permute-done | bytes 1056 | tf_op jit(solution)/shard_map/ppermute | solution.py:341
  42.4 0.9 %collective-permute-done.14.refs_5_ = f32[2,128]{1,0:T(2,128)S(1)} collective-permute-done((f32[2,128]{1,0:T(2,128)S(1)}, f32[2,128]{1,0:T(2,128)S(1)}, u32[]{:S(2)}, u32[]{:S(2)}) %collective-permute-start.14) | collective-permute-done | bytes 1056 | tf_op jit(solution)/shard_map/ppermute | solution.py:341
  43.3 1.5 %partial_weights.1.refs_1_ = f32[2,512]{1,0:T(2,128)S(1)} custom-call(f32[36,128]{1,0:T(8,128)S(1)} %get-tuple-element.58.eigen_ref, f32[9,512,256]{2,1,0:T(8,128)S(1)} %get-tuple-element.59.refs_0_, f32[9,512,256]{2,1,0:T(8,128)S(1)} %get-tuple-element.60.refs_1_, f32[2,128]{1,0:T(2,128)S(1)} %get-tuple-element.55.refs_2_, ...), custom_call_target="tpu_custom_call" | custom-call | bytes 9437184 | tf_op jit(solution)/shard_map/partial_weights/pallas_call | solution.py:447
  44.8 0.0 collective-permute-start.15
  44.8 0.7 %collective-permute-start.16 = (f32[2,512]{1,0:T(2,128)S(1)}, f32[2,512]{1,0:T(2,128)S(1)}, u32[]{:S(2)}, u32[]{:S(2)}) collective-permute-start(f32[2,512]{1,0:T(2,128)S(1)} %partial_weights.1.refs_1_), channel_id=1, source_target_pairs={{0,2},{1,3},{2,0},{3,1},{4,6},{5,7},{6,4},{7,5},{8,10},{9,11},{10,... | collective-permute-start | bytes 12296 | tf_op jit(solution)/shard_map/ppermute | solution.py:341
  45.5 1.1 %collective-permute-start.17 = (f32[2,512]{1,0:T(2,128)S(1)}, f32[2,512]{1,0:T(2,128)S(1)}, u32[]{:S(2)}, u32[]{:S(2)}) collective-permute-start(f32[2,512]{1,0:T(2,128)S(1)} %partial_weights.1.refs_1_), channel_id=1, source_target_pairs={{0,3},{1,2},{2,1},{3,0},{4,7},{5,6},{6,5},{7,4},{8,11},{9,10},{10,... | collective-permute-start | bytes 12296 | tf_op jit(solution)/shard_map/ppermute | solution.py:341
  46.7 4.9 %collective-permute-done.11.refs_1_ = bf16[1200,128]{1,0:T(8,128)(2,1)S(1)} collective-permute-done((bf16[1200,128]{1,0:T(8,128)(2,1)S(1)}, bf16[1200,128]{1,0:T(8,128)(2,1)S(1)}, u32[]{:S(2)}, u32[]{:S(2)}) %collective-permute-start.11) | collective-permute-done | bytes 307232 | tf_op jit(solution)/shard_map/ppermute | solution.py:341
  51.6 0.6 %add_chunks.1.own_ref = f32[36,32,128]{2,1,0:T(8,128)S(1)} custom-call(f32[36,32,128]{2,1,0:T(8,128)S(1)} %get-tuple-element.37.own_ref, bf16[1200,128]{1,0:T(8,128)(2,1)S(1)} %collective-permute-done.refs_0_, bf16[1200,128]{1,0:T(8,128)(2,1)S(1)} %collective-permute-done.11.refs_1_), custom_call_target="tpu_custom_call" | custom-call | bytes 2359296 | tf_op jit(solution)/shard_map/add_chunks/pallas_call | solution.py:463
  52.2 0.0 collective-permute-done.15.refs_2_
  52.3 0.0 collective-permute-done.16.refs_3_
  52.3 0.0 collective-permute-done.17.refs_4_
  52.3 1.7 %collective-permute-done.12.refs_0_ = bf16[1200,128]{1,0:T(8,128)(2,1)S(1)} collective-permute-done((bf16[1200,128]{1,0:T(8,128)(2,1)S(1)}, bf16[1200,128]{1,0:T(8,128)(2,1)S(1)}, u32[]{:S(2)}, u32[]{:S(2)}) %collective-permute-start.12) | collective-permute-done | bytes 307232 | tf_op jit(solution)/shard_map/ppermute | solution.py:341
  54.0 1.6 %last_sums.1 = (f32[8,32,128]{2,1,0:T(8,128)}, f32[28,32,128]{2,1,0:T(8,128)}, f32[1,512]{1,0:T(1,128)}) custom-call(f32[36,32,128]{2,1,0:T(8,128)S(1)} %add_chunks.1.own_ref, bf16[1200,128]{1,0:T(8,128)(2,1)S(1)} %collective-permute-done.12.refs_0_, f32[2,512]{1,0:T(2,128)S(1)} %partial_weights.1.refs_1_, f32[2,512]{1,0:T(2,128)S(1)} %collective-permute-done.15.refs_2_, ...), custom_call_target="tpu_custom_call" | custom-call | bytes 1769472 | tf_op jit(solution)/shard_map/last_sums/pallas_call | solution.py:471
Async XLA Ops:
  1.7 14.3 %collective-permute-start.2 = (bf16[18,32,128]{2,1,0:T(8,128)(2,1)S(1)}, bf16[18,32,128]{2,1,0:T(8,128)(2,1)S(1)}, u32[]{:S(2)}, u32[]{:S(2)}) collective-permute-start(bf16[18,32,128]{2,1,0:T(8,128)(2,1)S(1)} %get-tuple-element.43), channel_id=1, source_target_pairs={{0,12},{4,8},{8,4},{12,0},{1,13},{5,9},{9,5},{13,1},{2,14},{6,10},... | collective-permute-start | bytes 442376 | tf_op jit(solution)/shard_map/ppermute | solution.py:341
  6.8 13.5 %collective-permute-start.4 = (bf16[18,32,128]{2,1,0:T(8,128)(2,1)S(1)}, bf16[18,32,128]{2,1,0:T(8,128)(2,1)S(1)}, u32[]{:S(2)}, u32[]{:S(2)}) collective-permute-start(bf16[18,32,128]{2,1,0:T(8,128)(2,1)S(1)} %get-tuple-element.43), channel_id=1, source_target_pairs={{0,8},{4,12},{8,0},{12,4},{1,9},{5,13},{9,1},{13,5},{2,10},{6,14},... | collective-permute-start | bytes 442376 | tf_op jit(solution)/shard_map/ppermute | solution.py:341
  6.8 15.0 %collective-permute-start.1 = (bf16[36,32,128]{2,1,0:T(8,128)(2,1)S(1)}, bf16[36,32,128]{2,1,0:T(8,128)(2,1)S(1)}, u32[]{:S(2)}, u32[]{:S(2)}) collective-permute-start(bf16[36,32,128]{2,1,0:T(8,128)(2,1)S(1)} %get-tuple-element.42.refs_0_), channel_id=1, source_target_pairs={{0,4},{4,0},{8,12},{12,8},{1,5},{5,1},{9,13},{13,9},{2,6},{6,2},{1... | collective-permute-start | bytes 884744 | tf_op jit(solution)/shard_map/ppermute | solution.py:341
  12.0 18.9 %collective-permute-start.9 = (bf16[1200,128]{1,0:T(8,128)(2,1)S(1)}, bf16[1200,128]{1,0:T(8,128)(2,1)S(1)}, u32[]{:S(2)}, u32[]{:S(2)}) collective-permute-start(bf16[1200,128]{1,0:T(8,128)(2,1)S(1)} %get-tuple-element.38), channel_id=1, source_target_pairs={{0,4},{12,8},{1,5},{13,9},{2,6},{14,10},{3,7},{15,11},{16,20},{28,... | collective-permute-start | bytes 921608 | tf_op jit(solution)/shard_map/ppermute | solution.py:412
  15.4 16.1 %collective-permute-start = (bf16[1200,128]{1,0:T(8,128)(2,1)S(1)}, bf16[1200,128]{1,0:T(8,128)(2,1)S(1)}, u32[]{:S(2)}, u32[]{:S(2)}) collective-permute-start(bf16[1200,128]{1,0:T(8,128)(2,1)S(1)} %get-tuple-element.38), channel_id=1, source_target_pairs={{4,8},{8,4},{5,9},{9,5},{6,10},{10,6},{7,11},{11,7},{20,24},{24,20... | collective-permute-start | bytes 921608 | tf_op jit(solution)/shard_map/ppermute | solution.py:411
  16.1 6.8 %collective-permute-start.3 = (bf16[18,32,128]{2,1,0:T(8,128)(2,1)S(1)}, bf16[18,32,128]{2,1,0:T(8,128)(2,1)S(1)}, u32[]{:S(2)}, u32[]{:S(2)}) collective-permute-start(bf16[18,32,128]{2,1,0:T(8,128)(2,1)S(1)} %collective-permute-done.2.refs_2_), channel_id=1, source_target_pairs={{0,16},{16,0},{1,17},{17,1},{2,18},{18,2},{3,19},{19,3},{4,20},{20... | collective-permute-start | bytes 442376 | tf_op jit(solution)/shard_map/ppermute | solution.py:341
  20.3 5.1 %collective-permute-start.5 = (bf16[18,32,128]{2,1,0:T(8,128)(2,1)S(1)}, bf16[18,32,128]{2,1,0:T(8,128)(2,1)S(1)}, u32[]{:S(2)}, u32[]{:S(2)}) collective-permute-start(bf16[18,32,128]{2,1,0:T(8,128)(2,1)S(1)} %collective-permute-done.4.refs_3_), channel_id=1, source_target_pairs={{0,16},{16,0},{1,17},{17,1},{2,18},{18,2},{3,19},{19,3},{4,20},{20... | collective-permute-start | bytes 442376 | tf_op jit(solution)/shard_map/ppermute | solution.py:341
  26.5 5.1 %collective-permute-start.6 = (f32[36,128]{1,0:T(8,128)S(1)}, f32[36,128]{1,0:T(8,128)S(1)}, u32[]{:S(2)}, u32[]{:S(2)}) collective-permute-start(f32[36,128]{1,0:T(8,128)S(1)} %get-tuple-element.51.refs_0_), channel_id=1, source_target_pairs={{0,4},{4,0},{8,12},{12,8},{1,5},{5,1},{9,13},{13,9},{2,6},{6,2},{1... | collective-permute-start | bytes 55304 | tf_op jit(solution)/shard_map/ppermute | solution.py:341
  27.2 4.7 %collective-permute-start.7 = (f32[36,128]{1,0:T(8,128)S(1)}, f32[36,128]{1,0:T(8,128)S(1)}, u32[]{:S(2)}, u32[]{:S(2)}) collective-permute-start(f32[36,128]{1,0:T(8,128)S(1)} %get-tuple-element.51.refs_0_), channel_id=1, source_target_pairs={{0,8},{4,12},{8,0},{12,4},{1,9},{5,13},{9,1},{13,5},{2,10},{6,14},... | collective-permute-start | bytes 55304 | tf_op jit(solution)/shard_map/ppermute | solution.py:341
  29.7 5.6 %collective-permute-start.8 = (f32[36,128]{1,0:T(8,128)S(1)}, f32[36,128]{1,0:T(8,128)S(1)}, u32[]{:S(2)}, u32[]{:S(2)}) collective-permute-start(f32[36,128]{1,0:T(8,128)S(1)} %get-tuple-element.51.refs_0_), channel_id=1, source_target_pairs={{0,12},{4,8},{8,4},{12,0},{1,13},{5,9},{9,5},{13,1},{2,14},{6,10},... | collective-permute-start | bytes 55304 | tf_op jit(solution)/shard_map/ppermute | solution.py:341
  35.9 1.1 %collective-permute-start.10 = (f32[2,128]{1,0:T(2,128)S(1)}, f32[2,128]{1,0:T(2,128)S(1)}, u32[]{:S(2)}, u32[]{:S(2)}) collective-permute-start(f32[2,128]{1,0:T(2,128)S(1)} %get-tuple-element.55.refs_2_), channel_id=1, source_target_pairs={{0,1},{1,0},{2,3},{3,2},{4,5},{5,4},{6,7},{7,6},{8,9},{9,8},{10,11... | collective-permute-start | bytes 3080 | tf_op jit(solution)/shard_map/ppermute | solution.py:341
  37.1 14.5 %collective-permute-start.11 = (bf16[1200,128]{1,0:T(8,128)(2,1)S(1)}, bf16[1200,128]{1,0:T(8,128)(2,1)S(1)}, u32[]{:S(2)}, u32[]{:S(2)}) collective-permute-start(bf16[1200,128]{1,0:T(8,128)(2,1)S(1)} %get-tuple-element.56), channel_id=1, source_target_pairs={{0,4},{4,0},{8,12},{12,8},{1,5},{5,1},{9,13},{13,9},{2,6},{6,2},{1... | collective-permute-start | bytes 921608 | tf_op jit(solution)/shard_map/ppermute | solution.py:341
  37.1 16.9 %collective-permute-start.12 = (bf16[1200,128]{1,0:T(8,128)(2,1)S(1)}, bf16[1200,128]{1,0:T(8,128)(2,1)S(1)}, u32[]{:S(2)}, u32[]{:S(2)}) collective-permute-start(bf16[1200,128]{1,0:T(8,128)(2,1)S(1)} %relay_chunk.1), channel_id=1, source_target_pairs={{0,8},{4,12},{8,0},{12,4},{1,9},{5,13},{9,1},{13,5},{2,10},{6,14},... | collective-permute-start | bytes 921608 | tf_op jit(solution)/shard_map/ppermute | solution.py:341
  38.8 3.6 %collective-permute-start.13 = (f32[2,128]{1,0:T(2,128)S(1)}, f32[2,128]{1,0:T(2,128)S(1)}, u32[]{:S(2)}, u32[]{:S(2)}) collective-permute-start(f32[2,128]{1,0:T(2,128)S(1)} %get-tuple-element.55.refs_2_), channel_id=1, source_target_pairs={{0,2},{1,3},{2,0},{3,1},{4,6},{5,7},{6,4},{7,5},{8,10},{9,11},{10,... | collective-permute-start | bytes 3080 | tf_op jit(solution)/shard_map/ppermute | solution.py:341
  40.3 3.0 %collective-permute-start.14 = (f32[2,128]{1,0:T(2,128)S(1)}, f32[2,128]{1,0:T(2,128)S(1)}, u32[]{:S(2)}, u32[]{:S(2)}) collective-permute-start(f32[2,128]{1,0:T(2,128)S(1)} %get-tuple-element.55.refs_2_), channel_id=1, source_target_pairs={{0,3},{1,2},{2,1},{3,0},{4,7},{5,6},{6,5},{7,4},{8,11},{9,10},{10,... | collective-permute-start | bytes 3080 | tf_op jit(solution)/shard_map/ppermute | solution.py:341
  44.8 7.5 %collective-permute-start.15 = (f32[2,512]{1,0:T(2,128)S(1)}, f32[2,512]{1,0:T(2,128)S(1)}, u32[]{:S(2)}, u32[]{:S(2)}) collective-permute-start(f32[2,512]{1,0:T(2,128)S(1)} %partial_weights.1.refs_1_), channel_id=1, source_target_pairs={{0,1},{1,0},{2,3},{3,2},{4,5},{5,4},{6,7},{7,6},{8,9},{9,8},{10,11... | collective-permute-start | bytes 12296 | tf_op jit(solution)/shard_map/ppermute | solution.py:341
  44.8 7.5 %collective-permute-start.16 = (f32[2,512]{1,0:T(2,128)S(1)}, f32[2,512]{1,0:T(2,128)S(1)}, u32[]{:S(2)}, u32[]{:S(2)}) collective-permute-start(f32[2,512]{1,0:T(2,128)S(1)} %partial_weights.1.refs_1_), channel_id=1, source_target_pairs={{0,2},{1,3},{2,0},{3,1},{4,6},{5,7},{6,4},{7,5},{8,10},{9,11},{10,... | collective-permute-start | bytes 12296 | tf_op jit(solution)/shard_map/ppermute | solution.py:341
  45.5 6.7 %collective-permute-start.17 = (f32[2,512]{1,0:T(2,128)S(1)}, f32[2,512]{1,0:T(2,128)S(1)}, u32[]{:S(2)}, u32[]{:S(2)}) collective-permute-start(f32[2,512]{1,0:T(2,128)S(1)} %partial_weights.1.refs_1_), channel_id=1, source_target_pairs={{0,3},{1,2},{2,1},{3,0},{4,7},{5,6},{6,5},{7,4},{8,11},{9,10},{10,... | collective-permute-start | bytes 12296 | tf_op jit(solution)/shard_map/ppermute | solution.py:341

commit v9 on v8

--- a/solution.py
+++ b/solution.py
@@ -191,10 +191,9 @@
     sent_ref[blocks * rows :, :] = tops[...].astype(jnp.bfloat16)
 
 
-def last_add_kernel(messages, owners, own_ref, *refs):
+def last_add_kernel(messages, own_ref, *refs):
     sent_refs, refs = refs[: len(messages)], refs[len(messages) :]
-    weight_refs, refs = refs[:owners], refs[owners:]
-    act_ref, grad_ref, score_ref, *tops_refs, sums, sems = refs
+    act_ref, grad_ref, *tops_refs, sums, sems = refs
     blocks, rows, _ = own_ref.shape
     load_tops(messages, rows, sent_refs, tops_refs)
     copies = []
@@ -211,7 +210,6 @@
             )
         )
         copies[-1].start()
-    score_kernel(weight_refs, score_ref)
     for copy in copies:
         copy.wait()
 
@@ -329,7 +327,8 @@
         weight_ref[index : index + 1, :] = sums[0:1]
 
 
-def score_kernel(weight_refs, score_ref):
+def score_kernel(*refs):
+    *weight_refs, score_ref = refs
     weights = weight_refs[0][...]
     for weight_ref in weight_refs[1:]:
         weights = weights + weight_ref[...]
@@ -441,9 +440,9 @@
     )(side, *sums)
     arrived = {}
     sent.pop(3, None)
+    for mask in sent:
+        arrived[mask] = swap(after([sent[mask]], totals)[0], "dp", mask)
     totals = share(totals, "owner", direct)
-    for mask in sent:
-        arrived[mask] = swap(after([sent[mask]], totals[:2])[0], "dp", mask)
     weights = call(
         functools.partial(weight_kernel, halves, act_blocks // halves),
         f32(2, tokens), "partial_weights", 0, 4 * tokens * blocks * BLK,
@@ -465,26 +464,24 @@
             f32(*own.shape), "add_chunks", 0, 16 * own.size, [IN_VMEM] * 3, tops_of(2),
         )(own, middle, arrived.pop(1))
         weights[1:] = after(weights[1:], own)
+    token_scores = call(
+        score_kernel, f32(1, tokens), "token_scores", 0, 8 * tokens, [IN_VMEM] * len(weights)
+    )(*weights)
     chunks = list(arrived.values())
     if chunks:
-        anywhere = pl.BlockSpec(memory_space=pl.ANY)
-        *covariance, token_scores = call(
-            functools.partial(last_add_kernel, [(None, 0, blocks)] * len(chunks), len(weights)),
-            [f32(act_blocks, rows, BLK), f32(grad_blocks, rows, BLK), f32(1, tokens)],
-            "last_sums", 0, 12 * own.size, [IN_VMEM] * (1 + len(chunks) + len(weights)),
+        covariance = call(
+            functools.partial(last_add_kernel, [(None, 0, blocks)] * len(chunks)),
+            [f32(act_blocks, rows, BLK), f32(grad_blocks, rows, BLK)],
+            "add_last_chunk", 0, 12 * own.size, [IN_VMEM] * (1 + len(chunks)),
             [
                 *tops_of(len(chunks)),
                 pltpu.VMEM(own.shape, jnp.float32),
                 pltpu.SemaphoreType.DMA((blocks // GROUP,)),
             ],
-            out_spec=[anywhere, anywhere, IN_VMEM],
-        )(own, *chunks, *weights)
+            out_spec=[pl.BlockSpec(memory_space=pl.ANY)] * 2,
+        )(own, *chunks)
     else:
         covariance = own[:act_blocks], own[act_blocks:]
-        token_scores = call(
-            lambda *refs: score_kernel(refs[:-1], refs[-1]),
-            f32(1, tokens), "token_scores", 0, 8 * tokens, [IN_VMEM] * len(weights),
-        )(*weights)
     return (
         *covariance,
         act_eigen.reshape(-1),

time: 55.8 us -> 49.8 us (0.89)
  waiting for transfers between devices: 19.9 us -> 13.8 us
    ppermute x16, waiting for transfers between devices: 19.9 us -> 13.8 us  [swap(): return lax.ppermute(value, axis, [(i, i ^ mask) for i in range(count)])]
    pallas_call x0 -> x1, Pallas kernels: none -> 0.59 us  [local(): call(score_kernel, f32(1, tokens), 'token_scores', 0, 8 * tokens, [IN_VME...]
    pallas_call x1, Pallas kernels: 1.62 us -> 1.04 us  [local(): call(functools.partial(last_add_kernel, [(None, 0, blocks)] * len(chunks)...]
  transfers between devices with their start and end apart: 18 -> 18, of which waited for: 9 -> 8; matrix products, arithmetic and copies ran while one was open for 0% -> 0% of each run, Pallas kernels for 17% -> 20%
where the time goes in v9:
time: 49.8 us; the launch traced here: 49.7 us
  starting transfers between devices  22.6 us (45%)
  waiting for transfers between devices  13.8 us (28%)
  Pallas kernels  12.5 us (25%)
  between operations  0.75 us (2%)
    ppermute x16, starting transfers between devices, swap(): return lax.ppermute(value, axis, [(i, i ^ mask) for i in range(count)])  18.6 us
    ppermute x16, waiting for transfers between devices, swap(): return lax.ppermute(value, axis, [(i, i ^ mask) for i in range(count)])  13.8 us
    pallas_call x1, Pallas kernels, local(): call(functools.partial(gram_kernel, pieces, coded, scale), [bf16(*activat...  4.56 us
    ppermute x1, starting transfers between devices, local(): relayed = lax.ppermute(sent[3], 'dp', [(0, 1), (3, 2)])  3.32 us
    pallas_call x2, Pallas kernels, local(): call(functools.partial(eigen_kernel, part, halves, masks, pieces, scale),...  1.95 us
    pallas_call x1, Pallas kernels, local(): call(functools.partial(weight_kernel, halves, act_blocks // halves), f32(...  1.48 us
    pallas_call x1, Pallas kernels, local(): call(pack_kernel, [bf16(blocks // part, rows, BLK) for part in range(1, h...  1.08 us
    pallas_call x1, Pallas kernels, local(): call(functools.partial(last_add_kernel, [(None, 0, blocks)] * len(chunks)...  1.04 us
  transfers between devices with their start and end apart: 18, of which 8 were waited for; matrix products, arithmetic and copies ran while one was open for 0% of the time, Pallas kernels for 20%

profile of v9, /device:TPU:0, one launch (start us, length us, event | category | flops | bytes accessed | tf_op | source)
XLA Modules:
  0.0 49.7 jit_solution(16018186121079103728)
XLA Ops:
  0.6 1.1 %pack_basis.1 = (bf16[36,32,128]{2,1,0:T(8,128)(2,1)S(1)}, bf16[18,32,128]{2,1,0:T(8,128)(2,1)S(1)}) custom-call(s32[1]{0:T(128)} %bitcast.1.side_ref, bf16[8,32,128]{2,1,0:T(8,128)(2,1)} %act_ref.1, bf16[28,32,128]{2,1,0:T(8,128)(2,1)} %grad_ref.1), custom_call_target="tpu_custom_call" | custom-call | bytes 294912 | tf_op jit(solution)/shard_map/pack_basis/pallas_call | solution.py:368
  1.7 5.1 %collective-permute-start.2 = (bf16[18,32,128]{2,1,0:T(8,128)(2,1)S(1)}, bf16[18,32,128]{2,1,0:T(8,128)(2,1)S(1)}, u32[]{:S(2)}, u32[]{:S(2)}) collective-permute-start(bf16[18,32,128]{2,1,0:T(8,128)(2,1)S(1)} %get-tuple-element.42), channel_id=1, source_target_pairs={{0,12},{4,8},{8,4},{12,0},{1,13},{5,9},{9,5},{13,1},{2,14},{6,10},... | collective-permute-start | bytes 442376 | tf_op jit(solution)/shard_map/ppermute | solution.py:340
  6.8 0.0 collective-permute-start.4
  6.8 0.6 %collective-permute-start.1 = (bf16[36,32,128]{2,1,0:T(8,128)(2,1)S(1)}, bf16[36,32,128]{2,1,0:T(8,128)(2,1)S(1)}, u32[]{:S(2)}, u32[]{:S(2)}) collective-permute-start(bf16[36,32,128]{2,1,0:T(8,128)(2,1)S(1)} %get-tuple-element.41.refs_0_), channel_id=1, source_target_pairs={{0,4},{4,0},{8,12},{12,8},{1,5},{5,1},{9,13},{13,9},{2,6},{6,2},{1... | collective-permute-start | bytes 884744 | tf_op jit(solution)/shard_map/ppermute | solution.py:340
  7.5 4.6 %partial_gram.1 = (bf16[512,1024]{1,0:T(8,128)(2,1)S(1)}, bf16[512,3584]{1,0:T(8,128)(2,1)S(1)}, f32[36,32,128]{2,1,0:T(8,128)S(1)}, f32[36,32,128]{2,1,0:T(8,12...) custom-call(s32[1]{0:T(128)} %bitcast.me_ref, bf16[512,1024]{1,0:T(8,128)(2,1)} %act_hbm.1, ...), custom_call_target="tpu_custom_call" | custom-call | flops 1207959552 | bytes 4718592 | tf_op jit(solution)/shard_map/partial_gram/pallas_call | solution.py:389
  12.0 3.3 %collective-permute-start.9 = (bf16[1200,128]{1,0:T(8,128)(2,1)S(1)}, bf16[1200,128]{1,0:T(8,128)(2,1)S(1)}, u32[]{:S(2)}, u32[]{:S(2)}) collective-permute-start(bf16[1200,128]{1,0:T(8,128)(2,1)S(1)} %get-tuple-element.37), channel_id=1, source_target_pairs={{0,4},{12,8},{1,5},{13,9},{2,6},{14,10},{3,7},{15,11},{16,20},{28,... | collective-permute-start | bytes 921608 | tf_op jit(solution)/shard_map/ppermute | solution.py:411
  15.4 0.7 %collective-permute-start = (bf16[1200,128]{1,0:T(8,128)(2,1)S(1)}, bf16[1200,128]{1,0:T(8,128)(2,1)S(1)}, u32[]{:S(2)}, u32[]{:S(2)}) collective-permute-start(bf16[1200,128]{1,0:T(8,128)(2,1)S(1)} %get-tuple-element.37), channel_id=1, source_target_pairs={{4,8},{8,4},{5,9},{9,5},{6,10},{10,6},{7,11},{11,7},{20,24},{24,20... | collective-permute-start | bytes 921608 | tf_op jit(solution)/shard_map/ppermute | solution.py:410
  16.1 0.0 collective-permute-done.2.refs_2_
  16.1 1.6 %collective-permute-start.3 = (bf16[18,32,128]{2,1,0:T(8,128)(2,1)S(1)}, bf16[18,32,128]{2,1,0:T(8,128)(2,1)S(1)}, u32[]{:S(2)}, u32[]{:S(2)}) collective-permute-start(bf16[18,32,128]{2,1,0:T(8,128)(2,1)S(1)} %collective-permute-done.2.refs_2_), channel_id=1, source_target_pairs={{0,16},{16,0},{1,17},{17,1},{2,18},{18,2},{3,19},{19,3},{4,20},{20... | collective-permute-start | bytes 442376 | tf_op jit(solution)/shard_map/ppermute | solution.py:340
  17.6 2.7 %collective-permute-done.4.refs_3_ = bf16[18,32,128]{2,1,0:T(8,128)(2,1)S(1)} collective-permute-done((bf16[18,32,128]{2,1,0:T(8,128)(2,1)S(1)}, bf16[18,32,128]{2,1,0:T(8,128)(2,1)S(1)}, u32[]{:S(2)}, u32[]{:S(2)}) %collective-permute-start.4) | collective-permute-done | bytes 147488 | tf_op jit(solution)/shard_map/ppermute | solution.py:340
  20.3 1.5 %collective-permute-start.5 = (bf16[18,32,128]{2,1,0:T(8,128)(2,1)S(1)}, bf16[18,32,128]{2,1,0:T(8,128)(2,1)S(1)}, u32[]{:S(2)}, u32[]{:S(2)}) collective-permute-start(bf16[18,32,128]{2,1,0:T(8,128)(2,1)S(1)} %collective-permute-done.4.refs_3_), channel_id=1, source_target_pairs={{0,16},{16,0},{1,17},{17,1},{2,18},{18,2},{3,19},{19,3},{4,20},{20... | collective-permute-start | bytes 442376 | tf_op jit(solution)/shard_map/ppermute | solution.py:340
  21.8 0.0 collective-permute-done.1.refs_1_
  21.8 1.0 %partial_eigen.2 = (f32[9,512,256]{2,1,0:T(8,128)S(1)}, f32[18,128]{1,0:T(8,128)S(1)}) custom-call(s32[1]{0:T(128)} %bitcast.me_ref, s32[1]{0:T(128)} %bitcast.1.side_ref, bf16[512,1024]{1,0:T(8,128)(2,1)S(1)} %get-tuple-element.39.act_ref, bf16[512,3584]{1,0:T(8,128)(2,1)S(1)} %get-tuple-element.40.grad_ref, ...), custom_call_target="tpu_custom_call" | custom-call | flops 301989888 | bytes 2359296 | tf_op jit(solution)/shard_map/partial_eigen/pallas_call | solution.py:419
  22.8 0.0 collective-permute-done.3.refs_2_
  22.8 2.6 %collective-permute-done.5.refs_3_ = bf16[18,32,128]{2,1,0:T(8,128)(2,1)S(1)} collective-permute-done((bf16[18,32,128]{2,1,0:T(8,128)(2,1)S(1)}, bf16[18,32,128]{2,1,0:T(8,128)(2,1)S(1)}, u32[]{:S(2)}, u32[]{:S(2)}) %collective-permute-start.5) | collective-permute-done | bytes 147488 | tf_op jit(solution)/shard_map/ppermute | solution.py:340
  25.5 1.0 %partial_eigen.3 = (f32[9,512,256]{2,1,0:T(8,128)S(1)}, f32[36,128]{1,0:T(8,128)S(1)}) custom-call(s32[1]{0:T(128)} %bitcast.me_ref, s32[1]{0:T(128)} %bitcast.1.side_ref, bf16[512,1024]{1,0:T(8,128)(2,1)S(1)} %get-tuple-element.39.act_ref, bf16[512,3584]{1,0:T(8,128)(2,1)S(1)} %get-tuple-element.40.grad_ref, ...), custom_call_target="tpu_custom_call" | custom-call | flops 301989888 | bytes 2359296 | tf_op jit(solution)/shard_map/partial_eigen/pallas_call | solution.py:419
  26.5 0.7 %collective-permute-start.6 = (f32[36,128]{1,0:T(8,128)S(1)}, f32[36,128]{1,0:T(8,128)S(1)}, u32[]{:S(2)}, u32[]{:S(2)}) collective-permute-start(f32[36,128]{1,0:T(8,128)S(1)} %get-tuple-element.50.refs_0_), channel_id=1, source_target_pairs={{0,4},{4,0},{8,12},{12,8},{1,5},{5,1},{9,13},{13,9},{2,6},{6,2},{1... | collective-permute-start | bytes 55304 | tf_op jit(solution)/shard_map/ppermute | solution.py:340
  27.2 2.6 %collective-permute-start.7 = (f32[36,128]{1,0:T(8,128)S(1)}, f32[36,128]{1,0:T(8,128)S(1)}, u32[]{:S(2)}, u32[]{:S(2)}) collective-permute-start(f32[36,128]{1,0:T(8,128)S(1)} %get-tuple-element.50.refs_0_), channel_id=1, source_target_pairs={{0,8},{4,12},{8,0},{12,4},{1,9},{5,13},{9,1},{13,5},{2,10},{6,14},... | collective-permute-start | bytes 55304 | tf_op jit(solution)/shard_map/ppermute | solution.py:340
  29.7 1.2 %collective-permute-start.8 = (f32[36,128]{1,0:T(8,128)S(1)}, f32[36,128]{1,0:T(8,128)S(1)}, u32[]{:S(2)}, u32[]{:S(2)}) collective-permute-start(f32[36,128]{1,0:T(8,128)S(1)} %get-tuple-element.50.refs_0_), channel_id=1, source_target_pairs={{0,12},{4,8},{8,4},{12,0},{1,13},{5,9},{9,5},{13,1},{2,14},{6,10},... | collective-permute-start | bytes 55304 | tf_op jit(solution)/shard_map/ppermute | solution.py:340
  30.9 0.0 collective-permute-done.9.relayed_ref
  30.9 0.6 %relay_chunk.1 = bf16[1200,128]{1,0:T(8,128)(2,1)S(1)} custom-call(f32[36,32,128]{2,1,0:T(8,128)S(1)} %get-tuple-element.48.far_ref, bf16[1200,128]{1,0:T(8,128)(2,1)S(1)} %collective-permute-done.9.relayed_ref), custom_call_target="tpu_custom_call" | custom-call | bytes 1769472 | tf_op jit(solution)/shard_map/relay_chunk/pallas_call | solution.py:428
  31.5 0.0 collective-permute-done.refs_0_
  31.5 0.0 collective-permute-done.6.refs_1_
  31.5 0.3 collective-permute-done.7.refs_2_
  31.8 4.0 %collective-permute-done.8.refs_3_ = f32[36,128]{1,0:T(8,128)S(1)} collective-permute-done((f32[36,128]{1,0:T(8,128)S(1)}, f32[36,128]{1,0:T(8,128)S(1)}, u32[]{:S(2)}, u32[]{:S(2)}) %collective-permute-start.8) | collective-permute-done | bytes 18464 | tf_op jit(solution)/shard_map/ppermute | solution.py:340
  35.8 0.6 %combine_eigen.1 = (f32[8,128]{1,0:T(8,128)}, f32[28,128]{1,0:T(8,128)}, f32[36,128]{1,0:T(8,128)S(1)}, f32[2,128]{1,0:T(2,128)S(1)}) custom-call(s32[1]{0:T(128)} %bitcast.1.side_ref, f32[36,128]{1,0:T(8,128)S(1)} %get-tuple-element.50.refs_0_, f32[36,128]{1,0:T(8,128)S(1)} %collective-permute-done.6.refs_1_, f32[36,128]{1,0:T(8,128)S(1)} %collective-permute-done.7.refs_2_, ...), custom_call_target="tpu_custom_call" | custom-call | bytes 73728 | tf_op jit(solution)/shard_map/combine_eigen/pallas_call | solution.py:436
  36.4 0.0 collective-permute-start.10
  36.4 1.5 %collective-permute-start.11 = (bf16[1200,128]{1,0:T(8,128)(2,1)S(1)}, bf16[1200,128]{1,0:T(8,128)(2,1)S(1)}, u32[]{:S(2)}, u32[]{:S(2)}) collective-permute-start(bf16[1200,128]{1,0:T(8,128)(2,1)S(1)} %relay_chunk.1), channel_id=1, source_target_pairs={{0,8},{4,12},{8,0},{12,4},{1,9},{5,13},{9,1},{13,5},{2,10},{6,14},... | collective-permute-start | bytes 921608 | tf_op jit(solution)/shard_map/ppermute | solution.py:340
  37.9 0.0 collective-permute-start.12
  37.9 1.5 %collective-permute-start.13 = (f32[2,128]{1,0:T(2,128)S(1)}, f32[2,128]{1,0:T(2,128)S(1)}, u32[]{:S(2)}, u32[]{:S(2)}) collective-permute-start(f32[2,128]{1,0:T(2,128)S(1)} %get-tuple-element.54.refs_2_), channel_id=1, source_target_pairs={{0,2},{1,3},{2,0},{3,1},{4,6},{5,7},{6,4},{7,5},{8,10},{9,11},{10,... | collective-permute-start | bytes 3080 | tf_op jit(solution)/shard_map/ppermute | solution.py:340
  39.4 0.4 collective-permute-start.14
  39.8 0.0 collective-permute-done.12.refs_3_
  39.8 1.7 %collective-permute-done.13.refs_4_ = f32[2,128]{1,0:T(2,128)S(1)} collective-permute-done((f32[2,128]{1,0:T(2,128)S(1)}, f32[2,128]{1,0:T(2,128)S(1)}, u32[]{:S(2)}, u32[]{:S(2)}) %collective-permute-start.13) | collective-permute-done | bytes 1056 | tf_op jit(solution)/shard_map/ppermute | solution.py:340
  41.5 0.9 %collective-permute-done.14.refs_5_ = f32[2,128]{1,0:T(2,128)S(1)} collective-permute-done((f32[2,128]{1,0:T(2,128)S(1)}, f32[2,128]{1,0:T(2,128)S(1)}, u32[]{:S(2)}, u32[]{:S(2)}) %collective-permute-start.14) | collective-permute-done | bytes 1056 | tf_op jit(solution)/shard_map/ppermute | solution.py:340
  42.4 1.5 %partial_weights.1.refs_0_ = f32[2,512]{1,0:T(2,128)S(1)} custom-call(f32[36,128]{1,0:T(8,128)S(1)} %get-tuple-element.61.eigen_ref, f32[9,512,256]{2,1,0:T(8,128)S(1)} %get-tuple-element.62.refs_0_, f32[9,512,256]{2,1,0:T(8,128)S(1)} %get-tuple-element.63.refs_1_, f32[2,128]{1,0:T(2,128)S(1)} %get-tuple-element.54.refs_2_, ...), custom_call_target="tpu_custom_call" | custom-call | bytes 9437184 | tf_op jit(solution)/shard_map/partial_weights/pallas_call | solution.py:446
  43.9 0.5 %collective-permute-start.15 = (f32[2,512]{1,0:T(2,128)S(1)}, f32[2,512]{1,0:T(2,128)S(1)}, u32[]{:S(2)}, u32[]{:S(2)}) collective-permute-start(f32[2,512]{1,0:T(2,128)S(1)} %partial_weights.1.refs_0_), channel_id=1, source_target_pairs={{0,1},{1,0},{2,3},{3,2},{4,5},{5,4},{6,7},{7,6},{8,9},{9,8},{10,11... | collective-permute-start | bytes 12296 | tf_op jit(solution)/shard_map/ppermute | solution.py:340
  44.4 0.5 %collective-permute-start.16 = (f32[2,512]{1,0:T(2,128)S(1)}, f32[2,512]{1,0:T(2,128)S(1)}, u32[]{:S(2)}, u32[]{:S(2)}) collective-permute-start(f32[2,512]{1,0:T(2,128)S(1)} %partial_weights.1.refs_0_), channel_id=1, source_target_pairs={{0,2},{1,3},{2,0},{3,1},{4,6},{5,7},{6,4},{7,5},{8,10},{9,11},{10,... | collective-permute-start | bytes 12296 | tf_op jit(solution)/shard_map/ppermute | solution.py:340
  45.0 0.9 %collective-permute-start.17 = (f32[2,512]{1,0:T(2,128)S(1)}, f32[2,512]{1,0:T(2,128)S(1)}, u32[]{:S(2)}, u32[]{:S(2)}) collective-permute-start(f32[2,512]{1,0:T(2,128)S(1)} %partial_weights.1.refs_0_), channel_id=1, source_target_pairs={{0,3},{1,2},{2,1},{3,0},{4,7},{5,6},{6,5},{7,4},{8,11},{9,10},{10,... | collective-permute-start | bytes 12296 | tf_op jit(solution)/shard_map/ppermute | solution.py:340
  45.8 0.3 collective-permute-done.10.refs_1_
  46.1 0.6 %add_chunks.1.own_ref = f32[36,32,128]{2,1,0:T(8,128)S(1)} custom-call(f32[36,32,128]{2,1,0:T(8,128)S(1)} %get-tuple-element.36.own_ref, bf16[1200,128]{1,0:T(8,128)(2,1)S(1)} %collective-permute-done.refs_0_, bf16[1200,128]{1,0:T(8,128)(2,1)S(1)} %collective-permute-done.10.refs_1_), custom_call_target="tpu_custom_call" | custom-call | bytes 2359296 | tf_op jit(solution)/shard_map/add_chunks/pallas_call | solution.py:462
  46.7 0.0 collective-permute-done.15.refs_1_
  46.8 1.3 %collective-permute-done.16.refs_2_ = f32[2,512]{1,0:T(2,128)S(1)} collective-permute-done((f32[2,512]{1,0:T(2,128)S(1)}, f32[2,512]{1,0:T(2,128)S(1)}, u32[]{:S(2)}, u32[]{:S(2)}) %collective-permute-start.16) | collective-permute-done | bytes 4128 | tf_op jit(solution)/shard_map/ppermute | solution.py:340
  48.0 0.0 collective-permute-done.17.refs_3_
  48.0 0.6 %token_scores.1 = f32[1,512]{1,0:T(1,128)} custom-call(f32[2,512]{1,0:T(2,128)S(1)} %partial_weights.1.refs_0_, f32[2,512]{1,0:T(2,128)S(1)} %collective-permute-done.15.refs_1_, f32[2,512]{1,0:T(2,128)S(1)} %collective-permute-done.16.refs_2_, f32[2,512]{1,0:T(2,128)S(1)} %collective-permute-done.17.refs_3_), custom_call_target="tpu_custom_call" | custom-call | bytes 4096 | tf_op jit(solution)/shard_map/token_scores/pallas_call | solution.py:467
  48.6 0.0 collective-permute-done.11.refs_0_
  48.6 1.0 %add_last_chunk.1 = (f32[8,32,128]{2,1,0:T(8,128)}, f32[28,32,128]{2,1,0:T(8,128)}) custom-call(f32[36,32,128]{2,1,0:T(8,128)S(1)} %add_chunks.1.own_ref, bf16[1200,128]{1,0:T(8,128)(2,1)S(1)} %collective-permute-done.11.refs_0_), custom_call_target="tpu_custom_call" | custom-call | bytes 1769472 | tf_op jit(solution)/shard_map/add_last_chunk/pallas_call | solution.py:472
Async XLA Ops:
  1.7 14.3 %collective-permute-start.2 = (bf16[18,32,128]{2,1,0:T(8,128)(2,1)S(1)}, bf16[18,32,128]{2,1,0:T(8,128)(2,1)S(1)}, u32[]{:S(2)}, u32[]{:S(2)}) collective-permute-start(bf16[18,32,128]{2,1,0:T(8,128)(2,1)S(1)} %get-tuple-element.42), channel_id=1, source_target_pairs={{0,12},{4,8},{8,4},{12,0},{1,13},{5,9},{9,5},{13,1},{2,14},{6,10},... | collective-permute-start | bytes 442376 | tf_op jit(solution)/shard_map/ppermute | solution.py:340
  6.8 13.5 %collective-permute-start.4 = (bf16[18,32,128]{2,1,0:T(8,128)(2,1)S(1)}, bf16[18,32,128]{2,1,0:T(8,128)(2,1)S(1)}, u32[]{:S(2)}, u32[]{:S(2)}) collective-permute-start(bf16[18,32,128]{2,1,0:T(8,128)(2,1)S(1)} %get-tuple-element.42), channel_id=1, source_target_pairs={{0,8},{4,12},{8,0},{12,4},{1,9},{5,13},{9,1},{13,5},{2,10},{6,14},... | collective-permute-start | bytes 442376 | tf_op jit(solution)/shard_map/ppermute | solution.py:340
  6.8 15.0 %collective-permute-start.1 = (bf16[36,32,128]{2,1,0:T(8,128)(2,1)S(1)}, bf16[36,32,128]{2,1,0:T(8,128)(2,1)S(1)}, u32[]{:S(2)}, u32[]{:S(2)}) collective-permute-start(bf16[36,32,128]{2,1,0:T(8,128)(2,1)S(1)} %get-tuple-element.41.refs_0_), channel_id=1, source_target_pairs={{0,4},{4,0},{8,12},{12,8},{1,5},{5,1},{9,13},{13,9},{2,6},{6,2},{1... | collective-permute-start | bytes 884744 | tf_op jit(solution)/shard_map/ppermute | solution.py:340
  12.0 18.9 %collective-permute-start.9 = (bf16[1200,128]{1,0:T(8,128)(2,1)S(1)}, bf16[1200,128]{1,0:T(8,128)(2,1)S(1)}, u32[]{:S(2)}, u32[]{:S(2)}) collective-permute-start(bf16[1200,128]{1,0:T(8,128)(2,1)S(1)} %get-tuple-element.37), channel_id=1, source_target_pairs={{0,4},{12,8},{1,5},{13,9},{2,6},{14,10},{3,7},{15,11},{16,20},{28,... | collective-permute-start | bytes 921608 | tf_op jit(solution)/shard_map/ppermute | solution.py:411
  15.4 16.1 %collective-permute-start = (bf16[1200,128]{1,0:T(8,128)(2,1)S(1)}, bf16[1200,128]{1,0:T(8,128)(2,1)S(1)}, u32[]{:S(2)}, u32[]{:S(2)}) collective-permute-start(bf16[1200,128]{1,0:T(8,128)(2,1)S(1)} %get-tuple-element.37), channel_id=1, source_target_pairs={{4,8},{8,4},{5,9},{9,5},{6,10},{10,6},{7,11},{11,7},{20,24},{24,20... | collective-permute-start | bytes 921608 | tf_op jit(solution)/shard_map/ppermute | solution.py:410
  16.1 6.8 %collective-permute-start.3 = (bf16[18,32,128]{2,1,0:T(8,128)(2,1)S(1)}, bf16[18,32,128]{2,1,0:T(8,128)(2,1)S(1)}, u32[]{:S(2)}, u32[]{:S(2)}) collective-permute-start(bf16[18,32,128]{2,1,0:T(8,128)(2,1)S(1)} %collective-permute-done.2.refs_2_), channel_id=1, source_target_pairs={{0,16},{16,0},{1,17},{17,1},{2,18},{18,2},{3,19},{19,3},{4,20},{20... | collective-permute-start | bytes 442376 | tf_op jit(solution)/shard_map/ppermute | solution.py:340
  20.3 5.1 %collective-permute-start.5 = (bf16[18,32,128]{2,1,0:T(8,128)(2,1)S(1)}, bf16[18,32,128]{2,1,0:T(8,128)(2,1)S(1)}, u32[]{:S(2)}, u32[]{:S(2)}) collective-permute-start(bf16[18,32,128]{2,1,0:T(8,128)(2,1)S(1)} %collective-permute-done.4.refs_3_), channel_id=1, source_target_pairs={{0,16},{16,0},{1,17},{17,1},{2,18},{18,2},{3,19},{19,3},{4,20},{20... | collective-permute-start | bytes 442376 | tf_op jit(solution)/shard_map/ppermute | solution.py:340
  26.5 5.1 %collective-permute-start.6 = (f32[36,128]{1,0:T(8,128)S(1)}, f32[36,128]{1,0:T(8,128)S(1)}, u32[]{:S(2)}, u32[]{:S(2)}) collective-permute-start(f32[36,128]{1,0:T(8,128)S(1)} %get-tuple-element.50.refs_0_), channel_id=1, source_target_pairs={{0,4},{4,0},{8,12},{12,8},{1,5},{5,1},{9,13},{13,9},{2,6},{6,2},{1... | collective-permute-start | bytes 55304 | tf_op jit(solution)/shard_map/ppermute | solution.py:340
  27.2 4.7 %collective-permute-start.7 = (f32[36,128]{1,0:T(8,128)S(1)}, f32[36,128]{1,0:T(8,128)S(1)}, u32[]{:S(2)}, u32[]{:S(2)}) collective-permute-start(f32[36,128]{1,0:T(8,128)S(1)} %get-tuple-element.50.refs_0_), channel_id=1, source_target_pairs={{0,8},{4,12},{8,0},{12,4},{1,9},{5,13},{9,1},{13,5},{2,10},{6,14},... | collective-permute-start | bytes 55304 | tf_op jit(solution)/shard_map/ppermute | solution.py:340
  29.7 6.1 %collective-permute-start.8 = (f32[36,128]{1,0:T(8,128)S(1)}, f32[36,128]{1,0:T(8,128)S(1)}, u32[]{:S(2)}, u32[]{:S(2)}) collective-permute-start(f32[36,128]{1,0:T(8,128)S(1)} %get-tuple-element.50.refs_0_), channel_id=1, source_target_pairs={{0,12},{4,8},{8,4},{12,0},{1,13},{5,9},{9,5},{13,1},{2,14},{6,10},... | collective-permute-start | bytes 55304 | tf_op jit(solution)/shard_map/ppermute | solution.py:340
  36.4 9.7 %collective-permute-start.10 = (bf16[1200,128]{1,0:T(8,128)(2,1)S(1)}, bf16[1200,128]{1,0:T(8,128)(2,1)S(1)}, u32[]{:S(2)}, u32[]{:S(2)}) collective-permute-start(bf16[1200,128]{1,0:T(8,128)(2,1)S(1)} %get-tuple-element.55), channel_id=1, source_target_pairs={{0,4},{4,0},{8,12},{12,8},{1,5},{5,1},{9,13},{13,9},{2,6},{6,2},{1... | collective-permute-start | bytes 921608 | tf_op jit(solution)/shard_map/ppermute | solution.py:340
  36.4 12.2 %collective-permute-start.11 = (bf16[1200,128]{1,0:T(8,128)(2,1)S(1)}, bf16[1200,128]{1,0:T(8,128)(2,1)S(1)}, u32[]{:S(2)}, u32[]{:S(2)}) collective-permute-start(bf16[1200,128]{1,0:T(8,128)(2,1)S(1)} %relay_chunk.1), channel_id=1, source_target_pairs={{0,8},{4,12},{8,0},{12,4},{1,9},{5,13},{9,1},{13,5},{2,10},{6,14},... | collective-permute-start | bytes 921608 | tf_op jit(solution)/shard_map/ppermute | solution.py:340
  37.9 1.9 %collective-permute-start.12 = (f32[2,128]{1,0:T(2,128)S(1)}, f32[2,128]{1,0:T(2,128)S(1)}, u32[]{:S(2)}, u32[]{:S(2)}) collective-permute-start(f32[2,128]{1,0:T(2,128)S(1)} %get-tuple-element.54.refs_2_), channel_id=1, source_target_pairs={{0,1},{1,0},{2,3},{3,2},{4,5},{5,4},{6,7},{7,6},{8,9},{9,8},{10,11... | collective-permute-start | bytes 3080 | tf_op jit(solution)/shard_map/ppermute | solution.py:340
  37.9 3.6 %collective-permute-start.13 = (f32[2,128]{1,0:T(2,128)S(1)}, f32[2,128]{1,0:T(2,128)S(1)}, u32[]{:S(2)}, u32[]{:S(2)}) collective-permute-start(f32[2,128]{1,0:T(2,128)S(1)} %get-tuple-element.54.refs_2_), channel_id=1, source_target_pairs={{0,2},{1,3},{2,0},{3,1},{4,6},{5,7},{6,4},{7,5},{8,10},{9,11},{10,... | collective-permute-start | bytes 3080 | tf_op jit(solution)/shard_map/ppermute | solution.py:340
  39.4 3.0 %collective-permute-start.14 = (f32[2,128]{1,0:T(2,128)S(1)}, f32[2,128]{1,0:T(2,128)S(1)}, u32[]{:S(2)}, u32[]{:S(2)}) collective-permute-start(f32[2,128]{1,0:T(2,128)S(1)} %get-tuple-element.54.refs_2_), channel_id=1, source_target_pairs={{0,3},{1,2},{2,1},{3,0},{4,7},{5,6},{6,5},{7,4},{8,11},{9,10},{10,... | collective-permute-start | bytes 3080 | tf_op jit(solution)/shard_map/ppermute | solution.py:340
  43.9 2.9 %collective-permute-start.15 = (f32[2,512]{1,0:T(2,128)S(1)}, f32[2,512]{1,0:T(2,128)S(1)}, u32[]{:S(2)}, u32[]{:S(2)}) collective-permute-start(f32[2,512]{1,0:T(2,128)S(1)} %partial_weights.1.refs_0_), channel_id=1, source_target_pairs={{0,1},{1,0},{2,3},{3,2},{4,5},{5,4},{6,7},{7,6},{8,9},{9,8},{10,11... | collective-permute-start | bytes 12296 | tf_op jit(solution)/shard_map/ppermute | solution.py:340
  44.4 3.6 %collective-permute-start.16 = (f32[2,512]{1,0:T(2,128)S(1)}, f32[2,512]{1,0:T(2,128)S(1)}, u32[]{:S(2)}, u32[]{:S(2)}) collective-permute-start(f32[2,512]{1,0:T(2,128)S(1)} %partial_weights.1.refs_0_), channel_id=1, source_target_pairs={{0,2},{1,3},{2,0},{3,1},{4,6},{5,7},{6,4},{7,5},{8,10},{9,11},{10,... | collective-permute-start | bytes 12296 | tf_op jit(solution)/shard_map/ppermute | solution.py:340
  45.0 3.1 %collective-permute-start.17 = (f32[2,512]{1,0:T(2,128)S(1)}, f32[2,512]{1,0:T(2,128)S(1)}, u32[]{:S(2)}, u32[]{:S(2)}) collective-permute-start(f32[2,512]{1,0:T(2,128)S(1)} %partial_weights.1.refs_0_), channel_id=1, source_target_pairs={{0,3},{1,2},{2,1},{3,0},{4,7},{5,6},{6,5},{7,4},{8,11},{9,10},{10,... | collective-permute-start | bytes 12296 | tf_op jit(solution)/shard_map/ppermute | solution.py:340

commit v10 on v9

--- a/solution.py
+++ b/solution.py
@@ -263,6 +263,10 @@
         sums_ref[row + 1 : row + 2, :] = sums[:, BLK:]
 
 
+def pair_kernel(left_ref, right_ref, sum_ref):
+    sum_ref[...] = left_ref[...] + right_ref[...]
+
+
 def combine_kernel(halves, side_ref, *refs):
     *sums_refs, act_eigen_ref, grad_eigen_ref, eigen_ref, total_ref = refs
     side = side_ref[0]
@@ -430,7 +434,13 @@
             [IN_VMEM, IN_VMEM],
             [pltpu.VMEM((scale_rows(0, blocks), BLK), jnp.float32)] * 2,
         )(*after([grams[1], relayed], sums))
-    sums = share(sums[0], "dp", direct)
+    if pieces == 4:
+        pair = call(
+            pair_kernel, f32(blocks, BLK), "pair_eigen", 0, 12 * blocks * BLK, [IN_VMEM] * 2
+        )(sums[0], swap(sums[0], "dp", 1))
+        sums = [pair, swap(pair, "dp", 2)]
+    else:
+        sums = share(sums[0], "dp", direct)
     if pieces == 4:
         sums = after(sums, (middle, sent[2]))
     act_eigen, grad_eigen, eigen, totals = call(

time: 49.8 us -> 51 us (1.024)
  waiting for transfers between devices: 13.8 us -> 15.7 us
  starting transfers between devices: 22.6 us -> 21.9 us
    ppermute x16 -> x15, waiting for transfers between devices: 13.8 us -> 15.7 us  [swap(): return lax.ppermute(value, axis, [(i, i ^ mask) for i in range(count)])]
    ppermute x16 -> x15, starting transfers between devices: 18.6 us -> 17.9 us  [swap(): return lax.ppermute(value, axis, [(i, i ^ mask) for i in range(count)])]
  transfers between devices with their start and end apart: 18 -> 17, of which waited for: 8 -> 7; matrix products, arithmetic and copies ran while one was open for 0% -> 0% of each run, Pallas kernels for 20% -> 19%
where the time goes in v10:
time: 51 us; the launch traced here: 50.8 us
  starting transfers between devices  21.9 us (43%)
  waiting for transfers between devices  15.7 us (31%)
  Pallas kernels  12.5 us (25%)
  between operations  0.74 us (1%)
    ppermute x15, starting transfers between devices, swap(): return lax.ppermute(value, axis, [(i, i ^ mask) for i in range(count)])  17.9 us
    ppermute x15, waiting for transfers between devices, swap(): return lax.ppermute(value, axis, [(i, i ^ mask) for i in range(count)])  15.7 us
    pallas_call x1, Pallas kernels, local(): call(functools.partial(gram_kernel, pieces, coded, scale), [bf16(*activat...  4.56 us
    ppermute x1, starting transfers between devices, local(): relayed = lax.ppermute(sent[3], 'dp', [(0, 1), (3, 2)])  3.32 us
    pallas_call x2, Pallas kernels, local(): call(functools.partial(eigen_kernel, part, halves, masks, pieces, scale),...  1.95 us
    pallas_call x1, Pallas kernels, local(): call(functools.partial(weight_kernel, halves, act_blocks // halves), f32(...  1.48 us
    pallas_call x1, Pallas kernels, local(): call(pack_kernel, [bf16(blocks // part, rows, BLK) for part in range(1, h...  1.08 us
    pallas_call x1, Pallas kernels, local(): call(functools.partial(last_add_kernel, [(None, 0, blocks)] * len(chunks)...  1.04 us
  transfers between devices with their start and end apart: 17, of which 7 were waited for; matrix products, arithmetic and copies ran while one was open for 0% of the time, Pallas kernels for 19%

profile of v10, /device:TPU:0, one launch (start us, length us, event | category | flops | bytes accessed | tf_op | source)
XLA Modules:
  0.0 50.8 jit_solution(17591734809376842639)
XLA Ops:
  0.6 1.1 %pack_basis.1 = (bf16[36,32,128]{2,1,0:T(8,128)(2,1)S(1)}, bf16[18,32,128]{2,1,0:T(8,128)(2,1)S(1)}) custom-call(s32[1]{0:T(128)} %bitcast.1.side_ref, bf16[8,32,128]{2,1,0:T(8,128)(2,1)} %act_ref.1, bf16[28,32,128]{2,1,0:T(8,128)(2,1)} %grad_ref.1), custom_call_target="tpu_custom_call" | custom-call | bytes 294912 | tf_op jit(solution)/shard_map/pack_basis/pallas_call | solution.py:372
  1.7 5.1 %collective-permute-start.2 = (bf16[18,32,128]{2,1,0:T(8,128)(2,1)S(1)}, bf16[18,32,128]{2,1,0:T(8,128)(2,1)S(1)}, u32[]{:S(2)}, u32[]{:S(2)}) collective-permute-start(bf16[18,32,128]{2,1,0:T(8,128)(2,1)S(1)} %get-tuple-element.40), channel_id=1, source_target_pairs={{0,12},{4,8},{8,4},{12,0},{1,13},{5,9},{9,5},{13,1},{2,14},{6,10},... | collective-permute-start | bytes 442376 | tf_op jit(solution)/shard_map/ppermute | solution.py:344
  6.8 0.0 collective-permute-start.4
  6.8 0.6 %collective-permute-start.1 = (bf16[36,32,128]{2,1,0:T(8,128)(2,1)S(1)}, bf16[36,32,128]{2,1,0:T(8,128)(2,1)S(1)}, u32[]{:S(2)}, u32[]{:S(2)}) collective-permute-start(bf16[36,32,128]{2,1,0:T(8,128)(2,1)S(1)} %get-tuple-element.39.refs_0_), channel_id=1, source_target_pairs={{0,4},{4,0},{8,12},{12,8},{1,5},{5,1},{9,13},{13,9},{2,6},{6,2},{1... | collective-permute-start | bytes 884744 | tf_op jit(solution)/shard_map/ppermute | solution.py:344
  7.5 4.6 %partial_gram.1 = (bf16[512,1024]{1,0:T(8,128)(2,1)S(1)}, bf16[512,3584]{1,0:T(8,128)(2,1)S(1)}, f32[36,32,128]{2,1,0:T(8,128)S(1)}, f32[36,32,128]{2,1,0:T(8,12...) custom-call(s32[1]{0:T(128)} %bitcast.me_ref, bf16[512,1024]{1,0:T(8,128)(2,1)} %act_hbm.1, ...), custom_call_target="tpu_custom_call" | custom-call | flops 1207959552 | bytes 4718592 | tf_op jit(solution)/shard_map/partial_gram/pallas_call | solution.py:393
  12.0 3.3 %collective-permute-start.8 = (bf16[1200,128]{1,0:T(8,128)(2,1)S(1)}, bf16[1200,128]{1,0:T(8,128)(2,1)S(1)}, u32[]{:S(2)}, u32[]{:S(2)}) collective-permute-start(bf16[1200,128]{1,0:T(8,128)(2,1)S(1)} %get-tuple-element.35), channel_id=1, source_target_pairs={{0,4},{12,8},{1,5},{13,9},{2,6},{14,10},{3,7},{15,11},{16,20},{28,... | collective-permute-start | bytes 921608 | tf_op jit(solution)/shard_map/ppermute | solution.py:415
  15.4 0.7 %collective-permute-start = (bf16[1200,128]{1,0:T(8,128)(2,1)S(1)}, bf16[1200,128]{1,0:T(8,128)(2,1)S(1)}, u32[]{:S(2)}, u32[]{:S(2)}) collective-permute-start(bf16[1200,128]{1,0:T(8,128)(2,1)S(1)} %get-tuple-element.35), channel_id=1, source_target_pairs={{4,8},{8,4},{5,9},{9,5},{6,10},{10,6},{7,11},{11,7},{20,24},{24,20... | collective-permute-start | bytes 921608 | tf_op jit(solution)/shard_map/ppermute | solution.py:414
  16.1 0.0 collective-permute-done.2.refs_2_
  16.1 1.6 %collective-permute-start.3 = (bf16[18,32,128]{2,1,0:T(8,128)(2,1)S(1)}, bf16[18,32,128]{2,1,0:T(8,128)(2,1)S(1)}, u32[]{:S(2)}, u32[]{:S(2)}) collective-permute-start(bf16[18,32,128]{2,1,0:T(8,128)(2,1)S(1)} %collective-permute-done.2.refs_2_), channel_id=1, source_target_pairs={{0,16},{16,0},{1,17},{17,1},{2,18},{18,2},{3,19},{19,3},{4,20},{20... | collective-permute-start | bytes 442376 | tf_op jit(solution)/shard_map/ppermute | solution.py:344
  17.6 2.7 %collective-permute-done.4.refs_3_ = bf16[18,32,128]{2,1,0:T(8,128)(2,1)S(1)} collective-permute-done((bf16[18,32,128]{2,1,0:T(8,128)(2,1)S(1)}, bf16[18,32,128]{2,1,0:T(8,128)(2,1)S(1)}, u32[]{:S(2)}, u32[]{:S(2)}) %collective-permute-start.4) | collective-permute-done | bytes 147488 | tf_op jit(solution)/shard_map/ppermute | solution.py:344
  20.3 1.5 %collective-permute-start.5 = (bf16[18,32,128]{2,1,0:T(8,128)(2,1)S(1)}, bf16[18,32,128]{2,1,0:T(8,128)(2,1)S(1)}, u32[]{:S(2)}, u32[]{:S(2)}) collective-permute-start(bf16[18,32,128]{2,1,0:T(8,128)(2,1)S(1)} %collective-permute-done.4.refs_3_), channel_id=1, source_target_pairs={{0,16},{16,0},{1,17},{17,1},{2,18},{18,2},{3,19},{19,3},{4,20},{20... | collective-permute-start | bytes 442376 | tf_op jit(solution)/shard_map/ppermute | solution.py:344
  21.8 0.0 collective-permute-done.1.refs_1_
  21.8 1.0 %partial_eigen.2 = (f32[9,512,256]{2,1,0:T(8,128)S(1)}, f32[18,128]{1,0:T(8,128)S(1)}) custom-call(s32[1]{0:T(128)} %bitcast.me_ref, s32[1]{0:T(128)} %bitcast.1.side_ref, bf16[512,1024]{1,0:T(8,128)(2,1)S(1)} %get-tuple-element.37.act_ref, bf16[512,3584]{1,0:T(8,128)(2,1)S(1)} %get-tuple-element.38.grad_ref, ...), custom_call_target="tpu_custom_call" | custom-call | flops 301989888 | bytes 2359296 | tf_op jit(solution)/shard_map/partial_eigen/pallas_call | solution.py:423
  22.8 0.0 collective-permute-done.3.refs_2_
  22.8 2.6 %collective-permute-done.5.refs_3_ = bf16[18,32,128]{2,1,0:T(8,128)(2,1)S(1)} collective-permute-done((bf16[18,32,128]{2,1,0:T(8,128)(2,1)S(1)}, bf16[18,32,128]{2,1,0:T(8,128)(2,1)S(1)}, u32[]{:S(2)}, u32[]{:S(2)}) %collective-permute-start.5) | collective-permute-done | bytes 147488 | tf_op jit(solution)/shard_map/ppermute | solution.py:344
  25.5 1.0 %partial_eigen.3 = (f32[9,512,256]{2,1,0:T(8,128)S(1)}, f32[36,128]{1,0:T(8,128)S(1)}) custom-call(s32[1]{0:T(128)} %bitcast.me_ref, s32[1]{0:T(128)} %bitcast.1.side_ref, bf16[512,1024]{1,0:T(8,128)(2,1)S(1)} %get-tuple-element.37.act_ref, bf16[512,3584]{1,0:T(8,128)(2,1)S(1)} %get-tuple-element.38.grad_ref, ...), custom_call_target="tpu_custom_call" | custom-call | flops 301989888 | bytes 2359296 | tf_op jit(solution)/shard_map/partial_eigen/pallas_call | solution.py:423
  26.5 0.7 %collective-permute-start.6 = (f32[36,128]{1,0:T(8,128)S(1)}, f32[36,128]{1,0:T(8,128)S(1)}, u32[]{:S(2)}, u32[]{:S(2)}) collective-permute-start(f32[36,128]{1,0:T(8,128)S(1)} %get-tuple-element.44.left_ref), channel_id=1, source_target_pairs={{0,4},{4,0},{8,12},{12,8},{1,5},{5,1},{9,13},{13,9},{2,6},{6,2},{1... | collective-permute-start | bytes 55304 | tf_op jit(solution)/shard_map/ppermute | solution.py:344
  27.2 3.1 %collective-permute-done.6.right_ref = f32[36,128]{1,0:T(8,128)S(1)} collective-permute-done((f32[36,128]{1,0:T(8,128)S(1)}, f32[36,128]{1,0:T(8,128)S(1)}, u32[]{:S(2)}, u32[]{:S(2)}) %collective-permute-start.6) | collective-permute-done | bytes 18464 | tf_op jit(solution)/shard_map/ppermute | solution.py:344
  30.3 1.2 %collective-permute-start.7 = (f32[36,128]{1,0:T(8,128)S(1)}, f32[36,128]{1,0:T(8,128)S(1)}, u32[]{:S(2)}, u32[]{:S(2)}) collective-permute-start(f32[36,128]{1,0:T(8,128)S(1)} %pair_eigen.1.refs_0_), channel_id=1, source_target_pairs={{0,8},{4,12},{8,0},{12,4},{1,9},{5,13},{9,1},{13,5},{2,10},{6,14},... | collective-permute-start | bytes 55304 | tf_op jit(solution)/shard_map/ppermute | solution.py:344
  31.5 0.0 collective-permute-done.8.relayed_ref
  31.5 0.6 %relay_chunk.1 = bf16[1200,128]{1,0:T(8,128)(2,1)S(1)} custom-call(f32[36,32,128]{2,1,0:T(8,128)S(1)} %get-tuple-element.46.far_ref, bf16[1200,128]{1,0:T(8,128)(2,1)S(1)} %collective-permute-done.8.relayed_ref), custom_call_target="tpu_custom_call" | custom-call | bytes 1769472 | tf_op jit(solution)/shard_map/relay_chunk/pallas_call | solution.py:432
  32.1 0.0 collective-permute-done.refs_0_
  32.1 3.0 %collective-permute-done.7.refs_1_ = f32[36,128]{1,0:T(8,128)S(1)} collective-permute-done((f32[36,128]{1,0:T(8,128)S(1)}, f32[36,128]{1,0:T(8,128)S(1)}, u32[]{:S(2)}, u32[]{:S(2)}) %collective-permute-start.7) | collective-permute-done | bytes 18464 | tf_op jit(solution)/shard_map/ppermute | solution.py:344
  35.1 0.6 %combine_eigen.1 = (f32[8,128]{1,0:T(8,128)}, f32[28,128]{1,0:T(8,128)}, f32[36,128]{1,0:T(8,128)S(1)}, f32[2,128]{1,0:T(2,128)S(1)}) custom-call(s32[1]{0:T(128)} %bitcast.1.side_ref, f32[36,128]{1,0:T(8,128)S(1)} %pair_eigen.1.refs_0_, f32[36,128]{1,0:T(8,128)S(1)} %collective-permute-done.7.refs_1_), custom_call_target="tpu_custom_call" | custom-call | bytes 73728 | tf_op jit(solution)/shard_map/combine_eigen/pallas_call | solution.py:446
  35.8 0.7 %collective-permute-start.9 = (bf16[1200,128]{1,0:T(8,128)(2,1)S(1)}, bf16[1200,128]{1,0:T(8,128)(2,1)S(1)}, u32[]{:S(2)}, u32[]{:S(2)}) collective-permute-start(bf16[1200,128]{1,0:T(8,128)(2,1)S(1)} %get-tuple-element.51), channel_id=1, source_target_pairs={{0,4},{4,0},{8,12},{12,8},{1,5},{5,1},{9,13},{13,9},{2,6},{6,2},{1... | collective-permute-start | bytes 921608 | tf_op jit(solution)/shard_map/ppermute | solution.py:344
  36.5 2.6 %collective-permute-start.10 = (bf16[1200,128]{1,0:T(8,128)(2,1)S(1)}, bf16[1200,128]{1,0:T(8,128)(2,1)S(1)}, u32[]{:S(2)}, u32[]{:S(2)}) collective-permute-start(bf16[1200,128]{1,0:T(8,128)(2,1)S(1)} %relay_chunk.1), channel_id=1, source_target_pairs={{0,8},{4,12},{8,0},{12,4},{1,9},{5,13},{9,1},{13,5},{2,10},{6,14},... | collective-permute-start | bytes 921608 | tf_op jit(solution)/shard_map/ppermute | solution.py:344
  39.1 0.0 collective-permute-start.11
  39.1 1.5 %collective-permute-start.12 = (f32[2,128]{1,0:T(2,128)S(1)}, f32[2,128]{1,0:T(2,128)S(1)}, u32[]{:S(2)}, u32[]{:S(2)}) collective-permute-start(f32[2,128]{1,0:T(2,128)S(1)} %get-tuple-element.50.refs_2_), channel_id=1, source_target_pairs={{0,2},{1,3},{2,0},{3,1},{4,6},{5,7},{6,4},{7,5},{8,10},{9,11},{10,... | collective-permute-start | bytes 3080 | tf_op jit(solution)/shard_map/ppermute | solution.py:344
  40.6 0.4 collective-permute-start.13
  41.0 0.0 collective-permute-done.11.refs_3_
  41.0 1.7 %collective-permute-done.12.refs_4_ = f32[2,128]{1,0:T(2,128)S(1)} collective-permute-done((f32[2,128]{1,0:T(2,128)S(1)}, f32[2,128]{1,0:T(2,128)S(1)}, u32[]{:S(2)}, u32[]{:S(2)}) %collective-permute-start.12) | collective-permute-done | bytes 1056 | tf_op jit(solution)/shard_map/ppermute | solution.py:344
  42.7 0.9 %collective-permute-done.13.refs_5_ = f32[2,128]{1,0:T(2,128)S(1)} collective-permute-done((f32[2,128]{1,0:T(2,128)S(1)}, f32[2,128]{1,0:T(2,128)S(1)}, u32[]{:S(2)}, u32[]{:S(2)}) %collective-permute-start.13) | collective-permute-done | bytes 1056 | tf_op jit(solution)/shard_map/ppermute | solution.py:344
  43.6 1.5 %partial_weights.1.refs_0_ = f32[2,512]{1,0:T(2,128)S(1)} custom-call(f32[36,128]{1,0:T(8,128)S(1)} %get-tuple-element.57.eigen_ref, f32[9,512,256]{2,1,0:T(8,128)S(1)} %get-tuple-element.58.refs_0_, f32[9,512,256]{2,1,0:T(8,128)S(1)} %get-tuple-element.59.refs_1_, f32[2,128]{1,0:T(2,128)S(1)} %get-tuple-element.50.refs_2_, ...), custom_call_target="tpu_custom_call" | custom-call | bytes 9437184 | tf_op jit(solution)/shard_map/partial_weights/pallas_call | solution.py:456
  45.1 0.5 %collective-permute-start.14 = (f32[2,512]{1,0:T(2,128)S(1)}, f32[2,512]{1,0:T(2,128)S(1)}, u32[]{:S(2)}, u32[]{:S(2)}) collective-permute-start(f32[2,512]{1,0:T(2,128)S(1)} %partial_weights.1.refs_0_), channel_id=1, source_target_pairs={{0,1},{1,0},{2,3},{3,2},{4,5},{5,4},{6,7},{7,6},{8,9},{9,8},{10,11... | collective-permute-start | bytes 12296 | tf_op jit(solution)/shard_map/ppermute | solution.py:344
  45.6 0.5 %collective-permute-start.15 = (f32[2,512]{1,0:T(2,128)S(1)}, f32[2,512]{1,0:T(2,128)S(1)}, u32[]{:S(2)}, u32[]{:S(2)}) collective-permute-start(f32[2,512]{1,0:T(2,128)S(1)} %partial_weights.1.refs_0_), channel_id=1, source_target_pairs={{0,2},{1,3},{2,0},{3,1},{4,6},{5,7},{6,4},{7,5},{8,10},{9,11},{10,... | collective-permute-start | bytes 12296 | tf_op jit(solution)/shard_map/ppermute | solution.py:344
  46.1 0.9 %collective-permute-start.16 = (f32[2,512]{1,0:T(2,128)S(1)}, f32[2,512]{1,0:T(2,128)S(1)}, u32[]{:S(2)}, u32[]{:S(2)}) collective-permute-start(f32[2,512]{1,0:T(2,128)S(1)} %partial_weights.1.refs_0_), channel_id=1, source_target_pairs={{0,3},{1,2},{2,1},{3,0},{4,7},{5,6},{6,5},{7,4},{8,11},{9,10},{10,... | collective-permute-start | bytes 12296 | tf_op jit(solution)/shard_map/ppermute | solution.py:344
  47.0 0.0 collective-permute-done.9.refs_1_
  47.0 0.6 %add_chunks.1.own_ref = f32[36,32,128]{2,1,0:T(8,128)S(1)} custom-call(f32[36,32,128]{2,1,0:T(8,128)S(1)} %get-tuple-element.34.own_ref, bf16[1200,128]{1,0:T(8,128)(2,1)S(1)} %collective-permute-done.refs_0_, bf16[1200,128]{1,0:T(8,128)(2,1)S(1)} %collective-permute-done.9.refs_1_), custom_call_target="tpu_custom_call" | custom-call | bytes 2359296 | tf_op jit(solution)/shard_map/add_chunks/pallas_call | solution.py:472
  47.6 0.0 collective-permute-done.14.refs_1_
  47.7 1.6 %collective-permute-done.15.refs_2_ = f32[2,512]{1,0:T(2,128)S(1)} collective-permute-done((f32[2,512]{1,0:T(2,128)S(1)}, f32[2,512]{1,0:T(2,128)S(1)}, u32[]{:S(2)}, u32[]{:S(2)}) %collective-permute-start.15) | collective-permute-done | bytes 4128 | tf_op jit(solution)/shard_map/ppermute | solution.py:344
  49.2 0.0 collective-permute-done.16.refs_3_
  49.2 0.6 %token_scores.1 = f32[1,512]{1,0:T(1,128)} custom-call(f32[2,512]{1,0:T(2,128)S(1)} %partial_weights.1.refs_0_, f32[2,512]{1,0:T(2,128)S(1)} %collective-permute-done.14.refs_1_, f32[2,512]{1,0:T(2,128)S(1)} %collective-permute-done.15.refs_2_, f32[2,512]{1,0:T(2,128)S(1)} %collective-permute-done.16.refs_3_), custom_call_target="tpu_custom_call" | custom-call | bytes 4096 | tf_op jit(solution)/shard_map/token_scores/pallas_call | solution.py:477
  49.8 0.0 collective-permute-done.10.refs_0_
  49.8 1.0 %add_last_chunk.1 = (f32[8,32,128]{2,1,0:T(8,128)}, f32[28,32,128]{2,1,0:T(8,128)}) custom-call(f32[36,32,128]{2,1,0:T(8,128)S(1)} %add_chunks.1.own_ref, bf16[1200,128]{1,0:T(8,128)(2,1)S(1)} %collective-permute-done.10.refs_0_), custom_call_target="tpu_custom_call" | custom-call | bytes 1769472 | tf_op jit(solution)/shard_map/add_last_chunk/pallas_call | solution.py:482
  (1 shorter events, 0.0 us)
Async XLA Ops:
  1.7 14.3 %collective-permute-start.2 = (bf16[18,32,128]{2,1,0:T(8,128)(2,1)S(1)}, bf16[18,32,128]{2,1,0:T(8,128)(2,1)S(1)}, u32[]{:S(2)}, u32[]{:S(2)}) collective-permute-start(bf16[18,32,128]{2,1,0:T(8,128)(2,1)S(1)} %get-tuple-element.40), channel_id=1, source_target_pairs={{0,12},{4,8},{8,4},{12,0},{1,13},{5,9},{9,5},{13,1},{2,14},{6,10},... | collective-permute-start | bytes 442376 | tf_op jit(solution)/shard_map/ppermute | solution.py:344
  6.8 13.5 %collective-permute-start.4 = (bf16[18,32,128]{2,1,0:T(8,128)(2,1)S(1)}, bf16[18,32,128]{2,1,0:T(8,128)(2,1)S(1)}, u32[]{:S(2)}, u32[]{:S(2)}) collective-permute-start(bf16[18,32,128]{2,1,0:T(8,128)(2,1)S(1)} %get-tuple-element.40), channel_id=1, source_target_pairs={{0,8},{4,12},{8,0},{12,4},{1,9},{5,13},{9,1},{13,5},{2,10},{6,14},... | collective-permute-start | bytes 442376 | tf_op jit(solution)/shard_map/ppermute | solution.py:344
  6.8 15.0 %collective-permute-start.1 = (bf16[36,32,128]{2,1,0:T(8,128)(2,1)S(1)}, bf16[36,32,128]{2,1,0:T(8,128)(2,1)S(1)}, u32[]{:S(2)}, u32[]{:S(2)}) collective-permute-start(bf16[36,32,128]{2,1,0:T(8,128)(2,1)S(1)} %get-tuple-element.39.refs_0_), channel_id=1, source_target_pairs={{0,4},{4,0},{8,12},{12,8},{1,5},{5,1},{9,13},{13,9},{2,6},{6,2},{1... | collective-permute-start | bytes 884744 | tf_op jit(solution)/shard_map/ppermute | solution.py:344
  12.0 19.5 %collective-permute-start.8 = (bf16[1200,128]{1,0:T(8,128)(2,1)S(1)}, bf16[1200,128]{1,0:T(8,128)(2,1)S(1)}, u32[]{:S(2)}, u32[]{:S(2)}) collective-permute-start(bf16[1200,128]{1,0:T(8,128)(2,1)S(1)} %get-tuple-element.35), channel_id=1, source_target_pairs={{0,4},{12,8},{1,5},{13,9},{2,6},{14,10},{3,7},{15,11},{16,20},{28,... | collective-permute-start | bytes 921608 | tf_op jit(solution)/shard_map/ppermute | solution.py:415
  15.4 16.7 %collective-permute-start = (bf16[1200,128]{1,0:T(8,128)(2,1)S(1)}, bf16[1200,128]{1,0:T(8,128)(2,1)S(1)}, u32[]{:S(2)}, u32[]{:S(2)}) collective-permute-start(bf16[1200,128]{1,0:T(8,128)(2,1)S(1)} %get-tuple-element.35), channel_id=1, source_target_pairs={{4,8},{8,4},{5,9},{9,5},{6,10},{10,6},{7,11},{11,7},{20,24},{24,20... | collective-permute-start | bytes 921608 | tf_op jit(solution)/shard_map/ppermute | solution.py:414
  16.1 6.8 %collective-permute-start.3 = (bf16[18,32,128]{2,1,0:T(8,128)(2,1)S(1)}, bf16[18,32,128]{2,1,0:T(8,128)(2,1)S(1)}, u32[]{:S(2)}, u32[]{:S(2)}) collective-permute-start(bf16[18,32,128]{2,1,0:T(8,128)(2,1)S(1)} %collective-permute-done.2.refs_2_), channel_id=1, source_target_pairs={{0,16},{16,0},{1,17},{17,1},{2,18},{18,2},{3,19},{19,3},{4,20},{20... | collective-permute-start | bytes 442376 | tf_op jit(solution)/shard_map/ppermute | solution.py:344
  20.3 5.1 %collective-permute-start.5 = (bf16[18,32,128]{2,1,0:T(8,128)(2,1)S(1)}, bf16[18,32,128]{2,1,0:T(8,128)(2,1)S(1)}, u32[]{:S(2)}, u32[]{:S(2)}) collective-permute-start(bf16[18,32,128]{2,1,0:T(8,128)(2,1)S(1)} %collective-permute-done.4.refs_3_), channel_id=1, source_target_pairs={{0,16},{16,0},{1,17},{17,1},{2,18},{18,2},{3,19},{19,3},{4,20},{20... | collective-permute-start | bytes 442376 | tf_op jit(solution)/shard_map/ppermute | solution.py:344
  26.5 3.9 %collective-permute-start.6 = (f32[36,128]{1,0:T(8,128)S(1)}, f32[36,128]{1,0:T(8,128)S(1)}, u32[]{:S(2)}, u32[]{:S(2)}) collective-permute-start(f32[36,128]{1,0:T(8,128)S(1)} %get-tuple-element.44.left_ref), channel_id=1, source_target_pairs={{0,4},{4,0},{8,12},{12,8},{1,5},{5,1},{9,13},{13,9},{2,6},{6,2},{1... | collective-permute-start | bytes 55304 | tf_op jit(solution)/shard_map/ppermute | solution.py:344
  30.3 4.8 %collective-permute-start.7 = (f32[36,128]{1,0:T(8,128)S(1)}, f32[36,128]{1,0:T(8,128)S(1)}, u32[]{:S(2)}, u32[]{:S(2)}) collective-permute-start(f32[36,128]{1,0:T(8,128)S(1)} %pair_eigen.1.refs_0_), channel_id=1, source_target_pairs={{0,8},{4,12},{8,0},{12,4},{1,9},{5,13},{9,1},{13,5},{2,10},{6,14},... | collective-permute-start | bytes 55304 | tf_op jit(solution)/shard_map/ppermute | solution.py:344
  35.8 11.3 %collective-permute-start.9 = (bf16[1200,128]{1,0:T(8,128)(2,1)S(1)}, bf16[1200,128]{1,0:T(8,128)(2,1)S(1)}, u32[]{:S(2)}, u32[]{:S(2)}) collective-permute-start(bf16[1200,128]{1,0:T(8,128)(2,1)S(1)} %get-tuple-element.51), channel_id=1, source_target_pairs={{0,4},{4,0},{8,12},{12,8},{1,5},{5,1},{9,13},{13,9},{2,6},{6,2},{1... | collective-permute-start | bytes 921608 | tf_op jit(solution)/shard_map/ppermute | solution.py:344
  36.5 13.4 %collective-permute-start.10 = (bf16[1200,128]{1,0:T(8,128)(2,1)S(1)}, bf16[1200,128]{1,0:T(8,128)(2,1)S(1)}, u32[]{:S(2)}, u32[]{:S(2)}) collective-permute-start(bf16[1200,128]{1,0:T(8,128)(2,1)S(1)} %relay_chunk.1), channel_id=1, source_target_pairs={{0,8},{4,12},{8,0},{12,4},{1,9},{5,13},{9,1},{13,5},{2,10},{6,14},... | collective-permute-start | bytes 921608 | tf_op jit(solution)/shard_map/ppermute | solution.py:344
  39.1 1.9 %collective-permute-start.11 = (f32[2,128]{1,0:T(2,128)S(1)}, f32[2,128]{1,0:T(2,128)S(1)}, u32[]{:S(2)}, u32[]{:S(2)}) collective-permute-start(f32[2,128]{1,0:T(2,128)S(1)} %get-tuple-element.50.refs_2_), channel_id=1, source_target_pairs={{0,1},{1,0},{2,3},{3,2},{4,5},{5,4},{6,7},{7,6},{8,9},{9,8},{10,11... | collective-permute-start | bytes 3080 | tf_op jit(solution)/shard_map/ppermute | solution.py:344
  39.1 3.6 %collective-permute-start.12 = (f32[2,128]{1,0:T(2,128)S(1)}, f32[2,128]{1,0:T(2,128)S(1)}, u32[]{:S(2)}, u32[]{:S(2)}) collective-permute-start(f32[2,128]{1,0:T(2,128)S(1)} %get-tuple-element.50.refs_2_), channel_id=1, source_target_pairs={{0,2},{1,3},{2,0},{3,1},{4,6},{5,7},{6,4},{7,5},{8,10},{9,11},{10,... | collective-permute-start | bytes 3080 | tf_op jit(solution)/shard_map/ppermute | solution.py:344
  40.6 3.0 %collective-permute-start.13 = (f32[2,128]{1,0:T(2,128)S(1)}, f32[2,128]{1,0:T(2,128)S(1)}, u32[]{:S(2)}, u32[]{:S(2)}) collective-permute-start(f32[2,128]{1,0:T(2,128)S(1)} %get-tuple-element.50.refs_2_), channel_id=1, source_target_pairs={{0,3},{1,2},{2,1},{3,0},{4,7},{5,6},{6,5},{7,4},{8,11},{9,10},{10,... | collective-permute-start | bytes 3080 | tf_op jit(solution)/shard_map/ppermute | solution.py:344
  45.1 2.6 %collective-permute-start.14 = (f32[2,512]{1,0:T(2,128)S(1)}, f32[2,512]{1,0:T(2,128)S(1)}, u32[]{:S(2)}, u32[]{:S(2)}) collective-permute-start(f32[2,512]{1,0:T(2,128)S(1)} %partial_weights.1.refs_0_), channel_id=1, source_target_pairs={{0,1},{1,0},{2,3},{3,2},{4,5},{5,4},{6,7},{7,6},{8,9},{9,8},{10,11... | collective-permute-start | bytes 12296 | tf_op jit(solution)/shard_map/ppermute | solution.py:344
  45.6 3.6 %collective-permute-start.15 = (f32[2,512]{1,0:T(2,128)S(1)}, f32[2,512]{1,0:T(2,128)S(1)}, u32[]{:S(2)}, u32[]{:S(2)}) collective-permute-start(f32[2,512]{1,0:T(2,128)S(1)} %partial_weights.1.refs_0_), channel_id=1, source_target_pairs={{0,2},{1,3},{2,0},{3,1},{4,6},{5,7},{6,4},{7,5},{8,10},{9,11},{10,... | collective-permute-start | bytes 12296 | tf_op jit(solution)/shard_map/ppermute | solution.py:344
  46.1 3.1 %collective-permute-start.16 = (f32[2,512]{1,0:T(2,128)S(1)}, f32[2,512]{1,0:T(2,128)S(1)}, u32[]{:S(2)}, u32[]{:S(2)}) collective-permute-start(f32[2,512]{1,0:T(2,128)S(1)} %partial_weights.1.refs_0_), channel_id=1, source_target_pairs={{0,3},{1,2},{2,1},{3,0},{4,7},{5,6},{6,5},{7,4},{8,11},{9,10},{10,... | collective-permute-start | bytes 12296 | tf_op jit(solution)/shard_map/ppermute | solution.py:344

commit v11 on v9

--- a/solution.py
+++ b/solution.py
@@ -343,7 +343,7 @@
 def share(value, axis, direct):
     if not direct:
         return [lax.psum(value, axis)]
-    return [value] + [swap(value, axis, mask) for mask in range(1, lax.axis_size(axis))]
+    return [value] + [swap(value, axis, mask) for mask in reversed(range(1, lax.axis_size(axis)))]
 
 
 def after(values, done):

time: 49.8 us -> 48.6 us (0.976)
  waiting for transfers between devices: 13.8 us -> 11.4 us
  starting transfers between devices: 22.6 us -> 23.7 us
    ppermute x16, waiting for transfers between devices: 13.8 us -> 11.4 us  [swap(): return lax.ppermute(value, axis, [(i, i ^ mask) for i in range(count)])]
    ppermute x16, starting transfers between devices: 18.6 us -> 19.7 us  [swap(): return lax.ppermute(value, axis, [(i, i ^ mask) for i in range(count)])]
  transfers between devices with their start and end apart: 18 -> 18, of which waited for: 8 -> 7; matrix products, arithmetic and copies ran while one was open for 0% -> 0% of each run, Pallas kernels for 20% -> 20%
where the time goes in v11:
time: 48.6 us; the launch traced here: 48.4 us
  starting transfers between devices  23.7 us (49%)
  Pallas kernels  12.5 us (26%)
  waiting for transfers between devices  11.4 us (23%)
  between operations  0.75 us (2%)
    ppermute x16, starting transfers between devices, swap(): return lax.ppermute(value, axis, [(i, i ^ mask) for i in range(count)])  19.7 us
    ppermute x16, waiting for transfers between devices, swap(): return lax.ppermute(value, axis, [(i, i ^ mask) for i in range(count)])  11.4 us
    pallas_call x1, Pallas kernels, local(): call(functools.partial(gram_kernel, pieces, coded, scale), [bf16(*activat...  4.56 us
    ppermute x1, starting transfers between devices, local(): relayed = lax.ppermute(sent[3], 'dp', [(0, 1), (3, 2)])  3.32 us
    pallas_call x2, Pallas kernels, local(): call(functools.partial(eigen_kernel, part, halves, masks, pieces, scale),...  1.95 us
    pallas_call x1, Pallas kernels, local(): call(functools.partial(weight_kernel, halves, act_blocks // halves), f32(...  1.49 us
    pallas_call x1, Pallas kernels, local(): call(pack_kernel, [bf16(blocks // part, rows, BLK) for part in range(1, h...  1.08 us
    pallas_call x1, Pallas kernels, local(): call(functools.partial(last_add_kernel, [(None, 0, blocks)] * len(chunks)...  1.04 us
  transfers between devices with their start and end apart: 18, of which 7 were waited for; matrix products, arithmetic and copies ran while one was open for 0% of the time, Pallas kernels for 20%

profile of v11, /device:TPU:0, one launch (start us, length us, event | category | flops | bytes accessed | tf_op | source)
XLA Modules:
  0.0 48.4 jit_solution(11413451576257448173)
XLA Ops:
  0.6 1.1 %pack_basis.1 = (bf16[36,32,128]{2,1,0:T(8,128)(2,1)S(1)}, bf16[18,32,128]{2,1,0:T(8,128)(2,1)S(1)}) custom-call(s32[1]{0:T(128)} %bitcast.1.side_ref, bf16[8,32,128]{2,1,0:T(8,128)(2,1)} %act_ref.1, bf16[28,32,128]{2,1,0:T(8,128)(2,1)} %grad_ref.1), custom_call_target="tpu_custom_call" | custom-call | bytes 294912 | tf_op jit(solution)/shard_map/pack_basis/pallas_call | solution.py:368
  1.7 5.1 %collective-permute-start.2 = (bf16[18,32,128]{2,1,0:T(8,128)(2,1)S(1)}, bf16[18,32,128]{2,1,0:T(8,128)(2,1)S(1)}, u32[]{:S(2)}, u32[]{:S(2)}) collective-permute-start(bf16[18,32,128]{2,1,0:T(8,128)(2,1)S(1)} %get-tuple-element.42), channel_id=1, source_target_pairs={{0,12},{4,8},{8,4},{12,0},{1,13},{5,9},{9,5},{13,1},{2,14},{6,10},... | collective-permute-start | bytes 442376 | tf_op jit(solution)/shard_map/ppermute | solution.py:340
  6.8 0.0 collective-permute-start.4
  6.8 0.6 %collective-permute-start.1 = (bf16[36,32,128]{2,1,0:T(8,128)(2,1)S(1)}, bf16[36,32,128]{2,1,0:T(8,128)(2,1)S(1)}, u32[]{:S(2)}, u32[]{:S(2)}) collective-permute-start(bf16[36,32,128]{2,1,0:T(8,128)(2,1)S(1)} %get-tuple-element.41.refs_0_), channel_id=1, source_target_pairs={{0,4},{4,0},{8,12},{12,8},{1,5},{5,1},{9,13},{13,9},{2,6},{6,2},{1... | collective-permute-start | bytes 884744 | tf_op jit(solution)/shard_map/ppermute | solution.py:340
  7.5 4.6 %partial_gram.1 = (bf16[512,1024]{1,0:T(8,128)(2,1)S(1)}, bf16[512,3584]{1,0:T(8,128)(2,1)S(1)}, f32[36,32,128]{2,1,0:T(8,128)S(1)}, f32[36,32,128]{2,1,0:T(8,12...) custom-call(s32[1]{0:T(128)} %bitcast.me_ref, bf16[512,1024]{1,0:T(8,128)(2,1)} %act_hbm.1, ...), custom_call_target="tpu_custom_call" | custom-call | flops 1207959552 | bytes 4718592 | tf_op jit(solution)/shard_map/partial_gram/pallas_call | solution.py:389
  12.0 3.3 %collective-permute-start.9 = (bf16[1200,128]{1,0:T(8,128)(2,1)S(1)}, bf16[1200,128]{1,0:T(8,128)(2,1)S(1)}, u32[]{:S(2)}, u32[]{:S(2)}) collective-permute-start(bf16[1200,128]{1,0:T(8,128)(2,1)S(1)} %get-tuple-element.37), channel_id=1, source_target_pairs={{0,4},{12,8},{1,5},{13,9},{2,6},{14,10},{3,7},{15,11},{16,20},{28,... | collective-permute-start | bytes 921608 | tf_op jit(solution)/shard_map/ppermute | solution.py:411
  15.4 0.7 %collective-permute-start = (bf16[1200,128]{1,0:T(8,128)(2,1)S(1)}, bf16[1200,128]{1,0:T(8,128)(2,1)S(1)}, u32[]{:S(2)}, u32[]{:S(2)}) collective-permute-start(bf16[1200,128]{1,0:T(8,128)(2,1)S(1)} %get-tuple-element.37), channel_id=1, source_target_pairs={{4,8},{8,4},{5,9},{9,5},{6,10},{10,6},{7,11},{11,7},{20,24},{24,20... | collective-permute-start | bytes 921608 | tf_op jit(solution)/shard_map/ppermute | solution.py:410
  16.1 0.0 collective-permute-done.2.refs_2_
  16.1 1.6 %collective-permute-start.3 = (bf16[18,32,128]{2,1,0:T(8,128)(2,1)S(1)}, bf16[18,32,128]{2,1,0:T(8,128)(2,1)S(1)}, u32[]{:S(2)}, u32[]{:S(2)}) collective-permute-start(bf16[18,32,128]{2,1,0:T(8,128)(2,1)S(1)} %collective-permute-done.2.refs_2_), channel_id=1, source_target_pairs={{0,16},{16,0},{1,17},{17,1},{2,18},{18,2},{3,19},{19,3},{4,20},{20... | collective-permute-start | bytes 442376 | tf_op jit(solution)/shard_map/ppermute | solution.py:340
  17.6 2.7 %collective-permute-done.4.refs_3_ = bf16[18,32,128]{2,1,0:T(8,128)(2,1)S(1)} collective-permute-done((bf16[18,32,128]{2,1,0:T(8,128)(2,1)S(1)}, bf16[18,32,128]{2,1,0:T(8,128)(2,1)S(1)}, u32[]{:S(2)}, u32[]{:S(2)}) %collective-permute-start.4) | collective-permute-done | bytes 147488 | tf_op jit(solution)/shard_map/ppermute | solution.py:340
  20.3 1.5 %collective-permute-start.5 = (bf16[18,32,128]{2,1,0:T(8,128)(2,1)S(1)}, bf16[18,32,128]{2,1,0:T(8,128)(2,1)S(1)}, u32[]{:S(2)}, u32[]{:S(2)}) collective-permute-start(bf16[18,32,128]{2,1,0:T(8,128)(2,1)S(1)} %collective-permute-done.4.refs_3_), channel_id=1, source_target_pairs={{0,16},{16,0},{1,17},{17,1},{2,18},{18,2},{3,19},{19,3},{4,20},{20... | collective-permute-start | bytes 442376 | tf_op jit(solution)/shard_map/ppermute | solution.py:340
  21.8 0.0 collective-permute-done.1.refs_1_
  21.8 1.0 %partial_eigen.2 = (f32[9,512,256]{2,1,0:T(8,128)S(1)}, f32[18,128]{1,0:T(8,128)S(1)}) custom-call(s32[1]{0:T(128)} %bitcast.me_ref, s32[1]{0:T(128)} %bitcast.1.side_ref, bf16[512,1024]{1,0:T(8,128)(2,1)S(1)} %get-tuple-element.39.act_ref, bf16[512,3584]{1,0:T(8,128)(2,1)S(1)} %get-tuple-element.40.grad_ref, ...), custom_call_target="tpu_custom_call" | custom-call | flops 301989888 | bytes 2359296 | tf_op jit(solution)/shard_map/partial_eigen/pallas_call | solution.py:419
  22.8 0.0 collective-permute-done.3.refs_2_
  22.8 2.6 %collective-permute-done.5.refs_3_ = bf16[18,32,128]{2,1,0:T(8,128)(2,1)S(1)} collective-permute-done((bf16[18,32,128]{2,1,0:T(8,128)(2,1)S(1)}, bf16[18,32,128]{2,1,0:T(8,128)(2,1)S(1)}, u32[]{:S(2)}, u32[]{:S(2)}) %collective-permute-start.5) | collective-permute-done | bytes 147488 | tf_op jit(solution)/shard_map/ppermute | solution.py:340
  25.5 1.0 %partial_eigen.3 = (f32[9,512,256]{2,1,0:T(8,128)S(1)}, f32[36,128]{1,0:T(8,128)S(1)}) custom-call(s32[1]{0:T(128)} %bitcast.me_ref, s32[1]{0:T(128)} %bitcast.1.side_ref, bf16[512,1024]{1,0:T(8,128)(2,1)S(1)} %get-tuple-element.39.act_ref, bf16[512,3584]{1,0:T(8,128)(2,1)S(1)} %get-tuple-element.40.grad_ref, ...), custom_call_target="tpu_custom_call" | custom-call | flops 301989888 | bytes 2359296 | tf_op jit(solution)/shard_map/partial_eigen/pallas_call | solution.py:419
  26.5 2.7 %collective-permute-start.6 = (f32[36,128]{1,0:T(8,128)S(1)}, f32[36,128]{1,0:T(8,128)S(1)}, u32[]{:S(2)}, u32[]{:S(2)}) collective-permute-start(f32[36,128]{1,0:T(8,128)S(1)} %get-tuple-element.50.refs_0_), channel_id=1, source_target_pairs={{0,12},{4,8},{8,4},{12,0},{1,13},{5,9},{9,5},{13,1},{2,14},{6,10},... | collective-permute-start | bytes 55304 | tf_op jit(solution)/shard_map/ppermute | solution.py:340
  29.2 0.0 collective-permute-start.7
  29.2 1.7 %collective-permute-start.8 = (f32[36,128]{1,0:T(8,128)S(1)}, f32[36,128]{1,0:T(8,128)S(1)}, u32[]{:S(2)}, u32[]{:S(2)}) collective-permute-start(f32[36,128]{1,0:T(8,128)S(1)} %get-tuple-element.50.refs_0_), channel_id=1, source_target_pairs={{0,4},{4,0},{8,12},{12,8},{1,5},{5,1},{9,13},{13,9},{2,6},{6,2},{1... | collective-permute-start | bytes 55304 | tf_op jit(solution)/shard_map/ppermute | solution.py:340
  30.9 0.0 collective-permute-done.9.relayed_ref
  30.9 0.6 %relay_chunk.1 = bf16[1200,128]{1,0:T(8,128)(2,1)S(1)} custom-call(f32[36,32,128]{2,1,0:T(8,128)S(1)} %get-tuple-element.48.far_ref, bf16[1200,128]{1,0:T(8,128)(2,1)S(1)} %collective-permute-done.9.relayed_ref), custom_call_target="tpu_custom_call" | custom-call | bytes 1769472 | tf_op jit(solution)/shard_map/relay_chunk/pallas_call | solution.py:428
  31.5 0.0 collective-permute-done.refs_0_
  31.5 0.6 %collective-permute-done.6.refs_1_ = f32[36,128]{1,0:T(8,128)S(1)} collective-permute-done((f32[36,128]{1,0:T(8,128)S(1)}, f32[36,128]{1,0:T(8,128)S(1)}, u32[]{:S(2)}, u32[]{:S(2)}) %collective-permute-start.6) | collective-permute-done | bytes 18464 | tf_op jit(solution)/shard_map/ppermute | solution.py:340
  32.1 1.9 %collective-permute-done.7.refs_2_ = f32[36,128]{1,0:T(8,128)S(1)} collective-permute-done((f32[36,128]{1,0:T(8,128)S(1)}, f32[36,128]{1,0:T(8,128)S(1)}, u32[]{:S(2)}, u32[]{:S(2)}) %collective-permute-start.7) | collective-permute-done | bytes 18464 | tf_op jit(solution)/shard_map/ppermute | solution.py:340
  34.0 0.0 collective-permute-done.8.refs_3_
  34.0 0.6 %combine_eigen.1 = (f32[8,128]{1,0:T(8,128)}, f32[28,128]{1,0:T(8,128)}, f32[36,128]{1,0:T(8,128)S(1)}, f32[2,128]{1,0:T(2,128)S(1)}) custom-call(s32[1]{0:T(128)} %bitcast.1.side_ref, f32[36,128]{1,0:T(8,128)S(1)} %get-tuple-element.50.refs_0_, f32[36,128]{1,0:T(8,128)S(1)} %collective-permute-done.6.refs_1_, f32[36,128]{1,0:T(8,128)S(1)} %collective-permute-done.7.refs_2_, ...), custom_call_target="tpu_custom_call" | custom-call | bytes 73728 | tf_op jit(solution)/shard_map/combine_eigen/pallas_call | solution.py:436
  34.6 0.9 %collective-permute-start.10 = (bf16[1200,128]{1,0:T(8,128)(2,1)S(1)}, bf16[1200,128]{1,0:T(8,128)(2,1)S(1)}, u32[]{:S(2)}, u32[]{:S(2)}) collective-permute-start(bf16[1200,128]{1,0:T(8,128)(2,1)S(1)} %get-tuple-element.55), channel_id=1, source_target_pairs={{0,4},{4,0},{8,12},{12,8},{1,5},{5,1},{9,13},{13,9},{2,6},{6,2},{1... | collective-permute-start | bytes 921608 | tf_op jit(solution)/shard_map/ppermute | solution.py:340
  35.5 1.3 %collective-permute-start.11 = (bf16[1200,128]{1,0:T(8,128)(2,1)S(1)}, bf16[1200,128]{1,0:T(8,128)(2,1)S(1)}, u32[]{:S(2)}, u32[]{:S(2)}) collective-permute-start(bf16[1200,128]{1,0:T(8,128)(2,1)S(1)} %relay_chunk.1), channel_id=1, source_target_pairs={{0,8},{4,12},{8,0},{12,4},{1,9},{5,13},{9,1},{13,5},{2,10},{6,14},... | collective-permute-start | bytes 921608 | tf_op jit(solution)/shard_map/ppermute | solution.py:340
  36.8 0.0 collective-permute-start.12
  36.8 1.5 %collective-permute-start.13 = (f32[2,128]{1,0:T(2,128)S(1)}, f32[2,128]{1,0:T(2,128)S(1)}, u32[]{:S(2)}, u32[]{:S(2)}) collective-permute-start(f32[2,128]{1,0:T(2,128)S(1)} %get-tuple-element.54.refs_2_), channel_id=1, source_target_pairs={{0,2},{1,3},{2,0},{3,1},{4,6},{5,7},{6,4},{7,5},{8,10},{9,11},{10,... | collective-permute-start | bytes 3080 | tf_op jit(solution)/shard_map/ppermute | solution.py:340
  38.3 0.3 collective-permute-start.14
  38.7 1.1 %collective-permute-done.12.refs_3_ = f32[2,128]{1,0:T(2,128)S(1)} collective-permute-done((f32[2,128]{1,0:T(2,128)S(1)}, f32[2,128]{1,0:T(2,128)S(1)}, u32[]{:S(2)}, u32[]{:S(2)}) %collective-permute-start.12) | collective-permute-done | bytes 1056 | tf_op jit(solution)/shard_map/ppermute | solution.py:340
  39.8 0.6 %collective-permute-done.13.refs_4_ = f32[2,128]{1,0:T(2,128)S(1)} collective-permute-done((f32[2,128]{1,0:T(2,128)S(1)}, f32[2,128]{1,0:T(2,128)S(1)}, u32[]{:S(2)}, u32[]{:S(2)}) %collective-permute-start.13) | collective-permute-done | bytes 1056 | tf_op jit(solution)/shard_map/ppermute | solution.py:340
  40.4 0.0 collective-permute-done.14.refs_5_
  40.4 1.5 %partial_weights.1.refs_0_ = f32[2,512]{1,0:T(2,128)S(1)} custom-call(f32[36,128]{1,0:T(8,128)S(1)} %get-tuple-element.61.eigen_ref, f32[9,512,256]{2,1,0:T(8,128)S(1)} %get-tuple-element.62.refs_0_, f32[9,512,256]{2,1,0:T(8,128)S(1)} %get-tuple-element.63.refs_1_, f32[2,128]{1,0:T(2,128)S(1)} %get-tuple-element.54.refs_2_, ...), custom_call_target="tpu_custom_call" | custom-call | bytes 9437184 | tf_op jit(solution)/shard_map/partial_weights/pallas_call | solution.py:446
  41.9 0.9 %collective-permute-start.15 = (f32[2,512]{1,0:T(2,128)S(1)}, f32[2,512]{1,0:T(2,128)S(1)}, u32[]{:S(2)}, u32[]{:S(2)}) collective-permute-start(f32[2,512]{1,0:T(2,128)S(1)} %partial_weights.1.refs_0_), channel_id=1, source_target_pairs={{0,3},{1,2},{2,1},{3,0},{4,7},{5,6},{6,5},{7,4},{8,11},{9,10},{10,... | collective-permute-start | bytes 12296 | tf_op jit(solution)/shard_map/ppermute | solution.py:340
  42.8 1.5 %collective-permute-start.16 = (f32[2,512]{1,0:T(2,128)S(1)}, f32[2,512]{1,0:T(2,128)S(1)}, u32[]{:S(2)}, u32[]{:S(2)}) collective-permute-start(f32[2,512]{1,0:T(2,128)S(1)} %partial_weights.1.refs_0_), channel_id=1, source_target_pairs={{0,2},{1,3},{2,0},{3,1},{4,6},{5,7},{6,4},{7,5},{8,10},{9,11},{10,... | collective-permute-start | bytes 12296 | tf_op jit(solution)/shard_map/ppermute | solution.py:340
  44.3 0.0 collective-permute-start.17
  44.3 1.9 %collective-permute-done.10.refs_1_ = bf16[1200,128]{1,0:T(8,128)(2,1)S(1)} collective-permute-done((bf16[1200,128]{1,0:T(8,128)(2,1)S(1)}, bf16[1200,128]{1,0:T(8,128)(2,1)S(1)}, u32[]{:S(2)}, u32[]{:S(2)}) %collective-permute-start.10) | collective-permute-done | bytes 307232 | tf_op jit(solution)/shard_map/ppermute | solution.py:340
  46.1 0.6 %add_chunks.1.own_ref = f32[36,32,128]{2,1,0:T(8,128)S(1)} custom-call(f32[36,32,128]{2,1,0:T(8,128)S(1)} %get-tuple-element.36.own_ref, bf16[1200,128]{1,0:T(8,128)(2,1)S(1)} %collective-permute-done.refs_0_, bf16[1200,128]{1,0:T(8,128)(2,1)S(1)} %collective-permute-done.10.refs_1_), custom_call_target="tpu_custom_call" | custom-call | bytes 2359296 | tf_op jit(solution)/shard_map/add_chunks/pallas_call | solution.py:462
  46.8 0.0 collective-permute-done.15.refs_1_
  46.8 0.0 collective-permute-done.16.refs_2_
  46.8 0.0 collective-permute-done.17.refs_3_
  46.8 0.6 %token_scores.1 = f32[1,512]{1,0:T(1,128)} custom-call(f32[2,512]{1,0:T(2,128)S(1)} %partial_weights.1.refs_0_, f32[2,512]{1,0:T(2,128)S(1)} %collective-permute-done.15.refs_1_, f32[2,512]{1,0:T(2,128)S(1)} %collective-permute-done.16.refs_2_, f32[2,512]{1,0:T(2,128)S(1)} %collective-permute-done.17.refs_3_), custom_call_target="tpu_custom_call" | custom-call | bytes 4096 | tf_op jit(solution)/shard_map/token_scores/pallas_call | solution.py:467
  47.4 0.0 collective-permute-done.11.refs_0_
  47.4 1.0 %add_last_chunk.1 = (f32[8,32,128]{2,1,0:T(8,128)}, f32[28,32,128]{2,1,0:T(8,128)}) custom-call(f32[36,32,128]{2,1,0:T(8,128)S(1)} %add_chunks.1.own_ref, bf16[1200,128]{1,0:T(8,128)(2,1)S(1)} %collective-permute-done.11.refs_0_), custom_call_target="tpu_custom_call" | custom-call | bytes 1769472 | tf_op jit(solution)/shard_map/add_last_chunk/pallas_call | solution.py:472
Async XLA Ops:
  1.7 14.3 %collective-permute-start.2 = (bf16[18,32,128]{2,1,0:T(8,128)(2,1)S(1)}, bf16[18,32,128]{2,1,0:T(8,128)(2,1)S(1)}, u32[]{:S(2)}, u32[]{:S(2)}) collective-permute-start(bf16[18,32,128]{2,1,0:T(8,128)(2,1)S(1)} %get-tuple-element.42), channel_id=1, source_target_pairs={{0,12},{4,8},{8,4},{12,0},{1,13},{5,9},{9,5},{13,1},{2,14},{6,10},... | collective-permute-start | bytes 442376 | tf_op jit(solution)/shard_map/ppermute | solution.py:340
  6.8 13.5 %collective-permute-start.4 = (bf16[18,32,128]{2,1,0:T(8,128)(2,1)S(1)}, bf16[18,32,128]{2,1,0:T(8,128)(2,1)S(1)}, u32[]{:S(2)}, u32[]{:S(2)}) collective-permute-start(bf16[18,32,128]{2,1,0:T(8,128)(2,1)S(1)} %get-tuple-element.42), channel_id=1, source_target_pairs={{0,8},{4,12},{8,0},{12,4},{1,9},{5,13},{9,1},{13,5},{2,10},{6,14},... | collective-permute-start | bytes 442376 | tf_op jit(solution)/shard_map/ppermute | solution.py:340
  6.8 15.0 %collective-permute-start.1 = (bf16[36,32,128]{2,1,0:T(8,128)(2,1)S(1)}, bf16[36,32,128]{2,1,0:T(8,128)(2,1)S(1)}, u32[]{:S(2)}, u32[]{:S(2)}) collective-permute-start(bf16[36,32,128]{2,1,0:T(8,128)(2,1)S(1)} %get-tuple-element.41.refs_0_), channel_id=1, source_target_pairs={{0,4},{4,0},{8,12},{12,8},{1,5},{5,1},{9,13},{13,9},{2,6},{6,2},{1... | collective-permute-start | bytes 884744 | tf_op jit(solution)/shard_map/ppermute | solution.py:340
  12.0 18.9 %collective-permute-start.9 = (bf16[1200,128]{1,0:T(8,128)(2,1)S(1)}, bf16[1200,128]{1,0:T(8,128)(2,1)S(1)}, u32[]{:S(2)}, u32[]{:S(2)}) collective-permute-start(bf16[1200,128]{1,0:T(8,128)(2,1)S(1)} %get-tuple-element.37), channel_id=1, source_target_pairs={{0,4},{12,8},{1,5},{13,9},{2,6},{14,10},{3,7},{15,11},{16,20},{28,... | collective-permute-start | bytes 921608 | tf_op jit(solution)/shard_map/ppermute | solution.py:411
  15.4 16.1 %collective-permute-start = (bf16[1200,128]{1,0:T(8,128)(2,1)S(1)}, bf16[1200,128]{1,0:T(8,128)(2,1)S(1)}, u32[]{:S(2)}, u32[]{:S(2)}) collective-permute-start(bf16[1200,128]{1,0:T(8,128)(2,1)S(1)} %get-tuple-element.37), channel_id=1, source_target_pairs={{4,8},{8,4},{5,9},{9,5},{6,10},{10,6},{7,11},{11,7},{20,24},{24,20... | collective-permute-start | bytes 921608 | tf_op jit(solution)/shard_map/ppermute | solution.py:410
  16.1 6.8 %collective-permute-start.3 = (bf16[18,32,128]{2,1,0:T(8,128)(2,1)S(1)}, bf16[18,32,128]{2,1,0:T(8,128)(2,1)S(1)}, u32[]{:S(2)}, u32[]{:S(2)}) collective-permute-start(bf16[18,32,128]{2,1,0:T(8,128)(2,1)S(1)} %collective-permute-done.2.refs_2_), channel_id=1, source_target_pairs={{0,16},{16,0},{1,17},{17,1},{2,18},{18,2},{3,19},{19,3},{4,20},{20... | collective-permute-start | bytes 442376 | tf_op jit(solution)/shard_map/ppermute | solution.py:340
  20.3 5.1 %collective-permute-start.5 = (bf16[18,32,128]{2,1,0:T(8,128)(2,1)S(1)}, bf16[18,32,128]{2,1,0:T(8,128)(2,1)S(1)}, u32[]{:S(2)}, u32[]{:S(2)}) collective-permute-start(bf16[18,32,128]{2,1,0:T(8,128)(2,1)S(1)} %collective-permute-done.4.refs_3_), channel_id=1, source_target_pairs={{0,16},{16,0},{1,17},{17,1},{2,18},{18,2},{3,19},{19,3},{4,20},{20... | collective-permute-start | bytes 442376 | tf_op jit(solution)/shard_map/ppermute | solution.py:340
  26.5 5.6 %collective-permute-start.6 = (f32[36,128]{1,0:T(8,128)S(1)}, f32[36,128]{1,0:T(8,128)S(1)}, u32[]{:S(2)}, u32[]{:S(2)}) collective-permute-start(f32[36,128]{1,0:T(8,128)S(1)} %get-tuple-element.50.refs_0_), channel_id=1, source_target_pairs={{0,12},{4,8},{8,4},{12,0},{1,13},{5,9},{9,5},{13,1},{2,14},{6,10},... | collective-permute-start | bytes 55304 | tf_op jit(solution)/shard_map/ppermute | solution.py:340
  29.2 4.8 %collective-permute-start.7 = (f32[36,128]{1,0:T(8,128)S(1)}, f32[36,128]{1,0:T(8,128)S(1)}, u32[]{:S(2)}, u32[]{:S(2)}) collective-permute-start(f32[36,128]{1,0:T(8,128)S(1)} %get-tuple-element.50.refs_0_), channel_id=1, source_target_pairs={{0,8},{4,12},{8,0},{12,4},{1,9},{5,13},{9,1},{13,5},{2,10},{6,14},... | collective-permute-start | bytes 55304 | tf_op jit(solution)/shard_map/ppermute | solution.py:340
  29.2 4.8 %collective-permute-start.8 = (f32[36,128]{1,0:T(8,128)S(1)}, f32[36,128]{1,0:T(8,128)S(1)}, u32[]{:S(2)}, u32[]{:S(2)}) collective-permute-start(f32[36,128]{1,0:T(8,128)S(1)} %get-tuple-element.50.refs_0_), channel_id=1, source_target_pairs={{0,4},{4,0},{8,12},{12,8},{1,5},{5,1},{9,13},{13,9},{2,6},{6,2},{1... | collective-permute-start | bytes 55304 | tf_op jit(solution)/shard_map/ppermute | solution.py:340
  34.6 11.6 %collective-permute-start.10 = (bf16[1200,128]{1,0:T(8,128)(2,1)S(1)}, bf16[1200,128]{1,0:T(8,128)(2,1)S(1)}, u32[]{:S(2)}, u32[]{:S(2)}) collective-permute-start(bf16[1200,128]{1,0:T(8,128)(2,1)S(1)} %get-tuple-element.55), channel_id=1, source_target_pairs={{0,4},{4,0},{8,12},{12,8},{1,5},{5,1},{9,13},{13,9},{2,6},{6,2},{1... | collective-permute-start | bytes 921608 | tf_op jit(solution)/shard_map/ppermute | solution.py:340
  35.5 11.9 %collective-permute-start.11 = (bf16[1200,128]{1,0:T(8,128)(2,1)S(1)}, bf16[1200,128]{1,0:T(8,128)(2,1)S(1)}, u32[]{:S(2)}, u32[]{:S(2)}) collective-permute-start(bf16[1200,128]{1,0:T(8,128)(2,1)S(1)} %relay_chunk.1), channel_id=1, source_target_pairs={{0,8},{4,12},{8,0},{12,4},{1,9},{5,13},{9,1},{13,5},{2,10},{6,14},... | collective-permute-start | bytes 921608 | tf_op jit(solution)/shard_map/ppermute | solution.py:340
  36.8 3.0 %collective-permute-start.12 = (f32[2,128]{1,0:T(2,128)S(1)}, f32[2,128]{1,0:T(2,128)S(1)}, u32[]{:S(2)}, u32[]{:S(2)}) collective-permute-start(f32[2,128]{1,0:T(2,128)S(1)} %get-tuple-element.54.refs_2_), channel_id=1, source_target_pairs={{0,3},{1,2},{2,1},{3,0},{4,7},{5,6},{6,5},{7,4},{8,11},{9,10},{10,... | collective-permute-start | bytes 3080 | tf_op jit(solution)/shard_map/ppermute | solution.py:340
  36.8 3.6 %collective-permute-start.13 = (f32[2,128]{1,0:T(2,128)S(1)}, f32[2,128]{1,0:T(2,128)S(1)}, u32[]{:S(2)}, u32[]{:S(2)}) collective-permute-start(f32[2,128]{1,0:T(2,128)S(1)} %get-tuple-element.54.refs_2_), channel_id=1, source_target_pairs={{0,2},{1,3},{2,0},{3,1},{4,6},{5,7},{6,4},{7,5},{8,10},{9,11},{10,... | collective-permute-start | bytes 3080 | tf_op jit(solution)/shard_map/ppermute | solution.py:340
  38.3 2.1 %collective-permute-start.14 = (f32[2,128]{1,0:T(2,128)S(1)}, f32[2,128]{1,0:T(2,128)S(1)}, u32[]{:S(2)}, u32[]{:S(2)}) collective-permute-start(f32[2,128]{1,0:T(2,128)S(1)} %get-tuple-element.54.refs_2_), channel_id=1, source_target_pairs={{0,1},{1,0},{2,3},{3,2},{4,5},{5,4},{6,7},{7,6},{8,9},{9,8},{10,11... | collective-permute-start | bytes 3080 | tf_op jit(solution)/shard_map/ppermute | solution.py:340
  41.9 4.9 %collective-permute-start.15 = (f32[2,512]{1,0:T(2,128)S(1)}, f32[2,512]{1,0:T(2,128)S(1)}, u32[]{:S(2)}, u32[]{:S(2)}) collective-permute-start(f32[2,512]{1,0:T(2,128)S(1)} %partial_weights.1.refs_0_), channel_id=1, source_target_pairs={{0,3},{1,2},{2,1},{3,0},{4,7},{5,6},{6,5},{7,4},{8,11},{9,10},{10,... | collective-permute-start | bytes 12296 | tf_op jit(solution)/shard_map/ppermute | solution.py:340
  42.8 4.0 %collective-permute-start.16 = (f32[2,512]{1,0:T(2,128)S(1)}, f32[2,512]{1,0:T(2,128)S(1)}, u32[]{:S(2)}, u32[]{:S(2)}) collective-permute-start(f32[2,512]{1,0:T(2,128)S(1)} %partial_weights.1.refs_0_), channel_id=1, source_target_pairs={{0,2},{1,3},{2,0},{3,1},{4,6},{5,7},{6,4},{7,5},{8,10},{9,11},{10,... | collective-permute-start | bytes 12296 | tf_op jit(solution)/shard_map/ppermute | solution.py:340
  44.3 2.5 %collective-permute-start.17 = (f32[2,512]{1,0:T(2,128)S(1)}, f32[2,512]{1,0:T(2,128)S(1)}, u32[]{:S(2)}, u32[]{:S(2)}) collective-permute-start(f32[2,512]{1,0:T(2,128)S(1)} %partial_weights.1.refs_0_), channel_id=1, source_target_pairs={{0,1},{1,0},{2,3},{3,2},{4,5},{5,4},{6,7},{7,6},{8,9},{9,8},{10,11... | collective-permute-start | bytes 12296 | tf_op jit(solution)/shard_map/ppermute | solution.py:340

commit v12 on v9

--- a/solution.py
+++ b/solution.py
@@ -27,8 +27,8 @@
 IN_HBM = pl.BlockSpec(memory_space=pltpu.HBM)
 
 
-def scale_rows(first, end):
-    return 16 * pl.cdiv(end - first, 16)
+def scale_rows(blocks):
+    return 16 * pl.cdiv(blocks, 16)
 
 
 def call(
@@ -106,11 +106,24 @@
         copy.wait()
 
 
-def gram_kernel(pieces, messages, scale, me_ref, act_hbm, grad_hbm, act_ref, grad_ref, *refs):
+def pick(me, masks):
+    ends, middle = masks
+    return me ^ ends if ends == middle else jnp.where(in_middle(me), me ^ middle, me ^ ends)
+
+
+def in_middle(me):
+    return jnp.logical_or(me == 1, me == 2)
+
+
+def gram_kernel(pieces, plain, coded, scale, me_ref, act_hbm, grad_hbm, act_ref, grad_ref, *refs):
     refs, (whole, tops, sems) = refs[:-3], refs[-3:]
-    plain_refs, sent_refs = refs[: len(refs) - len(messages)], refs[len(refs) - len(messages) :]
+    plain_refs, sent_refs = refs[: len(plain)], refs[len(plain) :]
     rows = BLK // pieces
     me = me_ref[0]
+
+    def first_row(masks):
+        return pl.multiple_of(pick(me, masks) * rows, rows)
+
     steps = []
     for source, target in ((act_hbm, act_ref), (grad_hbm, grad_ref)):
         for first in range(0, source.shape[1], GROUP * BLK):
@@ -134,71 +147,62 @@
                 plain_refs[0][block] = gram
                 continue
             whole[offset] = gram
-            for ref_at, mask in zip(plain_refs, (0, 2)):
-                row = pl.multiple_of((me ^ mask) * rows, rows)
-                ref_at[block] = whole[offset, pl.ds(row, rows), :]
+            for plain_ref, masks in zip(plain_refs, plain):
+                plain_ref[block] = whole[offset, pl.ds(first_row(masks), rows), :]
             top = top_of(gram)
             tops[block : block + 1, :] = top
             gain = CODE_TOP / top
-            for sent_ref, (mask, first, end) in zip(sent_refs, messages):
-                if first <= block < end:
-                    row = pl.multiple_of((me ^ mask) * rows, rows)
-                    place = slice((block - first) * rows, (block - first + 1) * rows)
-                    sent_ref[place, :] = encode(whole[offset, pl.ds(row, rows), :] * gain)
-    for sent_ref, (_, first, end) in zip(sent_refs, messages):
-        sent_ref[(end - first) * rows :, :] = tops[
-            first : first + scale_rows(first, end), :
-        ].astype(jnp.bfloat16)
-
-
-def add_group(messages, rows, own_ref, sent_refs, tops_refs, step):
+            for sent_ref, masks in zip(sent_refs, coded):
+                sent_ref[block * rows : (block + 1) * rows, :] = encode(
+                    whole[offset, pl.ds(first_row(masks), rows), :] * gain
+                )
+    for sent_ref in sent_refs:
+        sent_ref[len(steps) * GROUP * rows :, :] = tops[...].astype(jnp.bfloat16)
+
+
+def add_group(own_ref, sent_refs, tops_refs, step):
+    rows = own_ref.shape[1]
     for block in range(step * GROUP, (step + 1) * GROUP):
         total = own_ref[block]
-        for (_, first, end), sent_ref, tops in zip(messages, sent_refs, tops_refs):
-            if first <= block < end:
-                at = block - first
-                values = decode(sent_ref[at * rows : (at + 1) * rows, :])
-                total = total + values * tops[at : at + 1, :]
+        for sent_ref, tops in zip(sent_refs, tops_refs):
+            values = decode(sent_ref[block * rows : (block + 1) * rows, :])
+            total = total + values * tops[block : block + 1, :]
         yield block, total
 
 
-def load_tops(messages, rows, sent_refs, tops_refs):
-    for (_, first, end), sent_ref, tops in zip(messages, sent_refs, tops_refs):
-        tops[...] = sent_ref[(end - first) * rows :, :].astype(jnp.float32) * (1.0 / CODE_TOP)
-
-
-def add_kernel(messages, own_ref, *refs):
-    sent_refs, sum_ref, tops_refs = refs[: len(messages)], refs[len(messages)], refs[len(messages) + 1 :]
+def load_tops(own_ref, sent_ref, tops, weight=1.0):
     blocks, rows, _ = own_ref.shape
-    load_tops(messages, rows, sent_refs, tops_refs)
-    for step in range(blocks // GROUP):
-        for block, total in add_group(messages, rows, own_ref, sent_refs, tops_refs, step):
+    tops[...] = sent_ref[blocks * rows :, :].astype(jnp.float32) * (weight / CODE_TOP)
+
+
+def add_kernel(me_ref, own_ref, *refs):
+    count = len(refs) // 2
+    sent_refs, sum_ref, tops_refs = refs[:count], refs[count], refs[count + 1 :]
+    ends = 1.0 - in_middle(me_ref[0]).astype(jnp.float32)
+    for index, (sent_ref, tops) in enumerate(zip(sent_refs, tops_refs)):
+        load_tops(own_ref, sent_ref, tops, ends if index == 0 else 1.0)
+    for step in range(own_ref.shape[0] // GROUP):
+        for block, total in add_group(own_ref, sent_refs, tops_refs, step):
             sum_ref[block] = total
 
 
-def relay_kernel(message, far_ref, relayed_ref, sent_ref, relayed_tops, tops):
-    messages = (message,)
+def relay_kernel(me_ref, far_ref, nearest_ref, sent_ref, relayed_tops, tops):
     blocks, rows, _ = far_ref.shape
-    load_tops(messages, rows, (relayed_ref,), (relayed_tops,))
+    load_tops(far_ref, nearest_ref, relayed_tops, in_middle(me_ref[0]).astype(jnp.float32))
     tops[...] = jnp.zeros_like(tops)
     for step in range(blocks // GROUP):
-        for block, total in add_group(
-            messages, rows, far_ref, (relayed_ref,), (relayed_tops,), step
-        ):
+        for block, total in add_group(far_ref, (nearest_ref,), (relayed_tops,), step):
             top = top_of(total)
             tops[block : block + 1, :] = top
             sent_ref[block * rows : (block + 1) * rows, :] = encode(total * (CODE_TOP / top))
     sent_ref[blocks * rows :, :] = tops[...].astype(jnp.bfloat16)
 
 
-def last_add_kernel(messages, own_ref, *refs):
-    sent_refs, refs = refs[: len(messages)], refs[len(messages) :]
-    act_ref, grad_ref, *tops_refs, sums, sems = refs
-    blocks, rows, _ = own_ref.shape
-    load_tops(messages, rows, sent_refs, tops_refs)
+def last_add_kernel(own_ref, sent_ref, act_ref, grad_ref, tops, sums, sems):
+    load_tops(own_ref, sent_ref, tops)
     copies = []
-    for step in range(blocks // GROUP):
-        for block, total in add_group(messages, rows, own_ref, sent_refs, tops_refs, step):
+    for step in range(own_ref.shape[0] // GROUP):
+        for block, total in add_group(own_ref, (sent_ref,), (tops,), step):
             sums[block] = total
         first = step * GROUP
         ref, at = act_ref, first
@@ -382,33 +386,32 @@
         far = {}
     masks = [*range(len(near)), *far]
 
-    message = bf16(blocks * rows + scale_rows(0, blocks), BLK)
-    whole_range = (0, blocks)
-    coded = {4: [(3, *whole_range), (1, *whole_range)], 2: [(1, *whole_range)], 1: []}[pieces]
-    plain = 2 if pieces == 4 else 1
+    plain = {4: [(0, 0), (1, 2)], 2: [(0, 0)], 1: [(0, 0)]}[pieces]
+    coded = {4: [(3, 1), (3, 3), (2, 2)], 2: [(1, 1)], 1: []}[pieces]
+    message = bf16(blocks * rows + scale_rows(blocks), BLK)
+    tops = pltpu.VMEM((scale_rows(blocks), BLK), jnp.float32)
     act_here, grad_here, *grams = call(
-        functools.partial(gram_kernel, pieces, coded, scale),
+        functools.partial(gram_kernel, pieces, plain, coded, scale),
         [
             bf16(*activations.shape),
             bf16(*gradients.shape),
-            *[f32(blocks, rows, BLK)] * plain,
+            *[f32(blocks, rows, BLK)] * len(plain),
             *[message] * len(coded),
         ],
         "partial_gram", 4 * macs, input_bytes,
         [IN_SMEM, IN_HBM, IN_HBM],
         [
             pltpu.VMEM((GROUP, BLK, BLK), jnp.float32),
-            pltpu.VMEM((scale_rows(0, blocks), BLK), jnp.float32),
+            tops,
             pltpu.SemaphoreType.DMA((blocks // GROUP,)),
         ],
     )(me, in_hbm(activations), in_hbm(gradients))
-    own = grams[0]
-    sent = {message[0]: chunk for message, chunk in zip(coded, grams[plain:])}
+    own, sent = grams[0], grams[len(plain) :]
     if not direct:
         own = lax.psum_scatter(own, "dp", scatter_dimension=1, tiled=True)
     if pieces == 4:
-        middle = lax.ppermute(sent[3], "dp", [(1, 2), (2, 1)])
-        relayed = lax.ppermute(sent[3], "dp", [(0, 1), (3, 2)])
+        nearest = swap(sent[0], "dp", 1)
+        middle = lax.ppermute(sent[1], "dp", [(1, 2), (2, 1)])
 
     parts = [[*near, *far.values()]]
     if halves == 2:
@@ -425,23 +428,25 @@
         )(me, side, act_here, grad_here, *shards, *sums)
         powers.append(power)
     if pieces == 4:
-        sent[2] = call(
-            functools.partial(relay_kernel, coded[0]), message, "relay_chunk", 0, 12 * own.size,
-            [IN_VMEM, IN_VMEM],
-            [pltpu.VMEM((scale_rows(0, blocks), BLK), jnp.float32)] * 2,
-        )(*after([grams[1], relayed], sums))
+        last = call(
+            relay_kernel, message, "relay_chunk", 0, 12 * own.size,
+            [IN_SMEM, IN_VMEM, IN_VMEM], [tops, tops],
+        )(me, *after([grams[1], nearest], sums))
+    elif pieces == 2:
+        last = sent[0]
     sums = share(sums[0], "dp", direct)
     if pieces == 4:
-        sums = after(sums, (middle, sent[2]))
+        sums = after(sums, (middle, last))
     act_eigen, grad_eigen, eigen, totals = call(
         functools.partial(combine_kernel, halves),
         [f32(act_blocks, BLK), f32(grad_blocks, BLK), f32(blocks, BLK), f32(2, BLK)],
         "combine_eigen", 0, 4 * blocks * BLK * pieces, [IN_SMEM] + [IN_VMEM] * len(sums),
     )(side, *sums)
-    arrived = {}
-    sent.pop(3, None)
-    for mask in sent:
-        arrived[mask] = swap(after([sent[mask]], totals)[0], "dp", mask)
+    if pieces == 4:
+        ends = lax.ppermute(after([sent[2]], totals)[0], "dp", [(0, 2), (3, 1)])
+    if pieces > 1:
+        ways = {4: [(0, 1), (3, 2), (1, 3), (2, 0)], 2: [(0, 1), (1, 0)]}[pieces]
+        last = lax.ppermute(after([last], totals)[0], "dp", ways)
     totals = share(totals, "owner", direct)
     weights = call(
         functools.partial(weight_kernel, halves, act_blocks // halves),
@@ -455,31 +460,23 @@
     )(eigen, *powers, *totals)
     weights = share(weights, "owner", direct)
 
-    def tops_of(count):
-        return [pltpu.VMEM((scale_rows(0, blocks), BLK), jnp.float32)] * count
-
     if pieces == 4:
         own = call(
-            functools.partial(add_kernel, [(None, 0, blocks)] * 2),
-            f32(*own.shape), "add_chunks", 0, 16 * own.size, [IN_VMEM] * 3, tops_of(2),
-        )(own, middle, arrived.pop(1))
+            add_kernel, f32(*own.shape), "add_chunks", 0, 20 * own.size,
+            [IN_SMEM] + [IN_VMEM] * 4, [tops] * 3,
+        )(me, own, nearest, middle, ends)
         weights[1:] = after(weights[1:], own)
     token_scores = call(
         score_kernel, f32(1, tokens), "token_scores", 0, 8 * tokens, [IN_VMEM] * len(weights)
     )(*weights)
-    chunks = list(arrived.values())
-    if chunks:
+    if pieces > 1:
         covariance = call(
-            functools.partial(last_add_kernel, [(None, 0, blocks)] * len(chunks)),
+            last_add_kernel,
             [f32(act_blocks, rows, BLK), f32(grad_blocks, rows, BLK)],
-            "add_last_chunk", 0, 12 * own.size, [IN_VMEM] * (1 + len(chunks)),
-            [
-                *tops_of(len(chunks)),
-                pltpu.VMEM(own.shape, jnp.float32),
-                pltpu.SemaphoreType.DMA((blocks // GROUP,)),
-            ],
+            "add_last_chunk", 0, 12 * own.size, [IN_VMEM] * 2,
+            [tops, pltpu.VMEM(own.shape, jnp.float32), pltpu.SemaphoreType.DMA((blocks // GROUP,))],
             out_spec=[pl.BlockSpec(memory_space=pl.ANY)] * 2,
-        )(own, *chunks)
+        )(own, last)
     else:
         covariance = own[:act_blocks], own[act_blocks:]
     return (

time: 49.8 us -> 54.6 us (1.096)
  starting transfers between devices: 22.6 us -> 24.9 us
  waiting for transfers between devices: 13.8 us -> 15.8 us
    ppermute x2 -> x3, waiting for transfers between devices: 0.01 us -> 3.86 us  [the longest x1 3.53 us: local(): last = lax.ppermute(after([last], totals)[0], 'dp', ways)]
    ppermute x16 -> x15, starting transfers between devices: 18.6 us -> 20.7 us  [swap(): return lax.ppermute(value, axis, [(i, i ^ mask) for i in range(count)])]
    ppermute x16 -> x15, waiting for transfers between devices: 13.8 us -> 11.9 us  [swap(): return lax.ppermute(value, axis, [(i, i ^ mask) for i in range(count)])]
    ppermute x2 -> x3, starting transfers between devices: 4 us -> 4.24 us  [the longest x1 3.51 us: local(): ends = lax.ppermute(after([sent[2]], totals)[0], 'dp', [(0, 2), (3, 1)])]
  transfers between devices with their start and end apart: 18 -> 18, of which waited for: 8 -> 10; matrix products, arithmetic and copies ran while one was open for 0% -> 0% of each run, Pallas kernels for 20% -> 19%
where the time goes in v12:
time: 54.6 us; the launch traced here: 54.4 us
  starting transfers between devices  24.9 us (46%)
  waiting for transfers between devices  15.8 us (29%)
  Pallas kernels  13 us (24%)
  between operations  0.75 us (1%)
    ppermute x15, starting transfers between devices, swap(): return lax.ppermute(value, axis, [(i, i ^ mask) for i in range(count)])  20.7 us
    ppermute x15, waiting for transfers between devices, swap(): return lax.ppermute(value, axis, [(i, i ^ mask) for i in range(count)])  11.9 us
    pallas_call x1, Pallas kernels, local(): call(functools.partial(gram_kernel, pieces, plain, coded, scale), [bf16(*...  4.71 us
    ppermute x1, waiting for transfers between devices, local(): last = lax.ppermute(after([last], totals)[0], 'dp', ways)  3.53 us
    ppermute x1, starting transfers between devices, local(): ends = lax.ppermute(after([sent[2]], totals)[0], 'dp', [(0, 2), (3, 1)])  3.51 us
    pallas_call x2, Pallas kernels, local(): call(functools.partial(eigen_kernel, part, halves, masks, pieces, scale),...  1.94 us
    pallas_call x1, Pallas kernels, local(): call(functools.partial(weight_kernel, halves, act_blocks // halves), f32(...  1.49 us
  transfers between devices with their start and end apart: 18, of which 10 were waited for; matrix products, arithmetic and copies ran while one was open for 0% of the time, Pallas kernels for 19%

profile of v12, /device:TPU:0, one launch (start us, length us, event | category | flops | bytes accessed | tf_op | source)
XLA Modules:
  0.0 54.4 jit_solution(15348107219183468922)
XLA Ops:
  0.6 1.1 %pack_basis.1 = (bf16[36,32,128]{2,1,0:T(8,128)(2,1)S(1)}, bf16[18,32,128]{2,1,0:T(8,128)(2,1)S(1)}) custom-call(s32[1]{0:T(128)} %bitcast.1.side_ref, bf16[8,32,128]{2,1,0:T(8,128)(2,1)} %act_ref.1, bf16[28,32,128]{2,1,0:T(8,128)(2,1)} %grad_ref.1), custom_call_target="tpu_custom_call" | custom-call | bytes 294912 | tf_op jit(solution)/shard_map/pack_basis/pallas_call | solution.py:372
  1.7 4.1 %collective-permute-start.5 = (bf16[18,32,128]{2,1,0:T(8,128)(2,1)S(1)}, bf16[18,32,128]{2,1,0:T(8,128)(2,1)S(1)}, u32[]{:S(2)}, u32[]{:S(2)}) collective-permute-start(bf16[18,32,128]{2,1,0:T(8,128)(2,1)S(1)} %get-tuple-element.44), channel_id=1, source_target_pairs={{0,8},{4,12},{8,0},{12,4},{1,9},{5,13},{9,1},{13,5},{2,10},{6,14},... | collective-permute-start | bytes 442376 | tf_op jit(solution)/shard_map/ppermute | solution.py:344
  5.8 1.3 %collective-permute-start.3 = (bf16[18,32,128]{2,1,0:T(8,128)(2,1)S(1)}, bf16[18,32,128]{2,1,0:T(8,128)(2,1)S(1)}, u32[]{:S(2)}, u32[]{:S(2)}) collective-permute-start(bf16[18,32,128]{2,1,0:T(8,128)(2,1)S(1)} %get-tuple-element.44), channel_id=1, source_target_pairs={{0,12},{4,8},{8,4},{12,0},{1,13},{5,9},{9,5},{13,1},{2,14},{6,10},... | collective-permute-start | bytes 442376 | tf_op jit(solution)/shard_map/ppermute | solution.py:344
  7.2 0.2 collective-permute-start.2
  7.4 4.7 %partial_gram.1 = (bf16[512,1024]{1,0:T(8,128)(2,1)S(1)}, bf16[512,3584]{1,0:T(8,128)(2,1)S(1)}, f32[36,32,128]{2,1,0:T(8,128)S(1)}, f32[36,32,128]{2,1,0:T(8,12...) custom-call(s32[1]{0:T(128)} %bitcast.me_ref, ...), custom_call_target="tpu_custom_call" | custom-call | flops 1207959552 | bytes 4718592 | tf_op jit(solution)/shard_map/partial_gram/pallas_call | solution.py:393
  12.1 1.9 %collective-permute-start = (bf16[1200,128]{1,0:T(8,128)(2,1)S(1)}, bf16[1200,128]{1,0:T(8,128)(2,1)S(1)}, u32[]{:S(2)}, u32[]{:S(2)}) collective-permute-start(bf16[1200,128]{1,0:T(8,128)(2,1)S(1)} %get-tuple-element.38), channel_id=1, source_target_pairs={{0,4},{4,0},{8,12},{12,8},{1,5},{5,1},{9,13},{13,9},{2,6},{6,2},{1... | collective-permute-start | bytes 921608 | tf_op jit(solution)/shard_map/ppermute | solution.py:344
  14.0 0.7 %collective-permute-start.1 = (bf16[1200,128]{1,0:T(8,128)(2,1)S(1)}, bf16[1200,128]{1,0:T(8,128)(2,1)S(1)}, u32[]{:S(2)}, u32[]{:S(2)}) collective-permute-start(bf16[1200,128]{1,0:T(8,128)(2,1)S(1)} %get-tuple-element.39), channel_id=1, source_target_pairs={{4,8},{8,4},{5,9},{9,5},{6,10},{10,6},{7,11},{11,7},{20,24},{24,20... | collective-permute-start | bytes 921608 | tf_op jit(solution)/shard_map/ppermute | solution.py:414
  14.7 2.2 %collective-permute-done.5.refs_3_ = bf16[18,32,128]{2,1,0:T(8,128)(2,1)S(1)} collective-permute-done((bf16[18,32,128]{2,1,0:T(8,128)(2,1)S(1)}, bf16[18,32,128]{2,1,0:T(8,128)(2,1)S(1)}, u32[]{:S(2)}, u32[]{:S(2)}) %collective-permute-start.5) | collective-permute-done | bytes 147488 | tf_op jit(solution)/shard_map/ppermute | solution.py:344
  16.9 0.0 collective-permute-done.3.refs_2_
  16.9 1.9 %collective-permute-start.4 = (bf16[18,32,128]{2,1,0:T(8,128)(2,1)S(1)}, bf16[18,32,128]{2,1,0:T(8,128)(2,1)S(1)}, u32[]{:S(2)}, u32[]{:S(2)}) collective-permute-start(bf16[18,32,128]{2,1,0:T(8,128)(2,1)S(1)} %collective-permute-done.3.refs_2_), channel_id=1, source_target_pairs={{0,16},{16,0},{1,17},{17,1},{2,18},{18,2},{3,19},{19,3},{4,20},{20... | collective-permute-start | bytes 442376 | tf_op jit(solution)/shard_map/ppermute | solution.py:344
  18.7 0.2 collective-permute-start.6
  18.9 2.9 %collective-permute-done.2.refs_1_ = bf16[36,32,128]{2,1,0:T(8,128)(2,1)S(1)} collective-permute-done((bf16[36,32,128]{2,1,0:T(8,128)(2,1)S(1)}, bf16[36,32,128]{2,1,0:T(8,128)(2,1)S(1)}, u32[]{:S(2)}, u32[]{:S(2)}) %collective-permute-start.2) | collective-permute-done | bytes 294944 | tf_op jit(solution)/shard_map/ppermute | solution.py:344
  21.8 1.0 %partial_eigen.2 = (f32[9,512,256]{2,1,0:T(8,128)S(1)}, f32[18,128]{1,0:T(8,128)S(1)}) custom-call(s32[1]{0:T(128)} %bitcast.me_ref, s32[1]{0:T(128)} %bitcast.1.side_ref, bf16[512,1024]{1,0:T(8,128)(2,1)S(1)} %get-tuple-element.41.act_ref, bf16[512,3584]{1,0:T(8,128)(2,1)S(1)} %get-tuple-element.42.grad_ref, ...), custom_call_target="tpu_custom_call" | custom-call | flops 301989888 | bytes 2359296 | tf_op jit(solution)/shard_map/partial_eigen/pallas_call | solution.py:422
  22.8 0.0 collective-permute-done.4.refs_2_
  22.8 1.4 %collective-permute-done.6.refs_3_ = bf16[18,32,128]{2,1,0:T(8,128)(2,1)S(1)} collective-permute-done((bf16[18,32,128]{2,1,0:T(8,128)(2,1)S(1)}, bf16[18,32,128]{2,1,0:T(8,128)(2,1)S(1)}, u32[]{:S(2)}, u32[]{:S(2)}) %collective-permute-start.6) | collective-permute-done | bytes 147488 | tf_op jit(solution)/shard_map/ppermute | solution.py:344
  24.2 1.0 %partial_eigen.3 = (f32[9,512,256]{2,1,0:T(8,128)S(1)}, f32[36,128]{1,0:T(8,128)S(1)}) custom-call(s32[1]{0:T(128)} %bitcast.me_ref, s32[1]{0:T(128)} %bitcast.1.side_ref, bf16[512,1024]{1,0:T(8,128)(2,1)S(1)} %get-tuple-element.41.act_ref, bf16[512,3584]{1,0:T(8,128)(2,1)S(1)} %get-tuple-element.42.grad_ref, ...), custom_call_target="tpu_custom_call" | custom-call | flops 301989888 | bytes 2359296 | tf_op jit(solution)/shard_map/partial_eigen/pallas_call | solution.py:422
  25.2 4.3 %collective-permute-start.9 = (f32[36,128]{1,0:T(8,128)S(1)}, f32[36,128]{1,0:T(8,128)S(1)}, u32[]{:S(2)}, u32[]{:S(2)}) collective-permute-start(f32[36,128]{1,0:T(8,128)S(1)} %get-tuple-element.52.refs_0_), channel_id=1, source_target_pairs={{0,12},{4,8},{8,4},{12,0},{1,13},{5,9},{9,5},{13,1},{2,14},{6,10},... | collective-permute-start | bytes 55304 | tf_op jit(solution)/shard_map/ppermute | solution.py:344
  29.5 2.3 %collective-permute-start.8 = (f32[36,128]{1,0:T(8,128)S(1)}, f32[36,128]{1,0:T(8,128)S(1)}, u32[]{:S(2)}, u32[]{:S(2)}) collective-permute-start(f32[36,128]{1,0:T(8,128)S(1)} %get-tuple-element.52.refs_0_), channel_id=1, source_target_pairs={{0,8},{4,12},{8,0},{12,4},{1,9},{5,13},{9,1},{13,5},{2,10},{6,14},... | collective-permute-start | bytes 55304 | tf_op jit(solution)/shard_map/ppermute | solution.py:344
  31.9 0.5 collective-permute-start.7
  32.4 0.0 collective-permute-done.nearest_ref.refs_0_
  32.4 0.6 %relay_chunk.1 = bf16[1200,128]{1,0:T(8,128)(2,1)S(1)} custom-call(s32[1]{0:T(128)} %bitcast.me_ref, f32[36,32,128]{2,1,0:T(8,128)S(1)} %get-tuple-element.50.far_ref, bf16[1200,128]{1,0:T(8,128)(2,1)S(1)} %collective-permute-done.nearest_ref.refs_0_), custom_call_target="tpu_custom_call" | custom-call | bytes 1769472 | tf_op jit(solution)/shard_map/relay_chunk/pallas_call | solution.py:431
  33.0 0.0 collective-permute-done.1.refs_1_
  33.0 0.0 collective-permute-done.9.refs_3_
  33.0 1.5 %collective-permute-done.8.refs_2_ = f32[36,128]{1,0:T(8,128)S(1)} collective-permute-done((f32[36,128]{1,0:T(8,128)S(1)}, f32[36,128]{1,0:T(8,128)S(1)}, u32[]{:S(2)}, u32[]{:S(2)}) %collective-permute-start.8) | collective-permute-done | bytes 18464 | tf_op jit(solution)/shard_map/ppermute | solution.py:344
  34.5 1.2 %collective-permute-done.7.refs_1_ = f32[36,128]{1,0:T(8,128)S(1)} collective-permute-done((f32[36,128]{1,0:T(8,128)S(1)}, f32[36,128]{1,0:T(8,128)S(1)}, u32[]{:S(2)}, u32[]{:S(2)}) %collective-permute-start.7) | collective-permute-done | bytes 18464 | tf_op jit(solution)/shard_map/ppermute | solution.py:344
  35.7 0.6 %combine_eigen.1 = (f32[8,128]{1,0:T(8,128)}, f32[28,128]{1,0:T(8,128)}, f32[36,128]{1,0:T(8,128)S(1)}, f32[2,128]{1,0:T(2,128)S(1)}) custom-call(s32[1]{0:T(128)} %bitcast.1.side_ref, f32[36,128]{1,0:T(8,128)S(1)} %get-tuple-element.52.refs_0_, f32[36,128]{1,0:T(8,128)S(1)} %collective-permute-done.7.refs_1_, f32[36,128]{1,0:T(8,128)S(1)} %collective-permute-done.8.refs_2_, ...), custom_call_target="tpu_custom_call" | custom-call | bytes 73728 | tf_op jit(solution)/shard_map/combine_eigen/pallas_call | solution.py:440
  36.3 3.5 %collective-permute-start.10 = (bf16[1200,128]{1,0:T(8,128)(2,1)S(1)}, bf16[1200,128]{1,0:T(8,128)(2,1)S(1)}, u32[]{:S(2)}, u32[]{:S(2)}) collective-permute-start(bf16[1200,128]{1,0:T(8,128)(2,1)S(1)} %get-tuple-element.57), channel_id=1, source_target_pairs={{0,8},{12,4},{1,9},{13,5},{2,10},{14,6},{3,11},{15,7},{16,24},{28,... | collective-permute-start | bytes 921608 | tf_op jit(solution)/shard_map/ppermute | solution.py:446
  39.8 0.1 collective-permute-start.11
  39.9 0.1 collective-permute-start.14
  40.0 1.6 %collective-permute-start.13 = (f32[2,128]{1,0:T(2,128)S(1)}, f32[2,128]{1,0:T(2,128)S(1)}, u32[]{:S(2)}, u32[]{:S(2)}) collective-permute-start(f32[2,128]{1,0:T(2,128)S(1)} %get-tuple-element.56.refs_2_), channel_id=1, source_target_pairs={{0,2},{1,3},{2,0},{3,1},{4,6},{5,7},{6,4},{7,5},{8,10},{9,11},{10,... | collective-permute-start | bytes 3080 | tf_op jit(solution)/shard_map/ppermute | solution.py:344
  41.5 0.3 collective-permute-start.12
  41.8 1.1 %collective-permute-done.14.refs_5_ = f32[2,128]{1,0:T(2,128)S(1)} collective-permute-done((f32[2,128]{1,0:T(2,128)S(1)}, f32[2,128]{1,0:T(2,128)S(1)}, u32[]{:S(2)}, u32[]{:S(2)}) %collective-permute-start.14) | collective-permute-done | bytes 1056 | tf_op jit(solution)/shard_map/ppermute | solution.py:344
  42.9 0.7 %collective-permute-done.13.refs_4_ = f32[2,128]{1,0:T(2,128)S(1)} collective-permute-done((f32[2,128]{1,0:T(2,128)S(1)}, f32[2,128]{1,0:T(2,128)S(1)}, u32[]{:S(2)}, u32[]{:S(2)}) %collective-permute-start.13) | collective-permute-done | bytes 1056 | tf_op jit(solution)/shard_map/ppermute | solution.py:344
  43.6 0.0 collective-permute-done.12.refs_3_
  43.6 1.5 %partial_weights.1.refs_0_ = f32[2,512]{1,0:T(2,128)S(1)} custom-call(f32[36,128]{1,0:T(8,128)S(1)} %get-tuple-element.63.eigen_ref, f32[9,512,256]{2,1,0:T(8,128)S(1)} %get-tuple-element.64.refs_0_, f32[9,512,256]{2,1,0:T(8,128)S(1)} %get-tuple-element.65.refs_1_, f32[2,128]{1,0:T(2,128)S(1)} %get-tuple-element.56.refs_2_, ...), custom_call_target="tpu_custom_call" | custom-call | bytes 9437184 | tf_op jit(solution)/shard_map/partial_weights/pallas_call | solution.py:451
  45.1 0.6 %collective-permute-start.17 = (f32[2,512]{1,0:T(2,128)S(1)}, f32[2,512]{1,0:T(2,128)S(1)}, u32[]{:S(2)}, u32[]{:S(2)}) collective-permute-start(f32[2,512]{1,0:T(2,128)S(1)} %partial_weights.1.refs_0_), channel_id=1, source_target_pairs={{0,3},{1,2},{2,1},{3,0},{4,7},{5,6},{6,5},{7,4},{8,11},{9,10},{10,... | collective-permute-start | bytes 12296 | tf_op jit(solution)/shard_map/ppermute | solution.py:344
  45.7 1.5 %collective-permute-start.16 = (f32[2,512]{1,0:T(2,128)S(1)}, f32[2,512]{1,0:T(2,128)S(1)}, u32[]{:S(2)}, u32[]{:S(2)}) collective-permute-start(f32[2,512]{1,0:T(2,128)S(1)} %partial_weights.1.refs_0_), channel_id=1, source_target_pairs={{0,2},{1,3},{2,0},{3,1},{4,6},{5,7},{6,4},{7,5},{8,10},{9,11},{10,... | collective-permute-start | bytes 12296 | tf_op jit(solution)/shard_map/ppermute | solution.py:344
  47.1 0.0 collective-permute-start.15
  47.1 0.3 collective-permute-done.10.refs_2_
  47.4 0.9 %add_chunks.1.own_ref = f32[36,32,128]{2,1,0:T(8,128)S(1)} custom-call(s32[1]{0:T(128)} %bitcast.me_ref, f32[36,32,128]{2,1,0:T(8,128)S(1)} %get-tuple-element.37.own_ref, bf16[1200,128]{1,0:T(8,128)(2,1)S(1)} %collective-permute-done.nearest_ref.refs_0_, bf16[1200,128]{1,0:T(8,128)(2,1)S(1)} %collective-permute-done.1.refs_1_, ...), custom_call_target="tpu_custom_call" | custom-call | bytes 2949120 | tf_op jit(solution)/shard_map/add_chunks/pallas_call | solution.py:464
  48.4 0.0 collective-permute-done.17.refs_3_
  48.4 0.9 %collective-permute-done.16.refs_2_ = f32[2,512]{1,0:T(2,128)S(1)} collective-permute-done((f32[2,512]{1,0:T(2,128)S(1)}, f32[2,512]{1,0:T(2,128)S(1)}, u32[]{:S(2)}, u32[]{:S(2)}) %collective-permute-start.16) | collective-permute-done | bytes 4128 | tf_op jit(solution)/shard_map/ppermute | solution.py:344
  49.3 0.0 collective-permute-done.15.refs_1_
  49.3 0.6 %token_scores.1 = f32[1,512]{1,0:T(1,128)} custom-call(f32[2,512]{1,0:T(2,128)S(1)} %partial_weights.1.refs_0_, f32[2,512]{1,0:T(2,128)S(1)} %collective-permute-done.15.refs_1_, f32[2,512]{1,0:T(2,128)S(1)} %collective-permute-done.16.refs_2_, f32[2,512]{1,0:T(2,128)S(1)} %collective-permute-done.17.refs_3_), custom_call_target="tpu_custom_call" | custom-call | bytes 4096 | tf_op jit(solution)/shard_map/token_scores/pallas_call | solution.py:469
  49.9 3.5 %collective-permute-done.11.sent_ref = bf16[1200,128]{1,0:T(8,128)(2,1)S(1)} collective-permute-done((bf16[1200,128]{1,0:T(8,128)(2,1)S(1)}, bf16[1200,128]{1,0:T(8,128)(2,1)S(1)}, u32[]{:S(2)}, u32[]{:S(2)}) %collective-permute-start.11) | collective-permute-done | bytes 307232 | tf_op jit(solution)/shard_map/ppermute | solution.py:449
  53.4 1.0 %add_last_chunk.1 = (f32[8,32,128]{2,1,0:T(8,128)}, f32[28,32,128]{2,1,0:T(8,128)}) custom-call(f32[36,32,128]{2,1,0:T(8,128)S(1)} %add_chunks.1.own_ref, bf16[1200,128]{1,0:T(8,128)(2,1)S(1)} %collective-permute-done.11.sent_ref), custom_call_target="tpu_custom_call" | custom-call | bytes 1769472 | tf_op jit(solution)/shard_map/add_last_chunk/pallas_call | solution.py:473
Async XLA Ops:
  1.7 15.1 %collective-permute-start.5 = (bf16[18,32,128]{2,1,0:T(8,128)(2,1)S(1)}, bf16[18,32,128]{2,1,0:T(8,128)(2,1)S(1)}, u32[]{:S(2)}, u32[]{:S(2)}) collective-permute-start(bf16[18,32,128]{2,1,0:T(8,128)(2,1)S(1)} %get-tuple-element.44), channel_id=1, source_target_pairs={{0,8},{4,12},{8,0},{12,4},{1,9},{5,13},{9,1},{13,5},{2,10},{6,14},... | collective-permute-start | bytes 442376 | tf_op jit(solution)/shard_map/ppermute | solution.py:344
  5.8 11.0 %collective-permute-start.3 = (bf16[18,32,128]{2,1,0:T(8,128)(2,1)S(1)}, bf16[18,32,128]{2,1,0:T(8,128)(2,1)S(1)}, u32[]{:S(2)}, u32[]{:S(2)}) collective-permute-start(bf16[18,32,128]{2,1,0:T(8,128)(2,1)S(1)} %get-tuple-element.44), channel_id=1, source_target_pairs={{0,12},{4,8},{8,4},{12,0},{1,13},{5,9},{9,5},{13,1},{2,14},{6,10},... | collective-permute-start | bytes 442376 | tf_op jit(solution)/shard_map/ppermute | solution.py:344
  7.2 14.7 %collective-permute-start.2 = (bf16[36,32,128]{2,1,0:T(8,128)(2,1)S(1)}, bf16[36,32,128]{2,1,0:T(8,128)(2,1)S(1)}, u32[]{:S(2)}, u32[]{:S(2)}) collective-permute-start(bf16[36,32,128]{2,1,0:T(8,128)(2,1)S(1)} %get-tuple-element.43.refs_0_), channel_id=1, source_target_pairs={{0,4},{4,0},{8,12},{12,8},{1,5},{5,1},{9,13},{13,9},{2,6},{6,2},{1... | collective-permute-start | bytes 884744 | tf_op jit(solution)/shard_map/ppermute | solution.py:344
  12.1 20.3 %collective-permute-start = (bf16[1200,128]{1,0:T(8,128)(2,1)S(1)}, bf16[1200,128]{1,0:T(8,128)(2,1)S(1)}, u32[]{:S(2)}, u32[]{:S(2)}) collective-permute-start(bf16[1200,128]{1,0:T(8,128)(2,1)S(1)} %get-tuple-element.38), channel_id=1, source_target_pairs={{0,4},{4,0},{8,12},{12,8},{1,5},{5,1},{9,13},{13,9},{2,6},{6,2},{1... | collective-permute-start | bytes 921608 | tf_op jit(solution)/shard_map/ppermute | solution.py:344
  14.0 19.0 %collective-permute-start.1 = (bf16[1200,128]{1,0:T(8,128)(2,1)S(1)}, bf16[1200,128]{1,0:T(8,128)(2,1)S(1)}, u32[]{:S(2)}, u32[]{:S(2)}) collective-permute-start(bf16[1200,128]{1,0:T(8,128)(2,1)S(1)} %get-tuple-element.39), channel_id=1, source_target_pairs={{4,8},{8,4},{5,9},{9,5},{6,10},{10,6},{7,11},{11,7},{20,24},{24,20... | collective-permute-start | bytes 921608 | tf_op jit(solution)/shard_map/ppermute | solution.py:414
  16.9 5.9 %collective-permute-start.4 = (bf16[18,32,128]{2,1,0:T(8,128)(2,1)S(1)}, bf16[18,32,128]{2,1,0:T(8,128)(2,1)S(1)}, u32[]{:S(2)}, u32[]{:S(2)}) collective-permute-start(bf16[18,32,128]{2,1,0:T(8,128)(2,1)S(1)} %collective-permute-done.3.refs_2_), channel_id=1, source_target_pairs={{0,16},{16,0},{1,17},{17,1},{2,18},{18,2},{3,19},{19,3},{4,20},{20... | collective-permute-start | bytes 442376 | tf_op jit(solution)/shard_map/ppermute | solution.py:344
  18.7 5.5 %collective-permute-start.6 = (bf16[18,32,128]{2,1,0:T(8,128)(2,1)S(1)}, bf16[18,32,128]{2,1,0:T(8,128)(2,1)S(1)}, u32[]{:S(2)}, u32[]{:S(2)}) collective-permute-start(bf16[18,32,128]{2,1,0:T(8,128)(2,1)S(1)} %collective-permute-done.5.refs_3_), channel_id=1, source_target_pairs={{0,16},{16,0},{1,17},{17,1},{2,18},{18,2},{3,19},{19,3},{4,20},{20... | collective-permute-start | bytes 442376 | tf_op jit(solution)/shard_map/ppermute | solution.py:344
  25.2 7.8 %collective-permute-start.9 = (f32[36,128]{1,0:T(8,128)S(1)}, f32[36,128]{1,0:T(8,128)S(1)}, u32[]{:S(2)}, u32[]{:S(2)}) collective-permute-start(f32[36,128]{1,0:T(8,128)S(1)} %get-tuple-element.52.refs_0_), channel_id=1, source_target_pairs={{0,12},{4,8},{8,4},{12,0},{1,13},{5,9},{9,5},{13,1},{2,14},{6,10},... | collective-permute-start | bytes 55304 | tf_op jit(solution)/shard_map/ppermute | solution.py:344
  29.5 4.9 %collective-permute-start.8 = (f32[36,128]{1,0:T(8,128)S(1)}, f32[36,128]{1,0:T(8,128)S(1)}, u32[]{:S(2)}, u32[]{:S(2)}) collective-permute-start(f32[36,128]{1,0:T(8,128)S(1)} %get-tuple-element.52.refs_0_), channel_id=1, source_target_pairs={{0,8},{4,12},{8,0},{12,4},{1,9},{5,13},{9,1},{13,5},{2,10},{6,14},... | collective-permute-start | bytes 55304 | tf_op jit(solution)/shard_map/ppermute | solution.py:344
  31.9 3.8 %collective-permute-start.7 = (f32[36,128]{1,0:T(8,128)S(1)}, f32[36,128]{1,0:T(8,128)S(1)}, u32[]{:S(2)}, u32[]{:S(2)}) collective-permute-start(f32[36,128]{1,0:T(8,128)S(1)} %get-tuple-element.52.refs_0_), channel_id=1, source_target_pairs={{0,4},{4,0},{8,12},{12,8},{1,5},{5,1},{9,13},{13,9},{2,6},{6,2},{1... | collective-permute-start | bytes 55304 | tf_op jit(solution)/shard_map/ppermute | solution.py:344
  36.3 11.1 %collective-permute-start.10 = (bf16[1200,128]{1,0:T(8,128)(2,1)S(1)}, bf16[1200,128]{1,0:T(8,128)(2,1)S(1)}, u32[]{:S(2)}, u32[]{:S(2)}) collective-permute-start(bf16[1200,128]{1,0:T(8,128)(2,1)S(1)} %get-tuple-element.57), channel_id=1, source_target_pairs={{0,8},{12,4},{1,9},{13,5},{2,10},{14,6},{3,11},{15,7},{16,24},{28,... | collective-permute-start | bytes 921608 | tf_op jit(solution)/shard_map/ppermute | solution.py:446
  39.8 13.6 %collective-permute-start.11 = (bf16[1200,128]{1,0:T(8,128)(2,1)S(1)}, bf16[1200,128]{1,0:T(8,128)(2,1)S(1)}, u32[]{:S(2)}, u32[]{:S(2)}) collective-permute-start(bf16[1200,128]{1,0:T(8,128)(2,1)S(1)} %relay_chunk.1), channel_id=1, source_target_pairs={{0,4},{12,8},{4,12},{8,0},{1,5},{13,9},{5,13},{9,1},{2,6},{14,10},... | collective-permute-start | bytes 921608 | tf_op jit(solution)/shard_map/ppermute | solution.py:449
  39.9 3.1 %collective-permute-start.14 = (f32[2,128]{1,0:T(2,128)S(1)}, f32[2,128]{1,0:T(2,128)S(1)}, u32[]{:S(2)}, u32[]{:S(2)}) collective-permute-start(f32[2,128]{1,0:T(2,128)S(1)} %get-tuple-element.56.refs_2_), channel_id=1, source_target_pairs={{0,3},{1,2},{2,1},{3,0},{4,7},{5,6},{6,5},{7,4},{8,11},{9,10},{10,... | collective-permute-start | bytes 3080 | tf_op jit(solution)/shard_map/ppermute | solution.py:344
  40.0 3.6 %collective-permute-start.13 = (f32[2,128]{1,0:T(2,128)S(1)}, f32[2,128]{1,0:T(2,128)S(1)}, u32[]{:S(2)}, u32[]{:S(2)}) collective-permute-start(f32[2,128]{1,0:T(2,128)S(1)} %get-tuple-element.56.refs_2_), channel_id=1, source_target_pairs={{0,2},{1,3},{2,0},{3,1},{4,6},{5,7},{6,4},{7,5},{8,10},{9,11},{10,... | collective-permute-start | bytes 3080 | tf_op jit(solution)/shard_map/ppermute | solution.py:344
  41.5 2.1 %collective-permute-start.12 = (f32[2,128]{1,0:T(2,128)S(1)}, f32[2,128]{1,0:T(2,128)S(1)}, u32[]{:S(2)}, u32[]{:S(2)}) collective-permute-start(f32[2,128]{1,0:T(2,128)S(1)} %get-tuple-element.56.refs_2_), channel_id=1, source_target_pairs={{0,1},{1,0},{2,3},{3,2},{4,5},{5,4},{6,7},{7,6},{8,9},{9,8},{10,11... | collective-permute-start | bytes 3080 | tf_op jit(solution)/shard_map/ppermute | solution.py:344
  45.1 3.3 %collective-permute-start.17 = (f32[2,512]{1,0:T(2,128)S(1)}, f32[2,512]{1,0:T(2,128)S(1)}, u32[]{:S(2)}, u32[]{:S(2)}) collective-permute-start(f32[2,512]{1,0:T(2,128)S(1)} %partial_weights.1.refs_0_), channel_id=1, source_target_pairs={{0,3},{1,2},{2,1},{3,0},{4,7},{5,6},{6,5},{7,4},{8,11},{9,10},{10,... | collective-permute-start | bytes 12296 | tf_op jit(solution)/shard_map/ppermute | solution.py:344
  45.7 3.6 %collective-permute-start.16 = (f32[2,512]{1,0:T(2,128)S(1)}, f32[2,512]{1,0:T(2,128)S(1)}, u32[]{:S(2)}, u32[]{:S(2)}) collective-permute-start(f32[2,512]{1,0:T(2,128)S(1)} %partial_weights.1.refs_0_), channel_id=1, source_target_pairs={{0,2},{1,3},{2,0},{3,1},{4,6},{5,7},{6,4},{7,5},{8,10},{9,11},{10,... | collective-permute-start | bytes 12296 | tf_op jit(solution)/shard_map/ppermute | solution.py:344
  47.1 2.2 %collective-permute-start.15 = (f32[2,512]{1,0:T(2,128)S(1)}, f32[2,512]{1,0:T(2,128)S(1)}, u32[]{:S(2)}, u32[]{:S(2)}) collective-permute-start(f32[2,512]{1,0:T(2,128)S(1)} %partial_weights.1.refs_0_), channel_id=1, source_target_pairs={{0,1},{1,0},{2,3},{3,2},{4,5},{5,4},{6,7},{7,6},{8,9},{9,8},{10,11... | collective-permute-start | bytes 12296 | tf_op jit(solution)/shard_map/ppermute | solution.py:344

commit v13 on v8

--- a/solution.py
+++ b/solution.py
@@ -167,8 +167,10 @@
         tops[...] = sent_ref[(end - first) * rows :, :].astype(jnp.float32) * (1.0 / CODE_TOP)
 
 
-def add_kernel(messages, own_ref, *refs):
-    sent_refs, sum_ref, tops_refs = refs[: len(messages)], refs[len(messages)], refs[len(messages) + 1 :]
+def add_kernel(messages, halves, side_ref, eigen_ref, own_ref, *refs):
+    sent_refs, refs = refs[: len(messages)], refs[len(messages) :]
+    sum_ref, act_eigen_ref, grad_eigen_ref, *tops_refs = refs
+    order_kernel(halves, side_ref, eigen_ref, act_eigen_ref, grad_eigen_ref)
     blocks, rows, _ = own_ref.shape
     load_tops(messages, rows, sent_refs, tops_refs)
     for step in range(blocks // GROUP):
@@ -194,10 +196,12 @@
 def last_add_kernel(messages, owners, own_ref, *refs):
     sent_refs, refs = refs[: len(messages)], refs[len(messages) :]
     weight_refs, refs = refs[:owners], refs[owners:]
-    act_ref, grad_ref, score_ref, *tops_refs, sums, sems = refs
+    act_ref, grad_ref, score_ref, *tops_refs, sums, scores, sems = refs
     blocks, rows, _ = own_ref.shape
+    score_kernel(*weight_refs, scores)
+    copies = [pltpu.make_async_copy(scores, score_ref, sems.at[blocks // GROUP])]
+    copies[0].start()
     load_tops(messages, rows, sent_refs, tops_refs)
-    copies = []
     for step in range(blocks // GROUP):
         for block, total in add_group(messages, rows, own_ref, sent_refs, tops_refs, step):
             sums[block] = total
@@ -211,7 +215,6 @@
             )
         )
         copies[-1].start()
-    score_kernel(weight_refs, score_ref)
     for copy in copies:
         copy.wait()
 
@@ -265,27 +268,34 @@
         sums_ref[row + 1 : row + 2, :] = sums[:, BLK:]
 
 
-def combine_kernel(halves, side_ref, *refs):
-    *sums_refs, act_eigen_ref, grad_eigen_ref, eigen_ref, total_ref = refs
-    side = side_ref[0]
-    act_half, grad_half = act_eigen_ref.shape[0] // halves, grad_eigen_ref.shape[0] // halves
+def combine_kernel(halves, act_half, *refs):
+    *sums_refs, eigen_ref, total_ref = refs
     eigen = sums_refs[0][...]
     for sums_ref in sums_refs[1:]:
         eigen = eigen + sums_ref[...]
     eigen_ref[...] = eigen
+    blocks_half = eigen.shape[0] // halves
     act_total = jnp.zeros((1, BLK), jnp.float32)
     grad_total = jnp.zeros((1, BLK), jnp.float32)
     for part in range(halves):
+        first = part * blocks_half
+        act_total += jnp.sum(eigen[first : first + act_half], axis=0, keepdims=True)
+        grad_total += jnp.sum(eigen[first + act_half : first + blocks_half], axis=0, keepdims=True)
+    total_ref[0:1, :] = act_total
+    total_ref[1:2, :] = grad_total
+
+
+def order_kernel(halves, side_ref, eigen_ref, act_eigen_ref, grad_eigen_ref):
+    side = side_ref[0]
+    act_half, grad_half = act_eigen_ref.shape[0] // halves, grad_eigen_ref.shape[0] // halves
+    for part in range(halves):
         half = lax.rem(side + part, halves)
         first = part * (act_half + grad_half)
-        act = eigen[first : first + act_half]
-        grad = eigen[first + act_half : first + act_half + grad_half]
-        act_total += jnp.sum(act, axis=0, keepdims=True)
-        grad_total += jnp.sum(grad, axis=0, keepdims=True)
-        act_eigen_ref[pl.ds(half * act_half, act_half), :] = act
-        grad_eigen_ref[pl.ds(half * grad_half, grad_half), :] = grad
-    total_ref[0:1, :] = act_total
-    total_ref[1:2, :] = grad_total
+        middle = first + act_half
+        act_eigen_ref[pl.ds(half * act_half, act_half), :] = eigen_ref[first:middle]
+        grad_eigen_ref[pl.ds(half * grad_half, grad_half), :] = eigen_ref[
+            middle : middle + grad_half
+        ]
 
 
 def weight_kernel(halves, act_half, eigen_ref, *refs):
@@ -329,7 +339,8 @@
         weight_ref[index : index + 1, :] = sums[0:1]
 
 
-def score_kernel(weight_refs, score_ref):
+def score_kernel(*refs):
+    *weight_refs, score_ref = refs
     weights = weight_refs[0][...]
     for weight_ref in weight_refs[1:]:
         weights = weights + weight_ref[...]
@@ -344,7 +355,7 @@
 def share(value, axis, direct):
     if not direct:
         return [lax.psum(value, axis)]
-    return [value] + [swap(value, axis, mask) for mask in range(1, lax.axis_size(axis))]
+    return [value] + [swap(value, axis, mask) for mask in reversed(range(1, lax.axis_size(axis)))]
 
 
 def after(values, done):
@@ -434,16 +445,16 @@
     sums = share(sums[0], "dp", direct)
     if pieces == 4:
         sums = after(sums, (middle, sent[2]))
-    act_eigen, grad_eigen, eigen, totals = call(
-        functools.partial(combine_kernel, halves),
-        [f32(act_blocks, BLK), f32(grad_blocks, BLK), f32(blocks, BLK), f32(2, BLK)],
-        "combine_eigen", 0, 4 * blocks * BLK * pieces, [IN_SMEM] + [IN_VMEM] * len(sums),
-    )(side, *sums)
+    eigen, totals = call(
+        functools.partial(combine_kernel, halves, act_blocks // halves),
+        [f32(blocks, BLK), f32(2, BLK)],
+        "combine_eigen", 0, 4 * blocks * BLK * pieces, [IN_VMEM] * len(sums),
+    )(*sums)
     arrived = {}
     sent.pop(3, None)
+    for mask in sent:
+        arrived[mask] = swap(after([sent[mask]], totals)[0], "dp", mask)
     totals = share(totals, "owner", direct)
-    for mask in sent:
-        arrived[mask] = swap(after([sent[mask]], totals[:2])[0], "dp", mask)
     weights = call(
         functools.partial(weight_kernel, halves, act_blocks // halves),
         f32(2, tokens), "partial_weights", 0, 4 * tokens * blocks * BLK,
@@ -459,36 +470,41 @@
     def tops_of(count):
         return [pltpu.VMEM((scale_rows(0, blocks), BLK), jnp.float32)] * count
 
+    eigens = [f32(act_blocks, BLK), f32(grad_blocks, BLK)]
     if pieces == 4:
-        own = call(
-            functools.partial(add_kernel, [(None, 0, blocks)] * 2),
-            f32(*own.shape), "add_chunks", 0, 16 * own.size, [IN_VMEM] * 3, tops_of(2),
-        )(own, middle, arrived.pop(1))
+        own, *eigens = call(
+            functools.partial(add_kernel, [(None, 0, blocks)], halves),
+            [f32(*own.shape), *eigens], "add_chunk", 0, 12 * own.size,
+            [IN_SMEM] + [IN_VMEM] * 3, tops_of(1),
+        )(side, eigen, own, middle)
         weights[1:] = after(weights[1:], own)
-    chunks = list(arrived.values())
+    else:
+        eigens = call(
+            functools.partial(order_kernel, halves), eigens, "order_eigen", 0,
+            8 * blocks * BLK, [IN_SMEM, IN_VMEM],
+        )(side, eigen)
+    chunks = list(arrived.values())[::-1]
     if chunks:
-        anywhere = pl.BlockSpec(memory_space=pl.ANY)
         *covariance, token_scores = call(
             functools.partial(last_add_kernel, [(None, 0, blocks)] * len(chunks), len(weights)),
             [f32(act_blocks, rows, BLK), f32(grad_blocks, rows, BLK), f32(1, tokens)],
-            "last_sums", 0, 12 * own.size, [IN_VMEM] * (1 + len(chunks) + len(weights)),
+            "last_sums", 0, 16 * own.size, [IN_VMEM] * (1 + len(chunks) + len(weights)),
             [
                 *tops_of(len(chunks)),
                 pltpu.VMEM(own.shape, jnp.float32),
-                pltpu.SemaphoreType.DMA((blocks // GROUP,)),
+                pltpu.VMEM((1, tokens), jnp.float32),
+                pltpu.SemaphoreType.DMA((blocks // GROUP + 1,)),
             ],
-            out_spec=[anywhere, anywhere, IN_VMEM],
+            out_spec=[pl.BlockSpec(memory_space=pl.ANY)] * 3,
         )(own, *chunks, *weights)
     else:
         covariance = own[:act_blocks], own[act_blocks:]
         token_scores = call(
-            lambda *refs: score_kernel(refs[:-1], refs[-1]),
-            f32(1, tokens), "token_scores", 0, 8 * tokens, [IN_VMEM] * len(weights),
+            score_kernel, f32(1, tokens), "token_scores", 0, 8 * tokens, [IN_VMEM] * len(weights)
         )(*weights)
     return (
         *covariance,
-        act_eigen.reshape(-1),
-        grad_eigen.reshape(-1),
+        *[eigen.reshape(-1) for eigen in eigens],
         token_scores.reshape(-1),
     )
 

time: 55.8 us -> 48.5 us (0.87)
  waiting for transfers between devices: 19.9 us -> 12.3 us
  starting transfers between devices: 22.4 us -> 23.7 us
  Pallas kernels: 12.5 us -> 11.6 us
    ppermute x16, waiting for transfers between devices: 19.9 us -> 12.3 us  [swap(): return lax.ppermute(value, axis, [(i, i ^ mask) for i in range(count)])]
    ppermute x16, starting transfers between devices: 18.4 us -> 19.7 us  [swap(): return lax.ppermute(value, axis, [(i, i ^ mask) for i in range(count)])]
    pallas_call x2, Pallas kernels: 1.25 us -> 0.64 us  [the longest x1 0.62 us: local(): call(functools.partial(add_kernel, [(None, 0, blocks)], halves), [f32(*ow...]
  transfers between devices with their start and end apart: 18 -> 18, of which waited for: 9 -> 9; matrix products, arithmetic and copies ran while one was open for 0% -> 0% of each run, Pallas kernels for 17% -> 19%
where the time goes in v13:
time: 48.5 us; the launch traced here: 48.3 us
  starting transfers between devices  23.7 us (49%)
  waiting for transfers between devices  12.3 us (25%)
  Pallas kernels  11.6 us (24%)
  between operations  0.73 us (2%)
    ppermute x16, starting transfers between devices, swap(): return lax.ppermute(value, axis, [(i, i ^ mask) for i in range(count)])  19.7 us
    ppermute x16, waiting for transfers between devices, swap(): return lax.ppermute(value, axis, [(i, i ^ mask) for i in range(count)])  12.3 us
    pallas_call x1, Pallas kernels, local(): call(functools.partial(gram_kernel, pieces, coded, scale), [bf16(*activat...  4.56 us
    ppermute x1, starting transfers between devices, local(): relayed = lax.ppermute(sent[3], 'dp', [(0, 1), (3, 2)])  3.32 us
    pallas_call x2, Pallas kernels, local(): call(functools.partial(eigen_kernel, part, halves, masks, pieces, scale),...  1.95 us
    pallas_call x1, Pallas kernels, local(): call(functools.partial(weight_kernel, halves, act_blocks // halves), f32(...  1.49 us
    pallas_call x1, Pallas kernels, local(): call(functools.partial(last_add_kernel, [(None, 0, blocks)] * len(chunks)...  1.35 us
    pallas_call x1, Pallas kernels, local(): call(pack_kernel, [bf16(blocks // part, rows, BLK) for part in range(1, h...  1.08 us
  transfers between devices with their start and end apart: 18, of which 9 were waited for; matrix products, arithmetic and copies ran while one was open for 0% of the time, Pallas kernels for 19%

profile of v13, /device:TPU:0, one launch (start us, length us, event | category | flops | bytes accessed | tf_op | source)
XLA Modules:
  0.0 48.3 jit_solution(7351595704833170314)
XLA Ops:
  0.6 1.1 %pack_basis.1 = (bf16[36,32,128]{2,1,0:T(8,128)(2,1)S(1)}, bf16[18,32,128]{2,1,0:T(8,128)(2,1)S(1)}) custom-call(s32[1]{0:T(128)} %bitcast.side_ref, bf16[8,32,128]{2,1,0:T(8,128)(2,1)} %act_ref.1, bf16[28,32,128]{2,1,0:T(8,128)(2,1)} %grad_ref.1), custom_call_target="tpu_custom_call" | custom-call | bytes 294912 | tf_op jit(solution)/shard_map/pack_basis/pallas_call | solution.py:380
  1.7 5.1 %collective-permute-start.1 = (bf16[18,32,128]{2,1,0:T(8,128)(2,1)S(1)}, bf16[18,32,128]{2,1,0:T(8,128)(2,1)S(1)}, u32[]{:S(2)}, u32[]{:S(2)}) collective-permute-start(bf16[18,32,128]{2,1,0:T(8,128)(2,1)S(1)} %get-tuple-element.41), channel_id=1, source_target_pairs={{0,12},{4,8},{8,4},{12,0},{1,13},{5,9},{9,5},{13,1},{2,14},{6,10},... | collective-permute-start | bytes 442376 | tf_op jit(solution)/shard_map/ppermute | solution.py:352
  6.8 0.0 collective-permute-start.3
  6.8 0.6 %collective-permute-start = (bf16[36,32,128]{2,1,0:T(8,128)(2,1)S(1)}, bf16[36,32,128]{2,1,0:T(8,128)(2,1)S(1)}, u32[]{:S(2)}, u32[]{:S(2)}) collective-permute-start(bf16[36,32,128]{2,1,0:T(8,128)(2,1)S(1)} %get-tuple-element.40.refs_0_), channel_id=1, source_target_pairs={{0,4},{4,0},{8,12},{12,8},{1,5},{5,1},{9,13},{13,9},{2,6},{6,2},{1... | collective-permute-start | bytes 884744 | tf_op jit(solution)/shard_map/ppermute | solution.py:352
  7.5 4.6 %partial_gram.1 = (bf16[512,1024]{1,0:T(8,128)(2,1)S(1)}, bf16[512,3584]{1,0:T(8,128)(2,1)S(1)}, f32[36,32,128]{2,1,0:T(8,128)S(1)}, f32[36,32,128]{2,1,0:T(8,12...) custom-call(s32[1]{0:T(128)} %bitcast.1.me_ref, bf16[512,1024]{1,0:T(8,128)(2,1)} %act_hbm.1, ...), custom_call_target="tpu_custom_call" | custom-call | flops 1207959552 | bytes 4718592 | tf_op jit(solution)/shard_map/partial_gram/pallas_call | solution.py:401
  12.0 3.3 %collective-permute-start.9 = (bf16[1200,128]{1,0:T(8,128)(2,1)S(1)}, bf16[1200,128]{1,0:T(8,128)(2,1)S(1)}, u32[]{:S(2)}, u32[]{:S(2)}) collective-permute-start(bf16[1200,128]{1,0:T(8,128)(2,1)S(1)} %get-tuple-element.47), channel_id=1, source_target_pairs={{0,4},{12,8},{1,5},{13,9},{2,6},{14,10},{3,7},{15,11},{16,20},{28,... | collective-permute-start | bytes 921608 | tf_op jit(solution)/shard_map/ppermute | solution.py:423
  15.4 0.7 %collective-permute-start.8 = (bf16[1200,128]{1,0:T(8,128)(2,1)S(1)}, bf16[1200,128]{1,0:T(8,128)(2,1)S(1)}, u32[]{:S(2)}, u32[]{:S(2)}) collective-permute-start(bf16[1200,128]{1,0:T(8,128)(2,1)S(1)} %get-tuple-element.47), channel_id=1, source_target_pairs={{4,8},{8,4},{5,9},{9,5},{6,10},{10,6},{7,11},{11,7},{20,24},{24,20... | collective-permute-start | bytes 921608 | tf_op jit(solution)/shard_map/ppermute | solution.py:422
  16.1 0.0 collective-permute-done.1.refs_2_
  16.1 1.6 %collective-permute-start.2 = (bf16[18,32,128]{2,1,0:T(8,128)(2,1)S(1)}, bf16[18,32,128]{2,1,0:T(8,128)(2,1)S(1)}, u32[]{:S(2)}, u32[]{:S(2)}) collective-permute-start(bf16[18,32,128]{2,1,0:T(8,128)(2,1)S(1)} %collective-permute-done.1.refs_2_), channel_id=1, source_target_pairs={{0,16},{16,0},{1,17},{17,1},{2,18},{18,2},{3,19},{19,3},{4,20},{20... | collective-permute-start | bytes 442376 | tf_op jit(solution)/shard_map/ppermute | solution.py:352
  17.6 2.7 %collective-permute-done.3.refs_3_ = bf16[18,32,128]{2,1,0:T(8,128)(2,1)S(1)} collective-permute-done((bf16[18,32,128]{2,1,0:T(8,128)(2,1)S(1)}, bf16[18,32,128]{2,1,0:T(8,128)(2,1)S(1)}, u32[]{:S(2)}, u32[]{:S(2)}) %collective-permute-start.3) | collective-permute-done | bytes 147488 | tf_op jit(solution)/shard_map/ppermute | solution.py:352
  20.3 1.5 %collective-permute-start.4 = (bf16[18,32,128]{2,1,0:T(8,128)(2,1)S(1)}, bf16[18,32,128]{2,1,0:T(8,128)(2,1)S(1)}, u32[]{:S(2)}, u32[]{:S(2)}) collective-permute-start(bf16[18,32,128]{2,1,0:T(8,128)(2,1)S(1)} %collective-permute-done.3.refs_3_), channel_id=1, source_target_pairs={{0,16},{16,0},{1,17},{17,1},{2,18},{18,2},{3,19},{19,3},{4,20},{20... | collective-permute-start | bytes 442376 | tf_op jit(solution)/shard_map/ppermute | solution.py:352
  21.8 0.0 collective-permute-done.refs_1_
  21.8 1.0 %partial_eigen.2 = (f32[9,512,256]{2,1,0:T(8,128)S(1)}, f32[18,128]{1,0:T(8,128)S(1)}) custom-call(s32[1]{0:T(128)} %bitcast.1.me_ref, s32[1]{0:T(128)} %bitcast.side_ref, bf16[512,1024]{1,0:T(8,128)(2,1)S(1)} %get-tuple-element.38.act_ref, bf16[512,3584]{1,0:T(8,128)(2,1)S(1)} %get-tuple-element.39.grad_ref, ...), custom_call_target="tpu_custom_call" | custom-call | flops 301989888 | bytes 2359296 | tf_op jit(solution)/shard_map/partial_eigen/pallas_call | solution.py:431
  22.8 0.0 collective-permute-done.2.refs_2_
  22.8 2.6 %collective-permute-done.4.refs_3_ = bf16[18,32,128]{2,1,0:T(8,128)(2,1)S(1)} collective-permute-done((bf16[18,32,128]{2,1,0:T(8,128)(2,1)S(1)}, bf16[18,32,128]{2,1,0:T(8,128)(2,1)S(1)}, u32[]{:S(2)}, u32[]{:S(2)}) %collective-permute-start.4) | collective-permute-done | bytes 147488 | tf_op jit(solution)/shard_map/ppermute | solution.py:352
  25.5 1.0 %partial_eigen.3 = (f32[9,512,256]{2,1,0:T(8,128)S(1)}, f32[36,128]{1,0:T(8,128)S(1)}) custom-call(s32[1]{0:T(128)} %bitcast.1.me_ref, s32[1]{0:T(128)} %bitcast.side_ref, bf16[512,1024]{1,0:T(8,128)(2,1)S(1)} %get-tuple-element.38.act_ref, bf16[512,3584]{1,0:T(8,128)(2,1)S(1)} %get-tuple-element.39.grad_ref, ...), custom_call_target="tpu_custom_call" | custom-call | flops 301989888 | bytes 2359296 | tf_op jit(solution)/shard_map/partial_eigen/pallas_call | solution.py:431
  26.5 2.7 %collective-permute-start.5 = (f32[36,128]{1,0:T(8,128)S(1)}, f32[36,128]{1,0:T(8,128)S(1)}, u32[]{:S(2)}, u32[]{:S(2)}) collective-permute-start(f32[36,128]{1,0:T(8,128)S(1)} %get-tuple-element.51.refs_0_), channel_id=1, source_target_pairs={{0,12},{4,8},{8,4},{12,0},{1,13},{5,9},{9,5},{13,1},{2,14},{6,10},... | collective-permute-start | bytes 55304 | tf_op jit(solution)/shard_map/ppermute | solution.py:352
  29.2 0.0 collective-permute-start.6
  29.2 1.7 %collective-permute-start.7 = (f32[36,128]{1,0:T(8,128)S(1)}, f32[36,128]{1,0:T(8,128)S(1)}, u32[]{:S(2)}, u32[]{:S(2)}) collective-permute-start(f32[36,128]{1,0:T(8,128)S(1)} %get-tuple-element.51.refs_0_), channel_id=1, source_target_pairs={{0,4},{4,0},{8,12},{12,8},{1,5},{5,1},{9,13},{13,9},{2,6},{6,2},{1... | collective-permute-start | bytes 55304 | tf_op jit(solution)/shard_map/ppermute | solution.py:352
  30.9 0.0 collective-permute-done.9.relayed_ref
  30.9 0.6 %relay_chunk.1 = bf16[1200,128]{1,0:T(8,128)(2,1)S(1)} custom-call(f32[36,32,128]{2,1,0:T(8,128)S(1)} %get-tuple-element.49.far_ref, bf16[1200,128]{1,0:T(8,128)(2,1)S(1)} %collective-permute-done.9.relayed_ref), custom_call_target="tpu_custom_call" | custom-call | bytes 1769472 | tf_op jit(solution)/shard_map/relay_chunk/pallas_call | solution.py:440
  31.5 0.0 collective-permute-done.8.refs_0_
  31.5 0.6 %collective-permute-done.5.refs_1_ = f32[36,128]{1,0:T(8,128)S(1)} collective-permute-done((f32[36,128]{1,0:T(8,128)S(1)}, f32[36,128]{1,0:T(8,128)S(1)}, u32[]{:S(2)}, u32[]{:S(2)}) %collective-permute-start.5) | collective-permute-done | bytes 18464 | tf_op jit(solution)/shard_map/ppermute | solution.py:352
  32.1 2.1 %collective-permute-done.6.refs_2_ = f32[36,128]{1,0:T(8,128)S(1)} collective-permute-done((f32[36,128]{1,0:T(8,128)S(1)}, f32[36,128]{1,0:T(8,128)S(1)}, u32[]{:S(2)}, u32[]{:S(2)}) %collective-permute-start.6) | collective-permute-done | bytes 18464 | tf_op jit(solution)/shard_map/ppermute | solution.py:352
  34.2 0.0 collective-permute-done.7.refs_3_
  34.2 0.8 %collective-permute-start.11 = (bf16[1200,128]{1,0:T(8,128)(2,1)S(1)}, bf16[1200,128]{1,0:T(8,128)(2,1)S(1)}, u32[]{:S(2)}, u32[]{:S(2)}) collective-permute-start(bf16[1200,128]{1,0:T(8,128)(2,1)S(1)} %get-tuple-element.60), channel_id=1, source_target_pairs={{0,4},{4,0},{8,12},{12,8},{1,5},{5,1},{9,13},{13,9},{2,6},{6,2},{1... | collective-permute-start | bytes 921608 | tf_op jit(solution)/shard_map/ppermute | solution.py:352
  35.1 1.3 %collective-permute-start.10 = (bf16[1200,128]{1,0:T(8,128)(2,1)S(1)}, bf16[1200,128]{1,0:T(8,128)(2,1)S(1)}, u32[]{:S(2)}, u32[]{:S(2)}) collective-permute-start(bf16[1200,128]{1,0:T(8,128)(2,1)S(1)} %relay_chunk.1), channel_id=1, source_target_pairs={{0,8},{4,12},{8,0},{12,4},{1,9},{5,13},{9,1},{13,5},{2,10},{6,14},... | collective-permute-start | bytes 921608 | tf_op jit(solution)/shard_map/ppermute | solution.py:352
  36.3 0.0 collective-permute-start.12
  36.3 1.5 %collective-permute-start.13 = (f32[2,128]{1,0:T(2,128)S(1)}, f32[2,128]{1,0:T(2,128)S(1)}, u32[]{:S(2)}, u32[]{:S(2)}) collective-permute-start(f32[2,128]{1,0:T(2,128)S(1)} %get-tuple-element.57.refs_2_), channel_id=1, source_target_pairs={{0,2},{1,3},{2,0},{3,1},{4,6},{5,7},{6,4},{7,5},{8,10},{9,11},{10,... | collective-permute-start | bytes 3080 | tf_op jit(solution)/shard_map/ppermute | solution.py:352
  37.9 0.3 collective-permute-start.14
  38.2 1.1 %collective-permute-done.12.refs_3_ = f32[2,128]{1,0:T(2,128)S(1)} collective-permute-done((f32[2,128]{1,0:T(2,128)S(1)}, f32[2,128]{1,0:T(2,128)S(1)}, u32[]{:S(2)}, u32[]{:S(2)}) %collective-permute-start.12) | collective-permute-done | bytes 1056 | tf_op jit(solution)/shard_map/ppermute | solution.py:352
  39.3 0.6 %collective-permute-done.13.refs_4_ = f32[2,128]{1,0:T(2,128)S(1)} collective-permute-done((f32[2,128]{1,0:T(2,128)S(1)}, f32[2,128]{1,0:T(2,128)S(1)}, u32[]{:S(2)}, u32[]{:S(2)}) %collective-permute-start.13) | collective-permute-done | bytes 1056 | tf_op jit(solution)/shard_map/ppermute | solution.py:352
  39.9 0.0 collective-permute-done.14.refs_5_
  39.9 1.5 %partial_weights.1.refs_2_ = f32[2,512]{1,0:T(2,128)S(1)} custom-call(f32[36,128]{1,0:T(8,128)S(1)} %get-tuple-element.55.eigen_ref, f32[9,512,256]{2,1,0:T(8,128)S(1)} %get-tuple-element.61.refs_0_, f32[9,512,256]{2,1,0:T(8,128)S(1)} %get-tuple-element.62.refs_1_, f32[2,128]{1,0:T(2,128)S(1)} %get-tuple-element.57.refs_2_, ...), custom_call_target="tpu_custom_call" | custom-call | bytes 9437184 | tf_op jit(solution)/shard_map/partial_weights/pallas_call | solution.py:458
  41.4 0.9 %collective-permute-start.15 = (f32[2,512]{1,0:T(2,128)S(1)}, f32[2,512]{1,0:T(2,128)S(1)}, u32[]{:S(2)}, u32[]{:S(2)}) collective-permute-start(f32[2,512]{1,0:T(2,128)S(1)} %partial_weights.1.refs_2_), channel_id=1, source_target_pairs={{0,3},{1,2},{2,1},{3,0},{4,7},{5,6},{6,5},{7,4},{8,11},{9,10},{10,... | collective-permute-start | bytes 12296 | tf_op jit(solution)/shard_map/ppermute | solution.py:352
  42.3 1.5 %collective-permute-start.16 = (f32[2,512]{1,0:T(2,128)S(1)}, f32[2,512]{1,0:T(2,128)S(1)}, u32[]{:S(2)}, u32[]{:S(2)}) collective-permute-start(f32[2,512]{1,0:T(2,128)S(1)} %partial_weights.1.refs_2_), channel_id=1, source_target_pairs={{0,2},{1,3},{2,0},{3,1},{4,6},{5,7},{6,4},{7,5},{8,10},{9,11},{10,... | collective-permute-start | bytes 12296 | tf_op jit(solution)/shard_map/ppermute | solution.py:352
  43.8 0.0 collective-permute-start.17
  43.8 0.6 %add_chunk.1 = (f32[36,32,128]{2,1,0:T(8,128)S(1)}, f32[8,128]{1,0:T(8,128)}, f32[28,128]{1,0:T(8,128)}) custom-call(s32[1]{0:T(128)} %bitcast.side_ref, f32[36,128]{1,0:T(8,128)S(1)} %get-tuple-element.55.eigen_ref, f32[36,32,128]{2,1,0:T(8,128)S(1)} %get-tuple-element.42.own_ref, bf16[1200,128]{1,0:T(8,128)(2,1)S(1)} %collective-permute-done.8.refs_0_), custom_call_target="tpu_custom_call" | custom-call | bytes 1769472 | tf_op jit(solution)/shard_map/add_chunk/pallas_call | solution.py:475
  44.4 0.1 collective-permute-done.15.refs_3_
  44.5 1.4 %collective-permute-done.16.refs_4_ = f32[2,512]{1,0:T(2,128)S(1)} collective-permute-done((f32[2,512]{1,0:T(2,128)S(1)}, f32[2,512]{1,0:T(2,128)S(1)}, u32[]{:S(2)}, u32[]{:S(2)}) %collective-permute-start.16) | collective-permute-done | bytes 4128 | tf_op jit(solution)/shard_map/ppermute | solution.py:352
  45.9 0.0 collective-permute-done.17.refs_5_
  45.9 0.0 collective-permute-done.11.refs_1_
  45.9 1.1 %collective-permute-done.10.refs_0_ = bf16[1200,128]{1,0:T(8,128)(2,1)S(1)} collective-permute-done((bf16[1200,128]{1,0:T(8,128)(2,1)S(1)}, bf16[1200,128]{1,0:T(8,128)(2,1)S(1)}, u32[]{:S(2)}, u32[]{:S(2)}) %collective-permute-start.10) | collective-permute-done | bytes 307232 | tf_op jit(solution)/shard_map/ppermute | solution.py:352
  47.0 1.4 %last_sums.1 = (f32[8,32,128]{2,1,0:T(8,128)}, f32[28,32,128]{2,1,0:T(8,128)}, f32[1,512]{1,0:T(1,128)}) custom-call(f32[36,32,128]{2,1,0:T(8,128)S(1)} %get-tuple-element.56.own_ref, bf16[1200,128]{1,0:T(8,128)(2,1)S(1)} %collective-permute-done.10.refs_0_, bf16[1200,128]{1,0:T(8,128)(2,1)S(1)} %collective-permute-done.11.refs_1_, ...), custom_call_target="tpu_custom_call" | custom-call | bytes 2359296 | tf_op jit(solution)/shard_map/last_sums/pallas_call | solution.py:488
  (1 shorter events, 0.0 us)
Async XLA Ops:
  1.7 14.3 %collective-permute-start.1 = (bf16[18,32,128]{2,1,0:T(8,128)(2,1)S(1)}, bf16[18,32,128]{2,1,0:T(8,128)(2,1)S(1)}, u32[]{:S(2)}, u32[]{:S(2)}) collective-permute-start(bf16[18,32,128]{2,1,0:T(8,128)(2,1)S(1)} %get-tuple-element.41), channel_id=1, source_target_pairs={{0,12},{4,8},{8,4},{12,0},{1,13},{5,9},{9,5},{13,1},{2,14},{6,10},... | collective-permute-start | bytes 442376 | tf_op jit(solution)/shard_map/ppermute | solution.py:352
  6.8 13.5 %collective-permute-start.3 = (bf16[18,32,128]{2,1,0:T(8,128)(2,1)S(1)}, bf16[18,32,128]{2,1,0:T(8,128)(2,1)S(1)}, u32[]{:S(2)}, u32[]{:S(2)}) collective-permute-start(bf16[18,32,128]{2,1,0:T(8,128)(2,1)S(1)} %get-tuple-element.41), channel_id=1, source_target_pairs={{0,8},{4,12},{8,0},{12,4},{1,9},{5,13},{9,1},{13,5},{2,10},{6,14},... | collective-permute-start | bytes 442376 | tf_op jit(solution)/shard_map/ppermute | solution.py:352
  6.8 15.0 %collective-permute-start = (bf16[36,32,128]{2,1,0:T(8,128)(2,1)S(1)}, bf16[36,32,128]{2,1,0:T(8,128)(2,1)S(1)}, u32[]{:S(2)}, u32[]{:S(2)}) collective-permute-start(bf16[36,32,128]{2,1,0:T(8,128)(2,1)S(1)} %get-tuple-element.40.refs_0_), channel_id=1, source_target_pairs={{0,4},{4,0},{8,12},{12,8},{1,5},{5,1},{9,13},{13,9},{2,6},{6,2},{1... | collective-permute-start | bytes 884744 | tf_op jit(solution)/shard_map/ppermute | solution.py:352
  12.0 18.9 %collective-permute-start.9 = (bf16[1200,128]{1,0:T(8,128)(2,1)S(1)}, bf16[1200,128]{1,0:T(8,128)(2,1)S(1)}, u32[]{:S(2)}, u32[]{:S(2)}) collective-permute-start(bf16[1200,128]{1,0:T(8,128)(2,1)S(1)} %get-tuple-element.47), channel_id=1, source_target_pairs={{0,4},{12,8},{1,5},{13,9},{2,6},{14,10},{3,7},{15,11},{16,20},{28,... | collective-permute-start | bytes 921608 | tf_op jit(solution)/shard_map/ppermute | solution.py:423
  15.4 16.1 %collective-permute-start.8 = (bf16[1200,128]{1,0:T(8,128)(2,1)S(1)}, bf16[1200,128]{1,0:T(8,128)(2,1)S(1)}, u32[]{:S(2)}, u32[]{:S(2)}) collective-permute-start(bf16[1200,128]{1,0:T(8,128)(2,1)S(1)} %get-tuple-element.47), channel_id=1, source_target_pairs={{4,8},{8,4},{5,9},{9,5},{6,10},{10,6},{7,11},{11,7},{20,24},{24,20... | collective-permute-start | bytes 921608 | tf_op jit(solution)/shard_map/ppermute | solution.py:422
  16.1 6.8 %collective-permute-start.2 = (bf16[18,32,128]{2,1,0:T(8,128)(2,1)S(1)}, bf16[18,32,128]{2,1,0:T(8,128)(2,1)S(1)}, u32[]{:S(2)}, u32[]{:S(2)}) collective-permute-start(bf16[18,32,128]{2,1,0:T(8,128)(2,1)S(1)} %collective-permute-done.1.refs_2_), channel_id=1, source_target_pairs={{0,16},{16,0},{1,17},{17,1},{2,18},{18,2},{3,19},{19,3},{4,20},{20... | collective-permute-start | bytes 442376 | tf_op jit(solution)/shard_map/ppermute | solution.py:352
  20.3 5.1 %collective-permute-start.4 = (bf16[18,32,128]{2,1,0:T(8,128)(2,1)S(1)}, bf16[18,32,128]{2,1,0:T(8,128)(2,1)S(1)}, u32[]{:S(2)}, u32[]{:S(2)}) collective-permute-start(bf16[18,32,128]{2,1,0:T(8,128)(2,1)S(1)} %collective-permute-done.3.refs_3_), channel_id=1, source_target_pairs={{0,16},{16,0},{1,17},{17,1},{2,18},{18,2},{3,19},{19,3},{4,20},{20... | collective-permute-start | bytes 442376 | tf_op jit(solution)/shard_map/ppermute | solution.py:352
  26.5 5.7 %collective-permute-start.5 = (f32[36,128]{1,0:T(8,128)S(1)}, f32[36,128]{1,0:T(8,128)S(1)}, u32[]{:S(2)}, u32[]{:S(2)}) collective-permute-start(f32[36,128]{1,0:T(8,128)S(1)} %get-tuple-element.51.refs_0_), channel_id=1, source_target_pairs={{0,12},{4,8},{8,4},{12,0},{1,13},{5,9},{9,5},{13,1},{2,14},{6,10},... | collective-permute-start | bytes 55304 | tf_op jit(solution)/shard_map/ppermute | solution.py:352
  29.2 5.0 %collective-permute-start.6 = (f32[36,128]{1,0:T(8,128)S(1)}, f32[36,128]{1,0:T(8,128)S(1)}, u32[]{:S(2)}, u32[]{:S(2)}) collective-permute-start(f32[36,128]{1,0:T(8,128)S(1)} %get-tuple-element.51.refs_0_), channel_id=1, source_target_pairs={{0,8},{4,12},{8,0},{12,4},{1,9},{5,13},{9,1},{13,5},{2,10},{6,14},... | collective-permute-start | bytes 55304 | tf_op jit(solution)/shard_map/ppermute | solution.py:352
  29.2 5.0 %collective-permute-start.7 = (f32[36,128]{1,0:T(8,128)S(1)}, f32[36,128]{1,0:T(8,128)S(1)}, u32[]{:S(2)}, u32[]{:S(2)}) collective-permute-start(f32[36,128]{1,0:T(8,128)S(1)} %get-tuple-element.51.refs_0_), channel_id=1, source_target_pairs={{0,4},{4,0},{8,12},{12,8},{1,5},{5,1},{9,13},{13,9},{2,6},{6,2},{1... | collective-permute-start | bytes 55304 | tf_op jit(solution)/shard_map/ppermute | solution.py:352
  34.2 11.7 %collective-permute-start.11 = (bf16[1200,128]{1,0:T(8,128)(2,1)S(1)}, bf16[1200,128]{1,0:T(8,128)(2,1)S(1)}, u32[]{:S(2)}, u32[]{:S(2)}) collective-permute-start(bf16[1200,128]{1,0:T(8,128)(2,1)S(1)} %get-tuple-element.60), channel_id=1, source_target_pairs={{0,4},{4,0},{8,12},{12,8},{1,5},{5,1},{9,13},{13,9},{2,6},{6,2},{1... | collective-permute-start | bytes 921608 | tf_op jit(solution)/shard_map/ppermute | solution.py:352
  35.1 11.9 %collective-permute-start.10 = (bf16[1200,128]{1,0:T(8,128)(2,1)S(1)}, bf16[1200,128]{1,0:T(8,128)(2,1)S(1)}, u32[]{:S(2)}, u32[]{:S(2)}) collective-permute-start(bf16[1200,128]{1,0:T(8,128)(2,1)S(1)} %relay_chunk.1), channel_id=1, source_target_pairs={{0,8},{4,12},{8,0},{12,4},{1,9},{5,13},{9,1},{13,5},{2,10},{6,14},... | collective-permute-start | bytes 921608 | tf_op jit(solution)/shard_map/ppermute | solution.py:352
  36.3 3.0 %collective-permute-start.12 = (f32[2,128]{1,0:T(2,128)S(1)}, f32[2,128]{1,0:T(2,128)S(1)}, u32[]{:S(2)}, u32[]{:S(2)}) collective-permute-start(f32[2,128]{1,0:T(2,128)S(1)} %get-tuple-element.57.refs_2_), channel_id=1, source_target_pairs={{0,3},{1,2},{2,1},{3,0},{4,7},{5,6},{6,5},{7,4},{8,11},{9,10},{10,... | collective-permute-start | bytes 3080 | tf_op jit(solution)/shard_map/ppermute | solution.py:352
  36.3 3.6 %collective-permute-start.13 = (f32[2,128]{1,0:T(2,128)S(1)}, f32[2,128]{1,0:T(2,128)S(1)}, u32[]{:S(2)}, u32[]{:S(2)}) collective-permute-start(f32[2,128]{1,0:T(2,128)S(1)} %get-tuple-element.57.refs_2_), channel_id=1, source_target_pairs={{0,2},{1,3},{2,0},{3,1},{4,6},{5,7},{6,4},{7,5},{8,10},{9,11},{10,... | collective-permute-start | bytes 3080 | tf_op jit(solution)/shard_map/ppermute | solution.py:352
  37.9 2.1 %collective-permute-start.14 = (f32[2,128]{1,0:T(2,128)S(1)}, f32[2,128]{1,0:T(2,128)S(1)}, u32[]{:S(2)}, u32[]{:S(2)}) collective-permute-start(f32[2,128]{1,0:T(2,128)S(1)} %get-tuple-element.57.refs_2_), channel_id=1, source_target_pairs={{0,1},{1,0},{2,3},{3,2},{4,5},{5,4},{6,7},{7,6},{8,9},{9,8},{10,11... | collective-permute-start | bytes 3080 | tf_op jit(solution)/shard_map/ppermute | solution.py:352
  41.4 3.1 %collective-permute-start.15 = (f32[2,512]{1,0:T(2,128)S(1)}, f32[2,512]{1,0:T(2,128)S(1)}, u32[]{:S(2)}, u32[]{:S(2)}) collective-permute-start(f32[2,512]{1,0:T(2,128)S(1)} %partial_weights.1.refs_2_), channel_id=1, source_target_pairs={{0,3},{1,2},{2,1},{3,0},{4,7},{5,6},{6,5},{7,4},{8,11},{9,10},{10,... | collective-permute-start | bytes 12296 | tf_op jit(solution)/shard_map/ppermute | solution.py:352
  42.3 3.6 %collective-permute-start.16 = (f32[2,512]{1,0:T(2,128)S(1)}, f32[2,512]{1,0:T(2,128)S(1)}, u32[]{:S(2)}, u32[]{:S(2)}) collective-permute-start(f32[2,512]{1,0:T(2,128)S(1)} %partial_weights.1.refs_2_), channel_id=1, source_target_pairs={{0,2},{1,3},{2,0},{3,1},{4,6},{5,7},{6,4},{7,5},{8,10},{9,11},{10,... | collective-permute-start | bytes 12296 | tf_op jit(solution)/shard_map/ppermute | solution.py:352
  43.8 2.1 %collective-permute-start.17 = (f32[2,512]{1,0:T(2,128)S(1)}, f32[2,512]{1,0:T(2,128)S(1)}, u32[]{:S(2)}, u32[]{:S(2)}) collective-permute-start(f32[2,512]{1,0:T(2,128)S(1)} %partial_weights.1.refs_2_), channel_id=1, source_target_pairs={{0,1},{1,0},{2,3},{3,2},{4,5},{5,4},{6,7},{7,6},{8,9},{9,8},{10,11... | collective-permute-start | bytes 12296 | tf_op jit(solution)/shard_map/ppermute | solution.py:352

commit v14 on v13

--- a/solution.py
+++ b/solution.py
@@ -483,7 +483,7 @@
             functools.partial(order_kernel, halves), eigens, "order_eigen", 0,
             8 * blocks * BLK, [IN_SMEM, IN_VMEM],
         )(side, eigen)
-    chunks = list(arrived.values())[::-1]
+    chunks = list(arrived.values())
     if chunks:
         *covariance, token_scores = call(
             functools.partial(last_add_kernel, [(None, 0, blocks)] * len(chunks), len(weights)),

time: 48.5 us -> 48.9 us (level)
  waiting for transfers between devices: 12.3 us -> 14.7 us
  starting transfers between devices: 23.7 us -> 21.7 us
    ppermute x16, waiting for transfers between devices: 12.3 us -> 14.7 us  [swap(): return lax.ppermute(value, axis, [(i, i ^ mask) for i in range(count)])]
    ppermute x16, starting transfers between devices: 19.7 us -> 17.7 us  [swap(): return lax.ppermute(value, axis, [(i, i ^ mask) for i in range(count)])]
  transfers between devices with their start and end apart: 18 -> 18, of which waited for: 9 -> 10; matrix products, arithmetic and copies ran while one was open for 0% -> 0% of each run, Pallas kernels for 19% -> 19%
where the time goes in v14:
time: 48.9 us; the launch traced here: 48.8 us
  starting transfers between devices  21.7 us (44%)
  waiting for transfers between devices  14.7 us (30%)
  Pallas kernels  11.6 us (24%)
  between operations  0.76 us (2%)
    ppermute x16, starting transfers between devices, swap(): return lax.ppermute(value, axis, [(i, i ^ mask) for i in range(count)])  17.7 us
    ppermute x16, waiting for transfers between devices, swap(): return lax.ppermute(value, axis, [(i, i ^ mask) for i in range(count)])  14.7 us
    pallas_call x1, Pallas kernels, local(): call(functools.partial(gram_kernel, pieces, coded, scale), [bf16(*activat...  4.56 us
    ppermute x1, starting transfers between devices, local(): relayed = lax.ppermute(sent[3], 'dp', [(0, 1), (3, 2)])  3.32 us
    pallas_call x2, Pallas kernels, local(): call(functools.partial(eigen_kernel, part, halves, masks, pieces, scale),...  1.95 us
    pallas_call x1, Pallas kernels, local(): call(functools.partial(weight_kernel, halves, act_blocks // halves), f32(...  1.49 us
    pallas_call x1, Pallas kernels, local(): call(functools.partial(last_add_kernel, [(None, 0, blocks)] * len(chunks)...  1.35 us
    pallas_call x1, Pallas kernels, local(): call(pack_kernel, [bf16(blocks // part, rows, BLK) for part in range(1, h...  1.08 us
  transfers between devices with their start and end apart: 18, of which 10 were waited for; matrix products, arithmetic and copies ran while one was open for 0% of the time, Pallas kernels for 19%

profile of v14, /device:TPU:0, one launch (start us, length us, event | category | flops | bytes accessed | tf_op | source)
XLA Modules:
  0.0 48.8 jit_solution(15020533079318586541)
XLA Ops:
  0.6 1.1 %pack_basis.1 = (bf16[36,32,128]{2,1,0:T(8,128)(2,1)S(1)}, bf16[18,32,128]{2,1,0:T(8,128)(2,1)S(1)}) custom-call(s32[1]{0:T(128)} %bitcast.side_ref, bf16[8,32,128]{2,1,0:T(8,128)(2,1)} %act_ref.1, bf16[28,32,128]{2,1,0:T(8,128)(2,1)} %grad_ref.1), custom_call_target="tpu_custom_call" | custom-call | bytes 294912 | tf_op jit(solution)/shard_map/pack_basis/pallas_call | solution.py:380
  1.7 5.1 %collective-permute-start.1 = (bf16[18,32,128]{2,1,0:T(8,128)(2,1)S(1)}, bf16[18,32,128]{2,1,0:T(8,128)(2,1)S(1)}, u32[]{:S(2)}, u32[]{:S(2)}) collective-permute-start(bf16[18,32,128]{2,1,0:T(8,128)(2,1)S(1)} %get-tuple-element.41), channel_id=1, source_target_pairs={{0,12},{4,8},{8,4},{12,0},{1,13},{5,9},{9,5},{13,1},{2,14},{6,10},... | collective-permute-start | bytes 442376 | tf_op jit(solution)/shard_map/ppermute | solution.py:352
  6.8 0.0 collective-permute-start.3
  6.8 0.6 %collective-permute-start = (bf16[36,32,128]{2,1,0:T(8,128)(2,1)S(1)}, bf16[36,32,128]{2,1,0:T(8,128)(2,1)S(1)}, u32[]{:S(2)}, u32[]{:S(2)}) collective-permute-start(bf16[36,32,128]{2,1,0:T(8,128)(2,1)S(1)} %get-tuple-element.40.refs_0_), channel_id=1, source_target_pairs={{0,4},{4,0},{8,12},{12,8},{1,5},{5,1},{9,13},{13,9},{2,6},{6,2},{1... | collective-permute-start | bytes 884744 | tf_op jit(solution)/shard_map/ppermute | solution.py:352
  7.5 4.6 %partial_gram.1 = (bf16[512,1024]{1,0:T(8,128)(2,1)S(1)}, bf16[512,3584]{1,0:T(8,128)(2,1)S(1)}, f32[36,32,128]{2,1,0:T(8,128)S(1)}, f32[36,32,128]{2,1,0:T(8,12...) custom-call(s32[1]{0:T(128)} %bitcast.1.me_ref, bf16[512,1024]{1,0:T(8,128)(2,1)} %act_hbm.1, ...), custom_call_target="tpu_custom_call" | custom-call | flops 1207959552 | bytes 4718592 | tf_op jit(solution)/shard_map/partial_gram/pallas_call | solution.py:401
  12.0 3.3 %collective-permute-start.9 = (bf16[1200,128]{1,0:T(8,128)(2,1)S(1)}, bf16[1200,128]{1,0:T(8,128)(2,1)S(1)}, u32[]{:S(2)}, u32[]{:S(2)}) collective-permute-start(bf16[1200,128]{1,0:T(8,128)(2,1)S(1)} %get-tuple-element.47), channel_id=1, source_target_pairs={{0,4},{12,8},{1,5},{13,9},{2,6},{14,10},{3,7},{15,11},{16,20},{28,... | collective-permute-start | bytes 921608 | tf_op jit(solution)/shard_map/ppermute | solution.py:423
  15.4 0.7 %collective-permute-start.8 = (bf16[1200,128]{1,0:T(8,128)(2,1)S(1)}, bf16[1200,128]{1,0:T(8,128)(2,1)S(1)}, u32[]{:S(2)}, u32[]{:S(2)}) collective-permute-start(bf16[1200,128]{1,0:T(8,128)(2,1)S(1)} %get-tuple-element.47), channel_id=1, source_target_pairs={{4,8},{8,4},{5,9},{9,5},{6,10},{10,6},{7,11},{11,7},{20,24},{24,20... | collective-permute-start | bytes 921608 | tf_op jit(solution)/shard_map/ppermute | solution.py:422
  16.1 0.0 collective-permute-done.1.refs_2_
  16.1 1.6 %collective-permute-start.2 = (bf16[18,32,128]{2,1,0:T(8,128)(2,1)S(1)}, bf16[18,32,128]{2,1,0:T(8,128)(2,1)S(1)}, u32[]{:S(2)}, u32[]{:S(2)}) collective-permute-start(bf16[18,32,128]{2,1,0:T(8,128)(2,1)S(1)} %collective-permute-done.1.refs_2_), channel_id=1, source_target_pairs={{0,16},{16,0},{1,17},{17,1},{2,18},{18,2},{3,19},{19,3},{4,20},{20... | collective-permute-start | bytes 442376 | tf_op jit(solution)/shard_map/ppermute | solution.py:352
  17.6 2.7 %collective-permute-done.3.refs_3_ = bf16[18,32,128]{2,1,0:T(8,128)(2,1)S(1)} collective-permute-done((bf16[18,32,128]{2,1,0:T(8,128)(2,1)S(1)}, bf16[18,32,128]{2,1,0:T(8,128)(2,1)S(1)}, u32[]{:S(2)}, u32[]{:S(2)}) %collective-permute-start.3) | collective-permute-done | bytes 147488 | tf_op jit(solution)/shard_map/ppermute | solution.py:352
  20.3 1.5 %collective-permute-start.4 = (bf16[18,32,128]{2,1,0:T(8,128)(2,1)S(1)}, bf16[18,32,128]{2,1,0:T(8,128)(2,1)S(1)}, u32[]{:S(2)}, u32[]{:S(2)}) collective-permute-start(bf16[18,32,128]{2,1,0:T(8,128)(2,1)S(1)} %collective-permute-done.3.refs_3_), channel_id=1, source_target_pairs={{0,16},{16,0},{1,17},{17,1},{2,18},{18,2},{3,19},{19,3},{4,20},{20... | collective-permute-start | bytes 442376 | tf_op jit(solution)/shard_map/ppermute | solution.py:352
  21.8 0.0 collective-permute-done.refs_1_
  21.8 1.0 %partial_eigen.2 = (f32[9,512,256]{2,1,0:T(8,128)S(1)}, f32[18,128]{1,0:T(8,128)S(1)}) custom-call(s32[1]{0:T(128)} %bitcast.1.me_ref, s32[1]{0:T(128)} %bitcast.side_ref, bf16[512,1024]{1,0:T(8,128)(2,1)S(1)} %get-tuple-element.38.act_ref, bf16[512,3584]{1,0:T(8,128)(2,1)S(1)} %get-tuple-element.39.grad_ref, ...), custom_call_target="tpu_custom_call" | custom-call | flops 301989888 | bytes 2359296 | tf_op jit(solution)/shard_map/partial_eigen/pallas_call | solution.py:431
  22.8 0.0 collective-permute-done.2.refs_2_
  22.8 2.6 %collective-permute-done.4.refs_3_ = bf16[18,32,128]{2,1,0:T(8,128)(2,1)S(1)} collective-permute-done((bf16[18,32,128]{2,1,0:T(8,128)(2,1)S(1)}, bf16[18,32,128]{2,1,0:T(8,128)(2,1)S(1)}, u32[]{:S(2)}, u32[]{:S(2)}) %collective-permute-start.4) | collective-permute-done | bytes 147488 | tf_op jit(solution)/shard_map/ppermute | solution.py:352
  25.5 1.0 %partial_eigen.3 = (f32[9,512,256]{2,1,0:T(8,128)S(1)}, f32[36,128]{1,0:T(8,128)S(1)}) custom-call(s32[1]{0:T(128)} %bitcast.1.me_ref, s32[1]{0:T(128)} %bitcast.side_ref, bf16[512,1024]{1,0:T(8,128)(2,1)S(1)} %get-tuple-element.38.act_ref, bf16[512,3584]{1,0:T(8,128)(2,1)S(1)} %get-tuple-element.39.grad_ref, ...), custom_call_target="tpu_custom_call" | custom-call | flops 301989888 | bytes 2359296 | tf_op jit(solution)/shard_map/partial_eigen/pallas_call | solution.py:431
  26.5 2.7 %collective-permute-start.5 = (f32[36,128]{1,0:T(8,128)S(1)}, f32[36,128]{1,0:T(8,128)S(1)}, u32[]{:S(2)}, u32[]{:S(2)}) collective-permute-start(f32[36,128]{1,0:T(8,128)S(1)} %get-tuple-element.51.refs_0_), channel_id=1, source_target_pairs={{0,12},{4,8},{8,4},{12,0},{1,13},{5,9},{9,5},{13,1},{2,14},{6,10},... | collective-permute-start | bytes 55304 | tf_op jit(solution)/shard_map/ppermute | solution.py:352
  29.2 0.0 collective-permute-start.6
  29.2 1.7 %collective-permute-start.7 = (f32[36,128]{1,0:T(8,128)S(1)}, f32[36,128]{1,0:T(8,128)S(1)}, u32[]{:S(2)}, u32[]{:S(2)}) collective-permute-start(f32[36,128]{1,0:T(8,128)S(1)} %get-tuple-element.51.refs_0_), channel_id=1, source_target_pairs={{0,4},{4,0},{8,12},{12,8},{1,5},{5,1},{9,13},{13,9},{2,6},{6,2},{1... | collective-permute-start | bytes 55304 | tf_op jit(solution)/shard_map/ppermute | solution.py:352
  30.9 0.0 collective-permute-done.9.relayed_ref
  30.9 0.6 %relay_chunk.1 = bf16[1200,128]{1,0:T(8,128)(2,1)S(1)} custom-call(f32[36,32,128]{2,1,0:T(8,128)S(1)} %get-tuple-element.49.far_ref, bf16[1200,128]{1,0:T(8,128)(2,1)S(1)} %collective-permute-done.9.relayed_ref), custom_call_target="tpu_custom_call" | custom-call | bytes 1769472 | tf_op jit(solution)/shard_map/relay_chunk/pallas_call | solution.py:440
  31.5 0.0 collective-permute-done.8.refs_0_
  31.5 0.6 %collective-permute-done.5.refs_1_ = f32[36,128]{1,0:T(8,128)S(1)} collective-permute-done((f32[36,128]{1,0:T(8,128)S(1)}, f32[36,128]{1,0:T(8,128)S(1)}, u32[]{:S(2)}, u32[]{:S(2)}) %collective-permute-start.5) | collective-permute-done | bytes 18464 | tf_op jit(solution)/shard_map/ppermute | solution.py:352
  32.1 5.0 %collective-permute-done.6.refs_2_ = f32[36,128]{1,0:T(8,128)S(1)} collective-permute-done((f32[36,128]{1,0:T(8,128)S(1)}, f32[36,128]{1,0:T(8,128)S(1)}, u32[]{:S(2)}, u32[]{:S(2)}) %collective-permute-start.6) | collective-permute-done | bytes 18464 | tf_op jit(solution)/shard_map/ppermute | solution.py:352
  37.1 0.0 collective-permute-done.7.refs_3_
  37.1 0.1 collective-permute-start.11
  37.2 0.1 collective-permute-start.10
  37.3 0.1 collective-permute-start.12
  37.4 1.5 %collective-permute-start.13 = (f32[2,128]{1,0:T(2,128)S(1)}, f32[2,128]{1,0:T(2,128)S(1)}, u32[]{:S(2)}, u32[]{:S(2)}) collective-permute-start(f32[2,128]{1,0:T(2,128)S(1)} %get-tuple-element.58.refs_2_), channel_id=1, source_target_pairs={{0,2},{1,3},{2,0},{3,1},{4,6},{5,7},{6,4},{7,5},{8,10},{9,11},{10,... | collective-permute-start | bytes 3080 | tf_op jit(solution)/shard_map/ppermute | solution.py:352
  38.9 0.3 collective-permute-start.14
  39.2 1.1 %collective-permute-done.12.refs_3_ = f32[2,128]{1,0:T(2,128)S(1)} collective-permute-done((f32[2,128]{1,0:T(2,128)S(1)}, f32[2,128]{1,0:T(2,128)S(1)}, u32[]{:S(2)}, u32[]{:S(2)}) %collective-permute-start.12) | collective-permute-done | bytes 1056 | tf_op jit(solution)/shard_map/ppermute | solution.py:352
  40.3 0.7 %collective-permute-done.13.refs_4_ = f32[2,128]{1,0:T(2,128)S(1)} collective-permute-done((f32[2,128]{1,0:T(2,128)S(1)}, f32[2,128]{1,0:T(2,128)S(1)}, u32[]{:S(2)}, u32[]{:S(2)}) %collective-permute-start.13) | collective-permute-done | bytes 1056 | tf_op jit(solution)/shard_map/ppermute | solution.py:352
  41.0 0.0 collective-permute-done.14.refs_5_
  41.0 1.5 %partial_weights.1.refs_2_ = f32[2,512]{1,0:T(2,128)S(1)} custom-call(f32[36,128]{1,0:T(8,128)S(1)} %get-tuple-element.55.eigen_ref, f32[9,512,256]{2,1,0:T(8,128)S(1)} %get-tuple-element.61.refs_0_, f32[9,512,256]{2,1,0:T(8,128)S(1)} %get-tuple-element.62.refs_1_, f32[2,128]{1,0:T(2,128)S(1)} %get-tuple-element.58.refs_2_, ...), custom_call_target="tpu_custom_call" | custom-call | bytes 9437184 | tf_op jit(solution)/shard_map/partial_weights/pallas_call | solution.py:458
  42.5 0.6 %collective-permute-start.15 = (f32[2,512]{1,0:T(2,128)S(1)}, f32[2,512]{1,0:T(2,128)S(1)}, u32[]{:S(2)}, u32[]{:S(2)}) collective-permute-start(f32[2,512]{1,0:T(2,128)S(1)} %partial_weights.1.refs_2_), channel_id=1, source_target_pairs={{0,3},{1,2},{2,1},{3,0},{4,7},{5,6},{6,5},{7,4},{8,11},{9,10},{10,... | collective-permute-start | bytes 12296 | tf_op jit(solution)/shard_map/ppermute | solution.py:352
  43.0 1.7 %collective-permute-start.16 = (f32[2,512]{1,0:T(2,128)S(1)}, f32[2,512]{1,0:T(2,128)S(1)}, u32[]{:S(2)}, u32[]{:S(2)}) collective-permute-start(f32[2,512]{1,0:T(2,128)S(1)} %partial_weights.1.refs_2_), channel_id=1, source_target_pairs={{0,2},{1,3},{2,0},{3,1},{4,6},{5,7},{6,4},{7,5},{8,10},{9,11},{10,... | collective-permute-start | bytes 12296 | tf_op jit(solution)/shard_map/ppermute | solution.py:352
  44.8 0.0 collective-permute-start.17
  44.8 0.6 %add_chunk.1 = (f32[36,32,128]{2,1,0:T(8,128)S(1)}, f32[8,128]{1,0:T(8,128)}, f32[28,128]{1,0:T(8,128)}) custom-call(s32[1]{0:T(128)} %bitcast.side_ref, f32[36,128]{1,0:T(8,128)S(1)} %get-tuple-element.55.eigen_ref, f32[36,32,128]{2,1,0:T(8,128)S(1)} %get-tuple-element.42.own_ref, bf16[1200,128]{1,0:T(8,128)(2,1)S(1)} %collective-permute-done.8.refs_0_), custom_call_target="tpu_custom_call" | custom-call | bytes 1769472 | tf_op jit(solution)/shard_map/add_chunk/pallas_call | solution.py:475
  45.4 0.1 collective-permute-done.15.refs_3_
  45.5 1.1 %collective-permute-done.16.refs_4_ = f32[2,512]{1,0:T(2,128)S(1)} collective-permute-done((f32[2,512]{1,0:T(2,128)S(1)}, f32[2,512]{1,0:T(2,128)S(1)}, u32[]{:S(2)}, u32[]{:S(2)}) %collective-permute-start.16) | collective-permute-done | bytes 4128 | tf_op jit(solution)/shard_map/ppermute | solution.py:352
  46.7 0.0 collective-permute-done.17.refs_5_
  46.7 0.1 collective-permute-done.11.refs_1_
  46.8 0.7 %collective-permute-done.10.refs_0_ = bf16[1200,128]{1,0:T(8,128)(2,1)S(1)} collective-permute-done((bf16[1200,128]{1,0:T(8,128)(2,1)S(1)}, bf16[1200,128]{1,0:T(8,128)(2,1)S(1)}, u32[]{:S(2)}, u32[]{:S(2)}) %collective-permute-start.10) | collective-permute-done | bytes 307232 | tf_op jit(solution)/shard_map/ppermute | solution.py:352
  47.4 1.4 %last_sums.1 = (f32[8,32,128]{2,1,0:T(8,128)}, f32[28,32,128]{2,1,0:T(8,128)}, f32[1,512]{1,0:T(1,128)}) custom-call(f32[36,32,128]{2,1,0:T(8,128)S(1)} %get-tuple-element.56.own_ref, bf16[1200,128]{1,0:T(8,128)(2,1)S(1)} %collective-permute-done.10.refs_0_, bf16[1200,128]{1,0:T(8,128)(2,1)S(1)} %collective-permute-done.11.refs_1_, ...), custom_call_target="tpu_custom_call" | custom-call | bytes 2359296 | tf_op jit(solution)/shard_map/last_sums/pallas_call | solution.py:488
  (1 shorter events, 0.0 us)
Async XLA Ops:
  1.7 14.3 %collective-permute-start.1 = (bf16[18,32,128]{2,1,0:T(8,128)(2,1)S(1)}, bf16[18,32,128]{2,1,0:T(8,128)(2,1)S(1)}, u32[]{:S(2)}, u32[]{:S(2)}) collective-permute-start(bf16[18,32,128]{2,1,0:T(8,128)(2,1)S(1)} %get-tuple-element.41), channel_id=1, source_target_pairs={{0,12},{4,8},{8,4},{12,0},{1,13},{5,9},{9,5},{13,1},{2,14},{6,10},... | collective-permute-start | bytes 442376 | tf_op jit(solution)/shard_map/ppermute | solution.py:352
  6.8 13.5 %collective-permute-start.3 = (bf16[18,32,128]{2,1,0:T(8,128)(2,1)S(1)}, bf16[18,32,128]{2,1,0:T(8,128)(2,1)S(1)}, u32[]{:S(2)}, u32[]{:S(2)}) collective-permute-start(bf16[18,32,128]{2,1,0:T(8,128)(2,1)S(1)} %get-tuple-element.41), channel_id=1, source_target_pairs={{0,8},{4,12},{8,0},{12,4},{1,9},{5,13},{9,1},{13,5},{2,10},{6,14},... | collective-permute-start | bytes 442376 | tf_op jit(solution)/shard_map/ppermute | solution.py:352
  6.8 15.0 %collective-permute-start = (bf16[36,32,128]{2,1,0:T(8,128)(2,1)S(1)}, bf16[36,32,128]{2,1,0:T(8,128)(2,1)S(1)}, u32[]{:S(2)}, u32[]{:S(2)}) collective-permute-start(bf16[36,32,128]{2,1,0:T(8,128)(2,1)S(1)} %get-tuple-element.40.refs_0_), channel_id=1, source_target_pairs={{0,4},{4,0},{8,12},{12,8},{1,5},{5,1},{9,13},{13,9},{2,6},{6,2},{1... | collective-permute-start | bytes 884744 | tf_op jit(solution)/shard_map/ppermute | solution.py:352
  12.0 18.9 %collective-permute-start.9 = (bf16[1200,128]{1,0:T(8,128)(2,1)S(1)}, bf16[1200,128]{1,0:T(8,128)(2,1)S(1)}, u32[]{:S(2)}, u32[]{:S(2)}) collective-permute-start(bf16[1200,128]{1,0:T(8,128)(2,1)S(1)} %get-tuple-element.47), channel_id=1, source_target_pairs={{0,4},{12,8},{1,5},{13,9},{2,6},{14,10},{3,7},{15,11},{16,20},{28,... | collective-permute-start | bytes 921608 | tf_op jit(solution)/shard_map/ppermute | solution.py:423
  15.4 16.1 %collective-permute-start.8 = (bf16[1200,128]{1,0:T(8,128)(2,1)S(1)}, bf16[1200,128]{1,0:T(8,128)(2,1)S(1)}, u32[]{:S(2)}, u32[]{:S(2)}) collective-permute-start(bf16[1200,128]{1,0:T(8,128)(2,1)S(1)} %get-tuple-element.47), channel_id=1, source_target_pairs={{4,8},{8,4},{5,9},{9,5},{6,10},{10,6},{7,11},{11,7},{20,24},{24,20... | collective-permute-start | bytes 921608 | tf_op jit(solution)/shard_map/ppermute | solution.py:422
  16.1 6.8 %collective-permute-start.2 = (bf16[18,32,128]{2,1,0:T(8,128)(2,1)S(1)}, bf16[18,32,128]{2,1,0:T(8,128)(2,1)S(1)}, u32[]{:S(2)}, u32[]{:S(2)}) collective-permute-start(bf16[18,32,128]{2,1,0:T(8,128)(2,1)S(1)} %collective-permute-done.1.refs_2_), channel_id=1, source_target_pairs={{0,16},{16,0},{1,17},{17,1},{2,18},{18,2},{3,19},{19,3},{4,20},{20... | collective-permute-start | bytes 442376 | tf_op jit(solution)/shard_map/ppermute | solution.py:352
  20.3 5.1 %collective-permute-start.4 = (bf16[18,32,128]{2,1,0:T(8,128)(2,1)S(1)}, bf16[18,32,128]{2,1,0:T(8,128)(2,1)S(1)}, u32[]{:S(2)}, u32[]{:S(2)}) collective-permute-start(bf16[18,32,128]{2,1,0:T(8,128)(2,1)S(1)} %collective-permute-done.3.refs_3_), channel_id=1, source_target_pairs={{0,16},{16,0},{1,17},{17,1},{2,18},{18,2},{3,19},{19,3},{4,20},{20... | collective-permute-start | bytes 442376 | tf_op jit(solution)/shard_map/ppermute | solution.py:352
  26.5 5.6 %collective-permute-start.5 = (f32[36,128]{1,0:T(8,128)S(1)}, f32[36,128]{1,0:T(8,128)S(1)}, u32[]{:S(2)}, u32[]{:S(2)}) collective-permute-start(f32[36,128]{1,0:T(8,128)S(1)} %get-tuple-element.51.refs_0_), channel_id=1, source_target_pairs={{0,12},{4,8},{8,4},{12,0},{1,13},{5,9},{9,5},{13,1},{2,14},{6,10},... | collective-permute-start | bytes 55304 | tf_op jit(solution)/shard_map/ppermute | solution.py:352
  29.2 7.9 %collective-permute-start.6 = (f32[36,128]{1,0:T(8,128)S(1)}, f32[36,128]{1,0:T(8,128)S(1)}, u32[]{:S(2)}, u32[]{:S(2)}) collective-permute-start(f32[36,128]{1,0:T(8,128)S(1)} %get-tuple-element.51.refs_0_), channel_id=1, source_target_pairs={{0,8},{4,12},{8,0},{12,4},{1,9},{5,13},{9,1},{13,5},{2,10},{6,14},... | collective-permute-start | bytes 55304 | tf_op jit(solution)/shard_map/ppermute | solution.py:352
  29.2 7.9 %collective-permute-start.7 = (f32[36,128]{1,0:T(8,128)S(1)}, f32[36,128]{1,0:T(8,128)S(1)}, u32[]{:S(2)}, u32[]{:S(2)}) collective-permute-start(f32[36,128]{1,0:T(8,128)S(1)} %get-tuple-element.51.refs_0_), channel_id=1, source_target_pairs={{0,4},{4,0},{8,12},{12,8},{1,5},{5,1},{9,13},{13,9},{2,6},{6,2},{1... | collective-permute-start | bytes 55304 | tf_op jit(solution)/shard_map/ppermute | solution.py:352
  37.1 9.6 %collective-permute-start.11 = (bf16[1200,128]{1,0:T(8,128)(2,1)S(1)}, bf16[1200,128]{1,0:T(8,128)(2,1)S(1)}, u32[]{:S(2)}, u32[]{:S(2)}) collective-permute-start(bf16[1200,128]{1,0:T(8,128)(2,1)S(1)} %relay_chunk.1), channel_id=1, source_target_pairs={{0,8},{4,12},{8,0},{12,4},{1,9},{5,13},{9,1},{13,5},{2,10},{6,14},... | collective-permute-start | bytes 921608 | tf_op jit(solution)/shard_map/ppermute | solution.py:352
  37.2 10.2 %collective-permute-start.10 = (bf16[1200,128]{1,0:T(8,128)(2,1)S(1)}, bf16[1200,128]{1,0:T(8,128)(2,1)S(1)}, u32[]{:S(2)}, u32[]{:S(2)}) collective-permute-start(bf16[1200,128]{1,0:T(8,128)(2,1)S(1)} %get-tuple-element.59), channel_id=1, source_target_pairs={{0,4},{4,0},{8,12},{12,8},{1,5},{5,1},{9,13},{13,9},{2,6},{6,2},{1... | collective-permute-start | bytes 921608 | tf_op jit(solution)/shard_map/ppermute | solution.py:352
  37.3 3.1 %collective-permute-start.12 = (f32[2,128]{1,0:T(2,128)S(1)}, f32[2,128]{1,0:T(2,128)S(1)}, u32[]{:S(2)}, u32[]{:S(2)}) collective-permute-start(f32[2,128]{1,0:T(2,128)S(1)} %get-tuple-element.58.refs_2_), channel_id=1, source_target_pairs={{0,3},{1,2},{2,1},{3,0},{4,7},{5,6},{6,5},{7,4},{8,11},{9,10},{10,... | collective-permute-start | bytes 3080 | tf_op jit(solution)/shard_map/ppermute | solution.py:352
  37.4 3.6 %collective-permute-start.13 = (f32[2,128]{1,0:T(2,128)S(1)}, f32[2,128]{1,0:T(2,128)S(1)}, u32[]{:S(2)}, u32[]{:S(2)}) collective-permute-start(f32[2,128]{1,0:T(2,128)S(1)} %get-tuple-element.58.refs_2_), channel_id=1, source_target_pairs={{0,2},{1,3},{2,0},{3,1},{4,6},{5,7},{6,4},{7,5},{8,10},{9,11},{10,... | collective-permute-start | bytes 3080 | tf_op jit(solution)/shard_map/ppermute | solution.py:352
  38.9 2.1 %collective-permute-start.14 = (f32[2,128]{1,0:T(2,128)S(1)}, f32[2,128]{1,0:T(2,128)S(1)}, u32[]{:S(2)}, u32[]{:S(2)}) collective-permute-start(f32[2,128]{1,0:T(2,128)S(1)} %get-tuple-element.58.refs_2_), channel_id=1, source_target_pairs={{0,1},{1,0},{2,3},{3,2},{4,5},{5,4},{6,7},{7,6},{8,9},{9,8},{10,11... | collective-permute-start | bytes 3080 | tf_op jit(solution)/shard_map/ppermute | solution.py:352
  42.5 3.1 %collective-permute-start.15 = (f32[2,512]{1,0:T(2,128)S(1)}, f32[2,512]{1,0:T(2,128)S(1)}, u32[]{:S(2)}, u32[]{:S(2)}) collective-permute-start(f32[2,512]{1,0:T(2,128)S(1)} %partial_weights.1.refs_2_), channel_id=1, source_target_pairs={{0,3},{1,2},{2,1},{3,0},{4,7},{5,6},{6,5},{7,4},{8,11},{9,10},{10,... | collective-permute-start | bytes 12296 | tf_op jit(solution)/shard_map/ppermute | solution.py:352
  43.0 3.6 %collective-permute-start.16 = (f32[2,512]{1,0:T(2,128)S(1)}, f32[2,512]{1,0:T(2,128)S(1)}, u32[]{:S(2)}, u32[]{:S(2)}) collective-permute-start(f32[2,512]{1,0:T(2,128)S(1)} %partial_weights.1.refs_2_), channel_id=1, source_target_pairs={{0,2},{1,3},{2,0},{3,1},{4,6},{5,7},{6,4},{7,5},{8,10},{9,11},{10,... | collective-permute-start | bytes 12296 | tf_op jit(solution)/shard_map/ppermute | solution.py:352
  44.8 1.9 %collective-permute-start.17 = (f32[2,512]{1,0:T(2,128)S(1)}, f32[2,512]{1,0:T(2,128)S(1)}, u32[]{:S(2)}, u32[]{:S(2)}) collective-permute-start(f32[2,512]{1,0:T(2,128)S(1)} %partial_weights.1.refs_2_), channel_id=1, source_target_pairs={{0,1},{1,0},{2,3},{3,2},{4,5},{5,4},{6,7},{7,6},{8,9},{9,8},{10,11... | collective-permute-start | bytes 12296 | tf_op jit(solution)/shard_map/ppermute | solution.py:352

commit v15 on v13

--- a/solution.py
+++ b/solution.py
@@ -383,8 +383,8 @@
             "pack_basis", 0, 2 * blocks * rows * BLK,
             [IN_SMEM, IN_HBM, IN_HBM], [pltpu.SemaphoreType.DMA((2 * halves,))],
         )(side, in_hbm(basis_act), in_hbm(basis_grad))
-        near = [shards[0], swap(shards[0], "dp", 1)]
-        far = {mask: swap(shards[-1], "dp", mask) for mask in range(pieces - 1, 1, -1)}
+        near = [shards[0]]
+        far = {mask: swap(shards[-1], "dp", mask) for mask in range(pieces - 1, 0, -1)}
     else:
         near = [
             jnp.concatenate(

time: 48.5 us -> 53.4 us (1.10)
  waiting for transfers between devices: 12.3 us -> 16.4 us
  starting transfers between devices: 23.7 us -> 24.4 us
    ppermute x16 -> x17, waiting for transfers between devices: 12.3 us -> 16.4 us  [swap(): return lax.ppermute(value, axis, [(i, i ^ mask) for i in range(count)])]
    ppermute x16 -> x17, starting transfers between devices: 19.7 us -> 20.4 us  [swap(): return lax.ppermute(value, axis, [(i, i ^ mask) for i in range(count)])]
  transfers between devices with their start and end apart: 18 -> 19, of which waited for: 9 -> 11; matrix products, arithmetic and copies ran while one was open for 0% -> 0% of each run, Pallas kernels for 19% -> 17%
where the time goes in v15:
time: 53.4 us; the launch traced here: 53.2 us
  starting transfers between devices  24.4 us (46%)
  waiting for transfers between devices  16.4 us (31%)
  Pallas kernels  11.6 us (22%)
  between operations  0.72 us (1%)
    ppermute x17, starting transfers between devices, swap(): return lax.ppermute(value, axis, [(i, i ^ mask) for i in range(count)])  20.4 us
    ppermute x17, waiting for transfers between devices, swap(): return lax.ppermute(value, axis, [(i, i ^ mask) for i in range(count)])  16.4 us
    pallas_call x1, Pallas kernels, local(): call(functools.partial(gram_kernel, pieces, coded, scale), [bf16(*activat...  4.56 us
    ppermute x1, starting transfers between devices, local(): relayed = lax.ppermute(sent[3], 'dp', [(0, 1), (3, 2)])  3.3 us
    pallas_call x2, Pallas kernels, local(): call(functools.partial(eigen_kernel, part, halves, masks, pieces, scale),...  1.95 us
    pallas_call x1, Pallas kernels, local(): call(functools.partial(weight_kernel, halves, act_blocks // halves), f32(...  1.49 us
    pallas_call x1, Pallas kernels, local(): call(functools.partial(last_add_kernel, [(None, 0, blocks)] * len(chunks)...  1.35 us
    pallas_call x1, Pallas kernels, local(): call(pack_kernel, [bf16(blocks // part, rows, BLK) for part in range(1, h...  1.08 us
  transfers between devices with their start and end apart: 19, of which 11 were waited for; matrix products, arithmetic and copies ran while one was open for 0% of the time, Pallas kernels for 17%

profile of v15, /device:TPU:0, one launch (start us, length us, event | category | flops | bytes accessed | tf_op | source)
XLA Modules:
  0.0 53.2 jit_solution(17035939859525720877)
XLA Ops:
  0.6 1.1 %pack_basis.1 = (bf16[36,32,128]{2,1,0:T(8,128)(2,1)S(1)}, bf16[18,32,128]{2,1,0:T(8,128)(2,1)S(1)}) custom-call(s32[1]{0:T(128)} %bitcast.side_ref, bf16[8,32,128]{2,1,0:T(8,128)(2,1)} %act_ref.1, bf16[28,32,128]{2,1,0:T(8,128)(2,1)} %grad_ref.1), custom_call_target="tpu_custom_call" | custom-call | bytes 294912 | tf_op jit(solution)/shard_map/pack_basis/pallas_call | solution.py:380
  1.7 5.1 %collective-permute-start = (bf16[18,32,128]{2,1,0:T(8,128)(2,1)S(1)}, bf16[18,32,128]{2,1,0:T(8,128)(2,1)S(1)}, u32[]{:S(2)}, u32[]{:S(2)}) collective-permute-start(bf16[18,32,128]{2,1,0:T(8,128)(2,1)S(1)} %get-tuple-element.42), channel_id=1, source_target_pairs={{0,12},{4,8},{8,4},{12,0},{1,13},{5,9},{9,5},{13,1},{2,14},{6,10},... | collective-permute-start | bytes 442376 | tf_op jit(solution)/shard_map/ppermute | solution.py:352
  6.8 0.0 collective-permute-start.2
  6.8 0.6 %collective-permute-start.4 = (bf16[18,32,128]{2,1,0:T(8,128)(2,1)S(1)}, bf16[18,32,128]{2,1,0:T(8,128)(2,1)S(1)}, u32[]{:S(2)}, u32[]{:S(2)}) collective-permute-start(bf16[18,32,128]{2,1,0:T(8,128)(2,1)S(1)} %get-tuple-element.42), channel_id=1, source_target_pairs={{0,4},{4,0},{8,12},{12,8},{1,5},{5,1},{9,13},{13,9},{2,6},{6,2},{1... | collective-permute-start | bytes 442376 | tf_op jit(solution)/shard_map/ppermute | solution.py:352
  7.5 4.6 %partial_gram.1 = (bf16[512,1024]{1,0:T(8,128)(2,1)S(1)}, bf16[512,3584]{1,0:T(8,128)(2,1)S(1)}, f32[36,32,128]{2,1,0:T(8,128)S(1)}, f32[36,32,128]{2,1,0:T(8,12...) custom-call(s32[1]{0:T(128)} %bitcast.1.me_ref, bf16[512,1024]{1,0:T(8,128)(2,1)} %act_hbm.1, ...), custom_call_target="tpu_custom_call" | custom-call | flops 1207959552 | bytes 4718592 | tf_op jit(solution)/shard_map/partial_gram/pallas_call | solution.py:401
  12.1 3.3 %collective-permute-start.10 = (bf16[1200,128]{1,0:T(8,128)(2,1)S(1)}, bf16[1200,128]{1,0:T(8,128)(2,1)S(1)}, u32[]{:S(2)}, u32[]{:S(2)}) collective-permute-start(bf16[1200,128]{1,0:T(8,128)(2,1)S(1)} %get-tuple-element.49), channel_id=1, source_target_pairs={{0,4},{12,8},{1,5},{13,9},{2,6},{14,10},{3,7},{15,11},{16,20},{28,... | collective-permute-start | bytes 921608 | tf_op jit(solution)/shard_map/ppermute | solution.py:423
  15.4 0.7 %collective-permute-start.9 = (bf16[1200,128]{1,0:T(8,128)(2,1)S(1)}, bf16[1200,128]{1,0:T(8,128)(2,1)S(1)}, u32[]{:S(2)}, u32[]{:S(2)}) collective-permute-start(bf16[1200,128]{1,0:T(8,128)(2,1)S(1)} %get-tuple-element.49), channel_id=1, source_target_pairs={{4,8},{8,4},{5,9},{9,5},{6,10},{10,6},{7,11},{11,7},{20,24},{24,20... | collective-permute-start | bytes 921608 | tf_op jit(solution)/shard_map/ppermute | solution.py:422
  16.1 4.2 %collective-permute-done.2.refs_2_ = bf16[18,32,128]{2,1,0:T(8,128)(2,1)S(1)} collective-permute-done((bf16[18,32,128]{2,1,0:T(8,128)(2,1)S(1)}, bf16[18,32,128]{2,1,0:T(8,128)(2,1)S(1)}, u32[]{:S(2)}, u32[]{:S(2)}) %collective-permute-start.2) | collective-permute-done | bytes 147488 | tf_op jit(solution)/shard_map/ppermute | solution.py:352
  20.3 1.5 %collective-permute-start.3 = (bf16[18,32,128]{2,1,0:T(8,128)(2,1)S(1)}, bf16[18,32,128]{2,1,0:T(8,128)(2,1)S(1)}, u32[]{:S(2)}, u32[]{:S(2)}) collective-permute-start(bf16[18,32,128]{2,1,0:T(8,128)(2,1)S(1)} %collective-permute-done.2.refs_2_), channel_id=1, source_target_pairs={{0,16},{16,0},{1,17},{17,1},{2,18},{18,2},{3,19},{19,3},{4,20},{20... | collective-permute-start | bytes 442376 | tf_op jit(solution)/shard_map/ppermute | solution.py:352
  21.8 0.0 collective-permute-done.4.refs_3_
  21.8 0.5 collective-permute-start.5
  22.3 0.0 collective-permute-done.refs_1_
  22.3 1.5 %collective-permute-start.1 = (bf16[18,32,128]{2,1,0:T(8,128)(2,1)S(1)}, bf16[18,32,128]{2,1,0:T(8,128)(2,1)S(1)}, u32[]{:S(2)}, u32[]{:S(2)}) collective-permute-start(bf16[18,32,128]{2,1,0:T(8,128)(2,1)S(1)} %collective-permute-done.refs_1_), channel_id=1, source_target_pairs={{0,16},{16,0},{1,17},{17,1},{2,18},{18,2},{3,19},{19,3},{4,20},{20... | collective-permute-start | bytes 442376 | tf_op jit(solution)/shard_map/ppermute | solution.py:352
  23.8 1.0 %partial_eigen.2 = (f32[9,512,256]{2,1,0:T(8,128)S(1)}, f32[18,128]{1,0:T(8,128)S(1)}) custom-call(s32[1]{0:T(128)} %bitcast.1.me_ref, s32[1]{0:T(128)} %bitcast.side_ref, bf16[512,1024]{1,0:T(8,128)(2,1)S(1)} %get-tuple-element.39.act_ref, bf16[512,3584]{1,0:T(8,128)(2,1)S(1)} %get-tuple-element.40.grad_ref, ...), custom_call_target="tpu_custom_call" | custom-call | flops 301989888 | bytes 2359296 | tf_op jit(solution)/shard_map/partial_eigen/pallas_call | solution.py:431
  24.8 2.2 %collective-permute-done.3.refs_2_ = bf16[18,32,128]{2,1,0:T(8,128)(2,1)S(1)} collective-permute-done((bf16[18,32,128]{2,1,0:T(8,128)(2,1)S(1)}, bf16[18,32,128]{2,1,0:T(8,128)(2,1)S(1)}, u32[]{:S(2)}, u32[]{:S(2)}) %collective-permute-start.3) | collective-permute-done | bytes 147488 | tf_op jit(solution)/shard_map/ppermute | solution.py:352
  27.1 1.9 %collective-permute-done.5.refs_3_ = bf16[18,32,128]{2,1,0:T(8,128)(2,1)S(1)} collective-permute-done((bf16[18,32,128]{2,1,0:T(8,128)(2,1)S(1)}, bf16[18,32,128]{2,1,0:T(8,128)(2,1)S(1)}, u32[]{:S(2)}, u32[]{:S(2)}) %collective-permute-start.5) | collective-permute-done | bytes 147488 | tf_op jit(solution)/shard_map/ppermute | solution.py:352
  29.0 1.6 %collective-permute-done.1.refs_1_ = bf16[18,32,128]{2,1,0:T(8,128)(2,1)S(1)} collective-permute-done((bf16[18,32,128]{2,1,0:T(8,128)(2,1)S(1)}, bf16[18,32,128]{2,1,0:T(8,128)(2,1)S(1)}, u32[]{:S(2)}, u32[]{:S(2)}) %collective-permute-start.1) | collective-permute-done | bytes 147488 | tf_op jit(solution)/shard_map/ppermute | solution.py:352
  30.5 1.0 %partial_eigen.3 = (f32[9,512,256]{2,1,0:T(8,128)S(1)}, f32[36,128]{1,0:T(8,128)S(1)}) custom-call(s32[1]{0:T(128)} %bitcast.1.me_ref, s32[1]{0:T(128)} %bitcast.side_ref, bf16[512,1024]{1,0:T(8,128)(2,1)S(1)} %get-tuple-element.39.act_ref, bf16[512,3584]{1,0:T(8,128)(2,1)S(1)} %get-tuple-element.40.grad_ref, ...), custom_call_target="tpu_custom_call" | custom-call | flops 301989888 | bytes 2359296 | tf_op jit(solution)/shard_map/partial_eigen/pallas_call | solution.py:431
  31.5 2.4 %collective-permute-start.6 = (f32[36,128]{1,0:T(8,128)S(1)}, f32[36,128]{1,0:T(8,128)S(1)}, u32[]{:S(2)}, u32[]{:S(2)}) collective-permute-start(f32[36,128]{1,0:T(8,128)S(1)} %get-tuple-element.53.refs_0_), channel_id=1, source_target_pairs={{0,12},{4,8},{8,4},{12,0},{1,13},{5,9},{9,5},{13,1},{2,14},{6,10},... | collective-permute-start | bytes 55304 | tf_op jit(solution)/shard_map/ppermute | solution.py:352
  33.9 0.0 collective-permute-start.7
  33.9 2.1 %collective-permute-start.8 = (f32[36,128]{1,0:T(8,128)S(1)}, f32[36,128]{1,0:T(8,128)S(1)}, u32[]{:S(2)}, u32[]{:S(2)}) collective-permute-start(f32[36,128]{1,0:T(8,128)S(1)} %get-tuple-element.53.refs_0_), channel_id=1, source_target_pairs={{0,4},{4,0},{8,12},{12,8},{1,5},{5,1},{9,13},{13,9},{2,6},{6,2},{1... | collective-permute-start | bytes 55304 | tf_op jit(solution)/shard_map/ppermute | solution.py:352
  36.0 0.0 collective-permute-done.10.relayed_ref
  36.0 0.6 %relay_chunk.1 = bf16[1200,128]{1,0:T(8,128)(2,1)S(1)} custom-call(f32[36,32,128]{2,1,0:T(8,128)S(1)} %get-tuple-element.51.far_ref, bf16[1200,128]{1,0:T(8,128)(2,1)S(1)} %collective-permute-done.10.relayed_ref), custom_call_target="tpu_custom_call" | custom-call | bytes 1769472 | tf_op jit(solution)/shard_map/relay_chunk/pallas_call | solution.py:440
  36.6 0.0 collective-permute-done.9.refs_0_
  36.6 0.7 %collective-permute-done.6.refs_1_ = f32[36,128]{1,0:T(8,128)S(1)} collective-permute-done((f32[36,128]{1,0:T(8,128)S(1)}, f32[36,128]{1,0:T(8,128)S(1)}, u32[]{:S(2)}, u32[]{:S(2)}) %collective-permute-start.6) | collective-permute-done | bytes 18464 | tf_op jit(solution)/shard_map/ppermute | solution.py:352
  37.3 1.4 %collective-permute-done.7.refs_2_ = f32[36,128]{1,0:T(8,128)S(1)} collective-permute-done((f32[36,128]{1,0:T(8,128)S(1)}, f32[36,128]{1,0:T(8,128)S(1)}, u32[]{:S(2)}, u32[]{:S(2)}) %collective-permute-start.7) | collective-permute-done | bytes 18464 | tf_op jit(solution)/shard_map/ppermute | solution.py:352
  38.7 0.0 collective-permute-done.8.refs_3_
  38.7 1.4 %collective-permute-start.12 = (bf16[1200,128]{1,0:T(8,128)(2,1)S(1)}, bf16[1200,128]{1,0:T(8,128)(2,1)S(1)}, u32[]{:S(2)}, u32[]{:S(2)}) collective-permute-start(bf16[1200,128]{1,0:T(8,128)(2,1)S(1)} %get-tuple-element.62), channel_id=1, source_target_pairs={{0,4},{4,0},{8,12},{12,8},{1,5},{5,1},{9,13},{13,9},{2,6},{6,2},{1... | collective-permute-start | bytes 921608 | tf_op jit(solution)/shard_map/ppermute | solution.py:352
  40.1 1.1 %collective-permute-start.11 = (bf16[1200,128]{1,0:T(8,128)(2,1)S(1)}, bf16[1200,128]{1,0:T(8,128)(2,1)S(1)}, u32[]{:S(2)}, u32[]{:S(2)}) collective-permute-start(bf16[1200,128]{1,0:T(8,128)(2,1)S(1)} %relay_chunk.1), channel_id=1, source_target_pairs={{0,8},{4,12},{8,0},{12,4},{1,9},{5,13},{9,1},{13,5},{2,10},{6,14},... | collective-permute-start | bytes 921608 | tf_op jit(solution)/shard_map/ppermute | solution.py:352
  41.2 0.0 collective-permute-start.13
  41.2 1.5 %collective-permute-start.14 = (f32[2,128]{1,0:T(2,128)S(1)}, f32[2,128]{1,0:T(2,128)S(1)}, u32[]{:S(2)}, u32[]{:S(2)}) collective-permute-start(f32[2,128]{1,0:T(2,128)S(1)} %get-tuple-element.59.refs_2_), channel_id=1, source_target_pairs={{0,2},{1,3},{2,0},{3,1},{4,6},{5,7},{6,4},{7,5},{8,10},{9,11},{10,... | collective-permute-start | bytes 3080 | tf_op jit(solution)/shard_map/ppermute | solution.py:352
  42.7 0.3 collective-permute-start.15
  43.0 1.1 %collective-permute-done.13.refs_3_ = f32[2,128]{1,0:T(2,128)S(1)} collective-permute-done((f32[2,128]{1,0:T(2,128)S(1)}, f32[2,128]{1,0:T(2,128)S(1)}, u32[]{:S(2)}, u32[]{:S(2)}) %collective-permute-start.13) | collective-permute-done | bytes 1056 | tf_op jit(solution)/shard_map/ppermute | solution.py:352
  44.2 0.6 %collective-permute-done.14.refs_4_ = f32[2,128]{1,0:T(2,128)S(1)} collective-permute-done((f32[2,128]{1,0:T(2,128)S(1)}, f32[2,128]{1,0:T(2,128)S(1)}, u32[]{:S(2)}, u32[]{:S(2)}) %collective-permute-start.14) | collective-permute-done | bytes 1056 | tf_op jit(solution)/shard_map/ppermute | solution.py:352
  44.8 0.0 collective-permute-done.15.refs_5_
  44.8 1.5 %partial_weights.1.refs_2_ = f32[2,512]{1,0:T(2,128)S(1)} custom-call(f32[36,128]{1,0:T(8,128)S(1)} %get-tuple-element.57.eigen_ref, f32[9,512,256]{2,1,0:T(8,128)S(1)} %get-tuple-element.63.refs_0_, f32[9,512,256]{2,1,0:T(8,128)S(1)} %get-tuple-element.64.refs_1_, f32[2,128]{1,0:T(2,128)S(1)} %get-tuple-element.59.refs_2_, ...), custom_call_target="tpu_custom_call" | custom-call | bytes 9437184 | tf_op jit(solution)/shard_map/partial_weights/pallas_call | solution.py:458
  46.3 0.9 %collective-permute-start.16 = (f32[2,512]{1,0:T(2,128)S(1)}, f32[2,512]{1,0:T(2,128)S(1)}, u32[]{:S(2)}, u32[]{:S(2)}) collective-permute-start(f32[2,512]{1,0:T(2,128)S(1)} %partial_weights.1.refs_2_), channel_id=1, source_target_pairs={{0,3},{1,2},{2,1},{3,0},{4,7},{5,6},{6,5},{7,4},{8,11},{9,10},{10,... | collective-permute-start | bytes 12296 | tf_op jit(solution)/shard_map/ppermute | solution.py:352
  47.2 1.5 %collective-permute-start.17 = (f32[2,512]{1,0:T(2,128)S(1)}, f32[2,512]{1,0:T(2,128)S(1)}, u32[]{:S(2)}, u32[]{:S(2)}) collective-permute-start(f32[2,512]{1,0:T(2,128)S(1)} %partial_weights.1.refs_2_), channel_id=1, source_target_pairs={{0,2},{1,3},{2,0},{3,1},{4,6},{5,7},{6,4},{7,5},{8,10},{9,11},{10,... | collective-permute-start | bytes 12296 | tf_op jit(solution)/shard_map/ppermute | solution.py:352
  48.6 0.0 collective-permute-start.18
  48.6 0.6 %add_chunk.1 = (f32[36,32,128]{2,1,0:T(8,128)S(1)}, f32[8,128]{1,0:T(8,128)}, f32[28,128]{1,0:T(8,128)}) custom-call(s32[1]{0:T(128)} %bitcast.side_ref, f32[36,128]{1,0:T(8,128)S(1)} %get-tuple-element.57.eigen_ref, f32[36,32,128]{2,1,0:T(8,128)S(1)} %get-tuple-element.43.own_ref, bf16[1200,128]{1,0:T(8,128)(2,1)S(1)} %collective-permute-done.9.refs_0_), custom_call_target="tpu_custom_call" | custom-call | bytes 1769472 | tf_op jit(solution)/shard_map/add_chunk/pallas_call | solution.py:475
  49.3 0.1 collective-permute-done.16.refs_3_
  49.3 1.4 %collective-permute-done.17.refs_4_ = f32[2,512]{1,0:T(2,128)S(1)} collective-permute-done((f32[2,512]{1,0:T(2,128)S(1)}, f32[2,512]{1,0:T(2,128)S(1)}, u32[]{:S(2)}, u32[]{:S(2)}) %collective-permute-start.17) | collective-permute-done | bytes 4128 | tf_op jit(solution)/shard_map/ppermute | solution.py:352
  50.8 0.0 collective-permute-done.18.refs_5_
  50.8 0.0 collective-permute-done.12.refs_1_
  50.8 1.1 %collective-permute-done.11.refs_0_ = bf16[1200,128]{1,0:T(8,128)(2,1)S(1)} collective-permute-done((bf16[1200,128]{1,0:T(8,128)(2,1)S(1)}, bf16[1200,128]{1,0:T(8,128)(2,1)S(1)}, u32[]{:S(2)}, u32[]{:S(2)}) %collective-permute-start.11) | collective-permute-done | bytes 307232 | tf_op jit(solution)/shard_map/ppermute | solution.py:352
  51.9 1.4 %last_sums.1 = (f32[8,32,128]{2,1,0:T(8,128)}, f32[28,32,128]{2,1,0:T(8,128)}, f32[1,512]{1,0:T(1,128)}) custom-call(f32[36,32,128]{2,1,0:T(8,128)S(1)} %get-tuple-element.58.own_ref, bf16[1200,128]{1,0:T(8,128)(2,1)S(1)} %collective-permute-done.11.refs_0_, bf16[1200,128]{1,0:T(8,128)(2,1)S(1)} %collective-permute-done.12.refs_1_, ...), custom_call_target="tpu_custom_call" | custom-call | bytes 2359296 | tf_op jit(solution)/shard_map/last_sums/pallas_call | solution.py:488
  (1 shorter events, 0.0 us)
Async XLA Ops:
  1.7 20.6 %collective-permute-start = (bf16[18,32,128]{2,1,0:T(8,128)(2,1)S(1)}, bf16[18,32,128]{2,1,0:T(8,128)(2,1)S(1)}, u32[]{:S(2)}, u32[]{:S(2)}) collective-permute-start(bf16[18,32,128]{2,1,0:T(8,128)(2,1)S(1)} %get-tuple-element.42), channel_id=1, source_target_pairs={{0,12},{4,8},{8,4},{12,0},{1,13},{5,9},{9,5},{13,1},{2,14},{6,10},... | collective-permute-start | bytes 442376 | tf_op jit(solution)/shard_map/ppermute | solution.py:352
  6.8 13.4 %collective-permute-start.2 = (bf16[18,32,128]{2,1,0:T(8,128)(2,1)S(1)}, bf16[18,32,128]{2,1,0:T(8,128)(2,1)S(1)}, u32[]{:S(2)}, u32[]{:S(2)}) collective-permute-start(bf16[18,32,128]{2,1,0:T(8,128)(2,1)S(1)} %get-tuple-element.42), channel_id=1, source_target_pairs={{0,8},{4,12},{8,0},{12,4},{1,9},{5,13},{9,1},{13,5},{2,10},{6,14},... | collective-permute-start | bytes 442376 | tf_op jit(solution)/shard_map/ppermute | solution.py:352
  6.8 15.0 %collective-permute-start.4 = (bf16[18,32,128]{2,1,0:T(8,128)(2,1)S(1)}, bf16[18,32,128]{2,1,0:T(8,128)(2,1)S(1)}, u32[]{:S(2)}, u32[]{:S(2)}) collective-permute-start(bf16[18,32,128]{2,1,0:T(8,128)(2,1)S(1)} %get-tuple-element.42), channel_id=1, source_target_pairs={{0,4},{4,0},{8,12},{12,8},{1,5},{5,1},{9,13},{13,9},{2,6},{6,2},{1... | collective-permute-start | bytes 442376 | tf_op jit(solution)/shard_map/ppermute | solution.py:352
  12.1 23.9 %collective-permute-start.10 = (bf16[1200,128]{1,0:T(8,128)(2,1)S(1)}, bf16[1200,128]{1,0:T(8,128)(2,1)S(1)}, u32[]{:S(2)}, u32[]{:S(2)}) collective-permute-start(bf16[1200,128]{1,0:T(8,128)(2,1)S(1)} %get-tuple-element.49), channel_id=1, source_target_pairs={{0,4},{12,8},{1,5},{13,9},{2,6},{14,10},{3,7},{15,11},{16,20},{28,... | collective-permute-start | bytes 921608 | tf_op jit(solution)/shard_map/ppermute | solution.py:423
  15.4 21.2 %collective-permute-start.9 = (bf16[1200,128]{1,0:T(8,128)(2,1)S(1)}, bf16[1200,128]{1,0:T(8,128)(2,1)S(1)}, u32[]{:S(2)}, u32[]{:S(2)}) collective-permute-start(bf16[1200,128]{1,0:T(8,128)(2,1)S(1)} %get-tuple-element.49), channel_id=1, source_target_pairs={{4,8},{8,4},{5,9},{9,5},{6,10},{10,6},{7,11},{11,7},{20,24},{24,20... | collective-permute-start | bytes 921608 | tf_op jit(solution)/shard_map/ppermute | solution.py:422
  20.3 6.8 %collective-permute-start.3 = (bf16[18,32,128]{2,1,0:T(8,128)(2,1)S(1)}, bf16[18,32,128]{2,1,0:T(8,128)(2,1)S(1)}, u32[]{:S(2)}, u32[]{:S(2)}) collective-permute-start(bf16[18,32,128]{2,1,0:T(8,128)(2,1)S(1)} %collective-permute-done.2.refs_2_), channel_id=1, source_target_pairs={{0,16},{16,0},{1,17},{17,1},{2,18},{18,2},{3,19},{19,3},{4,20},{20... | collective-permute-start | bytes 442376 | tf_op jit(solution)/shard_map/ppermute | solution.py:352
  21.8 7.2 %collective-permute-start.5 = (bf16[18,32,128]{2,1,0:T(8,128)(2,1)S(1)}, bf16[18,32,128]{2,1,0:T(8,128)(2,1)S(1)}, u32[]{:S(2)}, u32[]{:S(2)}) collective-permute-start(bf16[18,32,128]{2,1,0:T(8,128)(2,1)S(1)} %collective-permute-done.4.refs_3_), channel_id=1, source_target_pairs={{0,16},{16,0},{1,17},{17,1},{2,18},{18,2},{3,19},{19,3},{4,20},{20... | collective-permute-start | bytes 442376 | tf_op jit(solution)/shard_map/ppermute | solution.py:352
  22.3 8.2 %collective-permute-start.1 = (bf16[18,32,128]{2,1,0:T(8,128)(2,1)S(1)}, bf16[18,32,128]{2,1,0:T(8,128)(2,1)S(1)}, u32[]{:S(2)}, u32[]{:S(2)}) collective-permute-start(bf16[18,32,128]{2,1,0:T(8,128)(2,1)S(1)} %collective-permute-done.refs_1_), channel_id=1, source_target_pairs={{0,16},{16,0},{1,17},{17,1},{2,18},{18,2},{3,19},{19,3},{4,20},{20... | collective-permute-start | bytes 442376 | tf_op jit(solution)/shard_map/ppermute | solution.py:352
  31.5 5.8 %collective-permute-start.6 = (f32[36,128]{1,0:T(8,128)S(1)}, f32[36,128]{1,0:T(8,128)S(1)}, u32[]{:S(2)}, u32[]{:S(2)}) collective-permute-start(f32[36,128]{1,0:T(8,128)S(1)} %get-tuple-element.53.refs_0_), channel_id=1, source_target_pairs={{0,12},{4,8},{8,4},{12,0},{1,13},{5,9},{9,5},{13,1},{2,14},{6,10},... | collective-permute-start | bytes 55304 | tf_op jit(solution)/shard_map/ppermute | solution.py:352
  33.9 4.8 %collective-permute-start.7 = (f32[36,128]{1,0:T(8,128)S(1)}, f32[36,128]{1,0:T(8,128)S(1)}, u32[]{:S(2)}, u32[]{:S(2)}) collective-permute-start(f32[36,128]{1,0:T(8,128)S(1)} %get-tuple-element.53.refs_0_), channel_id=1, source_target_pairs={{0,8},{4,12},{8,0},{12,4},{1,9},{5,13},{9,1},{13,5},{2,10},{6,14},... | collective-permute-start | bytes 55304 | tf_op jit(solution)/shard_map/ppermute | solution.py:352
  33.9 4.8 %collective-permute-start.8 = (f32[36,128]{1,0:T(8,128)S(1)}, f32[36,128]{1,0:T(8,128)S(1)}, u32[]{:S(2)}, u32[]{:S(2)}) collective-permute-start(f32[36,128]{1,0:T(8,128)S(1)} %get-tuple-element.53.refs_0_), channel_id=1, source_target_pairs={{0,4},{4,0},{8,12},{12,8},{1,5},{5,1},{9,13},{13,9},{2,6},{6,2},{1... | collective-permute-start | bytes 55304 | tf_op jit(solution)/shard_map/ppermute | solution.py:352
  38.7 12.0 %collective-permute-start.12 = (bf16[1200,128]{1,0:T(8,128)(2,1)S(1)}, bf16[1200,128]{1,0:T(8,128)(2,1)S(1)}, u32[]{:S(2)}, u32[]{:S(2)}) collective-permute-start(bf16[1200,128]{1,0:T(8,128)(2,1)S(1)} %get-tuple-element.62), channel_id=1, source_target_pairs={{0,4},{4,0},{8,12},{12,8},{1,5},{5,1},{9,13},{13,9},{2,6},{6,2},{1... | collective-permute-start | bytes 921608 | tf_op jit(solution)/shard_map/ppermute | solution.py:352
  40.1 11.7 %collective-permute-start.11 = (bf16[1200,128]{1,0:T(8,128)(2,1)S(1)}, bf16[1200,128]{1,0:T(8,128)(2,1)S(1)}, u32[]{:S(2)}, u32[]{:S(2)}) collective-permute-start(bf16[1200,128]{1,0:T(8,128)(2,1)S(1)} %relay_chunk.1), channel_id=1, source_target_pairs={{0,8},{4,12},{8,0},{12,4},{1,9},{5,13},{9,1},{13,5},{2,10},{6,14},... | collective-permute-start | bytes 921608 | tf_op jit(solution)/shard_map/ppermute | solution.py:352
  41.2 3.0 %collective-permute-start.13 = (f32[2,128]{1,0:T(2,128)S(1)}, f32[2,128]{1,0:T(2,128)S(1)}, u32[]{:S(2)}, u32[]{:S(2)}) collective-permute-start(f32[2,128]{1,0:T(2,128)S(1)} %get-tuple-element.59.refs_2_), channel_id=1, source_target_pairs={{0,3},{1,2},{2,1},{3,0},{4,7},{5,6},{6,5},{7,4},{8,11},{9,10},{10,... | collective-permute-start | bytes 3080 | tf_op jit(solution)/shard_map/ppermute | solution.py:352
  41.2 3.6 %collective-permute-start.14 = (f32[2,128]{1,0:T(2,128)S(1)}, f32[2,128]{1,0:T(2,128)S(1)}, u32[]{:S(2)}, u32[]{:S(2)}) collective-permute-start(f32[2,128]{1,0:T(2,128)S(1)} %get-tuple-element.59.refs_2_), channel_id=1, source_target_pairs={{0,2},{1,3},{2,0},{3,1},{4,6},{5,7},{6,4},{7,5},{8,10},{9,11},{10,... | collective-permute-start | bytes 3080 | tf_op jit(solution)/shard_map/ppermute | solution.py:352
  42.7 2.1 %collective-permute-start.15 = (f32[2,128]{1,0:T(2,128)S(1)}, f32[2,128]{1,0:T(2,128)S(1)}, u32[]{:S(2)}, u32[]{:S(2)}) collective-permute-start(f32[2,128]{1,0:T(2,128)S(1)} %get-tuple-element.59.refs_2_), channel_id=1, source_target_pairs={{0,1},{1,0},{2,3},{3,2},{4,5},{5,4},{6,7},{7,6},{8,9},{9,8},{10,11... | collective-permute-start | bytes 3080 | tf_op jit(solution)/shard_map/ppermute | solution.py:352
  46.3 3.1 %collective-permute-start.16 = (f32[2,512]{1,0:T(2,128)S(1)}, f32[2,512]{1,0:T(2,128)S(1)}, u32[]{:S(2)}, u32[]{:S(2)}) collective-permute-start(f32[2,512]{1,0:T(2,128)S(1)} %partial_weights.1.refs_2_), channel_id=1, source_target_pairs={{0,3},{1,2},{2,1},{3,0},{4,7},{5,6},{6,5},{7,4},{8,11},{9,10},{10,... | collective-permute-start | bytes 12296 | tf_op jit(solution)/shard_map/ppermute | solution.py:352
  47.2 3.6 %collective-permute-start.17 = (f32[2,512]{1,0:T(2,128)S(1)}, f32[2,512]{1,0:T(2,128)S(1)}, u32[]{:S(2)}, u32[]{:S(2)}) collective-permute-start(f32[2,512]{1,0:T(2,128)S(1)} %partial_weights.1.refs_2_), channel_id=1, source_target_pairs={{0,2},{1,3},{2,0},{3,1},{4,6},{5,7},{6,4},{7,5},{8,10},{9,11},{10,... | collective-permute-start | bytes 12296 | tf_op jit(solution)/shard_map/ppermute | solution.py:352
  48.6 2.1 %collective-permute-start.18 = (f32[2,512]{1,0:T(2,128)S(1)}, f32[2,512]{1,0:T(2,128)S(1)}, u32[]{:S(2)}, u32[]{:S(2)}) collective-permute-start(f32[2,512]{1,0:T(2,128)S(1)} %partial_weights.1.refs_2_), channel_id=1, source_target_pairs={{0,1},{1,0},{2,3},{3,2},{4,5},{5,4},{6,7},{7,6},{8,9},{9,8},{10,11... | collective-permute-start | bytes 12296 | tf_op jit(solution)/shard_map/ppermute | solution.py:352

commit v16 on v14

--- a/solution.py
+++ b/solution.py
@@ -178,7 +178,8 @@
             sum_ref[block] = total
 
 
-def relay_kernel(message, far_ref, relayed_ref, sent_ref, relayed_tops, tops):
+def relay_kernel(message, core_ref, far_ref, relayed_ref, near_ref, first_ref, second_ref, *refs):
+    summed, relayed_tops, tops = refs
     messages = (message,)
     blocks, rows, _ = far_ref.shape
     load_tops(messages, rows, (relayed_ref,), (relayed_tops,))
@@ -189,8 +190,18 @@
         ):
             top = top_of(total)
             tops[block : block + 1, :] = top
-            sent_ref[block * rows : (block + 1) * rows, :] = encode(total * (CODE_TOP / top))
-    sent_ref[blocks * rows :, :] = tops[...].astype(jnp.bfloat16)
+            summed[block * rows : (block + 1) * rows, :] = encode(total * (CODE_TOP / top))
+    summed[blocks * rows :, :] = tops[...].astype(jnp.bfloat16)
+
+    @pl.when(core_ref[0] == 0)
+    def _():
+        first_ref[...] = summed[...]
+        second_ref[...] = near_ref[...]
+
+    @pl.when(core_ref[0] != 0)
+    def _():
+        first_ref[...] = near_ref[...]
+        second_ref[...] = summed[...]
 
 
 def last_add_kernel(messages, owners, own_ref, *refs):
@@ -437,23 +448,33 @@
         )(me, side, act_here, grad_here, *shards, *sums)
         powers.append(power)
     if pieces == 4:
-        sent[2] = call(
-            functools.partial(relay_kernel, coded[0]), message, "relay_chunk", 0, 12 * own.size,
-            [IN_VMEM, IN_VMEM],
-            [pltpu.VMEM((scale_rows(0, blocks), BLK), jnp.float32)] * 2,
-        )(*after([grams[1], relayed], sums))
+        core = jnp.full((1,), lax.axis_index("owner") % 2, jnp.int32)
+        far_chunk, relayed = after([grams[1], relayed], sums)
+        late = call(
+            functools.partial(relay_kernel, coded[0]), [message] * 2, "relay_chunk", 0, 16 * own.size,
+            [IN_SMEM, IN_VMEM, IN_VMEM, IN_VMEM],
+            [pltpu.VMEM(message.shape, jnp.bfloat16)]
+            + [pltpu.VMEM((scale_rows(0, blocks), BLK), jnp.float32)] * 2,
+        )(core, far_chunk, relayed, sent[1])
     sums = share(sums[0], "dp", direct)
     if pieces == 4:
-        sums = after(sums, (middle, sent[2]))
+        sums = after(sums, (middle, late))
     eigen, totals = call(
         functools.partial(combine_kernel, halves, act_blocks // halves),
         [f32(blocks, BLK), f32(2, BLK)],
         "combine_eigen", 0, 4 * blocks * BLK * pieces, [IN_VMEM] * len(sums),
     )(*sums)
-    arrived = {}
-    sent.pop(3, None)
-    for mask in sent:
-        arrived[mask] = swap(after([sent[mask]], totals)[0], "dp", mask)
+    chunks = []
+    if pieces == 4:
+        for chunk, order in zip(late, ((2, 1), (1, 2))):
+            ways = [
+                (at * owners + owner, (at ^ order[owner % 2]) * owners + owner)
+                for at in range(dp)
+                for owner in range(owners)
+            ]
+            chunks.append(lax.ppermute(after([chunk], totals)[0], ("dp", "owner"), ways))
+    elif pieces == 2:
+        chunks.append(swap(after([sent[1]], totals)[0], "dp", 1))
     totals = share(totals, "owner", direct)
     weights = call(
         functools.partial(weight_kernel, halves, act_blocks // halves),
@@ -483,7 +504,7 @@
             functools.partial(order_kernel, halves), eigens, "order_eigen", 0,
             8 * blocks * BLK, [IN_SMEM, IN_VMEM],
         )(side, eigen)
-    chunks = list(arrived.values())
+    chunks = chunks[::-1]
     if chunks:
         *covariance, token_scores = call(
             functools.partial(last_add_kernel, [(None, 0, blocks)] * len(chunks), len(weights)),

time: 48.9 us -> 54 us (1.10)
  local copies, waits for them, and re-layouts: 0 us -> 8.99 us
  waiting for transfers between devices: 14.7 us -> 8.74 us
  starting transfers between devices: 21.7 us -> 23.8 us
    unnamed x0 -> x8, local copies, waits for them, and re-layouts: none -> 8.99 us
    ppermute x16 -> x14, waiting for transfers between devices: 14.7 us -> 8.72 us  [swap(): return lax.ppermute(value, axis, [(i, i ^ mask) for i in range(count)])]
    ppermute x0 -> x2, starting transfers between devices: none -> 2.29 us  [local(): lax.ppermute(after([chunk], totals)[0], ('dp', 'owner'), ways)]
    ppermute x16 -> x14, starting transfers between devices: 17.7 us -> 17.5 us  [swap(): return lax.ppermute(value, axis, [(i, i ^ mask) for i in range(count)])]
  transfers between devices with their start and end apart: 18 -> 18, of which waited for: 10 -> 8; matrix products, arithmetic and copies ran while one was open for 0% -> 0% of each run, Pallas kernels for 19% -> 17%
where the time goes in v16:
time: 54 us; the launch traced here: 53.8 us
  starting transfers between devices  23.8 us (44%)
  Pallas kernels  11.6 us (21%)
  local copies, waits for them, and re-layouts  8.99 us (17%)
  waiting for transfers between devices  8.74 us (16%)
  between operations  0.75 us (1%)
    ppermute x14, starting transfers between devices, swap(): return lax.ppermute(value, axis, [(i, i ^ mask) for i in range(count)])  17.5 us
    unnamed x8, local copies, waits for them, and re-layouts  8.99 us
    ppermute x14, waiting for transfers between devices, swap(): return lax.ppermute(value, axis, [(i, i ^ mask) for i in range(count)])  8.72 us
    pallas_call x1, Pallas kernels, local(): call(functools.partial(gram_kernel, pieces, coded, scale), [bf16(*activat...  4.56 us
    ppermute x1, starting transfers between devices, local(): relayed = lax.ppermute(sent[3], 'dp', [(0, 1), (3, 2)])  3.32 us
    ppermute x2, starting transfers between devices, local(): lax.ppermute(after([chunk], totals)[0], ('dp', 'owner'), ways)  2.29 us
    pallas_call x2, Pallas kernels, local(): call(functools.partial(eigen_kernel, part, halves, masks, pieces, scale),...  1.94 us
    pallas_call x1, Pallas kernels, local(): call(functools.partial(weight_kernel, halves, act_blocks // halves), f32(...  1.37 us
  transfers between devices with their start and end apart: 18, of which 8 were waited for; matrix products, arithmetic and copies ran while one was open for 0% of the time, Pallas kernels for 17%

profile of v16, /device:TPU:0, one launch (start us, length us, event | category | flops | bytes accessed | tf_op | source)
XLA Modules:
  0.0 53.8 jit_solution(8104224713526274398)
XLA Ops:
  0.6 1.1 %pack_basis.1 = (bf16[36,32,128]{2,1,0:T(8,128)(2,1)S(1)}, bf16[18,32,128]{2,1,0:T(8,128)(2,1)S(1)}) custom-call(s32[1]{0:T(128)} %bitcast.side_ref, bf16[8,32,128]{2,1,0:T(8,128)(2,1)} %act_ref.1, bf16[28,32,128]{2,1,0:T(8,128)(2,1)} %grad_ref.1), custom_call_target="tpu_custom_call" | custom-call | bytes 294912 | tf_op jit(solution)/shard_map/pack_basis/pallas_call | solution.py:391
  1.7 5.1 %collective-permute-start.1 = (bf16[18,32,128]{2,1,0:T(8,128)(2,1)S(1)}, bf16[18,32,128]{2,1,0:T(8,128)(2,1)S(1)}, u32[]{:S(2)}, u32[]{:S(2)}) collective-permute-start(bf16[18,32,128]{2,1,0:T(8,128)(2,1)S(1)} %get-tuple-element.43), channel_id=1, source_target_pairs={{0,12},{4,8},{8,4},{12,0},{1,13},{5,9},{9,5},{13,1},{2,14},{6,10},... | collective-permute-start | bytes 442376 | tf_op jit(solution)/shard_map/ppermute | solution.py:363
  6.8 0.0 collective-permute-start.3
  6.8 0.6 %collective-permute-start = (bf16[36,32,128]{2,1,0:T(8,128)(2,1)S(1)}, bf16[36,32,128]{2,1,0:T(8,128)(2,1)S(1)}, u32[]{:S(2)}, u32[]{:S(2)}) collective-permute-start(bf16[36,32,128]{2,1,0:T(8,128)(2,1)S(1)} %get-tuple-element.42.refs_0_), channel_id=1, source_target_pairs={{0,4},{4,0},{8,12},{12,8},{1,5},{5,1},{9,13},{13,9},{2,6},{6,2},{1... | collective-permute-start | bytes 884744 | tf_op jit(solution)/shard_map/ppermute | solution.py:363
  7.5 4.6 %partial_gram.1 = (bf16[512,1024]{1,0:T(8,128)(2,1)S(1)}, bf16[512,3584]{1,0:T(8,128)(2,1)S(1)}, f32[36,32,128]{2,1,0:T(8,128)S(1)}, f32[36,32,128]{2,1,0:T(8,12...) custom-call(s32[1]{0:T(128)} %bitcast.1.me_ref, bf16[512,1024]{1,0:T(8,128)(2,1)} %act_hbm.1, ...), custom_call_target="tpu_custom_call" | custom-call | flops 1207959552 | bytes 4718592 | tf_op jit(solution)/shard_map/partial_gram/pallas_call | solution.py:412
  12.0 3.3 %collective-permute-start.9 = (bf16[1200,128]{1,0:T(8,128)(2,1)S(1)}, bf16[1200,128]{1,0:T(8,128)(2,1)S(1)}, u32[]{:S(2)}, u32[]{:S(2)}) collective-permute-start(bf16[1200,128]{1,0:T(8,128)(2,1)S(1)} %get-tuple-element.49), channel_id=1, source_target_pairs={{0,4},{12,8},{1,5},{13,9},{2,6},{14,10},{3,7},{15,11},{16,20},{28,... | collective-permute-start | bytes 921608 | tf_op jit(solution)/shard_map/ppermute | solution.py:434
  15.4 0.7 %collective-permute-start.8 = (bf16[1200,128]{1,0:T(8,128)(2,1)S(1)}, bf16[1200,128]{1,0:T(8,128)(2,1)S(1)}, u32[]{:S(2)}, u32[]{:S(2)}) collective-permute-start(bf16[1200,128]{1,0:T(8,128)(2,1)S(1)} %get-tuple-element.49), channel_id=1, source_target_pairs={{4,8},{8,4},{5,9},{9,5},{6,10},{10,6},{7,11},{11,7},{20,24},{24,20... | collective-permute-start | bytes 921608 | tf_op jit(solution)/shard_map/ppermute | solution.py:433
  16.1 0.0 collective-permute-done.1.refs_2_
  16.1 1.6 %collective-permute-start.2 = (bf16[18,32,128]{2,1,0:T(8,128)(2,1)S(1)}, bf16[18,32,128]{2,1,0:T(8,128)(2,1)S(1)}, u32[]{:S(2)}, u32[]{:S(2)}) collective-permute-start(bf16[18,32,128]{2,1,0:T(8,128)(2,1)S(1)} %collective-permute-done.1.refs_2_), channel_id=1, source_target_pairs={{0,16},{16,0},{1,17},{17,1},{2,18},{18,2},{3,19},{19,3},{4,20},{20... | collective-permute-start | bytes 442376 | tf_op jit(solution)/shard_map/ppermute | solution.py:363
  17.6 2.7 %collective-permute-done.3.refs_3_ = bf16[18,32,128]{2,1,0:T(8,128)(2,1)S(1)} collective-permute-done((bf16[18,32,128]{2,1,0:T(8,128)(2,1)S(1)}, bf16[18,32,128]{2,1,0:T(8,128)(2,1)S(1)}, u32[]{:S(2)}, u32[]{:S(2)}) %collective-permute-start.3) | collective-permute-done | bytes 147488 | tf_op jit(solution)/shard_map/ppermute | solution.py:363
  20.3 1.5 %collective-permute-start.4 = (bf16[18,32,128]{2,1,0:T(8,128)(2,1)S(1)}, bf16[18,32,128]{2,1,0:T(8,128)(2,1)S(1)}, u32[]{:S(2)}, u32[]{:S(2)}) collective-permute-start(bf16[18,32,128]{2,1,0:T(8,128)(2,1)S(1)} %collective-permute-done.3.refs_3_), channel_id=1, source_target_pairs={{0,16},{16,0},{1,17},{17,1},{2,18},{18,2},{3,19},{19,3},{4,20},{20... | collective-permute-start | bytes 442376 | tf_op jit(solution)/shard_map/ppermute | solution.py:363
  21.8 0.0 collective-permute-done.refs_1_
  21.8 1.0 %partial_eigen.2 = (f32[9,512,256]{2,1,0:T(8,128)S(1)}, f32[18,128]{1,0:T(8,128)S(1)}) custom-call(s32[1]{0:T(128)} %bitcast.1.me_ref, s32[1]{0:T(128)} %bitcast.side_ref, bf16[512,1024]{1,0:T(8,128)(2,1)S(1)} %get-tuple-element.40.act_ref, bf16[512,3584]{1,0:T(8,128)(2,1)S(1)} %get-tuple-element.41.grad_ref, ...), custom_call_target="tpu_custom_call" | custom-call | flops 301989888 | bytes 2359296 | tf_op jit(solution)/shard_map/partial_eigen/pallas_call | solution.py:442
  22.8 0.0 copy-start
  22.8 2.1 %copy-done = f32[9,512,256]{2,1,0:T(8,128)} copy-done((f32[9,512,256]{2,1,0:T(8,128)}, f32[9,512,256]{2,1,0:T(8,128)S(1)}, u32[]{:S(2)}) %copy-start) | copy-done | bytes 4718616
  25.0 0.0 collective-permute-done.2.refs_2_
  25.0 0.5 collective-permute-done.4.refs_3_
  25.5 1.0 %partial_eigen.3 = (f32[9,512,256]{2,1,0:T(8,128)S(1)}, f32[36,128]{1,0:T(8,128)S(1)}) custom-call(s32[1]{0:T(128)} %bitcast.1.me_ref, s32[1]{0:T(128)} %bitcast.side_ref, bf16[512,1024]{1,0:T(8,128)(2,1)S(1)} %get-tuple-element.40.act_ref, bf16[512,3584]{1,0:T(8,128)(2,1)S(1)} %get-tuple-element.41.grad_ref, ...), custom_call_target="tpu_custom_call" | custom-call | flops 301989888 | bytes 2359296 | tf_op jit(solution)/shard_map/partial_eigen/pallas_call | solution.py:442
  26.4 0.0 copy-start.2
  26.5 2.2 %copy-done.2 = f32[9,512,256]{2,1,0:T(8,128)} copy-done((f32[9,512,256]{2,1,0:T(8,128)}, f32[9,512,256]{2,1,0:T(8,128)S(1)}, u32[]{:S(2)}) %copy-start.2) | copy-done | bytes 4718616
  28.6 2.7 %collective-permute-start.5 = (f32[36,128]{1,0:T(8,128)S(1)}, f32[36,128]{1,0:T(8,128)S(1)}, u32[]{:S(2)}, u32[]{:S(2)}) collective-permute-start(f32[36,128]{1,0:T(8,128)S(1)} %get-tuple-element.56.refs_0_), channel_id=1, source_target_pairs={{0,12},{4,8},{8,4},{12,0},{1,13},{5,9},{9,5},{13,1},{2,14},{6,10},... | collective-permute-start | bytes 55304 | tf_op jit(solution)/shard_map/ppermute | solution.py:363
  31.3 0.0 collective-permute-start.6
  31.3 1.7 %collective-permute-start.7 = (f32[36,128]{1,0:T(8,128)S(1)}, f32[36,128]{1,0:T(8,128)S(1)}, u32[]{:S(2)}, u32[]{:S(2)}) collective-permute-start(f32[36,128]{1,0:T(8,128)S(1)} %get-tuple-element.56.refs_0_), channel_id=1, source_target_pairs={{0,4},{4,0},{8,12},{12,8},{1,5},{5,1},{9,13},{13,9},{2,6},{6,2},{1... | collective-permute-start | bytes 55304 | tf_op jit(solution)/shard_map/ppermute | solution.py:363
  33.0 0.0 collective-permute-done.9.relayed_ref
  33.0 0.6 %relay_chunk.1 = (bf16[1200,128]{1,0:T(8,128)(2,1)S(1)}, bf16[1200,128]{1,0:T(8,128)(2,1)S(1)}) custom-call(s32[1]{0:T(128)} %bitcast.2.core_ref, f32[36,32,128]{2,1,0:T(8,128)S(1)} %get-tuple-element.51.far_ref, bf16[1200,128]{1,0:T(8,128)(2,1)S(1)} %collective-permute-done.9.relayed_ref, bf16[1200,128]{1,0:T(8,128)(2,1)S(1)} %get-tuple-element.53.near_ref), custom_call_target="tpu_custom_call" | custom-call | bytes 2359296 | tf_op jit(solution)/shard_map/relay_chunk/pallas_call | solution.py:453
  33.7 0.0 collective-permute-done.8.refs_0_
  33.7 0.5 %collective-permute-done.5.refs_1_ = f32[36,128]{1,0:T(8,128)S(1)} collective-permute-done((f32[36,128]{1,0:T(8,128)S(1)}, f32[36,128]{1,0:T(8,128)S(1)}, u32[]{:S(2)}, u32[]{:S(2)}) %collective-permute-start.5) | collective-permute-done | bytes 18464 | tf_op jit(solution)/shard_map/ppermute | solution.py:363
  34.2 1.8 %collective-permute-done.6.refs_2_ = f32[36,128]{1,0:T(8,128)S(1)} collective-permute-done((f32[36,128]{1,0:T(8,128)S(1)}, f32[36,128]{1,0:T(8,128)S(1)}, u32[]{:S(2)}, u32[]{:S(2)}) %collective-permute-start.6) | collective-permute-done | bytes 18464 | tf_op jit(solution)/shard_map/ppermute | solution.py:363
  36.0 0.0 collective-permute-done.7.refs_3_
  36.0 2.3 %collective-permute-start.11 = (bf16[1200,128]{1,0:T(8,128)(2,1)S(1)}, bf16[1200,128]{1,0:T(8,128)(2,1)S(1)}, u32[]{:S(2)}, u32[]{:S(2)}) collective-permute-start(bf16[1200,128]{1,0:T(8,128)(2,1)S(1)} %get-tuple-element.64), channel_id=1, source_target_pairs={{0,8},{1,5},{2,10},{3,7},{4,12},{5,1},{6,14},{7,3},{8,0},{9,13},{1... | collective-permute-start | bytes 921608 | tf_op jit(solution)/shard_map/ppermute | solution.py:475
  38.3 0.0 collective-permute-start.10
  38.3 0.0 collective-permute-start.12
  38.3 1.5 %collective-permute-start.13 = (f32[2,128]{1,0:T(2,128)S(1)}, f32[2,128]{1,0:T(2,128)S(1)}, u32[]{:S(2)}, u32[]{:S(2)}) collective-permute-start(f32[2,128]{1,0:T(2,128)S(1)} %get-tuple-element.62.refs_2_), channel_id=1, source_target_pairs={{0,2},{1,3},{2,0},{3,1},{4,6},{5,7},{6,4},{7,5},{8,10},{9,11},{10,... | collective-permute-start | bytes 3080 | tf_op jit(solution)/shard_map/ppermute | solution.py:363
  39.8 0.3 collective-permute-start.14
  40.2 1.1 %collective-permute-done.12.refs_3_ = f32[2,128]{1,0:T(2,128)S(1)} collective-permute-done((f32[2,128]{1,0:T(2,128)S(1)}, f32[2,128]{1,0:T(2,128)S(1)}, u32[]{:S(2)}, u32[]{:S(2)}) %collective-permute-start.12) | collective-permute-done | bytes 1056 | tf_op jit(solution)/shard_map/ppermute | solution.py:363
  41.3 0.6 %collective-permute-done.13.refs_4_ = f32[2,128]{1,0:T(2,128)S(1)} collective-permute-done((f32[2,128]{1,0:T(2,128)S(1)}, f32[2,128]{1,0:T(2,128)S(1)}, u32[]{:S(2)}, u32[]{:S(2)}) %collective-permute-start.13) | collective-permute-done | bytes 1056 | tf_op jit(solution)/shard_map/ppermute | solution.py:363
  41.9 0.0 collective-permute-done.14.refs_5_
  41.9 0.0 copy-start.1
  41.9 2.3 %copy-done.1 = f32[9,512,256]{2,1,0:T(8,128)S(1)} copy-done((f32[9,512,256]{2,1,0:T(8,128)S(1)}, f32[9,512,256]{2,1,0:T(8,128)}, u32[]{:S(2)}) %copy-start.1) | copy-done | bytes 4718616
  44.2 0.0 copy-start.3
  44.2 2.3 %copy-done.3 = f32[9,512,256]{2,1,0:T(8,128)S(1)} copy-done((f32[9,512,256]{2,1,0:T(8,128)S(1)}, f32[9,512,256]{2,1,0:T(8,128)}, u32[]{:S(2)}) %copy-start.3) | copy-done | bytes 4718616
  46.6 1.4 %partial_weights.1.refs_2_ = f32[2,512]{1,0:T(2,128)S(1)} custom-call(f32[36,128]{1,0:T(8,128)S(1)} %get-tuple-element.60.eigen_ref, f32[9,512,256]{2,1,0:T(8,128)S(1)} %copy-done.1, f32[9,512,256]{2,1,0:T(8,128)S(1)} %copy-done.3, f32[2,128]{1,0:T(2,128)S(1)} %get-tuple-element.62.refs_2_, f32[2,128]{1,0:T(2,128)S(1)} %collective-permute-done.12.refs_3_, ...), custom_call_target="tpu_custom_call" | custom-call | bytes 9437184 | tf_op jit(solution)/shard_map/partial_weights/pallas_call | solution.py:479
  47.9 0.9 %collective-permute-start.15 = (f32[2,512]{1,0:T(2,128)S(1)}, f32[2,512]{1,0:T(2,128)S(1)}, u32[]{:S(2)}, u32[]{:S(2)}) collective-permute-start(f32[2,512]{1,0:T(2,128)S(1)} %partial_weights.1.refs_2_), channel_id=1, source_target_pairs={{0,3},{1,2},{2,1},{3,0},{4,7},{5,6},{6,5},{7,4},{8,11},{9,10},{10,... | collective-permute-start | bytes 12296 | tf_op jit(solution)/shard_map/ppermute | solution.py:363
  48.8 1.5 %collective-permute-start.16 = (f32[2,512]{1,0:T(2,128)S(1)}, f32[2,512]{1,0:T(2,128)S(1)}, u32[]{:S(2)}, u32[]{:S(2)}) collective-permute-start(f32[2,512]{1,0:T(2,128)S(1)} %partial_weights.1.refs_2_), channel_id=1, source_target_pairs={{0,2},{1,3},{2,0},{3,1},{4,6},{5,7},{6,4},{7,5},{8,10},{9,11},{10,... | collective-permute-start | bytes 12296 | tf_op jit(solution)/shard_map/ppermute | solution.py:363
  50.3 0.0 collective-permute-start.17
  50.3 0.6 %add_chunk.1 = (f32[36,32,128]{2,1,0:T(8,128)S(1)}, f32[8,128]{1,0:T(8,128)}, f32[28,128]{1,0:T(8,128)}) custom-call(s32[1]{0:T(128)} %bitcast.side_ref, f32[36,128]{1,0:T(8,128)S(1)} %get-tuple-element.60.eigen_ref, f32[36,32,128]{2,1,0:T(8,128)S(1)} %get-tuple-element.44.own_ref, bf16[1200,128]{1,0:T(8,128)(2,1)S(1)} %collective-permute-done.8.refs_0_), custom_call_target="tpu_custom_call" | custom-call | bytes 1769472 | tf_op jit(solution)/shard_map/add_chunk/pallas_call | solution.py:496
  50.9 0.1 collective-permute-done.15.refs_3_
  51.0 1.4 %collective-permute-done.16.refs_4_ = f32[2,512]{1,0:T(2,128)S(1)} collective-permute-done((f32[2,512]{1,0:T(2,128)S(1)}, f32[2,512]{1,0:T(2,128)S(1)}, u32[]{:S(2)}, u32[]{:S(2)}) %collective-permute-start.16) | collective-permute-done | bytes 4128 | tf_op jit(solution)/shard_map/ppermute | solution.py:363
  52.4 0.0 collective-permute-done.17.refs_5_
  52.4 0.0 collective-permute-done.11.refs_1_
  52.4 0.0 collective-permute-done.10.refs_0_
  52.4 1.4 %last_sums.1 = (f32[8,32,128]{2,1,0:T(8,128)}, f32[28,32,128]{2,1,0:T(8,128)}, f32[1,512]{1,0:T(1,128)}) custom-call(f32[36,32,128]{2,1,0:T(8,128)S(1)} %get-tuple-element.61.own_ref, bf16[1200,128]{1,0:T(8,128)(2,1)S(1)} %collective-permute-done.10.refs_0_, bf16[1200,128]{1,0:T(8,128)(2,1)S(1)} %collective-permute-done.11.refs_1_, ...), custom_call_target="tpu_custom_call" | custom-call | bytes 2359296 | tf_op jit(solution)/shard_map/last_sums/pallas_call | solution.py:509
  (1 shorter events, 0.0 us)
Async XLA Ops:
  1.7 14.3 %collective-permute-start.1 = (bf16[18,32,128]{2,1,0:T(8,128)(2,1)S(1)}, bf16[18,32,128]{2,1,0:T(8,128)(2,1)S(1)}, u32[]{:S(2)}, u32[]{:S(2)}) collective-permute-start(bf16[18,32,128]{2,1,0:T(8,128)(2,1)S(1)} %get-tuple-element.43), channel_id=1, source_target_pairs={{0,12},{4,8},{8,4},{12,0},{1,13},{5,9},{9,5},{13,1},{2,14},{6,10},... | collective-permute-start | bytes 442376 | tf_op jit(solution)/shard_map/ppermute | solution.py:363
  6.8 13.5 %collective-permute-start.3 = (bf16[18,32,128]{2,1,0:T(8,128)(2,1)S(1)}, bf16[18,32,128]{2,1,0:T(8,128)(2,1)S(1)}, u32[]{:S(2)}, u32[]{:S(2)}) collective-permute-start(bf16[18,32,128]{2,1,0:T(8,128)(2,1)S(1)} %get-tuple-element.43), channel_id=1, source_target_pairs={{0,8},{4,12},{8,0},{12,4},{1,9},{5,13},{9,1},{13,5},{2,10},{6,14},... | collective-permute-start | bytes 442376 | tf_op jit(solution)/shard_map/ppermute | solution.py:363
  6.8 15.0 %collective-permute-start = (bf16[36,32,128]{2,1,0:T(8,128)(2,1)S(1)}, bf16[36,32,128]{2,1,0:T(8,128)(2,1)S(1)}, u32[]{:S(2)}, u32[]{:S(2)}) collective-permute-start(bf16[36,32,128]{2,1,0:T(8,128)(2,1)S(1)} %get-tuple-element.42.refs_0_), channel_id=1, source_target_pairs={{0,4},{4,0},{8,12},{12,8},{1,5},{5,1},{9,13},{13,9},{2,6},{6,2},{1... | collective-permute-start | bytes 884744 | tf_op jit(solution)/shard_map/ppermute | solution.py:363
  12.0 21.0 %collective-permute-start.9 = (bf16[1200,128]{1,0:T(8,128)(2,1)S(1)}, bf16[1200,128]{1,0:T(8,128)(2,1)S(1)}, u32[]{:S(2)}, u32[]{:S(2)}) collective-permute-start(bf16[1200,128]{1,0:T(8,128)(2,1)S(1)} %get-tuple-element.49), channel_id=1, source_target_pairs={{0,4},{12,8},{1,5},{13,9},{2,6},{14,10},{3,7},{15,11},{16,20},{28,... | collective-permute-start | bytes 921608 | tf_op jit(solution)/shard_map/ppermute | solution.py:434
  15.4 18.3 %collective-permute-start.8 = (bf16[1200,128]{1,0:T(8,128)(2,1)S(1)}, bf16[1200,128]{1,0:T(8,128)(2,1)S(1)}, u32[]{:S(2)}, u32[]{:S(2)}) collective-permute-start(bf16[1200,128]{1,0:T(8,128)(2,1)S(1)} %get-tuple-element.49), channel_id=1, source_target_pairs={{4,8},{8,4},{5,9},{9,5},{6,10},{10,6},{7,11},{11,7},{20,24},{24,20... | collective-permute-start | bytes 921608 | tf_op jit(solution)/shard_map/ppermute | solution.py:433
  16.1 8.9 %collective-permute-start.2 = (bf16[18,32,128]{2,1,0:T(8,128)(2,1)S(1)}, bf16[18,32,128]{2,1,0:T(8,128)(2,1)S(1)}, u32[]{:S(2)}, u32[]{:S(2)}) collective-permute-start(bf16[18,32,128]{2,1,0:T(8,128)(2,1)S(1)} %collective-permute-done.1.refs_2_), channel_id=1, source_target_pairs={{0,16},{16,0},{1,17},{17,1},{2,18},{18,2},{3,19},{19,3},{4,20},{20... | collective-permute-start | bytes 442376 | tf_op jit(solution)/shard_map/ppermute | solution.py:363
  20.3 5.1 %collective-permute-start.4 = (bf16[18,32,128]{2,1,0:T(8,128)(2,1)S(1)}, bf16[18,32,128]{2,1,0:T(8,128)(2,1)S(1)}, u32[]{:S(2)}, u32[]{:S(2)}) collective-permute-start(bf16[18,32,128]{2,1,0:T(8,128)(2,1)S(1)} %collective-permute-done.3.refs_3_), channel_id=1, source_target_pairs={{0,16},{16,0},{1,17},{17,1},{2,18},{18,2},{3,19},{19,3},{4,20},{20... | collective-permute-start | bytes 442376 | tf_op jit(solution)/shard_map/ppermute | solution.py:363
  22.8 2.1 %copy-start = (f32[9,512,256]{2,1,0:T(8,128)}, f32[9,512,256]{2,1,0:T(8,128)S(1)}, u32[]{:S(2)}) copy-start(f32[9,512,256]{2,1,0:T(8,128)S(1)} %get-tuple-element.65.refs_0_) | copy-start | bytes 14155780
  26.4 2.2 %copy-start.2 = (f32[9,512,256]{2,1,0:T(8,128)}, f32[9,512,256]{2,1,0:T(8,128)S(1)}, u32[]{:S(2)}) copy-start(f32[9,512,256]{2,1,0:T(8,128)S(1)} %get-tuple-element.66.refs_1_) | copy-start | bytes 14155780
  28.6 5.6 %collective-permute-start.5 = (f32[36,128]{1,0:T(8,128)S(1)}, f32[36,128]{1,0:T(8,128)S(1)}, u32[]{:S(2)}, u32[]{:S(2)}) collective-permute-start(f32[36,128]{1,0:T(8,128)S(1)} %get-tuple-element.56.refs_0_), channel_id=1, source_target_pairs={{0,12},{4,8},{8,4},{12,0},{1,13},{5,9},{9,5},{13,1},{2,14},{6,10},... | collective-permute-start | bytes 55304 | tf_op jit(solution)/shard_map/ppermute | solution.py:363
  31.3 4.7 %collective-permute-start.6 = (f32[36,128]{1,0:T(8,128)S(1)}, f32[36,128]{1,0:T(8,128)S(1)}, u32[]{:S(2)}, u32[]{:S(2)}) collective-permute-start(f32[36,128]{1,0:T(8,128)S(1)} %get-tuple-element.56.refs_0_), channel_id=1, source_target_pairs={{0,8},{4,12},{8,0},{12,4},{1,9},{5,13},{9,1},{13,5},{2,10},{6,14},... | collective-permute-start | bytes 55304 | tf_op jit(solution)/shard_map/ppermute | solution.py:363
  31.3 4.7 %collective-permute-start.7 = (f32[36,128]{1,0:T(8,128)S(1)}, f32[36,128]{1,0:T(8,128)S(1)}, u32[]{:S(2)}, u32[]{:S(2)}) collective-permute-start(f32[36,128]{1,0:T(8,128)S(1)} %get-tuple-element.56.refs_0_), channel_id=1, source_target_pairs={{0,4},{4,0},{8,12},{12,8},{1,5},{5,1},{9,13},{13,9},{2,6},{6,2},{1... | collective-permute-start | bytes 55304 | tf_op jit(solution)/shard_map/ppermute | solution.py:363
  36.0 16.4 %collective-permute-start.11 = (bf16[1200,128]{1,0:T(8,128)(2,1)S(1)}, bf16[1200,128]{1,0:T(8,128)(2,1)S(1)}, u32[]{:S(2)}, u32[]{:S(2)}) collective-permute-start(bf16[1200,128]{1,0:T(8,128)(2,1)S(1)} %get-tuple-element.64), channel_id=1, source_target_pairs={{0,8},{1,5},{2,10},{3,7},{4,12},{5,1},{6,14},{7,3},{8,0},{9,13},{1... | collective-permute-start | bytes 921608 | tf_op jit(solution)/shard_map/ppermute | solution.py:475
  38.3 14.1 %collective-permute-start.10 = (bf16[1200,128]{1,0:T(8,128)(2,1)S(1)}, bf16[1200,128]{1,0:T(8,128)(2,1)S(1)}, u32[]{:S(2)}, u32[]{:S(2)}) collective-permute-start(bf16[1200,128]{1,0:T(8,128)(2,1)S(1)} %get-tuple-element.63), channel_id=1, source_target_pairs={{0,4},{1,9},{2,6},{3,11},{4,0},{5,13},{6,2},{7,15},{8,12},{9,1},{1... | collective-permute-start | bytes 921608 | tf_op jit(solution)/shard_map/ppermute | solution.py:475
  38.3 3.0 %collective-permute-start.12 = (f32[2,128]{1,0:T(2,128)S(1)}, f32[2,128]{1,0:T(2,128)S(1)}, u32[]{:S(2)}, u32[]{:S(2)}) collective-permute-start(f32[2,128]{1,0:T(2,128)S(1)} %get-tuple-element.62.refs_2_), channel_id=1, source_target_pairs={{0,3},{1,2},{2,1},{3,0},{4,7},{5,6},{6,5},{7,4},{8,11},{9,10},{10,... | collective-permute-start | bytes 3080 | tf_op jit(solution)/shard_map/ppermute | solution.py:363
  38.3 3.6 %collective-permute-start.13 = (f32[2,128]{1,0:T(2,128)S(1)}, f32[2,128]{1,0:T(2,128)S(1)}, u32[]{:S(2)}, u32[]{:S(2)}) collective-permute-start(f32[2,128]{1,0:T(2,128)S(1)} %get-tuple-element.62.refs_2_), channel_id=1, source_target_pairs={{0,2},{1,3},{2,0},{3,1},{4,6},{5,7},{6,4},{7,5},{8,10},{9,11},{10,... | collective-permute-start | bytes 3080 | tf_op jit(solution)/shard_map/ppermute | solution.py:363
  39.8 2.1 %collective-permute-start.14 = (f32[2,128]{1,0:T(2,128)S(1)}, f32[2,128]{1,0:T(2,128)S(1)}, u32[]{:S(2)}, u32[]{:S(2)}) collective-permute-start(f32[2,128]{1,0:T(2,128)S(1)} %get-tuple-element.62.refs_2_), channel_id=1, source_target_pairs={{0,1},{1,0},{2,3},{3,2},{4,5},{5,4},{6,7},{7,6},{8,9},{9,8},{10,11... | collective-permute-start | bytes 3080 | tf_op jit(solution)/shard_map/ppermute | solution.py:363
  41.9 2.3 %copy-start.1 = (f32[9,512,256]{2,1,0:T(8,128)S(1)}, f32[9,512,256]{2,1,0:T(8,128)}, u32[]{:S(2)}) copy-start(f32[9,512,256]{2,1,0:T(8,128)} %copy-done) | copy-start | bytes 14155780
  44.2 2.3 %copy-start.3 = (f32[9,512,256]{2,1,0:T(8,128)S(1)}, f32[9,512,256]{2,1,0:T(8,128)}, u32[]{:S(2)}) copy-start(f32[9,512,256]{2,1,0:T(8,128)} %copy-done.2) | copy-start | bytes 14155780
  47.9 3.1 %collective-permute-start.15 = (f32[2,512]{1,0:T(2,128)S(1)}, f32[2,512]{1,0:T(2,128)S(1)}, u32[]{:S(2)}, u32[]{:S(2)}) collective-permute-start(f32[2,512]{1,0:T(2,128)S(1)} %partial_weights.1.refs_2_), channel_id=1, source_target_pairs={{0,3},{1,2},{2,1},{3,0},{4,7},{5,6},{6,5},{7,4},{8,11},{9,10},{10,... | collective-permute-start | bytes 12296 | tf_op jit(solution)/shard_map/ppermute | solution.py:363
  48.8 3.6 %collective-permute-start.16 = (f32[2,512]{1,0:T(2,128)S(1)}, f32[2,512]{1,0:T(2,128)S(1)}, u32[]{:S(2)}, u32[]{:S(2)}) collective-permute-start(f32[2,512]{1,0:T(2,128)S(1)} %partial_weights.1.refs_2_), channel_id=1, source_target_pairs={{0,2},{1,3},{2,0},{3,1},{4,6},{5,7},{6,4},{7,5},{8,10},{9,11},{10,... | collective-permute-start | bytes 12296 | tf_op jit(solution)/shard_map/ppermute | solution.py:363
  50.3 2.1 %collective-permute-start.17 = (f32[2,512]{1,0:T(2,128)S(1)}, f32[2,512]{1,0:T(2,128)S(1)}, u32[]{:S(2)}, u32[]{:S(2)}) collective-permute-start(f32[2,512]{1,0:T(2,128)S(1)} %partial_weights.1.refs_2_), channel_id=1, source_target_pairs={{0,1},{1,0},{2,3},{3,2},{4,5},{5,4},{6,7},{7,6},{8,9},{9,8},{10,11... | collective-permute-start | bytes 12296 | tf_op jit(solution)/shard_map/ppermute | solution.py:363

commit v17 on v16

--- a/solution.py
+++ b/solution.py
@@ -82,7 +82,7 @@
     return jnp.where(coded > 0.0, root, jnp.where(coded < 0.0, -root, 0.0))
 
 
-def pack_kernel(side_ref, act_ref, grad_ref, *refs):
+def pack_kernel(side_ref, owner_ref, act_ref, grad_ref, *refs):
     *out_refs, sems = refs
     side = side_ref[0]
     blocks = out_refs[0].shape[0]
@@ -178,7 +178,7 @@
             sum_ref[block] = total
 
 
-def relay_kernel(message, core_ref, far_ref, relayed_ref, near_ref, first_ref, second_ref, *refs):
+def relay_kernel(message, owner_ref, far_ref, relayed_ref, near_ref, first_ref, second_ref, *refs):
     summed, relayed_tops, tops = refs
     messages = (message,)
     blocks, rows, _ = far_ref.shape
@@ -193,12 +193,14 @@
             summed[block * rows : (block + 1) * rows, :] = encode(total * (CODE_TOP / top))
     summed[blocks * rows :, :] = tops[...].astype(jnp.bfloat16)
 
-    @pl.when(core_ref[0] == 0)
+    core = owner_ref[0] & 1
+
+    @pl.when(core == 0)
     def _():
         first_ref[...] = summed[...]
         second_ref[...] = near_ref[...]
 
-    @pl.when(core_ref[0] != 0)
+    @pl.when(core != 0)
     def _():
         first_ref[...] = near_ref[...]
         second_ref[...] = summed[...]
@@ -385,6 +387,7 @@
     rows = BLK // pieces
     me = jnp.full((1,), lax.axis_index("dp") if direct else 0, jnp.int32)
     side = jnp.full((1,), lax.axis_index("groups"), jnp.int32)
+    owner = jnp.full((1,), lax.axis_index("owner"), jnp.int32)
     macs = tokens * blocks * BLK * BLK
     input_bytes = 2 * tokens * blocks * BLK
     if direct:
@@ -392,8 +395,8 @@
             pack_kernel,
             [bf16(blocks // part, rows, BLK) for part in range(1, halves + 1)],
             "pack_basis", 0, 2 * blocks * rows * BLK,
-            [IN_SMEM, IN_HBM, IN_HBM], [pltpu.SemaphoreType.DMA((2 * halves,))],
-        )(side, in_hbm(basis_act), in_hbm(basis_grad))
+            [IN_SMEM, IN_SMEM, IN_HBM, IN_HBM], [pltpu.SemaphoreType.DMA((2 * halves,))],
+        )(side, owner, in_hbm(basis_act), in_hbm(basis_grad))
         near = [shards[0], swap(shards[0], "dp", 1)]
         far = {mask: swap(shards[-1], "dp", mask) for mask in range(pieces - 1, 1, -1)}
     else:
@@ -448,14 +451,13 @@
         )(me, side, act_here, grad_here, *shards, *sums)
         powers.append(power)
     if pieces == 4:
-        core = jnp.full((1,), lax.axis_index("owner") % 2, jnp.int32)
         far_chunk, relayed = after([grams[1], relayed], sums)
         late = call(
             functools.partial(relay_kernel, coded[0]), [message] * 2, "relay_chunk", 0, 16 * own.size,
             [IN_SMEM, IN_VMEM, IN_VMEM, IN_VMEM],
             [pltpu.VMEM(message.shape, jnp.bfloat16)]
             + [pltpu.VMEM((scale_rows(0, blocks), BLK), jnp.float32)] * 2,
-        )(core, far_chunk, relayed, sent[1])
+        )(owner, far_chunk, relayed, sent[1])
     sums = share(sums[0], "dp", direct)
     if pieces == 4:
         sums = after(sums, (middle, late))

time: 54 us -> 48.5 us (0.90)
  local copies, waits for them, and re-layouts: 8.99 us -> 0 us
  waiting for transfers between devices: 8.74 us -> 12.2 us
    unnamed x8 -> x0, local copies, waits for them, and re-layouts: 8.99 us -> none
    ppermute x14, waiting for transfers between devices: 8.72 us -> 10.9 us  [swap(): return lax.ppermute(value, axis, [(i, i ^ mask) for i in range(count)])]
    ppermute x2, waiting for transfers between devices: 0.01 us -> 1.29 us  [local(): lax.ppermute(after([chunk], totals)[0], ('dp', 'owner'), ways)]
  transfers between devices with their start and end apart: 18 -> 18, of which waited for: 8 -> 9; matrix products, arithmetic and copies ran while one was open for 0% -> 0% of each run, Pallas kernels for 17% -> 19%
where the time goes in v17:
time: 48.5 us; the launch traced here: 48.3 us
  starting transfers between devices  23.6 us (49%)
  waiting for transfers between devices  12.2 us (25%)
  Pallas kernels  11.7 us (24%)
  between operations  0.74 us (2%)
    ppermute x14, starting transfers between devices, swap(): return lax.ppermute(value, axis, [(i, i ^ mask) for i in range(count)])  17.5 us
    ppermute x14, waiting for transfers between devices, swap(): return lax.ppermute(value, axis, [(i, i ^ mask) for i in range(count)])  10.9 us
    pallas_call x1, Pallas kernels, local(): call(functools.partial(gram_kernel, pieces, coded, scale), [bf16(*activat...  4.56 us
    ppermute x1, starting transfers between devices, local(): relayed = lax.ppermute(sent[3], 'dp', [(0, 1), (3, 2)])  3.32 us
    ppermute x2, starting transfers between devices, local(): lax.ppermute(after([chunk], totals)[0], ('dp', 'owner'), ways)  2.11 us
    pallas_call x2, Pallas kernels, local(): call(functools.partial(eigen_kernel, part, halves, masks, pieces, scale),...  1.95 us
    pallas_call x1, Pallas kernels, local(): call(functools.partial(weight_kernel, halves, act_blocks // halves), f32(...  1.49 us
    pallas_call x1, Pallas kernels, local(): call(functools.partial(last_add_kernel, [(None, 0, blocks)] * len(chunks)...  1.35 us
  transfers between devices with their start and end apart: 18, of which 9 were waited for; matrix products, arithmetic and copies ran while one was open for 0% of the time, Pallas kernels for 19%

profile of v17, /device:TPU:0, one launch (start us, length us, event | category | flops | bytes accessed | tf_op | source)
XLA Modules:
  0.0 48.3 jit_solution(17306044552136254730)
XLA Ops:
  0.6 1.1 %pack_basis.1 = (bf16[36,32,128]{2,1,0:T(8,128)(2,1)S(1)}, bf16[18,32,128]{2,1,0:T(8,128)(2,1)S(1)}) custom-call(s32[1]{0:T(128)} %bitcast.side_ref, s32[1]{0:T(128)} %bitcast.2.owner_ref, bf16[8,32,128]{2,1,0:T(8,128)(2,1)} %act_ref.1, bf16[28,32,128]{2,1,0:T(8,128)(2,1)} %grad_ref.1), custom_call_target="tpu_custom_call" | custom-call | bytes 294912 | tf_op jit(solution)/shard_map/pack_basis/pallas_call | solution.py:394
  1.7 5.1 %collective-permute-start.1 = (bf16[18,32,128]{2,1,0:T(8,128)(2,1)S(1)}, bf16[18,32,128]{2,1,0:T(8,128)(2,1)S(1)}, u32[]{:S(2)}, u32[]{:S(2)}) collective-permute-start(bf16[18,32,128]{2,1,0:T(8,128)(2,1)S(1)} %get-tuple-element.43), channel_id=1, source_target_pairs={{0,12},{4,8},{8,4},{12,0},{1,13},{5,9},{9,5},{13,1},{2,14},{6,10},... | collective-permute-start | bytes 442376 | tf_op jit(solution)/shard_map/ppermute | solution.py:365
  6.8 0.0 collective-permute-start.3
  6.8 0.6 %collective-permute-start = (bf16[36,32,128]{2,1,0:T(8,128)(2,1)S(1)}, bf16[36,32,128]{2,1,0:T(8,128)(2,1)S(1)}, u32[]{:S(2)}, u32[]{:S(2)}) collective-permute-start(bf16[36,32,128]{2,1,0:T(8,128)(2,1)S(1)} %get-tuple-element.42.refs_0_), channel_id=1, source_target_pairs={{0,4},{4,0},{8,12},{12,8},{1,5},{5,1},{9,13},{13,9},{2,6},{6,2},{1... | collective-permute-start | bytes 884744 | tf_op jit(solution)/shard_map/ppermute | solution.py:365
  7.5 4.6 %partial_gram.1 = (bf16[512,1024]{1,0:T(8,128)(2,1)S(1)}, bf16[512,3584]{1,0:T(8,128)(2,1)S(1)}, f32[36,32,128]{2,1,0:T(8,128)S(1)}, f32[36,32,128]{2,1,0:T(8,12...) custom-call(s32[1]{0:T(128)} %bitcast.1.me_ref, bf16[512,1024]{1,0:T(8,128)(2,1)} %act_hbm.1, ...), custom_call_target="tpu_custom_call" | custom-call | flops 1207959552 | bytes 4718592 | tf_op jit(solution)/shard_map/partial_gram/pallas_call | solution.py:415
  12.0 3.3 %collective-permute-start.9 = (bf16[1200,128]{1,0:T(8,128)(2,1)S(1)}, bf16[1200,128]{1,0:T(8,128)(2,1)S(1)}, u32[]{:S(2)}, u32[]{:S(2)}) collective-permute-start(bf16[1200,128]{1,0:T(8,128)(2,1)S(1)} %get-tuple-element.49), channel_id=1, source_target_pairs={{0,4},{12,8},{1,5},{13,9},{2,6},{14,10},{3,7},{15,11},{16,20},{28,... | collective-permute-start | bytes 921608 | tf_op jit(solution)/shard_map/ppermute | solution.py:437
  15.4 0.7 %collective-permute-start.8 = (bf16[1200,128]{1,0:T(8,128)(2,1)S(1)}, bf16[1200,128]{1,0:T(8,128)(2,1)S(1)}, u32[]{:S(2)}, u32[]{:S(2)}) collective-permute-start(bf16[1200,128]{1,0:T(8,128)(2,1)S(1)} %get-tuple-element.49), channel_id=1, source_target_pairs={{4,8},{8,4},{5,9},{9,5},{6,10},{10,6},{7,11},{11,7},{20,24},{24,20... | collective-permute-start | bytes 921608 | tf_op jit(solution)/shard_map/ppermute | solution.py:436
  16.1 0.0 collective-permute-done.1.refs_2_
  16.1 1.6 %collective-permute-start.2 = (bf16[18,32,128]{2,1,0:T(8,128)(2,1)S(1)}, bf16[18,32,128]{2,1,0:T(8,128)(2,1)S(1)}, u32[]{:S(2)}, u32[]{:S(2)}) collective-permute-start(bf16[18,32,128]{2,1,0:T(8,128)(2,1)S(1)} %collective-permute-done.1.refs_2_), channel_id=1, source_target_pairs={{0,16},{16,0},{1,17},{17,1},{2,18},{18,2},{3,19},{19,3},{4,20},{20... | collective-permute-start | bytes 442376 | tf_op jit(solution)/shard_map/ppermute | solution.py:365
  17.6 2.7 %collective-permute-done.3.refs_3_ = bf16[18,32,128]{2,1,0:T(8,128)(2,1)S(1)} collective-permute-done((bf16[18,32,128]{2,1,0:T(8,128)(2,1)S(1)}, bf16[18,32,128]{2,1,0:T(8,128)(2,1)S(1)}, u32[]{:S(2)}, u32[]{:S(2)}) %collective-permute-start.3) | collective-permute-done | bytes 147488 | tf_op jit(solution)/shard_map/ppermute | solution.py:365
  20.3 1.5 %collective-permute-start.4 = (bf16[18,32,128]{2,1,0:T(8,128)(2,1)S(1)}, bf16[18,32,128]{2,1,0:T(8,128)(2,1)S(1)}, u32[]{:S(2)}, u32[]{:S(2)}) collective-permute-start(bf16[18,32,128]{2,1,0:T(8,128)(2,1)S(1)} %collective-permute-done.3.refs_3_), channel_id=1, source_target_pairs={{0,16},{16,0},{1,17},{17,1},{2,18},{18,2},{3,19},{19,3},{4,20},{20... | collective-permute-start | bytes 442376 | tf_op jit(solution)/shard_map/ppermute | solution.py:365
  21.8 0.0 collective-permute-done.refs_1_
  21.8 1.0 %partial_eigen.2 = (f32[9,512,256]{2,1,0:T(8,128)S(1)}, f32[18,128]{1,0:T(8,128)S(1)}) custom-call(s32[1]{0:T(128)} %bitcast.1.me_ref, s32[1]{0:T(128)} %bitcast.side_ref, bf16[512,1024]{1,0:T(8,128)(2,1)S(1)} %get-tuple-element.40.act_ref, bf16[512,3584]{1,0:T(8,128)(2,1)S(1)} %get-tuple-element.41.grad_ref, ...), custom_call_target="tpu_custom_call" | custom-call | flops 301989888 | bytes 2359296 | tf_op jit(solution)/shard_map/partial_eigen/pallas_call | solution.py:445
  22.8 0.0 collective-permute-done.2.refs_2_
  22.8 2.6 %collective-permute-done.4.refs_3_ = bf16[18,32,128]{2,1,0:T(8,128)(2,1)S(1)} collective-permute-done((bf16[18,32,128]{2,1,0:T(8,128)(2,1)S(1)}, bf16[18,32,128]{2,1,0:T(8,128)(2,1)S(1)}, u32[]{:S(2)}, u32[]{:S(2)}) %collective-permute-start.4) | collective-permute-done | bytes 147488 | tf_op jit(solution)/shard_map/ppermute | solution.py:365
  25.5 1.0 %partial_eigen.3 = (f32[9,512,256]{2,1,0:T(8,128)S(1)}, f32[36,128]{1,0:T(8,128)S(1)}) custom-call(s32[1]{0:T(128)} %bitcast.1.me_ref, s32[1]{0:T(128)} %bitcast.side_ref, bf16[512,1024]{1,0:T(8,128)(2,1)S(1)} %get-tuple-element.40.act_ref, bf16[512,3584]{1,0:T(8,128)(2,1)S(1)} %get-tuple-element.41.grad_ref, ...), custom_call_target="tpu_custom_call" | custom-call | flops 301989888 | bytes 2359296 | tf_op jit(solution)/shard_map/partial_eigen/pallas_call | solution.py:445
  26.5 2.7 %collective-permute-start.5 = (f32[36,128]{1,0:T(8,128)S(1)}, f32[36,128]{1,0:T(8,128)S(1)}, u32[]{:S(2)}, u32[]{:S(2)}) collective-permute-start(f32[36,128]{1,0:T(8,128)S(1)} %get-tuple-element.56.refs_0_), channel_id=1, source_target_pairs={{0,12},{4,8},{8,4},{12,0},{1,13},{5,9},{9,5},{13,1},{2,14},{6,10},... | collective-permute-start | bytes 55304 | tf_op jit(solution)/shard_map/ppermute | solution.py:365
  29.2 0.0 collective-permute-start.6
  29.2 1.7 %collective-permute-start.7 = (f32[36,128]{1,0:T(8,128)S(1)}, f32[36,128]{1,0:T(8,128)S(1)}, u32[]{:S(2)}, u32[]{:S(2)}) collective-permute-start(f32[36,128]{1,0:T(8,128)S(1)} %get-tuple-element.56.refs_0_), channel_id=1, source_target_pairs={{0,4},{4,0},{8,12},{12,8},{1,5},{5,1},{9,13},{13,9},{2,6},{6,2},{1... | collective-permute-start | bytes 55304 | tf_op jit(solution)/shard_map/ppermute | solution.py:365
  30.9 0.0 collective-permute-done.9.relayed_ref
  30.9 0.6 %relay_chunk.1 = (bf16[1200,128]{1,0:T(8,128)(2,1)S(1)}, bf16[1200,128]{1,0:T(8,128)(2,1)S(1)}) custom-call(s32[1]{0:T(128)} %bitcast.2.owner_ref, f32[36,32,128]{2,1,0:T(8,128)S(1)} %get-tuple-element.51.far_ref, bf16[1200,128]{1,0:T(8,128)(2,1)S(1)} %collective-permute-done.9.relayed_ref, bf16[1200,128]{1,0:T(8,128)(2,1)S(1)} %get-tuple-element.53.near_ref), custom_call_target="tpu_custom_call" | custom-call | bytes 2359296 | tf_op jit(solution)/shard_map/relay_chunk/pallas_call | solution.py:455
  31.5 0.0 collective-permute-done.8.refs_0_
  31.5 0.6 %collective-permute-done.5.refs_1_ = f32[36,128]{1,0:T(8,128)S(1)} collective-permute-done((f32[36,128]{1,0:T(8,128)S(1)}, f32[36,128]{1,0:T(8,128)S(1)}, u32[]{:S(2)}, u32[]{:S(2)}) %collective-permute-start.5) | collective-permute-done | bytes 18464 | tf_op jit(solution)/shard_map/ppermute | solution.py:365
  32.1 2.1 %collective-permute-done.6.refs_2_ = f32[36,128]{1,0:T(8,128)S(1)} collective-permute-done((f32[36,128]{1,0:T(8,128)S(1)}, f32[36,128]{1,0:T(8,128)S(1)}, u32[]{:S(2)}, u32[]{:S(2)}) %collective-permute-start.6) | collective-permute-done | bytes 18464 | tf_op jit(solution)/shard_map/ppermute | solution.py:365
  34.2 0.0 collective-permute-done.7.refs_3_
  34.2 2.1 %collective-permute-start.11 = (bf16[1200,128]{1,0:T(8,128)(2,1)S(1)}, bf16[1200,128]{1,0:T(8,128)(2,1)S(1)}, u32[]{:S(2)}, u32[]{:S(2)}) collective-permute-start(bf16[1200,128]{1,0:T(8,128)(2,1)S(1)} %get-tuple-element.64), channel_id=1, source_target_pairs={{0,8},{1,5},{2,10},{3,7},{4,12},{5,1},{6,14},{7,3},{8,0},{9,13},{1... | collective-permute-start | bytes 921608 | tf_op jit(solution)/shard_map/ppermute | solution.py:477
  36.3 0.1 collective-permute-start.10
  36.3 0.0 collective-permute-start.12
  36.3 1.5 %collective-permute-start.13 = (f32[2,128]{1,0:T(2,128)S(1)}, f32[2,128]{1,0:T(2,128)S(1)}, u32[]{:S(2)}, u32[]{:S(2)}) collective-permute-start(f32[2,128]{1,0:T(2,128)S(1)} %get-tuple-element.62.refs_2_), channel_id=1, source_target_pairs={{0,2},{1,3},{2,0},{3,1},{4,6},{5,7},{6,4},{7,5},{8,10},{9,11},{10,... | collective-permute-start | bytes 3080 | tf_op jit(solution)/shard_map/ppermute | solution.py:365
  37.8 0.3 collective-permute-start.14
  38.2 1.1 %collective-permute-done.12.refs_3_ = f32[2,128]{1,0:T(2,128)S(1)} collective-permute-done((f32[2,128]{1,0:T(2,128)S(1)}, f32[2,128]{1,0:T(2,128)S(1)}, u32[]{:S(2)}, u32[]{:S(2)}) %collective-permute-start.12) | collective-permute-done | bytes 1056 | tf_op jit(solution)/shard_map/ppermute | solution.py:365
  39.3 0.6 %collective-permute-done.13.refs_4_ = f32[2,128]{1,0:T(2,128)S(1)} collective-permute-done((f32[2,128]{1,0:T(2,128)S(1)}, f32[2,128]{1,0:T(2,128)S(1)}, u32[]{:S(2)}, u32[]{:S(2)}) %collective-permute-start.13) | collective-permute-done | bytes 1056 | tf_op jit(solution)/shard_map/ppermute | solution.py:365
  39.9 0.0 collective-permute-done.14.refs_5_
  39.9 1.5 %partial_weights.1.refs_2_ = f32[2,512]{1,0:T(2,128)S(1)} custom-call(f32[36,128]{1,0:T(8,128)S(1)} %get-tuple-element.60.eigen_ref, f32[9,512,256]{2,1,0:T(8,128)S(1)} %get-tuple-element.65.refs_0_, f32[9,512,256]{2,1,0:T(8,128)S(1)} %get-tuple-element.66.refs_1_, f32[2,128]{1,0:T(2,128)S(1)} %get-tuple-element.62.refs_2_, ...), custom_call_target="tpu_custom_call" | custom-call | bytes 9437184 | tf_op jit(solution)/shard_map/partial_weights/pallas_call | solution.py:481
  41.4 0.6 %collective-permute-start.15 = (f32[2,512]{1,0:T(2,128)S(1)}, f32[2,512]{1,0:T(2,128)S(1)}, u32[]{:S(2)}, u32[]{:S(2)}) collective-permute-start(f32[2,512]{1,0:T(2,128)S(1)} %partial_weights.1.refs_2_), channel_id=1, source_target_pairs={{0,3},{1,2},{2,1},{3,0},{4,7},{5,6},{6,5},{7,4},{8,11},{9,10},{10,... | collective-permute-start | bytes 12296 | tf_op jit(solution)/shard_map/ppermute | solution.py:365
  42.0 1.7 %collective-permute-start.16 = (f32[2,512]{1,0:T(2,128)S(1)}, f32[2,512]{1,0:T(2,128)S(1)}, u32[]{:S(2)}, u32[]{:S(2)}) collective-permute-start(f32[2,512]{1,0:T(2,128)S(1)} %partial_weights.1.refs_2_), channel_id=1, source_target_pairs={{0,2},{1,3},{2,0},{3,1},{4,6},{5,7},{6,4},{7,5},{8,10},{9,11},{10,... | collective-permute-start | bytes 12296 | tf_op jit(solution)/shard_map/ppermute | solution.py:365
  43.8 0.0 collective-permute-start.17
  43.8 0.6 %add_chunk.1 = (f32[36,32,128]{2,1,0:T(8,128)S(1)}, f32[8,128]{1,0:T(8,128)}, f32[28,128]{1,0:T(8,128)}) custom-call(s32[1]{0:T(128)} %bitcast.side_ref, f32[36,128]{1,0:T(8,128)S(1)} %get-tuple-element.60.eigen_ref, f32[36,32,128]{2,1,0:T(8,128)S(1)} %get-tuple-element.44.own_ref, bf16[1200,128]{1,0:T(8,128)(2,1)S(1)} %collective-permute-done.8.refs_0_), custom_call_target="tpu_custom_call" | custom-call | bytes 1769472 | tf_op jit(solution)/shard_map/add_chunk/pallas_call | solution.py:498
  44.4 0.1 collective-permute-done.15.refs_3_
  44.5 1.2 %collective-permute-done.16.refs_4_ = f32[2,512]{1,0:T(2,128)S(1)} collective-permute-done((f32[2,512]{1,0:T(2,128)S(1)}, f32[2,512]{1,0:T(2,128)S(1)}, u32[]{:S(2)}, u32[]{:S(2)}) %collective-permute-start.16) | collective-permute-done | bytes 4128 | tf_op jit(solution)/shard_map/ppermute | solution.py:365
  45.6 0.0 collective-permute-done.17.refs_5_
  45.6 1.3 %collective-permute-done.11.refs_1_ = bf16[1200,128]{1,0:T(8,128)(2,1)S(1)} collective-permute-done((bf16[1200,128]{1,0:T(8,128)(2,1)S(1)}, bf16[1200,128]{1,0:T(8,128)(2,1)S(1)}, u32[]{:S(2)}, u32[]{:S(2)}) %collective-permute-start.11) | collective-permute-done | bytes 307232 | tf_op jit(solution)/shard_map/ppermute | solution.py:477
  46.9 0.0 collective-permute-done.10.refs_0_
  46.9 1.4 %last_sums.1 = (f32[8,32,128]{2,1,0:T(8,128)}, f32[28,32,128]{2,1,0:T(8,128)}, f32[1,512]{1,0:T(1,128)}) custom-call(f32[36,32,128]{2,1,0:T(8,128)S(1)} %get-tuple-element.61.own_ref, bf16[1200,128]{1,0:T(8,128)(2,1)S(1)} %collective-permute-done.10.refs_0_, bf16[1200,128]{1,0:T(8,128)(2,1)S(1)} %collective-permute-done.11.refs_1_, ...), custom_call_target="tpu_custom_call" | custom-call | bytes 2359296 | tf_op jit(solution)/shard_map/last_sums/pallas_call | solution.py:511
  (1 shorter events, 0.0 us)
Async XLA Ops:
  1.7 14.3 %collective-permute-start.1 = (bf16[18,32,128]{2,1,0:T(8,128)(2,1)S(1)}, bf16[18,32,128]{2,1,0:T(8,128)(2,1)S(1)}, u32[]{:S(2)}, u32[]{:S(2)}) collective-permute-start(bf16[18,32,128]{2,1,0:T(8,128)(2,1)S(1)} %get-tuple-element.43), channel_id=1, source_target_pairs={{0,12},{4,8},{8,4},{12,0},{1,13},{5,9},{9,5},{13,1},{2,14},{6,10},... | collective-permute-start | bytes 442376 | tf_op jit(solution)/shard_map/ppermute | solution.py:365
  6.8 13.5 %collective-permute-start.3 = (bf16[18,32,128]{2,1,0:T(8,128)(2,1)S(1)}, bf16[18,32,128]{2,1,0:T(8,128)(2,1)S(1)}, u32[]{:S(2)}, u32[]{:S(2)}) collective-permute-start(bf16[18,32,128]{2,1,0:T(8,128)(2,1)S(1)} %get-tuple-element.43), channel_id=1, source_target_pairs={{0,8},{4,12},{8,0},{12,4},{1,9},{5,13},{9,1},{13,5},{2,10},{6,14},... | collective-permute-start | bytes 442376 | tf_op jit(solution)/shard_map/ppermute | solution.py:365
  6.8 15.0 %collective-permute-start = (bf16[36,32,128]{2,1,0:T(8,128)(2,1)S(1)}, bf16[36,32,128]{2,1,0:T(8,128)(2,1)S(1)}, u32[]{:S(2)}, u32[]{:S(2)}) collective-permute-start(bf16[36,32,128]{2,1,0:T(8,128)(2,1)S(1)} %get-tuple-element.42.refs_0_), channel_id=1, source_target_pairs={{0,4},{4,0},{8,12},{12,8},{1,5},{5,1},{9,13},{13,9},{2,6},{6,2},{1... | collective-permute-start | bytes 884744 | tf_op jit(solution)/shard_map/ppermute | solution.py:365
  12.0 18.9 %collective-permute-start.9 = (bf16[1200,128]{1,0:T(8,128)(2,1)S(1)}, bf16[1200,128]{1,0:T(8,128)(2,1)S(1)}, u32[]{:S(2)}, u32[]{:S(2)}) collective-permute-start(bf16[1200,128]{1,0:T(8,128)(2,1)S(1)} %get-tuple-element.49), channel_id=1, source_target_pairs={{0,4},{12,8},{1,5},{13,9},{2,6},{14,10},{3,7},{15,11},{16,20},{28,... | collective-permute-start | bytes 921608 | tf_op jit(solution)/shard_map/ppermute | solution.py:437
  15.4 16.2 %collective-permute-start.8 = (bf16[1200,128]{1,0:T(8,128)(2,1)S(1)}, bf16[1200,128]{1,0:T(8,128)(2,1)S(1)}, u32[]{:S(2)}, u32[]{:S(2)}) collective-permute-start(bf16[1200,128]{1,0:T(8,128)(2,1)S(1)} %get-tuple-element.49), channel_id=1, source_target_pairs={{4,8},{8,4},{5,9},{9,5},{6,10},{10,6},{7,11},{11,7},{20,24},{24,20... | collective-permute-start | bytes 921608 | tf_op jit(solution)/shard_map/ppermute | solution.py:436
  16.1 6.8 %collective-permute-start.2 = (bf16[18,32,128]{2,1,0:T(8,128)(2,1)S(1)}, bf16[18,32,128]{2,1,0:T(8,128)(2,1)S(1)}, u32[]{:S(2)}, u32[]{:S(2)}) collective-permute-start(bf16[18,32,128]{2,1,0:T(8,128)(2,1)S(1)} %collective-permute-done.1.refs_2_), channel_id=1, source_target_pairs={{0,16},{16,0},{1,17},{17,1},{2,18},{18,2},{3,19},{19,3},{4,20},{20... | collective-permute-start | bytes 442376 | tf_op jit(solution)/shard_map/ppermute | solution.py:365
  20.3 5.1 %collective-permute-start.4 = (bf16[18,32,128]{2,1,0:T(8,128)(2,1)S(1)}, bf16[18,32,128]{2,1,0:T(8,128)(2,1)S(1)}, u32[]{:S(2)}, u32[]{:S(2)}) collective-permute-start(bf16[18,32,128]{2,1,0:T(8,128)(2,1)S(1)} %collective-permute-done.3.refs_3_), channel_id=1, source_target_pairs={{0,16},{16,0},{1,17},{17,1},{2,18},{18,2},{3,19},{19,3},{4,20},{20... | collective-permute-start | bytes 442376 | tf_op jit(solution)/shard_map/ppermute | solution.py:365
  26.5 5.7 %collective-permute-start.5 = (f32[36,128]{1,0:T(8,128)S(1)}, f32[36,128]{1,0:T(8,128)S(1)}, u32[]{:S(2)}, u32[]{:S(2)}) collective-permute-start(f32[36,128]{1,0:T(8,128)S(1)} %get-tuple-element.56.refs_0_), channel_id=1, source_target_pairs={{0,12},{4,8},{8,4},{12,0},{1,13},{5,9},{9,5},{13,1},{2,14},{6,10},... | collective-permute-start | bytes 55304 | tf_op jit(solution)/shard_map/ppermute | solution.py:365
  29.2 5.0 %collective-permute-start.6 = (f32[36,128]{1,0:T(8,128)S(1)}, f32[36,128]{1,0:T(8,128)S(1)}, u32[]{:S(2)}, u32[]{:S(2)}) collective-permute-start(f32[36,128]{1,0:T(8,128)S(1)} %get-tuple-element.56.refs_0_), channel_id=1, source_target_pairs={{0,8},{4,12},{8,0},{12,4},{1,9},{5,13},{9,1},{13,5},{2,10},{6,14},... | collective-permute-start | bytes 55304 | tf_op jit(solution)/shard_map/ppermute | solution.py:365
  29.2 5.0 %collective-permute-start.7 = (f32[36,128]{1,0:T(8,128)S(1)}, f32[36,128]{1,0:T(8,128)S(1)}, u32[]{:S(2)}, u32[]{:S(2)}) collective-permute-start(f32[36,128]{1,0:T(8,128)S(1)} %get-tuple-element.56.refs_0_), channel_id=1, source_target_pairs={{0,4},{4,0},{8,12},{12,8},{1,5},{5,1},{9,13},{13,9},{2,6},{6,2},{1... | collective-permute-start | bytes 55304 | tf_op jit(solution)/shard_map/ppermute | solution.py:365
  34.2 12.7 %collective-permute-start.11 = (bf16[1200,128]{1,0:T(8,128)(2,1)S(1)}, bf16[1200,128]{1,0:T(8,128)(2,1)S(1)}, u32[]{:S(2)}, u32[]{:S(2)}) collective-permute-start(bf16[1200,128]{1,0:T(8,128)(2,1)S(1)} %get-tuple-element.64), channel_id=1, source_target_pairs={{0,8},{1,5},{2,10},{3,7},{4,12},{5,1},{6,14},{7,3},{8,0},{9,13},{1... | collective-permute-start | bytes 921608 | tf_op jit(solution)/shard_map/ppermute | solution.py:477
  36.3 10.7 %collective-permute-start.10 = (bf16[1200,128]{1,0:T(8,128)(2,1)S(1)}, bf16[1200,128]{1,0:T(8,128)(2,1)S(1)}, u32[]{:S(2)}, u32[]{:S(2)}) collective-permute-start(bf16[1200,128]{1,0:T(8,128)(2,1)S(1)} %get-tuple-element.63), channel_id=1, source_target_pairs={{0,4},{1,9},{2,6},{3,11},{4,0},{5,13},{6,2},{7,15},{8,12},{9,1},{1... | collective-permute-start | bytes 921608 | tf_op jit(solution)/shard_map/ppermute | solution.py:477
  36.3 3.0 %collective-permute-start.12 = (f32[2,128]{1,0:T(2,128)S(1)}, f32[2,128]{1,0:T(2,128)S(1)}, u32[]{:S(2)}, u32[]{:S(2)}) collective-permute-start(f32[2,128]{1,0:T(2,128)S(1)} %get-tuple-element.62.refs_2_), channel_id=1, source_target_pairs={{0,3},{1,2},{2,1},{3,0},{4,7},{5,6},{6,5},{7,4},{8,11},{9,10},{10,... | collective-permute-start | bytes 3080 | tf_op jit(solution)/shard_map/ppermute | solution.py:365
  36.3 3.6 %collective-permute-start.13 = (f32[2,128]{1,0:T(2,128)S(1)}, f32[2,128]{1,0:T(2,128)S(1)}, u32[]{:S(2)}, u32[]{:S(2)}) collective-permute-start(f32[2,128]{1,0:T(2,128)S(1)} %get-tuple-element.62.refs_2_), channel_id=1, source_target_pairs={{0,2},{1,3},{2,0},{3,1},{4,6},{5,7},{6,4},{7,5},{8,10},{9,11},{10,... | collective-permute-start | bytes 3080 | tf_op jit(solution)/shard_map/ppermute | solution.py:365
  37.8 2.1 %collective-permute-start.14 = (f32[2,128]{1,0:T(2,128)S(1)}, f32[2,128]{1,0:T(2,128)S(1)}, u32[]{:S(2)}, u32[]{:S(2)}) collective-permute-start(f32[2,128]{1,0:T(2,128)S(1)} %get-tuple-element.62.refs_2_), channel_id=1, source_target_pairs={{0,1},{1,0},{2,3},{3,2},{4,5},{5,4},{6,7},{7,6},{8,9},{9,8},{10,11... | collective-permute-start | bytes 3080 | tf_op jit(solution)/shard_map/ppermute | solution.py:365
  41.4 3.1 %collective-permute-start.15 = (f32[2,512]{1,0:T(2,128)S(1)}, f32[2,512]{1,0:T(2,128)S(1)}, u32[]{:S(2)}, u32[]{:S(2)}) collective-permute-start(f32[2,512]{1,0:T(2,128)S(1)} %partial_weights.1.refs_2_), channel_id=1, source_target_pairs={{0,3},{1,2},{2,1},{3,0},{4,7},{5,6},{6,5},{7,4},{8,11},{9,10},{10,... | collective-permute-start | bytes 12296 | tf_op jit(solution)/shard_map/ppermute | solution.py:365
  42.0 3.6 %collective-permute-start.16 = (f32[2,512]{1,0:T(2,128)S(1)}, f32[2,512]{1,0:T(2,128)S(1)}, u32[]{:S(2)}, u32[]{:S(2)}) collective-permute-start(f32[2,512]{1,0:T(2,128)S(1)} %partial_weights.1.refs_2_), channel_id=1, source_target_pairs={{0,2},{1,3},{2,0},{3,1},{4,6},{5,7},{6,4},{7,5},{8,10},{9,11},{10,... | collective-permute-start | bytes 12296 | tf_op jit(solution)/shard_map/ppermute | solution.py:365
  43.8 1.9 %collective-permute-start.17 = (f32[2,512]{1,0:T(2,128)S(1)}, f32[2,512]{1,0:T(2,128)S(1)}, u32[]{:S(2)}, u32[]{:S(2)}) collective-permute-start(f32[2,512]{1,0:T(2,128)S(1)} %partial_weights.1.refs_2_), channel_id=1, source_target_pairs={{0,1},{1,0},{2,3},{3,2},{4,5},{5,4},{6,7},{7,6},{8,9},{9,8},{10,11... | collective-permute-start | bytes 12296 | tf_op jit(solution)/shard_map/ppermute | solution.py:365

commit v18 on v13

--- a/solution.py
+++ b/solution.py
@@ -1,4 +1,5 @@
 import functools
+import math
 
 import jax
 import jax.numpy as jnp
@@ -16,6 +17,7 @@
 VMEM_LIMIT = 24 * 1024 * 1024
 CODE_TOP = 2.0**7.875
 SMALLEST = 1e-36
+SIXTEENTH = 1.0 / (16.0 * math.log(2.0))
 
 damp_root = 0.31622776601683794
 contract_rows = (((0,), (0,)), ((), ()))
@@ -76,9 +78,7 @@
 
 def decode(coded):
     coded = coded.astype(jnp.float32)
-    root = jnp.abs(coded)
-    for _ in range(4):
-        root = lax.rsqrt(root)
+    root = jnp.exp2(jnp.log(jnp.abs(coded)) * SIXTEENTH)
     return jnp.where(coded > 0.0, root, jnp.where(coded < 0.0, -root, 0.0))
 
 

time: 48.5 us -> 48.4 us (level)
  no operation moved by 1% of the time
where the time goes in v18:
time: 48.4 us; the launch traced here: 48.2 us
  starting transfers between devices  23.7 us (49%)
  waiting for transfers between devices  12.4 us (26%)
  Pallas kernels  11.5 us (24%)
  between operations  0.73 us (2%)
    ppermute x16, starting transfers between devices, swap(): return lax.ppermute(value, axis, [(i, i ^ mask) for i in range(count)])  19.7 us
    ppermute x16, waiting for transfers between devices, swap(): return lax.ppermute(value, axis, [(i, i ^ mask) for i in range(count)])  12.4 us
    pallas_call x1, Pallas kernels, local(): call(functools.partial(gram_kernel, pieces, coded, scale), [bf16(*activat...  4.56 us
    ppermute x1, starting transfers between devices, local(): relayed = lax.ppermute(sent[3], 'dp', [(0, 1), (3, 2)])  3.32 us
    pallas_call x2, Pallas kernels, local(): call(functools.partial(eigen_kernel, part, halves, masks, pieces, scale),...  1.95 us
    pallas_call x1, Pallas kernels, local(): call(functools.partial(weight_kernel, halves, act_blocks // halves), f32(...  1.49 us
    pallas_call x1, Pallas kernels, local(): call(functools.partial(last_add_kernel, [(None, 0, blocks)] * len(chunks)...  1.23 us
    pallas_call x1, Pallas kernels, local(): call(pack_kernel, [bf16(blocks // part, rows, BLK) for part in range(1, h...  1.08 us
  transfers between devices with their start and end apart: 18, of which 9 were waited for; matrix products, arithmetic and copies ran while one was open for 0% of the time, Pallas kernels for 19%

profile of v18, /device:TPU:0, one launch (start us, length us, event | category | flops | bytes accessed | tf_op | source)
XLA Modules:
  0.0 48.2 jit_solution(9569626277194862622)
XLA Ops:
  0.6 1.1 %pack_basis.1 = (bf16[36,32,128]{2,1,0:T(8,128)(2,1)S(1)}, bf16[18,32,128]{2,1,0:T(8,128)(2,1)S(1)}) custom-call(s32[1]{0:T(128)} %bitcast.side_ref, bf16[8,32,128]{2,1,0:T(8,128)(2,1)} %act_ref.1, bf16[28,32,128]{2,1,0:T(8,128)(2,1)} %grad_ref.1), custom_call_target="tpu_custom_call" | custom-call | bytes 294912 | tf_op jit(solution)/shard_map/pack_basis/pallas_call | solution.py:380
  1.7 5.1 %collective-permute-start.1 = (bf16[18,32,128]{2,1,0:T(8,128)(2,1)S(1)}, bf16[18,32,128]{2,1,0:T(8,128)(2,1)S(1)}, u32[]{:S(2)}, u32[]{:S(2)}) collective-permute-start(bf16[18,32,128]{2,1,0:T(8,128)(2,1)S(1)} %get-tuple-element.41), channel_id=1, source_target_pairs={{0,12},{4,8},{8,4},{12,0},{1,13},{5,9},{9,5},{13,1},{2,14},{6,10},... | collective-permute-start | bytes 442376 | tf_op jit(solution)/shard_map/ppermute | solution.py:352
  6.8 0.0 collective-permute-start.3
  6.8 0.6 %collective-permute-start = (bf16[36,32,128]{2,1,0:T(8,128)(2,1)S(1)}, bf16[36,32,128]{2,1,0:T(8,128)(2,1)S(1)}, u32[]{:S(2)}, u32[]{:S(2)}) collective-permute-start(bf16[36,32,128]{2,1,0:T(8,128)(2,1)S(1)} %get-tuple-element.40.refs_0_), channel_id=1, source_target_pairs={{0,4},{4,0},{8,12},{12,8},{1,5},{5,1},{9,13},{13,9},{2,6},{6,2},{1... | collective-permute-start | bytes 884744 | tf_op jit(solution)/shard_map/ppermute | solution.py:352
  7.5 4.6 %partial_gram.1 = (bf16[512,1024]{1,0:T(8,128)(2,1)S(1)}, bf16[512,3584]{1,0:T(8,128)(2,1)S(1)}, f32[36,32,128]{2,1,0:T(8,128)S(1)}, f32[36,32,128]{2,1,0:T(8,12...) custom-call(s32[1]{0:T(128)} %bitcast.1.me_ref, bf16[512,1024]{1,0:T(8,128)(2,1)} %act_hbm.1, ...), custom_call_target="tpu_custom_call" | custom-call | flops 1207959552 | bytes 4718592 | tf_op jit(solution)/shard_map/partial_gram/pallas_call | solution.py:401
  12.0 3.3 %collective-permute-start.9 = (bf16[1200,128]{1,0:T(8,128)(2,1)S(1)}, bf16[1200,128]{1,0:T(8,128)(2,1)S(1)}, u32[]{:S(2)}, u32[]{:S(2)}) collective-permute-start(bf16[1200,128]{1,0:T(8,128)(2,1)S(1)} %get-tuple-element.47), channel_id=1, source_target_pairs={{0,4},{12,8},{1,5},{13,9},{2,6},{14,10},{3,7},{15,11},{16,20},{28,... | collective-permute-start | bytes 921608 | tf_op jit(solution)/shard_map/ppermute | solution.py:423
  15.4 0.7 %collective-permute-start.8 = (bf16[1200,128]{1,0:T(8,128)(2,1)S(1)}, bf16[1200,128]{1,0:T(8,128)(2,1)S(1)}, u32[]{:S(2)}, u32[]{:S(2)}) collective-permute-start(bf16[1200,128]{1,0:T(8,128)(2,1)S(1)} %get-tuple-element.47), channel_id=1, source_target_pairs={{4,8},{8,4},{5,9},{9,5},{6,10},{10,6},{7,11},{11,7},{20,24},{24,20... | collective-permute-start | bytes 921608 | tf_op jit(solution)/shard_map/ppermute | solution.py:422
  16.1 0.0 collective-permute-done.1.refs_2_
  16.1 1.6 %collective-permute-start.2 = (bf16[18,32,128]{2,1,0:T(8,128)(2,1)S(1)}, bf16[18,32,128]{2,1,0:T(8,128)(2,1)S(1)}, u32[]{:S(2)}, u32[]{:S(2)}) collective-permute-start(bf16[18,32,128]{2,1,0:T(8,128)(2,1)S(1)} %collective-permute-done.1.refs_2_), channel_id=1, source_target_pairs={{0,16},{16,0},{1,17},{17,1},{2,18},{18,2},{3,19},{19,3},{4,20},{20... | collective-permute-start | bytes 442376 | tf_op jit(solution)/shard_map/ppermute | solution.py:352
  17.6 2.7 %collective-permute-done.3.refs_3_ = bf16[18,32,128]{2,1,0:T(8,128)(2,1)S(1)} collective-permute-done((bf16[18,32,128]{2,1,0:T(8,128)(2,1)S(1)}, bf16[18,32,128]{2,1,0:T(8,128)(2,1)S(1)}, u32[]{:S(2)}, u32[]{:S(2)}) %collective-permute-start.3) | collective-permute-done | bytes 147488 | tf_op jit(solution)/shard_map/ppermute | solution.py:352
  20.3 1.5 %collective-permute-start.4 = (bf16[18,32,128]{2,1,0:T(8,128)(2,1)S(1)}, bf16[18,32,128]{2,1,0:T(8,128)(2,1)S(1)}, u32[]{:S(2)}, u32[]{:S(2)}) collective-permute-start(bf16[18,32,128]{2,1,0:T(8,128)(2,1)S(1)} %collective-permute-done.3.refs_3_), channel_id=1, source_target_pairs={{0,16},{16,0},{1,17},{17,1},{2,18},{18,2},{3,19},{19,3},{4,20},{20... | collective-permute-start | bytes 442376 | tf_op jit(solution)/shard_map/ppermute | solution.py:352
  21.8 0.0 collective-permute-done.refs_1_
  21.8 1.0 %partial_eigen.2 = (f32[9,512,256]{2,1,0:T(8,128)S(1)}, f32[18,128]{1,0:T(8,128)S(1)}) custom-call(s32[1]{0:T(128)} %bitcast.1.me_ref, s32[1]{0:T(128)} %bitcast.side_ref, bf16[512,1024]{1,0:T(8,128)(2,1)S(1)} %get-tuple-element.38.act_ref, bf16[512,3584]{1,0:T(8,128)(2,1)S(1)} %get-tuple-element.39.grad_ref, ...), custom_call_target="tpu_custom_call" | custom-call | flops 301989888 | bytes 2359296 | tf_op jit(solution)/shard_map/partial_eigen/pallas_call | solution.py:431
  22.8 0.0 collective-permute-done.2.refs_2_
  22.8 2.6 %collective-permute-done.4.refs_3_ = bf16[18,32,128]{2,1,0:T(8,128)(2,1)S(1)} collective-permute-done((bf16[18,32,128]{2,1,0:T(8,128)(2,1)S(1)}, bf16[18,32,128]{2,1,0:T(8,128)(2,1)S(1)}, u32[]{:S(2)}, u32[]{:S(2)}) %collective-permute-start.4) | collective-permute-done | bytes 147488 | tf_op jit(solution)/shard_map/ppermute | solution.py:352
  25.5 1.0 %partial_eigen.3 = (f32[9,512,256]{2,1,0:T(8,128)S(1)}, f32[36,128]{1,0:T(8,128)S(1)}) custom-call(s32[1]{0:T(128)} %bitcast.1.me_ref, s32[1]{0:T(128)} %bitcast.side_ref, bf16[512,1024]{1,0:T(8,128)(2,1)S(1)} %get-tuple-element.38.act_ref, bf16[512,3584]{1,0:T(8,128)(2,1)S(1)} %get-tuple-element.39.grad_ref, ...), custom_call_target="tpu_custom_call" | custom-call | flops 301989888 | bytes 2359296 | tf_op jit(solution)/shard_map/partial_eigen/pallas_call | solution.py:431
  26.5 2.7 %collective-permute-start.5 = (f32[36,128]{1,0:T(8,128)S(1)}, f32[36,128]{1,0:T(8,128)S(1)}, u32[]{:S(2)}, u32[]{:S(2)}) collective-permute-start(f32[36,128]{1,0:T(8,128)S(1)} %get-tuple-element.51.refs_0_), channel_id=1, source_target_pairs={{0,12},{4,8},{8,4},{12,0},{1,13},{5,9},{9,5},{13,1},{2,14},{6,10},... | collective-permute-start | bytes 55304 | tf_op jit(solution)/shard_map/ppermute | solution.py:352
  29.2 0.0 collective-permute-start.6
  29.2 1.7 %collective-permute-start.7 = (f32[36,128]{1,0:T(8,128)S(1)}, f32[36,128]{1,0:T(8,128)S(1)}, u32[]{:S(2)}, u32[]{:S(2)}) collective-permute-start(f32[36,128]{1,0:T(8,128)S(1)} %get-tuple-element.51.refs_0_), channel_id=1, source_target_pairs={{0,4},{4,0},{8,12},{12,8},{1,5},{5,1},{9,13},{13,9},{2,6},{6,2},{1... | collective-permute-start | bytes 55304 | tf_op jit(solution)/shard_map/ppermute | solution.py:352
  30.9 0.0 collective-permute-done.9.relayed_ref
  30.9 0.5 %relay_chunk.1 = bf16[1200,128]{1,0:T(8,128)(2,1)S(1)} custom-call(f32[36,32,128]{2,1,0:T(8,128)S(1)} %get-tuple-element.49.far_ref, bf16[1200,128]{1,0:T(8,128)(2,1)S(1)} %collective-permute-done.9.relayed_ref), custom_call_target="tpu_custom_call" | custom-call | bytes 1769472 | tf_op jit(solution)/shard_map/relay_chunk/pallas_call | solution.py:440
  31.4 0.0 collective-permute-done.8.refs_0_
  31.4 0.7 %collective-permute-done.5.refs_1_ = f32[36,128]{1,0:T(8,128)S(1)} collective-permute-done((f32[36,128]{1,0:T(8,128)S(1)}, f32[36,128]{1,0:T(8,128)S(1)}, u32[]{:S(2)}, u32[]{:S(2)}) %collective-permute-start.5) | collective-permute-done | bytes 18464 | tf_op jit(solution)/shard_map/ppermute | solution.py:352
  32.1 2.1 %collective-permute-done.6.refs_2_ = f32[36,128]{1,0:T(8,128)S(1)} collective-permute-done((f32[36,128]{1,0:T(8,128)S(1)}, f32[36,128]{1,0:T(8,128)S(1)}, u32[]{:S(2)}, u32[]{:S(2)}) %collective-permute-start.6) | collective-permute-done | bytes 18464 | tf_op jit(solution)/shard_map/ppermute | solution.py:352
  34.2 0.0 collective-permute-done.7.refs_3_
  34.2 0.8 %collective-permute-start.11 = (bf16[1200,128]{1,0:T(8,128)(2,1)S(1)}, bf16[1200,128]{1,0:T(8,128)(2,1)S(1)}, u32[]{:S(2)}, u32[]{:S(2)}) collective-permute-start(bf16[1200,128]{1,0:T(8,128)(2,1)S(1)} %get-tuple-element.60), channel_id=1, source_target_pairs={{0,4},{4,0},{8,12},{12,8},{1,5},{5,1},{9,13},{13,9},{2,6},{6,2},{1... | collective-permute-start | bytes 921608 | tf_op jit(solution)/shard_map/ppermute | solution.py:352
  35.1 1.3 %collective-permute-start.10 = (bf16[1200,128]{1,0:T(8,128)(2,1)S(1)}, bf16[1200,128]{1,0:T(8,128)(2,1)S(1)}, u32[]{:S(2)}, u32[]{:S(2)}) collective-permute-start(bf16[1200,128]{1,0:T(8,128)(2,1)S(1)} %relay_chunk.1), channel_id=1, source_target_pairs={{0,8},{4,12},{8,0},{12,4},{1,9},{5,13},{9,1},{13,5},{2,10},{6,14},... | collective-permute-start | bytes 921608 | tf_op jit(solution)/shard_map/ppermute | solution.py:352
  36.3 0.0 collective-permute-start.12
  36.3 1.5 %collective-permute-start.13 = (f32[2,128]{1,0:T(2,128)S(1)}, f32[2,128]{1,0:T(2,128)S(1)}, u32[]{:S(2)}, u32[]{:S(2)}) collective-permute-start(f32[2,128]{1,0:T(2,128)S(1)} %get-tuple-element.57.refs_2_), channel_id=1, source_target_pairs={{0,2},{1,3},{2,0},{3,1},{4,6},{5,7},{6,4},{7,5},{8,10},{9,11},{10,... | collective-permute-start | bytes 3080 | tf_op jit(solution)/shard_map/ppermute | solution.py:352
  37.9 0.3 collective-permute-start.14
  38.2 1.1 %collective-permute-done.12.refs_3_ = f32[2,128]{1,0:T(2,128)S(1)} collective-permute-done((f32[2,128]{1,0:T(2,128)S(1)}, f32[2,128]{1,0:T(2,128)S(1)}, u32[]{:S(2)}, u32[]{:S(2)}) %collective-permute-start.12) | collective-permute-done | bytes 1056 | tf_op jit(solution)/shard_map/ppermute | solution.py:352
  39.3 0.6 %collective-permute-done.13.refs_4_ = f32[2,128]{1,0:T(2,128)S(1)} collective-permute-done((f32[2,128]{1,0:T(2,128)S(1)}, f32[2,128]{1,0:T(2,128)S(1)}, u32[]{:S(2)}, u32[]{:S(2)}) %collective-permute-start.13) | collective-permute-done | bytes 1056 | tf_op jit(solution)/shard_map/ppermute | solution.py:352
  39.9 0.0 collective-permute-done.14.refs_5_
  39.9 1.5 %partial_weights.1.refs_2_ = f32[2,512]{1,0:T(2,128)S(1)} custom-call(f32[36,128]{1,0:T(8,128)S(1)} %get-tuple-element.55.eigen_ref, f32[9,512,256]{2,1,0:T(8,128)S(1)} %get-tuple-element.61.refs_0_, f32[9,512,256]{2,1,0:T(8,128)S(1)} %get-tuple-element.62.refs_1_, f32[2,128]{1,0:T(2,128)S(1)} %get-tuple-element.57.refs_2_, ...), custom_call_target="tpu_custom_call" | custom-call | bytes 9437184 | tf_op jit(solution)/shard_map/partial_weights/pallas_call | solution.py:458
  41.4 0.9 %collective-permute-start.15 = (f32[2,512]{1,0:T(2,128)S(1)}, f32[2,512]{1,0:T(2,128)S(1)}, u32[]{:S(2)}, u32[]{:S(2)}) collective-permute-start(f32[2,512]{1,0:T(2,128)S(1)} %partial_weights.1.refs_2_), channel_id=1, source_target_pairs={{0,3},{1,2},{2,1},{3,0},{4,7},{5,6},{6,5},{7,4},{8,11},{9,10},{10,... | collective-permute-start | bytes 12296 | tf_op jit(solution)/shard_map/ppermute | solution.py:352
  42.3 1.5 %collective-permute-start.16 = (f32[2,512]{1,0:T(2,128)S(1)}, f32[2,512]{1,0:T(2,128)S(1)}, u32[]{:S(2)}, u32[]{:S(2)}) collective-permute-start(f32[2,512]{1,0:T(2,128)S(1)} %partial_weights.1.refs_2_), channel_id=1, source_target_pairs={{0,2},{1,3},{2,0},{3,1},{4,6},{5,7},{6,4},{7,5},{8,10},{9,11},{10,... | collective-permute-start | bytes 12296 | tf_op jit(solution)/shard_map/ppermute | solution.py:352
  43.8 0.0 collective-permute-start.17
  43.8 0.6 %add_chunk.1 = (f32[36,32,128]{2,1,0:T(8,128)S(1)}, f32[8,128]{1,0:T(8,128)}, f32[28,128]{1,0:T(8,128)}) custom-call(s32[1]{0:T(128)} %bitcast.side_ref, f32[36,128]{1,0:T(8,128)S(1)} %get-tuple-element.55.eigen_ref, f32[36,32,128]{2,1,0:T(8,128)S(1)} %get-tuple-element.42.own_ref, bf16[1200,128]{1,0:T(8,128)(2,1)S(1)} %collective-permute-done.8.refs_0_), custom_call_target="tpu_custom_call" | custom-call | bytes 1769472 | tf_op jit(solution)/shard_map/add_chunk/pallas_call | solution.py:475
  44.4 0.1 collective-permute-done.15.refs_3_
  44.5 1.4 %collective-permute-done.16.refs_4_ = f32[2,512]{1,0:T(2,128)S(1)} collective-permute-done((f32[2,512]{1,0:T(2,128)S(1)}, f32[2,512]{1,0:T(2,128)S(1)}, u32[]{:S(2)}, u32[]{:S(2)}) %collective-permute-start.16) | collective-permute-done | bytes 4128 | tf_op jit(solution)/shard_map/ppermute | solution.py:352
  45.9 0.0 collective-permute-done.17.refs_5_
  45.9 0.0 collective-permute-done.11.refs_1_
  45.9 1.1 %collective-permute-done.10.refs_0_ = bf16[1200,128]{1,0:T(8,128)(2,1)S(1)} collective-permute-done((bf16[1200,128]{1,0:T(8,128)(2,1)S(1)}, bf16[1200,128]{1,0:T(8,128)(2,1)S(1)}, u32[]{:S(2)}, u32[]{:S(2)}) %collective-permute-start.10) | collective-permute-done | bytes 307232 | tf_op jit(solution)/shard_map/ppermute | solution.py:352
  47.0 1.2 %last_sums.1 = (f32[8,32,128]{2,1,0:T(8,128)}, f32[28,32,128]{2,1,0:T(8,128)}, f32[1,512]{1,0:T(1,128)}) custom-call(f32[36,32,128]{2,1,0:T(8,128)S(1)} %get-tuple-element.56.own_ref, bf16[1200,128]{1,0:T(8,128)(2,1)S(1)} %collective-permute-done.10.refs_0_, bf16[1200,128]{1,0:T(8,128)(2,1)S(1)} %collective-permute-done.11.refs_1_, ...), custom_call_target="tpu_custom_call" | custom-call | bytes 2359296 | tf_op jit(solution)/shard_map/last_sums/pallas_call | solution.py:488
  (1 shorter events, 0.0 us)
Async XLA Ops:
  1.7 14.3 %collective-permute-start.1 = (bf16[18,32,128]{2,1,0:T(8,128)(2,1)S(1)}, bf16[18,32,128]{2,1,0:T(8,128)(2,1)S(1)}, u32[]{:S(2)}, u32[]{:S(2)}) collective-permute-start(bf16[18,32,128]{2,1,0:T(8,128)(2,1)S(1)} %get-tuple-element.41), channel_id=1, source_target_pairs={{0,12},{4,8},{8,4},{12,0},{1,13},{5,9},{9,5},{13,1},{2,14},{6,10},... | collective-permute-start | bytes 442376 | tf_op jit(solution)/shard_map/ppermute | solution.py:352
  6.8 13.5 %collective-permute-start.3 = (bf16[18,32,128]{2,1,0:T(8,128)(2,1)S(1)}, bf16[18,32,128]{2,1,0:T(8,128)(2,1)S(1)}, u32[]{:S(2)}, u32[]{:S(2)}) collective-permute-start(bf16[18,32,128]{2,1,0:T(8,128)(2,1)S(1)} %get-tuple-element.41), channel_id=1, source_target_pairs={{0,8},{4,12},{8,0},{12,4},{1,9},{5,13},{9,1},{13,5},{2,10},{6,14},... | collective-permute-start | bytes 442376 | tf_op jit(solution)/shard_map/ppermute | solution.py:352
  6.8 15.0 %collective-permute-start = (bf16[36,32,128]{2,1,0:T(8,128)(2,1)S(1)}, bf16[36,32,128]{2,1,0:T(8,128)(2,1)S(1)}, u32[]{:S(2)}, u32[]{:S(2)}) collective-permute-start(bf16[36,32,128]{2,1,0:T(8,128)(2,1)S(1)} %get-tuple-element.40.refs_0_), channel_id=1, source_target_pairs={{0,4},{4,0},{8,12},{12,8},{1,5},{5,1},{9,13},{13,9},{2,6},{6,2},{1... | collective-permute-start | bytes 884744 | tf_op jit(solution)/shard_map/ppermute | solution.py:352
  12.0 18.9 %collective-permute-start.9 = (bf16[1200,128]{1,0:T(8,128)(2,1)S(1)}, bf16[1200,128]{1,0:T(8,128)(2,1)S(1)}, u32[]{:S(2)}, u32[]{:S(2)}) collective-permute-start(bf16[1200,128]{1,0:T(8,128)(2,1)S(1)} %get-tuple-element.47), channel_id=1, source_target_pairs={{0,4},{12,8},{1,5},{13,9},{2,6},{14,10},{3,7},{15,11},{16,20},{28,... | collective-permute-start | bytes 921608 | tf_op jit(solution)/shard_map/ppermute | solution.py:423
  15.4 16.1 %collective-permute-start.8 = (bf16[1200,128]{1,0:T(8,128)(2,1)S(1)}, bf16[1200,128]{1,0:T(8,128)(2,1)S(1)}, u32[]{:S(2)}, u32[]{:S(2)}) collective-permute-start(bf16[1200,128]{1,0:T(8,128)(2,1)S(1)} %get-tuple-element.47), channel_id=1, source_target_pairs={{4,8},{8,4},{5,9},{9,5},{6,10},{10,6},{7,11},{11,7},{20,24},{24,20... | collective-permute-start | bytes 921608 | tf_op jit(solution)/shard_map/ppermute | solution.py:422
  16.1 6.8 %collective-permute-start.2 = (bf16[18,32,128]{2,1,0:T(8,128)(2,1)S(1)}, bf16[18,32,128]{2,1,0:T(8,128)(2,1)S(1)}, u32[]{:S(2)}, u32[]{:S(2)}) collective-permute-start(bf16[18,32,128]{2,1,0:T(8,128)(2,1)S(1)} %collective-permute-done.1.refs_2_), channel_id=1, source_target_pairs={{0,16},{16,0},{1,17},{17,1},{2,18},{18,2},{3,19},{19,3},{4,20},{20... | collective-permute-start | bytes 442376 | tf_op jit(solution)/shard_map/ppermute | solution.py:352
  20.3 5.1 %collective-permute-start.4 = (bf16[18,32,128]{2,1,0:T(8,128)(2,1)S(1)}, bf16[18,32,128]{2,1,0:T(8,128)(2,1)S(1)}, u32[]{:S(2)}, u32[]{:S(2)}) collective-permute-start(bf16[18,32,128]{2,1,0:T(8,128)(2,1)S(1)} %collective-permute-done.3.refs_3_), channel_id=1, source_target_pairs={{0,16},{16,0},{1,17},{17,1},{2,18},{18,2},{3,19},{19,3},{4,20},{20... | collective-permute-start | bytes 442376 | tf_op jit(solution)/shard_map/ppermute | solution.py:352
  26.5 5.7 %collective-permute-start.5 = (f32[36,128]{1,0:T(8,128)S(1)}, f32[36,128]{1,0:T(8,128)S(1)}, u32[]{:S(2)}, u32[]{:S(2)}) collective-permute-start(f32[36,128]{1,0:T(8,128)S(1)} %get-tuple-element.51.refs_0_), channel_id=1, source_target_pairs={{0,12},{4,8},{8,4},{12,0},{1,13},{5,9},{9,5},{13,1},{2,14},{6,10},... | collective-permute-start | bytes 55304 | tf_op jit(solution)/shard_map/ppermute | solution.py:352
  29.2 5.0 %collective-permute-start.6 = (f32[36,128]{1,0:T(8,128)S(1)}, f32[36,128]{1,0:T(8,128)S(1)}, u32[]{:S(2)}, u32[]{:S(2)}) collective-permute-start(f32[36,128]{1,0:T(8,128)S(1)} %get-tuple-element.51.refs_0_), channel_id=1, source_target_pairs={{0,8},{4,12},{8,0},{12,4},{1,9},{5,13},{9,1},{13,5},{2,10},{6,14},... | collective-permute-start | bytes 55304 | tf_op jit(solution)/shard_map/ppermute | solution.py:352
  29.2 5.0 %collective-permute-start.7 = (f32[36,128]{1,0:T(8,128)S(1)}, f32[36,128]{1,0:T(8,128)S(1)}, u32[]{:S(2)}, u32[]{:S(2)}) collective-permute-start(f32[36,128]{1,0:T(8,128)S(1)} %get-tuple-element.51.refs_0_), channel_id=1, source_target_pairs={{0,4},{4,0},{8,12},{12,8},{1,5},{5,1},{9,13},{13,9},{2,6},{6,2},{1... | collective-permute-start | bytes 55304 | tf_op jit(solution)/shard_map/ppermute | solution.py:352
  34.2 11.7 %collective-permute-start.11 = (bf16[1200,128]{1,0:T(8,128)(2,1)S(1)}, bf16[1200,128]{1,0:T(8,128)(2,1)S(1)}, u32[]{:S(2)}, u32[]{:S(2)}) collective-permute-start(bf16[1200,128]{1,0:T(8,128)(2,1)S(1)} %get-tuple-element.60), channel_id=1, source_target_pairs={{0,4},{4,0},{8,12},{12,8},{1,5},{5,1},{9,13},{13,9},{2,6},{6,2},{1... | collective-permute-start | bytes 921608 | tf_op jit(solution)/shard_map/ppermute | solution.py:352
  35.1 11.9 %collective-permute-start.10 = (bf16[1200,128]{1,0:T(8,128)(2,1)S(1)}, bf16[1200,128]{1,0:T(8,128)(2,1)S(1)}, u32[]{:S(2)}, u32[]{:S(2)}) collective-permute-start(bf16[1200,128]{1,0:T(8,128)(2,1)S(1)} %relay_chunk.1), channel_id=1, source_target_pairs={{0,8},{4,12},{8,0},{12,4},{1,9},{5,13},{9,1},{13,5},{2,10},{6,14},... | collective-permute-start | bytes 921608 | tf_op jit(solution)/shard_map/ppermute | solution.py:352
  36.3 3.0 %collective-permute-start.12 = (f32[2,128]{1,0:T(2,128)S(1)}, f32[2,128]{1,0:T(2,128)S(1)}, u32[]{:S(2)}, u32[]{:S(2)}) collective-permute-start(f32[2,128]{1,0:T(2,128)S(1)} %get-tuple-element.57.refs_2_), channel_id=1, source_target_pairs={{0,3},{1,2},{2,1},{3,0},{4,7},{5,6},{6,5},{7,4},{8,11},{9,10},{10,... | collective-permute-start | bytes 3080 | tf_op jit(solution)/shard_map/ppermute | solution.py:352
  36.3 3.6 %collective-permute-start.13 = (f32[2,128]{1,0:T(2,128)S(1)}, f32[2,128]{1,0:T(2,128)S(1)}, u32[]{:S(2)}, u32[]{:S(2)}) collective-permute-start(f32[2,128]{1,0:T(2,128)S(1)} %get-tuple-element.57.refs_2_), channel_id=1, source_target_pairs={{0,2},{1,3},{2,0},{3,1},{4,6},{5,7},{6,4},{7,5},{8,10},{9,11},{10,... | collective-permute-start | bytes 3080 | tf_op jit(solution)/shard_map/ppermute | solution.py:352
  37.9 2.1 %collective-permute-start.14 = (f32[2,128]{1,0:T(2,128)S(1)}, f32[2,128]{1,0:T(2,128)S(1)}, u32[]{:S(2)}, u32[]{:S(2)}) collective-permute-start(f32[2,128]{1,0:T(2,128)S(1)} %get-tuple-element.57.refs_2_), channel_id=1, source_target_pairs={{0,1},{1,0},{2,3},{3,2},{4,5},{5,4},{6,7},{7,6},{8,9},{9,8},{10,11... | collective-permute-start | bytes 3080 | tf_op jit(solution)/shard_map/ppermute | solution.py:352
  41.4 3.1 %collective-permute-start.15 = (f32[2,512]{1,0:T(2,128)S(1)}, f32[2,512]{1,0:T(2,128)S(1)}, u32[]{:S(2)}, u32[]{:S(2)}) collective-permute-start(f32[2,512]{1,0:T(2,128)S(1)} %partial_weights.1.refs_2_), channel_id=1, source_target_pairs={{0,3},{1,2},{2,1},{3,0},{4,7},{5,6},{6,5},{7,4},{8,11},{9,10},{10,... | collective-permute-start | bytes 12296 | tf_op jit(solution)/shard_map/ppermute | solution.py:352
  42.3 3.6 %collective-permute-start.16 = (f32[2,512]{1,0:T(2,128)S(1)}, f32[2,512]{1,0:T(2,128)S(1)}, u32[]{:S(2)}, u32[]{:S(2)}) collective-permute-start(f32[2,512]{1,0:T(2,128)S(1)} %partial_weights.1.refs_2_), channel_id=1, source_target_pairs={{0,2},{1,3},{2,0},{3,1},{4,6},{5,7},{6,4},{7,5},{8,10},{9,11},{10,... | collective-permute-start | bytes 12296 | tf_op jit(solution)/shard_map/ppermute | solution.py:352
  43.8 2.1 %collective-permute-start.17 = (f32[2,512]{1,0:T(2,128)S(1)}, f32[2,512]{1,0:T(2,128)S(1)}, u32[]{:S(2)}, u32[]{:S(2)}) collective-permute-start(f32[2,512]{1,0:T(2,128)S(1)} %partial_weights.1.refs_2_), channel_id=1, source_target_pairs={{0,1},{1,0},{2,3},{3,2},{4,5},{5,4},{6,7},{7,6},{8,9},{9,8},{10,11... | collective-permute-start | bytes 12296 | tf_op jit(solution)/shard_map/ppermute | solution.py:352

commit v19 on v13

--- a/solution.py
+++ b/solution.py
@@ -441,7 +441,7 @@
             functools.partial(relay_kernel, coded[0]), message, "relay_chunk", 0, 12 * own.size,
             [IN_VMEM, IN_VMEM],
             [pltpu.VMEM((scale_rows(0, blocks), BLK), jnp.float32)] * 2,
-        )(*after([grams[1], relayed], sums))
+        )(*after([grams[1], relayed], (sums, middle)))
     sums = share(sums[0], "dp", direct)
     if pieces == 4:
         sums = after(sums, (middle, sent[2]))

time: 48.5 us -> 50.1 us (1.033)
  starting transfers between devices: 23.7 us -> 26.9 us
  waiting for transfers between devices: 12.3 us -> 10.7 us
    ppermute x1, starting transfers between devices: 3.32 us -> 6 us  [local(): relayed = lax.ppermute(sent[3], 'dp', [(0, 1), (3, 2)])]
    ppermute x16, waiting for transfers between devices: 12.3 us -> 10.7 us  [swap(): return lax.ppermute(value, axis, [(i, i ^ mask) for i in range(count)])]
    ppermute x16, starting transfers between devices: 19.7 us -> 20.2 us  [swap(): return lax.ppermute(value, axis, [(i, i ^ mask) for i in range(count)])]
  transfers between devices with their start and end apart: 18 -> 18, of which waited for: 9 -> 10; matrix products, arithmetic and copies ran while one was open for 0% -> 0% of each run, Pallas kernels for 19% -> 18%
where the time goes in v19:
time: 50.1 us; the launch traced here: 49.9 us
  starting transfers between devices  26.9 us (54%)
  Pallas kernels  11.6 us (23%)
  waiting for transfers between devices  10.7 us (21%)
  between operations  0.72 us (1%)
    ppermute x16, starting transfers between devices, swap(): return lax.ppermute(value, axis, [(i, i ^ mask) for i in range(count)])  20.2 us
    ppermute x16, waiting for transfers between devices, swap(): return lax.ppermute(value, axis, [(i, i ^ mask) for i in range(count)])  10.7 us
    ppermute x1, starting transfers between devices, local(): relayed = lax.ppermute(sent[3], 'dp', [(0, 1), (3, 2)])  6 us
    pallas_call x1, Pallas kernels, local(): call(functools.partial(gram_kernel, pieces, coded, scale), [bf16(*activat...  4.56 us
    pallas_call x2, Pallas kernels, local(): call(functools.partial(eigen_kernel, part, halves, masks, pieces, scale),...  1.94 us
    pallas_call x1, Pallas kernels, local(): call(functools.partial(weight_kernel, halves, act_blocks // halves), f32(...  1.49 us
    pallas_call x1, Pallas kernels, local(): call(functools.partial(last_add_kernel, [(None, 0, blocks)] * len(chunks)...  1.35 us
    pallas_call x1, Pallas kernels, local(): call(pack_kernel, [bf16(blocks // part, rows, BLK) for part in range(1, h...  1.08 us
  transfers between devices with their start and end apart: 18, of which 10 were waited for; matrix products, arithmetic and copies ran while one was open for 0% of the time, Pallas kernels for 18%

profile of v19, /device:TPU:0, one launch (start us, length us, event | category | flops | bytes accessed | tf_op | source)
XLA Modules:
  0.0 49.9 jit_solution(4547225298790932049)
XLA Ops:
  0.6 1.1 %pack_basis.1 = (bf16[36,32,128]{2,1,0:T(8,128)(2,1)S(1)}, bf16[18,32,128]{2,1,0:T(8,128)(2,1)S(1)}) custom-call(s32[1]{0:T(128)} %bitcast.side_ref, bf16[8,32,128]{2,1,0:T(8,128)(2,1)} %act_ref.1, bf16[28,32,128]{2,1,0:T(8,128)(2,1)} %grad_ref.1), custom_call_target="tpu_custom_call" | custom-call | bytes 294912 | tf_op jit(solution)/shard_map/pack_basis/pallas_call | solution.py:380
  1.7 5.1 %collective-permute-start.1 = (bf16[18,32,128]{2,1,0:T(8,128)(2,1)S(1)}, bf16[18,32,128]{2,1,0:T(8,128)(2,1)S(1)}, u32[]{:S(2)}, u32[]{:S(2)}) collective-permute-start(bf16[18,32,128]{2,1,0:T(8,128)(2,1)S(1)} %get-tuple-element.41), channel_id=1, source_target_pairs={{0,12},{4,8},{8,4},{12,0},{1,13},{5,9},{9,5},{13,1},{2,14},{6,10},... | collective-permute-start | bytes 442376 | tf_op jit(solution)/shard_map/ppermute | solution.py:352
  6.8 0.0 collective-permute-start.3
  6.8 0.6 %collective-permute-start = (bf16[36,32,128]{2,1,0:T(8,128)(2,1)S(1)}, bf16[36,32,128]{2,1,0:T(8,128)(2,1)S(1)}, u32[]{:S(2)}, u32[]{:S(2)}) collective-permute-start(bf16[36,32,128]{2,1,0:T(8,128)(2,1)S(1)} %get-tuple-element.40.refs_0_), channel_id=1, source_target_pairs={{0,4},{4,0},{8,12},{12,8},{1,5},{5,1},{9,13},{13,9},{2,6},{6,2},{1... | collective-permute-start | bytes 884744 | tf_op jit(solution)/shard_map/ppermute | solution.py:352
  7.5 4.6 %partial_gram.1 = (bf16[512,1024]{1,0:T(8,128)(2,1)S(1)}, bf16[512,3584]{1,0:T(8,128)(2,1)S(1)}, f32[36,32,128]{2,1,0:T(8,128)S(1)}, f32[36,32,128]{2,1,0:T(8,12...) custom-call(s32[1]{0:T(128)} %bitcast.1.me_ref, bf16[512,1024]{1,0:T(8,128)(2,1)} %act_hbm.1, ...), custom_call_target="tpu_custom_call" | custom-call | flops 1207959552 | bytes 4718592 | tf_op jit(solution)/shard_map/partial_gram/pallas_call | solution.py:401
  12.0 0.7 %collective-permute-start.8 = (bf16[1200,128]{1,0:T(8,128)(2,1)S(1)}, bf16[1200,128]{1,0:T(8,128)(2,1)S(1)}, u32[]{:S(2)}, u32[]{:S(2)}) collective-permute-start(bf16[1200,128]{1,0:T(8,128)(2,1)S(1)} %get-tuple-element.47), channel_id=1, source_target_pairs={{4,8},{8,4},{5,9},{9,5},{6,10},{10,6},{7,11},{11,7},{20,24},{24,20... | collective-permute-start | bytes 921608 | tf_op jit(solution)/shard_map/ppermute | solution.py:422
  12.7 6.0 %collective-permute-start.9 = (bf16[1200,128]{1,0:T(8,128)(2,1)S(1)}, bf16[1200,128]{1,0:T(8,128)(2,1)S(1)}, u32[]{:S(2)}, u32[]{:S(2)}) collective-permute-start(bf16[1200,128]{1,0:T(8,128)(2,1)S(1)} %get-tuple-element.47), channel_id=1, source_target_pairs={{0,4},{12,8},{1,5},{13,9},{2,6},{14,10},{3,7},{15,11},{16,20},{28,... | collective-permute-start | bytes 921608 | tf_op jit(solution)/shard_map/ppermute | solution.py:423
  18.7 0.0 collective-permute-done.1.refs_2_
  18.8 1.6 %collective-permute-start.2 = (bf16[18,32,128]{2,1,0:T(8,128)(2,1)S(1)}, bf16[18,32,128]{2,1,0:T(8,128)(2,1)S(1)}, u32[]{:S(2)}, u32[]{:S(2)}) collective-permute-start(bf16[18,32,128]{2,1,0:T(8,128)(2,1)S(1)} %collective-permute-done.1.refs_2_), channel_id=1, source_target_pairs={{0,16},{16,0},{1,17},{17,1},{2,18},{18,2},{3,19},{19,3},{4,20},{20... | collective-permute-start | bytes 442376 | tf_op jit(solution)/shard_map/ppermute | solution.py:352
  20.3 0.0 collective-permute-done.3.refs_3_
  20.3 1.5 %collective-permute-start.4 = (bf16[18,32,128]{2,1,0:T(8,128)(2,1)S(1)}, bf16[18,32,128]{2,1,0:T(8,128)(2,1)S(1)}, u32[]{:S(2)}, u32[]{:S(2)}) collective-permute-start(bf16[18,32,128]{2,1,0:T(8,128)(2,1)S(1)} %collective-permute-done.3.refs_3_), channel_id=1, source_target_pairs={{0,16},{16,0},{1,17},{17,1},{2,18},{18,2},{3,19},{19,3},{4,20},{20... | collective-permute-start | bytes 442376 | tf_op jit(solution)/shard_map/ppermute | solution.py:352
  21.8 0.0 collective-permute-done.refs_1_
  21.8 1.0 %partial_eigen.2 = (f32[9,512,256]{2,1,0:T(8,128)S(1)}, f32[18,128]{1,0:T(8,128)S(1)}) custom-call(s32[1]{0:T(128)} %bitcast.1.me_ref, s32[1]{0:T(128)} %bitcast.side_ref, bf16[512,1024]{1,0:T(8,128)(2,1)S(1)} %get-tuple-element.38.act_ref, bf16[512,3584]{1,0:T(8,128)(2,1)S(1)} %get-tuple-element.39.grad_ref, ...), custom_call_target="tpu_custom_call" | custom-call | flops 301989888 | bytes 2359296 | tf_op jit(solution)/shard_map/partial_eigen/pallas_call | solution.py:431
  22.8 2.1 %collective-permute-done.2.refs_2_ = bf16[18,32,128]{2,1,0:T(8,128)(2,1)S(1)} collective-permute-done((bf16[18,32,128]{2,1,0:T(8,128)(2,1)S(1)}, bf16[18,32,128]{2,1,0:T(8,128)(2,1)S(1)}, u32[]{:S(2)}, u32[]{:S(2)}) %collective-permute-start.2) | collective-permute-done | bytes 147488 | tf_op jit(solution)/shard_map/ppermute | solution.py:352
  24.9 1.6 %collective-permute-done.4.refs_3_ = bf16[18,32,128]{2,1,0:T(8,128)(2,1)S(1)} collective-permute-done((bf16[18,32,128]{2,1,0:T(8,128)(2,1)S(1)}, bf16[18,32,128]{2,1,0:T(8,128)(2,1)S(1)}, u32[]{:S(2)}, u32[]{:S(2)}) %collective-permute-start.4) | collective-permute-done | bytes 147488 | tf_op jit(solution)/shard_map/ppermute | solution.py:352
  26.5 1.0 %partial_eigen.3 = (f32[9,512,256]{2,1,0:T(8,128)S(1)}, f32[36,128]{1,0:T(8,128)S(1)}) custom-call(s32[1]{0:T(128)} %bitcast.1.me_ref, s32[1]{0:T(128)} %bitcast.side_ref, bf16[512,1024]{1,0:T(8,128)(2,1)S(1)} %get-tuple-element.38.act_ref, bf16[512,3584]{1,0:T(8,128)(2,1)S(1)} %get-tuple-element.39.grad_ref, ...), custom_call_target="tpu_custom_call" | custom-call | flops 301989888 | bytes 2359296 | tf_op jit(solution)/shard_map/partial_eigen/pallas_call | solution.py:431
  27.4 1.7 %collective-permute-start.5 = (f32[36,128]{1,0:T(8,128)S(1)}, f32[36,128]{1,0:T(8,128)S(1)}, u32[]{:S(2)}, u32[]{:S(2)}) collective-permute-start(f32[36,128]{1,0:T(8,128)S(1)} %get-tuple-element.51.refs_0_), channel_id=1, source_target_pairs={{0,12},{4,8},{8,4},{12,0},{1,13},{5,9},{9,5},{13,1},{2,14},{6,10},... | collective-permute-start | bytes 55304 | tf_op jit(solution)/shard_map/ppermute | solution.py:352
  29.2 0.0 collective-permute-start.6
  29.2 2.7 %collective-permute-start.7 = (f32[36,128]{1,0:T(8,128)S(1)}, f32[36,128]{1,0:T(8,128)S(1)}, u32[]{:S(2)}, u32[]{:S(2)}) collective-permute-start(f32[36,128]{1,0:T(8,128)S(1)} %get-tuple-element.51.refs_0_), channel_id=1, source_target_pairs={{0,4},{4,0},{8,12},{12,8},{1,5},{5,1},{9,13},{13,9},{2,6},{6,2},{1... | collective-permute-start | bytes 55304 | tf_op jit(solution)/shard_map/ppermute | solution.py:352
  31.9 0.0 collective-permute-done.8.refs_0_
  31.9 0.0 collective-permute-done.9.relayed_ref
  31.9 0.6 %relay_chunk.1 = bf16[1200,128]{1,0:T(8,128)(2,1)S(1)} custom-call(f32[36,32,128]{2,1,0:T(8,128)S(1)} %get-tuple-element.49.far_ref, bf16[1200,128]{1,0:T(8,128)(2,1)S(1)} %collective-permute-done.9.relayed_ref), custom_call_target="tpu_custom_call" | custom-call | bytes 1769472 | tf_op jit(solution)/shard_map/relay_chunk/pallas_call | solution.py:440
  32.5 0.6 %collective-permute-done.5.refs_1_ = f32[36,128]{1,0:T(8,128)S(1)} collective-permute-done((f32[36,128]{1,0:T(8,128)S(1)}, f32[36,128]{1,0:T(8,128)S(1)}, u32[]{:S(2)}, u32[]{:S(2)}) %collective-permute-start.5) | collective-permute-done | bytes 18464 | tf_op jit(solution)/shard_map/ppermute | solution.py:352
  33.1 0.9 %collective-permute-done.6.refs_2_ = f32[36,128]{1,0:T(8,128)S(1)} collective-permute-done((f32[36,128]{1,0:T(8,128)S(1)}, f32[36,128]{1,0:T(8,128)S(1)}, u32[]{:S(2)}, u32[]{:S(2)}) %collective-permute-start.6) | collective-permute-done | bytes 18464 | tf_op jit(solution)/shard_map/ppermute | solution.py:352
  34.0 0.1 collective-permute-done.7.refs_3_
  34.1 1.9 %collective-permute-start.11 = (bf16[1200,128]{1,0:T(8,128)(2,1)S(1)}, bf16[1200,128]{1,0:T(8,128)(2,1)S(1)}, u32[]{:S(2)}, u32[]{:S(2)}) collective-permute-start(bf16[1200,128]{1,0:T(8,128)(2,1)S(1)} %get-tuple-element.60), channel_id=1, source_target_pairs={{0,4},{4,0},{8,12},{12,8},{1,5},{5,1},{9,13},{13,9},{2,6},{6,2},{1... | collective-permute-start | bytes 921608 | tf_op jit(solution)/shard_map/ppermute | solution.py:352
  36.0 0.8 %collective-permute-start.10 = (bf16[1200,128]{1,0:T(8,128)(2,1)S(1)}, bf16[1200,128]{1,0:T(8,128)(2,1)S(1)}, u32[]{:S(2)}, u32[]{:S(2)}) collective-permute-start(bf16[1200,128]{1,0:T(8,128)(2,1)S(1)} %relay_chunk.1), channel_id=1, source_target_pairs={{0,8},{4,12},{8,0},{12,4},{1,9},{5,13},{9,1},{13,5},{2,10},{6,14},... | collective-permute-start | bytes 921608 | tf_op jit(solution)/shard_map/ppermute | solution.py:352
  36.8 0.0 collective-permute-start.12
  36.8 1.5 %collective-permute-start.13 = (f32[2,128]{1,0:T(2,128)S(1)}, f32[2,128]{1,0:T(2,128)S(1)}, u32[]{:S(2)}, u32[]{:S(2)}) collective-permute-start(f32[2,128]{1,0:T(2,128)S(1)} %get-tuple-element.57.refs_2_), channel_id=1, source_target_pairs={{0,2},{1,3},{2,0},{3,1},{4,6},{5,7},{6,4},{7,5},{8,10},{9,11},{10,... | collective-permute-start | bytes 3080 | tf_op jit(solution)/shard_map/ppermute | solution.py:352
  38.3 0.3 collective-permute-start.14
  38.6 1.1 %collective-permute-done.12.refs_3_ = f32[2,128]{1,0:T(2,128)S(1)} collective-permute-done((f32[2,128]{1,0:T(2,128)S(1)}, f32[2,128]{1,0:T(2,128)S(1)}, u32[]{:S(2)}, u32[]{:S(2)}) %collective-permute-start.12) | collective-permute-done | bytes 1056 | tf_op jit(solution)/shard_map/ppermute | solution.py:352
  39.8 0.6 %collective-permute-done.13.refs_4_ = f32[2,128]{1,0:T(2,128)S(1)} collective-permute-done((f32[2,128]{1,0:T(2,128)S(1)}, f32[2,128]{1,0:T(2,128)S(1)}, u32[]{:S(2)}, u32[]{:S(2)}) %collective-permute-start.13) | collective-permute-done | bytes 1056 | tf_op jit(solution)/shard_map/ppermute | solution.py:352
  40.4 0.0 collective-permute-done.14.refs_5_
  40.4 1.5 %partial_weights.1.refs_2_ = f32[2,512]{1,0:T(2,128)S(1)} custom-call(f32[36,128]{1,0:T(8,128)S(1)} %get-tuple-element.55.eigen_ref, f32[9,512,256]{2,1,0:T(8,128)S(1)} %get-tuple-element.61.refs_0_, f32[9,512,256]{2,1,0:T(8,128)S(1)} %get-tuple-element.62.refs_1_, f32[2,128]{1,0:T(2,128)S(1)} %get-tuple-element.57.refs_2_, ...), custom_call_target="tpu_custom_call" | custom-call | bytes 9437184 | tf_op jit(solution)/shard_map/partial_weights/pallas_call | solution.py:458
  41.9 0.9 %collective-permute-start.15 = (f32[2,512]{1,0:T(2,128)S(1)}, f32[2,512]{1,0:T(2,128)S(1)}, u32[]{:S(2)}, u32[]{:S(2)}) collective-permute-start(f32[2,512]{1,0:T(2,128)S(1)} %partial_weights.1.refs_2_), channel_id=1, source_target_pairs={{0,3},{1,2},{2,1},{3,0},{4,7},{5,6},{6,5},{7,4},{8,11},{9,10},{10,... | collective-permute-start | bytes 12296 | tf_op jit(solution)/shard_map/ppermute | solution.py:352
  42.7 1.5 %collective-permute-start.16 = (f32[2,512]{1,0:T(2,128)S(1)}, f32[2,512]{1,0:T(2,128)S(1)}, u32[]{:S(2)}, u32[]{:S(2)}) collective-permute-start(f32[2,512]{1,0:T(2,128)S(1)} %partial_weights.1.refs_2_), channel_id=1, source_target_pairs={{0,2},{1,3},{2,0},{3,1},{4,6},{5,7},{6,4},{7,5},{8,10},{9,11},{10,... | collective-permute-start | bytes 12296 | tf_op jit(solution)/shard_map/ppermute | solution.py:352
  44.2 0.0 collective-permute-start.17
  44.2 0.6 %add_chunk.1 = (f32[36,32,128]{2,1,0:T(8,128)S(1)}, f32[8,128]{1,0:T(8,128)}, f32[28,128]{1,0:T(8,128)}) custom-call(s32[1]{0:T(128)} %bitcast.side_ref, f32[36,128]{1,0:T(8,128)S(1)} %get-tuple-element.55.eigen_ref, f32[36,32,128]{2,1,0:T(8,128)S(1)} %get-tuple-element.42.own_ref, bf16[1200,128]{1,0:T(8,128)(2,1)S(1)} %collective-permute-done.8.refs_0_), custom_call_target="tpu_custom_call" | custom-call | bytes 1769472 | tf_op jit(solution)/shard_map/add_chunk/pallas_call | solution.py:475
  44.9 0.1 collective-permute-done.15.refs_3_
  44.9 1.4 %collective-permute-done.16.refs_4_ = f32[2,512]{1,0:T(2,128)S(1)} collective-permute-done((f32[2,512]{1,0:T(2,128)S(1)}, f32[2,512]{1,0:T(2,128)S(1)}, u32[]{:S(2)}, u32[]{:S(2)}) %collective-permute-start.16) | collective-permute-done | bytes 4128 | tf_op jit(solution)/shard_map/ppermute | solution.py:352
  46.4 0.0 collective-permute-done.17.refs_5_
  46.4 0.0 collective-permute-done.11.refs_1_
  46.4 2.2 %collective-permute-done.10.refs_0_ = bf16[1200,128]{1,0:T(8,128)(2,1)S(1)} collective-permute-done((bf16[1200,128]{1,0:T(8,128)(2,1)S(1)}, bf16[1200,128]{1,0:T(8,128)(2,1)S(1)}, u32[]{:S(2)}, u32[]{:S(2)}) %collective-permute-start.10) | collective-permute-done | bytes 307232 | tf_op jit(solution)/shard_map/ppermute | solution.py:352
  48.5 1.4 %last_sums.1 = (f32[8,32,128]{2,1,0:T(8,128)}, f32[28,32,128]{2,1,0:T(8,128)}, f32[1,512]{1,0:T(1,128)}) custom-call(f32[36,32,128]{2,1,0:T(8,128)S(1)} %get-tuple-element.56.own_ref, bf16[1200,128]{1,0:T(8,128)(2,1)S(1)} %collective-permute-done.10.refs_0_, bf16[1200,128]{1,0:T(8,128)(2,1)S(1)} %collective-permute-done.11.refs_1_, ...), custom_call_target="tpu_custom_call" | custom-call | bytes 2359296 | tf_op jit(solution)/shard_map/last_sums/pallas_call | solution.py:488
  (1 shorter events, 0.0 us)
Async XLA Ops:
  1.7 17.0 %collective-permute-start.1 = (bf16[18,32,128]{2,1,0:T(8,128)(2,1)S(1)}, bf16[18,32,128]{2,1,0:T(8,128)(2,1)S(1)}, u32[]{:S(2)}, u32[]{:S(2)}) collective-permute-start(bf16[18,32,128]{2,1,0:T(8,128)(2,1)S(1)} %get-tuple-element.41), channel_id=1, source_target_pairs={{0,12},{4,8},{8,4},{12,0},{1,13},{5,9},{9,5},{13,1},{2,14},{6,10},... | collective-permute-start | bytes 442376 | tf_op jit(solution)/shard_map/ppermute | solution.py:352
  6.8 13.5 %collective-permute-start.3 = (bf16[18,32,128]{2,1,0:T(8,128)(2,1)S(1)}, bf16[18,32,128]{2,1,0:T(8,128)(2,1)S(1)}, u32[]{:S(2)}, u32[]{:S(2)}) collective-permute-start(bf16[18,32,128]{2,1,0:T(8,128)(2,1)S(1)} %get-tuple-element.41), channel_id=1, source_target_pairs={{0,8},{4,12},{8,0},{12,4},{1,9},{5,13},{9,1},{13,5},{2,10},{6,14},... | collective-permute-start | bytes 442376 | tf_op jit(solution)/shard_map/ppermute | solution.py:352
  6.8 15.0 %collective-permute-start = (bf16[36,32,128]{2,1,0:T(8,128)(2,1)S(1)}, bf16[36,32,128]{2,1,0:T(8,128)(2,1)S(1)}, u32[]{:S(2)}, u32[]{:S(2)}) collective-permute-start(bf16[36,32,128]{2,1,0:T(8,128)(2,1)S(1)} %get-tuple-element.40.refs_0_), channel_id=1, source_target_pairs={{0,4},{4,0},{8,12},{12,8},{1,5},{5,1},{9,13},{13,9},{2,6},{6,2},{1... | collective-permute-start | bytes 884744 | tf_op jit(solution)/shard_map/ppermute | solution.py:352
  12.0 19.8 %collective-permute-start.8 = (bf16[1200,128]{1,0:T(8,128)(2,1)S(1)}, bf16[1200,128]{1,0:T(8,128)(2,1)S(1)}, u32[]{:S(2)}, u32[]{:S(2)}) collective-permute-start(bf16[1200,128]{1,0:T(8,128)(2,1)S(1)} %get-tuple-element.47), channel_id=1, source_target_pairs={{4,8},{8,4},{5,9},{9,5},{6,10},{10,6},{7,11},{11,7},{20,24},{24,20... | collective-permute-start | bytes 921608 | tf_op jit(solution)/shard_map/ppermute | solution.py:422
  12.7 19.2 %collective-permute-start.9 = (bf16[1200,128]{1,0:T(8,128)(2,1)S(1)}, bf16[1200,128]{1,0:T(8,128)(2,1)S(1)}, u32[]{:S(2)}, u32[]{:S(2)}) collective-permute-start(bf16[1200,128]{1,0:T(8,128)(2,1)S(1)} %get-tuple-element.47), channel_id=1, source_target_pairs={{0,4},{12,8},{1,5},{13,9},{2,6},{14,10},{3,7},{15,11},{16,20},{28,... | collective-permute-start | bytes 921608 | tf_op jit(solution)/shard_map/ppermute | solution.py:423
  18.8 6.1 %collective-permute-start.2 = (bf16[18,32,128]{2,1,0:T(8,128)(2,1)S(1)}, bf16[18,32,128]{2,1,0:T(8,128)(2,1)S(1)}, u32[]{:S(2)}, u32[]{:S(2)}) collective-permute-start(bf16[18,32,128]{2,1,0:T(8,128)(2,1)S(1)} %collective-permute-done.1.refs_2_), channel_id=1, source_target_pairs={{0,16},{16,0},{1,17},{17,1},{2,18},{18,2},{3,19},{19,3},{4,20},{20... | collective-permute-start | bytes 442376 | tf_op jit(solution)/shard_map/ppermute | solution.py:352
  20.3 6.1 %collective-permute-start.4 = (bf16[18,32,128]{2,1,0:T(8,128)(2,1)S(1)}, bf16[18,32,128]{2,1,0:T(8,128)(2,1)S(1)}, u32[]{:S(2)}, u32[]{:S(2)}) collective-permute-start(bf16[18,32,128]{2,1,0:T(8,128)(2,1)S(1)} %collective-permute-done.3.refs_3_), channel_id=1, source_target_pairs={{0,16},{16,0},{1,17},{17,1},{2,18},{18,2},{3,19},{19,3},{4,20},{20... | collective-permute-start | bytes 442376 | tf_op jit(solution)/shard_map/ppermute | solution.py:352
  27.4 5.6 %collective-permute-start.5 = (f32[36,128]{1,0:T(8,128)S(1)}, f32[36,128]{1,0:T(8,128)S(1)}, u32[]{:S(2)}, u32[]{:S(2)}) collective-permute-start(f32[36,128]{1,0:T(8,128)S(1)} %get-tuple-element.51.refs_0_), channel_id=1, source_target_pairs={{0,12},{4,8},{8,4},{12,0},{1,13},{5,9},{9,5},{13,1},{2,14},{6,10},... | collective-permute-start | bytes 55304 | tf_op jit(solution)/shard_map/ppermute | solution.py:352
  29.2 4.8 %collective-permute-start.6 = (f32[36,128]{1,0:T(8,128)S(1)}, f32[36,128]{1,0:T(8,128)S(1)}, u32[]{:S(2)}, u32[]{:S(2)}) collective-permute-start(f32[36,128]{1,0:T(8,128)S(1)} %get-tuple-element.51.refs_0_), channel_id=1, source_target_pairs={{0,8},{4,12},{8,0},{12,4},{1,9},{5,13},{9,1},{13,5},{2,10},{6,14},... | collective-permute-start | bytes 55304 | tf_op jit(solution)/shard_map/ppermute | solution.py:352
  29.2 4.9 %collective-permute-start.7 = (f32[36,128]{1,0:T(8,128)S(1)}, f32[36,128]{1,0:T(8,128)S(1)}, u32[]{:S(2)}, u32[]{:S(2)}) collective-permute-start(f32[36,128]{1,0:T(8,128)S(1)} %get-tuple-element.51.refs_0_), channel_id=1, source_target_pairs={{0,4},{4,0},{8,12},{12,8},{1,5},{5,1},{9,13},{13,9},{2,6},{6,2},{1... | collective-permute-start | bytes 55304 | tf_op jit(solution)/shard_map/ppermute | solution.py:352
  34.1 12.2 %collective-permute-start.11 = (bf16[1200,128]{1,0:T(8,128)(2,1)S(1)}, bf16[1200,128]{1,0:T(8,128)(2,1)S(1)}, u32[]{:S(2)}, u32[]{:S(2)}) collective-permute-start(bf16[1200,128]{1,0:T(8,128)(2,1)S(1)} %get-tuple-element.60), channel_id=1, source_target_pairs={{0,4},{4,0},{8,12},{12,8},{1,5},{5,1},{9,13},{13,9},{2,6},{6,2},{1... | collective-permute-start | bytes 921608 | tf_op jit(solution)/shard_map/ppermute | solution.py:352
  36.0 12.6 %collective-permute-start.10 = (bf16[1200,128]{1,0:T(8,128)(2,1)S(1)}, bf16[1200,128]{1,0:T(8,128)(2,1)S(1)}, u32[]{:S(2)}, u32[]{:S(2)}) collective-permute-start(bf16[1200,128]{1,0:T(8,128)(2,1)S(1)} %relay_chunk.1), channel_id=1, source_target_pairs={{0,8},{4,12},{8,0},{12,4},{1,9},{5,13},{9,1},{13,5},{2,10},{6,14},... | collective-permute-start | bytes 921608 | tf_op jit(solution)/shard_map/ppermute | solution.py:352
  36.8 3.0 %collective-permute-start.12 = (f32[2,128]{1,0:T(2,128)S(1)}, f32[2,128]{1,0:T(2,128)S(1)}, u32[]{:S(2)}, u32[]{:S(2)}) collective-permute-start(f32[2,128]{1,0:T(2,128)S(1)} %get-tuple-element.57.refs_2_), channel_id=1, source_target_pairs={{0,3},{1,2},{2,1},{3,0},{4,7},{5,6},{6,5},{7,4},{8,11},{9,10},{10,... | collective-permute-start | bytes 3080 | tf_op jit(solution)/shard_map/ppermute | solution.py:352
  36.8 3.6 %collective-permute-start.13 = (f32[2,128]{1,0:T(2,128)S(1)}, f32[2,128]{1,0:T(2,128)S(1)}, u32[]{:S(2)}, u32[]{:S(2)}) collective-permute-start(f32[2,128]{1,0:T(2,128)S(1)} %get-tuple-element.57.refs_2_), channel_id=1, source_target_pairs={{0,2},{1,3},{2,0},{3,1},{4,6},{5,7},{6,4},{7,5},{8,10},{9,11},{10,... | collective-permute-start | bytes 3080 | tf_op jit(solution)/shard_map/ppermute | solution.py:352
  38.3 2.1 %collective-permute-start.14 = (f32[2,128]{1,0:T(2,128)S(1)}, f32[2,128]{1,0:T(2,128)S(1)}, u32[]{:S(2)}, u32[]{:S(2)}) collective-permute-start(f32[2,128]{1,0:T(2,128)S(1)} %get-tuple-element.57.refs_2_), channel_id=1, source_target_pairs={{0,1},{1,0},{2,3},{3,2},{4,5},{5,4},{6,7},{7,6},{8,9},{9,8},{10,11... | collective-permute-start | bytes 3080 | tf_op jit(solution)/shard_map/ppermute | solution.py:352
  41.9 3.1 %collective-permute-start.15 = (f32[2,512]{1,0:T(2,128)S(1)}, f32[2,512]{1,0:T(2,128)S(1)}, u32[]{:S(2)}, u32[]{:S(2)}) collective-permute-start(f32[2,512]{1,0:T(2,128)S(1)} %partial_weights.1.refs_2_), channel_id=1, source_target_pairs={{0,3},{1,2},{2,1},{3,0},{4,7},{5,6},{6,5},{7,4},{8,11},{9,10},{10,... | collective-permute-start | bytes 12296 | tf_op jit(solution)/shard_map/ppermute | solution.py:352
  42.7 3.6 %collective-permute-start.16 = (f32[2,512]{1,0:T(2,128)S(1)}, f32[2,512]{1,0:T(2,128)S(1)}, u32[]{:S(2)}, u32[]{:S(2)}) collective-permute-start(f32[2,512]{1,0:T(2,128)S(1)} %partial_weights.1.refs_2_), channel_id=1, source_target_pairs={{0,2},{1,3},{2,0},{3,1},{4,6},{5,7},{6,4},{7,5},{8,10},{9,11},{10,... | collective-permute-start | bytes 12296 | tf_op jit(solution)/shard_map/ppermute | solution.py:352
  44.2 2.1 %collective-permute-start.17 = (f32[2,512]{1,0:T(2,128)S(1)}, f32[2,512]{1,0:T(2,128)S(1)}, u32[]{:S(2)}, u32[]{:S(2)}) collective-permute-start(f32[2,512]{1,0:T(2,128)S(1)} %partial_weights.1.refs_2_), channel_id=1, source_target_pairs={{0,1},{1,0},{2,3},{3,2},{4,5},{5,4},{6,7},{7,6},{8,9},{9,8},{10,11... | collective-permute-start | bytes 12296 | tf_op jit(solution)/shard_map/ppermute | solution.py:352

commit v20 on v18

--- a/solution.py
+++ b/solution.py
@@ -175,6 +175,14 @@
     load_tops(messages, rows, sent_refs, tops_refs)
     for step in range(blocks // GROUP):
         for block, total in add_group(messages, rows, own_ref, sent_refs, tops_refs, step):
+            sum_ref[block] = total
+
+
+def near_kernel(messages, own_ref, sent_ref, sum_ref, tops):
+    blocks, rows, _ = own_ref.shape
+    load_tops(messages, rows, (sent_ref,), (tops,))
+    for step in range(blocks // GROUP):
+        for block, total in add_group(messages, rows, own_ref, (sent_ref,), (tops,), step):
             sum_ref[block] = total
 
 
@@ -483,7 +491,12 @@
             functools.partial(order_kernel, halves), eigens, "order_eigen", 0,
             8 * blocks * BLK, [IN_SMEM, IN_VMEM],
         )(side, eigen)
-    chunks = list(arrived.values())[::-1]
+    if pieces == 4:
+        own = call(
+            functools.partial(near_kernel, [(None, 0, blocks)]), f32(*own.shape), "add_near", 0,
+            12 * own.size, [IN_VMEM] * 2, tops_of(1),
+        )(own, arrived.pop(1))
+    chunks = list(arrived.values())
     if chunks:
         *covariance, token_scores = call(
             functools.partial(last_add_kernel, [(None, 0, blocks)] * len(chunks), len(weights)),

time: 48.4 us -> 48.1 us (level)
  transfers between devices with their start and end apart: 18 -> 18, of which waited for: 9 -> 9; matrix products, arithmetic and copies ran while one was open for 0% -> 0% of each run, Pallas kernels for 19% -> 20%
where the time goes in v20:
time: 48.1 us; the launch traced here: 48 us
  starting transfers between devices  23.7 us (49%)
  waiting for transfers between devices  12.1 us (25%)
  Pallas kernels  11.5 us (24%)
  between operations  0.74 us (2%)
    ppermute x16, starting transfers between devices, swap(): return lax.ppermute(value, axis, [(i, i ^ mask) for i in range(count)])  19.7 us
    ppermute x16, waiting for transfers between devices, swap(): return lax.ppermute(value, axis, [(i, i ^ mask) for i in range(count)])  12.1 us
    pallas_call x1, Pallas kernels, local(): call(functools.partial(gram_kernel, pieces, coded, scale), [bf16(*activat...  4.56 us
    ppermute x1, starting transfers between devices, local(): relayed = lax.ppermute(sent[3], 'dp', [(0, 1), (3, 2)])  3.32 us
    pallas_call x2, Pallas kernels, local(): call(functools.partial(eigen_kernel, part, halves, masks, pieces, scale),...  1.95 us
    pallas_call x1, Pallas kernels, local(): call(functools.partial(weight_kernel, halves, act_blocks // halves), f32(...  1.49 us
    pallas_call x1, Pallas kernels, local(): call(pack_kernel, [bf16(blocks // part, rows, BLK) for part in range(1, h...  1.08 us
    pallas_call x1, Pallas kernels, local(): call(functools.partial(last_add_kernel, [(None, 0, blocks)] * len(chunks)...  0.99 us
  transfers between devices with their start and end apart: 18, of which 9 were waited for; matrix products, arithmetic and copies ran while one was open for 0% of the time, Pallas kernels for 20%

profile of v20, /device:TPU:0, one launch (start us, length us, event | category | flops | bytes accessed | tf_op | source)
XLA Modules:
  0.0 48.0 jit_solution(3679742991818603018)
XLA Ops:
  0.6 1.1 %pack_basis.1 = (bf16[36,32,128]{2,1,0:T(8,128)(2,1)S(1)}, bf16[18,32,128]{2,1,0:T(8,128)(2,1)S(1)}) custom-call(s32[1]{0:T(128)} %bitcast.side_ref, bf16[8,32,128]{2,1,0:T(8,128)(2,1)} %act_ref.1, bf16[28,32,128]{2,1,0:T(8,128)(2,1)} %grad_ref.1), custom_call_target="tpu_custom_call" | custom-call | bytes 294912 | tf_op jit(solution)/shard_map/pack_basis/pallas_call | solution.py:388
  1.7 5.1 %collective-permute-start.1 = (bf16[18,32,128]{2,1,0:T(8,128)(2,1)S(1)}, bf16[18,32,128]{2,1,0:T(8,128)(2,1)S(1)}, u32[]{:S(2)}, u32[]{:S(2)}) collective-permute-start(bf16[18,32,128]{2,1,0:T(8,128)(2,1)S(1)} %get-tuple-element.41), channel_id=1, source_target_pairs={{0,12},{4,8},{8,4},{12,0},{1,13},{5,9},{9,5},{13,1},{2,14},{6,10},... | collective-permute-start | bytes 442376 | tf_op jit(solution)/shard_map/ppermute | solution.py:360
  6.8 0.0 collective-permute-start.3
  6.8 0.6 %collective-permute-start = (bf16[36,32,128]{2,1,0:T(8,128)(2,1)S(1)}, bf16[36,32,128]{2,1,0:T(8,128)(2,1)S(1)}, u32[]{:S(2)}, u32[]{:S(2)}) collective-permute-start(bf16[36,32,128]{2,1,0:T(8,128)(2,1)S(1)} %get-tuple-element.40.refs_0_), channel_id=1, source_target_pairs={{0,4},{4,0},{8,12},{12,8},{1,5},{5,1},{9,13},{13,9},{2,6},{6,2},{1... | collective-permute-start | bytes 884744 | tf_op jit(solution)/shard_map/ppermute | solution.py:360
  7.5 4.6 %partial_gram.1 = (bf16[512,1024]{1,0:T(8,128)(2,1)S(1)}, bf16[512,3584]{1,0:T(8,128)(2,1)S(1)}, f32[36,32,128]{2,1,0:T(8,128)S(1)}, f32[36,32,128]{2,1,0:T(8,12...) custom-call(s32[1]{0:T(128)} %bitcast.1.me_ref, bf16[512,1024]{1,0:T(8,128)(2,1)} %act_hbm.1, ...), custom_call_target="tpu_custom_call" | custom-call | flops 1207959552 | bytes 4718592 | tf_op jit(solution)/shard_map/partial_gram/pallas_call | solution.py:409
  12.0 3.3 %collective-permute-start.9 = (bf16[1200,128]{1,0:T(8,128)(2,1)S(1)}, bf16[1200,128]{1,0:T(8,128)(2,1)S(1)}, u32[]{:S(2)}, u32[]{:S(2)}) collective-permute-start(bf16[1200,128]{1,0:T(8,128)(2,1)S(1)} %get-tuple-element.47), channel_id=1, source_target_pairs={{0,4},{12,8},{1,5},{13,9},{2,6},{14,10},{3,7},{15,11},{16,20},{28,... | collective-permute-start | bytes 921608 | tf_op jit(solution)/shard_map/ppermute | solution.py:431
  15.4 0.7 %collective-permute-start.8 = (bf16[1200,128]{1,0:T(8,128)(2,1)S(1)}, bf16[1200,128]{1,0:T(8,128)(2,1)S(1)}, u32[]{:S(2)}, u32[]{:S(2)}) collective-permute-start(bf16[1200,128]{1,0:T(8,128)(2,1)S(1)} %get-tuple-element.47), channel_id=1, source_target_pairs={{4,8},{8,4},{5,9},{9,5},{6,10},{10,6},{7,11},{11,7},{20,24},{24,20... | collective-permute-start | bytes 921608 | tf_op jit(solution)/shard_map/ppermute | solution.py:430
  16.1 0.0 collective-permute-done.1.refs_2_
  16.1 1.6 %collective-permute-start.2 = (bf16[18,32,128]{2,1,0:T(8,128)(2,1)S(1)}, bf16[18,32,128]{2,1,0:T(8,128)(2,1)S(1)}, u32[]{:S(2)}, u32[]{:S(2)}) collective-permute-start(bf16[18,32,128]{2,1,0:T(8,128)(2,1)S(1)} %collective-permute-done.1.refs_2_), channel_id=1, source_target_pairs={{0,16},{16,0},{1,17},{17,1},{2,18},{18,2},{3,19},{19,3},{4,20},{20... | collective-permute-start | bytes 442376 | tf_op jit(solution)/shard_map/ppermute | solution.py:360
  17.6 2.7 %collective-permute-done.3.refs_3_ = bf16[18,32,128]{2,1,0:T(8,128)(2,1)S(1)} collective-permute-done((bf16[18,32,128]{2,1,0:T(8,128)(2,1)S(1)}, bf16[18,32,128]{2,1,0:T(8,128)(2,1)S(1)}, u32[]{:S(2)}, u32[]{:S(2)}) %collective-permute-start.3) | collective-permute-done | bytes 147488 | tf_op jit(solution)/shard_map/ppermute | solution.py:360
  20.3 1.5 %collective-permute-start.4 = (bf16[18,32,128]{2,1,0:T(8,128)(2,1)S(1)}, bf16[18,32,128]{2,1,0:T(8,128)(2,1)S(1)}, u32[]{:S(2)}, u32[]{:S(2)}) collective-permute-start(bf16[18,32,128]{2,1,0:T(8,128)(2,1)S(1)} %collective-permute-done.3.refs_3_), channel_id=1, source_target_pairs={{0,16},{16,0},{1,17},{17,1},{2,18},{18,2},{3,19},{19,3},{4,20},{20... | collective-permute-start | bytes 442376 | tf_op jit(solution)/shard_map/ppermute | solution.py:360
  21.8 0.0 collective-permute-done.refs_1_
  21.8 1.0 %partial_eigen.2 = (f32[9,512,256]{2,1,0:T(8,128)S(1)}, f32[18,128]{1,0:T(8,128)S(1)}) custom-call(s32[1]{0:T(128)} %bitcast.1.me_ref, s32[1]{0:T(128)} %bitcast.side_ref, bf16[512,1024]{1,0:T(8,128)(2,1)S(1)} %get-tuple-element.38.act_ref, bf16[512,3584]{1,0:T(8,128)(2,1)S(1)} %get-tuple-element.39.grad_ref, ...), custom_call_target="tpu_custom_call" | custom-call | flops 301989888 | bytes 2359296 | tf_op jit(solution)/shard_map/partial_eigen/pallas_call | solution.py:439
  22.8 0.0 collective-permute-done.2.refs_2_
  22.8 2.6 %collective-permute-done.4.refs_3_ = bf16[18,32,128]{2,1,0:T(8,128)(2,1)S(1)} collective-permute-done((bf16[18,32,128]{2,1,0:T(8,128)(2,1)S(1)}, bf16[18,32,128]{2,1,0:T(8,128)(2,1)S(1)}, u32[]{:S(2)}, u32[]{:S(2)}) %collective-permute-start.4) | collective-permute-done | bytes 147488 | tf_op jit(solution)/shard_map/ppermute | solution.py:360
  25.5 1.0 %partial_eigen.3 = (f32[9,512,256]{2,1,0:T(8,128)S(1)}, f32[36,128]{1,0:T(8,128)S(1)}) custom-call(s32[1]{0:T(128)} %bitcast.1.me_ref, s32[1]{0:T(128)} %bitcast.side_ref, bf16[512,1024]{1,0:T(8,128)(2,1)S(1)} %get-tuple-element.38.act_ref, bf16[512,3584]{1,0:T(8,128)(2,1)S(1)} %get-tuple-element.39.grad_ref, ...), custom_call_target="tpu_custom_call" | custom-call | flops 301989888 | bytes 2359296 | tf_op jit(solution)/shard_map/partial_eigen/pallas_call | solution.py:439
  26.5 2.7 %collective-permute-start.5 = (f32[36,128]{1,0:T(8,128)S(1)}, f32[36,128]{1,0:T(8,128)S(1)}, u32[]{:S(2)}, u32[]{:S(2)}) collective-permute-start(f32[36,128]{1,0:T(8,128)S(1)} %get-tuple-element.51.refs_0_), channel_id=1, source_target_pairs={{0,12},{4,8},{8,4},{12,0},{1,13},{5,9},{9,5},{13,1},{2,14},{6,10},... | collective-permute-start | bytes 55304 | tf_op jit(solution)/shard_map/ppermute | solution.py:360
  29.2 0.0 collective-permute-start.6
  29.2 1.7 %collective-permute-start.7 = (f32[36,128]{1,0:T(8,128)S(1)}, f32[36,128]{1,0:T(8,128)S(1)}, u32[]{:S(2)}, u32[]{:S(2)}) collective-permute-start(f32[36,128]{1,0:T(8,128)S(1)} %get-tuple-element.51.refs_0_), channel_id=1, source_target_pairs={{0,4},{4,0},{8,12},{12,8},{1,5},{5,1},{9,13},{13,9},{2,6},{6,2},{1... | collective-permute-start | bytes 55304 | tf_op jit(solution)/shard_map/ppermute | solution.py:360
  30.9 0.0 collective-permute-done.9.relayed_ref
  30.9 0.5 %relay_chunk.1 = bf16[1200,128]{1,0:T(8,128)(2,1)S(1)} custom-call(f32[36,32,128]{2,1,0:T(8,128)S(1)} %get-tuple-element.49.far_ref, bf16[1200,128]{1,0:T(8,128)(2,1)S(1)} %collective-permute-done.9.relayed_ref), custom_call_target="tpu_custom_call" | custom-call | bytes 1769472 | tf_op jit(solution)/shard_map/relay_chunk/pallas_call | solution.py:448
  31.4 0.0 collective-permute-done.8.refs_0_
  31.4 0.7 %collective-permute-done.5.refs_1_ = f32[36,128]{1,0:T(8,128)S(1)} collective-permute-done((f32[36,128]{1,0:T(8,128)S(1)}, f32[36,128]{1,0:T(8,128)S(1)}, u32[]{:S(2)}, u32[]{:S(2)}) %collective-permute-start.5) | collective-permute-done | bytes 18464 | tf_op jit(solution)/shard_map/ppermute | solution.py:360
  32.1 2.1 %collective-permute-done.6.refs_2_ = f32[36,128]{1,0:T(8,128)S(1)} collective-permute-done((f32[36,128]{1,0:T(8,128)S(1)}, f32[36,128]{1,0:T(8,128)S(1)}, u32[]{:S(2)}, u32[]{:S(2)}) %collective-permute-start.6) | collective-permute-done | bytes 18464 | tf_op jit(solution)/shard_map/ppermute | solution.py:360
  34.2 0.0 collective-permute-done.7.refs_3_
  34.2 0.8 %collective-permute-start.10 = (bf16[1200,128]{1,0:T(8,128)(2,1)S(1)}, bf16[1200,128]{1,0:T(8,128)(2,1)S(1)}, u32[]{:S(2)}, u32[]{:S(2)}) collective-permute-start(bf16[1200,128]{1,0:T(8,128)(2,1)S(1)} %get-tuple-element.59), channel_id=1, source_target_pairs={{0,4},{4,0},{8,12},{12,8},{1,5},{5,1},{9,13},{13,9},{2,6},{6,2},{1... | collective-permute-start | bytes 921608 | tf_op jit(solution)/shard_map/ppermute | solution.py:360
  35.1 1.3 %collective-permute-start.11 = (bf16[1200,128]{1,0:T(8,128)(2,1)S(1)}, bf16[1200,128]{1,0:T(8,128)(2,1)S(1)}, u32[]{:S(2)}, u32[]{:S(2)}) collective-permute-start(bf16[1200,128]{1,0:T(8,128)(2,1)S(1)} %relay_chunk.1), channel_id=1, source_target_pairs={{0,8},{4,12},{8,0},{12,4},{1,9},{5,13},{9,1},{13,5},{2,10},{6,14},... | collective-permute-start | bytes 921608 | tf_op jit(solution)/shard_map/ppermute | solution.py:360
  36.3 0.0 collective-permute-start.12
  36.3 1.5 %collective-permute-start.13 = (f32[2,128]{1,0:T(2,128)S(1)}, f32[2,128]{1,0:T(2,128)S(1)}, u32[]{:S(2)}, u32[]{:S(2)}) collective-permute-start(f32[2,128]{1,0:T(2,128)S(1)} %get-tuple-element.58.refs_2_), channel_id=1, source_target_pairs={{0,2},{1,3},{2,0},{3,1},{4,6},{5,7},{6,4},{7,5},{8,10},{9,11},{10,... | collective-permute-start | bytes 3080 | tf_op jit(solution)/shard_map/ppermute | solution.py:360
  37.9 0.3 collective-permute-start.14
  38.2 1.1 %collective-permute-done.12.refs_3_ = f32[2,128]{1,0:T(2,128)S(1)} collective-permute-done((f32[2,128]{1,0:T(2,128)S(1)}, f32[2,128]{1,0:T(2,128)S(1)}, u32[]{:S(2)}, u32[]{:S(2)}) %collective-permute-start.12) | collective-permute-done | bytes 1056 | tf_op jit(solution)/shard_map/ppermute | solution.py:360
  39.3 0.6 %collective-permute-done.13.refs_4_ = f32[2,128]{1,0:T(2,128)S(1)} collective-permute-done((f32[2,128]{1,0:T(2,128)S(1)}, f32[2,128]{1,0:T(2,128)S(1)}, u32[]{:S(2)}, u32[]{:S(2)}) %collective-permute-start.13) | collective-permute-done | bytes 1056 | tf_op jit(solution)/shard_map/ppermute | solution.py:360
  39.9 0.0 collective-permute-done.14.refs_5_
  39.9 1.5 %partial_weights.1.refs_1_ = f32[2,512]{1,0:T(2,128)S(1)} custom-call(f32[36,128]{1,0:T(8,128)S(1)} %get-tuple-element.55.eigen_ref, f32[9,512,256]{2,1,0:T(8,128)S(1)} %get-tuple-element.61.refs_0_, f32[9,512,256]{2,1,0:T(8,128)S(1)} %get-tuple-element.62.refs_1_, f32[2,128]{1,0:T(2,128)S(1)} %get-tuple-element.58.refs_2_, ...), custom_call_target="tpu_custom_call" | custom-call | bytes 9437184 | tf_op jit(solution)/shard_map/partial_weights/pallas_call | solution.py:466
  41.4 0.9 %collective-permute-start.15 = (f32[2,512]{1,0:T(2,128)S(1)}, f32[2,512]{1,0:T(2,128)S(1)}, u32[]{:S(2)}, u32[]{:S(2)}) collective-permute-start(f32[2,512]{1,0:T(2,128)S(1)} %partial_weights.1.refs_1_), channel_id=1, source_target_pairs={{0,3},{1,2},{2,1},{3,0},{4,7},{5,6},{6,5},{7,4},{8,11},{9,10},{10,... | collective-permute-start | bytes 12296 | tf_op jit(solution)/shard_map/ppermute | solution.py:360
  42.3 1.5 %collective-permute-start.16 = (f32[2,512]{1,0:T(2,128)S(1)}, f32[2,512]{1,0:T(2,128)S(1)}, u32[]{:S(2)}, u32[]{:S(2)}) collective-permute-start(f32[2,512]{1,0:T(2,128)S(1)} %partial_weights.1.refs_1_), channel_id=1, source_target_pairs={{0,2},{1,3},{2,0},{3,1},{4,6},{5,7},{6,4},{7,5},{8,10},{9,11},{10,... | collective-permute-start | bytes 12296 | tf_op jit(solution)/shard_map/ppermute | solution.py:360
  43.8 0.0 collective-permute-start.17
  43.8 0.6 %add_chunk.1 = (f32[36,32,128]{2,1,0:T(8,128)S(1)}, f32[8,128]{1,0:T(8,128)}, f32[28,128]{1,0:T(8,128)}) custom-call(s32[1]{0:T(128)} %bitcast.side_ref, f32[36,128]{1,0:T(8,128)S(1)} %get-tuple-element.55.eigen_ref, f32[36,32,128]{2,1,0:T(8,128)S(1)} %get-tuple-element.42.own_ref, bf16[1200,128]{1,0:T(8,128)(2,1)S(1)} %collective-permute-done.8.refs_0_), custom_call_target="tpu_custom_call" | custom-call | bytes 1769472 | tf_op jit(solution)/shard_map/add_chunk/pallas_call | solution.py:483
  44.4 0.1 collective-permute-done.15.refs_2_
  44.5 1.4 %collective-permute-done.16.refs_3_ = f32[2,512]{1,0:T(2,128)S(1)} collective-permute-done((f32[2,512]{1,0:T(2,128)S(1)}, f32[2,512]{1,0:T(2,128)S(1)}, u32[]{:S(2)}, u32[]{:S(2)}) %collective-permute-start.16) | collective-permute-done | bytes 4128 | tf_op jit(solution)/shard_map/ppermute | solution.py:360
  45.9 0.0 collective-permute-done.17.refs_4_
  45.9 0.0 collective-permute-done.10.sent_ref
  45.9 0.3 add_near.1.own_ref
  46.2 0.8 %collective-permute-done.11.refs_0_ = bf16[1200,128]{1,0:T(8,128)(2,1)S(1)} collective-permute-done((bf16[1200,128]{1,0:T(8,128)(2,1)S(1)}, bf16[1200,128]{1,0:T(8,128)(2,1)S(1)}, u32[]{:S(2)}, u32[]{:S(2)}) %collective-permute-start.11) | collective-permute-done | bytes 307232 | tf_op jit(solution)/shard_map/ppermute | solution.py:360
  47.0 1.0 %last_sums.1 = (f32[8,32,128]{2,1,0:T(8,128)}, f32[28,32,128]{2,1,0:T(8,128)}, f32[1,512]{1,0:T(1,128)}) custom-call(f32[36,32,128]{2,1,0:T(8,128)S(1)} %add_near.1.own_ref, bf16[1200,128]{1,0:T(8,128)(2,1)S(1)} %collective-permute-done.11.refs_0_, f32[2,512]{1,0:T(2,128)S(1)} %partial_weights.1.refs_1_, f32[2,512]{1,0:T(2,128)S(1)} %collective-permute-done.15.refs_2_, ...), custom_call_target="tpu_custom_call" | custom-call | bytes 2359296 | tf_op jit(solution)/shard_map/last_sums/pallas_call | solution.py:501
  (1 shorter events, 0.0 us)
Async XLA Ops:
  1.7 14.3 %collective-permute-start.1 = (bf16[18,32,128]{2,1,0:T(8,128)(2,1)S(1)}, bf16[18,32,128]{2,1,0:T(8,128)(2,1)S(1)}, u32[]{:S(2)}, u32[]{:S(2)}) collective-permute-start(bf16[18,32,128]{2,1,0:T(8,128)(2,1)S(1)} %get-tuple-element.41), channel_id=1, source_target_pairs={{0,12},{4,8},{8,4},{12,0},{1,13},{5,9},{9,5},{13,1},{2,14},{6,10},... | collective-permute-start | bytes 442376 | tf_op jit(solution)/shard_map/ppermute | solution.py:360
  6.8 13.5 %collective-permute-start.3 = (bf16[18,32,128]{2,1,0:T(8,128)(2,1)S(1)}, bf16[18,32,128]{2,1,0:T(8,128)(2,1)S(1)}, u32[]{:S(2)}, u32[]{:S(2)}) collective-permute-start(bf16[18,32,128]{2,1,0:T(8,128)(2,1)S(1)} %get-tuple-element.41), channel_id=1, source_target_pairs={{0,8},{4,12},{8,0},{12,4},{1,9},{5,13},{9,1},{13,5},{2,10},{6,14},... | collective-permute-start | bytes 442376 | tf_op jit(solution)/shard_map/ppermute | solution.py:360
  6.8 15.0 %collective-permute-start = (bf16[36,32,128]{2,1,0:T(8,128)(2,1)S(1)}, bf16[36,32,128]{2,1,0:T(8,128)(2,1)S(1)}, u32[]{:S(2)}, u32[]{:S(2)}) collective-permute-start(bf16[36,32,128]{2,1,0:T(8,128)(2,1)S(1)} %get-tuple-element.40.refs_0_), channel_id=1, source_target_pairs={{0,4},{4,0},{8,12},{12,8},{1,5},{5,1},{9,13},{13,9},{2,6},{6,2},{1... | collective-permute-start | bytes 884744 | tf_op jit(solution)/shard_map/ppermute | solution.py:360
  12.0 18.9 %collective-permute-start.9 = (bf16[1200,128]{1,0:T(8,128)(2,1)S(1)}, bf16[1200,128]{1,0:T(8,128)(2,1)S(1)}, u32[]{:S(2)}, u32[]{:S(2)}) collective-permute-start(bf16[1200,128]{1,0:T(8,128)(2,1)S(1)} %get-tuple-element.47), channel_id=1, source_target_pairs={{0,4},{12,8},{1,5},{13,9},{2,6},{14,10},{3,7},{15,11},{16,20},{28,... | collective-permute-start | bytes 921608 | tf_op jit(solution)/shard_map/ppermute | solution.py:431
  15.4 16.1 %collective-permute-start.8 = (bf16[1200,128]{1,0:T(8,128)(2,1)S(1)}, bf16[1200,128]{1,0:T(8,128)(2,1)S(1)}, u32[]{:S(2)}, u32[]{:S(2)}) collective-permute-start(bf16[1200,128]{1,0:T(8,128)(2,1)S(1)} %get-tuple-element.47), channel_id=1, source_target_pairs={{4,8},{8,4},{5,9},{9,5},{6,10},{10,6},{7,11},{11,7},{20,24},{24,20... | collective-permute-start | bytes 921608 | tf_op jit(solution)/shard_map/ppermute | solution.py:430
  16.1 6.8 %collective-permute-start.2 = (bf16[18,32,128]{2,1,0:T(8,128)(2,1)S(1)}, bf16[18,32,128]{2,1,0:T(8,128)(2,1)S(1)}, u32[]{:S(2)}, u32[]{:S(2)}) collective-permute-start(bf16[18,32,128]{2,1,0:T(8,128)(2,1)S(1)} %collective-permute-done.1.refs_2_), channel_id=1, source_target_pairs={{0,16},{16,0},{1,17},{17,1},{2,18},{18,2},{3,19},{19,3},{4,20},{20... | collective-permute-start | bytes 442376 | tf_op jit(solution)/shard_map/ppermute | solution.py:360
  20.3 5.1 %collective-permute-start.4 = (bf16[18,32,128]{2,1,0:T(8,128)(2,1)S(1)}, bf16[18,32,128]{2,1,0:T(8,128)(2,1)S(1)}, u32[]{:S(2)}, u32[]{:S(2)}) collective-permute-start(bf16[18,32,128]{2,1,0:T(8,128)(2,1)S(1)} %collective-permute-done.3.refs_3_), channel_id=1, source_target_pairs={{0,16},{16,0},{1,17},{17,1},{2,18},{18,2},{3,19},{19,3},{4,20},{20... | collective-permute-start | bytes 442376 | tf_op jit(solution)/shard_map/ppermute | solution.py:360
  26.5 5.7 %collective-permute-start.5 = (f32[36,128]{1,0:T(8,128)S(1)}, f32[36,128]{1,0:T(8,128)S(1)}, u32[]{:S(2)}, u32[]{:S(2)}) collective-permute-start(f32[36,128]{1,0:T(8,128)S(1)} %get-tuple-element.51.refs_0_), channel_id=1, source_target_pairs={{0,12},{4,8},{8,4},{12,0},{1,13},{5,9},{9,5},{13,1},{2,14},{6,10},... | collective-permute-start | bytes 55304 | tf_op jit(solution)/shard_map/ppermute | solution.py:360
  29.2 5.0 %collective-permute-start.6 = (f32[36,128]{1,0:T(8,128)S(1)}, f32[36,128]{1,0:T(8,128)S(1)}, u32[]{:S(2)}, u32[]{:S(2)}) collective-permute-start(f32[36,128]{1,0:T(8,128)S(1)} %get-tuple-element.51.refs_0_), channel_id=1, source_target_pairs={{0,8},{4,12},{8,0},{12,4},{1,9},{5,13},{9,1},{13,5},{2,10},{6,14},... | collective-permute-start | bytes 55304 | tf_op jit(solution)/shard_map/ppermute | solution.py:360
  29.2 5.0 %collective-permute-start.7 = (f32[36,128]{1,0:T(8,128)S(1)}, f32[36,128]{1,0:T(8,128)S(1)}, u32[]{:S(2)}, u32[]{:S(2)}) collective-permute-start(f32[36,128]{1,0:T(8,128)S(1)} %get-tuple-element.51.refs_0_), channel_id=1, source_target_pairs={{0,4},{4,0},{8,12},{12,8},{1,5},{5,1},{9,13},{13,9},{2,6},{6,2},{1... | collective-permute-start | bytes 55304 | tf_op jit(solution)/shard_map/ppermute | solution.py:360
  34.2 11.7 %collective-permute-start.10 = (bf16[1200,128]{1,0:T(8,128)(2,1)S(1)}, bf16[1200,128]{1,0:T(8,128)(2,1)S(1)}, u32[]{:S(2)}, u32[]{:S(2)}) collective-permute-start(bf16[1200,128]{1,0:T(8,128)(2,1)S(1)} %get-tuple-element.59), channel_id=1, source_target_pairs={{0,4},{4,0},{8,12},{12,8},{1,5},{5,1},{9,13},{13,9},{2,6},{6,2},{1... | collective-permute-start | bytes 921608 | tf_op jit(solution)/shard_map/ppermute | solution.py:360
  35.1 11.9 %collective-permute-start.11 = (bf16[1200,128]{1,0:T(8,128)(2,1)S(1)}, bf16[1200,128]{1,0:T(8,128)(2,1)S(1)}, u32[]{:S(2)}, u32[]{:S(2)}) collective-permute-start(bf16[1200,128]{1,0:T(8,128)(2,1)S(1)} %relay_chunk.1), channel_id=1, source_target_pairs={{0,8},{4,12},{8,0},{12,4},{1,9},{5,13},{9,1},{13,5},{2,10},{6,14},... | collective-permute-start | bytes 921608 | tf_op jit(solution)/shard_map/ppermute | solution.py:360
  36.3 3.0 %collective-permute-start.12 = (f32[2,128]{1,0:T(2,128)S(1)}, f32[2,128]{1,0:T(2,128)S(1)}, u32[]{:S(2)}, u32[]{:S(2)}) collective-permute-start(f32[2,128]{1,0:T(2,128)S(1)} %get-tuple-element.58.refs_2_), channel_id=1, source_target_pairs={{0,3},{1,2},{2,1},{3,0},{4,7},{5,6},{6,5},{7,4},{8,11},{9,10},{10,... | collective-permute-start | bytes 3080 | tf_op jit(solution)/shard_map/ppermute | solution.py:360
  36.3 3.6 %collective-permute-start.13 = (f32[2,128]{1,0:T(2,128)S(1)}, f32[2,128]{1,0:T(2,128)S(1)}, u32[]{:S(2)}, u32[]{:S(2)}) collective-permute-start(f32[2,128]{1,0:T(2,128)S(1)} %get-tuple-element.58.refs_2_), channel_id=1, source_target_pairs={{0,2},{1,3},{2,0},{3,1},{4,6},{5,7},{6,4},{7,5},{8,10},{9,11},{10,... | collective-permute-start | bytes 3080 | tf_op jit(solution)/shard_map/ppermute | solution.py:360
  37.9 2.1 %collective-permute-start.14 = (f32[2,128]{1,0:T(2,128)S(1)}, f32[2,128]{1,0:T(2,128)S(1)}, u32[]{:S(2)}, u32[]{:S(2)}) collective-permute-start(f32[2,128]{1,0:T(2,128)S(1)} %get-tuple-element.58.refs_2_), channel_id=1, source_target_pairs={{0,1},{1,0},{2,3},{3,2},{4,5},{5,4},{6,7},{7,6},{8,9},{9,8},{10,11... | collective-permute-start | bytes 3080 | tf_op jit(solution)/shard_map/ppermute | solution.py:360
  41.4 3.1 %collective-permute-start.15 = (f32[2,512]{1,0:T(2,128)S(1)}, f32[2,512]{1,0:T(2,128)S(1)}, u32[]{:S(2)}, u32[]{:S(2)}) collective-permute-start(f32[2,512]{1,0:T(2,128)S(1)} %partial_weights.1.refs_1_), channel_id=1, source_target_pairs={{0,3},{1,2},{2,1},{3,0},{4,7},{5,6},{6,5},{7,4},{8,11},{9,10},{10,... | collective-permute-start | bytes 12296 | tf_op jit(solution)/shard_map/ppermute | solution.py:360
  42.3 3.6 %collective-permute-start.16 = (f32[2,512]{1,0:T(2,128)S(1)}, f32[2,512]{1,0:T(2,128)S(1)}, u32[]{:S(2)}, u32[]{:S(2)}) collective-permute-start(f32[2,512]{1,0:T(2,128)S(1)} %partial_weights.1.refs_1_), channel_id=1, source_target_pairs={{0,2},{1,3},{2,0},{3,1},{4,6},{5,7},{6,4},{7,5},{8,10},{9,11},{10,... | collective-permute-start | bytes 12296 | tf_op jit(solution)/shard_map/ppermute | solution.py:360
  43.8 2.1 %collective-permute-start.17 = (f32[2,512]{1,0:T(2,128)S(1)}, f32[2,512]{1,0:T(2,128)S(1)}, u32[]{:S(2)}, u32[]{:S(2)}) collective-permute-start(f32[2,512]{1,0:T(2,128)S(1)} %partial_weights.1.refs_1_), channel_id=1, source_target_pairs={{0,1},{1,0},{2,3},{3,2},{4,5},{5,4},{6,7},{7,6},{8,9},{9,8},{10,11... | collective-permute-start | bytes 12296 | tf_op jit(solution)/shard_map/ppermute | solution.py:360

commit v21 on v20

--- a/solution.py
+++ b/solution.py
@@ -178,12 +178,17 @@
             sum_ref[block] = total
 
 
-def near_kernel(messages, own_ref, sent_ref, sum_ref, tops):
+def near_kernel(messages, own_ref, sent_ref, *refs):
+    *weight_refs, sum_ref, score_ref, tops, scores, sem = refs
     blocks, rows, _ = own_ref.shape
+    score_kernel(*weight_refs, scores)
+    copy = pltpu.make_async_copy(scores, score_ref, sem)
+    copy.start()
     load_tops(messages, rows, (sent_ref,), (tops,))
     for step in range(blocks // GROUP):
         for block, total in add_group(messages, rows, own_ref, (sent_ref,), (tops,), step):
             sum_ref[block] = total
+    copy.wait()
 
 
 def relay_kernel(message, far_ref, relayed_ref, sent_ref, relayed_tops, tops):
@@ -204,11 +209,14 @@
 def last_add_kernel(messages, owners, own_ref, *refs):
     sent_refs, refs = refs[: len(messages)], refs[len(messages) :]
     weight_refs, refs = refs[:owners], refs[owners:]
-    act_ref, grad_ref, score_ref, *tops_refs, sums, scores, sems = refs
+    act_ref, grad_ref, *score_ref = refs[: 3 if owners else 2]
+    *tops_refs, sums, scores, sems = refs[3 if owners else 2 :]
     blocks, rows, _ = own_ref.shape
-    score_kernel(*weight_refs, scores)
-    copies = [pltpu.make_async_copy(scores, score_ref, sems.at[blocks // GROUP])]
-    copies[0].start()
+    copies = []
+    if weight_refs:
+        score_kernel(*weight_refs, scores)
+        copies = [pltpu.make_async_copy(scores, score_ref[0], sems.at[blocks // GROUP])]
+        copies[0].start()
     load_tops(messages, rows, sent_refs, tops_refs)
     for step in range(blocks // GROUP):
         for block, total in add_group(messages, rows, own_ref, sent_refs, tops_refs, step):
@@ -492,15 +500,20 @@
             8 * blocks * BLK, [IN_SMEM, IN_VMEM],
         )(side, eigen)
     if pieces == 4:
-        own = call(
-            functools.partial(near_kernel, [(None, 0, blocks)]), f32(*own.shape), "add_near", 0,
-            12 * own.size, [IN_VMEM] * 2, tops_of(1),
-        )(own, arrived.pop(1))
+        own, token_scores = call(
+            functools.partial(near_kernel, [(None, 0, blocks)]),
+            [f32(*own.shape), f32(1, tokens)], "add_near", 0, 12 * own.size,
+            [IN_VMEM] * (2 + len(weights)),
+            [*tops_of(1), pltpu.VMEM((1, tokens), jnp.float32), pltpu.SemaphoreType.DMA],
+            out_spec=[IN_VMEM, pl.BlockSpec(memory_space=pl.ANY)],
+        )(own, arrived.pop(1), *weights)
+        weights = []
     chunks = list(arrived.values())
     if chunks:
-        *covariance, token_scores = call(
+        outputs = call(
             functools.partial(last_add_kernel, [(None, 0, blocks)] * len(chunks), len(weights)),
-            [f32(act_blocks, rows, BLK), f32(grad_blocks, rows, BLK), f32(1, tokens)],
+            [f32(act_blocks, rows, BLK), f32(grad_blocks, rows, BLK)]
+            + [f32(1, tokens)] * bool(weights),
             "last_sums", 0, 16 * own.size, [IN_VMEM] * (1 + len(chunks) + len(weights)),
             [
                 *tops_of(len(chunks)),
@@ -508,8 +521,11 @@
                 pltpu.VMEM((1, tokens), jnp.float32),
                 pltpu.SemaphoreType.DMA((blocks // GROUP + 1,)),
             ],
-            out_spec=[pl.BlockSpec(memory_space=pl.ANY)] * 3,
+            out_spec=[pl.BlockSpec(memory_space=pl.ANY)] * (3 if weights else 2),
         )(own, *chunks, *weights)
+        covariance = outputs[:2]
+        if weights:
+            token_scores = outputs[2]
     else:
         covariance = own[:act_blocks], own[act_blocks:]
         token_scores = call(

time: 48.1 us -> 48.1 us (level)
  no operation moved by 1% of the time
where the time goes in v21:
time: 48.1 us; the launch traced here: 48 us
  starting transfers between devices  23.7 us (49%)
  Pallas kernels  11.8 us (25%)
  waiting for transfers between devices  11.8 us (25%)
  between operations  0.74 us (2%)
    ppermute x16, starting transfers between devices, swap(): return lax.ppermute(value, axis, [(i, i ^ mask) for i in range(count)])  19.7 us
    ppermute x16, waiting for transfers between devices, swap(): return lax.ppermute(value, axis, [(i, i ^ mask) for i in range(count)])  11.8 us
    pallas_call x1, Pallas kernels, local(): call(functools.partial(gram_kernel, pieces, coded, scale), [bf16(*activat...  4.56 us
    ppermute x1, starting transfers between devices, local(): relayed = lax.ppermute(sent[3], 'dp', [(0, 1), (3, 2)])  3.32 us
    pallas_call x2, Pallas kernels, local(): call(functools.partial(eigen_kernel, part, halves, masks, pieces, scale),...  1.95 us
    pallas_call x1, Pallas kernels, local(): call(functools.partial(weight_kernel, halves, act_blocks // halves), f32(...  1.49 us
    pallas_call x1, Pallas kernels, local(): call(pack_kernel, [bf16(blocks // part, rows, BLK) for part in range(1, h...  1.08 us
    pallas_call x1, Pallas kernels, local(): call(functools.partial(last_add_kernel, [(None, 0, blocks)] * len(chunks)...  0.98 us
  transfers between devices with their start and end apart: 18, of which 9 were waited for; matrix products, arithmetic and copies ran while one was open for 0% of the time, Pallas kernels for 20%

profile of v21, /device:TPU:0, one launch (start us, length us, event | category | flops | bytes accessed | tf_op | source)
XLA Modules:
  0.0 48.0 jit_solution(17979577979490357849)
XLA Ops:
  0.6 1.1 %pack_basis.1 = (bf16[36,32,128]{2,1,0:T(8,128)(2,1)S(1)}, bf16[18,32,128]{2,1,0:T(8,128)(2,1)S(1)}) custom-call(s32[1]{0:T(128)} %bitcast.side_ref, bf16[8,32,128]{2,1,0:T(8,128)(2,1)} %act_ref.1, bf16[28,32,128]{2,1,0:T(8,128)(2,1)} %grad_ref.1), custom_call_target="tpu_custom_call" | custom-call | bytes 294912 | tf_op jit(solution)/shard_map/pack_basis/pallas_call | solution.py:396
  1.7 5.1 %collective-permute-start.1 = (bf16[18,32,128]{2,1,0:T(8,128)(2,1)S(1)}, bf16[18,32,128]{2,1,0:T(8,128)(2,1)S(1)}, u32[]{:S(2)}, u32[]{:S(2)}) collective-permute-start(bf16[18,32,128]{2,1,0:T(8,128)(2,1)S(1)} %get-tuple-element.42), channel_id=1, source_target_pairs={{0,12},{4,8},{8,4},{12,0},{1,13},{5,9},{9,5},{13,1},{2,14},{6,10},... | collective-permute-start | bytes 442376 | tf_op jit(solution)/shard_map/ppermute | solution.py:368
  6.8 0.0 collective-permute-start.3
  6.8 0.6 %collective-permute-start = (bf16[36,32,128]{2,1,0:T(8,128)(2,1)S(1)}, bf16[36,32,128]{2,1,0:T(8,128)(2,1)S(1)}, u32[]{:S(2)}, u32[]{:S(2)}) collective-permute-start(bf16[36,32,128]{2,1,0:T(8,128)(2,1)S(1)} %get-tuple-element.41.refs_0_), channel_id=1, source_target_pairs={{0,4},{4,0},{8,12},{12,8},{1,5},{5,1},{9,13},{13,9},{2,6},{6,2},{1... | collective-permute-start | bytes 884744 | tf_op jit(solution)/shard_map/ppermute | solution.py:368
  7.5 4.6 %partial_gram.1 = (bf16[512,1024]{1,0:T(8,128)(2,1)S(1)}, bf16[512,3584]{1,0:T(8,128)(2,1)S(1)}, f32[36,32,128]{2,1,0:T(8,128)S(1)}, f32[36,32,128]{2,1,0:T(8,12...) custom-call(s32[1]{0:T(128)} %bitcast.1.me_ref, bf16[512,1024]{1,0:T(8,128)(2,1)} %act_hbm.1, ...), custom_call_target="tpu_custom_call" | custom-call | flops 1207959552 | bytes 4718592 | tf_op jit(solution)/shard_map/partial_gram/pallas_call | solution.py:417
  12.0 3.3 %collective-permute-start.9 = (bf16[1200,128]{1,0:T(8,128)(2,1)S(1)}, bf16[1200,128]{1,0:T(8,128)(2,1)S(1)}, u32[]{:S(2)}, u32[]{:S(2)}) collective-permute-start(bf16[1200,128]{1,0:T(8,128)(2,1)S(1)} %get-tuple-element.48), channel_id=1, source_target_pairs={{0,4},{12,8},{1,5},{13,9},{2,6},{14,10},{3,7},{15,11},{16,20},{28,... | collective-permute-start | bytes 921608 | tf_op jit(solution)/shard_map/ppermute | solution.py:439
  15.4 0.7 %collective-permute-start.8 = (bf16[1200,128]{1,0:T(8,128)(2,1)S(1)}, bf16[1200,128]{1,0:T(8,128)(2,1)S(1)}, u32[]{:S(2)}, u32[]{:S(2)}) collective-permute-start(bf16[1200,128]{1,0:T(8,128)(2,1)S(1)} %get-tuple-element.48), channel_id=1, source_target_pairs={{4,8},{8,4},{5,9},{9,5},{6,10},{10,6},{7,11},{11,7},{20,24},{24,20... | collective-permute-start | bytes 921608 | tf_op jit(solution)/shard_map/ppermute | solution.py:438
  16.1 0.0 collective-permute-done.1.refs_2_
  16.1 1.6 %collective-permute-start.2 = (bf16[18,32,128]{2,1,0:T(8,128)(2,1)S(1)}, bf16[18,32,128]{2,1,0:T(8,128)(2,1)S(1)}, u32[]{:S(2)}, u32[]{:S(2)}) collective-permute-start(bf16[18,32,128]{2,1,0:T(8,128)(2,1)S(1)} %collective-permute-done.1.refs_2_), channel_id=1, source_target_pairs={{0,16},{16,0},{1,17},{17,1},{2,18},{18,2},{3,19},{19,3},{4,20},{20... | collective-permute-start | bytes 442376 | tf_op jit(solution)/shard_map/ppermute | solution.py:368
  17.6 2.7 %collective-permute-done.3.refs_3_ = bf16[18,32,128]{2,1,0:T(8,128)(2,1)S(1)} collective-permute-done((bf16[18,32,128]{2,1,0:T(8,128)(2,1)S(1)}, bf16[18,32,128]{2,1,0:T(8,128)(2,1)S(1)}, u32[]{:S(2)}, u32[]{:S(2)}) %collective-permute-start.3) | collective-permute-done | bytes 147488 | tf_op jit(solution)/shard_map/ppermute | solution.py:368
  20.3 1.5 %collective-permute-start.4 = (bf16[18,32,128]{2,1,0:T(8,128)(2,1)S(1)}, bf16[18,32,128]{2,1,0:T(8,128)(2,1)S(1)}, u32[]{:S(2)}, u32[]{:S(2)}) collective-permute-start(bf16[18,32,128]{2,1,0:T(8,128)(2,1)S(1)} %collective-permute-done.3.refs_3_), channel_id=1, source_target_pairs={{0,16},{16,0},{1,17},{17,1},{2,18},{18,2},{3,19},{19,3},{4,20},{20... | collective-permute-start | bytes 442376 | tf_op jit(solution)/shard_map/ppermute | solution.py:368
  21.8 0.0 collective-permute-done.refs_1_
  21.8 1.0 %partial_eigen.2 = (f32[9,512,256]{2,1,0:T(8,128)S(1)}, f32[18,128]{1,0:T(8,128)S(1)}) custom-call(s32[1]{0:T(128)} %bitcast.1.me_ref, s32[1]{0:T(128)} %bitcast.side_ref, bf16[512,1024]{1,0:T(8,128)(2,1)S(1)} %get-tuple-element.39.act_ref, bf16[512,3584]{1,0:T(8,128)(2,1)S(1)} %get-tuple-element.40.grad_ref, ...), custom_call_target="tpu_custom_call" | custom-call | flops 301989888 | bytes 2359296 | tf_op jit(solution)/shard_map/partial_eigen/pallas_call | solution.py:447
  22.8 0.0 collective-permute-done.2.refs_2_
  22.8 2.6 %collective-permute-done.4.refs_3_ = bf16[18,32,128]{2,1,0:T(8,128)(2,1)S(1)} collective-permute-done((bf16[18,32,128]{2,1,0:T(8,128)(2,1)S(1)}, bf16[18,32,128]{2,1,0:T(8,128)(2,1)S(1)}, u32[]{:S(2)}, u32[]{:S(2)}) %collective-permute-start.4) | collective-permute-done | bytes 147488 | tf_op jit(solution)/shard_map/ppermute | solution.py:368
  25.5 1.0 %partial_eigen.3 = (f32[9,512,256]{2,1,0:T(8,128)S(1)}, f32[36,128]{1,0:T(8,128)S(1)}) custom-call(s32[1]{0:T(128)} %bitcast.1.me_ref, s32[1]{0:T(128)} %bitcast.side_ref, bf16[512,1024]{1,0:T(8,128)(2,1)S(1)} %get-tuple-element.39.act_ref, bf16[512,3584]{1,0:T(8,128)(2,1)S(1)} %get-tuple-element.40.grad_ref, ...), custom_call_target="tpu_custom_call" | custom-call | flops 301989888 | bytes 2359296 | tf_op jit(solution)/shard_map/partial_eigen/pallas_call | solution.py:447
  26.5 2.7 %collective-permute-start.5 = (f32[36,128]{1,0:T(8,128)S(1)}, f32[36,128]{1,0:T(8,128)S(1)}, u32[]{:S(2)}, u32[]{:S(2)}) collective-permute-start(f32[36,128]{1,0:T(8,128)S(1)} %get-tuple-element.52.refs_0_), channel_id=1, source_target_pairs={{0,12},{4,8},{8,4},{12,0},{1,13},{5,9},{9,5},{13,1},{2,14},{6,10},... | collective-permute-start | bytes 55304 | tf_op jit(solution)/shard_map/ppermute | solution.py:368
  29.2 0.0 collective-permute-start.6
  29.2 1.7 %collective-permute-start.7 = (f32[36,128]{1,0:T(8,128)S(1)}, f32[36,128]{1,0:T(8,128)S(1)}, u32[]{:S(2)}, u32[]{:S(2)}) collective-permute-start(f32[36,128]{1,0:T(8,128)S(1)} %get-tuple-element.52.refs_0_), channel_id=1, source_target_pairs={{0,4},{4,0},{8,12},{12,8},{1,5},{5,1},{9,13},{13,9},{2,6},{6,2},{1... | collective-permute-start | bytes 55304 | tf_op jit(solution)/shard_map/ppermute | solution.py:368
  30.9 0.0 collective-permute-done.9.relayed_ref
  30.9 0.5 %relay_chunk.1 = bf16[1200,128]{1,0:T(8,128)(2,1)S(1)} custom-call(f32[36,32,128]{2,1,0:T(8,128)S(1)} %get-tuple-element.50.far_ref, bf16[1200,128]{1,0:T(8,128)(2,1)S(1)} %collective-permute-done.9.relayed_ref), custom_call_target="tpu_custom_call" | custom-call | bytes 1769472 | tf_op jit(solution)/shard_map/relay_chunk/pallas_call | solution.py:456
  31.4 0.0 collective-permute-done.8.refs_0_
  31.4 0.7 %collective-permute-done.5.refs_1_ = f32[36,128]{1,0:T(8,128)S(1)} collective-permute-done((f32[36,128]{1,0:T(8,128)S(1)}, f32[36,128]{1,0:T(8,128)S(1)}, u32[]{:S(2)}, u32[]{:S(2)}) %collective-permute-start.5) | collective-permute-done | bytes 18464 | tf_op jit(solution)/shard_map/ppermute | solution.py:368
  32.1 2.1 %collective-permute-done.6.refs_2_ = f32[36,128]{1,0:T(8,128)S(1)} collective-permute-done((f32[36,128]{1,0:T(8,128)S(1)}, f32[36,128]{1,0:T(8,128)S(1)}, u32[]{:S(2)}, u32[]{:S(2)}) %collective-permute-start.6) | collective-permute-done | bytes 18464 | tf_op jit(solution)/shard_map/ppermute | solution.py:368
  34.2 0.0 collective-permute-done.7.refs_3_
  34.2 0.8 %collective-permute-start.10 = (bf16[1200,128]{1,0:T(8,128)(2,1)S(1)}, bf16[1200,128]{1,0:T(8,128)(2,1)S(1)}, u32[]{:S(2)}, u32[]{:S(2)}) collective-permute-start(bf16[1200,128]{1,0:T(8,128)(2,1)S(1)} %get-tuple-element.60), channel_id=1, source_target_pairs={{0,4},{4,0},{8,12},{12,8},{1,5},{5,1},{9,13},{13,9},{2,6},{6,2},{1... | collective-permute-start | bytes 921608 | tf_op jit(solution)/shard_map/ppermute | solution.py:368
  35.1 1.3 %collective-permute-start.17 = (bf16[1200,128]{1,0:T(8,128)(2,1)S(1)}, bf16[1200,128]{1,0:T(8,128)(2,1)S(1)}, u32[]{:S(2)}, u32[]{:S(2)}) collective-permute-start(bf16[1200,128]{1,0:T(8,128)(2,1)S(1)} %relay_chunk.1), channel_id=1, source_target_pairs={{0,8},{4,12},{8,0},{12,4},{1,9},{5,13},{9,1},{13,5},{2,10},{6,14},... | collective-permute-start | bytes 921608 | tf_op jit(solution)/shard_map/ppermute | solution.py:368
  36.3 0.0 collective-permute-start.11
  36.3 1.5 %collective-permute-start.12 = (f32[2,128]{1,0:T(2,128)S(1)}, f32[2,128]{1,0:T(2,128)S(1)}, u32[]{:S(2)}, u32[]{:S(2)}) collective-permute-start(f32[2,128]{1,0:T(2,128)S(1)} %get-tuple-element.59.refs_2_), channel_id=1, source_target_pairs={{0,2},{1,3},{2,0},{3,1},{4,6},{5,7},{6,4},{7,5},{8,10},{9,11},{10,... | collective-permute-start | bytes 3080 | tf_op jit(solution)/shard_map/ppermute | solution.py:368
  37.9 0.3 collective-permute-start.13
  38.2 1.1 %collective-permute-done.11.refs_3_ = f32[2,128]{1,0:T(2,128)S(1)} collective-permute-done((f32[2,128]{1,0:T(2,128)S(1)}, f32[2,128]{1,0:T(2,128)S(1)}, u32[]{:S(2)}, u32[]{:S(2)}) %collective-permute-start.11) | collective-permute-done | bytes 1056 | tf_op jit(solution)/shard_map/ppermute | solution.py:368
  39.3 0.6 %collective-permute-done.12.refs_4_ = f32[2,128]{1,0:T(2,128)S(1)} collective-permute-done((f32[2,128]{1,0:T(2,128)S(1)}, f32[2,128]{1,0:T(2,128)S(1)}, u32[]{:S(2)}, u32[]{:S(2)}) %collective-permute-start.12) | collective-permute-done | bytes 1056 | tf_op jit(solution)/shard_map/ppermute | solution.py:368
  39.9 0.0 collective-permute-done.13.refs_5_
  39.9 1.5 %partial_weights.1.refs_0_ = f32[2,512]{1,0:T(2,128)S(1)} custom-call(f32[36,128]{1,0:T(8,128)S(1)} %get-tuple-element.56.eigen_ref, f32[9,512,256]{2,1,0:T(8,128)S(1)} %get-tuple-element.61.refs_0_, f32[9,512,256]{2,1,0:T(8,128)S(1)} %get-tuple-element.62.refs_1_, f32[2,128]{1,0:T(2,128)S(1)} %get-tuple-element.59.refs_2_, ...), custom_call_target="tpu_custom_call" | custom-call | bytes 9437184 | tf_op jit(solution)/shard_map/partial_weights/pallas_call | solution.py:474
  41.4 0.9 %collective-permute-start.14 = (f32[2,512]{1,0:T(2,128)S(1)}, f32[2,512]{1,0:T(2,128)S(1)}, u32[]{:S(2)}, u32[]{:S(2)}) collective-permute-start(f32[2,512]{1,0:T(2,128)S(1)} %partial_weights.1.refs_0_), channel_id=1, source_target_pairs={{0,3},{1,2},{2,1},{3,0},{4,7},{5,6},{6,5},{7,4},{8,11},{9,10},{10,... | collective-permute-start | bytes 12296 | tf_op jit(solution)/shard_map/ppermute | solution.py:368
  42.3 1.5 %collective-permute-start.15 = (f32[2,512]{1,0:T(2,128)S(1)}, f32[2,512]{1,0:T(2,128)S(1)}, u32[]{:S(2)}, u32[]{:S(2)}) collective-permute-start(f32[2,512]{1,0:T(2,128)S(1)} %partial_weights.1.refs_0_), channel_id=1, source_target_pairs={{0,2},{1,3},{2,0},{3,1},{4,6},{5,7},{6,4},{7,5},{8,10},{9,11},{10,... | collective-permute-start | bytes 12296 | tf_op jit(solution)/shard_map/ppermute | solution.py:368
  43.8 0.0 collective-permute-start.16
  43.8 0.6 %add_chunk.1 = (f32[36,32,128]{2,1,0:T(8,128)S(1)}, f32[8,128]{1,0:T(8,128)}, f32[28,128]{1,0:T(8,128)}) custom-call(s32[1]{0:T(128)} %bitcast.side_ref, f32[36,128]{1,0:T(8,128)S(1)} %get-tuple-element.56.eigen_ref, f32[36,32,128]{2,1,0:T(8,128)S(1)} %get-tuple-element.43.own_ref, bf16[1200,128]{1,0:T(8,128)(2,1)S(1)} %collective-permute-done.8.refs_0_), custom_call_target="tpu_custom_call" | custom-call | bytes 1769472 | tf_op jit(solution)/shard_map/add_chunk/pallas_call | solution.py:491
  44.4 0.1 collective-permute-done.14.refs_1_
  44.5 1.4 %collective-permute-done.15.refs_2_ = f32[2,512]{1,0:T(2,128)S(1)} collective-permute-done((f32[2,512]{1,0:T(2,128)S(1)}, f32[2,512]{1,0:T(2,128)S(1)}, u32[]{:S(2)}, u32[]{:S(2)}) %collective-permute-start.15) | collective-permute-done | bytes 4128 | tf_op jit(solution)/shard_map/ppermute | solution.py:368
  45.9 0.0 collective-permute-done.16.refs_3_
  45.9 0.0 collective-permute-done.10.sent_ref
  45.9 0.6 %add_near.1 = (f32[36,32,128]{2,1,0:T(8,128)S(1)}, f32[1,512]{1,0:T(1,128)}) custom-call(f32[36,32,128]{2,1,0:T(8,128)S(1)} %get-tuple-element.57.own_ref, bf16[1200,128]{1,0:T(8,128)(2,1)S(1)} %collective-permute-done.10.sent_ref, f32[2,512]{1,0:T(2,128)S(1)} %partial_weights.1.refs_0_, f32[2,512]{1,0:T(2,128)S(1)} %collective-permute-done.14.refs_1_, ...), custom_call_target="tpu_custom_call" | custom-call | bytes 1769472 | tf_op jit(solution)/shard_map/add_near/pallas_call | solution.py:503
  46.5 0.4 collective-permute-done.17.refs_0_
  47.0 1.0 %last_sums.1 = (f32[8,32,128]{2,1,0:T(8,128)}, f32[28,32,128]{2,1,0:T(8,128)}) custom-call(f32[36,32,128]{2,1,0:T(8,128)S(1)} %get-tuple-element.66.own_ref, bf16[1200,128]{1,0:T(8,128)(2,1)S(1)} %collective-permute-done.17.refs_0_), custom_call_target="tpu_custom_call" | custom-call | bytes 2359296 | tf_op jit(solution)/shard_map/last_sums/pallas_call | solution.py:513
  (1 shorter events, 0.0 us)
Async XLA Ops:
  1.7 14.3 %collective-permute-start.1 = (bf16[18,32,128]{2,1,0:T(8,128)(2,1)S(1)}, bf16[18,32,128]{2,1,0:T(8,128)(2,1)S(1)}, u32[]{:S(2)}, u32[]{:S(2)}) collective-permute-start(bf16[18,32,128]{2,1,0:T(8,128)(2,1)S(1)} %get-tuple-element.42), channel_id=1, source_target_pairs={{0,12},{4,8},{8,4},{12,0},{1,13},{5,9},{9,5},{13,1},{2,14},{6,10},... | collective-permute-start | bytes 442376 | tf_op jit(solution)/shard_map/ppermute | solution.py:368
  6.8 13.5 %collective-permute-start.3 = (bf16[18,32,128]{2,1,0:T(8,128)(2,1)S(1)}, bf16[18,32,128]{2,1,0:T(8,128)(2,1)S(1)}, u32[]{:S(2)}, u32[]{:S(2)}) collective-permute-start(bf16[18,32,128]{2,1,0:T(8,128)(2,1)S(1)} %get-tuple-element.42), channel_id=1, source_target_pairs={{0,8},{4,12},{8,0},{12,4},{1,9},{5,13},{9,1},{13,5},{2,10},{6,14},... | collective-permute-start | bytes 442376 | tf_op jit(solution)/shard_map/ppermute | solution.py:368
  6.8 15.0 %collective-permute-start = (bf16[36,32,128]{2,1,0:T(8,128)(2,1)S(1)}, bf16[36,32,128]{2,1,0:T(8,128)(2,1)S(1)}, u32[]{:S(2)}, u32[]{:S(2)}) collective-permute-start(bf16[36,32,128]{2,1,0:T(8,128)(2,1)S(1)} %get-tuple-element.41.refs_0_), channel_id=1, source_target_pairs={{0,4},{4,0},{8,12},{12,8},{1,5},{5,1},{9,13},{13,9},{2,6},{6,2},{1... | collective-permute-start | bytes 884744 | tf_op jit(solution)/shard_map/ppermute | solution.py:368
  12.0 18.9 %collective-permute-start.9 = (bf16[1200,128]{1,0:T(8,128)(2,1)S(1)}, bf16[1200,128]{1,0:T(8,128)(2,1)S(1)}, u32[]{:S(2)}, u32[]{:S(2)}) collective-permute-start(bf16[1200,128]{1,0:T(8,128)(2,1)S(1)} %get-tuple-element.48), channel_id=1, source_target_pairs={{0,4},{12,8},{1,5},{13,9},{2,6},{14,10},{3,7},{15,11},{16,20},{28,... | collective-permute-start | bytes 921608 | tf_op jit(solution)/shard_map/ppermute | solution.py:439
  15.4 16.1 %collective-permute-start.8 = (bf16[1200,128]{1,0:T(8,128)(2,1)S(1)}, bf16[1200,128]{1,0:T(8,128)(2,1)S(1)}, u32[]{:S(2)}, u32[]{:S(2)}) collective-permute-start(bf16[1200,128]{1,0:T(8,128)(2,1)S(1)} %get-tuple-element.48), channel_id=1, source_target_pairs={{4,8},{8,4},{5,9},{9,5},{6,10},{10,6},{7,11},{11,7},{20,24},{24,20... | collective-permute-start | bytes 921608 | tf_op jit(solution)/shard_map/ppermute | solution.py:438
  16.1 6.8 %collective-permute-start.2 = (bf16[18,32,128]{2,1,0:T(8,128)(2,1)S(1)}, bf16[18,32,128]{2,1,0:T(8,128)(2,1)S(1)}, u32[]{:S(2)}, u32[]{:S(2)}) collective-permute-start(bf16[18,32,128]{2,1,0:T(8,128)(2,1)S(1)} %collective-permute-done.1.refs_2_), channel_id=1, source_target_pairs={{0,16},{16,0},{1,17},{17,1},{2,18},{18,2},{3,19},{19,3},{4,20},{20... | collective-permute-start | bytes 442376 | tf_op jit(solution)/shard_map/ppermute | solution.py:368
  20.3 5.1 %collective-permute-start.4 = (bf16[18,32,128]{2,1,0:T(8,128)(2,1)S(1)}, bf16[18,32,128]{2,1,0:T(8,128)(2,1)S(1)}, u32[]{:S(2)}, u32[]{:S(2)}) collective-permute-start(bf16[18,32,128]{2,1,0:T(8,128)(2,1)S(1)} %collective-permute-done.3.refs_3_), channel_id=1, source_target_pairs={{0,16},{16,0},{1,17},{17,1},{2,18},{18,2},{3,19},{19,3},{4,20},{20... | collective-permute-start | bytes 442376 | tf_op jit(solution)/shard_map/ppermute | solution.py:368
  26.5 5.7 %collective-permute-start.5 = (f32[36,128]{1,0:T(8,128)S(1)}, f32[36,128]{1,0:T(8,128)S(1)}, u32[]{:S(2)}, u32[]{:S(2)}) collective-permute-start(f32[36,128]{1,0:T(8,128)S(1)} %get-tuple-element.52.refs_0_), channel_id=1, source_target_pairs={{0,12},{4,8},{8,4},{12,0},{1,13},{5,9},{9,5},{13,1},{2,14},{6,10},... | collective-permute-start | bytes 55304 | tf_op jit(solution)/shard_map/ppermute | solution.py:368
  29.2 5.0 %collective-permute-start.6 = (f32[36,128]{1,0:T(8,128)S(1)}, f32[36,128]{1,0:T(8,128)S(1)}, u32[]{:S(2)}, u32[]{:S(2)}) collective-permute-start(f32[36,128]{1,0:T(8,128)S(1)} %get-tuple-element.52.refs_0_), channel_id=1, source_target_pairs={{0,8},{4,12},{8,0},{12,4},{1,9},{5,13},{9,1},{13,5},{2,10},{6,14},... | collective-permute-start | bytes 55304 | tf_op jit(solution)/shard_map/ppermute | solution.py:368
  29.2 5.0 %collective-permute-start.7 = (f32[36,128]{1,0:T(8,128)S(1)}, f32[36,128]{1,0:T(8,128)S(1)}, u32[]{:S(2)}, u32[]{:S(2)}) collective-permute-start(f32[36,128]{1,0:T(8,128)S(1)} %get-tuple-element.52.refs_0_), channel_id=1, source_target_pairs={{0,4},{4,0},{8,12},{12,8},{1,5},{5,1},{9,13},{13,9},{2,6},{6,2},{1... | collective-permute-start | bytes 55304 | tf_op jit(solution)/shard_map/ppermute | solution.py:368
  34.2 11.7 %collective-permute-start.10 = (bf16[1200,128]{1,0:T(8,128)(2,1)S(1)}, bf16[1200,128]{1,0:T(8,128)(2,1)S(1)}, u32[]{:S(2)}, u32[]{:S(2)}) collective-permute-start(bf16[1200,128]{1,0:T(8,128)(2,1)S(1)} %get-tuple-element.60), channel_id=1, source_target_pairs={{0,4},{4,0},{8,12},{12,8},{1,5},{5,1},{9,13},{13,9},{2,6},{6,2},{1... | collective-permute-start | bytes 921608 | tf_op jit(solution)/shard_map/ppermute | solution.py:368
  35.1 11.9 %collective-permute-start.17 = (bf16[1200,128]{1,0:T(8,128)(2,1)S(1)}, bf16[1200,128]{1,0:T(8,128)(2,1)S(1)}, u32[]{:S(2)}, u32[]{:S(2)}) collective-permute-start(bf16[1200,128]{1,0:T(8,128)(2,1)S(1)} %relay_chunk.1), channel_id=1, source_target_pairs={{0,8},{4,12},{8,0},{12,4},{1,9},{5,13},{9,1},{13,5},{2,10},{6,14},... | collective-permute-start | bytes 921608 | tf_op jit(solution)/shard_map/ppermute | solution.py:368
  36.3 3.0 %collective-permute-start.11 = (f32[2,128]{1,0:T(2,128)S(1)}, f32[2,128]{1,0:T(2,128)S(1)}, u32[]{:S(2)}, u32[]{:S(2)}) collective-permute-start(f32[2,128]{1,0:T(2,128)S(1)} %get-tuple-element.59.refs_2_), channel_id=1, source_target_pairs={{0,3},{1,2},{2,1},{3,0},{4,7},{5,6},{6,5},{7,4},{8,11},{9,10},{10,... | collective-permute-start | bytes 3080 | tf_op jit(solution)/shard_map/ppermute | solution.py:368
  36.3 3.6 %collective-permute-start.12 = (f32[2,128]{1,0:T(2,128)S(1)}, f32[2,128]{1,0:T(2,128)S(1)}, u32[]{:S(2)}, u32[]{:S(2)}) collective-permute-start(f32[2,128]{1,0:T(2,128)S(1)} %get-tuple-element.59.refs_2_), channel_id=1, source_target_pairs={{0,2},{1,3},{2,0},{3,1},{4,6},{5,7},{6,4},{7,5},{8,10},{9,11},{10,... | collective-permute-start | bytes 3080 | tf_op jit(solution)/shard_map/ppermute | solution.py:368
  37.9 2.1 %collective-permute-start.13 = (f32[2,128]{1,0:T(2,128)S(1)}, f32[2,128]{1,0:T(2,128)S(1)}, u32[]{:S(2)}, u32[]{:S(2)}) collective-permute-start(f32[2,128]{1,0:T(2,128)S(1)} %get-tuple-element.59.refs_2_), channel_id=1, source_target_pairs={{0,1},{1,0},{2,3},{3,2},{4,5},{5,4},{6,7},{7,6},{8,9},{9,8},{10,11... | collective-permute-start | bytes 3080 | tf_op jit(solution)/shard_map/ppermute | solution.py:368
  41.4 3.1 %collective-permute-start.14 = (f32[2,512]{1,0:T(2,128)S(1)}, f32[2,512]{1,0:T(2,128)S(1)}, u32[]{:S(2)}, u32[]{:S(2)}) collective-permute-start(f32[2,512]{1,0:T(2,128)S(1)} %partial_weights.1.refs_0_), channel_id=1, source_target_pairs={{0,3},{1,2},{2,1},{3,0},{4,7},{5,6},{6,5},{7,4},{8,11},{9,10},{10,... | collective-permute-start | bytes 12296 | tf_op jit(solution)/shard_map/ppermute | solution.py:368
  42.3 3.6 %collective-permute-start.15 = (f32[2,512]{1,0:T(2,128)S(1)}, f32[2,512]{1,0:T(2,128)S(1)}, u32[]{:S(2)}, u32[]{:S(2)}) collective-permute-start(f32[2,512]{1,0:T(2,128)S(1)} %partial_weights.1.refs_0_), channel_id=1, source_target_pairs={{0,2},{1,3},{2,0},{3,1},{4,6},{5,7},{6,4},{7,5},{8,10},{9,11},{10,... | collective-permute-start | bytes 12296 | tf_op jit(solution)/shard_map/ppermute | solution.py:368
  43.8 2.1 %collective-permute-start.16 = (f32[2,512]{1,0:T(2,128)S(1)}, f32[2,512]{1,0:T(2,128)S(1)}, u32[]{:S(2)}, u32[]{:S(2)}) collective-permute-start(f32[2,512]{1,0:T(2,128)S(1)} %partial_weights.1.refs_0_), channel_id=1, source_target_pairs={{0,1},{1,0},{2,3},{3,2},{4,5},{5,4},{6,7},{7,6},{8,9},{9,8},{10,11... | collective-permute-start | bytes 12296 | tf_op jit(solution)/shard_map/ppermute | solution.py:368
